TPU v7x, 32 devices: a whole 2x2x4 slice. The times are simulated.
32 devices in a mesh: row: 8 (over y, x, core), col: 4 (over z).
Axes of the slice: x: 2, y: 2, z: 4, core: 2. Of those that a mesh axis runs over, the one named last changes fastest.
Arguments:
- node_feats: bfloat16 [16384, 512], P('row', 'col'), may hold values from -6 to 6
- hidden_act: bfloat16 [16384, 512], P('row', 'col'), may hold values from 0 to 2
- grad_out: bfloat16 [16384, 512], P('row', 'col'), may hold values from -6 to 6
- relu_mask: int32 [16384, 512], P('row', 'col'), may hold values 0 or 1
- edge_tiles: bfloat16 [128, 20, 128, 128], P('row'), may hold values from -0.125 to 0.125
- block_cols: int32 [128, 20], P('row'), may hold values from 0 to 127
- weight_one: bfloat16 [512, 512], P('col'), may hold values from -0.25 to 0.25
- weight_two: bfloat16 [512, 512], P('col'), may hold values from -0.25 to 0.25
Outputs:
- input_grad: bfloat16 [16384, 512], P('row', 'col')
- first_grad: float32 [512, 512], P('col')
- second_grad: float32 [512, 512], P('col')
All inputs are finite; a program needn't handle non-finite values. No bound on the sum of `relu_mask` on one device may be relied on, other than what follows from the above.
Results may differ from a plain program's by a relative error of at most 0.03.
Values may be sent and summed in bfloat16 or wider, within the bound.
No kernel may reach another device: no remote copies, remote signals or barrier semaphores. Data moves between devices by JAX's collectives and lax.ppermute only.
A program may use at most 128 MiB of HBM per device.

v0:
```python
import jax
import jax.numpy as jnp
from jax import lax
from jax.sharding import PartitionSpec as P


def tile_terms(edge_tiles, values):
    local_blocks, per_row, tile_rows, _ = edge_tiles.shape
    feat_cols = values.shape[1]
    blocks = values.reshape(local_blocks, tile_rows, feat_cols)
    terms = jnp.einsum("rkij,rid->rkjd", edge_tiles, blocks, preferred_element_type=jnp.float32)
    flat = terms.reshape(local_blocks * per_row, tile_rows * feat_cols)
    upper = flat.astype(jnp.bfloat16)
    lower = (flat - upper.astype(jnp.float32)).astype(jnp.bfloat16)
    return (upper, lower, feat_cols)


def collect_terms(split_terms, flat_cols, first_row, row_count):
    upper, lower, feat_cols = split_terms
    tile_rows = upper.shape[1] // feat_cols
    first_block = first_row // tile_rows
    block_count = row_count // tile_rows
    targets = first_block + jnp.arange(block_count, dtype=jnp.int32)
    selector = (targets[:, None] == flat_cols[None, :]).astype(jnp.bfloat16)
    summed = jnp.dot(selector, upper, preferred_element_type=jnp.float32)
    summed = summed + jnp.dot(selector, lower, preferred_element_type=jnp.float32)
    return summed.reshape(row_count, feat_cols)


def spread_hidden(split_terms, flat_cols, rows_dev):
    total_rows = lax.axis_size("row") * rows_dev
    dense_terms = collect_terms(split_terms, flat_cols, 0, total_rows)
    return lax.psum_scatter(
        dense_terms.astype(jnp.bfloat16), "row", scatter_dimension=0, tiled=True
    ).astype(jnp.float32)


def spread_input(split_terms, flat_cols, rows_dev):
    total_rows = lax.axis_size("row") * rows_dev
    dense_terms = collect_terms(split_terms, flat_cols, 0, total_rows)
    return lax.psum_scatter(
        dense_terms.astype(jnp.bfloat16), "row", scatter_dimension=0, tiled=True
    ).astype(jnp.float32)


def per_device(
    node_feats, hidden_act, grad_out, relu_mask, edge_tiles, block_cols, weight_one, weight_two
):
    rows_dev, feat_cols = node_feats.shape
    tile_rows = edge_tiles.shape[2]
    flat_cols = block_cols.reshape(-1)
    contract_rows = (((0,), (0,)), ((), ()))
    contract_cols = (((1,), (1,)), ((), ()))
    stacked = jnp.concatenate([node_feats, hidden_act], axis=1)
    gathered = lax.all_gather(stacked, "row", axis=0, tiled=True)
    table = gathered.reshape(gathered.shape[0] // tile_rows, tile_rows, 2 * feat_cols)
    picked = table[block_cols]
    summed = jnp.einsum("rkij,rkjd->rid", edge_tiles, picked, preferred_element_type=jnp.float32)
    summed = summed.astype(jnp.bfloat16).reshape(rows_dev, 2 * feat_cols)
    agg_feats = summed[:, :feat_cols]
    agg_hidden = summed[:, feat_cols:]
    grad_full = lax.all_gather(grad_out, "col", axis=1, tiled=True)
    second_part = lax.dot_general(
        agg_hidden, grad_full, contract_rows, preferred_element_type=jnp.float32
    )
    second_grad = lax.psum(second_part.astype(jnp.bfloat16), "row").astype(jnp.float32)
    d_hidden_agg = lax.dot_general(
        grad_full, weight_two, contract_cols, preferred_element_type=jnp.float32
    ).astype(jnp.bfloat16)
    hidden_grad = spread_hidden(tile_terms(edge_tiles, d_hidden_agg), flat_cols, rows_dev)
    delta = (hidden_grad * relu_mask.astype(jnp.float32)).astype(jnp.bfloat16)
    delta_full = lax.all_gather(delta, "col", axis=1, tiled=True)
    first_part = lax.dot_general(
        agg_feats, delta_full, contract_rows, preferred_element_type=jnp.float32
    )
    first_grad = lax.psum(first_part.astype(jnp.bfloat16), "row").astype(jnp.float32)
    d_feats_agg = lax.dot_general(
        delta_full, weight_one, contract_cols, preferred_element_type=jnp.float32
    ).astype(jnp.bfloat16)
    input_grad = spread_input(tile_terms(edge_tiles, d_feats_agg), flat_cols, rows_dev).astype(
        jnp.bfloat16
    )
    return (input_grad, first_grad, second_grad)


def solution(mesh):
    in_specs = (
        P("row", "col"),
        P("row", "col"),
        P("row", "col"),
        P("row", "col"),
        P("row", None, None, None),
        P("row", None),
        P("col", None),
        P("col", None),
    )
    out_specs = (P("row", "col"), P("col", None), P("col", None))
    return jax.shard_map(
        per_device, mesh=mesh, in_specs=in_specs, out_specs=out_specs, check_vma=False
    )
```

profile of v0, /device:TPU:0, one launch (start us, length us, event | category | flops | bytes accessed | tf_op | source)
XLA Modules:
  0.0 452.2 jit_solution(1187033594891286419)
XLA Ops:
  7.2 0.0 copy-start
  7.2 0.0 all-gather.4.cloned.1.call-start
  7.2 0.7 all-gather.4.cloned.1.call-update
  7.9 0.0 reduce-scatter.3.cloned.1.call-start
  8.0 0.8 eq.9
  8.7 49.8 %all-gather.4.cloned.1.call-done = bf16[2048,512]{1,0:T(8,128)(2,1)} async-done(((bf16[2048,128]{1,0:T(8,128)(2,1)}), bf16[2048,512]{1,0:T(8,128)(2,1)}) %all-gather.4.cloned.1.call-update) | async-done | bytes 2097168 | tf_op jit(solution)/shard_map/all_gather | solution.py:62
  58.5 0.0 copy-done
  58.6 2.3 convolution_convert_fusion.1
  60.9 13.9 %convolution_bitcast_fusion.1 = f32[16,20,128,128]{2,3,1,0:T(8,128)} fusion(bf16[16,128,128,1]{2,1,3,0:T(8,128)(2,1)S(1)} %bitcast.64, bf16[16,20,128,128]{3,2,1,0:T(8,128)(2,1)} %param.12), kind=kOutput, calls=%fused_computation.14 | convolution fusion | flops 1342177280 | bytes 31981568 | tf_op jit(solution)/shard_map/rkij,rid->rkjd/dot_general | solution.py:11
  74.7 20.1 %copy.14 = f32[16,20,128,128]{3,2,1,0:T(8,128)} copy(f32[16,20,128,128]{2,3,1,0:T(8,128)} %convolution_bitcast_fusion.1) | data formatting | bytes 41943040 | tf_op jit(solution)/shard_map/rkij,rid->rkjd/dot_general | solution.py:11
  94.9 22.7 %fusion.4 = f32[128,16384]{1,0:T(8,128)} fusion(f32[40,8,128,128]{3,2,1,0:T(8,128)} %bitcast.58, s32[320]{0:T(512)S(1)} %eq.9), kind=kOutput, calls=%fused_computation.11 | convolution fusion | flops 1342218240 | bytes 29361408 | tf_op jit(solution)/shard_map/dot_general | solution.py:25
  117.6 24.6 %fusion.2 = bf16[128,16384]{1,0:T(8,128)(2,1)} fusion(f32[128,16384]{1,0:T(8,128)} %fusion.4, f32[40,8,128,128]{3,2,1,0:T(8,128)} %bitcast.59, s32[320]{0:T(512)S(1)} %eq.9), kind=kOutput, calls=%fused_computation.9 | convolution fusion | flops 1367384064 | bytes 33555712 | tf_op jit(solution)/shard_map/dot_general | solution.py:26
  142.2 0.0 copy-start.4
  142.2 0.0 copy-start.5
  142.2 0.0 copy-start.6
  142.2 0.0 copy-start.8
  142.2 0.0 copy-start.7
  142.2 7.5 %convert_element_type.72 = bf16[16384,128]{1,0:T(8,128)(2,1)} reshape(bf16[128,16384]{1,0:T(8,128)(2,1)} %fusion.2) | data formatting | bytes 8388608 | tf_op jit(solution)/shard_map/convert_element_type | solution.py:34
  149.8 0.0 reduce-scatter.3.cloned.1.call-update
  149.8 0.0 all-gather.6.cloned.1.call-start
  149.8 49.7 %reduce-scatter.3.cloned.1.call-done = bf16[2048,128]{1,0:T(8,128)(2,1)} async-done(((bf16[16384,128]{1,0:T(8,128)(2,1)}), bf16[2048,128]{1,0:T(8,128)(2,1)}) %reduce-scatter.3.cloned.1.call-update) | async-done | bytes 524304 | tf_op jit(solution)/shard_map/reduce_scatter | solution.py:33
  199.5 0.0 copy-done.4
  199.5 2.0 multiply_convert_fusion
  201.5 0.0 all-gather.6.cloned.1.call-update
  201.5 0.0 all-gather.8.cloned.1.call-start
  201.6 0.0 copy-done.5
  201.6 0.0 copy-done.6
  201.6 1.1 pad_maximum_fusion
  202.7 0.0 all-gather.8.cloned.1.call-update
  202.7 0.0 all-reduce.3.cloned.1.call-start
  202.8 0.0 copy-done.8
  202.8 0.1 reshape.37
  202.9 45.1 %all-gather.6.cloned.1.call-done = bf16[2048,512]{1,0:T(8,128)(2,1)} async-done(((bf16[2048,128]{1,0:T(8,128)(2,1)}), bf16[2048,512]{1,0:T(8,128)(2,1)}) %all-gather.6.cloned.1.call-update) | async-done | bytes 2097168 | tf_op jit(solution)/shard_map/all_gather | solution.py:72
  248.0 0.0 copy-done.7
  248.0 2.3 convolution_convert_fusion
  250.3 13.9 %convolution_bitcast_fusion = f32[16,20,128,128]{2,3,1,0:T(8,128)} fusion(bf16[16,128,128,1]{2,1,3,0:T(8,128)(2,1)S(1)} %bitcast.65, bf16[16,20,128,128]{3,2,1,0:T(8,128)(2,1)} %param.12), kind=kOutput, calls=%fused_computation.13 | convolution fusion | flops 1342177280 | bytes 31981568 | tf_op jit(solution)/shard_map/rkij,rid->rkjd/dot_general | solution.py:11
  264.2 20.8 %copy.16 = f32[16,20,128,128]{3,2,1,0:T(8,128)} copy(f32[16,20,128,128]{2,3,1,0:T(8,128)} %convolution_bitcast_fusion) | data formatting | bytes 41943040 | tf_op jit(solution)/shard_map/rkij,rid->rkjd/dot_general | solution.py:11
  285.0 22.8 %fusion.5 = f32[128,16384]{1,0:T(8,128)} fusion(f32[40,8,128,128]{3,2,1,0:T(8,128)} %bitcast.56, s32[320]{0:T(512)S(1)} %eq.9), kind=kOutput, calls=%fused_computation.12 | convolution fusion | flops 1342218240 | bytes 29361408 | tf_op jit(solution)/shard_map/dot_general | solution.py:25
  307.9 0.0 all-gather.8.cloned.1.call-done
  307.9 14.9 %gather_fusion = bf16[320,128,256]{2,1,0:T(8,128)(2,1)} fusion(bf16[128,128,256]{2,1,0:T(8,128)(2,1)} %bitcast.61, s32[1024]{0:T(1024)S(1)} %pad_clamp_fusion), kind=kCustom, calls=%fused_computation | custom fusion | bytes 41944320 | tf_op jit(solution)/shard_map/gather | solution.py:57
  322.8 0.0 copy-start.2
  322.8 0.0 copy-start.3
  322.8 13.0 %bitcast_convert_fusion.4 = bf16[16,256,128]{1,2,0:T(8,128)(2,1)S(1)} fusion(bf16[16,20,128,128]{3,2,1,0:T(8,128)(2,1)} %param.12, bf16[16,20,128,256]{3,2,1,0:T(8,128)(2,1)} %bitcast.60), kind=kOutput, calls=%fused_computation.17 | convolution fusion | flops 2684878848 | bytes 32505856 | tf_op jit(solution)/shard_map/rkij,rkjd->rid/dot_general | solution.py:58
  335.8 0.0 copy-done.2
  335.9 1.1 convolution_convert_fusion.2
  337.0 0.0 copy-done.3
  337.0 1.1 convolution_convert_fusion.3
  338.1 0.0 all-reduce.3.cloned.1.call-update
  338.1 0.0 reduce-scatter.5.cloned.1.call-start
  338.2 0.0 copy-start.1
  338.2 24.2 %fusion.3 = bf16[128,16384]{1,0:T(8,128)(2,1)} fusion(f32[128,16384]{1,0:T(8,128)} %fusion.5, f32[40,8,128,128]{3,2,1,0:T(8,128)} %bitcast.57, s32[320]{0:T(512)S(1)} %eq.9), kind=kOutput, calls=%fused_computation.10 | convolution fusion | flops 1367384064 | bytes 33555712 | tf_op jit(solution)/shard_map/dot_general | solution.py:26
  362.4 7.4 %convert_element_type.81 = bf16[16384,128]{1,0:T(8,128)(2,1)} reshape(bf16[128,16384]{1,0:T(8,128)(2,1)} %fusion.3) | data formatting | bytes 8388608 | tf_op jit(solution)/shard_map/convert_element_type | solution.py:42
  369.8 0.0 reduce-scatter.5.cloned.1.call-update
  369.8 20.7 %all-reduce.3.cloned.1.call-done = (bf16[128,512]{1,0:T(8,128)(2,1)}, bf16[128,512]{1,0:T(8,128)(2,1)}) async-done(((bf16[128,512]{1,0:T(8,128)(2,1)}, bf16[128,512]{1,0:T(8,128)(2,1)}), (bf16[128,512]{1,0:T(8,128)(2,1)}, bf16[128,512]{1,0:T(8,128)(2,1)})) %all-reduce.3.cloned.1.call-update) | async-done | bytes 262160 | tf_op jit(solution)/shard_map/psum | solution.py:76
  390.6 1.6 convert_element_type.85
  392.2 1.6 convert_element_type.87
  393.8 51.2 %reduce-scatter.5.cloned.1.call-done = bf16[2048,128]{1,0:T(8,128)(2,1)} async-done(((bf16[16384,128]{1,0:T(8,128)(2,1)}), bf16[2048,128]{1,0:T(8,128)(2,1)}) %reduce-scatter.5.cloned.1.call-update) | async-done | bytes 524304 | tf_op jit(solution)/shard_map/reduce_scatter | solution.py:41
  445.0 0.0 copy-done.1
  (2 shorter events, 0.0 us)
Async XLA Ops:
  7.2 51.4 %copy-start = (bf16[128,512]{1,0:T(8,128)(2,1)S(1)}, bf16[128,512]{1,0:T(8,128)(2,1)}, u32[]{:S(2)}) copy-start(bf16[128,512]{1,0:T(8,128)(2,1)} %param.15) | copy-start | bytes 393220
  7.2 51.4 %all-gather.4.cloned.1.call-start = ((), (), s32[]{:S(2)}) async-start(), calls=%async_computation.2 | async-start | bytes 2621440 | tf_op jit(solution)/shard_map/all_gather | solution.py:62
  7.9 191.6 %reduce-scatter.3.cloned.1.call-start = ((), (), s32[]{:S(2)}) async-start(), calls=%async_computation.3 | async-start | bytes 4718592 | tf_op jit(solution)/shard_map/reduce_scatter | solution.py:33
  142.2 57.3 %copy-start.4 = (s32[2048,128]{1,0:T(8,128)S(1)}, s32[2048,128]{1,0:T(8,128)}, u32[]{:S(2)}) copy-start(s32[2048,128]{1,0:T(8,128)} %param.11) | copy-start | bytes 3145732
  142.2 59.3 %copy-start.5 = (bf16[2048,128]{1,0:T(8,128)(2,1)S(1)}, bf16[2048,128]{1,0:T(8,128)(2,1)}, u32[]{:S(2)}) copy-start(bf16[2048,128]{1,0:T(8,128)(2,1)} %param.9) | copy-start | bytes 1572868
  142.2 59.4 %copy-start.6 = (bf16[2048,128]{1,0:T(8,128)(2,1)S(1)}, bf16[2048,128]{1,0:T(8,128)(2,1)}, u32[]{:S(2)}) copy-start(bf16[2048,128]{1,0:T(8,128)(2,1)} %param.8) | copy-start | bytes 1572868
  142.2 60.5 %copy-start.8 = (s32[16,20]{1,0:T(8,128)S(1)}, s32[16,20]{1,0:T(8,128)}, u32[]{:S(2)}) copy-start(s32[16,20]{1,0:T(8,128)} %param.13) | copy-start | bytes 3844
  142.2 105.8 %copy-start.7 = (bf16[128,512]{1,0:T(8,128)(2,1)S(1)}, bf16[128,512]{1,0:T(8,128)(2,1)}, u32[]{:S(2)}) copy-start(bf16[128,512]{1,0:T(8,128)(2,1)} %param.14) | copy-start | bytes 393220
  149.8 98.2 %all-gather.6.cloned.1.call-start = ((), (), s32[]{:S(2)}) async-start(), calls=%async_computation.4 | async-start | bytes 2621440 | tf_op jit(solution)/shard_map/all_gather | solution.py:72
  201.5 106.4 %all-gather.8.cloned.1.call-start = ((), (), s32[]{:S(2)}) async-start(), calls=%async_computation.6 | async-start | bytes 9437184 | tf_op jit(solution)/shard_map/all_gather | solution.py:55
  202.7 187.8 %all-reduce.3.cloned.1.call-start = ((), (), s32[]{:S(2)}) async-start(), calls=%async_computation.7 | async-start | bytes 524288 | tf_op jit(solution)/shard_map/psum | solution.py:76
  322.8 13.0 %copy-start.2 = (bf16[2048,512]{1,0:T(8,128)(2,1)S(1)}, bf16[2048,512]{1,0:T(8,128)(2,1)}, u32[]{:S(2)}) copy-start(bf16[2048,512]{1,0:T(8,128)(2,1)} %all-gather.4.cloned.1.call-done) | copy-start | bytes 6291460
  322.8 14.1 %copy-start.3 = (bf16[2048,512]{1,0:T(8,128)(2,1)S(1)}, bf16[2048,512]{1,0:T(8,128)(2,1)}, u32[]{:S(2)}) copy-start(bf16[2048,512]{1,0:T(8,128)(2,1)} %all-gather.6.cloned.1.call-done) | copy-start | bytes 6291460
  338.1 106.9 %reduce-scatter.5.cloned.1.call-start = ((), (), s32[]{:S(2)}) async-start(), calls=%async_computation.5 | async-start | bytes 4718592 | tf_op jit(solution)/shard_map/reduce_scatter | solution.py:41
  338.2 106.8 %copy-start.1 = (bf16[128,512]{1,0:T(8,128)(2,1)S(1)}, bf16[128,512]{1,0:T(8,128)(2,1)}, u32[]{:S(2)}) copy-start(bf16[128,512]{1,0:T(8,128)(2,1)} %param.15) | copy-start | bytes 393220
Sparse Core Ops, SparseCore 0:
  9.6 48.9 all-gather.3
  149.9 49.5 reduce-scatter.2
  201.7 46.2 all-gather.5
  249.9 52.6 all-gather.7
  338.3 52.2 all-reduce.2
  394.3 50.6 reduce-scatter.4
where the time goes:
time: 457 us; the launch traced here: 452 us
  waiting for transfers between devices  217 us (47%)
  matrix products  142 us (31%)
  local copies, waits for them, and re-layouts  71.7 us (16%)
  between operations  14.6 us (3%)
  other arithmetic  6.35 us (1%)
    reduce_scatter x1, waiting for transfers between devices, spread_input(): lax.psum_scatter(dense_terms.astype(jnp.bfloat16), 'row', scatter_dimensi...  51.2 us
    all_gather x1, waiting for transfers between devices, per_device(): grad_full = lax.all_gather(grad_out, 'col', axis=1, tiled=True)  49.8 us
    reduce_scatter x1, waiting for transfers between devices, spread_hidden(): lax.psum_scatter(dense_terms.astype(jnp.bfloat16), 'row', scatter_dimensi...  49.7 us
    dot_general x2, matrix products, collect_terms(): jnp.dot(selector, lower, preferred_element_type=jnp.float32)  48.9 us
    dot_general x2, matrix products, collect_terms(): summed = jnp.dot(selector, upper, preferred_element_type=jnp.float32)  45.6 us
    all_gather x1, waiting for transfers between devices, per_device(): delta_full = lax.all_gather(delta, 'col', axis=1, tiled=True)  45.1 us
    dot_general x2, local copies, waits for them, and re-layouts, tile_terms(): jnp.einsum('rkij,rid->rkjd', edge_tiles, blocks, preferred_element_type=j...  40.9 us
    dot_general x2, matrix products, tile_terms(): jnp.einsum('rkij,rid->rkjd', edge_tiles, blocks, preferred_element_type=j...  27.8 us
  transfers between devices with their start and end apart: 6, of which 5 were waited for; matrix products, arithmetic and copies ran while one was open for 21% of the time, Pallas kernels for 0%

commit v1 on v0

v1 whole, which is shorter than its diff:
```python
import functools

import jax
import jax.numpy as jnp
from jax import lax
from jax.experimental import pallas as pl
from jax.experimental.pallas import tpu as pltpu
from jax.sharding import PartitionSpec as P

VMEM_LIMIT = 56 * 1024 * 1024
GROUPS = 2
F32 = jnp.float32
BF16 = jnp.bfloat16


def spread_kernel(groups, flip, cols_ref, me_ref, tiles_ref, vals_ref, *rest):
    outs, acc = rest[:-1], rest[-1]
    step = pl.program_id(0)
    per_row = tiles_ref.shape[1]
    width = tiles_ref.shape[3]

    @pl.when(step == 0)
    def _():
        acc[...] = jnp.zeros_like(acc)

    left = vals_ref[0]
    if flip:
        left = left.astype(F32).T.astype(BF16)
    for k in range(0, per_row, 2):
        pair = jnp.concatenate([tiles_ref[0, k], tiles_ref[0, k + 1]], axis=1)
        both = jnp.dot(left, pair, preferred_element_type=F32)
        for side in range(2):
            target = cols_ref[step, k + side]
            acc[target] += both[:, side * width : (side + 1) * width]

    @pl.when(step == pl.num_programs(0) - 1)
    def _():
        me = me_ref[0]
        halves = outs[0].shape[0]
        size = outs[0].shape[1]
        blocks_dev = groups * size
        for g in range(groups):
            for side in range(2):
                out = outs[2 * g + side]
                for rel in range(halves):
                    owner = jnp.bitwise_xor(me, 2 * rel + side)
                    first = owner * blocks_dev + g * size
                    out[rel] = acc[pl.ds(first, size)].astype(BF16)


def spread(edge_tiles, block_cols, vals, me, rows, flip):
    blocks, per_row, size, _ = edge_tiles.shape
    feat = vals.shape[2] if flip else vals.shape[1]
    per_group = blocks // GROUPS
    out_shape = jax.ShapeDtypeStruct((rows // 2, per_group, feat, size), BF16)
    whole = lambda step, *_: (0, 0, 0, 0)
    return pl.pallas_call(
        functools.partial(spread_kernel, GROUPS, flip),
        out_shape=[out_shape] * (2 * GROUPS),
        grid_spec=pltpu.PrefetchScalarGridSpec(
            num_scalar_prefetch=2,
            grid=(blocks,),
            in_specs=[
                pl.BlockSpec((1, per_row, size, size), lambda step, *_: (step, 0, 0, 0)),
                pl.BlockSpec((1,) + vals.shape[1:], lambda step, *_: (step, 0, 0)),
            ],
            out_specs=[pl.BlockSpec(out_shape.shape, whole)] * (2 * GROUPS),
            scratch_shapes=[pltpu.VMEM((rows * blocks, feat, size), F32)],
        ),
        compiler_params=pltpu.CompilerParams(vmem_limit_bytes=VMEM_LIMIT),
    )(block_cols, me.reshape(1), edge_tiles, vals)


def dense_kernel(cols, final, col_ref, weight_ref, *rest):
    shards, rest = rest[: 2 * cols - 1], rest[2 * cols - 1 :]
    if final:
        side_ref, out_ref, grad_ref = rest
    else:
        side_ref, mask_ref, out_ref, grad_ref = rest
    own, ups, downs = shards[0], shards[1:cols], shards[cols:]
    col = col_ref[0]
    blocks, feat, size = own.shape
    weight = weight_ref[...]
    total = None
    for b in range(blocks):
        parts = [own[b]]
        for s in range(1, cols):
            parts.append(jnp.where(col >= s, ups[s - 1][b], downs[cols - s - 1][b]))
        stacked = jnp.concatenate(parts, axis=0)
        res = jnp.dot(weight, stacked, preferred_element_type=F32)
        if final:
            out_ref[b] = res.T.astype(BF16)
        else:
            out_ref[b] = (res * mask_ref[b].astype(F32)).astype(BF16)
        term = jnp.dot(stacked, side_ref[b], preferred_element_type=F32)
        total = term if total is None else total + term
    for s in range(cols):
        place = lax.rem(col - s + cols, cols)
        grad_ref[place] = total[s * feat : (s + 1) * feat]


def dense(weight, shards, side, mask, col, cols):
    own = shards[0]
    blocks, feat, size = own.shape
    final = mask is None
    out = (blocks, size, feat) if final else (blocks, feat, size)
    grad = (cols, feat, side.shape[2])
    args = [weight, *shards, side] + ([] if final else [mask])
    vmem = pl.BlockSpec(memory_space=pltpu.VMEM)
    return pl.pallas_call(
        functools.partial(dense_kernel, cols, final),
        out_shape=[jax.ShapeDtypeStruct(out, BF16), jax.ShapeDtypeStruct(grad, F32)],
        in_specs=[pl.BlockSpec(memory_space=pltpu.SMEM)] + [vmem] * len(args),
        out_specs=[vmem, vmem],
        compiler_params=pltpu.CompilerParams(vmem_limit_bytes=VMEM_LIMIT),
    )(col.reshape(1), *args)


def swap(value, mask, rows):
    return lax.ppermute(value, "row", [(i, i ^ mask) for i in range(rows)])


def add(a, b):
    return (a.astype(F32) + b.astype(F32)).astype(BF16)


def scatter_chunk(keep, got, masks):
    rows = lax.axis_size("row")
    left = sorted(masks, reverse=True)
    for mask in masks:
        axis = left.index(mask)
        part = lambda v, i: lax.index_in_dim(v, i, axis, keepdims=False)
        sent = swap(add(part(keep, 1), part(got, 1)), mask, rows)
        keep = add(part(keep, 0), part(got, 0))
        got = sent
        left.remove(mask)
    return add(keep, got)


def scatter_group(keep, send):
    rows = lax.axis_size("row")
    got = swap(send, 1, rows)
    bits = rows.bit_length() - 1
    masks = [1 << b for b in range(1, bits)]
    lead = (2,) * len(masks)
    keep = keep.reshape(lead + keep.shape[1:])
    got = got.reshape(lead + got.shape[1:])
    axis = len(lead)
    half = keep.shape[axis] // 2
    done = []
    for i, order in enumerate((masks, masks[::-1])):
        cut = lambda v: lax.slice_in_dim(v, i * half, (i + 1) * half, axis=axis)
        done.append(scatter_chunk(cut(keep), cut(got), order))
    return jnp.concatenate(done, axis=0)


def chain_gather(own, cols):
    ups, downs = [], []
    up, down = own, own
    for s in range(1, cols):
        up = lax.ppermute(up, "col", [(i, i + 1) for i in range(s - 1, cols - 1)])
        down = lax.ppermute(down, "col", [(i, i - 1) for i in range(1, cols - s + 1)])
        ups.append(up)
        downs.append(down)
    return [own, *ups, *downs]


def row_sum(value, rows):
    mask = 1
    while mask < rows:
        value = value.astype(BF16)
        value = value.astype(F32) + swap(value, mask, rows).astype(F32)
        mask *= 2
    return value


def layer(edge_tiles, block_cols, vals, weight, side, mask, me, col, rows, cols, flip):
    pieces = spread(edge_tiles, block_cols, vals, me, rows, flip)
    outs, grads = [], []
    per_group = edge_tiles.shape[0] // GROUPS
    for g in range(GROUPS):
        shard = scatter_group(pieces[2 * g], pieces[2 * g + 1])
        shards = chain_gather(shard, cols)
        cut = slice(g * per_group, (g + 1) * per_group)
        out, grad = dense(weight, shards, side[cut], None if mask is None else mask[cut], col, cols)
        outs.append(out)
        grads.append(grad)
    grad = row_sum(sum(grads), rows)
    feat_all, own = grad.shape[0] * grad.shape[1], grad.shape[2]
    return jnp.concatenate(outs, axis=0), grad.reshape(feat_all, own).T


def ring_order(weight, col, cols):
    out_rows, total = weight.shape
    split = weight.reshape(out_rows, cols, total // cols)
    parts = [lax.dynamic_index_in_dim(split, lax.rem(col - s + cols, cols), 1, keepdims=False) for s in range(cols)]
    return jnp.concatenate(parts, axis=1)


def per_device(
    node_feats, hidden_act, grad_out, relu_mask, edge_tiles, block_cols, weight_one, weight_two
):
    rows, cols = lax.axis_size("row"), lax.axis_size("col")
    me, col = lax.axis_index("row").astype(jnp.int32), lax.axis_index("col").astype(jnp.int32)
    size = edge_tiles.shape[2]
    blocked = lambda v: v.reshape(v.shape[0] // size, size, v.shape[1])
    mask = blocked(relu_mask).astype(BF16).transpose(0, 2, 1)
    weight_two = ring_order(weight_two, col, cols)
    weight_one = ring_order(weight_one, col, cols)
    delta, second_grad = layer(
        edge_tiles, block_cols, blocked(grad_out), weight_two, blocked(hidden_act), mask, me, col, rows, cols, True
    )
    out, first_grad = layer(
        edge_tiles, block_cols, delta, weight_one, blocked(node_feats), None, me, col, rows, cols, False
    )
    return out.reshape(node_feats.shape), first_grad, second_grad


def solution(mesh):
    in_specs = (
        P("row", "col"),
        P("row", "col"),
        P("row", "col"),
        P("row", "col"),
        P("row", None, None, None),
        P("row", None),
        P("col", None),
        P("col", None),
    )
    out_specs = (P("row", "col"), P("col", None), P("col", None))
    return jax.shard_map(
        per_device, mesh=mesh, in_specs=in_specs, out_specs=out_specs, check_vma=False
    )
```

time: 457 us -> 192 us (0.42)
  waiting for transfers between devices: 217 us -> 52.2 us
  matrix products: 142 us -> 0 us
  starting transfers between devices: 0.24 us -> 66.8 us
  local copies, waits for them, and re-layouts: 71.7 us -> 8.17 us
  Pallas kernels: 0 us -> 45.4 us
  between operations: 14.6 us -> 1.57 us
  other arithmetic: 6.35 us -> 16.7 us
    dot_general x11 -> x0, matrix products: 142 us -> none  [the longest x2 48.9 us: collect_terms(): jnp.dot(selector, lower, preferred_element_type=jnp.float32)]
    reduce_scatter x2 -> x0, waiting for transfers between devices: 101 us -> none  [the longest x1 51.2 us: spread_input(): lax.psum_scatter(dense_terms.astype(jnp.bfloat16), 'row', scatter_dimensi...]
    all_gather x3 -> x0, waiting for transfers between devices: 94.9 us -> none  [the longest x1 49.8 us: per_device(): grad_full = lax.all_gather(grad_out, 'col', axis=1, tiled=True)]
    ppermute x0 -> x50, starting transfers between devices: none -> 66.8 us  [the longest x26 28.2 us: swap(): return lax.ppermute(value, 'row', [(i, i ^ mask) for i in range(rows)])]
    ppermute x0 -> x50, waiting for transfers between devices: none -> 52.2 us  [the longest x12 28.1 us: chain_gather(): lax.ppermute(down, 'col', [(i, i - 1) for i in range(1, cols - s + 1)])]
    pallas_call x0 -> x6, Pallas kernels: none -> 45.4 us  [the longest x2 32.9 us: spread(): pl.pallas_call(functools.partial(spread_kernel, GROUPS, flip), out_shape=...]
    dot_general x2 -> x0, local copies, waits for them, and re-layouts: 40.9 us -> none  [tile_terms(): jnp.einsum('rkij,rid->rkjd', edge_tiles, blocks, preferred_element_type=j...]
    psum x1 -> x0, waiting for transfers between devices: 20.7 us -> none  [per_device(): lax.psum(first_part.astype(jnp.bfloat16), 'row').astype(jnp.float32)]
  transfers between devices with their start and end apart: 6 -> 50, of which waited for: 5 -> 24; matrix products, arithmetic and copies ran while one was open for 21% -> 10% of each run, Pallas kernels for 0% -> 5%
where the time goes in v1:
time: 192 us; the launch traced here: 191 us
  starting transfers between devices  66.8 us (35%)
  waiting for transfers between devices  52.2 us (27%)
  Pallas kernels  45.4 us (24%)
  other arithmetic  16.7 us (9%)
  local copies, waits for them, and re-layouts  8.17 us (4%)
    pallas_call x2, Pallas kernels, spread(): pl.pallas_call(functools.partial(spread_kernel, GROUPS, flip), out_shape=...  32.9 us
    ppermute x26, starting transfers between devices, swap(): return lax.ppermute(value, 'row', [(i, i ^ mask) for i in range(rows)])  28.2 us
    ppermute x12, waiting for transfers between devices, chain_gather(): lax.ppermute(down, 'col', [(i, i - 1) for i in range(1, cols - s + 1)])  28.1 us
    ppermute x12, starting transfers between devices, chain_gather(): up = lax.ppermute(up, 'col', [(i, i + 1) for i in range(s - 1, cols - 1)])  23 us
    ppermute x26, waiting for transfers between devices, swap(): return lax.ppermute(value, 'row', [(i, i ^ mask) for i in range(rows)])  23 us
    ppermute x12, starting transfers between devices, chain_gather(): lax.ppermute(down, 'col', [(i, i - 1) for i in range(1, cols - s + 1)])  15.6 us
    pallas_call x4, Pallas kernels, dense(): pl.pallas_call(functools.partial(dense_kernel, cols, final), out_shape=[j...  12.4 us
    convert_element_type x24, other arithmetic, add(): return (a.astype(F32) + b.astype(F32)).astype(BF16)  10.1 us
  transfers between devices with their start and end apart: 50, of which 24 were waited for; matrix products, arithmetic and copies ran while one was open for 10% of the time, Pallas kernels for 5%

profile of v1, /device:TPU:0, one launch (start us, length us, event | category | flops | bytes accessed | tf_op | source)
XLA Modules:
  0.0 190.8 jit_solution(6232035556844525799)
XLA Ops:
  0.7 16.7 %shard_map.103 = (bf16[4,8,128,128]{3,2,1,0:T(8,128)(2,1)}, bf16[4,8,128,128]{3,2,1,0:T(8,128)(2,1)}, bf16[4,8,128,128]{3,2,1,0:T(8,128)(2,1)}, bf16[4,8,128,128]{3,2,1,0:T(8,128)(2,1)}) custom-call(s32[16,20]{1,0:T(8,128)} %cols_ref.3, s32[1]{0:T(128)} %bitcast.5.me_ref, bf16[16,20,128,128]{3,2,1,0:T(8,128)(2,1)} %tiles_ref.3, bf16[16,128,128]{2,1,0:T(8,128)(2,1)} %bitcast.222), custom_call_target="tpu_custom_call" | custom-call | tf_op jit(solution)/shard_map/pallas_call | solution.py:57
  17.9 2.4 %collective-permute-done = bf16[4,8,128,128]{3,2,1,0:T(8,128)(2,1)S(1)} collective-permute-done((bf16[4,8,128,128]{3,2,1,0:T(8,128)(2,1)}, bf16[4,8,128,128]{3,2,1,0:T(8,128)(2,1)S(1)}, u32[]{:S(2)}, u32[]{:S(2)}) %collective-permute-start) | collective-permute-done | bytes 1048608 | tf_op jit(solution)/shard_map/ppermute | solution.py:120
  20.3 1.2 add_convert_fusion.15
  21.5 2.9 %collective-permute-start.1 = (bf16[2,4,128,128]{3,2,1,0:T(8,128)(2,1)S(1)}, bf16[2,4,128,128]{3,2,1,0:T(8,128)(2,1)S(1)}, u32[]{:S(2)}, u32[]{:S(2)}) collective-permute-start(bf16[2,4,128,128]{3,2,1,0:T(8,128)(2,1)S(1)} %get-tuple-element.44), channel_id=1, source_target_pairs={{0,8},{4,12},{8,0},{12,4},{16,24},{20,28},{24,16},{28,20},{1,9},{5... | collective-permute-start | bytes 786440 | tf_op jit(solution)/shard_map/ppermute | solution.py:120
  24.4 1.2 add_convert_fusion.13
  25.6 1.6 collective-permute-start.3
  27.2 1.2 add_convert_fusion.11
  28.4 1.2 add_convert_fusion.9
  31.1 2.3 %collective-permute-start.2 = (bf16[4,128,128]{2,1,0:T(8,128)(2,1)S(1)}, bf16[4,128,128]{2,1,0:T(8,128)(2,1)S(1)}, u32[]{:S(2)}, u32[]{:S(2)}) collective-permute-start(bf16[4,128,128]{2,1,0:T(8,128)(2,1)S(1)} %fusion.33), channel_id=1, source_target_pairs={{0,16},{4,20},{8,24},{12,28},{16,0},{20,4},{24,8},{28,12},{1,17},{... | collective-permute-start | bytes 393224 | tf_op jit(solution)/shard_map/ppermute | solution.py:120
  33.3 1.5 collective-permute-done.3
  35.3 3.5 %collective-permute-done.12 = bf16[2,4,128,128]{3,2,1,0:T(8,128)(2,1)S(1)} collective-permute-done((bf16[2,4,128,128]{3,2,1,0:T(8,128)(2,1)S(1)}, bf16[2,4,128,128]{3,2,1,0:T(8,128)(2,1)S(1)}, u32[]{:S(2)}, u32[]{:S(2)}) %collective-permute-start.12) | collective-permute-done | bytes 262176 | tf_op jit(solution)/shard_map/ppermute | solution.py:120
  39.5 1.0 collective-permute-done.14
  41.0 2.3 %collective-permute-done.2 = bf16[4,128,128]{2,1,0:T(8,128)(2,1)S(1)} collective-permute-done((bf16[4,128,128]{2,1,0:T(8,128)(2,1)S(1)}, bf16[4,128,128]{2,1,0:T(8,128)(2,1)S(1)}, u32[]{:S(2)}, u32[]{:S(2)}) %collective-permute-start.2) | collective-permute-done | bytes 131104 | tf_op jit(solution)/shard_map/ppermute | solution.py:120
  43.5 1.3 collective-permute-start.8
  44.8 4.6 %collective-permute-start.5 = (bf16[8,128,128]{2,1,0:T(8,128)(2,1)S(1)}, bf16[8,128,128]{2,1,0:T(8,128)(2,1)S(1)}, u32[]{:S(2)}, u32[]{:S(2)}) collective-permute-start(bf16[8,128,128]{2,1,0:T(8,128)(2,1)S(1)} %pad_maximum_fusion.2.rest_0_), channel_id=1, source_target_pairs={{0,1},{1,2},{2,3},{4,5},{5,6},{6,7},{8,9},{9,10},{10,11},{12,13},{... | collective-permute-start | bytes 786440 | tf_op jit(solution)/shard_map/ppermute | solution.py:161
  49.5 4.2 %collective-permute-start.16 = (bf16[8,128,128]{2,1,0:T(8,128)(2,1)S(1)}, bf16[8,128,128]{2,1,0:T(8,128)(2,1)}, u32[]{:S(2)}, u32[]{:S(2)}) collective-permute-start(bf16[8,128,128]{2,1,0:T(8,128)(2,1)S(1)} %pad_maximum_fusion.3.rest_0_), channel_id=1, source_target_pairs={{0,1},{1,2},{2,3},{4,5},{5,6},{6,7},{8,9},{9,10},{10,11},{12,13},{... | collective-permute-start | bytes 786440 | tf_op jit(solution)/shard_map/ppermute | solution.py:161
  53.7 1.3 collective-permute-start.19
  55.2 1.3 collective-permute-start.9
  56.5 1.4 collective-permute-start.6
  58.8 1.4 collective-permute-start.17
  60.2 3.5 %collective-permute-done.19.rest_4_ = bf16[8,128,128]{2,1,0:T(8,128)(2,1)} collective-permute-done((bf16[8,128,128]{2,1,0:T(8,128)(2,1)S(1)}, bf16[8,128,128]{2,1,0:T(8,128)(2,1)}, u32[]{:S(2)}, u32[]{:S(2)}) %collective-permute-start.19) | collective-permute-done | bytes 262176 | tf_op jit(solution)/shard_map/ppermute | solution.py:162
  63.8 1.3 collective-permute-start.20
  66.9 1.3 collective-permute-start.10
  69.6 6.6 %collective-permute-done.20.rest_5_ = bf16[8,128,128]{2,1,0:T(8,128)(2,1)} collective-permute-done((bf16[8,128,128]{2,1,0:T(8,128)(2,1)}, bf16[8,128,128]{2,1,0:T(8,128)(2,1)}, u32[]{:S(2)}, u32[]{:S(2)}) %collective-permute-start.20) | collective-permute-done | bytes 262176 | tf_op jit(solution)/shard_map/ppermute | solution.py:162
  76.1 1.3 collective-permute-start.21
  78.9 1.7 collective-permute-done.10.rest_6_
  81.4 3.2 %shard_map.104 = (bf16[8,128,128]{2,1,0:T(8,128)(2,1)}, f32[4,128,128]{2,1,0:T(8,128)}) custom-call(s32[1]{0:T(128)} %bitcast.col_ref, bf16[128,512]{1,0:T(8,128)(2,1)} %pad_maximum_fusion.7.weight_ref, bf16[8,128,128]{2,1,0:T(8,128)(2,1)} %copy-done.3, bf16[8,128,128]{2,1,0:T(8,128)(2,1)} %copy-done.22, ...), custom_call_target="tpu_custom_call" | custom-call | tf_op jit(solution)/shard_map/pallas_call | solution.py:110
  85.4 3.1 %shard_map.105 = (bf16[8,128,128]{2,1,0:T(8,128)(2,1)}, f32[4,128,128]{2,1,0:T(8,128)}) custom-call(s32[1]{0:T(128)} %bitcast.col_ref, bf16[128,512]{1,0:T(8,128)(2,1)} %pad_maximum_fusion.7.weight_ref, bf16[8,128,128]{2,1,0:T(8,128)(2,1)} %copy-done.4, bf16[8,128,128]{2,1,0:T(8,128)(2,1)} %collective-permute-done.16.rest_1_, ...), custom_call_target="tpu_custom_call" | custom-call | tf_op jit(solution)/shard_map/pallas_call | solution.py:110
  88.5 1.9 pad_maximum_fusion.vals_ref
  90.4 16.2 %shard_map.106 = (bf16[4,8,128,128]{3,2,1,0:T(8,128)(2,1)}, bf16[4,8,128,128]{3,2,1,0:T(8,128)(2,1)}, bf16[4,8,128,128]{3,2,1,0:T(8,128)(2,1)}, bf16[4,8,128,128]{3,2,1,0:T(8,128)(2,1)}) custom-call(s32[16,20]{1,0:T(8,128)} %cols_ref.3, s32[1]{0:T(128)} %bitcast.5.me_ref, bf16[16,20,128,128]{3,2,1,0:T(8,128)(2,1)} %tiles_ref.3, ...), custom_call_target="tpu_custom_call" | custom-call | tf_op jit(solution)/shard_map/pallas_call | solution.py:57
  107.1 2.4 %collective-permute-done.22 = bf16[4,8,128,128]{3,2,1,0:T(8,128)(2,1)S(1)} collective-permute-done((bf16[4,8,128,128]{3,2,1,0:T(8,128)(2,1)}, bf16[4,8,128,128]{3,2,1,0:T(8,128)(2,1)S(1)}, u32[]{:S(2)}, u32[]{:S(2)}) %collective-permute-start.22) | collective-permute-done | bytes 1048608 | tf_op jit(solution)/shard_map/ppermute | solution.py:120
  109.5 1.2 add_convert_fusion.7
  111.4 1.2 add_convert_fusion.5
  112.6 1.5 collective-permute-start.25
  114.0 1.2 add_convert_fusion.3
  115.2 1.2 add_convert_fusion.1
  116.4 1.5 collective-permute-start.34
  119.5 2.0 %collective-permute-start.24 = (bf16[4,128,128]{2,1,0:T(8,128)(2,1)S(1)}, bf16[4,128,128]{2,1,0:T(8,128)(2,1)S(1)}, u32[]{:S(2)}, u32[]{:S(2)}) collective-permute-start(bf16[4,128,128]{2,1,0:T(8,128)(2,1)S(1)} %fusion.41), channel_id=1, source_target_pairs={{0,16},{4,20},{8,24},{12,28},{16,0},{20,4},{24,8},{28,12},{1,17},{... | collective-permute-start | bytes 393224 | tf_op jit(solution)/shard_map/ppermute | solution.py:120
  121.5 1.7 collective-permute-start.26
  123.3 2.4 %collective-permute-done.34 = bf16[2,4,128,128]{3,2,1,0:T(8,128)(2,1)S(1)} collective-permute-done((bf16[2,4,128,128]{3,2,1,0:T(8,128)(2,1)S(1)}, bf16[2,4,128,128]{3,2,1,0:T(8,128)(2,1)S(1)}, u32[]{:S(2)}, u32[]{:S(2)}) %collective-permute-start.34) | collective-permute-done | bytes 262176 | tf_op jit(solution)/shard_map/ppermute | solution.py:120
  125.7 1.4 collective-permute-start.35
  127.2 1.7 collective-permute-start.37
  128.9 1.1 collective-permute-done.24
  130.2 2.9 %collective-permute-start.27 = (bf16[8,128,128]{2,1,0:T(8,128)(2,1)S(1)}, bf16[8,128,128]{2,1,0:T(8,128)(2,1)S(1)}, u32[]{:S(2)}, u32[]{:S(2)}) collective-permute-start(bf16[8,128,128]{2,1,0:T(8,128)(2,1)S(1)} %pad_maximum_fusion.4.rest_0_), channel_id=1, source_target_pairs={{0,1},{1,2},{2,3},{4,5},{5,6},{6,7},{8,9},{9,10},{10,11},{12,13},{... | collective-permute-start | bytes 786440 | tf_op jit(solution)/shard_map/ppermute | solution.py:161
  133.1 1.3 collective-permute-start.30
  134.6 4.6 %collective-permute-start.38 = (bf16[8,128,128]{2,1,0:T(8,128)(2,1)S(1)}, bf16[8,128,128]{2,1,0:T(8,128)(2,1)S(1)}, u32[]{:S(2)}, u32[]{:S(2)}) collective-permute-start(bf16[8,128,128]{2,1,0:T(8,128)(2,1)S(1)} %pad_maximum_fusion.5.rest_0_), channel_id=1, source_target_pairs={{0,1},{1,2},{2,3},{4,5},{5,6},{6,7},{8,9},{9,10},{10,11},{12,13},{... | collective-permute-start | bytes 786440 | tf_op jit(solution)/shard_map/ppermute | solution.py:161
  139.1 1.3 collective-permute-start.41
  141.5 1.3 collective-permute-start.31
  143.7 6.2 %collective-permute-done.41.rest_4_ = bf16[8,128,128]{2,1,0:T(8,128)(2,1)S(1)} collective-permute-done((bf16[8,128,128]{2,1,0:T(8,128)(2,1)S(1)}, bf16[8,128,128]{2,1,0:T(8,128)(2,1)S(1)}, u32[]{:S(2)}, u32[]{:S(2)}) %collective-permute-start.41) | collective-permute-done | bytes 262176 | tf_op jit(solution)/shard_map/ppermute | solution.py:162
  149.9 1.3 collective-permute-start.42
  152.8 2.7 %collective-permute-done.31.rest_5_ = bf16[8,128,128]{2,1,0:T(8,128)(2,1)S(1)} collective-permute-done((bf16[8,128,128]{2,1,0:T(8,128)(2,1)S(1)}, bf16[8,128,128]{2,1,0:T(8,128)(2,1)S(1)}, u32[]{:S(2)}, u32[]{:S(2)}) %collective-permute-start.31) | collective-permute-done | bytes 262176 | tf_op jit(solution)/shard_map/ppermute | solution.py:162
  155.5 1.3 collective-permute-start.32
  157.5 3.6 %collective-permute-done.42.rest_5_ = bf16[8,128,128]{2,1,0:T(8,128)(2,1)S(1)} collective-permute-done((bf16[8,128,128]{2,1,0:T(8,128)(2,1)S(1)}, bf16[8,128,128]{2,1,0:T(8,128)(2,1)S(1)}, u32[]{:S(2)}, u32[]{:S(2)}) %collective-permute-start.42) | collective-permute-done | bytes 262176 | tf_op jit(solution)/shard_map/ppermute | solution.py:162
  161.1 1.5 collective-permute-start.43
  163.4 3.3 %collective-permute-done.32.rest_6_ = bf16[8,128,128]{2,1,0:T(8,128)(2,1)S(1)} collective-permute-done((bf16[8,128,128]{2,1,0:T(8,128)(2,1)S(1)}, bf16[8,128,128]{2,1,0:T(8,128)(2,1)S(1)}, u32[]{:S(2)}, u32[]{:S(2)}) %collective-permute-start.32) | collective-permute-done | bytes 262176 | tf_op jit(solution)/shard_map/ppermute | solution.py:162
  167.4 3.1 %shard_map.107 = (bf16[8,128,128]{2,1,0:T(8,128)(2,1)}, f32[4,128,128]{2,1,0:T(8,128)}) custom-call(s32[1]{0:T(128)} %bitcast.col_ref, bf16[128,512]{1,0:T(8,128)(2,1)} %pad_maximum_fusion.6.weight_ref, bf16[8,128,128]{2,1,0:T(8,128)(2,1)} %copy-done, bf16[8,128,128]{2,1,0:T(8,128)(2,1)} %copy-done.7, bf16[8,128,128]{2,1,0:T(8,128)(2,1)} %copy-done.12, ...), custom_call_target="tpu_custom_call" | custom-call | tf_op jit(solution)/shard_map/pallas_call | solution.py:110
  171.3 3.1 %shard_map.108 = (bf16[8,128,128]{2,1,0:T(8,128)(2,1)}, f32[4,128,128]{2,1,0:T(8,128)}) custom-call(s32[1]{0:T(128)} %bitcast.col_ref, bf16[128,512]{1,0:T(8,128)(2,1)} %pad_maximum_fusion.6.weight_ref, bf16[8,128,128]{2,1,0:T(8,128)(2,1)} %copy-done.1, bf16[8,128,128]{2,1,0:T(8,128)(2,1)} %copy-done.9, bf16[8,128,128]{2,1,0:T(8,128)(2,1)} %copy-done.11, ...), custom_call_target="tpu_custom_call" | custom-call | tf_op jit(solution)/shard_map/pallas_call | solution.py:110
  174.4 1.1 add_convert_fusion.21
  175.6 2.0 %collective-permute-start.48 = (bf16[4,128,128]{2,1,0:T(8,128)(2,1)S(1)}, bf16[4,128,128]{2,1,0:T(8,128)(2,1)S(1)}, u32[]{:S(2)}, u32[]{:S(2)}) collective-permute-start(bf16[4,128,128]{2,1,0:T(8,128)(2,1)S(1)} %add_convert_fusion.17), channel_id=1, source_target_pairs={{0,8},{4,12},{8,0},{12,4},{16,24},{20,28},{24,16},{28,20},{1,9},{5... | collective-permute-start | bytes 393224 | tf_op jit(solution)/shard_map/ppermute | solution.py:120
  177.6 1.3 collective-permute-start.45
  178.9 3.1 %collective-permute-done.48 = bf16[4,128,128]{2,1,0:T(8,128)(2,1)S(1)} collective-permute-done((bf16[4,128,128]{2,1,0:T(8,128)(2,1)S(1)}, bf16[4,128,128]{2,1,0:T(8,128)(2,1)S(1)}, u32[]{:S(2)}, u32[]{:S(2)}) %collective-permute-start.48) | collective-permute-done | bytes 131104 | tf_op jit(solution)/shard_map/ppermute | solution.py:120
  182.1 1.9 %collective-permute-start.49 = (bf16[4,128,128]{2,1,0:T(8,128)(2,1)S(1)}, bf16[4,128,128]{2,1,0:T(8,128)(2,1)S(1)}, u32[]{:S(2)}, u32[]{:S(2)}) collective-permute-start(bf16[4,128,128]{2,1,0:T(8,128)(2,1)S(1)} %add_convert_fusion.16), channel_id=1, source_target_pairs={{0,16},{4,20},{8,24},{12,28},{16,0},{20,4},{24,8},{28,12},{1,17},{... | collective-permute-start | bytes 393224 | tf_op jit(solution)/shard_map/ppermute | solution.py:120
  184.5 1.8 collective-permute-start.46
  188.0 1.9 pad_maximum_fusion.1
  (158 shorter events, 24.0 us)
Async XLA Ops:
  0.6 54.4 %copy-start.27 = (bf16[128,512]{1,0:T(8,128)(2,1)S(1)}, bf16[128,512]{1,0:T(8,128)(2,1)}, u32[]{:S(2)}) copy-start(bf16[128,512]{1,0:T(8,128)(2,1)} %param.14) | copy-start | bytes 393220
  0.6 54.4 %copy-start.28 = (bf16[128,512]{1,0:T(8,128)(2,1)S(1)}, bf16[128,512]{1,0:T(8,128)(2,1)}, u32[]{:S(2)}) copy-start(bf16[128,512]{1,0:T(8,128)(2,1)} %param.15) | copy-start | bytes 393220
  0.7 65.0 %copy-start.2 = (s32[2048,128]{1,0:T(8,128)S(1)}, s32[2048,128]{1,0:T(8,128)}, u32[]{:S(2)}) copy-start(s32[2048,128]{1,0:T(8,128)} %param.11) | copy-start | bytes 3145732
  17.4 60.7 %copy-start.5 = (bf16[2048,128]{1,0:T(8,128)(2,1)S(1)}, bf16[2048,128]{1,0:T(8,128)(2,1)}, u32[]{:S(2)}) copy-start(bf16[2048,128]{1,0:T(8,128)(2,1)} %param.9) | copy-start | bytes 1572868
  17.4 2.9 %collective-permute-start = (bf16[4,8,128,128]{3,2,1,0:T(8,128)(2,1)}, bf16[4,8,128,128]{3,2,1,0:T(8,128)(2,1)S(1)}, u32[]{:S(2)}, u32[]{:S(2)}) collective-permute-start(bf16[4,8,128,128]{3,2,1,0:T(8,128)(2,1)} %get-tuple-element.20), channel_id=1, source_target_pairs={{0,4},{4,0},{8,12},{12,8},{16,20},{20,16},{24,28},{28,24},{1,5},{5... | collective-permute-start | bytes 3145736 | tf_op jit(solution)/shard_map/ppermute | solution.py:120
  17.8 9.4 %collective-permute-start.11 = (bf16[4,8,128,128]{3,2,1,0:T(8,128)(2,1)}, bf16[4,8,128,128]{3,2,1,0:T(8,128)(2,1)S(1)}, u32[]{:S(2)}, u32[]{:S(2)}) collective-permute-start(bf16[4,8,128,128]{3,2,1,0:T(8,128)(2,1)} %get-tuple-element.23), channel_id=1, source_target_pairs={{0,4},{4,0},{8,12},{12,8},{16,20},{20,16},{24,28},{28,24},{1,5},{5... | collective-permute-start | bytes 3145736 | tf_op jit(solution)/shard_map/ppermute | solution.py:120
  21.5 9.5 %collective-permute-start.1 = (bf16[2,4,128,128]{3,2,1,0:T(8,128)(2,1)S(1)}, bf16[2,4,128,128]{3,2,1,0:T(8,128)(2,1)S(1)}, u32[]{:S(2)}, u32[]{:S(2)}) collective-permute-start(bf16[2,4,128,128]{3,2,1,0:T(8,128)(2,1)S(1)} %get-tuple-element.44), channel_id=1, source_target_pairs={{0,8},{4,12},{8,0},{12,4},{16,24},{20,28},{24,16},{28,20},{1,9},{5... | collective-permute-start | bytes 786440 | tf_op jit(solution)/shard_map/ppermute | solution.py:120
  25.6 9.3 %collective-permute-start.3 = (bf16[2,4,128,128]{3,2,1,0:T(8,128)(2,1)S(1)}, bf16[2,4,128,128]{3,2,1,0:T(8,128)(2,1)S(1)}, u32[]{:S(2)}, u32[]{:S(2)}) collective-permute-start(bf16[2,4,128,128]{3,2,1,0:T(8,128)(2,1)S(1)} %get-tuple-element.46), channel_id=1, source_target_pairs={{0,16},{4,20},{8,24},{12,28},{16,0},{20,4},{24,8},{28,12},{1,17},{... | collective-permute-start | bytes 786440 | tf_op jit(solution)/shard_map/ppermute | solution.py:120
  29.6 9.3 %collective-permute-start.12 = (bf16[2,4,128,128]{3,2,1,0:T(8,128)(2,1)S(1)}, bf16[2,4,128,128]{3,2,1,0:T(8,128)(2,1)S(1)}, u32[]{:S(2)}, u32[]{:S(2)}) collective-permute-start(bf16[2,4,128,128]{3,2,1,0:T(8,128)(2,1)S(1)} %get-tuple-element.48), channel_id=1, source_target_pairs={{0,8},{4,12},{8,0},{12,4},{16,24},{20,28},{24,16},{28,20},{1,9},{5... | collective-permute-start | bytes 786440 | tf_op jit(solution)/shard_map/ppermute | solution.py:120
  30.2 10.3 %collective-permute-start.14 = (bf16[2,4,128,128]{3,2,1,0:T(8,128)(2,1)S(1)}, bf16[2,4,128,128]{3,2,1,0:T(8,128)(2,1)S(1)}, u32[]{:S(2)}, u32[]{:S(2)}) collective-permute-start(bf16[2,4,128,128]{3,2,1,0:T(8,128)(2,1)S(1)} %get-tuple-element.50), channel_id=1, source_target_pairs={{0,16},{4,20},{8,24},{12,28},{16,0},{20,4},{24,8},{28,12},{1,17},{... | collective-permute-start | bytes 786440 | tf_op jit(solution)/shard_map/ppermute | solution.py:120
  31.1 12.2 %collective-permute-start.2 = (bf16[4,128,128]{2,1,0:T(8,128)(2,1)S(1)}, bf16[4,128,128]{2,1,0:T(8,128)(2,1)S(1)}, u32[]{:S(2)}, u32[]{:S(2)}) collective-permute-start(bf16[4,128,128]{2,1,0:T(8,128)(2,1)S(1)} %fusion.33), channel_id=1, source_target_pairs={{0,16},{4,20},{8,24},{12,28},{16,0},{20,4},{24,8},{28,12},{1,17},{... | collective-permute-start | bytes 393224 | tf_op jit(solution)/shard_map/ppermute | solution.py:120
  34.9 8.4 %collective-permute-start.4 = (bf16[4,128,128]{2,1,0:T(8,128)(2,1)S(1)}, bf16[4,128,128]{2,1,0:T(8,128)(2,1)S(1)}, u32[]{:S(2)}, u32[]{:S(2)}) collective-permute-start(bf16[4,128,128]{2,1,0:T(8,128)(2,1)S(1)} %fusion.35), channel_id=1, source_target_pairs={{0,8},{4,12},{8,0},{12,4},{16,24},{20,28},{24,16},{28,20},{1,9},{5... | collective-permute-start | bytes 393224 | tf_op jit(solution)/shard_map/ppermute | solution.py:120
  38.9 10.5 %collective-permute-start.13 = (bf16[4,128,128]{2,1,0:T(8,128)(2,1)S(1)}, bf16[4,128,128]{2,1,0:T(8,128)(2,1)S(1)}, u32[]{:S(2)}, u32[]{:S(2)}) collective-permute-start(bf16[4,128,128]{2,1,0:T(8,128)(2,1)S(1)} %fusion.37), channel_id=1, source_target_pairs={{0,16},{4,20},{8,24},{12,28},{16,0},{20,4},{24,8},{28,12},{1,17},{... | collective-permute-start | bytes 393224 | tf_op jit(solution)/shard_map/ppermute | solution.py:120
  40.5 8.9 %collective-permute-start.15 = (bf16[4,128,128]{2,1,0:T(8,128)(2,1)S(1)}, bf16[4,128,128]{2,1,0:T(8,128)(2,1)S(1)}, u32[]{:S(2)}, u32[]{:S(2)}) collective-permute-start(bf16[4,128,128]{2,1,0:T(8,128)(2,1)S(1)} %fusion.39), channel_id=1, source_target_pairs={{0,8},{4,12},{8,0},{12,4},{16,24},{20,28},{24,16},{28,20},{1,9},{5... | collective-permute-start | bytes 393224 | tf_op jit(solution)/shard_map/ppermute | solution.py:120
  43.5 37.2 %copy-start.3 = (bf16[8,128,128]{2,1,0:T(8,128)(2,1)}, bf16[8,128,128]{2,1,0:T(8,128)(2,1)S(1)}, u32[]{:S(2)}) copy-start(bf16[8,128,128]{2,1,0:T(8,128)(2,1)S(1)} %pad_maximum_fusion.2.rest_0_) | copy-start | bytes 786436
  43.5 11.7 %collective-permute-start.8 = (bf16[8,128,128]{2,1,0:T(8,128)(2,1)S(1)}, bf16[8,128,128]{2,1,0:T(8,128)(2,1)S(1)}, u32[]{:S(2)}, u32[]{:S(2)}) collective-permute-start(bf16[8,128,128]{2,1,0:T(8,128)(2,1)S(1)} %pad_maximum_fusion.2.rest_0_), channel_id=1, source_target_pairs={{1,0},{2,1},{3,2},{5,4},{6,5},{7,6},{9,8},{10,9},{11,10},{13,12},{... | collective-permute-start | bytes 786440 | tf_op jit(solution)/shard_map/ppermute | solution.py:162
  44.8 11.7 %collective-permute-start.5 = (bf16[8,128,128]{2,1,0:T(8,128)(2,1)S(1)}, bf16[8,128,128]{2,1,0:T(8,128)(2,1)S(1)}, u32[]{:S(2)}, u32[]{:S(2)}) collective-permute-start(bf16[8,128,128]{2,1,0:T(8,128)(2,1)S(1)} %pad_maximum_fusion.2.rest_0_), channel_id=1, source_target_pairs={{0,1},{1,2},{2,3},{4,5},{5,6},{6,7},{8,9},{9,10},{10,11},{12,13},{... | collective-permute-start | bytes 786440 | tf_op jit(solution)/shard_map/ppermute | solution.py:161
  49.5 35.1 %copy-start.4 = (bf16[8,128,128]{2,1,0:T(8,128)(2,1)}, bf16[8,128,128]{2,1,0:T(8,128)(2,1)S(1)}, u32[]{:S(2)}) copy-start(bf16[8,128,128]{2,1,0:T(8,128)(2,1)S(1)} %pad_maximum_fusion.3.rest_0_) | copy-start | bytes 786436
  49.5 9.3 %collective-permute-start.16 = (bf16[8,128,128]{2,1,0:T(8,128)(2,1)S(1)}, bf16[8,128,128]{2,1,0:T(8,128)(2,1)}, u32[]{:S(2)}, u32[]{:S(2)}) collective-permute-start(bf16[8,128,128]{2,1,0:T(8,128)(2,1)S(1)} %pad_maximum_fusion.3.rest_0_), channel_id=1, source_target_pairs={{0,1},{1,2},{2,3},{4,5},{5,6},{6,7},{8,9},{9,10},{10,11},{12,13},{... | collective-permute-start | bytes 786440 | tf_op jit(solution)/shard_map/ppermute | solution.py:161
  53.7 10.0 %collective-permute-start.19 = (bf16[8,128,128]{2,1,0:T(8,128)(2,1)S(1)}, bf16[8,128,128]{2,1,0:T(8,128)(2,1)}, u32[]{:S(2)}, u32[]{:S(2)}) collective-permute-start(bf16[8,128,128]{2,1,0:T(8,128)(2,1)S(1)} %pad_maximum_fusion.3.rest_0_), channel_id=1, source_target_pairs={{1,0},{2,1},{3,2},{5,4},{6,5},{7,6},{9,8},{10,9},{11,10},{13,12},{... | collective-permute-start | bytes 786440 | tf_op jit(solution)/shard_map/ppermute | solution.py:162
  55.1 25.5 %copy-start.21 = (bf16[8,128,128]{2,1,0:T(8,128)(2,1)}, bf16[8,128,128]{2,1,0:T(8,128)(2,1)S(1)}, u32[]{:S(2)}) copy-start(bf16[8,128,128]{2,1,0:T(8,128)(2,1)S(1)} %collective-permute-done.8.rest_4_) | copy-start | bytes 786436
  55.2 11.7 %collective-permute-start.9 = (bf16[8,128,128]{2,1,0:T(8,128)(2,1)S(1)}, bf16[8,128,128]{2,1,0:T(8,128)(2,1)}, u32[]{:S(2)}, u32[]{:S(2)}) collective-permute-start(bf16[8,128,128]{2,1,0:T(8,128)(2,1)S(1)} %collective-permute-done.8.rest_4_), channel_id=1, source_target_pairs={{1,0},{2,1},{5,4},{6,5},{9,8},{10,9},{13,12},{14,13},{17,16},{18,1... | collective-permute-start | bytes 786440 | tf_op jit(solution)/shard_map/ppermute | solution.py:162
  56.5 11.7 %collective-permute-start.6 = (bf16[8,128,128]{2,1,0:T(8,128)(2,1)S(1)}, bf16[8,128,128]{2,1,0:T(8,128)(2,1)}, u32[]{:S(2)}, u32[]{:S(2)}) collective-permute-start(bf16[8,128,128]{2,1,0:T(8,128)(2,1)S(1)} %collective-permute-done.5.rest_1_), channel_id=1, source_target_pairs={{1,2},{2,3},{5,6},{6,7},{9,10},{10,11},{13,14},{14,15},{17,18},{18... | collective-permute-start | bytes 786440 | tf_op jit(solution)/shard_map/ppermute | solution.py:161
  58.8 10.1 %collective-permute-start.17 = (bf16[8,128,128]{2,1,0:T(8,128)(2,1)}, bf16[8,128,128]{2,1,0:T(8,128)(2,1)}, u32[]{:S(2)}, u32[]{:S(2)}) collective-permute-start(bf16[8,128,128]{2,1,0:T(8,128)(2,1)} %collective-permute-done.16.rest_1_), channel_id=1, source_target_pairs={{1,2},{2,3},{5,6},{6,7},{9,10},{10,11},{13,14},{14,15},{17,18},{18... | collective-permute-start | bytes 786440 | tf_op jit(solution)/shard_map/ppermute | solution.py:161
  63.8 12.4 %collective-permute-start.20 = (bf16[8,128,128]{2,1,0:T(8,128)(2,1)}, bf16[8,128,128]{2,1,0:T(8,128)(2,1)}, u32[]{:S(2)}, u32[]{:S(2)}) collective-permute-start(bf16[8,128,128]{2,1,0:T(8,128)(2,1)} %collective-permute-done.19.rest_4_), channel_id=1, source_target_pairs={{1,0},{2,1},{5,4},{6,5},{9,8},{10,9},{13,12},{14,13},{17,16},{18,1... | collective-permute-start | bytes 786440 | tf_op jit(solution)/shard_map/ppermute | solution.py:162
  66.9 13.7 %collective-permute-start.10 = (bf16[8,128,128]{2,1,0:T(8,128)(2,1)}, bf16[8,128,128]{2,1,0:T(8,128)(2,1)S(1)}, u32[]{:S(2)}, u32[]{:S(2)}) collective-permute-start(bf16[8,128,128]{2,1,0:T(8,128)(2,1)} %collective-permute-done.9.rest_5_), channel_id=1, source_target_pairs={{1,0},{5,4},{9,8},{13,12},{17,16},{21,20},{25,24},{29,28}} | collective-permute-start | bytes 786440 | tf_op jit(solution)/shard_map/ppermute | solution.py:162
  68.2 12.4 %collective-permute-start.7 = (bf16[8,128,128]{2,1,0:T(8,128)(2,1)}, bf16[8,128,128]{2,1,0:T(8,128)(2,1)S(1)}, u32[]{:S(2)}, u32[]{:S(2)}) collective-permute-start(bf16[8,128,128]{2,1,0:T(8,128)(2,1)} %collective-permute-done.6.rest_2_), channel_id=1, source_target_pairs={{2,3},{6,7},{10,11},{14,15},{18,19},{22,23},{26,27},{30,31}} | collective-permute-start | bytes 786440 | tf_op jit(solution)/shard_map/ppermute | solution.py:161
  68.9 15.7 %collective-permute-start.18 = (bf16[8,128,128]{2,1,0:T(8,128)(2,1)}, bf16[8,128,128]{2,1,0:T(8,128)(2,1)S(1)}, u32[]{:S(2)}, u32[]{:S(2)}) collective-permute-start(bf16[8,128,128]{2,1,0:T(8,128)(2,1)} %collective-permute-done.17.rest_2_), channel_id=1, source_target_pairs={{2,3},{6,7},{10,11},{14,15},{18,19},{22,23},{26,27},{30,31}} | collective-permute-start | bytes 786440 | tf_op jit(solution)/shard_map/ppermute | solution.py:161
  76.1 8.5 %collective-permute-start.21 = (bf16[8,128,128]{2,1,0:T(8,128)(2,1)}, bf16[8,128,128]{2,1,0:T(8,128)(2,1)S(1)}, u32[]{:S(2)}, u32[]{:S(2)}) collective-permute-start(bf16[8,128,128]{2,1,0:T(8,128)(2,1)} %collective-permute-done.20.rest_5_), channel_id=1, source_target_pairs={{1,0},{5,4},{9,8},{13,12},{17,16},{21,20},{25,24},{29,28}} | collective-permute-start | bytes 786440 | tf_op jit(solution)/shard_map/ppermute | solution.py:162
  90.4 60.9 %copy-start.6 = (bf16[2048,128]{1,0:T(8,128)(2,1)S(1)}, bf16[2048,128]{1,0:T(8,128)(2,1)}, u32[]{:S(2)}) copy-start(bf16[2048,128]{1,0:T(8,128)(2,1)} %param.8) | copy-start | bytes 1572868
  90.4 72.9 %copy-start.19 = (f32[4,128,128]{2,1,0:T(8,128)S(1)}, f32[4,128,128]{2,1,0:T(8,128)}, u32[]{:S(2)}) copy-start(f32[4,128,128]{2,1,0:T(8,128)} %get-tuple-element.33) | copy-start | bytes 786436
  90.4 72.9 %copy-start.20 = (f32[4,128,128]{2,1,0:T(8,128)S(1)}, f32[4,128,128]{2,1,0:T(8,128)}, u32[]{:S(2)}) copy-start(f32[4,128,128]{2,1,0:T(8,128)} %get-tuple-element.34) | copy-start | bytes 786436
  106.6 2.9 %collective-permute-start.22 = (bf16[4,8,128,128]{3,2,1,0:T(8,128)(2,1)}, bf16[4,8,128,128]{3,2,1,0:T(8,128)(2,1)S(1)}, u32[]{:S(2)}, u32[]{:S(2)}) collective-permute-start(bf16[4,8,128,128]{3,2,1,0:T(8,128)(2,1)} %get-tuple-element.26), channel_id=1, source_target_pairs={{0,4},{4,0},{8,12},{12,8},{16,20},{20,16},{24,28},{28,24},{1,5},{5... | collective-permute-start | bytes 3145736 | tf_op jit(solution)/shard_map/ppermute | solution.py:120
  106.6 7.4 %collective-permute-start.33 = (bf16[4,8,128,128]{3,2,1,0:T(8,128)(2,1)}, bf16[4,8,128,128]{3,2,1,0:T(8,128)(2,1)S(1)}, u32[]{:S(2)}, u32[]{:S(2)}) collective-permute-start(bf16[4,8,128,128]{3,2,1,0:T(8,128)(2,1)} %get-tuple-element.29), channel_id=1, source_target_pairs={{0,4},{4,0},{8,12},{12,8},{16,20},{20,16},{24,28},{28,24},{1,5},{5... | collective-permute-start | bytes 3145736 | tf_op jit(solution)/shard_map/ppermute | solution.py:120
  110.7 8.8 %collective-permute-start.23 = (bf16[2,4,128,128]{3,2,1,0:T(8,128)(2,1)S(1)}, bf16[2,4,128,128]{3,2,1,0:T(8,128)(2,1)S(1)}, u32[]{:S(2)}, u32[]{:S(2)}) collective-permute-start(bf16[2,4,128,128]{3,2,1,0:T(8,128)(2,1)S(1)} %get-tuple-element.36), channel_id=1, source_target_pairs={{0,8},{4,12},{8,0},{12,4},{16,24},{20,28},{24,16},{28,20},{1,9},{5... | collective-permute-start | bytes 786440 | tf_op jit(solution)/shard_map/ppermute | solution.py:120
  112.6 9.0 %collective-permute-start.25 = (bf16[2,4,128,128]{3,2,1,0:T(8,128)(2,1)S(1)}, bf16[2,4,128,128]{3,2,1,0:T(8,128)(2,1)S(1)}, u32[]{:S(2)}, u32[]{:S(2)}) collective-permute-start(bf16[2,4,128,128]{3,2,1,0:T(8,128)(2,1)S(1)} %get-tuple-element.38), channel_id=1, source_target_pairs={{0,16},{4,20},{8,24},{12,28},{16,0},{20,4},{24,8},{28,12},{1,17},{... | collective-permute-start | bytes 786440 | tf_op jit(solution)/shard_map/ppermute | solution.py:120
  116.4 9.3 %collective-permute-start.34 = (bf16[2,4,128,128]{3,2,1,0:T(8,128)(2,1)S(1)}, bf16[2,4,128,128]{3,2,1,0:T(8,128)(2,1)S(1)}, u32[]{:S(2)}, u32[]{:S(2)}) collective-permute-start(bf16[2,4,128,128]{3,2,1,0:T(8,128)(2,1)S(1)} %get-tuple-element.40), channel_id=1, source_target_pairs={{0,8},{4,12},{8,0},{12,4},{16,24},{20,28},{24,16},{28,20},{1,9},{5... | collective-permute-start | bytes 786440 | tf_op jit(solution)/shard_map/ppermute | solution.py:120
  117.9 9.2 %collective-permute-start.36 = (bf16[2,4,128,128]{3,2,1,0:T(8,128)(2,1)S(1)}, bf16[2,4,128,128]{3,2,1,0:T(8,128)(2,1)S(1)}, u32[]{:S(2)}, u32[]{:S(2)}) collective-permute-start(bf16[2,4,128,128]{3,2,1,0:T(8,128)(2,1)S(1)} %get-tuple-element.42), channel_id=1, source_target_pairs={{0,16},{4,20},{8,24},{12,28},{16,0},{20,4},{24,8},{28,12},{1,17},{... | collective-permute-start | bytes 786440 | tf_op jit(solution)/shard_map/ppermute | solution.py:120
  119.5 10.5 %collective-permute-start.24 = (bf16[4,128,128]{2,1,0:T(8,128)(2,1)S(1)}, bf16[4,128,128]{2,1,0:T(8,128)(2,1)S(1)}, u32[]{:S(2)}, u32[]{:S(2)}) collective-permute-start(bf16[4,128,128]{2,1,0:T(8,128)(2,1)S(1)} %fusion.41), channel_id=1, source_target_pairs={{0,16},{4,20},{8,24},{12,28},{16,0},{20,4},{24,8},{28,12},{1,17},{... | collective-permute-start | bytes 393224 | tf_op jit(solution)/shard_map/ppermute | solution.py:120
  121.5 8.5 %collective-permute-start.26 = (bf16[4,128,128]{2,1,0:T(8,128)(2,1)S(1)}, bf16[4,128,128]{2,1,0:T(8,128)(2,1)S(1)}, u32[]{:S(2)}, u32[]{:S(2)}) collective-permute-start(bf16[4,128,128]{2,1,0:T(8,128)(2,1)S(1)} %fusion.43), channel_id=1, source_target_pairs={{0,8},{4,12},{8,0},{12,4},{16,24},{20,28},{24,16},{28,20},{1,9},{5... | collective-permute-start | bytes 393224 | tf_op jit(solution)/shard_map/ppermute | solution.py:120
  125.7 8.6 %collective-permute-start.35 = (bf16[4,128,128]{2,1,0:T(8,128)(2,1)S(1)}, bf16[4,128,128]{2,1,0:T(8,128)(2,1)S(1)}, u32[]{:S(2)}, u32[]{:S(2)}) collective-permute-start(bf16[4,128,128]{2,1,0:T(8,128)(2,1)S(1)} %fusion.45), channel_id=1, source_target_pairs={{0,16},{4,20},{8,24},{12,28},{16,0},{20,4},{24,8},{28,12},{1,17},{... | collective-permute-start | bytes 393224 | tf_op jit(solution)/shard_map/ppermute | solution.py:120
  127.2 7.2 %collective-permute-start.37 = (bf16[4,128,128]{2,1,0:T(8,128)(2,1)S(1)}, bf16[4,128,128]{2,1,0:T(8,128)(2,1)S(1)}, u32[]{:S(2)}, u32[]{:S(2)}) collective-permute-start(bf16[4,128,128]{2,1,0:T(8,128)(2,1)S(1)} %fusion.47), channel_id=1, source_target_pairs={{0,8},{4,12},{8,0},{12,4},{16,24},{20,28},{24,16},{28,20},{1,9},{5... | collective-permute-start | bytes 393224 | tf_op jit(solution)/shard_map/ppermute | solution.py:120
  130.2 36.6 %copy-start = (bf16[8,128,128]{2,1,0:T(8,128)(2,1)}, bf16[8,128,128]{2,1,0:T(8,128)(2,1)S(1)}, u32[]{:S(2)}) copy-start(bf16[8,128,128]{2,1,0:T(8,128)(2,1)S(1)} %pad_maximum_fusion.4.rest_0_) | copy-start | bytes 786436
  130.2 10.3 %collective-permute-start.27 = (bf16[8,128,128]{2,1,0:T(8,128)(2,1)S(1)}, bf16[8,128,128]{2,1,0:T(8,128)(2,1)S(1)}, u32[]{:S(2)}, u32[]{:S(2)}) collective-permute-start(bf16[8,128,128]{2,1,0:T(8,128)(2,1)S(1)} %pad_maximum_fusion.4.rest_0_), channel_id=1, source_target_pairs={{0,1},{1,2},{2,3},{4,5},{5,6},{6,7},{8,9},{9,10},{10,11},{12,13},{... | collective-permute-start | bytes 786440 | tf_op jit(solution)/shard_map/ppermute | solution.py:161
  133.1 8.4 %collective-permute-start.30 = (bf16[8,128,128]{2,1,0:T(8,128)(2,1)S(1)}, bf16[8,128,128]{2,1,0:T(8,128)(2,1)S(1)}, u32[]{:S(2)}, u32[]{:S(2)}) collective-permute-start(bf16[8,128,128]{2,1,0:T(8,128)(2,1)S(1)} %pad_maximum_fusion.4.rest_0_), channel_id=1, source_target_pairs={{1,0},{2,1},{3,2},{5,4},{6,5},{7,6},{9,8},{10,9},{11,10},{13,12},{... | collective-permute-start | bytes 786440 | tf_op jit(solution)/shard_map/ppermute | solution.py:162
  134.6 36.0 %copy-start.1 = (bf16[8,128,128]{2,1,0:T(8,128)(2,1)}, bf16[8,128,128]{2,1,0:T(8,128)(2,1)S(1)}, u32[]{:S(2)}) copy-start(bf16[8,128,128]{2,1,0:T(8,128)(2,1)S(1)} %pad_maximum_fusion.5.rest_0_) | copy-start | bytes 786436
  134.6 8.4 %collective-permute-start.38 = (bf16[8,128,128]{2,1,0:T(8,128)(2,1)S(1)}, bf16[8,128,128]{2,1,0:T(8,128)(2,1)S(1)}, u32[]{:S(2)}, u32[]{:S(2)}) collective-permute-start(bf16[8,128,128]{2,1,0:T(8,128)(2,1)S(1)} %pad_maximum_fusion.5.rest_0_), channel_id=1, source_target_pairs={{0,1},{1,2},{2,3},{4,5},{5,6},{6,7},{8,9},{9,10},{10,11},{12,13},{... | collective-permute-start | bytes 786440 | tf_op jit(solution)/shard_map/ppermute | solution.py:161
  139.1 10.7 %collective-permute-start.41 = (bf16[8,128,128]{2,1,0:T(8,128)(2,1)S(1)}, bf16[8,128,128]{2,1,0:T(8,128)(2,1)S(1)}, u32[]{:S(2)}, u32[]{:S(2)}) collective-permute-start(bf16[8,128,128]{2,1,0:T(8,128)(2,1)S(1)} %pad_maximum_fusion.5.rest_0_), channel_id=1, source_target_pairs={{1,0},{2,1},{3,2},{5,4},{6,5},{7,6},{9,8},{10,9},{11,10},{13,12},{... | collective-permute-start | bytes 786440 | tf_op jit(solution)/shard_map/ppermute | solution.py:162
  140.5 26.3 %copy-start.7 = (bf16[8,128,128]{2,1,0:T(8,128)(2,1)}, bf16[8,128,128]{2,1,0:T(8,128)(2,1)S(1)}, u32[]{:S(2)}) copy-start(bf16[8,128,128]{2,1,0:T(8,128)(2,1)S(1)} %collective-permute-done.27.rest_1_) | copy-start | bytes 786436
  140.5 11.6 %collective-permute-start.28 = (bf16[8,128,128]{2,1,0:T(8,128)(2,1)S(1)}, bf16[8,128,128]{2,1,0:T(8,128)(2,1)S(1)}, u32[]{:S(2)}, u32[]{:S(2)}) collective-permute-start(bf16[8,128,128]{2,1,0:T(8,128)(2,1)S(1)} %collective-permute-done.27.rest_1_), channel_id=1, source_target_pairs={{1,2},{2,3},{5,6},{6,7},{9,10},{10,11},{13,14},{14,15},{17,18},{18... | collective-permute-start | bytes 786440 | tf_op jit(solution)/shard_map/ppermute | solution.py:161
  141.5 14.0 %collective-permute-start.31 = (bf16[8,128,128]{2,1,0:T(8,128)(2,1)S(1)}, bf16[8,128,128]{2,1,0:T(8,128)(2,1)S(1)}, u32[]{:S(2)}, u32[]{:S(2)}) collective-permute-start(bf16[8,128,128]{2,1,0:T(8,128)(2,1)S(1)} %collective-permute-done.30.rest_4_), channel_id=1, source_target_pairs={{1,0},{2,1},{5,4},{6,5},{9,8},{10,9},{13,12},{14,13},{17,16},{18,1... | collective-permute-start | bytes 786440 | tf_op jit(solution)/shard_map/ppermute | solution.py:162
  143.0 27.6 %copy-start.9 = (bf16[8,128,128]{2,1,0:T(8,128)(2,1)}, bf16[8,128,128]{2,1,0:T(8,128)(2,1)S(1)}, u32[]{:S(2)}) copy-start(bf16[8,128,128]{2,1,0:T(8,128)(2,1)S(1)} %collective-permute-done.38.rest_1_) | copy-start | bytes 786436
  143.0 13.8 %collective-permute-start.39 = (bf16[8,128,128]{2,1,0:T(8,128)(2,1)S(1)}, bf16[8,128,128]{2,1,0:T(8,128)(2,1)S(1)}, u32[]{:S(2)}, u32[]{:S(2)}) collective-permute-start(bf16[8,128,128]{2,1,0:T(8,128)(2,1)S(1)} %collective-permute-done.38.rest_1_), channel_id=1, source_target_pairs={{1,2},{2,3},{5,6},{6,7},{9,10},{10,11},{13,14},{14,15},{17,18},{18... | collective-permute-start | bytes 786440 | tf_op jit(solution)/shard_map/ppermute | solution.py:161
  149.9 11.2 %collective-permute-start.42 = (bf16[8,128,128]{2,1,0:T(8,128)(2,1)S(1)}, bf16[8,128,128]{2,1,0:T(8,128)(2,1)S(1)}, u32[]{:S(2)}, u32[]{:S(2)}) collective-permute-start(bf16[8,128,128]{2,1,0:T(8,128)(2,1)S(1)} %collective-permute-done.41.rest_4_), channel_id=1, source_target_pairs={{1,0},{2,1},{5,4},{6,5},{9,8},{10,9},{13,12},{14,13},{17,16},{18,1... | collective-permute-start | bytes 786440 | tf_op jit(solution)/shard_map/ppermute | solution.py:162
  152.1 11.3 %collective-permute-start.29 = (bf16[8,128,128]{2,1,0:T(8,128)(2,1)S(1)}, bf16[8,128,128]{2,1,0:T(8,128)(2,1)S(1)}, u32[]{:S(2)}, u32[]{:S(2)}) collective-permute-start(bf16[8,128,128]{2,1,0:T(8,128)(2,1)S(1)} %collective-permute-done.28.rest_2_), channel_id=1, source_target_pairs={{2,3},{6,7},{10,11},{14,15},{18,19},{22,23},{26,27},{30,31}} | collective-permute-start | bytes 786440 | tf_op jit(solution)/shard_map/ppermute | solution.py:161
  155.5 11.2 %collective-permute-start.32 = (bf16[8,128,128]{2,1,0:T(8,128)(2,1)S(1)}, bf16[8,128,128]{2,1,0:T(8,128)(2,1)S(1)}, u32[]{:S(2)}, u32[]{:S(2)}) collective-permute-start(bf16[8,128,128]{2,1,0:T(8,128)(2,1)S(1)} %collective-permute-done.31.rest_5_), channel_id=1, source_target_pairs={{1,0},{5,4},{9,8},{13,12},{17,16},{21,20},{25,24},{29,28}} | collective-permute-start | bytes 786440 | tf_op jit(solution)/shard_map/ppermute | solution.py:162
  156.8 13.7 %collective-permute-start.40 = (bf16[8,128,128]{2,1,0:T(8,128)(2,1)S(1)}, bf16[8,128,128]{2,1,0:T(8,128)(2,1)S(1)}, u32[]{:S(2)}, u32[]{:S(2)}) collective-permute-start(bf16[8,128,128]{2,1,0:T(8,128)(2,1)S(1)} %collective-permute-done.39.rest_2_), channel_id=1, source_target_pairs={{2,3},{6,7},{10,11},{14,15},{18,19},{22,23},{26,27},{30,31}} | collective-permute-start | bytes 786440 | tf_op jit(solution)/shard_map/ppermute | solution.py:161
  161.1 9.4 %collective-permute-start.43 = (bf16[8,128,128]{2,1,0:T(8,128)(2,1)S(1)}, bf16[8,128,128]{2,1,0:T(8,128)(2,1)S(1)}, u32[]{:S(2)}, u32[]{:S(2)}) collective-permute-start(bf16[8,128,128]{2,1,0:T(8,128)(2,1)S(1)} %collective-permute-done.42.rest_5_), channel_id=1, source_target_pairs={{1,0},{5,4},{9,8},{13,12},{17,16},{21,20},{25,24},{29,28}} | collective-permute-start | bytes 786440 | tf_op jit(solution)/shard_map/ppermute | solution.py:162
  163.3 12.2 %collective-permute-start.47 = (bf16[4,128,128]{2,1,0:T(8,128)(2,1)S(1)}, bf16[4,128,128]{2,1,0:T(8,128)(2,1)S(1)}, u32[]{:S(2)}, u32[]{:S(2)}) collective-permute-start(bf16[4,128,128]{2,1,0:T(8,128)(2,1)S(1)} %add_convert_fusion.18), channel_id=1, source_target_pairs={{0,4},{4,0},{8,12},{12,8},{16,20},{20,16},{24,28},{28,24},{1,5},{5... | collective-permute-start | bytes 393224 | tf_op jit(solution)/shard_map/ppermute | solution.py:120
  175.4 2.1 %collective-permute-start.44 = (bf16[4,128,128]{2,1,0:T(8,128)(2,1)S(1)}, bf16[4,128,128]{2,1,0:T(8,128)(2,1)S(1)}, u32[]{:S(2)}, u32[]{:S(2)}) collective-permute-start(bf16[4,128,128]{2,1,0:T(8,128)(2,1)S(1)} %add_convert_fusion.21), channel_id=1, source_target_pairs={{0,4},{4,0},{8,12},{12,8},{16,20},{20,16},{24,28},{28,24},{1,5},{5... | collective-permute-start | bytes 393224 | tf_op jit(solution)/shard_map/ppermute | solution.py:120
  175.6 6.4 %collective-permute-start.48 = (bf16[4,128,128]{2,1,0:T(8,128)(2,1)S(1)}, bf16[4,128,128]{2,1,0:T(8,128)(2,1)S(1)}, u32[]{:S(2)}, u32[]{:S(2)}) collective-permute-start(bf16[4,128,128]{2,1,0:T(8,128)(2,1)S(1)} %add_convert_fusion.17), channel_id=1, source_target_pairs={{0,8},{4,12},{8,0},{12,4},{16,24},{20,28},{24,16},{28,20},{1,9},{5... | collective-permute-start | bytes 393224 | tf_op jit(solution)/shard_map/ppermute | solution.py:120
  177.6 6.9 %collective-permute-start.45 = (bf16[4,128,128]{2,1,0:T(8,128)(2,1)S(1)}, bf16[4,128,128]{2,1,0:T(8,128)(2,1)S(1)}, u32[]{:S(2)}, u32[]{:S(2)}) collective-permute-start(bf16[4,128,128]{2,1,0:T(8,128)(2,1)S(1)} %add_convert_fusion.20), channel_id=1, source_target_pairs={{0,8},{4,12},{8,0},{12,4},{16,24},{20,28},{24,16},{28,20},{1,9},{5... | collective-permute-start | bytes 393224 | tf_op jit(solution)/shard_map/ppermute | solution.py:120
  182.1 5.1 %collective-permute-start.49 = (bf16[4,128,128]{2,1,0:T(8,128)(2,1)S(1)}, bf16[4,128,128]{2,1,0:T(8,128)(2,1)S(1)}, u32[]{:S(2)}, u32[]{:S(2)}) collective-permute-start(bf16[4,128,128]{2,1,0:T(8,128)(2,1)S(1)} %add_convert_fusion.16), channel_id=1, source_target_pairs={{0,16},{4,20},{8,24},{12,28},{16,0},{20,4},{24,8},{28,12},{1,17},{... | collective-permute-start | bytes 393224 | tf_op jit(solution)/shard_map/ppermute | solution.py:120
  184.5 5.4 %collective-permute-start.46 = (bf16[4,128,128]{2,1,0:T(8,128)(2,1)S(1)}, bf16[4,128,128]{2,1,0:T(8,128)(2,1)S(1)}, u32[]{:S(2)}, u32[]{:S(2)}) collective-permute-start(bf16[4,128,128]{2,1,0:T(8,128)(2,1)S(1)} %add_convert_fusion.19), channel_id=1, source_target_pairs={{0,16},{4,20},{8,24},{12,28},{16,0},{20,4},{24,8},{28,12},{1,17},{... | collective-permute-start | bytes 393224 | tf_op jit(solution)/shard_map/ppermute | solution.py:120
  (15 other events, 127.8 us)

commit v2 on v0

v2 whole, which is shorter than its diff:
```python
import functools

import jax
import jax.numpy as jnp
from jax import lax
from jax.experimental import pallas as pl
from jax.experimental.pallas import tpu as pltpu
from jax.sharding import PartitionSpec as P

VMEM_LIMIT = 48 * 1024 * 1024
CHUNKS = 2
COPIES = 4
F32 = jnp.float32
BF16 = jnp.bfloat16
VMEM = pl.BlockSpec(memory_space=pltpu.VMEM)
SMEM = pl.BlockSpec(memory_space=pltpu.SMEM)
PARAMS = pltpu.CompilerParams(vmem_limit_bytes=VMEM_LIMIT)


def tile_copy(tiles_ref, held, sems, i):
    per = held.shape[0] // COPIES
    part = pl.ds(i * per, per)
    return pltpu.make_async_copy(tiles_ref.at[part], held.at[part], sems.at[i])


def over_rows(tiles_ref, held, sems, one_row):
    per = held.shape[0] // COPIES

    def piece(i, carry):
        tile_copy(tiles_ref, held, sems, i).wait()
        for j in range(per):
            one_row(i * per + j)
        return carry

    lax.fori_loop(0, COPIES, piece, 0)


def spread_kernel(flip, pieces, cols_ref, at_ref, tiles_ref, *rest):
    vals, rest = rest[:pieces], rest[pieces:]
    outs, (acc, held, left_ref, sems) = rest[: 2 * CHUNKS], rest[2 * CHUNKS :]
    for i in range(COPIES):
        tile_copy(tiles_ref, held, sems, i).start()
    acc[...] = jnp.zeros_like(acc)
    per_row, size = held.shape[1], held.shape[3]
    me, col = at_ref[0], at_ref[1]
    if not flip:
        count = vals[0].shape[0]
        for m in range(pieces):
            left_ref[pl.ds(jnp.bitwise_xor(col, m) * count, count)] = vals[m][...]

    def one_row(r):
        left = vals[0][r].astype(F32).T.astype(BF16) if flip else left_ref[r]
        for k in range(0, per_row, 2):
            pair = jnp.concatenate([held[r, k], held[r, k + 1]], axis=1)
            both = jnp.dot(left, pair, preferred_element_type=F32)
            for side in range(2):
                acc[cols_ref[r, k + side]] += both[:, side * size : (side + 1) * size]

    over_rows(tiles_ref, held, sems, one_row)
    halves, count = outs[0].shape[:2]
    for g in range(CHUNKS):
        for side in range(2):
            for rel in range(halves):
                owner = jnp.bitwise_xor(me, 2 * rel + side)
                first = (owner * CHUNKS + g) * count
                outs[2 * g + side][rel] = acc[pl.ds(first, count)].astype(BF16)


def spread(edge_tiles, block_cols, vals, at, rows, flip):
    blocks, _, size, _ = edge_tiles.shape
    feat = vals[0].shape[2] if flip else vals[0].shape[1]
    out = jax.ShapeDtypeStruct((rows // 2, blocks // CHUNKS, feat, size), BF16)
    return pl.pallas_call(
        functools.partial(spread_kernel, flip, len(vals)),
        out_shape=[out] * (2 * CHUNKS),
        in_specs=[SMEM, SMEM, pl.BlockSpec(memory_space=pl.ANY)] + [VMEM] * len(vals),
        out_specs=[VMEM] * (2 * CHUNKS),
        scratch_shapes=[
            pltpu.VMEM((rows * blocks, feat, size), F32),
            pltpu.VMEM(edge_tiles.shape, BF16),
            pltpu.VMEM((blocks, feat, size), BF16),
            pltpu.SemaphoreType.DMA((COPIES,)),
        ],
        compiler_params=PARAMS,
        cost_estimate=pl.CostEstimate(flops=2 * edge_tiles.size * feat, bytes_accessed=40_000_000, transcendentals=0),
        name="spread",
    )(block_cols, at, edge_tiles, *vals)


def aggregate_kernel(cols_ref, tiles_ref, table_ref, out_ref, held, sems):
    for i in range(COPIES):
        tile_copy(tiles_ref, held, sems, i).start()
    per_row = held.shape[1]

    def one_row(r):
        total = None
        for k in range(0, per_row, 2):
            pair = jnp.concatenate([held[r, k], held[r, k + 1]], axis=1)
            picked = jnp.concatenate([table_ref[cols_ref[r, k]], table_ref[cols_ref[r, k + 1]]], axis=0)
            term = jnp.dot(pair, picked, preferred_element_type=F32)
            total = term if total is None else total + term
        out_ref[r] = total.astype(BF16)

    over_rows(tiles_ref, held, sems, one_row)


def aggregate(edge_tiles, block_cols, table):
    blocks, _, size, _ = edge_tiles.shape
    feat = table.shape[2]
    return pl.pallas_call(
        aggregate_kernel,
        out_shape=jax.ShapeDtypeStruct((blocks, size, feat), BF16),
        in_specs=[SMEM, pl.BlockSpec(memory_space=pl.ANY), VMEM],
        out_specs=VMEM,
        scratch_shapes=[pltpu.VMEM(edge_tiles.shape, BF16), pltpu.SemaphoreType.DMA((COPIES,))],
        compiler_params=PARAMS,
        cost_estimate=pl.CostEstimate(flops=2 * edge_tiles.size * feat, bytes_accessed=30_000_000, transcendentals=0),
        name="aggregate",
    )(block_cols, edge_tiles, table)


def finish_kernel(pieces, at_ref, *rest):
    parts, outs = rest[: 2 * CHUNKS], rest[2 * CHUNKS : 2 * CHUNKS + max(pieces, 1)]
    total = [parts[2 * g][...].astype(F32) + parts[2 * g + 1][...].astype(F32) for g in range(CHUNKS)]
    count = parts[0].shape[0]
    if pieces == 0:
        for g in range(CHUNKS):
            for b in range(count):
                outs[0][g * count + b] = total[g][b].T.astype(BF16)
        return
    held = rest[-1]
    for g in range(CHUNKS):
        held[g * count : (g + 1) * count] = total[g].astype(BF16)
    per = outs[0].shape[0]
    for m in range(pieces):
        outs[m][...] = held[pl.ds(jnp.bitwise_xor(at_ref[1], m) * per, per)]


def finish(parts, at, pieces):
    count, feat, size = parts[0].shape
    blocks = count * CHUNKS
    if pieces == 0:
        outs, scratch = [jax.ShapeDtypeStruct((blocks, size, feat), BF16)], []
    else:
        outs = [jax.ShapeDtypeStruct((blocks // pieces, feat, size), BF16)] * pieces
        scratch = [pltpu.VMEM((blocks, feat, size), BF16)]
    return pl.pallas_call(
        functools.partial(finish_kernel, pieces),
        out_shape=outs,
        in_specs=[SMEM] + [VMEM] * len(parts),
        out_specs=[VMEM] * len(outs),
        scratch_shapes=scratch,
        compiler_params=PARAMS,
        name="finish",
    )(at, *parts)


def dense_kernel(cols, at_ref, weights_ref, *rest):
    sums, rest = rest[:cols], rest[cols:]
    sides, rest = rest[:cols], rest[cols:]
    outs, rest = rest[:cols], rest[cols:]
    delta_ref, rest = rest[0], rest[1:]
    grads, (held, mask) = rest[:cols], rest[cols:]
    col = at_ref[1]
    count, feat, size = sums[0].shape
    width = cols * feat
    for m in range(cols):
        place = jnp.bitwise_xor(col, m)
        for b in range(count):
            held[place, b] = sums[m][b]
            mask[place, b] = sides[m][b, size:].astype(F32).T
    outer = [weights_ref[q, 0] for q in range(cols)]
    inner = [weights_ref[q, 1] for q in range(cols)]
    for b in range(count):
        stacked = jnp.concatenate([held[q, b] for q in range(cols)], axis=0)
        for q in range(cols):
            grad = jnp.dot(outer[q], stacked, preferred_element_type=F32)
            delta_ref[q, b] = (grad * mask[q, b]).astype(BF16)
        delta = jnp.concatenate([delta_ref[q, b] for q in range(cols)], axis=0)
        for q in range(cols):
            held[q, b] = jnp.dot(inner[q], delta, preferred_element_type=F32).astype(BF16)
        for m in range(cols):
            term = jnp.dot(stacked, sides[m][b, :size], preferred_element_type=F32)
            if b == 0:
                grads[m][...] = term
            else:
                grads[m][...] += term
    for m in range(cols):
        outs[m][...] = held[jnp.bitwise_xor(col, m)]


def dense(weights, sums, sides, at):
    cols = len(sums)
    count, feat, size = sums[0].shape
    out = jax.ShapeDtypeStruct((count, feat, size), BF16)
    delta = jax.ShapeDtypeStruct((cols, count, feat, size), BF16)
    grad = jax.ShapeDtypeStruct((cols * feat, feat), F32)
    res = pl.pallas_call(
        functools.partial(dense_kernel, cols),
        out_shape=[out] * cols + [delta] + [grad] * cols,
        in_specs=[SMEM] + [VMEM] * (1 + 2 * cols),
        out_specs=[VMEM] * (2 * cols + 1),
        scratch_shapes=[pltpu.VMEM((cols, count, feat, size), BF16), pltpu.VMEM((cols, count, feat, size), F32)],
        compiler_params=PARAMS,
        name="dense",
    )(at, weights, *sums, *sides)
    return res[:cols], res[cols], res[cols + 1 :]


def weight_terms_kernel(cols, delta_ref, *rest):
    sides, grads = rest[:cols], rest[cols:]
    count = delta_ref.shape[1]
    for b in range(count):
        delta = jnp.concatenate([delta_ref[q, b] for q in range(cols)], axis=0)
        for m in range(cols):
            term = jnp.dot(delta, sides[m][b], preferred_element_type=F32)
            if b == 0:
                grads[m][...] = term
            else:
                grads[m][...] += term


def weight_terms(delta, sides):
    cols, _, feat, _ = delta.shape
    return pl.pallas_call(
        functools.partial(weight_terms_kernel, cols),
        out_shape=[jax.ShapeDtypeStruct((cols * feat, feat), F32)] * cols,
        in_specs=[VMEM] * (1 + cols),
        out_specs=[VMEM] * cols,
        compiler_params=PARAMS,
        name="weight_terms",
    )(delta, *sides)


def swap(value, mask, axis):
    return lax.ppermute(value, axis, [(i, i ^ mask) for i in range(lax.axis_size(axis))])


def swap_all(pieces, axis):
    return [pieces[0]] + [swap(pieces[m], m, axis) for m in range(1, len(pieces))]


def add(a, b):
    return (a.astype(F32) + b.astype(F32)).astype(BF16)


def scatter_chunk(keep, got, masks):
    left = sorted(masks, reverse=True)
    for mask in masks:
        axis = left.index(mask)
        part = lambda v, i: lax.index_in_dim(v, i, axis, keepdims=False)
        sent = swap(add(part(keep, 1), part(got, 1)), mask, "row")
        keep = add(part(keep, 0), part(got, 0))
        got = sent
        left.remove(mask)
    return [keep, got]


def scatter(pieces, rows):
    masks = [1 << b for b in range(1, rows.bit_length() - 1)]
    lead = (2,) * len(masks)
    done = []
    for g in range(CHUNKS):
        keep, got = pieces[2 * g], swap(pieces[2 * g + 1], 1, "row")
        order = masks if g % 2 == 0 else masks[::-1]
        done += scatter_chunk(keep.reshape(lead + keep.shape[1:]), got.reshape(lead + got.shape[1:]), order)
    return done


def reduced(terms):
    got = swap_all([terms[0]] + [t.astype(BF16) for t in terms[1:]], "col")
    value = sum(g.astype(F32) for g in got)
    mask = 1
    while mask < lax.axis_size("row"):
        value = value.astype(BF16)
        value = value.astype(F32) + swap(value, mask, "row").astype(F32)
        mask *= 2
    return value.T


def per_device(
    node_feats, hidden_act, grad_out, relu_mask, edge_tiles, block_cols, weight_one, weight_two
):
    rows, cols = lax.axis_size("row"), lax.axis_size("col")
    col = lax.axis_index("col").astype(jnp.int32)
    at = jnp.stack([lax.axis_index("row").astype(jnp.int32), col])
    blocks, _, size, _ = edge_tiles.shape
    blocked = lambda v: v.reshape(v.shape[0] // size, size, v.shape[1])

    def by_distance(v):
        per = blocks // cols
        return [lax.dynamic_slice_in_dim(v, (col ^ m) * per, per, 0) for m in range(cols)]

    weights = lax.all_gather(jnp.stack([weight_two, weight_one]), "col", axis=0)
    table = blocked(lax.all_gather(node_feats, "row", axis=0, tiled=True))

    pieces = spread(edge_tiles, block_cols, [blocked(grad_out)], at, rows, True)
    both = jnp.concatenate([blocked(hidden_act), blocked(relu_mask).astype(BF16)], axis=1)
    pieces, both = lax.optimization_barrier((pieces, both))
    sides = swap_all(by_distance(both), "col")
    sums = finish(scatter(pieces, rows), at, cols)
    sums = swap_all(sums, "col")
    spread_in, delta, second_terms = dense(weights, sums, sides, at)
    back = swap_all(spread_in, "col")
    agg_feats = by_distance(aggregate(edge_tiles, block_cols, table))
    first_terms = weight_terms(delta, swap_all(agg_feats, "col"))
    pieces = spread(edge_tiles, block_cols, back, at, rows, False)
    (out,) = finish(scatter(pieces, rows), at, 0)
    return out.reshape(node_feats.shape), reduced(first_terms), reduced(second_terms)


def solution(mesh):
    in_specs = (
        P("row", "col"),
        P("row", "col"),
        P("row", "col"),
        P("row", "col"),
        P("row", None, None, None),
        P("row", None),
        P("col", None),
        P("col", None),
    )
    out_specs = (P("row", "col"), P("col", None), P("col", None))
    return jax.shard_map(
        per_device, mesh=mesh, in_specs=in_specs, out_specs=out_specs, check_vma=False
    )
```

time: 457 us -> 188 us (0.41)
  matrix products: 142 us -> 0 us
  waiting for transfers between devices: 217 us -> 81.5 us
  local copies, waits for them, and re-layouts: 71.7 us -> 5.22 us
  starting transfers between devices: 0.24 us -> 50.9 us
  Pallas kernels: 0 us -> 25.4 us
    dot_general x11 -> x0, matrix products: 142 us -> none  [the longest x2 48.9 us: collect_terms(): jnp.dot(selector, lower, preferred_element_type=jnp.float32)]
    reduce_scatter x2 -> x0, waiting for transfers between devices: 101 us -> none  [the longest x1 51.2 us: spread_input(): lax.psum_scatter(dense_terms.astype(jnp.bfloat16), 'row', scatter_dimensi...]
    all_gather x3 -> x2, waiting for transfers between devices: 94.9 us -> 0.01 us  [the longest x1 0.01 us: per_device(): weights = lax.all_gather(jnp.stack([weight_two, weight_one]), 'col', axis=0)]
    ppermute x0 -> x36, waiting for transfers between devices: none -> 80.8 us  [swap(): lax.ppermute(value, axis, [(i, i ^ mask) for i in range(lax.axis_size(axi...]
    ppermute x0 -> x36, starting transfers between devices: none -> 50.8 us  [swap(): lax.ppermute(value, axis, [(i, i ^ mask) for i in range(lax.axis_size(axi...]
    dot_general x2 -> x0, local copies, waits for them, and re-layouts: 40.9 us -> none  [tile_terms(): jnp.einsum('rkij,rid->rkjd', edge_tiles, blocks, preferred_element_type=j...]
    pallas_call x0 -> x7, Pallas kernels: none -> 25.4 us  [the longest x2 13.3 us: spread(): pl.pallas_call(functools.partial(spread_kernel, flip, len(vals)), out_sha...]
    psum x1 -> x0, waiting for transfers between devices: 20.7 us -> none  [per_device(): lax.psum(first_part.astype(jnp.bfloat16), 'row').astype(jnp.float32)]
  transfers between devices with their start and end apart: 6 -> 38, of which waited for: 5 -> 21; matrix products, arithmetic and copies ran while one was open for 21% -> 5% of each run, Pallas kernels for 0% -> 14%
where the time goes in v2:
time: 188 us
  waiting for transfers between devices  81.5 us (43%)
  starting transfers between devices  50.9 us (27%)
  Pallas kernels  25.4 us (14%)
  between operations  14.3 us (8%)
  other arithmetic  10.3 us (5%)
  local copies, waits for them, and re-layouts  5.22 us (3%)
    ppermute x36, waiting for transfers between devices, swap(): lax.ppermute(value, axis, [(i, i ^ mask) for i in range(lax.axis_size(axi...  80.8 us
    ppermute x36, starting transfers between devices, swap(): lax.ppermute(value, axis, [(i, i ^ mask) for i in range(lax.axis_size(axi...  50.8 us
    pallas_call x2, Pallas kernels, spread(): pl.pallas_call(functools.partial(spread_kernel, flip, len(vals)), out_sha...  13.3 us
    convert_element_type x8, other arithmetic, add(): return (a.astype(F32) + b.astype(F32)).astype(BF16)  6.72 us
    pallas_call x1, Pallas kernels, aggregate(): pl.pallas_call(aggregate_kernel, out_shape=jax.ShapeDtypeStruct((blocks,...  6.02 us
    unnamed x12, local copies, waits for them, and re-layouts  5.1 us
  transfers between devices with their start and end apart: 38, of which 21 were waited for; matrix products, arithmetic and copies ran while one was open for 5% of the time, Pallas kernels for 14%

profile of v2, /device:TPU:0, one launch (start us, length us, event | category | flops | bytes accessed | tf_op | source)
XLA Modules:
  0.0 187.6 jit_solution(10338939125134575763)
XLA Ops:
  7.2 1.7 pad_maximum_fusion.1
  9.8 1.3 convert_element_type.304
  11.1 6.8 %spread.2 = (bf16[4,8,128,128]{3,2,1,0:T(8,128)(2,1)S(1)}, bf16[4,8,128,128]{3,2,1,0:T(8,128)(2,1)S(1)}, bf16[4,8,128,128]{3,2,1,0:T(8,128)(2,1)S(1)}, bf16[4,8,128,128]{3,2,1,0:T(8,128)(2,1)S(1)}) custom-call(s32[16,20]{1,0:T(8,128)S(1)} %copy-done.3, s32[2]{0:T(128)S(1)} %pad_add_fusion.at_ref, bf16[16,20,128,128]{3,2,1,0:T(8,128)(2,1)} %tiles_ref.5, ...), custom_call_target="tpu_custom_call" | custom-call | flops 1342177280 | bytes 40000000 | tf_op jit(solution)/shard_map/spread/pallas_call | solution.py:73
  18.6 2.2 %collective-permute-done.3 = bf16[4,8,128,128]{3,2,1,0:T(8,128)(2,1)S(1)} collective-permute-done((bf16[4,8,128,128]{3,2,1,0:T(8,128)(2,1)S(1)}, bf16[4,8,128,128]{3,2,1,0:T(8,128)(2,1)S(1)}, u32[]{:S(2)}, u32[]{:S(2)}) %collective-permute-start.3) | collective-permute-done | bytes 1048608 | tf_op jit(solution)/shard_map/ppermute | solution.py:236
  20.8 1.2 add_convert_fusion.5
  22.0 2.9 %collective-permute-start.4 = (bf16[2,8,128,128]{3,2,1,0:T(8,128)(2,1)}, bf16[2,8,128,128]{3,2,1,0:T(8,128)(2,1)S(1)}, u32[]{:S(2)}, u32[]{:S(2)}) collective-permute-start(bf16[2,8,128,128]{3,2,1,0:T(8,128)(2,1)} %get-tuple-element.74), channel_id=1, source_target_pairs={{0,16},{4,20},{8,24},{12,28},{16,0},{20,4},{24,8},{28,12},{1,17},{... | collective-permute-start | bytes 1572872 | tf_op jit(solution)/shard_map/ppermute | solution.py:236
  24.9 1.2 add_convert_fusion.7
  26.1 1.5 collective-permute-start.1
  27.6 9.8 %collective-permute-done.4 = bf16[2,8,128,128]{3,2,1,0:T(8,128)(2,1)S(1)} collective-permute-done((bf16[2,8,128,128]{3,2,1,0:T(8,128)(2,1)}, bf16[2,8,128,128]{3,2,1,0:T(8,128)(2,1)S(1)}, u32[]{:S(2)}, u32[]{:S(2)}) %collective-permute-start.4) | collective-permute-done | bytes 524320 | tf_op jit(solution)/shard_map/ppermute | solution.py:236
  37.5 1.8 collective-permute-start.5
  39.3 0.8 collective-permute-done.1
  40.2 0.8 collective-permute-start.2
  41.1 2.7 %collective-permute-start.10 = (bf16[4,256,128]{2,1,0:T(8,128)(2,1)S(1)}, bf16[4,256,128]{2,1,0:T(8,128)(2,1)S(1)}, u32[]{:S(2)}, u32[]{:S(2)}) collective-permute-start(bf16[4,256,128]{2,1,0:T(8,128)(2,1)S(1)} %get-tuple-element.82), channel_id=1, source_target_pairs={{0,2},{1,3},{2,0},{3,1},{4,6},{5,7},{6,4},{7,5},{8,10},{9,11},{10,... | collective-permute-start | bytes 786440 | tf_op jit(solution)/shard_map/ppermute | solution.py:236
  43.7 1.3 collective-permute-start.11
  45.6 1.9 %collective-permute-done.2.rest_1_ = bf16[8,128,128]{2,1,0:T(8,128)(2,1)S(1)} collective-permute-done((bf16[8,128,128]{2,1,0:T(8,128)(2,1)S(1)}, bf16[8,128,128]{2,1,0:T(8,128)(2,1)S(1)}, u32[]{:S(2)}, u32[]{:S(2)}) %collective-permute-start.2) | collective-permute-done | bytes 262176 | tf_op jit(solution)/shard_map/ppermute | solution.py:236
  47.5 0.8 finish.2
  48.3 1.6 collective-permute-start.6
  49.9 2.6 %collective-permute-start.7 = (bf16[4,128,128]{2,1,0:T(8,128)(2,1)S(1)}, bf16[4,128,128]{2,1,0:T(8,128)(2,1)S(1)}, u32[]{:S(2)}, u32[]{:S(2)}) collective-permute-start(bf16[4,128,128]{2,1,0:T(8,128)(2,1)S(1)} %get-tuple-element.43), channel_id=1, source_target_pairs={{0,2},{1,3},{2,0},{3,1},{4,6},{5,7},{6,4},{7,5},{8,10},{9,11},{10,... | collective-permute-start | bytes 393224 | tf_op jit(solution)/shard_map/ppermute | solution.py:236
  52.5 9.0 %collective-permute-done.10.rest_6_ = bf16[4,256,128]{2,1,0:T(8,128)(2,1)S(1)} collective-permute-done((bf16[4,256,128]{2,1,0:T(8,128)(2,1)S(1)}, bf16[4,256,128]{2,1,0:T(8,128)(2,1)S(1)}, u32[]{:S(2)}, u32[]{:S(2)}) %collective-permute-start.10) | collective-permute-done | bytes 262176 | tf_op jit(solution)/shard_map/ppermute | solution.py:236
  61.5 2.5 %collective-permute-start.8 = (bf16[4,128,128]{2,1,0:T(8,128)(2,1)S(1)}, bf16[4,128,128]{2,1,0:T(8,128)(2,1)S(1)}, u32[]{:S(2)}, u32[]{:S(2)}) collective-permute-start(bf16[4,128,128]{2,1,0:T(8,128)(2,1)S(1)} %get-tuple-element.44), channel_id=1, source_target_pairs={{0,3},{1,2},{2,1},{3,0},{4,7},{5,6},{6,5},{7,4},{8,11},{9,10},{10,... | collective-permute-start | bytes 393224 | tf_op jit(solution)/shard_map/ppermute | solution.py:236
  64.7 10.9 %collective-permute-done.7.rest_2_ = bf16[4,128,128]{2,1,0:T(8,128)(2,1)S(1)} collective-permute-done((bf16[4,128,128]{2,1,0:T(8,128)(2,1)S(1)}, bf16[4,128,128]{2,1,0:T(8,128)(2,1)S(1)}, u32[]{:S(2)}, u32[]{:S(2)}) %collective-permute-start.7) | collective-permute-done | bytes 131104 | tf_op jit(solution)/shard_map/ppermute | solution.py:236
  75.6 1.2 copy-done.1
  76.8 3.0 %dense.1 = (bf16[4,128,128]{2,1,0:T(8,128)(2,1)S(1)}, bf16[4,128,128]{2,1,0:T(8,128)(2,1)S(1)}, bf16[4,128,128]{2,1,0:T(8,128)(2,1)S(1)}, bf16[4,128,128]{2,1,0:...) custom-call(s32[2]{0:T(128)S(1)} %pad_add_fusion.at_ref, ...), custom_call_target="tpu_custom_call" | custom-call | tf_op jit(solution)/shard_map/dense/pallas_call | solution.py:198
  79.8 2.4 %collective-permute-start.12 = (bf16[4,128,128]{2,1,0:T(8,128)(2,1)S(1)}, bf16[4,128,128]{2,1,0:T(8,128)(2,1)S(1)}, u32[]{:S(2)}, u32[]{:S(2)}) collective-permute-start(bf16[4,128,128]{2,1,0:T(8,128)(2,1)S(1)} %get-tuple-element.47), channel_id=1, source_target_pairs={{0,1},{1,0},{2,3},{3,2},{4,5},{5,4},{6,7},{7,6},{8,9},{9,8},{10,11... | collective-permute-start | bytes 393224 | tf_op jit(solution)/shard_map/ppermute | solution.py:236
  82.2 2.0 %collective-permute-start.13 = (bf16[4,128,128]{2,1,0:T(8,128)(2,1)S(1)}, bf16[4,128,128]{2,1,0:T(8,128)(2,1)S(1)}, u32[]{:S(2)}, u32[]{:S(2)}) collective-permute-start(bf16[4,128,128]{2,1,0:T(8,128)(2,1)S(1)} %get-tuple-element.48), channel_id=1, source_target_pairs={{0,2},{1,3},{2,0},{3,1},{4,6},{5,7},{6,4},{7,5},{8,10},{9,11},{10,... | collective-permute-start | bytes 393224 | tf_op jit(solution)/shard_map/ppermute | solution.py:236
  84.3 1.4 collective-permute-start.14
  85.7 2.8 %collective-permute-done.12.rest_1_ = bf16[4,128,128]{2,1,0:T(8,128)(2,1)S(1)} collective-permute-done((bf16[4,128,128]{2,1,0:T(8,128)(2,1)S(1)}, bf16[4,128,128]{2,1,0:T(8,128)(2,1)S(1)}, u32[]{:S(2)}, u32[]{:S(2)}) %collective-permute-start.12) | collective-permute-done | bytes 131104 | tf_op jit(solution)/shard_map/ppermute | solution.py:236
  88.5 1.0 collective-permute-done.13.rest_2_
  89.4 5.4 %collective-permute-done.14.rest_3_ = bf16[4,128,128]{2,1,0:T(8,128)(2,1)S(1)} collective-permute-done((bf16[4,128,128]{2,1,0:T(8,128)(2,1)S(1)}, bf16[4,128,128]{2,1,0:T(8,128)(2,1)S(1)}, u32[]{:S(2)}, u32[]{:S(2)}) %collective-permute-start.14) | collective-permute-done | bytes 131104 | tf_op jit(solution)/shard_map/ppermute | solution.py:236
  94.8 6.5 %spread.3 = (bf16[4,8,128,128]{3,2,1,0:T(8,128)(2,1)S(1)}, bf16[4,8,128,128]{3,2,1,0:T(8,128)(2,1)S(1)}, bf16[4,8,128,128]{3,2,1,0:T(8,128)(2,1)S(1)}, bf16[4,8,128,128]{3,2,1,0:T(8,128)(2,1)S(1)}) custom-call(s32[16,20]{1,0:T(8,128)S(1)} %copy-done.3, s32[2]{0:T(128)S(1)} %pad_add_fusion.at_ref, bf16[16,20,128,128]{3,2,1,0:T(8,128)(2,1)} %tiles_ref.5, ...), custom_call_target="tpu_custom_call" | custom-call | flops 1342177280 | bytes 40000000 | tf_op jit(solution)/shard_map/spread/pallas_call | solution.py:73
  101.5 2.5 %collective-permute-start.30 = (bf16[512,128]{1,0:T(8,128)(2,1)S(1)}, bf16[512,128]{1,0:T(8,128)(2,1)S(1)}, u32[]{:S(2)}, u32[]{:S(2)}) collective-permute-start(bf16[512,128]{1,0:T(8,128)(2,1)S(1)} %convert_element_type.383), channel_id=1, source_target_pairs={{0,1},{1,0},{2,3},{3,2},{4,5},{5,4},{6,7},{7,6},{8,9},{9,8},{10,11... | collective-permute-start | bytes 393224 | tf_op jit(solution)/shard_map/ppermute | solution.py:236
  104.0 2.0 %collective-permute-start.31 = (bf16[512,128]{1,0:T(8,128)(2,1)S(1)}, bf16[512,128]{1,0:T(8,128)(2,1)S(1)}, u32[]{:S(2)}, u32[]{:S(2)}) collective-permute-start(bf16[512,128]{1,0:T(8,128)(2,1)S(1)} %convert_element_type.385), channel_id=1, source_target_pairs={{0,2},{1,3},{2,0},{3,1},{4,6},{5,7},{6,4},{7,5},{8,10},{9,11},{10,... | collective-permute-start | bytes 393224 | tf_op jit(solution)/shard_map/ppermute | solution.py:236
  106.0 1.5 collective-permute-start.32
  107.5 3.2 %collective-permute-done.30 = bf16[512,128]{1,0:T(8,128)(2,1)S(1)} collective-permute-done((bf16[512,128]{1,0:T(8,128)(2,1)S(1)}, bf16[512,128]{1,0:T(8,128)(2,1)S(1)}, u32[]{:S(2)}, u32[]{:S(2)}) %collective-permute-start.30) | collective-permute-done | bytes 131104 | tf_op jit(solution)/shard_map/ppermute | solution.py:236
  110.7 0.8 collective-permute-done.31
  111.5 5.4 %collective-permute-done.32 = bf16[512,128]{1,0:T(8,128)(2,1)S(1)} collective-permute-done((bf16[512,128]{1,0:T(8,128)(2,1)S(1)}, bf16[512,128]{1,0:T(8,128)(2,1)S(1)}, u32[]{:S(2)}, u32[]{:S(2)}) %collective-permute-start.32) | collective-permute-done | bytes 131104 | tf_op jit(solution)/shard_map/ppermute | solution.py:236
  117.6 0.8 collective-permute-done.33
  118.4 1.5 collective-permute-start.34
  119.9 1.2 add_convert_fusion.1
  121.1 1.2 collective-permute-start.19
  122.3 2.2 %copy-done = bf16[16384,128]{1,0:T(8,128)(2,1)S(1)} copy-done((bf16[16384,128]{1,0:T(8,128)(2,1)S(1)}, bf16[16384,128]{1,0:T(8,128)(2,1)}, u32[]{:S(2)}) %copy-start) | copy-done | bytes 4194328
  124.5 6.0 %aggregate.1 = bf16[16,128,128]{2,1,0:T(8,128)(2,1)S(1)} custom-call(s32[16,20]{1,0:T(8,128)S(1)} %copy-done.3, bf16[16,20,128,128]{3,2,1,0:T(8,128)(2,1)} %tiles_ref.5, bf16[128,128,128]{2,1,0:T(8,128)(2,1)S(1)} %bitcast.58), custom_call_target="tpu_custom_call" | custom-call | flops 1342177280 | bytes 30000000 | tf_op jit(solution)/shard_map/aggregate/pallas_call | solution.py:110
  130.5 2.8 %collective-permute-start.21 = (bf16[4,128,128]{2,1,0:T(8,128)(2,1)S(1)}, bf16[4,128,128]{2,1,0:T(8,128)(2,1)S(1)}, u32[]{:S(2)}, u32[]{:S(2)}) collective-permute-start(bf16[4,128,128]{2,1,0:T(8,128)(2,1)S(1)} %get-tuple-element.91), channel_id=1, source_target_pairs={{0,1},{1,0},{2,3},{3,2},{4,5},{5,4},{6,7},{7,6},{8,9},{9,8},{10,11... | collective-permute-start | bytes 393224 | tf_op jit(solution)/shard_map/ppermute | solution.py:236
  133.3 1.8 collective-permute-start.22
  135.1 1.4 collective-permute-start.23
  136.5 1.8 collective-permute-done.21.rest_1_
  138.3 0.9 collective-permute-start.35
  139.3 6.6 %collective-permute-done.22.rest_2_ = bf16[4,128,128]{2,1,0:T(8,128)(2,1)S(1)} collective-permute-done((bf16[4,128,128]{2,1,0:T(8,128)(2,1)S(1)}, bf16[4,128,128]{2,1,0:T(8,128)(2,1)S(1)}, u32[]{:S(2)}, u32[]{:S(2)}) %collective-permute-start.22) | collective-permute-done | bytes 131104 | tf_op jit(solution)/shard_map/ppermute | solution.py:236
  146.6 2.4 %collective-permute-start.24 = (bf16[512,128]{1,0:T(8,128)(2,1)S(1)}, bf16[512,128]{1,0:T(8,128)(2,1)S(1)}, u32[]{:S(2)}, u32[]{:S(2)}) collective-permute-start(bf16[512,128]{1,0:T(8,128)(2,1)S(1)} %convert_element_type.368), channel_id=1, source_target_pairs={{0,1},{1,0},{2,3},{3,2},{4,5},{5,4},{6,7},{7,6},{8,9},{9,8},{10,11... | collective-permute-start | bytes 393224 | tf_op jit(solution)/shard_map/ppermute | solution.py:236
  149.0 1.4 collective-permute-start.25
  150.4 1.5 collective-permute-start.26
  151.9 1.6 add_convert_fusion.3
  153.5 0.7 collective-permute-start.16
  154.2 7.1 %collective-permute-done.25 = bf16[512,128]{1,0:T(8,128)(2,1)S(1)} collective-permute-done((bf16[512,128]{1,0:T(8,128)(2,1)S(1)}, bf16[512,128]{1,0:T(8,128)(2,1)S(1)}, u32[]{:S(2)}, u32[]{:S(2)}) %collective-permute-start.25) | collective-permute-done | bytes 131104 | tf_op jit(solution)/shard_map/ppermute | solution.py:236
  161.5 1.2 fusion.9
  163.4 1.4 collective-permute-start.28
  164.9 1.3 collective-permute-done.16
  166.4 1.0 collective-permute-start.17
  167.4 7.1 %collective-permute-done.28 = bf16[512,128]{1,0:T(8,128)(2,1)S(1)} collective-permute-done((bf16[512,128]{1,0:T(8,128)(2,1)S(1)}, bf16[512,128]{1,0:T(8,128)(2,1)S(1)}, u32[]{:S(2)}, u32[]{:S(2)}) %collective-permute-start.28) | collective-permute-done | bytes 131104 | tf_op jit(solution)/shard_map/ppermute | solution.py:236
  174.5 1.0 collective-permute-start.29
  175.6 0.8 copy.14
  176.4 1.6 finish.3
  178.0 1.9 %collective-permute-done.29 = bf16[512,128]{1,0:T(8,128)(2,1)S(1)} collective-permute-done((bf16[512,128]{1,0:T(8,128)(2,1)S(1)}, bf16[512,128]{1,0:T(8,128)(2,1)S(1)}, u32[]{:S(2)}, u32[]{:S(2)}) %collective-permute-start.29) | collective-permute-done | bytes 131104 | tf_op jit(solution)/shard_map/ppermute | solution.py:236
  179.9 0.8 copy.13
  (61 shorter events, 5.9 us)
Async XLA Ops:
  7.2 4.0 %copy-start.2 = (bf16[2048,128]{1,0:T(8,128)(2,1)S(1)}, bf16[2048,128]{1,0:T(8,128)(2,1)}, u32[]{:S(2)}) copy-start(bf16[2048,128]{1,0:T(8,128)(2,1)} %param.10) | copy-start | bytes 1572868
  7.2 3.9 %copy-start.3 = (s32[16,20]{1,0:T(8,128)S(1)}, s32[16,20]{1,0:T(8,128)}, u32[]{:S(2)}) copy-start(s32[16,20]{1,0:T(8,128)} %cols_ref.5) | copy-start | bytes 3844
  7.2 56.8 %all-gather.6.cloned.1.call-start = ((), (), s32[]{:S(2)}) async-start(), calls=%async_computation.1 | async-start | bytes 1310720 | tf_op jit(solution)/shard_map/all_gather | solution.py:294
  9.0 113.3 %all-gather.4.cloned.1.call-start = ((), (), s32[]{:S(2)}) async-start(), calls=%async_computation | async-start | bytes 4718592 | tf_op jit(solution)/shard_map/all_gather | solution.py:295
  11.1 6.8 %copy-start.4 = (bf16[2048,128]{1,0:T(8,128)(2,1)S(1)}, bf16[2048,128]{1,0:T(8,128)(2,1)}, u32[]{:S(2)}) copy-start(bf16[2048,128]{1,0:T(8,128)(2,1)} %param.9) | copy-start | bytes 1572868
  18.0 2.8 %collective-permute-start.3 = (bf16[4,8,128,128]{3,2,1,0:T(8,128)(2,1)S(1)}, bf16[4,8,128,128]{3,2,1,0:T(8,128)(2,1)S(1)}, u32[]{:S(2)}, u32[]{:S(2)}) collective-permute-start(bf16[4,8,128,128]{3,2,1,0:T(8,128)(2,1)S(1)} %get-tuple-element.40), channel_id=1, source_target_pairs={{0,4},{4,0},{8,12},{12,8},{16,20},{20,16},{24,28},{28,24},{1,5},{5... | collective-permute-start | bytes 3145736 | tf_op jit(solution)/shard_map/ppermute | solution.py:236
  18.5 6.4 %collective-permute-start = (bf16[4,8,128,128]{3,2,1,0:T(8,128)(2,1)S(1)}, bf16[4,8,128,128]{3,2,1,0:T(8,128)(2,1)S(1)}, u32[]{:S(2)}, u32[]{:S(2)}) collective-permute-start(bf16[4,8,128,128]{3,2,1,0:T(8,128)(2,1)S(1)} %get-tuple-element.38), channel_id=1, source_target_pairs={{0,4},{4,0},{8,12},{12,8},{16,20},{20,16},{24,28},{28,24},{1,5},{5... | collective-permute-start | bytes 3145736 | tf_op jit(solution)/shard_map/ppermute | solution.py:236
  22.0 15.3 %collective-permute-start.4 = (bf16[2,8,128,128]{3,2,1,0:T(8,128)(2,1)}, bf16[2,8,128,128]{3,2,1,0:T(8,128)(2,1)S(1)}, u32[]{:S(2)}, u32[]{:S(2)}) collective-permute-start(bf16[2,8,128,128]{3,2,1,0:T(8,128)(2,1)} %get-tuple-element.74), channel_id=1, source_target_pairs={{0,16},{4,20},{8,24},{12,28},{16,0},{20,4},{24,8},{28,12},{1,17},{... | collective-permute-start | bytes 1572872 | tf_op jit(solution)/shard_map/ppermute | solution.py:236
  26.1 13.9 %collective-permute-start.1 = (bf16[2,8,128,128]{3,2,1,0:T(8,128)(2,1)}, bf16[2,8,128,128]{3,2,1,0:T(8,128)(2,1)S(1)}, u32[]{:S(2)}, u32[]{:S(2)}) collective-permute-start(bf16[2,8,128,128]{3,2,1,0:T(8,128)(2,1)} %get-tuple-element.76), channel_id=1, source_target_pairs={{0,8},{4,12},{8,0},{12,4},{16,24},{20,28},{24,16},{28,20},{1,9},{5... | collective-permute-start | bytes 1572872 | tf_op jit(solution)/shard_map/ppermute | solution.py:236
  37.5 8.1 %collective-permute-start.5 = (bf16[8,128,128]{2,1,0:T(8,128)(2,1)S(1)}, bf16[8,128,128]{2,1,0:T(8,128)(2,1)S(1)}, u32[]{:S(2)}, u32[]{:S(2)}) collective-permute-start(bf16[8,128,128]{2,1,0:T(8,128)(2,1)S(1)} %get-tuple-element.85), channel_id=1, source_target_pairs={{0,8},{4,12},{8,0},{12,4},{16,24},{20,28},{24,16},{28,20},{1,9},{5... | collective-permute-start | bytes 786440 | tf_op jit(solution)/shard_map/ppermute | solution.py:236
  40.2 7.3 %collective-permute-start.2 = (bf16[8,128,128]{2,1,0:T(8,128)(2,1)S(1)}, bf16[8,128,128]{2,1,0:T(8,128)(2,1)S(1)}, u32[]{:S(2)}, u32[]{:S(2)}) collective-permute-start(bf16[8,128,128]{2,1,0:T(8,128)(2,1)S(1)} %get-tuple-element.87), channel_id=1, source_target_pairs={{0,16},{4,20},{8,24},{12,28},{16,0},{20,4},{24,8},{28,12},{1,17},{... | collective-permute-start | bytes 786440 | tf_op jit(solution)/shard_map/ppermute | solution.py:236
  41.1 20.4 %collective-permute-start.10 = (bf16[4,256,128]{2,1,0:T(8,128)(2,1)S(1)}, bf16[4,256,128]{2,1,0:T(8,128)(2,1)S(1)}, u32[]{:S(2)}, u32[]{:S(2)}) collective-permute-start(bf16[4,256,128]{2,1,0:T(8,128)(2,1)S(1)} %get-tuple-element.82), channel_id=1, source_target_pairs={{0,2},{1,3},{2,0},{3,1},{4,6},{5,7},{6,4},{7,5},{8,10},{9,11},{10,... | collective-permute-start | bytes 786440 | tf_op jit(solution)/shard_map/ppermute | solution.py:236
  43.7 20.2 %collective-permute-start.11 = (bf16[4,256,128]{2,1,0:T(8,128)(2,1)S(1)}, bf16[4,256,128]{2,1,0:T(8,128)(2,1)S(1)}, u32[]{:S(2)}, u32[]{:S(2)}) collective-permute-start(bf16[4,256,128]{2,1,0:T(8,128)(2,1)S(1)} %get-tuple-element.81), channel_id=1, source_target_pairs={{0,3},{1,2},{2,1},{3,0},{4,7},{5,6},{6,5},{7,4},{8,11},{9,10},{10,... | collective-permute-start | bytes 786440 | tf_op jit(solution)/shard_map/ppermute | solution.py:236
  45.1 18.9 %collective-permute-start.9 = (bf16[4,256,128]{2,1,0:T(8,128)(2,1)S(1)}, bf16[4,256,128]{2,1,0:T(8,128)(2,1)S(1)}, u32[]{:S(2)}, u32[]{:S(2)}) collective-permute-start(bf16[4,256,128]{2,1,0:T(8,128)(2,1)S(1)} %get-tuple-element.83), channel_id=1, source_target_pairs={{0,1},{1,0},{2,3},{3,2},{4,5},{5,4},{6,7},{7,6},{8,9},{9,8},{10,11... | collective-permute-start | bytes 786440 | tf_op jit(solution)/shard_map/ppermute | solution.py:236
  48.3 16.4 %collective-permute-start.6 = (bf16[4,128,128]{2,1,0:T(8,128)(2,1)S(1)}, bf16[4,128,128]{2,1,0:T(8,128)(2,1)S(1)}, u32[]{:S(2)}, u32[]{:S(2)}) collective-permute-start(bf16[4,128,128]{2,1,0:T(8,128)(2,1)S(1)} %get-tuple-element.42), channel_id=1, source_target_pairs={{0,1},{1,0},{2,3},{3,2},{4,5},{5,4},{6,7},{7,6},{8,9},{9,8},{10,11... | collective-permute-start | bytes 393224 | tf_op jit(solution)/shard_map/ppermute | solution.py:236
  49.9 25.6 %collective-permute-start.7 = (bf16[4,128,128]{2,1,0:T(8,128)(2,1)S(1)}, bf16[4,128,128]{2,1,0:T(8,128)(2,1)S(1)}, u32[]{:S(2)}, u32[]{:S(2)}) collective-permute-start(bf16[4,128,128]{2,1,0:T(8,128)(2,1)S(1)} %get-tuple-element.43), channel_id=1, source_target_pairs={{0,2},{1,3},{2,0},{3,1},{4,6},{5,7},{6,4},{7,5},{8,10},{9,11},{10,... | collective-permute-start | bytes 393224 | tf_op jit(solution)/shard_map/ppermute | solution.py:236
  61.5 14.0 %collective-permute-start.8 = (bf16[4,128,128]{2,1,0:T(8,128)(2,1)S(1)}, bf16[4,128,128]{2,1,0:T(8,128)(2,1)S(1)}, u32[]{:S(2)}, u32[]{:S(2)}) collective-permute-start(bf16[4,128,128]{2,1,0:T(8,128)(2,1)S(1)} %get-tuple-element.44), channel_id=1, source_target_pairs={{0,3},{1,2},{2,1},{3,0},{4,7},{5,6},{6,5},{7,4},{8,11},{9,10},{10,... | collective-permute-start | bytes 393224 | tf_op jit(solution)/shard_map/ppermute | solution.py:236
  75.6 1.2 copy-start.1
  79.8 8.7 %collective-permute-start.12 = (bf16[4,128,128]{2,1,0:T(8,128)(2,1)S(1)}, bf16[4,128,128]{2,1,0:T(8,128)(2,1)S(1)}, u32[]{:S(2)}, u32[]{:S(2)}) collective-permute-start(bf16[4,128,128]{2,1,0:T(8,128)(2,1)S(1)} %get-tuple-element.47), channel_id=1, source_target_pairs={{0,1},{1,0},{2,3},{3,2},{4,5},{5,4},{6,7},{7,6},{8,9},{9,8},{10,11... | collective-permute-start | bytes 393224 | tf_op jit(solution)/shard_map/ppermute | solution.py:236
  82.2 7.2 %collective-permute-start.13 = (bf16[4,128,128]{2,1,0:T(8,128)(2,1)S(1)}, bf16[4,128,128]{2,1,0:T(8,128)(2,1)S(1)}, u32[]{:S(2)}, u32[]{:S(2)}) collective-permute-start(bf16[4,128,128]{2,1,0:T(8,128)(2,1)S(1)} %get-tuple-element.48), channel_id=1, source_target_pairs={{0,2},{1,3},{2,0},{3,1},{4,6},{5,7},{6,4},{7,5},{8,10},{9,11},{10,... | collective-permute-start | bytes 393224 | tf_op jit(solution)/shard_map/ppermute | solution.py:236
  84.3 10.6 %collective-permute-start.14 = (bf16[4,128,128]{2,1,0:T(8,128)(2,1)S(1)}, bf16[4,128,128]{2,1,0:T(8,128)(2,1)S(1)}, u32[]{:S(2)}, u32[]{:S(2)}) collective-permute-start(bf16[4,128,128]{2,1,0:T(8,128)(2,1)S(1)} %get-tuple-element.49), channel_id=1, source_target_pairs={{0,3},{1,2},{2,1},{3,0},{4,7},{5,6},{6,5},{7,4},{8,11},{9,10},{10,... | collective-permute-start | bytes 393224 | tf_op jit(solution)/shard_map/ppermute | solution.py:236
  101.3 18.6 %collective-permute-start.18 = (bf16[4,8,128,128]{3,2,1,0:T(8,128)(2,1)S(1)}, bf16[4,8,128,128]{3,2,1,0:T(8,128)(2,1)S(1)}, u32[]{:S(2)}, u32[]{:S(2)}) collective-permute-start(bf16[4,8,128,128]{3,2,1,0:T(8,128)(2,1)S(1)} %get-tuple-element.53), channel_id=1, source_target_pairs={{0,4},{4,0},{8,12},{12,8},{16,20},{20,16},{24,28},{28,24},{1,5},{5... | collective-permute-start | bytes 3145736 | tf_op jit(solution)/shard_map/ppermute | solution.py:236
  101.5 9.3 %collective-permute-start.30 = (bf16[512,128]{1,0:T(8,128)(2,1)S(1)}, bf16[512,128]{1,0:T(8,128)(2,1)S(1)}, u32[]{:S(2)}, u32[]{:S(2)}) collective-permute-start(bf16[512,128]{1,0:T(8,128)(2,1)S(1)} %convert_element_type.383), channel_id=1, source_target_pairs={{0,1},{1,0},{2,3},{3,2},{4,5},{5,4},{6,7},{7,6},{8,9},{9,8},{10,11... | collective-permute-start | bytes 393224 | tf_op jit(solution)/shard_map/ppermute | solution.py:236
  104.0 7.5 %collective-permute-start.31 = (bf16[512,128]{1,0:T(8,128)(2,1)S(1)}, bf16[512,128]{1,0:T(8,128)(2,1)S(1)}, u32[]{:S(2)}, u32[]{:S(2)}) collective-permute-start(bf16[512,128]{1,0:T(8,128)(2,1)S(1)} %convert_element_type.385), channel_id=1, source_target_pairs={{0,2},{1,3},{2,0},{3,1},{4,6},{5,7},{6,4},{7,5},{8,10},{9,11},{10,... | collective-permute-start | bytes 393224 | tf_op jit(solution)/shard_map/ppermute | solution.py:236
  106.0 10.9 %collective-permute-start.32 = (bf16[512,128]{1,0:T(8,128)(2,1)S(1)}, bf16[512,128]{1,0:T(8,128)(2,1)S(1)}, u32[]{:S(2)}, u32[]{:S(2)}) collective-permute-start(bf16[512,128]{1,0:T(8,128)(2,1)S(1)} %convert_element_type.387), channel_id=1, source_target_pairs={{0,3},{1,2},{2,1},{3,0},{4,7},{5,6},{6,5},{7,4},{8,11},{9,10},{10,... | collective-permute-start | bytes 393224 | tf_op jit(solution)/shard_map/ppermute | solution.py:236
  117.0 1.4 collective-permute-start.33
  117.1 33.3 %collective-permute-start.15 = (bf16[4,8,128,128]{3,2,1,0:T(8,128)(2,1)S(1)}, bf16[4,8,128,128]{3,2,1,0:T(8,128)(2,1)}, u32[]{:S(2)}, u32[]{:S(2)}) collective-permute-start(bf16[4,8,128,128]{3,2,1,0:T(8,128)(2,1)S(1)} %get-tuple-element.51), channel_id=1, source_target_pairs={{0,4},{4,0},{8,12},{12,8},{16,20},{20,16},{24,28},{28,24},{1,5},{5... | collective-permute-start | bytes 3145736 | tf_op jit(solution)/shard_map/ppermute | solution.py:236
  118.4 16.7 %collective-permute-start.34 = (bf16[512,128]{1,0:T(8,128)(2,1)S(1)}, bf16[512,128]{1,0:T(8,128)(2,1)S(1)}, u32[]{:S(2)}, u32[]{:S(2)}) collective-permute-start(bf16[512,128]{1,0:T(8,128)(2,1)S(1)} %add_convert_fusion.13), channel_id=1, source_target_pairs={{0,8},{4,12},{8,0},{12,4},{16,24},{20,28},{24,16},{28,20},{1,9},{5... | collective-permute-start | bytes 393224 | tf_op jit(solution)/shard_map/ppermute | solution.py:236
  121.1 40.4 %collective-permute-start.19 = (bf16[2,8,128,128]{3,2,1,0:T(8,128)(2,1)}, bf16[2,8,128,128]{3,2,1,0:T(8,128)(2,1)}, u32[]{:S(2)}, u32[]{:S(2)}) collective-permute-start(bf16[2,8,128,128]{3,2,1,0:T(8,128)(2,1)} %get-tuple-element.70), channel_id=1, source_target_pairs={{0,16},{4,20},{8,24},{12,28},{16,0},{20,4},{24,8},{28,12},{1,17},{... | collective-permute-start | bytes 1572872 | tf_op jit(solution)/shard_map/ppermute | solution.py:236
  122.3 2.2 %copy-start = (bf16[16384,128]{1,0:T(8,128)(2,1)S(1)}, bf16[16384,128]{1,0:T(8,128)(2,1)}, u32[]{:S(2)}) copy-start(bf16[16384,128]{1,0:T(8,128)(2,1)} %all-gather.4.cloned.1.call-done) | copy-start | bytes 12582916
  130.5 7.8 %collective-permute-start.21 = (bf16[4,128,128]{2,1,0:T(8,128)(2,1)S(1)}, bf16[4,128,128]{2,1,0:T(8,128)(2,1)S(1)}, u32[]{:S(2)}, u32[]{:S(2)}) collective-permute-start(bf16[4,128,128]{2,1,0:T(8,128)(2,1)S(1)} %get-tuple-element.91), channel_id=1, source_target_pairs={{0,1},{1,0},{2,3},{3,2},{4,5},{5,4},{6,7},{7,6},{8,9},{9,8},{10,11... | collective-permute-start | bytes 393224 | tf_op jit(solution)/shard_map/ppermute | solution.py:236
  133.3 12.5 %collective-permute-start.22 = (bf16[4,128,128]{2,1,0:T(8,128)(2,1)S(1)}, bf16[4,128,128]{2,1,0:T(8,128)(2,1)S(1)}, u32[]{:S(2)}, u32[]{:S(2)}) collective-permute-start(bf16[4,128,128]{2,1,0:T(8,128)(2,1)S(1)} %get-tuple-element.90), channel_id=1, source_target_pairs={{0,2},{1,3},{2,0},{3,1},{4,6},{5,7},{6,4},{7,5},{8,10},{9,11},{10,... | collective-permute-start | bytes 393224 | tf_op jit(solution)/shard_map/ppermute | solution.py:236
  135.1 10.7 %collective-permute-start.23 = (bf16[4,128,128]{2,1,0:T(8,128)(2,1)S(1)}, bf16[4,128,128]{2,1,0:T(8,128)(2,1)S(1)}, u32[]{:S(2)}, u32[]{:S(2)}) collective-permute-start(bf16[4,128,128]{2,1,0:T(8,128)(2,1)S(1)} %get-tuple-element.89), channel_id=1, source_target_pairs={{0,3},{1,2},{2,1},{3,0},{4,7},{5,6},{6,5},{7,4},{8,11},{9,10},{10,... | collective-permute-start | bytes 393224 | tf_op jit(solution)/shard_map/ppermute | solution.py:236
  138.3 37.2 %collective-permute-start.35 = (bf16[512,128]{1,0:T(8,128)(2,1)S(1)}, bf16[512,128]{1,0:T(8,128)(2,1)S(1)}, u32[]{:S(2)}, u32[]{:S(2)}) collective-permute-start(bf16[512,128]{1,0:T(8,128)(2,1)S(1)} %add_convert_fusion.12), channel_id=1, source_target_pairs={{0,16},{4,20},{8,24},{12,28},{16,0},{20,4},{24,8},{28,12},{1,17},{... | collective-permute-start | bytes 393224 | tf_op jit(solution)/shard_map/ppermute | solution.py:236
  146.6 6.9 %collective-permute-start.24 = (bf16[512,128]{1,0:T(8,128)(2,1)S(1)}, bf16[512,128]{1,0:T(8,128)(2,1)S(1)}, u32[]{:S(2)}, u32[]{:S(2)}) collective-permute-start(bf16[512,128]{1,0:T(8,128)(2,1)S(1)} %convert_element_type.368), channel_id=1, source_target_pairs={{0,1},{1,0},{2,3},{3,2},{4,5},{5,4},{6,7},{7,6},{8,9},{9,8},{10,11... | collective-permute-start | bytes 393224 | tf_op jit(solution)/shard_map/ppermute | solution.py:236
  149.0 12.4 %collective-permute-start.25 = (bf16[512,128]{1,0:T(8,128)(2,1)S(1)}, bf16[512,128]{1,0:T(8,128)(2,1)S(1)}, u32[]{:S(2)}, u32[]{:S(2)}) collective-permute-start(bf16[512,128]{1,0:T(8,128)(2,1)S(1)} %convert_element_type.370), channel_id=1, source_target_pairs={{0,2},{1,3},{2,0},{3,1},{4,6},{5,7},{6,4},{7,5},{8,10},{9,11},{10,... | collective-permute-start | bytes 393224 | tf_op jit(solution)/shard_map/ppermute | solution.py:236
  150.4 10.9 %collective-permute-start.26 = (bf16[512,128]{1,0:T(8,128)(2,1)S(1)}, bf16[512,128]{1,0:T(8,128)(2,1)S(1)}, u32[]{:S(2)}, u32[]{:S(2)}) collective-permute-start(bf16[512,128]{1,0:T(8,128)(2,1)S(1)} %convert_element_type.372), channel_id=1, source_target_pairs={{0,3},{1,2},{2,1},{3,0},{4,7},{5,6},{6,5},{7,4},{8,11},{9,10},{10,... | collective-permute-start | bytes 393224 | tf_op jit(solution)/shard_map/ppermute | solution.py:236
  153.5 12.7 %collective-permute-start.16 = (bf16[2,8,128,128]{3,2,1,0:T(8,128)(2,1)S(1)}, bf16[2,8,128,128]{3,2,1,0:T(8,128)(2,1)S(1)}, u32[]{:S(2)}, u32[]{:S(2)}) collective-permute-start(bf16[2,8,128,128]{3,2,1,0:T(8,128)(2,1)S(1)} %get-tuple-element.72), channel_id=1, source_target_pairs={{0,8},{4,12},{8,0},{12,4},{16,24},{20,28},{24,16},{28,20},{1,9},{5... | collective-permute-start | bytes 1572872 | tf_op jit(solution)/shard_map/ppermute | solution.py:236
  161.4 2.0 %collective-permute-start.27 = (bf16[512,128]{1,0:T(8,128)(2,1)S(1)}, bf16[512,128]{1,0:T(8,128)(2,1)S(1)}, u32[]{:S(2)}, u32[]{:S(2)}) collective-permute-start(bf16[512,128]{1,0:T(8,128)(2,1)S(1)} %add_convert_fusion.17), channel_id=1, source_target_pairs={{0,4},{4,0},{8,12},{12,8},{16,20},{20,16},{24,28},{28,24},{1,5},{5... | collective-permute-start | bytes 393224 | tf_op jit(solution)/shard_map/ppermute | solution.py:236
  162.7 13.7 %collective-permute-start.20 = (bf16[8,128,128]{2,1,0:T(8,128)(2,1)S(1)}, bf16[8,128,128]{2,1,0:T(8,128)(2,1)S(1)}, u32[]{:S(2)}, u32[]{:S(2)}) collective-permute-start(bf16[8,128,128]{2,1,0:T(8,128)(2,1)S(1)} %get-tuple-element.77), channel_id=1, source_target_pairs={{0,8},{4,12},{8,0},{12,4},{16,24},{20,28},{24,16},{28,20},{1,9},{5... | collective-permute-start | bytes 786440 | tf_op jit(solution)/shard_map/ppermute | solution.py:236
  163.4 11.0 %collective-permute-start.28 = (bf16[512,128]{1,0:T(8,128)(2,1)S(1)}, bf16[512,128]{1,0:T(8,128)(2,1)S(1)}, u32[]{:S(2)}, u32[]{:S(2)}) collective-permute-start(bf16[512,128]{1,0:T(8,128)(2,1)S(1)} %add_convert_fusion.16), channel_id=1, source_target_pairs={{0,8},{4,12},{8,0},{12,4},{16,24},{20,28},{24,16},{28,20},{1,9},{5... | collective-permute-start | bytes 393224 | tf_op jit(solution)/shard_map/ppermute | solution.py:236
  166.4 10.0 %collective-permute-start.17 = (bf16[8,128,128]{2,1,0:T(8,128)(2,1)S(1)}, bf16[8,128,128]{2,1,0:T(8,128)(2,1)S(1)}, u32[]{:S(2)}, u32[]{:S(2)}) collective-permute-start(bf16[8,128,128]{2,1,0:T(8,128)(2,1)S(1)} %get-tuple-element.79), channel_id=1, source_target_pairs={{0,16},{4,20},{8,24},{12,28},{16,0},{20,4},{24,8},{28,12},{1,17},{... | collective-permute-start | bytes 786440 | tf_op jit(solution)/shard_map/ppermute | solution.py:236
  174.5 5.3 %collective-permute-start.29 = (bf16[512,128]{1,0:T(8,128)(2,1)S(1)}, bf16[512,128]{1,0:T(8,128)(2,1)S(1)}, u32[]{:S(2)}, u32[]{:S(2)}) collective-permute-start(bf16[512,128]{1,0:T(8,128)(2,1)S(1)} %add_convert_fusion.15), channel_id=1, source_target_pairs={{0,16},{4,20},{8,24},{12,28},{16,0},{20,4},{24,8},{28,12},{1,17},{... | collective-permute-start | bytes 393224 | tf_op jit(solution)/shard_map/ppermute | solution.py:236
Sparse Core Ops, SparseCore 0:
  10.2 30.6 all-gather.5
  42.7 36.1 all-gather.3

commit v3 on v2

--- a/solution.py
+++ b/solution.py
@@ -37,13 +37,26 @@
 
 def spread_kernel(flip, pieces, cols_ref, at_ref, tiles_ref, *rest):
     vals, rest = rest[:pieces], rest[pieces:]
-    outs, (acc, held, left_ref, sems) = rest[: 2 * CHUNKS], rest[2 * CHUNKS :]
+    if flip:
+        (hidden_ref, mask_ref, outer_ref, inner_ref), rest = rest[:4], rest[4:]
+    outs, rest = rest[: 2 * CHUNKS], rest[2 * CHUNKS :]
+    if flip:
+        weights_ref, sides, rest = rest[0], rest[1:-4], rest[-4:]
+    acc, held, left_ref, sems = rest
     for i in range(COPIES):
         tile_copy(tiles_ref, held, sems, i).start()
     acc[...] = jnp.zeros_like(acc)
     per_row, size = held.shape[1], held.shape[3]
     me, col = at_ref[0], at_ref[1]
-    if not flip:
+    if flip:
+        weights_ref[0] = outer_ref[...]
+        weights_ref[1] = inner_ref[...]
+        for m in range(len(sides)):
+            count = sides[m].shape[0]
+            part = pl.ds(jnp.bitwise_xor(col, m) * count, count)
+            sides[m][:, :size] = hidden_ref[part]
+            sides[m][:, size:] = mask_ref[part].astype(F32).astype(BF16)
+    else:
         count = vals[0].shape[0]
         for m in range(pieces):
             left_ref[pl.ds(jnp.bitwise_xor(col, m) * count, count)] = vals[m][...]
@@ -66,15 +79,20 @@
                 outs[2 * g + side][rel] = acc[pl.ds(first, count)].astype(BF16)
 
 
-def spread(edge_tiles, block_cols, vals, at, rows, flip):
+def spread(edge_tiles, block_cols, vals, at, rows, cols, prepare=()):
     blocks, _, size, _ = edge_tiles.shape
+    flip = len(prepare) > 0
     feat = vals[0].shape[2] if flip else vals[0].shape[1]
     out = jax.ShapeDtypeStruct((rows // 2, blocks // CHUNKS, feat, size), BF16)
+    outs = [out] * (2 * CHUNKS)
+    if flip:
+        outs.append(jax.ShapeDtypeStruct((2,) + prepare[2].shape, BF16))
+        outs += [jax.ShapeDtypeStruct((blocks // cols, 2 * size, feat), BF16)] * cols
     return pl.pallas_call(
         functools.partial(spread_kernel, flip, len(vals)),
-        out_shape=[out] * (2 * CHUNKS),
-        in_specs=[SMEM, SMEM, pl.BlockSpec(memory_space=pl.ANY)] + [VMEM] * len(vals),
-        out_specs=[VMEM] * (2 * CHUNKS),
+        out_shape=outs,
+        in_specs=[SMEM, SMEM, pl.BlockSpec(memory_space=pl.ANY)] + [VMEM] * (len(vals) + len(prepare)),
+        out_specs=[VMEM] * len(outs),
         scratch_shapes=[
             pltpu.VMEM((rows * blocks, feat, size), F32),
             pltpu.VMEM(edge_tiles.shape, BF16),
@@ -84,7 +102,7 @@
         compiler_params=PARAMS,
         cost_estimate=pl.CostEstimate(flops=2 * edge_tiles.size * feat, bytes_accessed=40_000_000, transcendentals=0),
         name="spread",
-    )(block_cols, at, edge_tiles, *vals)
+    )(block_cols, at, edge_tiles, *vals, *prepare)
 
 
 def aggregate_kernel(cols_ref, tiles_ref, table_ref, out_ref, held, sems):
@@ -158,33 +176,23 @@
 def dense_kernel(cols, at_ref, weights_ref, *rest):
     sums, rest = rest[:cols], rest[cols:]
     sides, rest = rest[:cols], rest[cols:]
-    outs, rest = rest[:cols], rest[cols:]
-    delta_ref, rest = rest[0], rest[1:]
-    grads, (held, mask) = rest[:cols], rest[cols:]
+    outs, (sum_ref, delta_ref, held, mask) = rest[:cols], rest[cols:]
     col = at_ref[1]
     count, feat, size = sums[0].shape
-    width = cols * feat
     for m in range(cols):
         place = jnp.bitwise_xor(col, m)
         for b in range(count):
-            held[place, b] = sums[m][b]
-            mask[place, b] = sides[m][b, size:].astype(F32).T
-    outer = [weights_ref[q, 0] for q in range(cols)]
-    inner = [weights_ref[q, 1] for q in range(cols)]
-    for b in range(count):
-        stacked = jnp.concatenate([held[q, b] for q in range(cols)], axis=0)
-        for q in range(cols):
-            grad = jnp.dot(outer[q], stacked, preferred_element_type=F32)
-            delta_ref[q, b] = (grad * mask[q, b]).astype(BF16)
-        delta = jnp.concatenate([delta_ref[q, b] for q in range(cols)], axis=0)
-        for q in range(cols):
-            held[q, b] = jnp.dot(inner[q], delta, preferred_element_type=F32).astype(BF16)
-        for m in range(cols):
-            term = jnp.dot(stacked, sides[m][b, :size], preferred_element_type=F32)
-            if b == 0:
-                grads[m][...] = term
-            else:
-                grads[m][...] += term
+            sum_ref[place, :, b * size : (b + 1) * size] = sums[m][b]
+            mask[place, :, b * size : (b + 1) * size] = sides[m][b, size:].astype(F32).T
+    stacked = jnp.concatenate([sum_ref[q] for q in range(cols)], axis=0)
+    for q in range(cols):
+        grad = jnp.dot(weights_ref[q, 0], stacked, preferred_element_type=F32)
+        delta_ref[q] = (grad * mask[q]).astype(BF16)
+    delta = jnp.concatenate([delta_ref[q] for q in range(cols)], axis=0)
+    for q in range(cols):
+        res = jnp.dot(weights_ref[q, 1], delta, preferred_element_type=F32).astype(BF16)
+        for b in range(count):
+            held[q, b] = res[:, b * size : (b + 1) * size]
     for m in range(cols):
         outs[m][...] = held[jnp.bitwise_xor(col, m)]
 
@@ -193,43 +201,46 @@
     cols = len(sums)
     count, feat, size = sums[0].shape
     out = jax.ShapeDtypeStruct((count, feat, size), BF16)
-    delta = jax.ShapeDtypeStruct((cols, count, feat, size), BF16)
-    grad = jax.ShapeDtypeStruct((cols * feat, feat), F32)
+    flat = jax.ShapeDtypeStruct((cols, feat, count * size), BF16)
     res = pl.pallas_call(
         functools.partial(dense_kernel, cols),
-        out_shape=[out] * cols + [delta] + [grad] * cols,
+        out_shape=[out] * cols + [flat] * 2,
         in_specs=[SMEM] + [VMEM] * (1 + 2 * cols),
-        out_specs=[VMEM] * (2 * cols + 1),
-        scratch_shapes=[pltpu.VMEM((cols, count, feat, size), BF16), pltpu.VMEM((cols, count, feat, size), F32)],
+        out_specs=[VMEM] * (cols + 2),
+        scratch_shapes=[pltpu.VMEM((cols, count, feat, size), BF16), pltpu.VMEM((cols, feat, count * size), F32)],
         compiler_params=PARAMS,
         name="dense",
     )(at, weights, *sums, *sides)
-    return res[:cols], res[cols], res[cols + 1 :]
-
-
-def weight_terms_kernel(cols, delta_ref, *rest):
-    sides, grads = rest[:cols], rest[cols:]
-    count = delta_ref.shape[1]
-    for b in range(count):
-        delta = jnp.concatenate([delta_ref[q, b] for q in range(cols)], axis=0)
-        for m in range(cols):
-            term = jnp.dot(delta, sides[m][b], preferred_element_type=F32)
-            if b == 0:
-                grads[m][...] = term
-            else:
-                grads[m][...] += term
-
-
-def weight_terms(delta, sides):
-    cols, _, feat, _ = delta.shape
+    return res[:cols], res[cols], res[cols + 1]
+
+
+def weight_terms_kernel(cols, at_ref, sum_ref, delta_ref, *rest):
+    sides, rest = rest[:cols], rest[cols:]
+    aggs, (keep_ref, send_ref) = rest[:cols], rest[cols:]
+    even = jnp.bitwise_and(at_ref[0], 1) == 0
+    count, size, feat = aggs[0].shape
+    sums = jnp.concatenate([sum_ref[q] for q in range(cols)], axis=0)
+    delta = jnp.concatenate([delta_ref[q] for q in range(cols)], axis=0)
+    for m in range(cols):
+        hidden = jnp.concatenate([sides[m][b, :size] for b in range(count)], axis=0)
+        agg = jnp.concatenate([aggs[m][b] for b in range(count)], axis=0)
+        second = jnp.dot(sums, hidden, preferred_element_type=F32)
+        first = jnp.dot(delta, agg, preferred_element_type=F32)
+        keep_ref[m] = jnp.where(even, second, first).T
+        send_ref[m] = jnp.where(even, first, second).T.astype(BF16)
+
+
+def weight_terms(sums, delta, sides, aggs, at):
+    cols, feat, _ = delta.shape
+    shape = (cols, feat, cols * feat)
     return pl.pallas_call(
         functools.partial(weight_terms_kernel, cols),
-        out_shape=[jax.ShapeDtypeStruct((cols * feat, feat), F32)] * cols,
-        in_specs=[VMEM] * (1 + cols),
-        out_specs=[VMEM] * cols,
+        out_shape=[jax.ShapeDtypeStruct(shape, F32), jax.ShapeDtypeStruct(shape, BF16)],
+        in_specs=[SMEM] + [VMEM] * (2 + 2 * cols),
+        out_specs=[VMEM] * 2,
         compiler_params=PARAMS,
         name="weight_terms",
-    )(delta, *sides)
+    )(at, sums, delta, *sides, *aggs)
 
 
 def swap(value, mask, axis):
@@ -267,23 +278,27 @@
     return done
 
 
-def reduced(terms):
-    got = swap_all([terms[0]] + [t.astype(BF16) for t in terms[1:]], "col")
+def reduced(keep, send, me):
+    terms = keep + swap(send, 1, "row").astype(F32)
+    cols = terms.shape[0]
+    got = swap_all([terms[0]] + [terms[m].astype(BF16) for m in range(1, cols)], "col")
     value = sum(g.astype(F32) for g in got)
-    mask = 1
+    mask = 2
     while mask < lax.axis_size("row"):
         value = value.astype(BF16)
         value = value.astype(F32) + swap(value, mask, "row").astype(F32)
         mask *= 2
-    return value.T
+    other = swap(value, 1, "row")
+    even = me % 2 == 0
+    return jnp.where(even, other, value), jnp.where(even, value, other)
 
 
 def per_device(
     node_feats, hidden_act, grad_out, relu_mask, edge_tiles, block_cols, weight_one, weight_two
 ):
     rows, cols = lax.axis_size("row"), lax.axis_size("col")
-    col = lax.axis_index("col").astype(jnp.int32)
-    at = jnp.stack([lax.axis_index("row").astype(jnp.int32), col])
+    me, col = lax.axis_index("row").astype(jnp.int32), lax.axis_index("col").astype(jnp.int32)
+    at = jnp.stack([me, col])
     blocks, _, size, _ = edge_tiles.shape
     blocked = lambda v: v.reshape(v.shape[0] // size, size, v.shape[1])
 
@@ -291,22 +306,27 @@
         per = blocks // cols
         return [lax.dynamic_slice_in_dim(v, (col ^ m) * per, per, 0) for m in range(cols)]
 
-    weights = lax.all_gather(jnp.stack([weight_two, weight_one]), "col", axis=0)
     table = blocked(lax.all_gather(node_feats, "row", axis=0, tiled=True))
-
-    pieces = spread(edge_tiles, block_cols, [blocked(grad_out)], at, rows, True)
-    both = jnp.concatenate([blocked(hidden_act), blocked(relu_mask).astype(BF16)], axis=1)
-    pieces, both = lax.optimization_barrier((pieces, both))
-    sides = swap_all(by_distance(both), "col")
+    prepare = [blocked(hidden_act), blocked(relu_mask), weight_two, weight_one]
+    pieces = spread(edge_tiles, block_cols, [blocked(grad_out)], at, rows, cols, prepare)
+    pieces, weights, sides = pieces[: 2 * CHUNKS], pieces[2 * CHUNKS], pieces[2 * CHUNKS + 1 :]
+    weights = lax.all_gather(weights, "col", axis=0)
+    sides = swap_all(sides, "col")
     sums = finish(scatter(pieces, rows), at, cols)
+    sums, sides = lax.optimization_barrier((sums, sides))
     sums = swap_all(sums, "col")
-    spread_in, delta, second_terms = dense(weights, sums, sides, at)
+    agg_feats = aggregate(edge_tiles, block_cols, table)
+    sums, agg_feats = lax.optimization_barrier((sums, agg_feats))
+    spread_in, sums, delta = dense(weights, sums, sides, at)
+    agg_feats = swap_all(by_distance(agg_feats), "col")
+    spread_in, agg_feats = lax.optimization_barrier((spread_in, agg_feats))
     back = swap_all(spread_in, "col")
-    agg_feats = by_distance(aggregate(edge_tiles, block_cols, table))
-    first_terms = weight_terms(delta, swap_all(agg_feats, "col"))
-    pieces = spread(edge_tiles, block_cols, back, at, rows, False)
+    terms = weight_terms(sums, delta, sides, agg_feats, at)
+    back, terms = lax.optimization_barrier((back, terms))
+    pieces = spread(edge_tiles, block_cols, back, at, rows, cols)
     (out,) = finish(scatter(pieces, rows), at, 0)
-    return out.reshape(node_feats.shape), reduced(first_terms), reduced(second_terms)
+    first_grad, second_grad = reduced(*terms, me)
+    return out.reshape(node_feats.shape), first_grad, second_grad
 
 
 def solution(mesh):

time: 188 us -> 206 us (1.096)
  waiting for transfers between devices: 81.5 us -> 92.8 us
  local copies, waits for them, and re-layouts: 5.22 us -> 10.2 us
  other arithmetic: 10.3 us -> 5.92 us
  starting transfers between devices: 50.9 us -> 55.1 us
    ppermute x36 -> x31, waiting for transfers between devices: 80.8 us -> 92.1 us  [swap(): lax.ppermute(value, axis, [(i, i ^ mask) for i in range(lax.axis_size(axi...]
    unnamed x12 -> x22, local copies, waits for them, and re-layouts: 5.1 us -> 10.1 us
    ppermute x36 -> x31, starting transfers between devices: 50.8 us -> 55 us  [swap(): lax.ppermute(value, axis, [(i, i ^ mask) for i in range(lax.axis_size(axi...]
    convert_element_type x8, other arithmetic: 6.72 us -> 4.65 us  [add(): return (a.astype(F32) + b.astype(F32)).astype(BF16)]
  transfers between devices with their start and end apart: 38 -> 33, of which waited for: 21 -> 17; matrix products, arithmetic and copies ran while one was open for 5% -> 3% of each run, Pallas kernels for 14% -> 12%
where the time goes in v3:
time: 206 us; the launch traced here: 205 us
  waiting for transfers between devices  92.8 us (45%)
  starting transfers between devices  55.1 us (27%)
  Pallas kernels  26.8 us (13%)
  between operations  14.3 us (7%)
  local copies, waits for them, and re-layouts  10.2 us (5%)
  other arithmetic  5.92 us (3%)
    ppermute x31, waiting for transfers between devices, swap(): lax.ppermute(value, axis, [(i, i ^ mask) for i in range(lax.axis_size(axi...  92.1 us
    ppermute x31, starting transfers between devices, swap(): lax.ppermute(value, axis, [(i, i ^ mask) for i in range(lax.axis_size(axi...  55 us
    pallas_call x2, Pallas kernels, spread(): pl.pallas_call(functools.partial(spread_kernel, flip, len(vals)), out_sha...  15.2 us
    unnamed x22, local copies, waits for them, and re-layouts  10.1 us
    pallas_call x1, Pallas kernels, aggregate(): pl.pallas_call(aggregate_kernel, out_shape=jax.ShapeDtypeStruct((blocks,...  5.8 us
    convert_element_type x8, other arithmetic, add(): return (a.astype(F32) + b.astype(F32)).astype(BF16)  4.65 us
  transfers between devices with their start and end apart: 33, of which 17 were waited for; matrix products, arithmetic and copies ran while one was open for 3% of the time, Pallas kernels for 12%

profile of v3, /device:TPU:0, one launch (start us, length us, event | category | flops | bytes accessed | tf_op | source)
XLA Modules:
  0.0 205.1 jit_solution(1976746031685014981)
XLA Ops:
  7.2 0.7 all-gather.4.cloned.1.call-update
  8.0 1.0 copy-done.2
  9.1 1.0 copy-done.3
  10.1 0.9 copy-done.4
  11.0 0.9 copy-done.5
  11.9 0.7 copy-done.6
  12.6 8.6 %spread.2 = (bf16[4,8,128,128]{3,2,1,0:T(8,128)(2,1)S(1)}, bf16[4,8,128,128]{3,2,1,0:T(8,128)(2,1)S(1)}, bf16[4,8,128,128]{3,2,1,0:T(8,128)(2,1)S(1)}, bf16[4,8,...) custom-call(s32[16,20]{1,0:T(8,128)S(1)} %copy-done.6, ...), custom_call_target="tpu_custom_call" | custom-call | flops 1342177280 | bytes 40000000 | tf_op jit(solution)/shard_map/spread/pallas_call | solution.py:91
  21.3 0.7 copy-done.8
  22.0 0.7 copy-done.9
  22.7 0.7 copy-done.10
  23.4 0.5 collective-permute-start.3
  23.9 3.5 %collective-permute-done.3 = bf16[4,8,128,128]{3,2,1,0:T(8,128)(2,1)} collective-permute-done((bf16[4,8,128,128]{3,2,1,0:T(8,128)(2,1)}, bf16[4,8,128,128]{3,2,1,0:T(8,128)(2,1)}, u32[]{:S(2)}, u32[]{:S(2)}) %collective-permute-start.3) | collective-permute-done | bytes 1048608 | tf_op jit(solution)/shard_map/ppermute | solution.py:247
  27.4 1.6 add_convert_fusion.5
  29.0 3.5 %collective-permute-start.4 = (bf16[2,8,128,128]{3,2,1,0:T(8,128)(2,1)S(1)}, bf16[2,8,128,128]{3,2,1,0:T(8,128)(2,1)S(1)}, u32[]{:S(2)}, u32[]{:S(2)}) collective-permute-start(bf16[2,8,128,128]{3,2,1,0:T(8,128)(2,1)S(1)} %get-tuple-element.114), channel_id=1, source_target_pairs={{0,16},{4,20},{8,24},{12,28},{16,0},{20,4},{24,8},{28,12},{1,17},{... | collective-permute-start | bytes 1572872 | tf_op jit(solution)/shard_map/ppermute | solution.py:247
  32.5 1.6 add_convert_fusion.7
  34.1 1.6 collective-permute-start.1
  35.6 18.9 %collective-permute-done.4 = bf16[2,8,128,128]{3,2,1,0:T(8,128)(2,1)S(1)} collective-permute-done((bf16[2,8,128,128]{3,2,1,0:T(8,128)(2,1)S(1)}, bf16[2,8,128,128]{3,2,1,0:T(8,128)(2,1)S(1)}, u32[]{:S(2)}, u32[]{:S(2)}) %collective-permute-start.4) | collective-permute-done | bytes 524320 | tf_op jit(solution)/shard_map/ppermute | solution.py:247
  54.6 1.4 collective-permute-start.5
  56.0 3.2 %collective-permute-done.1 = bf16[2,8,128,128]{3,2,1,0:T(8,128)(2,1)S(1)} collective-permute-done((bf16[2,8,128,128]{3,2,1,0:T(8,128)(2,1)S(1)}, bf16[2,8,128,128]{3,2,1,0:T(8,128)(2,1)S(1)}, u32[]{:S(2)}, u32[]{:S(2)}) %collective-permute-start.1) | collective-permute-done | bytes 524320 | tf_op jit(solution)/shard_map/ppermute | solution.py:247
  59.3 0.6 collective-permute-start.2
  60.0 2.1 %collective-permute-start.6 = (bf16[4,256,128]{2,1,0:T(8,128)(2,1)}, bf16[4,256,128]{2,1,0:T(8,128)(2,1)S(1)}, u32[]{:S(2)}, u32[]{:S(2)}) collective-permute-start(bf16[4,256,128]{2,1,0:T(8,128)(2,1)} %copy-done.10), channel_id=1, source_target_pairs={{0,1},{1,0},{2,3},{3,2},{4,5},{5,4},{6,7},{7,6},{8,9},{9,8},{10,11... | collective-permute-start | bytes 786440 | tf_op jit(solution)/shard_map/ppermute | solution.py:247
  62.0 2.4 %collective-permute-start.7 = (bf16[4,256,128]{2,1,0:T(8,128)(2,1)}, bf16[4,256,128]{2,1,0:T(8,128)(2,1)S(1)}, u32[]{:S(2)}, u32[]{:S(2)}) collective-permute-start(bf16[4,256,128]{2,1,0:T(8,128)(2,1)} %copy-done.9), channel_id=1, source_target_pairs={{0,2},{1,3},{2,0},{3,1},{4,6},{5,7},{6,4},{7,5},{8,10},{9,11},{10,... | collective-permute-start | bytes 786440 | tf_op jit(solution)/shard_map/ppermute | solution.py:247
  64.5 2.7 %collective-permute-done.2.rest_1_ = bf16[8,128,128]{2,1,0:T(8,128)(2,1)S(1)} collective-permute-done((bf16[8,128,128]{2,1,0:T(8,128)(2,1)S(1)}, bf16[8,128,128]{2,1,0:T(8,128)(2,1)S(1)}, u32[]{:S(2)}, u32[]{:S(2)}) %collective-permute-start.2) | collective-permute-done | bytes 262176 | tf_op jit(solution)/shard_map/ppermute | solution.py:247
  67.1 0.8 finish.2
  67.9 3.5 %collective-permute-done.6.rest_5_.rest_1_ = bf16[4,256,128]{2,1,0:T(8,128)(2,1)S(1)} collective-permute-done((bf16[4,256,128]{2,1,0:T(8,128)(2,1)}, bf16[4,256,128]{2,1,0:T(8,128)(2,1)S(1)}, u32[]{:S(2)}, u32[]{:S(2)}) %collective-permute-start.6) | collective-permute-done | bytes 262176 | tf_op jit(solution)/shard_map/ppermute | solution.py:247
  71.4 20.0 %collective-permute-done.7.rest_6_.rest_2_ = bf16[4,256,128]{2,1,0:T(8,128)(2,1)S(1)} collective-permute-done((bf16[4,256,128]{2,1,0:T(8,128)(2,1)}, bf16[4,256,128]{2,1,0:T(8,128)(2,1)S(1)}, u32[]{:S(2)}, u32[]{:S(2)}) %collective-permute-start.7) | collective-permute-done | bytes 262176 | tf_op jit(solution)/shard_map/ppermute | solution.py:247
  91.4 18.5 %collective-permute-start.10 = (bf16[4,128,128]{2,1,0:T(8,128)(2,1)S(1)}, bf16[4,128,128]{2,1,0:T(8,128)(2,1)S(1)}, u32[]{:S(2)}, u32[]{:S(2)}) collective-permute-start(bf16[4,128,128]{2,1,0:T(8,128)(2,1)S(1)} %get-tuple-element.70), channel_id=1, source_target_pairs={{0,2},{1,3},{2,0},{3,1},{4,6},{5,7},{6,4},{7,5},{8,10},{9,11},{10,... | collective-permute-start | bytes 393224 | tf_op jit(solution)/shard_map/ppermute | solution.py:247
  109.9 0.9 collective-permute-start.11
  110.8 2.2 %copy-done = bf16[16384,128]{1,0:T(8,128)(2,1)S(1)} copy-done((bf16[16384,128]{1,0:T(8,128)(2,1)S(1)}, bf16[16384,128]{1,0:T(8,128)(2,1)}, u32[]{:S(2)}) %copy-start) | copy-done | bytes 4194328
  112.9 5.8 %aggregate.1 = bf16[16,128,128]{2,1,0:T(8,128)(2,1)S(1)} custom-call(s32[16,20]{1,0:T(8,128)S(1)} %copy-done.7, bf16[16,20,128,128]{3,2,1,0:T(8,128)(2,1)} %tiles_ref.5, bf16[128,128,128]{2,1,0:T(8,128)(2,1)S(1)} %bitcast.68), custom_call_target="tpu_custom_call" | custom-call | flops 1342177280 | bytes 30000000 | tf_op jit(solution)/shard_map/aggregate/pallas_call | solution.py:128
  118.8 3.5 %collective-permute-start.12 = (bf16[4,128,128]{2,1,0:T(8,128)(2,1)S(1)}, bf16[4,128,128]{2,1,0:T(8,128)(2,1)S(1)}, u32[]{:S(2)}, u32[]{:S(2)}) collective-permute-start(bf16[4,128,128]{2,1,0:T(8,128)(2,1)S(1)} %get-tuple-element.132), channel_id=1, source_target_pairs={{0,1},{1,0},{2,3},{3,2},{4,5},{5,4},{6,7},{7,6},{8,9},{9,8},{10,11... | collective-permute-start | bytes 393224 | tf_op jit(solution)/shard_map/ppermute | solution.py:247
  122.3 0.4 collective-permute-start.13
  122.7 2.1 %collective-permute-start.14 = (bf16[4,128,128]{2,1,0:T(8,128)(2,1)S(1)}, bf16[4,128,128]{2,1,0:T(8,128)(2,1)S(1)}, u32[]{:S(2)}, u32[]{:S(2)}) collective-permute-start(bf16[4,128,128]{2,1,0:T(8,128)(2,1)S(1)} %get-tuple-element.130), channel_id=1, source_target_pairs={{0,3},{1,2},{2,1},{3,0},{4,7},{5,6},{6,5},{7,4},{8,11},{9,10},{10,... | collective-permute-start | bytes 393224 | tf_op jit(solution)/shard_map/ppermute | solution.py:247
  124.8 1.2 copy-done.1
  126.0 1.5 dense.1
  127.5 0.9 collective-permute-done.12.rest_5_
  128.4 6.8 %collective-permute-done.13.rest_6_ = bf16[4,128,128]{2,1,0:T(8,128)(2,1)S(1)} collective-permute-done((bf16[4,128,128]{2,1,0:T(8,128)(2,1)S(1)}, bf16[4,128,128]{2,1,0:T(8,128)(2,1)S(1)}, u32[]{:S(2)}, u32[]{:S(2)}) %collective-permute-start.13) | collective-permute-done | bytes 131104 | tf_op jit(solution)/shard_map/ppermute | solution.py:247
  135.2 2.9 %collective-permute-start.15 = (bf16[4,128,128]{2,1,0:T(8,128)(2,1)S(1)}, bf16[4,128,128]{2,1,0:T(8,128)(2,1)S(1)}, u32[]{:S(2)}, u32[]{:S(2)}) collective-permute-start(bf16[4,128,128]{2,1,0:T(8,128)(2,1)S(1)} %get-tuple-element.86), channel_id=1, source_target_pairs={{0,1},{1,0},{2,3},{3,2},{4,5},{5,4},{6,7},{7,6},{8,9},{9,8},{10,11... | collective-permute-start | bytes 393224 | tf_op jit(solution)/shard_map/ppermute | solution.py:247
  138.2 2.3 %collective-permute-start.17 = (bf16[4,128,128]{2,1,0:T(8,128)(2,1)S(1)}, bf16[4,128,128]{2,1,0:T(8,128)(2,1)S(1)}, u32[]{:S(2)}, u32[]{:S(2)}) collective-permute-start(bf16[4,128,128]{2,1,0:T(8,128)(2,1)S(1)} %get-tuple-element.88), channel_id=1, source_target_pairs={{0,3},{1,2},{2,1},{3,0},{4,7},{5,6},{6,5},{7,4},{8,11},{9,10},{10,... | collective-permute-start | bytes 393224 | tf_op jit(solution)/shard_map/ppermute | solution.py:247
  140.4 1.9 weight_terms.1
  142.4 4.4 %collective-permute-done.16.rest_2_ = bf16[4,128,128]{2,1,0:T(8,128)(2,1)S(1)} collective-permute-done((bf16[4,128,128]{2,1,0:T(8,128)(2,1)S(1)}, bf16[4,128,128]{2,1,0:T(8,128)(2,1)S(1)}, u32[]{:S(2)}, u32[]{:S(2)}) %collective-permute-start.16) | collective-permute-done | bytes 131104 | tf_op jit(solution)/shard_map/ppermute | solution.py:247
  146.8 6.6 %spread.3 = (bf16[4,8,128,128]{3,2,1,0:T(8,128)(2,1)S(1)}, bf16[4,8,128,128]{3,2,1,0:T(8,128)(2,1)S(1)}, bf16[4,8,128,128]{3,2,1,0:T(8,128)(2,1)S(1)}, bf16[4,8,128,128]{3,2,1,0:T(8,128)(2,1)S(1)}) custom-call(s32[16,20]{1,0:T(8,128)S(1)} %copy-done.7, s32[2]{0:T(128)S(1)} %pad_add_fusion.at_ref, bf16[16,20,128,128]{3,2,1,0:T(8,128)(2,1)} %tiles_ref.5, ...), custom_call_target="tpu_custom_call" | custom-call | flops 1342177280 | bytes 40000000 | tf_op jit(solution)/shard_map/spread/pallas_call | solution.py:91
  153.4 0.6 collective-permute-start.21
  154.0 0.2 fusion.18
  154.3 2.0 collective-permute-start.25
  156.3 0.2 collective-permute-start.26
  156.5 2.3 %collective-permute-start.27 = (bf16[128,512]{1,0:T(8,128)(2,1)S(1)}, bf16[128,512]{1,0:T(8,128)(2,1)S(1)}, u32[]{:S(2)}, u32[]{:S(2)}) collective-permute-start(bf16[128,512]{1,0:T(8,128)(2,1)S(1)} %get-tuple-element.128), channel_id=1, source_target_pairs={{0,3},{1,2},{2,1},{3,0},{4,7},{5,6},{6,5},{7,4},{8,11},{9,10},{10,... | collective-permute-start | bytes 393224 | tf_op jit(solution)/shard_map/ppermute | solution.py:247
  158.7 3.3 %collective-permute-done.25 = bf16[128,512]{1,0:T(8,128)(2,1)S(1)} collective-permute-done((bf16[128,512]{1,0:T(8,128)(2,1)S(1)}, bf16[128,512]{1,0:T(8,128)(2,1)S(1)}, u32[]{:S(2)}, u32[]{:S(2)}) %collective-permute-start.25) | collective-permute-done | bytes 131104 | tf_op jit(solution)/shard_map/ppermute | solution.py:247
  162.0 7.2 %collective-permute-done.26 = bf16[128,512]{1,0:T(8,128)(2,1)S(1)} collective-permute-done((bf16[128,512]{1,0:T(8,128)(2,1)S(1)}, bf16[128,512]{1,0:T(8,128)(2,1)S(1)}, u32[]{:S(2)}, u32[]{:S(2)}) %collective-permute-start.26) | collective-permute-done | bytes 131104 | tf_op jit(solution)/shard_map/ppermute | solution.py:247
  169.3 1.5 collective-permute-start.28
  170.7 3.6 %collective-permute-done.28 = bf16[128,512]{1,0:T(8,128)(2,1)S(1)} collective-permute-done((bf16[128,512]{1,0:T(8,128)(2,1)S(1)}, bf16[128,512]{1,0:T(8,128)(2,1)S(1)}, u32[]{:S(2)}, u32[]{:S(2)}) %collective-permute-start.28) | collective-permute-done | bytes 131104 | tf_op jit(solution)/shard_map/ppermute | solution.py:247
  174.4 1.5 collective-permute-start.29
  175.8 0.5 add_convert_fusion.1
  176.3 0.7 collective-permute-start.22
  177.0 0.5 add_convert_fusion.3
  177.4 1.5 collective-permute-start.19
  178.9 1.9 collective-permute-done.29
  181.0 7.7 %collective-permute-done.22 = bf16[2,8,128,128]{3,2,1,0:T(8,128)(2,1)S(1)} collective-permute-done((bf16[2,8,128,128]{3,2,1,0:T(8,128)(2,1)S(1)}, bf16[2,8,128,128]{3,2,1,0:T(8,128)(2,1)S(1)}, u32[]{:S(2)}, u32[]{:S(2)}) %collective-permute-start.22) | collective-permute-done | bytes 524320 | tf_op jit(solution)/shard_map/ppermute | solution.py:247
  188.9 1.2 collective-permute-start.23
  190.2 0.9 collective-permute-start.20
  191.2 0.9 broadcast_select_fusion
  192.0 3.3 %collective-permute-done.23.rest_3_ = bf16[8,128,128]{2,1,0:T(8,128)(2,1)S(1)} collective-permute-done((bf16[8,128,128]{2,1,0:T(8,128)(2,1)S(1)}, bf16[8,128,128]{2,1,0:T(8,128)(2,1)S(1)}, u32[]{:S(2)}, u32[]{:S(2)}) %collective-permute-start.23) | collective-permute-done | bytes 262176 | tf_op jit(solution)/shard_map/ppermute | solution.py:247
  195.3 1.4 collective-permute-done.20.rest_1_
  196.7 1.6 finish.3
  (49 shorter events, 1.4 us)
Async XLA Ops:
  7.2 103.6 %all-gather.4.cloned.1.call-start = ((), (), s32[]{:S(2)}) async-start(), calls=%async_computation | async-start | bytes 4718592 | tf_op jit(solution)/shard_map/all_gather | solution.py:309
  7.9 116.9 %all-gather.6.cloned.1.call-start = ((), (), s32[]{:S(2)}) async-start(), calls=%async_computation.1 | async-start | bytes 1310720 | tf_op jit(solution)/shard_map/all_gather | solution.py:313
  8.0 1.0 copy-start.2
  9.1 1.0 copy-start.3
  10.1 0.9 copy-start.4
  11.0 0.9 copy-start.5
  11.9 0.7 copy-start.6
  12.6 98.1 %copy-start.7 = (s32[16,20]{1,0:T(8,128)S(1)}, s32[16,20]{1,0:T(8,128)}, u32[]{:S(2)}) copy-start(s32[16,20]{1,0:T(8,128)} %cols_ref.5) | copy-start | bytes 3844
  21.3 0.7 copy-start.8
  22.0 0.7 copy-start.9
  22.7 0.7 copy-start.10
  23.4 4.0 %collective-permute-start.3 = (bf16[4,8,128,128]{3,2,1,0:T(8,128)(2,1)}, bf16[4,8,128,128]{3,2,1,0:T(8,128)(2,1)}, u32[]{:S(2)}, u32[]{:S(2)}) collective-permute-start(bf16[4,8,128,128]{3,2,1,0:T(8,128)(2,1)} %get-tuple-element.59), channel_id=1, source_target_pairs={{0,4},{4,0},{8,12},{12,8},{16,20},{20,16},{24,28},{28,24},{1,5},{5... | collective-permute-start | bytes 3145736 | tf_op jit(solution)/shard_map/ppermute | solution.py:247
  23.8 8.6 %collective-permute-start = (bf16[4,8,128,128]{3,2,1,0:T(8,128)(2,1)S(1)}, bf16[4,8,128,128]{3,2,1,0:T(8,128)(2,1)}, u32[]{:S(2)}, u32[]{:S(2)}) collective-permute-start(bf16[4,8,128,128]{3,2,1,0:T(8,128)(2,1)S(1)} %get-tuple-element.57), channel_id=1, source_target_pairs={{0,4},{4,0},{8,12},{12,8},{16,20},{20,16},{24,28},{28,24},{1,5},{5... | collective-permute-start | bytes 3145736 | tf_op jit(solution)/shard_map/ppermute | solution.py:247
  29.0 25.5 %collective-permute-start.4 = (bf16[2,8,128,128]{3,2,1,0:T(8,128)(2,1)S(1)}, bf16[2,8,128,128]{3,2,1,0:T(8,128)(2,1)S(1)}, u32[]{:S(2)}, u32[]{:S(2)}) collective-permute-start(bf16[2,8,128,128]{3,2,1,0:T(8,128)(2,1)S(1)} %get-tuple-element.114), channel_id=1, source_target_pairs={{0,16},{4,20},{8,24},{12,28},{16,0},{20,4},{24,8},{28,12},{1,17},{... | collective-permute-start | bytes 1572872 | tf_op jit(solution)/shard_map/ppermute | solution.py:247
  34.1 25.1 %collective-permute-start.1 = (bf16[2,8,128,128]{3,2,1,0:T(8,128)(2,1)S(1)}, bf16[2,8,128,128]{3,2,1,0:T(8,128)(2,1)S(1)}, u32[]{:S(2)}, u32[]{:S(2)}) collective-permute-start(bf16[2,8,128,128]{3,2,1,0:T(8,128)(2,1)S(1)} %get-tuple-element.116), channel_id=1, source_target_pairs={{0,8},{4,12},{8,0},{12,4},{16,24},{20,28},{24,16},{28,20},{1,9},{5... | collective-permute-start | bytes 1572872 | tf_op jit(solution)/shard_map/ppermute | solution.py:247
  54.6 9.8 %collective-permute-start.5 = (bf16[8,128,128]{2,1,0:T(8,128)(2,1)S(1)}, bf16[8,128,128]{2,1,0:T(8,128)(2,1)S(1)}, u32[]{:S(2)}, u32[]{:S(2)}) collective-permute-start(bf16[8,128,128]{2,1,0:T(8,128)(2,1)S(1)} %get-tuple-element.121), channel_id=1, source_target_pairs={{0,8},{4,12},{8,0},{12,4},{16,24},{20,28},{24,16},{28,20},{1,9},{5... | collective-permute-start | bytes 786440 | tf_op jit(solution)/shard_map/ppermute | solution.py:247
  59.3 7.8 %collective-permute-start.2 = (bf16[8,128,128]{2,1,0:T(8,128)(2,1)S(1)}, bf16[8,128,128]{2,1,0:T(8,128)(2,1)S(1)}, u32[]{:S(2)}, u32[]{:S(2)}) collective-permute-start(bf16[8,128,128]{2,1,0:T(8,128)(2,1)S(1)} %get-tuple-element.123), channel_id=1, source_target_pairs={{0,16},{4,20},{8,24},{12,28},{16,0},{20,4},{24,8},{28,12},{1,17},{... | collective-permute-start | bytes 786440 | tf_op jit(solution)/shard_map/ppermute | solution.py:247
  60.0 11.4 %collective-permute-start.6 = (bf16[4,256,128]{2,1,0:T(8,128)(2,1)}, bf16[4,256,128]{2,1,0:T(8,128)(2,1)S(1)}, u32[]{:S(2)}, u32[]{:S(2)}) collective-permute-start(bf16[4,256,128]{2,1,0:T(8,128)(2,1)} %copy-done.10), channel_id=1, source_target_pairs={{0,1},{1,0},{2,3},{3,2},{4,5},{5,4},{6,7},{7,6},{8,9},{9,8},{10,11... | collective-permute-start | bytes 786440 | tf_op jit(solution)/shard_map/ppermute | solution.py:247
  62.0 29.4 %collective-permute-start.7 = (bf16[4,256,128]{2,1,0:T(8,128)(2,1)}, bf16[4,256,128]{2,1,0:T(8,128)(2,1)S(1)}, u32[]{:S(2)}, u32[]{:S(2)}) collective-permute-start(bf16[4,256,128]{2,1,0:T(8,128)(2,1)} %copy-done.9), channel_id=1, source_target_pairs={{0,2},{1,3},{2,0},{3,1},{4,6},{5,7},{6,4},{7,5},{8,10},{9,11},{10,... | collective-permute-start | bytes 786440 | tf_op jit(solution)/shard_map/ppermute | solution.py:247
  64.4 27.0 %collective-permute-start.8 = (bf16[4,256,128]{2,1,0:T(8,128)(2,1)}, bf16[4,256,128]{2,1,0:T(8,128)(2,1)S(1)}, u32[]{:S(2)}, u32[]{:S(2)}) collective-permute-start(bf16[4,256,128]{2,1,0:T(8,128)(2,1)} %copy-done.8), channel_id=1, source_target_pairs={{0,3},{1,2},{2,1},{3,0},{4,7},{5,6},{6,5},{7,4},{8,11},{9,10},{10,... | collective-permute-start | bytes 786440 | tf_op jit(solution)/shard_map/ppermute | solution.py:247
  91.4 27.4 %collective-permute-start.10 = (bf16[4,128,128]{2,1,0:T(8,128)(2,1)S(1)}, bf16[4,128,128]{2,1,0:T(8,128)(2,1)S(1)}, u32[]{:S(2)}, u32[]{:S(2)}) collective-permute-start(bf16[4,128,128]{2,1,0:T(8,128)(2,1)S(1)} %get-tuple-element.70), channel_id=1, source_target_pairs={{0,2},{1,3},{2,0},{3,1},{4,6},{5,7},{6,4},{7,5},{8,10},{9,11},{10,... | collective-permute-start | bytes 393224 | tf_op jit(solution)/shard_map/ppermute | solution.py:247
  109.9 8.9 %collective-permute-start.11 = (bf16[4,128,128]{2,1,0:T(8,128)(2,1)S(1)}, bf16[4,128,128]{2,1,0:T(8,128)(2,1)S(1)}, u32[]{:S(2)}, u32[]{:S(2)}) collective-permute-start(bf16[4,128,128]{2,1,0:T(8,128)(2,1)S(1)} %get-tuple-element.71), channel_id=1, source_target_pairs={{0,3},{1,2},{2,1},{3,0},{4,7},{5,6},{6,5},{7,4},{8,11},{9,10},{10,... | collective-permute-start | bytes 393224 | tf_op jit(solution)/shard_map/ppermute | solution.py:247
  110.7 8.0 %collective-permute-start.9 = (bf16[4,128,128]{2,1,0:T(8,128)(2,1)S(1)}, bf16[4,128,128]{2,1,0:T(8,128)(2,1)S(1)}, u32[]{:S(2)}, u32[]{:S(2)}) collective-permute-start(bf16[4,128,128]{2,1,0:T(8,128)(2,1)S(1)} %get-tuple-element.69), channel_id=1, source_target_pairs={{0,1},{1,0},{2,3},{3,2},{4,5},{5,4},{6,7},{7,6},{8,9},{9,8},{10,11... | collective-permute-start | bytes 393224 | tf_op jit(solution)/shard_map/ppermute | solution.py:247
  110.7 2.2 %copy-start = (bf16[16384,128]{1,0:T(8,128)(2,1)S(1)}, bf16[16384,128]{1,0:T(8,128)(2,1)}, u32[]{:S(2)}) copy-start(bf16[16384,128]{1,0:T(8,128)(2,1)} %all-gather.4.cloned.1.call-done) | copy-start | bytes 12582916
  118.8 9.6 %collective-permute-start.12 = (bf16[4,128,128]{2,1,0:T(8,128)(2,1)S(1)}, bf16[4,128,128]{2,1,0:T(8,128)(2,1)S(1)}, u32[]{:S(2)}, u32[]{:S(2)}) collective-permute-start(bf16[4,128,128]{2,1,0:T(8,128)(2,1)S(1)} %get-tuple-element.132), channel_id=1, source_target_pairs={{0,1},{1,0},{2,3},{3,2},{4,5},{5,4},{6,7},{7,6},{8,9},{9,8},{10,11... | collective-permute-start | bytes 393224 | tf_op jit(solution)/shard_map/ppermute | solution.py:247
  122.3 12.9 %collective-permute-start.13 = (bf16[4,128,128]{2,1,0:T(8,128)(2,1)S(1)}, bf16[4,128,128]{2,1,0:T(8,128)(2,1)S(1)}, u32[]{:S(2)}, u32[]{:S(2)}) collective-permute-start(bf16[4,128,128]{2,1,0:T(8,128)(2,1)S(1)} %get-tuple-element.131), channel_id=1, source_target_pairs={{0,2},{1,3},{2,0},{3,1},{4,6},{5,7},{6,4},{7,5},{8,10},{9,11},{10,... | collective-permute-start | bytes 393224 | tf_op jit(solution)/shard_map/ppermute | solution.py:247
  122.7 12.5 %collective-permute-start.14 = (bf16[4,128,128]{2,1,0:T(8,128)(2,1)S(1)}, bf16[4,128,128]{2,1,0:T(8,128)(2,1)S(1)}, u32[]{:S(2)}, u32[]{:S(2)}) collective-permute-start(bf16[4,128,128]{2,1,0:T(8,128)(2,1)S(1)} %get-tuple-element.130), channel_id=1, source_target_pairs={{0,3},{1,2},{2,1},{3,0},{4,7},{5,6},{6,5},{7,4},{8,11},{9,10},{10,... | collective-permute-start | bytes 393224 | tf_op jit(solution)/shard_map/ppermute | solution.py:247
  124.8 1.2 copy-start.1
  135.2 7.2 %collective-permute-start.15 = (bf16[4,128,128]{2,1,0:T(8,128)(2,1)S(1)}, bf16[4,128,128]{2,1,0:T(8,128)(2,1)S(1)}, u32[]{:S(2)}, u32[]{:S(2)}) collective-permute-start(bf16[4,128,128]{2,1,0:T(8,128)(2,1)S(1)} %get-tuple-element.86), channel_id=1, source_target_pairs={{0,1},{1,0},{2,3},{3,2},{4,5},{5,4},{6,7},{7,6},{8,9},{9,8},{10,11... | collective-permute-start | bytes 393224 | tf_op jit(solution)/shard_map/ppermute | solution.py:247
  138.1 8.7 %collective-permute-start.16 = (bf16[4,128,128]{2,1,0:T(8,128)(2,1)S(1)}, bf16[4,128,128]{2,1,0:T(8,128)(2,1)S(1)}, u32[]{:S(2)}, u32[]{:S(2)}) collective-permute-start(bf16[4,128,128]{2,1,0:T(8,128)(2,1)S(1)} %get-tuple-element.87), channel_id=1, source_target_pairs={{0,2},{1,3},{2,0},{3,1},{4,6},{5,7},{6,4},{7,5},{8,10},{9,11},{10,... | collective-permute-start | bytes 393224 | tf_op jit(solution)/shard_map/ppermute | solution.py:247
  138.2 8.6 %collective-permute-start.17 = (bf16[4,128,128]{2,1,0:T(8,128)(2,1)S(1)}, bf16[4,128,128]{2,1,0:T(8,128)(2,1)S(1)}, u32[]{:S(2)}, u32[]{:S(2)}) collective-permute-start(bf16[4,128,128]{2,1,0:T(8,128)(2,1)S(1)} %get-tuple-element.88), channel_id=1, source_target_pairs={{0,3},{1,2},{2,1},{3,0},{4,7},{5,6},{6,5},{7,4},{8,11},{9,10},{10,... | collective-permute-start | bytes 393224 | tf_op jit(solution)/shard_map/ppermute | solution.py:247
  146.8 7.2 %collective-permute-start.24 = (bf16[4,128,512]{2,1,0:T(8,128)(2,1)S(1)}, bf16[4,128,512]{2,1,0:T(8,128)(2,1)S(1)}, u32[]{:S(2)}, u32[]{:S(2)}) collective-permute-start(bf16[4,128,512]{2,1,0:T(8,128)(2,1)S(1)} %get-tuple-element.106), channel_id=1, source_target_pairs={{0,4},{4,0},{8,12},{12,8},{16,20},{20,16},{24,28},{28,24},{1,5},{5... | collective-permute-start | bytes 1572872 | tf_op jit(solution)/shard_map/ppermute | solution.py:247
  153.4 22.5 %collective-permute-start.21 = (bf16[4,8,128,128]{3,2,1,0:T(8,128)(2,1)S(1)}, bf16[4,8,128,128]{3,2,1,0:T(8,128)(2,1)S(1)}, u32[]{:S(2)}, u32[]{:S(2)}) collective-permute-start(bf16[4,8,128,128]{3,2,1,0:T(8,128)(2,1)S(1)} %get-tuple-element.104), channel_id=1, source_target_pairs={{0,4},{4,0},{8,12},{12,8},{16,20},{20,16},{24,28},{28,24},{1,5},{5... | collective-permute-start | bytes 3145736 | tf_op jit(solution)/shard_map/ppermute | solution.py:247
  153.9 23.1 %collective-permute-start.18 = (bf16[4,8,128,128]{3,2,1,0:T(8,128)(2,1)S(1)}, bf16[4,8,128,128]{3,2,1,0:T(8,128)(2,1)S(1)}, u32[]{:S(2)}, u32[]{:S(2)}) collective-permute-start(bf16[4,8,128,128]{3,2,1,0:T(8,128)(2,1)S(1)} %get-tuple-element.102), channel_id=1, source_target_pairs={{0,4},{4,0},{8,12},{12,8},{16,20},{20,16},{24,28},{28,24},{1,5},{5... | collective-permute-start | bytes 3145736 | tf_op jit(solution)/shard_map/ppermute | solution.py:247
  154.3 7.7 %collective-permute-start.25 = (bf16[128,512]{1,0:T(8,128)(2,1)S(1)}, bf16[128,512]{1,0:T(8,128)(2,1)S(1)}, u32[]{:S(2)}, u32[]{:S(2)}) collective-permute-start(bf16[128,512]{1,0:T(8,128)(2,1)S(1)} %get-tuple-element.127), channel_id=1, source_target_pairs={{0,1},{1,0},{2,3},{3,2},{4,5},{5,4},{6,7},{7,6},{8,9},{9,8},{10,11... | collective-permute-start | bytes 393224 | tf_op jit(solution)/shard_map/ppermute | solution.py:247
  156.3 12.9 %collective-permute-start.26 = (bf16[128,512]{1,0:T(8,128)(2,1)S(1)}, bf16[128,512]{1,0:T(8,128)(2,1)S(1)}, u32[]{:S(2)}, u32[]{:S(2)}) collective-permute-start(bf16[128,512]{1,0:T(8,128)(2,1)S(1)} %get-tuple-element.129), channel_id=1, source_target_pairs={{0,2},{1,3},{2,0},{3,1},{4,6},{5,7},{6,4},{7,5},{8,10},{9,11},{10,... | collective-permute-start | bytes 393224 | tf_op jit(solution)/shard_map/ppermute | solution.py:247
  156.5 12.7 %collective-permute-start.27 = (bf16[128,512]{1,0:T(8,128)(2,1)S(1)}, bf16[128,512]{1,0:T(8,128)(2,1)S(1)}, u32[]{:S(2)}, u32[]{:S(2)}) collective-permute-start(bf16[128,512]{1,0:T(8,128)(2,1)S(1)} %get-tuple-element.128), channel_id=1, source_target_pairs={{0,3},{1,2},{2,1},{3,0},{4,7},{5,6},{6,5},{7,4},{8,11},{9,10},{10,... | collective-permute-start | bytes 393224 | tf_op jit(solution)/shard_map/ppermute | solution.py:247
  169.3 5.0 %collective-permute-start.28 = (bf16[128,512]{1,0:T(8,128)(2,1)S(1)}, bf16[128,512]{1,0:T(8,128)(2,1)S(1)}, u32[]{:S(2)}, u32[]{:S(2)}) collective-permute-start(bf16[128,512]{1,0:T(8,128)(2,1)S(1)} %fusion.17), channel_id=1, source_target_pairs={{0,8},{4,12},{8,0},{12,4},{16,24},{20,28},{24,16},{28,20},{1,9},{5... | collective-permute-start | bytes 393224 | tf_op jit(solution)/shard_map/ppermute | solution.py:247
  174.4 6.5 %collective-permute-start.29 = (bf16[128,512]{1,0:T(8,128)(2,1)S(1)}, bf16[128,512]{1,0:T(8,128)(2,1)S(1)}, u32[]{:S(2)}, u32[]{:S(2)}) collective-permute-start(bf16[128,512]{1,0:T(8,128)(2,1)S(1)} %add_convert_fusion.12), channel_id=1, source_target_pairs={{0,16},{4,20},{8,24},{12,28},{16,0},{20,4},{24,8},{28,12},{1,17},{... | collective-permute-start | bytes 393224 | tf_op jit(solution)/shard_map/ppermute | solution.py:247
  176.3 12.4 %collective-permute-start.22 = (bf16[2,8,128,128]{3,2,1,0:T(8,128)(2,1)S(1)}, bf16[2,8,128,128]{3,2,1,0:T(8,128)(2,1)S(1)}, u32[]{:S(2)}, u32[]{:S(2)}) collective-permute-start(bf16[2,8,128,128]{3,2,1,0:T(8,128)(2,1)S(1)} %get-tuple-element.110), channel_id=1, source_target_pairs={{0,16},{4,20},{8,24},{12,28},{16,0},{20,4},{24,8},{28,12},{1,17},{... | collective-permute-start | bytes 1572872 | tf_op jit(solution)/shard_map/ppermute | solution.py:247
  177.4 12.6 %collective-permute-start.19 = (bf16[2,8,128,128]{3,2,1,0:T(8,128)(2,1)S(1)}, bf16[2,8,128,128]{3,2,1,0:T(8,128)(2,1)S(1)}, u32[]{:S(2)}, u32[]{:S(2)}) collective-permute-start(bf16[2,8,128,128]{3,2,1,0:T(8,128)(2,1)S(1)} %get-tuple-element.112), channel_id=1, source_target_pairs={{0,8},{4,12},{8,0},{12,4},{16,24},{20,28},{24,16},{28,20},{1,9},{5... | collective-permute-start | bytes 1572872 | tf_op jit(solution)/shard_map/ppermute | solution.py:247
  180.9 10.3 %collective-permute-start.30 = (f32[128,512]{1,0:T(8,128)S(1)}, f32[128,512]{1,0:T(8,128)S(1)}, u32[]{:S(2)}, u32[]{:S(2)}) collective-permute-start(f32[128,512]{1,0:T(8,128)S(1)} %convert_add_fusion.5), channel_id=1, source_target_pairs={{0,4},{4,0},{8,12},{12,8},{16,20},{20,16},{24,28},{28,24},{1,5},{5... | collective-permute-start | bytes 786440 | tf_op jit(solution)/shard_map/ppermute | solution.py:247
  188.9 6.4 %collective-permute-start.23 = (bf16[8,128,128]{2,1,0:T(8,128)(2,1)S(1)}, bf16[8,128,128]{2,1,0:T(8,128)(2,1)S(1)}, u32[]{:S(2)}, u32[]{:S(2)}) collective-permute-start(bf16[8,128,128]{2,1,0:T(8,128)(2,1)S(1)} %get-tuple-element.117), channel_id=1, source_target_pairs={{0,8},{4,12},{8,0},{12,4},{16,24},{20,28},{24,16},{28,20},{1,9},{5... | collective-permute-start | bytes 786440 | tf_op jit(solution)/shard_map/ppermute | solution.py:247
  190.2 6.4 %collective-permute-start.20 = (bf16[8,128,128]{2,1,0:T(8,128)(2,1)S(1)}, bf16[8,128,128]{2,1,0:T(8,128)(2,1)S(1)}, u32[]{:S(2)}, u32[]{:S(2)}) collective-permute-start(bf16[8,128,128]{2,1,0:T(8,128)(2,1)S(1)} %get-tuple-element.119), channel_id=1, source_target_pairs={{0,16},{4,20},{8,24},{12,28},{16,0},{20,4},{24,8},{28,12},{1,17},{... | collective-permute-start | bytes 786440 | tf_op jit(solution)/shard_map/ppermute | solution.py:247
Sparse Core Ops, SparseCore 0:
  9.9 50.1 all-gather.3
  62.3 45.8 all-gather.5

commit v4 on v3

v4 whole, which is shorter than its diff:
```python
import functools

import jax
import jax.numpy as jnp
from jax import lax
from jax.experimental import pallas as pl
from jax.experimental.pallas import tpu as pltpu
from jax.sharding import PartitionSpec as P

VMEM_LIMIT = 48 * 1024 * 1024
CHUNKS = 2
COPIES = 4
F32 = jnp.float32
BF16 = jnp.bfloat16
VMEM = pl.BlockSpec(memory_space=pltpu.VMEM)
SMEM = pl.BlockSpec(memory_space=pltpu.SMEM)
PARAMS = pltpu.CompilerParams(vmem_limit_bytes=VMEM_LIMIT)


def tile_copy(tiles_ref, held, sems, i):
    per = held.shape[0] // COPIES
    part = pl.ds(i * per, per)
    return pltpu.make_async_copy(tiles_ref.at[part], held.at[part], sems.at[i])


def over_rows(tiles_ref, held, sems, one_row):
    per = held.shape[0] // COPIES

    def piece(i, carry):
        tile_copy(tiles_ref, held, sems, i).wait()
        for j in range(per):
            one_row(i * per + j)
        return carry

    lax.fori_loop(0, COPIES, piece, 0)


def spread_kernel(first, pieces, cols_ref, at_ref, tiles_ref, *rest):
    vals, rest = rest[:pieces], rest[pieces:]
    if first:
        (hidden_ref, mask_ref), rest = rest[:2], rest[2:]
    outs, rest = rest[: 2 * CHUNKS], rest[2 * CHUNKS :]
    if first:
        mask_out, sides, rest = rest[0], rest[1:-6], rest[-6:]
        acc, held, sems, left_ref, mask_held, sides_held = rest
        loads = [(vals[0], left_ref), (hidden_ref, sides_held), (mask_ref, mask_held)]
        loads = [pltpu.make_async_copy(src, dst, sems.at[COPIES + i]) for i, (src, dst) in enumerate(loads)]
        loads[0].start()
    else:
        acc, held, sems, left_ref = rest
    for i in range(COPIES):
        tile_copy(tiles_ref, held, sems, i).start()
    if first:
        loads[1].start()
        loads[2].start()
    acc[...] = jnp.zeros_like(acc)
    per_row, size = held.shape[1], held.shape[3]
    me, col = at_ref[0], at_ref[1]
    if first:
        loads[0].wait()
    else:
        for m in range(pieces):
            count = vals[m].shape[0]
            left_ref[pl.ds(jnp.bitwise_xor(col, m) * count, count)] = vals[m][...]

    def one_row(r):
        left = left_ref[r].astype(F32).T.astype(BF16) if first else left_ref[r]
        for k in range(0, per_row, 2):
            pair = jnp.concatenate([held[r, k], held[r, k + 1]], axis=1)
            both = jnp.dot(left, pair, preferred_element_type=F32)
            for side in range(2):
                acc[cols_ref[r, k + side]] += both[:, side * size : (side + 1) * size]

    over_rows(tiles_ref, held, sems, one_row)
    halves, count = outs[0].shape[:2]
    for g in range(CHUNKS):
        for side in range(2):
            for rel in range(halves):
                owner = jnp.bitwise_xor(me, 2 * rel + side)
                start = (owner * CHUNKS + g) * count
                outs[2 * g + side][rel] = acc[pl.ds(start, count)].astype(BF16)
    if first:
        loads[1].wait()
        for m in range(len(sides)):
            per = sides[m].shape[0]
            sides[m][...] = sides_held[pl.ds(jnp.bitwise_xor(col, m) * per, per)]
        loads[2].wait()
        for b in range(mask_held.shape[0]):
            mask_out[b] = mask_held[b].astype(F32).T.astype(BF16)


def spread(edge_tiles, block_cols, vals, at, rows, cols, prepare=()):
    blocks, _, size, _ = edge_tiles.shape
    first = len(prepare) > 0
    feat = vals[0].shape[2] if first else vals[0].shape[1]
    out = jax.ShapeDtypeStruct((rows // 2, blocks // CHUNKS, feat, size), BF16)
    outs = [out] * (2 * CHUNKS)
    scratch = [
        pltpu.VMEM((rows * blocks, feat, size), F32),
        pltpu.VMEM(edge_tiles.shape, BF16),
        pltpu.SemaphoreType.DMA((COPIES + 3,)),
    ]
    if first:
        outs.append(jax.ShapeDtypeStruct((blocks, feat, size), BF16))
        outs += [jax.ShapeDtypeStruct((blocks // cols, size, feat), BF16)] * cols
        scratch += [pltpu.VMEM(v.shape, v.dtype) for v in (vals[0], prepare[1], prepare[0])]
    else:
        scratch.append(pltpu.VMEM((blocks, feat, size), BF16))
    place = pl.BlockSpec(memory_space=pl.ANY) if first else VMEM
    return pl.pallas_call(
        functools.partial(spread_kernel, first, len(vals)),
        out_shape=outs,
        in_specs=[SMEM, SMEM, pl.BlockSpec(memory_space=pl.ANY)] + [place] * (len(vals) + len(prepare)),
        out_specs=[VMEM] * len(outs),
        scratch_shapes=scratch,
        compiler_params=PARAMS,
        cost_estimate=pl.CostEstimate(flops=2 * edge_tiles.size * feat, bytes_accessed=40_000_000, transcendentals=0),
        name="spread",
    )(block_cols, at, edge_tiles, *vals, *prepare)


def aggregate_kernel(cols_ref, at_ref, tiles_ref, *rest):
    parts, (out_ref, held, table, sems) = rest[:-4], rest[-4:]
    blocks, per_row = held.shape[:2]
    loads = []
    for rel, part in enumerate(parts):
        place = table.at[pl.ds(jnp.bitwise_xor(at_ref[0], rel) * blocks, blocks)]
        loads.append(pltpu.make_async_copy(part, place, sems.at[COPIES + rel]))
    for load in loads:
        load.start()
    for i in range(COPIES):
        tile_copy(tiles_ref, held, sems, i).start()
    for load in loads:
        load.wait()

    def one_row(r):
        total = None
        for k in range(0, per_row, 2):
            pair = jnp.concatenate([held[r, k], held[r, k + 1]], axis=1)
            picked = jnp.concatenate([table[cols_ref[r, k]], table[cols_ref[r, k + 1]]], axis=0)
            term = jnp.dot(pair, picked, preferred_element_type=F32)
            total = term if total is None else total + term
        out_ref[r] = total.astype(BF16)

    over_rows(tiles_ref, held, sems, one_row)


def aggregate(edge_tiles, block_cols, parts, at):
    blocks, _, size, _ = edge_tiles.shape
    feat = parts[0].shape[2]
    anywhere = pl.BlockSpec(memory_space=pl.ANY)
    return pl.pallas_call(
        aggregate_kernel,
        out_shape=jax.ShapeDtypeStruct((blocks, size, feat), BF16),
        in_specs=[SMEM, SMEM, anywhere] + [anywhere] * len(parts),
        out_specs=VMEM,
        scratch_shapes=[
            pltpu.VMEM(edge_tiles.shape, BF16),
            pltpu.VMEM((len(parts) * blocks, size, feat), BF16),
            pltpu.SemaphoreType.DMA((COPIES + len(parts),)),
        ],
        compiler_params=PARAMS,
        cost_estimate=pl.CostEstimate(flops=2 * edge_tiles.size * feat, bytes_accessed=30_000_000, transcendentals=0),
        name="aggregate",
    )(block_cols, at, edge_tiles, *parts)


def finish_kernel(pieces, at_ref, *rest):
    parts, rest = rest[: 2 * CHUNKS], rest[2 * CHUNKS :]
    total = [parts[2 * g][...].astype(F32) + parts[2 * g + 1][...].astype(F32) for g in range(CHUNKS)]
    count = parts[0].shape[0]
    if pieces == 0:
        for g in range(CHUNKS):
            for b in range(count):
                rest[0][g * count + b] = total[g][b].T.astype(BF16)
        return
    mask_ref, outs, held = rest[0], rest[1:-1], rest[-1]
    for g in range(CHUNKS):
        held[g * count : (g + 1) * count] = total[g].astype(BF16)
    per, feat = outs[0].shape[0], held.shape[1]
    for m in range(pieces):
        part = pl.ds(jnp.bitwise_xor(at_ref[1], m) * per, per)
        outs[m][:, :feat] = held[part]
        outs[m][:, feat:] = mask_ref[part]


def finish(parts, at, pieces, mask=()):
    count, feat, size = parts[0].shape
    blocks = count * CHUNKS
    if pieces == 0:
        outs, scratch = [jax.ShapeDtypeStruct((blocks, size, feat), BF16)], []
    else:
        outs = [jax.ShapeDtypeStruct((blocks // pieces, 2 * feat, size), BF16)] * pieces
        scratch = [pltpu.VMEM((blocks, feat, size), BF16)]
    return pl.pallas_call(
        functools.partial(finish_kernel, pieces),
        out_shape=outs,
        in_specs=[SMEM] + [VMEM] * (len(parts) + len(mask)),
        out_specs=[VMEM] * len(outs),
        scratch_shapes=scratch,
        compiler_params=PARAMS,
        name="finish",
    )(at, *parts, *mask)


def dense_kernel(cols, at_ref, weights_ref, *rest):
    sums, rest = rest[:cols], rest[cols:]
    outs, (sum_ref, delta_ref, held, mask) = rest[:cols], rest[cols:]
    col = at_ref[1]
    count, feat, size = outs[0].shape
    for m in range(cols):
        place = jnp.bitwise_xor(col, m)
        for b in range(count):
            sum_ref[place, :, b * size : (b + 1) * size] = sums[m][b, :feat]
            mask[place, :, b * size : (b + 1) * size] = sums[m][b, feat:].astype(F32)
    stacked = jnp.concatenate([sum_ref[q] for q in range(cols)], axis=0)
    for q in range(cols):
        grad = jnp.dot(weights_ref[q, 0], stacked, preferred_element_type=F32)
        delta_ref[q] = (grad * mask[q]).astype(BF16)
    delta = jnp.concatenate([delta_ref[q] for q in range(cols)], axis=0)
    for q in range(cols):
        res = jnp.dot(weights_ref[q, 1], delta, preferred_element_type=F32).astype(BF16)
        for b in range(count):
            held[q, b] = res[:, b * size : (b + 1) * size]
    for m in range(cols):
        outs[m][...] = held[jnp.bitwise_xor(col, m)]


def dense(weights, sums, at):
    cols = len(sums)
    count, feat, size = sums[0].shape
    feat = feat // 2
    out = jax.ShapeDtypeStruct((count, feat, size), BF16)
    flat = jax.ShapeDtypeStruct((cols, feat, count * size), BF16)
    res = pl.pallas_call(
        functools.partial(dense_kernel, cols),
        out_shape=[out] * cols + [flat] * 2,
        in_specs=[SMEM] + [VMEM] * (1 + cols),
        out_specs=[VMEM] * (cols + 2),
        scratch_shapes=[pltpu.VMEM((cols, count, feat, size), BF16), pltpu.VMEM((cols, feat, count * size), F32)],
        compiler_params=PARAMS,
        name="dense",
    )(at, weights, *sums)
    return res[:cols], res[cols], res[cols + 1]


def weight_terms_kernel(cols, at_ref, sum_ref, delta_ref, *rest):
    sides, rest = rest[:cols], rest[cols:]
    aggs, (keep_ref, send_ref) = rest[:cols], rest[cols:]
    even = jnp.bitwise_and(at_ref[0], 1) == 0
    count = aggs[0].shape[0]
    sums = jnp.concatenate([sum_ref[q] for q in range(cols)], axis=0)
    delta = jnp.concatenate([delta_ref[q] for q in range(cols)], axis=0)
    for m in range(cols):
        hidden = jnp.concatenate([sides[m][b] for b in range(count)], axis=0)
        agg = jnp.concatenate([aggs[m][b] for b in range(count)], axis=0)
        second = jnp.dot(sums, hidden, preferred_element_type=F32)
        first = jnp.dot(delta, agg, preferred_element_type=F32)
        keep_ref[m] = jnp.where(even, second, first).T
        send_ref[m] = jnp.where(even, first, second).T.astype(BF16)


def weight_terms(sums, delta, sides, aggs, at):
    cols, feat, _ = delta.shape
    shape = (cols, feat, cols * feat)
    return pl.pallas_call(
        functools.partial(weight_terms_kernel, cols),
        out_shape=[jax.ShapeDtypeStruct(shape, F32), jax.ShapeDtypeStruct(shape, BF16)],
        in_specs=[SMEM] + [VMEM] * (2 + 2 * cols),
        out_specs=[VMEM] * 2,
        compiler_params=PARAMS,
        name="weight_terms",
    )(at, sums, delta, *sides, *aggs)


def swap(value, mask, axis):
    return lax.ppermute(value, axis, [(i, i ^ mask) for i in range(lax.axis_size(axis))])


def swap_all(pieces, axis):
    return [pieces[0]] + [swap(pieces[m], m, axis) for m in range(1, len(pieces))]


def add(a, b):
    return (a.astype(F32) + b.astype(F32)).astype(BF16)


def scatter_chunk(keep, got, masks, beside):
    left = sorted(masks, reverse=True)
    for mask in masks:
        axis = left.index(mask)
        part = lambda v, i: lax.index_in_dim(v, i, axis, keepdims=False)
        sent = swap(add(part(keep, 1), part(got, 1)), mask, "row")
        keep = add(part(keep, 0), part(got, 0))
        got = sent
        left.remove(mask)
        if mask == masks[0]:
            got, beside = lax.optimization_barrier((got, beside))
    return [keep, got], beside


def scatter(pieces, rows, beside):
    masks = [1 << b for b in range(1, rows.bit_length() - 1)]
    lead = (2,) * len(masks)
    done = []
    for g in range(CHUNKS):
        keep, got = pieces[2 * g], swap(pieces[2 * g + 1], 1, "row")
        order = masks if g % 2 == 0 else masks[::-1]
        terms, beside = scatter_chunk(keep.reshape(lead + keep.shape[1:]), got.reshape(lead + got.shape[1:]), order, beside)
        done += terms
    return done, beside


def column_terms(keep, send):
    terms = keep + swap(send, 1, "row").astype(F32)
    return swap_all([terms[0]] + [terms[m].astype(BF16) for m in range(1, terms.shape[0])], "col")


def reduced(terms, me):
    value = sum(t.astype(F32) for t in terms)
    mask = 2
    while mask < lax.axis_size("row"):
        value = value.astype(BF16)
        value = value.astype(F32) + swap(value, mask, "row").astype(F32)
        mask *= 2
    other = swap(value, 1, "row")
    even = me % 2 == 0
    return jnp.where(even, other, value), jnp.where(even, value, other)


def gather_weights(weights, me, rows):
    kinds, out_rows, width = weights.shape
    part = lax.dynamic_slice_in_dim(weights, me * (out_rows // rows), out_rows // rows, 1)
    whole = lax.all_gather(part, ("row", "col"), axis=0)
    whole = whole.reshape(rows, -1, kinds, out_rows // rows, width)
    return whole.transpose(1, 2, 0, 3, 4).reshape(-1, kinds, out_rows, width)


def per_device(
    node_feats, hidden_act, grad_out, relu_mask, edge_tiles, block_cols, weight_one, weight_two
):
    rows, cols = lax.axis_size("row"), lax.axis_size("col")
    me, col = lax.axis_index("row").astype(jnp.int32), lax.axis_index("col").astype(jnp.int32)
    at = jnp.stack([me, col])
    blocks, _, size, _ = edge_tiles.shape
    blocked = lambda v: v.reshape(v.shape[0] // size, size, v.shape[1])
    after = lax.optimization_barrier

    def by_distance(v):
        per = blocks // cols
        return [lax.dynamic_slice_in_dim(v, (col ^ m) * per, per, 0) for m in range(cols)]

    weights = gather_weights(jnp.stack([weight_two, weight_one]), me, rows)
    node_feats = blocked(node_feats)
    near = {0: node_feats}
    for rel in [1 << b for b in range(rows.bit_length() - 1)]:
        near[rel] = swap(node_feats, rel, "row")
    pieces = spread(
        edge_tiles, block_cols, [blocked(grad_out)], at, rows, cols, [blocked(hidden_act), blocked(relu_mask)]
    )
    pieces, mask, sides = pieces[: 2 * CHUNKS], pieces[2 * CHUNKS], pieces[2 * CHUNKS + 1 :]
    pieces, near = after((pieces, near))
    terms, (sides, near) = scatter(pieces, rows, (swap_all(sides, "col"), near))
    for rel in range(2, rows):
        low, top = rel & 1, 1 << (rel.bit_length() - 1)
        if rel not in near:
            near[rel] = swap(near[rel - 1], 1, "row") if low else swap(near[rel - top], top, "row")
    last = near.pop(rows - 1)
    terms, near = after((terms, near))
    near[rows - 1] = last
    sums = swap_all(finish(terms, at, cols, [mask]), "col")
    parts = [near[rel] for rel in range(rows)]
    sums[1], weights = after((sums[1], weights))
    agg_feats = aggregate(edge_tiles, block_cols, parts, at)
    sums, agg_feats = after((sums, agg_feats))
    spread_in, sums, delta = dense(weights, sums, at)
    back = swap_all(spread_in, "col")
    agg_feats = swap_all(by_distance(agg_feats), "col")
    back, agg_feats = after((back, agg_feats))
    pieces = spread(edge_tiles, block_cols, back, at, rows, cols)
    grads = column_terms(*weight_terms(sums, delta, sides, agg_feats, at))
    terms, grads = scatter(pieces, rows, grads)
    (out,) = finish(terms, at, 0)
    first_grad, second_grad = reduced(grads, me)
    return out.reshape(-1, out.shape[2]), first_grad, second_grad


def solution(mesh):
    in_specs = (
        P("row", "col"),
        P("row", "col"),
        P("row", "col"),
        P("row", "col"),
        P("row", None, None, None),
        P("row", None),
        P("col", None),
        P("col", None),
    )
    out_specs = (P("row", "col"), P("col", None), P("col", None))
    return jax.shard_map(
        per_device, mesh=mesh, in_specs=in_specs, out_specs=out_specs, check_vma=False
    )
```

time: 206 us -> 183 us (0.89)
  waiting for transfers between devices: 92.8 us -> 71.4 us
  starting transfers between devices: 55.1 us -> 51.9 us
    ppermute x31 -> x38, waiting for transfers between devices: 92.1 us -> 61.6 us  [swap(): lax.ppermute(value, axis, [(i, i ^ mask) for i in range(lax.axis_size(axi...]
    all_gather x2 -> x1, waiting for transfers between devices: 0.01 us -> 9.88 us  [gather_weights(): whole = lax.all_gather(part, ('row', 'col'), axis=0)]
    ppermute x31 -> x38, starting transfers between devices: 55 us -> 51.8 us  [swap(): lax.ppermute(value, axis, [(i, i ^ mask) for i in range(lax.axis_size(axi...]
    unnamed x22 -> x34, local copies, waits for them, and re-layouts: 10.1 us -> 7.83 us
  transfers between devices with their start and end apart: 33 -> 39, of which waited for: 17 -> 17; matrix products, arithmetic and copies ran while one was open for 3% -> 4% of each run, Pallas kernels for 12% -> 11%
where the time goes in v4:
time: 183 us
  waiting for transfers between devices  71.4 us (39%)
  starting transfers between devices  51.9 us (28%)
  Pallas kernels  28.7 us (16%)
  between operations  14.3 us (8%)
  local copies, waits for them, and re-layouts  9.22 us (5%)
  other arithmetic  7.14 us (4%)
    ppermute x38, waiting for transfers between devices, swap(): lax.ppermute(value, axis, [(i, i ^ mask) for i in range(lax.axis_size(axi...  61.6 us
    ppermute x38, starting transfers between devices, swap(): lax.ppermute(value, axis, [(i, i ^ mask) for i in range(lax.axis_size(axi...  51.8 us
    pallas_call x2, Pallas kernels, spread(): pl.pallas_call(functools.partial(spread_kernel, first, len(vals)), out_sh...  15.1 us
    all_gather x1, waiting for transfers between devices, gather_weights(): whole = lax.all_gather(part, ('row', 'col'), axis=0)  9.88 us
    unnamed x34, local copies, waits for them, and re-layouts  7.83 us
    pallas_call x1, Pallas kernels, aggregate(): pl.pallas_call(aggregate_kernel, out_shape=jax.ShapeDtypeStruct((blocks,...  6.32 us
    convert_element_type x8, other arithmetic, add(): return (a.astype(F32) + b.astype(F32)).astype(BF16)  4.49 us
  transfers between devices with their start and end apart: 39, of which 17 were waited for; matrix products, arithmetic and copies ran while one was open for 4% of the time, Pallas kernels for 11%

profile of v4, /device:TPU:0, one launch (start us, length us, event | category | flops | bytes accessed | tf_op | source)
XLA Modules:
  0.0 182.7 jit_solution(10423882281510108148)
XLA Ops:
  7.2 0.5 collective-permute-start
  7.7 2.6 %collective-permute-start.1 = (bf16[16,128,128]{2,1,0:T(8,128)(2,1)}, bf16[16,128,128]{2,1,0:T(8,128)(2,1)}, u32[]{:S(2)}, u32[]{:S(2)}) collective-permute-start(bf16[16,128,128]{2,1,0:T(8,128)(2,1)} %bitcast.71), channel_id=1, source_target_pairs={{0,8},{4,12},{8,0},{12,4},{16,24},{20,28},{24,16},{28,20},{1,9},{5... | collective-permute-start | bytes 1572872 | tf_op jit(solution)/shard_map/ppermute | solution.py:277
  10.3 1.5 collective-permute-start.2
  11.9 1.0 copy-done
  12.9 1.0 copy-done.1
  14.0 0.7 copy-done.13
  14.7 8.3 %spread.2 = (bf16[4,8,128,128]{3,2,1,0:T(8,128)(2,1)S(1)}, bf16[4,8,128,128]{3,2,1,0:T(8,128)(2,1)}, bf16[4,8,128,128]{3,2,1,0:T(8,128)(2,1)S(1)}, bf16[4,8,128,...) custom-call(s32[16,20]{1,0:T(8,128)S(1)} %copy-done.13, ...), custom_call_target="tpu_custom_call" | custom-call | flops 1342177280 | bytes 40000000 | tf_op jit(solution)/shard_map/spread/pallas_call | solution.py:110
  23.0 0.8 copy-done.5
  23.8 0.7 copy-done.16
  24.6 0.5 collective-permute-start.9
  25.1 1.4 fusion.14
  26.5 1.1 collective-permute-done.3
  27.6 1.6 fusion
  29.2 0.5 collective-permute-start.4
  29.7 1.6 add_convert_fusion.4
  31.3 1.7 collective-permute-start.10
  33.0 1.6 collective-permute-start.5
  34.5 2.6 %collective-permute-start.6 = (bf16[4,128,128]{2,1,0:T(8,128)(2,1)S(1)}, bf16[4,128,128]{2,1,0:T(8,128)(2,1)S(1)}, u32[]{:S(2)}, u32[]{:S(2)}) collective-permute-start(bf16[4,128,128]{2,1,0:T(8,128)(2,1)S(1)} %get-tuple-element.98), channel_id=1, source_target_pairs={{0,2},{1,3},{2,0},{3,1},{4,6},{5,7},{6,4},{7,5},{8,10},{9,11},{10,... | collective-permute-start | bytes 393224 | tf_op jit(solution)/shard_map/ppermute | solution.py:277
  37.4 2.6 %collective-permute-done.5.rest_1_ = bf16[4,128,128]{2,1,0:T(8,128)(2,1)S(1)} collective-permute-done((bf16[4,128,128]{2,1,0:T(8,128)(2,1)}, bf16[4,128,128]{2,1,0:T(8,128)(2,1)S(1)}, u32[]{:S(2)}, u32[]{:S(2)}) %collective-permute-start.5) | collective-permute-done | bytes 131104 | tf_op jit(solution)/shard_map/ppermute | solution.py:277
  39.9 7.9 %collective-permute-done.6.rest_2_ = bf16[4,128,128]{2,1,0:T(8,128)(2,1)S(1)} collective-permute-done((bf16[4,128,128]{2,1,0:T(8,128)(2,1)S(1)}, bf16[4,128,128]{2,1,0:T(8,128)(2,1)S(1)}, u32[]{:S(2)}, u32[]{:S(2)}) %collective-permute-start.6) | collective-permute-done | bytes 131104 | tf_op jit(solution)/shard_map/ppermute | solution.py:277
  47.9 0.7 copy-done.11
  48.6 0.4 collective-permute-start.14
  49.0 0.5 collective-permute-start.13
  49.7 1.6 collective-permute-start.11
  51.4 1.6 collective-permute-start.8
  53.1 9.6 %collective-permute-done.14.rest_6_ = bf16[16,128,128]{2,1,0:T(8,128)(2,1)S(1)} collective-permute-done((bf16[16,128,128]{2,1,0:T(8,128)(2,1)}, bf16[16,128,128]{2,1,0:T(8,128)(2,1)S(1)}, u32[]{:S(2)}, u32[]{:S(2)}) %collective-permute-start.14) | collective-permute-done | bytes 524320 | tf_op jit(solution)/shard_map/ppermute | solution.py:277
  62.6 2.8 %collective-permute-done.8.rest_1_ = bf16[8,128,128]{2,1,0:T(8,128)(2,1)S(1)} collective-permute-done((bf16[8,128,128]{2,1,0:T(8,128)(2,1)S(1)}, bf16[8,128,128]{2,1,0:T(8,128)(2,1)S(1)}, u32[]{:S(2)}, u32[]{:S(2)}) %collective-permute-start.8) | collective-permute-done | bytes 262176 | tf_op jit(solution)/shard_map/ppermute | solution.py:277
  65.5 1.0 copy-done.6
  66.5 1.7 finish.2
  68.2 4.0 %collective-permute-start.15 = (bf16[4,256,128]{2,1,0:T(8,128)(2,1)}, bf16[4,256,128]{2,1,0:T(8,128)(2,1)}, u32[]{:S(2)}, u32[]{:S(2)}) collective-permute-start(bf16[4,256,128]{2,1,0:T(8,128)(2,1)} %get-tuple-element.125), channel_id=1, source_target_pairs={{0,1},{1,0},{2,3},{3,2},{4,5},{5,4},{6,7},{7,6},{8,9},{9,8},{10,11... | collective-permute-start | bytes 786440 | tf_op jit(solution)/shard_map/ppermute | solution.py:277
  72.1 1.0 collective-permute-start.16
  73.1 1.5 collective-permute-start.17
  74.6 9.9 %all-gather.3.cloned.1.call-done = bf16[64,16,512]{2,1,0:T(8,128)(2,1)} async-done(((bf16[2,16,512]{2,1,0:T(8,128)(2,1)}), bf16[64,16,512]{2,1,0:T(8,128)(2,1)}) %all-gather.3.cloned.1.call-update) | async-done | bytes 1048592 | tf_op jit(solution)/shard_map/all_gather | solution.py:334
  84.5 1.3 copy.12
  85.8 0.8 copy-done.3
  86.6 1.0 copy-done.4
  87.7 6.3 %aggregate.1 = bf16[16,128,128]{2,1,0:T(8,128)(2,1)S(1)} custom-call(s32[16,20]{1,0:T(8,128)S(1)} %copy-done.14, s32[2]{0:T(128)S(1)} %pad_add_fusion.at_ref, bf16[16,20,128,128]{3,2,1,0:T(8,128)(2,1)} %tiles_ref.5, bf16[16,128,128]{2,1,0:T(8,128)(2,1)S(1)} %bitcast.73, bf16[16,128,128]{2,1,0:T(8,128)(2,1)S(1)} %collective-permute-done.rest_1_, ...), custom_call_target="tpu_custom_call" | custom-call | flops 1342177280 | bytes 30000000 | tf_op jit(solution)/shard_map/aggregate/pallas_call | solution.py:152
  94.0 1.6 collective-permute-done.16.rest_2_
  95.6 2.1 %dense.1 = (bf16[4,128,128]{2,1,0:T(8,128)(2,1)S(1)}, bf16[4,128,128]{2,1,0:T(8,128)(2,1)S(1)}, bf16[4,128,128]{2,1,0:T(8,128)(2,1)S(1)}, bf16[4,128,128]{2,1,0:...) custom-call(s32[2]{0:T(128)S(1)} %pad_add_fusion.at_ref, ...), custom_call_target="tpu_custom_call" | custom-call | tf_op jit(solution)/shard_map/dense/pallas_call | solution.py:235
  97.8 3.8 %collective-permute-start.19 = (bf16[4,128,128]{2,1,0:T(8,128)(2,1)S(1)}, bf16[4,128,128]{2,1,0:T(8,128)(2,1)S(1)}, u32[]{:S(2)}, u32[]{:S(2)}) collective-permute-start(bf16[4,128,128]{2,1,0:T(8,128)(2,1)S(1)} %get-tuple-element.143), channel_id=1, source_target_pairs={{0,1},{1,0},{2,3},{3,2},{4,5},{5,4},{6,7},{7,6},{8,9},{9,8},{10,11... | collective-permute-start | bytes 393224 | tf_op jit(solution)/shard_map/ppermute | solution.py:277
  101.9 2.1 %collective-permute-start.21 = (bf16[4,128,128]{2,1,0:T(8,128)(2,1)S(1)}, bf16[4,128,128]{2,1,0:T(8,128)(2,1)S(1)}, u32[]{:S(2)}, u32[]{:S(2)}) collective-permute-start(bf16[4,128,128]{2,1,0:T(8,128)(2,1)S(1)} %get-tuple-element.145), channel_id=1, source_target_pairs={{0,3},{1,2},{2,1},{3,0},{4,7},{5,6},{6,5},{7,4},{8,11},{9,10},{10,... | collective-permute-start | bytes 393224 | tf_op jit(solution)/shard_map/ppermute | solution.py:277
  104.0 1.1 collective-permute-start.22
  105.1 1.3 collective-permute-start.23
  106.4 2.5 %collective-permute-done.19.rest_1_ = bf16[4,128,128]{2,1,0:T(8,128)(2,1)S(1)} collective-permute-done((bf16[4,128,128]{2,1,0:T(8,128)(2,1)S(1)}, bf16[4,128,128]{2,1,0:T(8,128)(2,1)S(1)}, u32[]{:S(2)}, u32[]{:S(2)}) %collective-permute-start.19) | collective-permute-done | bytes 131104 | tf_op jit(solution)/shard_map/ppermute | solution.py:277
  109.3 5.3 %collective-permute-done.20.rest_2_ = bf16[4,128,128]{2,1,0:T(8,128)(2,1)S(1)} collective-permute-done((bf16[4,128,128]{2,1,0:T(8,128)(2,1)S(1)}, bf16[4,128,128]{2,1,0:T(8,128)(2,1)S(1)}, u32[]{:S(2)}, u32[]{:S(2)}) %collective-permute-start.20) | collective-permute-done | bytes 131104 | tf_op jit(solution)/shard_map/ppermute | solution.py:277
  114.5 8.4 %collective-permute-done.23.rest_6_ = bf16[4,128,128]{2,1,0:T(8,128)(2,1)S(1)} collective-permute-done((bf16[4,128,128]{2,1,0:T(8,128)(2,1)S(1)}, bf16[4,128,128]{2,1,0:T(8,128)(2,1)S(1)}, u32[]{:S(2)}, u32[]{:S(2)}) %collective-permute-start.23) | collective-permute-done | bytes 131104 | tf_op jit(solution)/shard_map/ppermute | solution.py:277
  123.0 6.8 %spread.3 = (bf16[4,8,128,128]{3,2,1,0:T(8,128)(2,1)S(1)}, bf16[4,8,128,128]{3,2,1,0:T(8,128)(2,1)S(1)}, bf16[4,8,128,128]{3,2,1,0:T(8,128)(2,1)S(1)}, bf16[4,8,128,128]{3,2,1,0:T(8,128)(2,1)S(1)}) custom-call(s32[16,20]{1,0:T(8,128)S(1)} %copy-done.14, s32[2]{0:T(128)S(1)} %pad_add_fusion.at_ref, bf16[16,20,128,128]{3,2,1,0:T(8,128)(2,1)} %tiles_ref.5, ...), custom_call_target="tpu_custom_call" | custom-call | flops 1342177280 | bytes 40000000 | tf_op jit(solution)/shard_map/spread/pallas_call | solution.py:110
  129.8 0.5 collective-permute-start.25
  130.3 1.9 %weight_terms.1 = (f32[4,128,512]{2,1,0:T(8,128)S(1)}, bf16[4,128,512]{2,1,0:T(8,128)(2,1)S(1)}) custom-call(s32[2]{0:T(128)S(1)} %pad_add_fusion.at_ref, bf16[4,128,512]{2,1,0:T(8,128)(2,1)S(1)} %get-tuple-element.153.sum_ref, bf16[4,128,512]{2,1,0:T(8,128)(2,1)S(1)} %get-tuple-element.154.delta_ref, bf16[4,128,128]{2,1,0:T(8,128)(2,1)S(1)} %get-tuple-element.155.rest_0_, ...), custom_call_target="tpu_custom_call" | custom-call | tf_op jit(solution)/shard_map/weight_terms/pallas_call | solution.py:266
  132.8 8.8 %collective-permute-start.33 = (bf16[2,8,128,128]{3,2,1,0:T(8,128)(2,1)S(1)}, bf16[2,8,128,128]{3,2,1,0:T(8,128)(2,1)S(1)}, u32[]{:S(2)}, u32[]{:S(2)}) collective-permute-start(bf16[2,8,128,128]{3,2,1,0:T(8,128)(2,1)S(1)} %get-tuple-element.179), channel_id=1, source_target_pairs={{0,16},{4,20},{8,24},{12,28},{16,0},{20,4},{24,8},{28,12},{1,17},{... | collective-permute-start | bytes 1572872 | tf_op jit(solution)/shard_map/ppermute | solution.py:277
  142.0 1.5 collective-permute-start.26
  143.8 2.8 %collective-permute-start.28 = (bf16[128,512]{1,0:T(8,128)(2,1)S(1)}, bf16[128,512]{1,0:T(8,128)(2,1)S(1)}, u32[]{:S(2)}, u32[]{:S(2)}) collective-permute-start(bf16[128,512]{1,0:T(8,128)(2,1)S(1)} %get-tuple-element.199), channel_id=1, source_target_pairs={{0,1},{1,0},{2,3},{3,2},{4,5},{5,4},{6,7},{7,6},{8,9},{9,8},{10,11... | collective-permute-start | bytes 393224 | tf_op jit(solution)/shard_map/ppermute | solution.py:277
  146.6 2.4 %collective-permute-start.30 = (bf16[128,512]{1,0:T(8,128)(2,1)S(1)}, bf16[128,512]{1,0:T(8,128)(2,1)S(1)}, u32[]{:S(2)}, u32[]{:S(2)}) collective-permute-start(bf16[128,512]{1,0:T(8,128)(2,1)S(1)} %get-tuple-element.197), channel_id=1, source_target_pairs={{0,3},{1,2},{2,1},{3,0},{4,7},{5,6},{6,5},{7,4},{8,11},{9,10},{10,... | collective-permute-start | bytes 393224 | tf_op jit(solution)/shard_map/ppermute | solution.py:277
  149.1 1.7 collective-permute-done.28
  150.8 8.2 %collective-permute-done.29 = bf16[128,512]{1,0:T(8,128)(2,1)S(1)} collective-permute-done((bf16[128,512]{1,0:T(8,128)(2,1)S(1)}, bf16[128,512]{1,0:T(8,128)(2,1)S(1)}, u32[]{:S(2)}, u32[]{:S(2)}) %collective-permute-start.29) | collective-permute-done | bytes 131104 | tf_op jit(solution)/shard_map/ppermute | solution.py:277
  159.1 0.7 collective-permute-start.35
  159.9 1.5 collective-permute-start.34
  161.4 4.2 %collective-permute-done.35 = bf16[128,512]{1,0:T(8,128)(2,1)S(1)} collective-permute-done((bf16[128,512]{1,0:T(8,128)(2,1)S(1)}, bf16[128,512]{1,0:T(8,128)(2,1)S(1)}, u32[]{:S(2)}, u32[]{:S(2)}) %collective-permute-start.35) | collective-permute-done | bytes 131104 | tf_op jit(solution)/shard_map/ppermute | solution.py:277
  165.6 1.2 collective-permute-start.36
  166.9 0.9 collective-permute-start.31
  167.9 2.7 %collective-permute-done.36 = bf16[128,512]{1,0:T(8,128)(2,1)S(1)} collective-permute-done((bf16[128,512]{1,0:T(8,128)(2,1)S(1)}, bf16[128,512]{1,0:T(8,128)(2,1)S(1)}, u32[]{:S(2)}, u32[]{:S(2)}) %collective-permute-start.36) | collective-permute-done | bytes 131104 | tf_op jit(solution)/shard_map/ppermute | solution.py:277
  170.8 2.7 %collective-permute-done.31.rest_1_ = bf16[8,128,128]{2,1,0:T(8,128)(2,1)S(1)} collective-permute-done((bf16[8,128,128]{2,1,0:T(8,128)(2,1)S(1)}, bf16[8,128,128]{2,1,0:T(8,128)(2,1)S(1)}, u32[]{:S(2)}, u32[]{:S(2)}) %collective-permute-start.31) | collective-permute-done | bytes 262176 | tf_op jit(solution)/shard_map/ppermute | solution.py:277
  173.4 1.6 finish.3
  175.0 0.9 broadcast_select_fusion
  (75 shorter events, 3.5 us)
Async XLA Ops:
  7.2 77.3 %all-gather.3.cloned.1.call-start = ((), (), s32[]{:S(2)}) async-start(), calls=%async_computation | async-start | bytes 1081344 | tf_op jit(solution)/shard_map/all_gather | solution.py:334
  7.2 17.2 %collective-permute-start = (bf16[16,128,128]{2,1,0:T(8,128)(2,1)}, bf16[16,128,128]{2,1,0:T(8,128)(2,1)S(1)}, u32[]{:S(2)}, u32[]{:S(2)}) collective-permute-start(bf16[16,128,128]{2,1,0:T(8,128)(2,1)} %bitcast.70), channel_id=1, source_target_pairs={{0,4},{4,0},{8,12},{12,8},{16,20},{20,16},{24,28},{28,24},{1,5},{5... | collective-permute-start | bytes 1572872 | tf_op jit(solution)/shard_map/ppermute | solution.py:277
  7.7 16.7 %collective-permute-start.1 = (bf16[16,128,128]{2,1,0:T(8,128)(2,1)}, bf16[16,128,128]{2,1,0:T(8,128)(2,1)}, u32[]{:S(2)}, u32[]{:S(2)}) collective-permute-start(bf16[16,128,128]{2,1,0:T(8,128)(2,1)} %bitcast.71), channel_id=1, source_target_pairs={{0,8},{4,12},{8,0},{12,4},{16,24},{20,28},{24,16},{28,20},{1,9},{5... | collective-permute-start | bytes 1572872 | tf_op jit(solution)/shard_map/ppermute | solution.py:277
  10.3 14.3 %collective-permute-start.2 = (bf16[16,128,128]{2,1,0:T(8,128)(2,1)}, bf16[16,128,128]{2,1,0:T(8,128)(2,1)}, u32[]{:S(2)}, u32[]{:S(2)}) collective-permute-start(bf16[16,128,128]{2,1,0:T(8,128)(2,1)} %bitcast.72), channel_id=1, source_target_pairs={{0,16},{4,20},{8,24},{12,28},{16,0},{20,4},{24,8},{28,12},{1,17},{... | collective-permute-start | bytes 1572872 | tf_op jit(solution)/shard_map/ppermute | solution.py:277
  11.9 1.0 copy-start
  12.9 1.0 copy-start.1
  14.0 0.7 copy-start.13
  14.7 71.9 %copy-start.2 = (bf16[2048,128]{1,0:T(8,128)(2,1)S(1)}, bf16[2048,128]{1,0:T(8,128)(2,1)}, u32[]{:S(2)}) copy-start(bf16[2048,128]{1,0:T(8,128)(2,1)} %param.8) | copy-start | bytes 1572868
  14.7 71.9 %copy-start.14 = (s32[16,20]{1,0:T(8,128)S(1)}, s32[16,20]{1,0:T(8,128)}, u32[]{:S(2)}) copy-start(s32[16,20]{1,0:T(8,128)} %cols_ref.5) | copy-start | bytes 3844
  23.0 0.8 copy-start.5
  23.8 0.7 copy-start.16
  24.4 8.5 %copy-start.15 = (bf16[4,128,128]{2,1,0:T(8,128)(2,1)}, bf16[4,128,128]{2,1,0:T(8,128)(2,1)S(1)}, u32[]{:S(2)}) copy-start(bf16[4,128,128]{2,1,0:T(8,128)(2,1)S(1)} %get-tuple-element.99) | copy-start | bytes 393220
  24.6 3.0 %collective-permute-start.3 = (bf16[4,8,128,128]{3,2,1,0:T(8,128)(2,1)}, bf16[4,8,128,128]{3,2,1,0:T(8,128)(2,1)}, u32[]{:S(2)}, u32[]{:S(2)}) collective-permute-start(bf16[4,8,128,128]{3,2,1,0:T(8,128)(2,1)} %get-tuple-element.95), channel_id=1, source_target_pairs={{0,4},{4,0},{8,12},{12,8},{16,20},{20,16},{24,28},{28,24},{1,5},{5... | collective-permute-start | bytes 3145736 | tf_op jit(solution)/shard_map/ppermute | solution.py:277
  24.6 5.1 %collective-permute-start.9 = (bf16[4,8,128,128]{3,2,1,0:T(8,128)(2,1)}, bf16[4,8,128,128]{3,2,1,0:T(8,128)(2,1)}, u32[]{:S(2)}, u32[]{:S(2)}) collective-permute-start(bf16[4,8,128,128]{3,2,1,0:T(8,128)(2,1)} %get-tuple-element.106), channel_id=1, source_target_pairs={{0,4},{4,0},{8,12},{12,8},{16,20},{20,16},{24,28},{28,24},{1,5},{5... | collective-permute-start | bytes 3145736 | tf_op jit(solution)/shard_map/ppermute | solution.py:277
  29.2 19.4 %collective-permute-start.4 = (bf16[2,8,128,128]{3,2,1,0:T(8,128)(2,1)S(1)}, bf16[2,8,128,128]{3,2,1,0:T(8,128)(2,1)S(1)}, u32[]{:S(2)}, u32[]{:S(2)}) collective-permute-start(bf16[2,8,128,128]{3,2,1,0:T(8,128)(2,1)S(1)} %get-tuple-element.185), channel_id=1, source_target_pairs={{0,8},{4,12},{8,0},{12,4},{16,24},{20,28},{24,16},{28,20},{1,9},{5... | collective-permute-start | bytes 1572872 | tf_op jit(solution)/shard_map/ppermute | solution.py:277
  31.3 17.3 %collective-permute-start.10 = (bf16[2,8,128,128]{3,2,1,0:T(8,128)(2,1)S(1)}, bf16[2,8,128,128]{3,2,1,0:T(8,128)(2,1)S(1)}, u32[]{:S(2)}, u32[]{:S(2)}) collective-permute-start(bf16[2,8,128,128]{3,2,1,0:T(8,128)(2,1)S(1)} %get-tuple-element.183), channel_id=1, source_target_pairs={{0,16},{4,20},{8,24},{12,28},{16,0},{20,4},{24,8},{28,12},{1,17},{... | collective-permute-start | bytes 1572872 | tf_op jit(solution)/shard_map/ppermute | solution.py:277
  33.0 7.0 %collective-permute-start.5 = (bf16[4,128,128]{2,1,0:T(8,128)(2,1)}, bf16[4,128,128]{2,1,0:T(8,128)(2,1)S(1)}, u32[]{:S(2)}, u32[]{:S(2)}) collective-permute-start(bf16[4,128,128]{2,1,0:T(8,128)(2,1)} %copy-done.16), channel_id=1, source_target_pairs={{0,1},{1,0},{2,3},{3,2},{4,5},{5,4},{6,7},{7,6},{8,9},{9,8},{10,11... | collective-permute-start | bytes 393224 | tf_op jit(solution)/shard_map/ppermute | solution.py:277
  34.5 13.3 %collective-permute-start.6 = (bf16[4,128,128]{2,1,0:T(8,128)(2,1)S(1)}, bf16[4,128,128]{2,1,0:T(8,128)(2,1)S(1)}, u32[]{:S(2)}, u32[]{:S(2)}) collective-permute-start(bf16[4,128,128]{2,1,0:T(8,128)(2,1)S(1)} %get-tuple-element.98), channel_id=1, source_target_pairs={{0,2},{1,3},{2,0},{3,1},{4,6},{5,7},{6,4},{7,5},{8,10},{9,11},{10,... | collective-permute-start | bytes 393224 | tf_op jit(solution)/shard_map/ppermute | solution.py:277
  37.1 10.7 %collective-permute-start.7 = (bf16[4,128,128]{2,1,0:T(8,128)(2,1)}, bf16[4,128,128]{2,1,0:T(8,128)(2,1)S(1)}, u32[]{:S(2)}, u32[]{:S(2)}) collective-permute-start(bf16[4,128,128]{2,1,0:T(8,128)(2,1)} %copy-done.15), channel_id=1, source_target_pairs={{0,3},{1,2},{2,1},{3,0},{4,7},{5,6},{6,5},{7,4},{8,11},{9,10},{10,... | collective-permute-start | bytes 393224 | tf_op jit(solution)/shard_map/ppermute | solution.py:277
  39.9 25.5 %copy-start.7 = (bf16[4,128,128]{2,1,0:T(8,128)(2,1)}, bf16[4,128,128]{2,1,0:T(8,128)(2,1)S(1)}, u32[]{:S(2)}) copy-start(bf16[4,128,128]{2,1,0:T(8,128)(2,1)S(1)} %collective-permute-done.5.rest_1_) | copy-start | bytes 393220
  47.9 17.6 %copy-start.9 = (bf16[4,128,128]{2,1,0:T(8,128)(2,1)}, bf16[4,128,128]{2,1,0:T(8,128)(2,1)S(1)}, u32[]{:S(2)}) copy-start(bf16[4,128,128]{2,1,0:T(8,128)(2,1)S(1)} %collective-permute-done.6.rest_2_) | copy-start | bytes 393220
  47.9 0.7 copy-start.11
  48.6 14.0 %collective-permute-start.14 = (bf16[16,128,128]{2,1,0:T(8,128)(2,1)}, bf16[16,128,128]{2,1,0:T(8,128)(2,1)S(1)}, u32[]{:S(2)}, u32[]{:S(2)}) collective-permute-start(bf16[16,128,128]{2,1,0:T(8,128)(2,1)} %collective-permute-done.1.rest_2_), channel_id=1, source_target_pairs={{0,16},{4,20},{8,24},{12,28},{16,0},{20,4},{24,8},{28,12},{1,17},{... | collective-permute-start | bytes 1572872 | tf_op jit(solution)/shard_map/ppermute | solution.py:277
  49.0 16.4 %collective-permute-start.12 = (bf16[16,128,128]{2,1,0:T(8,128)(2,1)}, bf16[16,128,128]{2,1,0:T(8,128)(2,1)S(1)}, u32[]{:S(2)}, u32[]{:S(2)}) collective-permute-start(bf16[16,128,128]{2,1,0:T(8,128)(2,1)} %collective-permute-done.1.rest_2_), channel_id=1, source_target_pairs={{0,4},{4,0},{8,12},{12,8},{16,20},{20,16},{24,28},{28,24},{1,5},{5... | collective-permute-start | bytes 1572872 | tf_op jit(solution)/shard_map/ppermute | solution.py:277
  49.0 16.4 %collective-permute-start.13 = (bf16[16,128,128]{2,1,0:T(8,128)(2,1)}, bf16[16,128,128]{2,1,0:T(8,128)(2,1)S(1)}, u32[]{:S(2)}, u32[]{:S(2)}) collective-permute-start(bf16[16,128,128]{2,1,0:T(8,128)(2,1)} %collective-permute-done.2.rest_4_), channel_id=1, source_target_pairs={{0,4},{4,0},{8,12},{12,8},{16,20},{20,16},{24,28},{28,24},{1,5},{5... | collective-permute-start | bytes 1572872 | tf_op jit(solution)/shard_map/ppermute | solution.py:277
  49.7 12.9 %collective-permute-start.11 = (bf16[8,128,128]{2,1,0:T(8,128)(2,1)S(1)}, bf16[8,128,128]{2,1,0:T(8,128)(2,1)S(1)}, u32[]{:S(2)}, u32[]{:S(2)}) collective-permute-start(bf16[8,128,128]{2,1,0:T(8,128)(2,1)S(1)} %get-tuple-element.191), channel_id=1, source_target_pairs={{0,8},{4,12},{8,0},{12,4},{16,24},{20,28},{24,16},{28,20},{1,9},{5... | collective-permute-start | bytes 786440 | tf_op jit(solution)/shard_map/ppermute | solution.py:277
  51.4 14.0 %collective-permute-start.8 = (bf16[8,128,128]{2,1,0:T(8,128)(2,1)S(1)}, bf16[8,128,128]{2,1,0:T(8,128)(2,1)S(1)}, u32[]{:S(2)}, u32[]{:S(2)}) collective-permute-start(bf16[8,128,128]{2,1,0:T(8,128)(2,1)S(1)} %get-tuple-element.193), channel_id=1, source_target_pairs={{0,16},{4,20},{8,24},{12,28},{16,0},{20,4},{24,8},{28,12},{1,17},{... | collective-permute-start | bytes 786440 | tf_op jit(solution)/shard_map/ppermute | solution.py:277
  62.6 23.2 %collective-permute-start.18 = (bf16[16,128,128]{2,1,0:T(8,128)(2,1)S(1)}, bf16[16,128,128]{2,1,0:T(8,128)(2,1)S(1)}, u32[]{:S(2)}, u32[]{:S(2)}) collective-permute-start(bf16[16,128,128]{2,1,0:T(8,128)(2,1)S(1)} %collective-permute-done.14.rest_6_), channel_id=1, source_target_pairs={{0,4},{4,0},{8,12},{12,8},{16,20},{20,16},{24,28},{28,24},{1,5},{5... | collective-permute-start | bytes 1572872 | tf_op jit(solution)/shard_map/ppermute | solution.py:277
  65.4 1.0 copy-start.6
  68.2 17.6 %collective-permute-start.15 = (bf16[4,256,128]{2,1,0:T(8,128)(2,1)}, bf16[4,256,128]{2,1,0:T(8,128)(2,1)}, u32[]{:S(2)}, u32[]{:S(2)}) collective-permute-start(bf16[4,256,128]{2,1,0:T(8,128)(2,1)} %get-tuple-element.125), channel_id=1, source_target_pairs={{0,1},{1,0},{2,3},{3,2},{4,5},{5,4},{6,7},{7,6},{8,9},{9,8},{10,11... | collective-permute-start | bytes 786440 | tf_op jit(solution)/shard_map/ppermute | solution.py:277
  72.1 23.5 %collective-permute-start.16 = (bf16[4,256,128]{2,1,0:T(8,128)(2,1)}, bf16[4,256,128]{2,1,0:T(8,128)(2,1)}, u32[]{:S(2)}, u32[]{:S(2)}) collective-permute-start(bf16[4,256,128]{2,1,0:T(8,128)(2,1)} %get-tuple-element.129), channel_id=1, source_target_pairs={{0,2},{1,3},{2,0},{3,1},{4,6},{5,7},{6,4},{7,5},{8,10},{9,11},{10,... | collective-permute-start | bytes 786440 | tf_op jit(solution)/shard_map/ppermute | solution.py:277
  73.1 22.5 %collective-permute-start.17 = (bf16[4,256,128]{2,1,0:T(8,128)(2,1)}, bf16[4,256,128]{2,1,0:T(8,128)(2,1)}, u32[]{:S(2)}, u32[]{:S(2)}) collective-permute-start(bf16[4,256,128]{2,1,0:T(8,128)(2,1)} %get-tuple-element.130), channel_id=1, source_target_pairs={{0,3},{1,2},{2,1},{3,0},{4,7},{5,6},{6,5},{7,4},{8,11},{9,10},{10,... | collective-permute-start | bytes 786440 | tf_op jit(solution)/shard_map/ppermute | solution.py:277
  85.8 0.8 copy-start.3
  86.6 1.0 copy-start.4
  94.0 36.3 %copy-start.8 = (bf16[4,128,128]{2,1,0:T(8,128)(2,1)S(1)}, bf16[4,128,128]{2,1,0:T(8,128)(2,1)}, u32[]{:S(2)}) copy-start(bf16[4,128,128]{2,1,0:T(8,128)(2,1)} %copy-done.7) | copy-start | bytes 393220
  94.0 36.3 %copy-start.10 = (bf16[4,128,128]{2,1,0:T(8,128)(2,1)S(1)}, bf16[4,128,128]{2,1,0:T(8,128)(2,1)}, u32[]{:S(2)}) copy-start(bf16[4,128,128]{2,1,0:T(8,128)(2,1)} %copy-done.9) | copy-start | bytes 393220
  94.0 36.3 %copy-start.12 = (bf16[4,128,128]{2,1,0:T(8,128)(2,1)S(1)}, bf16[4,128,128]{2,1,0:T(8,128)(2,1)}, u32[]{:S(2)}) copy-start(bf16[4,128,128]{2,1,0:T(8,128)(2,1)} %copy-done.11) | copy-start | bytes 393220
  97.8 11.2 %collective-permute-start.19 = (bf16[4,128,128]{2,1,0:T(8,128)(2,1)S(1)}, bf16[4,128,128]{2,1,0:T(8,128)(2,1)S(1)}, u32[]{:S(2)}, u32[]{:S(2)}) collective-permute-start(bf16[4,128,128]{2,1,0:T(8,128)(2,1)S(1)} %get-tuple-element.143), channel_id=1, source_target_pairs={{0,1},{1,0},{2,3},{3,2},{4,5},{5,4},{6,7},{7,6},{8,9},{9,8},{10,11... | collective-permute-start | bytes 393224 | tf_op jit(solution)/shard_map/ppermute | solution.py:277
  101.5 13.0 %collective-permute-start.20 = (bf16[4,128,128]{2,1,0:T(8,128)(2,1)S(1)}, bf16[4,128,128]{2,1,0:T(8,128)(2,1)S(1)}, u32[]{:S(2)}, u32[]{:S(2)}) collective-permute-start(bf16[4,128,128]{2,1,0:T(8,128)(2,1)S(1)} %get-tuple-element.144), channel_id=1, source_target_pairs={{0,2},{1,3},{2,0},{3,1},{4,6},{5,7},{6,4},{7,5},{8,10},{9,11},{10,... | collective-permute-start | bytes 393224 | tf_op jit(solution)/shard_map/ppermute | solution.py:277
  101.9 12.6 %collective-permute-start.21 = (bf16[4,128,128]{2,1,0:T(8,128)(2,1)S(1)}, bf16[4,128,128]{2,1,0:T(8,128)(2,1)S(1)}, u32[]{:S(2)}, u32[]{:S(2)}) collective-permute-start(bf16[4,128,128]{2,1,0:T(8,128)(2,1)S(1)} %get-tuple-element.145), channel_id=1, source_target_pairs={{0,3},{1,2},{2,1},{3,0},{4,7},{5,6},{6,5},{7,4},{8,11},{9,10},{10,... | collective-permute-start | bytes 393224 | tf_op jit(solution)/shard_map/ppermute | solution.py:277
  104.0 10.5 %collective-permute-start.22 = (bf16[4,128,128]{2,1,0:T(8,128)(2,1)S(1)}, bf16[4,128,128]{2,1,0:T(8,128)(2,1)S(1)}, u32[]{:S(2)}, u32[]{:S(2)}) collective-permute-start(bf16[4,128,128]{2,1,0:T(8,128)(2,1)S(1)} %get-tuple-element.202), channel_id=1, source_target_pairs={{0,1},{1,0},{2,3},{3,2},{4,5},{5,4},{6,7},{7,6},{8,9},{9,8},{10,11... | collective-permute-start | bytes 393224 | tf_op jit(solution)/shard_map/ppermute | solution.py:277
  105.1 17.8 %collective-permute-start.23 = (bf16[4,128,128]{2,1,0:T(8,128)(2,1)S(1)}, bf16[4,128,128]{2,1,0:T(8,128)(2,1)S(1)}, u32[]{:S(2)}, u32[]{:S(2)}) collective-permute-start(bf16[4,128,128]{2,1,0:T(8,128)(2,1)S(1)} %get-tuple-element.201), channel_id=1, source_target_pairs={{0,2},{1,3},{2,0},{3,1},{4,6},{5,7},{6,4},{7,5},{8,10},{9,11},{10,... | collective-permute-start | bytes 393224 | tf_op jit(solution)/shard_map/ppermute | solution.py:277
  109.0 14.0 %collective-permute-start.24 = (bf16[4,128,128]{2,1,0:T(8,128)(2,1)S(1)}, bf16[4,128,128]{2,1,0:T(8,128)(2,1)S(1)}, u32[]{:S(2)}, u32[]{:S(2)}) collective-permute-start(bf16[4,128,128]{2,1,0:T(8,128)(2,1)S(1)} %get-tuple-element.200), channel_id=1, source_target_pairs={{0,3},{1,2},{2,1},{3,0},{4,7},{5,6},{6,5},{7,4},{8,11},{9,10},{10,... | collective-permute-start | bytes 393224 | tf_op jit(solution)/shard_map/ppermute | solution.py:277
  129.7 2.7 %collective-permute-start.32 = (bf16[4,8,128,128]{3,2,1,0:T(8,128)(2,1)S(1)}, bf16[4,8,128,128]{3,2,1,0:T(8,128)(2,1)S(1)}, u32[]{:S(2)}, u32[]{:S(2)}) collective-permute-start(bf16[4,8,128,128]{3,2,1,0:T(8,128)(2,1)S(1)} %get-tuple-element.167), channel_id=1, source_target_pairs={{0,4},{4,0},{8,12},{12,8},{16,20},{20,16},{24,28},{28,24},{1,5},{5... | collective-permute-start | bytes 3145736 | tf_op jit(solution)/shard_map/ppermute | solution.py:277
  129.8 11.9 %collective-permute-start.25 = (bf16[4,8,128,128]{3,2,1,0:T(8,128)(2,1)S(1)}, bf16[4,8,128,128]{3,2,1,0:T(8,128)(2,1)S(1)}, u32[]{:S(2)}, u32[]{:S(2)}) collective-permute-start(bf16[4,8,128,128]{3,2,1,0:T(8,128)(2,1)S(1)} %get-tuple-element.152), channel_id=1, source_target_pairs={{0,4},{4,0},{8,12},{12,8},{16,20},{20,16},{24,28},{28,24},{1,5},{5... | collective-permute-start | bytes 3145736 | tf_op jit(solution)/shard_map/ppermute | solution.py:277
  132.2 11.3 %collective-permute-start.27 = (bf16[4,128,512]{2,1,0:T(8,128)(2,1)S(1)}, bf16[4,128,512]{2,1,0:T(8,128)(2,1)S(1)}, u32[]{:S(2)}, u32[]{:S(2)}) collective-permute-start(bf16[4,128,512]{2,1,0:T(8,128)(2,1)S(1)} %get-tuple-element.164), channel_id=1, source_target_pairs={{0,4},{4,0},{8,12},{12,8},{16,20},{20,16},{24,28},{28,24},{1,5},{5... | collective-permute-start | bytes 1572872 | tf_op jit(solution)/shard_map/ppermute | solution.py:277
  132.8 26.2 %collective-permute-start.33 = (bf16[2,8,128,128]{3,2,1,0:T(8,128)(2,1)S(1)}, bf16[2,8,128,128]{3,2,1,0:T(8,128)(2,1)S(1)}, u32[]{:S(2)}, u32[]{:S(2)}) collective-permute-start(bf16[2,8,128,128]{3,2,1,0:T(8,128)(2,1)S(1)} %get-tuple-element.179), channel_id=1, source_target_pairs={{0,16},{4,20},{8,24},{12,28},{16,0},{20,4},{24,8},{28,12},{1,17},{... | collective-permute-start | bytes 1572872 | tf_op jit(solution)/shard_map/ppermute | solution.py:277
  142.0 17.0 %collective-permute-start.26 = (bf16[2,8,128,128]{3,2,1,0:T(8,128)(2,1)S(1)}, bf16[2,8,128,128]{3,2,1,0:T(8,128)(2,1)S(1)}, u32[]{:S(2)}, u32[]{:S(2)}) collective-permute-start(bf16[2,8,128,128]{3,2,1,0:T(8,128)(2,1)S(1)} %get-tuple-element.181), channel_id=1, source_target_pairs={{0,8},{4,12},{8,0},{12,4},{16,24},{20,28},{24,16},{28,20},{1,9},{5... | collective-permute-start | bytes 1572872 | tf_op jit(solution)/shard_map/ppermute | solution.py:277
  143.8 7.0 %collective-permute-start.28 = (bf16[128,512]{1,0:T(8,128)(2,1)S(1)}, bf16[128,512]{1,0:T(8,128)(2,1)S(1)}, u32[]{:S(2)}, u32[]{:S(2)}) collective-permute-start(bf16[128,512]{1,0:T(8,128)(2,1)S(1)} %get-tuple-element.199), channel_id=1, source_target_pairs={{0,1},{1,0},{2,3},{3,2},{4,5},{5,4},{6,7},{7,6},{8,9},{9,8},{10,11... | collective-permute-start | bytes 393224 | tf_op jit(solution)/shard_map/ppermute | solution.py:277
  146.6 12.4 %collective-permute-start.29 = (bf16[128,512]{1,0:T(8,128)(2,1)S(1)}, bf16[128,512]{1,0:T(8,128)(2,1)S(1)}, u32[]{:S(2)}, u32[]{:S(2)}) collective-permute-start(bf16[128,512]{1,0:T(8,128)(2,1)S(1)} %get-tuple-element.198), channel_id=1, source_target_pairs={{0,2},{1,3},{2,0},{3,1},{4,6},{5,7},{6,4},{7,5},{8,10},{9,11},{10,... | collective-permute-start | bytes 393224 | tf_op jit(solution)/shard_map/ppermute | solution.py:277
  146.6 12.4 %collective-permute-start.30 = (bf16[128,512]{1,0:T(8,128)(2,1)S(1)}, bf16[128,512]{1,0:T(8,128)(2,1)S(1)}, u32[]{:S(2)}, u32[]{:S(2)}) collective-permute-start(bf16[128,512]{1,0:T(8,128)(2,1)S(1)} %get-tuple-element.197), channel_id=1, source_target_pairs={{0,3},{1,2},{2,1},{3,0},{4,7},{5,6},{6,5},{7,4},{8,11},{9,10},{10,... | collective-permute-start | bytes 393224 | tf_op jit(solution)/shard_map/ppermute | solution.py:277
  159.1 6.5 %collective-permute-start.35 = (bf16[128,512]{1,0:T(8,128)(2,1)S(1)}, bf16[128,512]{1,0:T(8,128)(2,1)S(1)}, u32[]{:S(2)}, u32[]{:S(2)}) collective-permute-start(bf16[128,512]{1,0:T(8,128)(2,1)S(1)} %add_convert_fusion.13), channel_id=1, source_target_pairs={{0,8},{4,12},{8,0},{12,4},{16,24},{20,28},{24,16},{28,20},{1,9},{5... | collective-permute-start | bytes 393224 | tf_op jit(solution)/shard_map/ppermute | solution.py:277
  159.9 10.9 %collective-permute-start.34 = (bf16[8,128,128]{2,1,0:T(8,128)(2,1)S(1)}, bf16[8,128,128]{2,1,0:T(8,128)(2,1)S(1)}, u32[]{:S(2)}, u32[]{:S(2)}) collective-permute-start(bf16[8,128,128]{2,1,0:T(8,128)(2,1)S(1)} %get-tuple-element.187), channel_id=1, source_target_pairs={{0,8},{4,12},{8,0},{12,4},{16,24},{20,28},{24,16},{28,20},{1,9},{5... | collective-permute-start | bytes 786440 | tf_op jit(solution)/shard_map/ppermute | solution.py:277
  165.6 5.0 %collective-permute-start.36 = (bf16[128,512]{1,0:T(8,128)(2,1)S(1)}, bf16[128,512]{1,0:T(8,128)(2,1)S(1)}, u32[]{:S(2)}, u32[]{:S(2)}) collective-permute-start(bf16[128,512]{1,0:T(8,128)(2,1)S(1)} %add_convert_fusion.12), channel_id=1, source_target_pairs={{0,16},{4,20},{8,24},{12,28},{16,0},{20,4},{24,8},{28,12},{1,17},{... | collective-permute-start | bytes 393224 | tf_op jit(solution)/shard_map/ppermute | solution.py:277
  166.9 6.5 %collective-permute-start.31 = (bf16[8,128,128]{2,1,0:T(8,128)(2,1)S(1)}, bf16[8,128,128]{2,1,0:T(8,128)(2,1)S(1)}, u32[]{:S(2)}, u32[]{:S(2)}) collective-permute-start(bf16[8,128,128]{2,1,0:T(8,128)(2,1)S(1)} %get-tuple-element.189), channel_id=1, source_target_pairs={{0,16},{4,20},{8,24},{12,28},{16,0},{20,4},{24,8},{28,12},{1,17},{... | collective-permute-start | bytes 786440 | tf_op jit(solution)/shard_map/ppermute | solution.py:277
  170.7 4.3 %collective-permute-start.37 = (f32[128,512]{1,0:T(8,128)S(1)}, f32[128,512]{1,0:T(8,128)S(1)}, u32[]{:S(2)}, u32[]{:S(2)}) collective-permute-start(f32[128,512]{1,0:T(8,128)S(1)} %convert_add_fusion.5), channel_id=1, source_target_pairs={{0,4},{4,0},{8,12},{12,8},{16,20},{20,16},{24,28},{28,24},{1,5},{5... | collective-permute-start | bytes 786440 | tf_op jit(solution)/shard_map/ppermute | solution.py:277
Sparse Core Ops, SparseCore 0:
  26.6 57.8 all-gather.2

commit v5 on v4

v5 whole, which is shorter than its diff:
```python
import functools

import jax
import jax.numpy as jnp
from jax import lax
from jax.experimental import pallas as pl
from jax.experimental.pallas import tpu as pltpu
from jax.sharding import PartitionSpec as P

VMEM_LIMIT = 48 * 1024 * 1024
GROUPS = 2
COPIES = 4
F32 = jnp.float32
BF16 = jnp.bfloat16
VMEM = pl.BlockSpec(memory_space=pltpu.VMEM)
SMEM = pl.BlockSpec(memory_space=pltpu.SMEM)
PARAMS = pltpu.CompilerParams(vmem_limit_bytes=VMEM_LIMIT)


def tile_copy(tiles_ref, held, sems, i):
    per = held.shape[0] // COPIES
    part = pl.ds(i * per, per)
    return pltpu.make_async_copy(tiles_ref.at[part], held.at[part], sems.at[i])


def over_rows(tiles_ref, held, sems, one_row):
    per = held.shape[0] // COPIES

    def piece(i, carry):
        tile_copy(tiles_ref, held, sems, i).wait()
        for j in range(per):
            one_row(i * per + j)
        return carry

    lax.fori_loop(0, COPIES, piece, 0)


def spread_kernel(first, cols_ref, me_ref, tiles_ref, *rest):
    if first:
        vals_ref, mask_ref, *rest = rest
        outs, (mask_out, acc, held, sems, left_ref, mask_held) = rest[: 2 * GROUPS], rest[2 * GROUPS :]
        loads = [
            pltpu.make_async_copy(vals_ref, left_ref, sems.at[COPIES]),
            pltpu.make_async_copy(mask_ref, mask_held, sems.at[COPIES + 1]),
        ]
        loads[0].start()
    else:
        vals, rest = rest[:GROUPS], rest[GROUPS:]
        outs, (acc, held, sems, left_ref) = rest[: 2 * GROUPS], rest[2 * GROUPS :]
    for i in range(COPIES):
        tile_copy(tiles_ref, held, sems, i).start()
    if first:
        loads[1].start()
    acc[...] = jnp.zeros_like(acc)
    per_row, size = held.shape[1], held.shape[3]
    me = me_ref[0]
    if first:
        loads[0].wait()
    else:
        for g in range(GROUPS):
            count = vals[g].shape[0]
            left_ref[g * count : (g + 1) * count] = vals[g][...]

    def one_row(r):
        left = left_ref[r].astype(F32).T.astype(BF16) if first else left_ref[r]
        for k in range(0, per_row, 2):
            pair = jnp.concatenate([held[r, k], held[r, k + 1]], axis=1)
            both = jnp.dot(left, pair, preferred_element_type=F32)
            for side in range(2):
                acc[cols_ref[r, k + side]] += both[:, side * size : (side + 1) * size]

    over_rows(tiles_ref, held, sems, one_row)
    halves, count = outs[0].shape[:2]
    for g in range(GROUPS):
        for side in range(2):
            for rel in range(halves):
                owner = jnp.bitwise_xor(me, 2 * rel + side)
                start = (owner * GROUPS + g) * count
                outs[2 * g + side][rel] = acc[pl.ds(start, count)].astype(BF16)
    if first:
        loads[1].wait()
        for b in range(mask_held.shape[0]):
            mask_out[b] = mask_held[b].astype(F32).T.astype(BF16)


def spread(edge_tiles, block_cols, vals, me, rows, mask=None):
    blocks, _, size, _ = edge_tiles.shape
    first = mask is not None
    feat = vals[0].shape[2] if first else vals[0].shape[1]
    out = jax.ShapeDtypeStruct((rows // 2, blocks // GROUPS, feat, size), BF16)
    outs = [out] * (2 * GROUPS)
    scratch = [
        pltpu.VMEM((rows * blocks, feat, size), F32),
        pltpu.VMEM(edge_tiles.shape, BF16),
        pltpu.SemaphoreType.DMA((COPIES + 2,)),
    ]
    anywhere = pl.BlockSpec(memory_space=pl.ANY)
    if first:
        outs.append(jax.ShapeDtypeStruct((blocks, feat, size), BF16))
        scratch += [pltpu.VMEM(v.shape, v.dtype) for v in (vals[0], mask)]
        args, place = [vals[0], mask], anywhere
    else:
        scratch.append(pltpu.VMEM((blocks, feat, size), BF16))
        args, place = vals, VMEM
    return pl.pallas_call(
        functools.partial(spread_kernel, first),
        out_shape=outs,
        in_specs=[SMEM, SMEM, anywhere] + [place] * len(args),
        out_specs=[VMEM] * len(outs),
        scratch_shapes=scratch,
        compiler_params=PARAMS,
        cost_estimate=pl.CostEstimate(flops=2 * edge_tiles.size * feat, bytes_accessed=30_000_000, transcendentals=0),
        name="spread",
    )(block_cols, me, edge_tiles, *args)


def aggregate_kernel(cols_ref, tiles_ref, values_ref, out_ref, held, table, sems):
    load = pltpu.make_async_copy(values_ref, table, sems.at[COPIES])
    load.start()
    for i in range(COPIES):
        tile_copy(tiles_ref, held, sems, i).start()
    load.wait()
    per_row = held.shape[1]

    def one_row(r):
        total = None
        for k in range(0, per_row, 2):
            pair = jnp.concatenate([held[r, k], held[r, k + 1]], axis=1)
            picked = jnp.concatenate([table[cols_ref[r, k]], table[cols_ref[r, k + 1]]], axis=0)
            term = jnp.dot(pair, picked, preferred_element_type=F32)
            total = term if total is None else total + term
        out_ref[r] = total.astype(BF16)

    over_rows(tiles_ref, held, sems, one_row)


def aggregate(edge_tiles, block_cols, values):
    blocks, _, size, _ = edge_tiles.shape
    feat = values.shape[2]
    anywhere = pl.BlockSpec(memory_space=pl.ANY)
    return pl.pallas_call(
        aggregate_kernel,
        out_shape=jax.ShapeDtypeStruct((blocks, size, feat), BF16),
        in_specs=[SMEM, anywhere, anywhere],
        out_specs=VMEM,
        scratch_shapes=[
            pltpu.VMEM(edge_tiles.shape, BF16),
            pltpu.VMEM(values.shape, BF16),
            pltpu.SemaphoreType.DMA((COPIES + 1,)),
        ],
        compiler_params=PARAMS,
        cost_estimate=pl.CostEstimate(flops=2 * edge_tiles.size * feat, bytes_accessed=20_000_000, transcendentals=0),
        name="aggregate",
    )(block_cols, edge_tiles, values)


def sum_kernel(keep_ref, got_ref, out_ref):
    out_ref[...] = (keep_ref[...].astype(F32) + got_ref[...].astype(F32)).astype(BF16)


def last_sum(keep, got):
    return pl.pallas_call(
        sum_kernel,
        out_shape=jax.ShapeDtypeStruct(keep.shape, BF16),
        in_specs=[VMEM] * 2,
        out_specs=VMEM,
        compiler_params=PARAMS,
        name="last_sum",
    )(keep, got)


def finish_kernel(*refs):
    parts, out_ref = refs[:-1], refs[-1]
    count = parts[0].shape[0]
    for g in range(GROUPS):
        for b in range(count):
            total = parts[2 * g][b].astype(F32) + parts[2 * g + 1][b].astype(F32)
            out_ref[g * count + b] = total.T.astype(BF16)


def finish(parts):
    count, feat, size = parts[0].shape
    return pl.pallas_call(
        finish_kernel,
        out_shape=jax.ShapeDtypeStruct((count * GROUPS, size, feat), BF16),
        in_specs=[VMEM] * len(parts),
        out_specs=VMEM,
        compiler_params=PARAMS,
        name="finish",
    )(*parts)


def dense_kernel(cols, masked, col_ref, weight_ref, *rest):
    shards, rest = rest[: 2 * cols - 1], rest[2 * cols - 1 :]
    side_ref, rest = rest[0], rest[1:]
    if masked:
        mask_ref, rest = rest[0], rest[1:]
    out_ref, grad_ref, whole_ref = rest
    own, ups, downs = shards[0], shards[1:cols], shards[cols:]
    col = col_ref[0]
    blocks, feat, size = own.shape
    for s in range(cols):
        place = lax.rem(col - s + cols, cols)
        for b in range(blocks):
            part = own[b] if s == 0 else jnp.where(col >= s, ups[s - 1][b], downs[cols - s - 1][b])
            whole_ref[place, :, b * size : (b + 1) * size] = part
    whole = jnp.concatenate([whole_ref[q] for q in range(cols)], axis=0)
    res = jnp.dot(weight_ref[...], whole, preferred_element_type=F32)
    for b in range(blocks):
        part = res[:, b * size : (b + 1) * size]
        out_ref[b] = (part * mask_ref[b].astype(F32) if masked else part).astype(BF16)
    side = jnp.concatenate([side_ref[b] for b in range(blocks)], axis=0)
    grad_ref[...] = jnp.dot(whole, side, preferred_element_type=F32)


def dense(weight, shards, side, mask, col, cols):
    blocks, feat, size = shards[0].shape
    args = [weight, *shards, side] + ([] if mask is None else [mask])
    return pl.pallas_call(
        functools.partial(dense_kernel, cols, mask is not None),
        out_shape=[
            jax.ShapeDtypeStruct((blocks, feat, size), BF16),
            jax.ShapeDtypeStruct((cols * feat, side.shape[2]), F32),
        ],
        in_specs=[SMEM] + [VMEM] * len(args),
        out_specs=[VMEM, VMEM],
        scratch_shapes=[pltpu.VMEM((cols, feat, blocks * size), BF16)],
        compiler_params=PARAMS,
        name="dense",
    )(col, *args)


def weight_terms_kernel(me_ref, *refs):
    firsts, seconds = refs[:GROUPS], refs[GROUPS : 2 * GROUPS]
    keep_ref, send_ref = refs[2 * GROUPS :]
    first, second = sum(r[...] for r in firsts).T, sum(r[...] for r in seconds).T
    even = jnp.bitwise_and(me_ref[0], 1) == 0
    keep_ref[...] = jnp.where(even, second, first)
    send_ref[...] = jnp.where(even, first, second).astype(BF16)


def weight_terms(firsts, seconds, me):
    shape = firsts[0].shape[::-1]
    return pl.pallas_call(
        weight_terms_kernel,
        out_shape=[jax.ShapeDtypeStruct(shape, F32), jax.ShapeDtypeStruct(shape, BF16)],
        in_specs=[SMEM] + [VMEM] * (2 * GROUPS),
        out_specs=[VMEM] * 2,
        compiler_params=PARAMS,
        name="weight_terms",
    )(me, *firsts, *seconds)


def swap(value, mask, axis):
    return lax.ppermute(value, axis, [(i, i ^ mask) for i in range(lax.axis_size(axis))])


def add(a, b):
    return (a.astype(F32) + b.astype(F32)).astype(BF16)


def scatter_group(keep, got, masks, beside):
    left = sorted(masks, reverse=True)
    for mask in masks:
        axis = left.index(mask)
        part = lambda v, i: lax.index_in_dim(v, i, axis, keepdims=False)
        sent = swap(add(part(keep, 1), part(got, 1)), mask, "row")
        keep = add(part(keep, 0), part(got, 0))
        got = sent
        left.remove(mask)
        if beside is not None and mask == masks[0]:
            got, beside = lax.optimization_barrier((got, beside))
    return [keep, got], beside


def scatter(pieces, rows, beside=None):
    masks = [1 << b for b in range(1, rows.bit_length() - 1)]
    lead = (2,) * len(masks)
    done = []
    for g in range(GROUPS):
        keep, got = pieces[2 * g], swap(pieces[2 * g + 1], 1, "row")
        order = masks if g % 2 == 0 else masks[::-1]
        terms, beside = scatter_group(keep.reshape(lead + keep.shape[1:]), got.reshape(lead + got.shape[1:]), order, beside)
        done.append(terms)
    return done, beside


def chain_gather(own, cols):
    ups, downs = [], []
    up, down = own, own
    for s in range(1, cols):
        up = lax.ppermute(up, "col", [(i, i + 1) for i in range(s - 1, cols - 1)])
        down = lax.ppermute(down, "col", [(i, i - 1) for i in range(1, cols - s + 1)])
        ups.append(up)
        downs.append(down)
    return [own, *ups, *downs]


def reduced(value, me):
    mask = 2
    while mask < lax.axis_size("row"):
        value = value.astype(BF16)
        value = value.astype(F32) + swap(value, mask, "row").astype(F32)
        mask *= 2
    other = swap(value, 1, "row")
    even = me % 2 == 0
    return jnp.where(even, other, value), jnp.where(even, value, other)


def per_device(
    node_feats, hidden_act, grad_out, relu_mask, edge_tiles, block_cols, weight_one, weight_two
):
    rows, cols = lax.axis_size("row"), lax.axis_size("col")
    me, col = lax.axis_index("row").astype(jnp.int32), lax.axis_index("col").astype(jnp.int32)
    me_at, col_at = me.reshape(1), col.reshape(1)
    size = edge_tiles.shape[2]
    per = edge_tiles.shape[0] // GROUPS
    blocked = lambda v: v.reshape(v.shape[0] // size, size, v.shape[1])
    cut = lambda v, g: v[g * per : (g + 1) * per]

    *pieces, mask = spread(edge_tiles, block_cols, [blocked(grad_out)], me_at, rows, blocked(relu_mask))
    terms, _ = scatter(pieces, rows)
    terms, node_feats = lax.optimization_barrier((terms, node_feats))
    table = blocked(lax.all_gather(node_feats, "row", axis=0, tiled=True))
    deltas, seconds, inputs, firsts = [], [], [], []
    hidden = blocked(hidden_act)
    for g in range(GROUPS):
        shards = chain_gather(last_sum(*terms[g]), cols)
        delta, grad = dense(weight_two, shards, cut(hidden, g), cut(mask, g), col_at, cols)
        deltas.append(delta)
        seconds.append(grad)
    agg_feats = aggregate(edge_tiles, block_cols, table)
    for g in range(GROUPS):
        shards = chain_gather(deltas[g], cols)
        out, grad = dense(weight_one, shards, cut(agg_feats, g), None, col_at, cols)
        inputs.append(out)
        firsts.append(grad)
    pieces = spread(edge_tiles, block_cols, inputs, me_at, rows)
    keep, send = weight_terms(firsts, seconds, me_at)
    terms, value = scatter(pieces, rows, keep + swap(send, 1, "row").astype(F32))
    out = finish([t for pair in terms for t in pair])
    first_grad, second_grad = reduced(value, me)
    return out.reshape(-1, out.shape[2]), first_grad, second_grad


def solution(mesh):
    in_specs = (
        P("row", "col"),
        P("row", "col"),
        P("row", "col"),
        P("row", "col"),
        P("row", None, None, None),
        P("row", None),
        P("col", None),
        P("col", None),
    )
    out_specs = (P("row", "col"), P("col", None), P("col", None))
    return jax.shard_map(
        per_device, mesh=mesh, in_specs=in_specs, out_specs=out_specs, check_vma=False
    )
```

time: 183 us -> 175 us (0.956)
  waiting for transfers between devices: 71.4 us -> 60.9 us
  starting transfers between devices: 51.9 us -> 60.7 us
  other arithmetic: 7.14 us -> 3.07 us
  local copies, waits for them, and re-layouts: 9.22 us -> 5.84 us
    ppermute x0 -> x24, starting transfers between devices: none -> 42.4 us  [the longest x12 26.9 us: chain_gather(): up = lax.ppermute(up, 'col', [(i, i + 1) for i in range(s - 1, cols - 1)])]
    ppermute x38 -> x16, starting transfers between devices: 51.8 us -> 18.3 us  [swap(): lax.ppermute(value, axis, [(i, i ^ mask) for i in range(lax.axis_size(axi...]
    ppermute x38 -> x16, waiting for transfers between devices: 61.6 us -> 39 us  [swap(): lax.ppermute(value, axis, [(i, i ^ mask) for i in range(lax.axis_size(axi...]
    ppermute x0 -> x24, waiting for transfers between devices: none -> 21.9 us  [the longest x12 21.8 us: chain_gather(): lax.ppermute(down, 'col', [(i, i - 1) for i in range(1, cols - s + 1)])]
    all_gather x1, waiting for transfers between devices: 9.88 us -> 0.02 us  [per_device(): table = blocked(lax.all_gather(node_feats, 'row', axis=0, tiled=True))]
    unnamed x34 -> x20, local copies, waits for them, and re-layouts: 7.83 us -> 4.64 us
    convert_element_type x8, other arithmetic: 4.49 us -> 2.12 us  [add(): return (a.astype(F32) + b.astype(F32)).astype(BF16)]
    pallas_call x6 -> x10, Pallas kernels: 22.4 us -> 21.8 us  [the longest x2 13.6 us: spread(): pl.pallas_call(functools.partial(spread_kernel, first), out_shape=outs, i...]
  transfers between devices with their start and end apart: 39 -> 41, of which waited for: 17 -> 18; matrix products, arithmetic and copies ran while one was open for 4% -> 2% of each run, Pallas kernels for 11% -> 8%
where the time goes in v5:
time: 175 us; the launch traced here: 173 us
  waiting for transfers between devices  60.9 us (35%)
  starting transfers between devices  60.7 us (35%)
  Pallas kernels  27.9 us (16%)
  between operations  14.6 us (8%)
  local copies, waits for them, and re-layouts  5.84 us (3%)
  other arithmetic  3.07 us (2%)
    ppermute x16, waiting for transfers between devices, swap(): lax.ppermute(value, axis, [(i, i ^ mask) for i in range(lax.axis_size(axi...  39 us
    ppermute x12, starting transfers between devices, chain_gather(): up = lax.ppermute(up, 'col', [(i, i + 1) for i in range(s - 1, cols - 1)])  26.9 us
    ppermute x12, waiting for transfers between devices, chain_gather(): lax.ppermute(down, 'col', [(i, i - 1) for i in range(1, cols - s + 1)])  21.8 us
    ppermute x16, starting transfers between devices, swap(): lax.ppermute(value, axis, [(i, i ^ mask) for i in range(lax.axis_size(axi...  18.3 us
    ppermute x12, starting transfers between devices, chain_gather(): lax.ppermute(down, 'col', [(i, i - 1) for i in range(1, cols - s + 1)])  15.4 us
    pallas_call x2, Pallas kernels, spread(): pl.pallas_call(functools.partial(spread_kernel, first), out_shape=outs, i...  13.6 us
    pallas_call x4, Pallas kernels, dense(): pl.pallas_call(functools.partial(dense_kernel, cols, mask is not None), o...  6.89 us
    pallas_call x1, Pallas kernels, aggregate(): pl.pallas_call(aggregate_kernel, out_shape=jax.ShapeDtypeStruct((blocks,...  6.09 us
  transfers between devices with their start and end apart: 41, of which 18 were waited for; matrix products, arithmetic and copies ran while one was open for 2% of the time, Pallas kernels for 8%

profile of v5, /device:TPU:0, one launch (start us, length us, event | category | flops | bytes accessed | tf_op | source)
XLA Modules:
  0.0 173.0 jit_solution(5882832310210292023)
XLA Ops:
  7.2 1.0 copy-done.2
  8.3 0.7 copy-done.8
  9.0 7.0 %spread.2 = (bf16[4,8,128,128]{3,2,1,0:T(8,128)(2,1)S(1)}, bf16[4,8,128,128]{3,2,1,0:T(8,128)(2,1)S(1)}, bf16[4,8,128,128]{3,2,1,0:T(8,128)(2,1)S(1)}, bf16[4,8,...) custom-call(s32[16,20]{1,0:T(8,128)S(1)} %copy-done.8, s32[1]{0:T(128)} %bitcast.me_ref, ...), custom_call_target="tpu_custom_call" | custom-call | flops 1342177280 | bytes 30000000 | tf_op jit(solution)/shard_map/spread/pallas_call | solution.py:105
  16.6 2.2 %collective-permute-done = bf16[4,8,128,128]{3,2,1,0:T(8,128)(2,1)S(1)} collective-permute-done((bf16[4,8,128,128]{3,2,1,0:T(8,128)(2,1)S(1)}, bf16[4,8,128,128]{3,2,1,0:T(8,128)(2,1)S(1)}, u32[]{:S(2)}, u32[]{:S(2)}) %collective-permute-start) | collective-permute-done | bytes 1048608 | tf_op jit(solution)/shard_map/ppermute | solution.py:255
  19.2 2.9 %collective-permute-start.1 = (bf16[2,8,128,128]{3,2,1,0:T(8,128)(2,1)S(1)}, bf16[2,8,128,128]{3,2,1,0:T(8,128)(2,1)S(1)}, u32[]{:S(2)}, u32[]{:S(2)}) collective-permute-start(bf16[2,8,128,128]{3,2,1,0:T(8,128)(2,1)S(1)} %get-tuple-element.66), channel_id=1, source_target_pairs={{0,8},{4,12},{8,0},{12,4},{16,24},{20,28},{24,16},{28,20},{1,9},{5... | collective-permute-start | bytes 1572872 | tf_op jit(solution)/shard_map/ppermute | solution.py:255
  22.6 1.6 collective-permute-start.4
  24.1 10.2 %collective-permute-done.1 = bf16[2,8,128,128]{3,2,1,0:T(8,128)(2,1)S(1)} collective-permute-done((bf16[2,8,128,128]{3,2,1,0:T(8,128)(2,1)S(1)}, bf16[2,8,128,128]{3,2,1,0:T(8,128)(2,1)S(1)}, u32[]{:S(2)}, u32[]{:S(2)}) %collective-permute-start.1) | collective-permute-done | bytes 524320 | tf_op jit(solution)/shard_map/ppermute | solution.py:255
  34.5 1.8 %collective-permute-start.2 = (bf16[8,128,128]{2,1,0:T(8,128)(2,1)S(1)}, bf16[8,128,128]{2,1,0:T(8,128)(2,1)S(1)}, u32[]{:S(2)}, u32[]{:S(2)}) collective-permute-start(bf16[8,128,128]{2,1,0:T(8,128)(2,1)S(1)} %get-tuple-element.73), channel_id=1, source_target_pairs={{0,16},{4,20},{8,24},{12,28},{16,0},{20,4},{24,8},{28,12},{1,17},{... | collective-permute-start | bytes 786440 | tf_op jit(solution)/shard_map/ppermute | solution.py:255
  36.5 1.6 collective-permute-start.5
  38.1 4.4 %collective-permute-done.2.got_ref = bf16[8,128,128]{2,1,0:T(8,128)(2,1)S(1)} collective-permute-done((bf16[8,128,128]{2,1,0:T(8,128)(2,1)S(1)}, bf16[8,128,128]{2,1,0:T(8,128)(2,1)S(1)}, u32[]{:S(2)}, u32[]{:S(2)}) %collective-permute-start.2) | collective-permute-done | bytes 262176 | tf_op jit(solution)/shard_map/ppermute | solution.py:255
  42.4 1.4 collective-permute-done.5.got_ref
  43.9 1.3 collective-permute-start.21
  45.2 4.6 %collective-permute-start.18 = (bf16[8,128,128]{2,1,0:T(8,128)(2,1)S(1)}, bf16[8,128,128]{2,1,0:T(8,128)(2,1)S(1)}, u32[]{:S(2)}, u32[]{:S(2)}) collective-permute-start(bf16[8,128,128]{2,1,0:T(8,128)(2,1)S(1)} %last_sum.3.rest_0_), channel_id=1, source_target_pairs={{0,1},{1,2},{2,3},{4,5},{5,6},{6,7},{8,9},{9,10},{10,11},{12,13},{... | collective-permute-start | bytes 786440 | tf_op jit(solution)/shard_map/ppermute | solution.py:292
  49.8 1.3 collective-permute-start.9
  51.1 4.6 %collective-permute-start.6 = (bf16[8,128,128]{2,1,0:T(8,128)(2,1)S(1)}, bf16[8,128,128]{2,1,0:T(8,128)(2,1)S(1)}, u32[]{:S(2)}, u32[]{:S(2)}) collective-permute-start(bf16[8,128,128]{2,1,0:T(8,128)(2,1)S(1)} %last_sum.2.rest_0_), channel_id=1, source_target_pairs={{0,1},{1,2},{2,3},{4,5},{5,6},{6,7},{8,9},{9,10},{10,11},{12,13},{... | collective-permute-start | bytes 786440 | tf_op jit(solution)/shard_map/ppermute | solution.py:292
  55.7 1.3 collective-permute-start.22
  57.0 1.4 collective-permute-start.19
  59.0 1.3 collective-permute-start.10
  60.3 0.7 collective-permute-start.7
  60.9 4.0 %collective-permute-done.22.rest_5_ = bf16[8,128,128]{2,1,0:T(8,128)(2,1)S(1)} collective-permute-done((bf16[8,128,128]{2,1,0:T(8,128)(2,1)S(1)}, bf16[8,128,128]{2,1,0:T(8,128)(2,1)S(1)}, u32[]{:S(2)}, u32[]{:S(2)}) %collective-permute-start.22) | collective-permute-done | bytes 262176 | tf_op jit(solution)/shard_map/ppermute | solution.py:293
  64.9 1.3 collective-permute-start.23
  66.2 1.4 collective-permute-start.20
  67.6 5.0 %collective-permute-done.10.rest_5_ = bf16[8,128,128]{2,1,0:T(8,128)(2,1)S(1)} collective-permute-done((bf16[8,128,128]{2,1,0:T(8,128)(2,1)S(1)}, bf16[8,128,128]{2,1,0:T(8,128)(2,1)S(1)}, u32[]{:S(2)}, u32[]{:S(2)}) %collective-permute-start.10) | collective-permute-done | bytes 262176 | tf_op jit(solution)/shard_map/ppermute | solution.py:293
  72.5 1.3 collective-permute-start.11
  73.8 1.4 collective-permute-start.8
  75.2 1.1 fusion.16
  76.4 2.0 %collective-permute-done.23.rest_6_ = bf16[8,128,128]{2,1,0:T(8,128)(2,1)} collective-permute-done((bf16[8,128,128]{2,1,0:T(8,128)(2,1)S(1)}, bf16[8,128,128]{2,1,0:T(8,128)(2,1)}, u32[]{:S(2)}, u32[]{:S(2)}) %collective-permute-start.23) | collective-permute-done | bytes 262176 | tf_op jit(solution)/shard_map/ppermute | solution.py:293
  78.4 2.1 %dense.6 = (bf16[8,128,128]{2,1,0:T(8,128)(2,1)S(1)}, f32[512,128]{1,0:T(8,128)S(1)}) custom-call(s32[1]{0:T(128)} %bitcast.1.col_ref, bf16[128,512]{1,0:T(8,128)(2,1)S(1)} %copy-done.3, bf16[8,128,128]{2,1,0:T(8,128)(2,1)S(1)} %last_sum.3.rest_0_, bf16[8,128,128]{2,1,0:T(8,128)(2,1)S(1)} %collective-permute-done.18.rest_1_, ...), custom_call_target="tpu_custom_call" | custom-call | tf_op jit(solution)/shard_map/dense/pallas_call | solution.py:219
  80.5 1.3 collective-permute-start.27
  81.8 4.6 %collective-permute-start.24 = (bf16[8,128,128]{2,1,0:T(8,128)(2,1)S(1)}, bf16[8,128,128]{2,1,0:T(8,128)(2,1)S(1)}, u32[]{:S(2)}, u32[]{:S(2)}) collective-permute-start(bf16[8,128,128]{2,1,0:T(8,128)(2,1)S(1)} %get-tuple-element.43.rest_0_), channel_id=1, source_target_pairs={{0,1},{1,2},{2,3},{4,5},{5,6},{6,7},{8,9},{9,10},{10,11},{12,13},{... | collective-permute-start | bytes 786440 | tf_op jit(solution)/shard_map/ppermute | solution.py:292
  86.3 2.0 %dense.4 = (bf16[8,128,128]{2,1,0:T(8,128)(2,1)S(1)}, f32[512,128]{1,0:T(8,128)S(1)}) custom-call(s32[1]{0:T(128)} %bitcast.1.col_ref, bf16[128,512]{1,0:T(8,128)(2,1)S(1)} %copy-done.3, bf16[8,128,128]{2,1,0:T(8,128)(2,1)S(1)} %last_sum.2.rest_0_, bf16[8,128,128]{2,1,0:T(8,128)(2,1)S(1)} %collective-permute-done.6.rest_1_, ...), custom_call_target="tpu_custom_call" | custom-call | tf_op jit(solution)/shard_map/dense/pallas_call | solution.py:219
  88.3 0.7 copy-done.6
  89.0 1.3 collective-permute-start.15
  90.3 4.9 %collective-permute-start.12 = (bf16[8,128,128]{2,1,0:T(8,128)(2,1)S(1)}, bf16[8,128,128]{2,1,0:T(8,128)(2,1)S(1)}, u32[]{:S(2)}, u32[]{:S(2)}) collective-permute-start(bf16[8,128,128]{2,1,0:T(8,128)(2,1)S(1)} %get-tuple-element.38.rest_0_), channel_id=1, source_target_pairs={{0,1},{1,2},{2,3},{4,5},{5,6},{6,7},{8,9},{9,10},{10,11},{12,13},{... | collective-permute-start | bytes 786440 | tf_op jit(solution)/shard_map/ppermute | solution.py:292
  95.2 1.3 collective-permute-start.28
  97.2 2.8 %collective-permute-done.15.rest_4_ = bf16[8,128,128]{2,1,0:T(8,128)(2,1)S(1)} collective-permute-done((bf16[8,128,128]{2,1,0:T(8,128)(2,1)S(1)}, bf16[8,128,128]{2,1,0:T(8,128)(2,1)S(1)}, u32[]{:S(2)}, u32[]{:S(2)}) %collective-permute-start.15) | collective-permute-done | bytes 262176 | tf_op jit(solution)/shard_map/ppermute | solution.py:293
  100.0 1.3 collective-permute-start.16
  101.3 0.7 collective-permute-start.13
  102.0 4.3 %collective-permute-done.28.rest_5_ = bf16[8,128,128]{2,1,0:T(8,128)(2,1)S(1)} collective-permute-done((bf16[8,128,128]{2,1,0:T(8,128)(2,1)S(1)}, bf16[8,128,128]{2,1,0:T(8,128)(2,1)S(1)}, u32[]{:S(2)}, u32[]{:S(2)}) %collective-permute-start.28) | collective-permute-done | bytes 262176 | tf_op jit(solution)/shard_map/ppermute | solution.py:293
  106.3 1.3 collective-permute-start.29
  107.6 1.4 collective-permute-start.26
  109.0 3.3 %collective-permute-done.16.rest_5_ = bf16[8,128,128]{2,1,0:T(8,128)(2,1)S(1)} collective-permute-done((bf16[8,128,128]{2,1,0:T(8,128)(2,1)S(1)}, bf16[8,128,128]{2,1,0:T(8,128)(2,1)S(1)}, u32[]{:S(2)}, u32[]{:S(2)}) %collective-permute-start.16) | collective-permute-done | bytes 262176 | tf_op jit(solution)/shard_map/ppermute | solution.py:293
  112.2 1.3 collective-permute-start.17
  113.5 0.9 collective-permute-start.14
  114.5 2.2 %copy-done = bf16[16384,128]{1,0:T(8,128)(2,1)S(1)} copy-done((bf16[16384,128]{1,0:T(8,128)(2,1)S(1)}, bf16[16384,128]{1,0:T(8,128)(2,1)}, u32[]{:S(2)}) %copy-start) | copy-done | bytes 4194328
  116.6 6.1 %aggregate.1 = bf16[16,128,128]{2,1,0:T(8,128)(2,1)S(1)} custom-call(s32[16,20]{1,0:T(8,128)S(1)} %copy-done.9, bf16[16,20,128,128]{3,2,1,0:T(8,128)(2,1)} %tiles_ref.5, bf16[128,128,128]{2,1,0:T(8,128)(2,1)S(1)} %bitcast.52), custom_call_target="tpu_custom_call" | custom-call | flops 1342177280 | bytes 20000000 | tf_op jit(solution)/shard_map/aggregate/pallas_call | solution.py:141
  122.8 1.9 %dense.7 = (bf16[8,128,128]{2,1,0:T(8,128)(2,1)S(1)}, f32[512,128]{1,0:T(8,128)S(1)}) custom-call(s32[1]{0:T(128)} %bitcast.1.col_ref, bf16[128,512]{1,0:T(8,128)(2,1)S(1)} %copy-done.1, bf16[8,128,128]{2,1,0:T(8,128)(2,1)S(1)} %get-tuple-element.43.rest_0_, bf16[8,128,128]{2,1,0:T(8,128)(2,1)S(1)} %collective-permute-done.24.rest_1_, ...), custom_call_target="tpu_custom_call" | custom-call | tf_op jit(solution)/shard_map/dense/pallas_call | solution.py:219
  124.8 0.9 dense.5
  125.7 6.5 %spread.3 = (bf16[4,8,128,128]{3,2,1,0:T(8,128)(2,1)S(1)}, bf16[4,8,128,128]{3,2,1,0:T(8,128)(2,1)S(1)}, bf16[4,8,128,128]{3,2,1,0:T(8,128)(2,1)S(1)}, bf16[4,8,128,128]{3,2,1,0:T(8,128)(2,1)S(1)}) custom-call(s32[16,20]{1,0:T(8,128)S(1)} %copy-done.9, s32[1]{0:T(128)} %bitcast.me_ref, bf16[16,20,128,128]{3,2,1,0:T(8,128)(2,1)} %tiles_ref.5, ...), custom_call_target="tpu_custom_call" | custom-call | flops 1342177280 | bytes 30000000 | tf_op jit(solution)/shard_map/spread/pallas_call | solution.py:105
  132.8 2.1 %collective-permute-done.30 = bf16[4,8,128,128]{3,2,1,0:T(8,128)(2,1)S(1)} collective-permute-done((bf16[4,8,128,128]{3,2,1,0:T(8,128)(2,1)S(1)}, bf16[4,8,128,128]{3,2,1,0:T(8,128)(2,1)S(1)}, u32[]{:S(2)}, u32[]{:S(2)}) %collective-permute-start.30) | collective-permute-done | bytes 1048608 | tf_op jit(solution)/shard_map/ppermute | solution.py:255
  135.4 1.6 collective-permute-start.31
  137.4 1.6 collective-permute-start.35
  139.3 1.3 collective-permute-done.32
  140.6 8.8 %collective-permute-done.31 = bf16[2,8,128,128]{3,2,1,0:T(8,128)(2,1)S(1)} collective-permute-done((bf16[2,8,128,128]{3,2,1,0:T(8,128)(2,1)S(1)}, bf16[2,8,128,128]{3,2,1,0:T(8,128)(2,1)S(1)}, u32[]{:S(2)}, u32[]{:S(2)}) %collective-permute-start.31) | collective-permute-done | bytes 524320 | tf_op jit(solution)/shard_map/ppermute | solution.py:255
  149.4 1.7 collective-permute-done.35
  151.1 1.3 collective-permute-start.37
  152.6 1.6 collective-permute-start.33
  154.2 1.9 %collective-permute-done.37 = bf16[128,512]{1,0:T(8,128)(2,1)S(1)} collective-permute-done((bf16[128,512]{1,0:T(8,128)(2,1)S(1)}, bf16[128,512]{1,0:T(8,128)(2,1)S(1)}, u32[]{:S(2)}, u32[]{:S(2)}) %collective-permute-start.37) | collective-permute-done | bytes 131104 | tf_op jit(solution)/shard_map/ppermute | solution.py:255
  156.1 1.6 collective-permute-start.38
  157.9 1.4 collective-permute-start.36
  159.2 3.5 %collective-permute-done.38 = bf16[128,512]{1,0:T(8,128)(2,1)S(1)} collective-permute-done((bf16[128,512]{1,0:T(8,128)(2,1)S(1)}, bf16[128,512]{1,0:T(8,128)(2,1)S(1)}, u32[]{:S(2)}, u32[]{:S(2)}) %collective-permute-start.38) | collective-permute-done | bytes 131104 | tf_op jit(solution)/shard_map/ppermute | solution.py:255
  162.8 1.5 collective-permute-done.36.refs_3_
  164.3 1.0 finish.1
  165.3 0.9 broadcast_select_fusion
  (65 shorter events, 5.3 us)
Async XLA Ops:
  7.2 107.3 %all-gather.2.cloned.1.call-start = ((), (), s32[]{:S(2)}) async-start(), calls=%async_computation | async-start | bytes 4718592 | tf_op jit(solution)/shard_map/all_gather | solution.py:324
  7.2 1.0 copy-start.2
  8.3 0.7 copy-start.8
  9.0 69.4 %copy-start.3 = (bf16[128,512]{1,0:T(8,128)(2,1)S(1)}, bf16[128,512]{1,0:T(8,128)(2,1)}, u32[]{:S(2)}) copy-start(bf16[128,512]{1,0:T(8,128)(2,1)} %weight_ref.6) | copy-start | bytes 393220
  16.0 98.4 %copy-start.9 = (s32[16,20]{1,0:T(8,128)S(1)}, s32[16,20]{1,0:T(8,128)}, u32[]{:S(2)}) copy-start(s32[16,20]{1,0:T(8,128)} %cols_ref.5) | copy-start | bytes 3844
  16.0 2.8 %collective-permute-start = (bf16[4,8,128,128]{3,2,1,0:T(8,128)(2,1)S(1)}, bf16[4,8,128,128]{3,2,1,0:T(8,128)(2,1)S(1)}, u32[]{:S(2)}, u32[]{:S(2)}) collective-permute-start(bf16[4,8,128,128]{3,2,1,0:T(8,128)(2,1)S(1)} %get-tuple-element.32), channel_id=1, source_target_pairs={{0,4},{4,0},{8,12},{12,8},{16,20},{20,16},{24,28},{28,24},{1,5},{5... | collective-permute-start | bytes 3145736 | tf_op jit(solution)/shard_map/ppermute | solution.py:255
  16.5 5.6 %collective-permute-start.3 = (bf16[4,8,128,128]{3,2,1,0:T(8,128)(2,1)S(1)}, bf16[4,8,128,128]{3,2,1,0:T(8,128)(2,1)S(1)}, u32[]{:S(2)}, u32[]{:S(2)}) collective-permute-start(bf16[4,8,128,128]{3,2,1,0:T(8,128)(2,1)S(1)} %get-tuple-element.34), channel_id=1, source_target_pairs={{0,4},{4,0},{8,12},{12,8},{16,20},{20,16},{24,28},{28,24},{1,5},{5... | collective-permute-start | bytes 3145736 | tf_op jit(solution)/shard_map/ppermute | solution.py:255
  19.2 15.1 %collective-permute-start.1 = (bf16[2,8,128,128]{3,2,1,0:T(8,128)(2,1)S(1)}, bf16[2,8,128,128]{3,2,1,0:T(8,128)(2,1)S(1)}, u32[]{:S(2)}, u32[]{:S(2)}) collective-permute-start(bf16[2,8,128,128]{3,2,1,0:T(8,128)(2,1)S(1)} %get-tuple-element.66), channel_id=1, source_target_pairs={{0,8},{4,12},{8,0},{12,4},{16,24},{20,28},{24,16},{28,20},{1,9},{5... | collective-permute-start | bytes 1572872 | tf_op jit(solution)/shard_map/ppermute | solution.py:255
  22.6 13.8 %collective-permute-start.4 = (bf16[2,8,128,128]{3,2,1,0:T(8,128)(2,1)S(1)}, bf16[2,8,128,128]{3,2,1,0:T(8,128)(2,1)S(1)}, u32[]{:S(2)}, u32[]{:S(2)}) collective-permute-start(bf16[2,8,128,128]{3,2,1,0:T(8,128)(2,1)S(1)} %get-tuple-element.64), channel_id=1, source_target_pairs={{0,16},{4,20},{8,24},{12,28},{16,0},{20,4},{24,8},{28,12},{1,17},{... | collective-permute-start | bytes 1572872 | tf_op jit(solution)/shard_map/ppermute | solution.py:255
  34.5 7.9 %collective-permute-start.2 = (bf16[8,128,128]{2,1,0:T(8,128)(2,1)S(1)}, bf16[8,128,128]{2,1,0:T(8,128)(2,1)S(1)}, u32[]{:S(2)}, u32[]{:S(2)}) collective-permute-start(bf16[8,128,128]{2,1,0:T(8,128)(2,1)S(1)} %get-tuple-element.73), channel_id=1, source_target_pairs={{0,16},{4,20},{8,24},{12,28},{16,0},{20,4},{24,8},{28,12},{1,17},{... | collective-permute-start | bytes 786440 | tf_op jit(solution)/shard_map/ppermute | solution.py:255
  36.5 7.3 %collective-permute-start.5 = (bf16[8,128,128]{2,1,0:T(8,128)(2,1)S(1)}, bf16[8,128,128]{2,1,0:T(8,128)(2,1)S(1)}, u32[]{:S(2)}, u32[]{:S(2)}) collective-permute-start(bf16[8,128,128]{2,1,0:T(8,128)(2,1)S(1)} %get-tuple-element.71), channel_id=1, source_target_pairs={{0,8},{4,12},{8,0},{12,4},{16,24},{20,28},{24,16},{28,20},{1,9},{5... | collective-permute-start | bytes 786440 | tf_op jit(solution)/shard_map/ppermute | solution.py:255
  43.9 11.8 %collective-permute-start.21 = (bf16[8,128,128]{2,1,0:T(8,128)(2,1)S(1)}, bf16[8,128,128]{2,1,0:T(8,128)(2,1)S(1)}, u32[]{:S(2)}, u32[]{:S(2)}) collective-permute-start(bf16[8,128,128]{2,1,0:T(8,128)(2,1)S(1)} %last_sum.3.rest_0_), channel_id=1, source_target_pairs={{1,0},{2,1},{3,2},{5,4},{6,5},{7,6},{9,8},{10,9},{11,10},{13,12},{... | collective-permute-start | bytes 786440 | tf_op jit(solution)/shard_map/ppermute | solution.py:293
  45.2 11.8 %collective-permute-start.18 = (bf16[8,128,128]{2,1,0:T(8,128)(2,1)S(1)}, bf16[8,128,128]{2,1,0:T(8,128)(2,1)S(1)}, u32[]{:S(2)}, u32[]{:S(2)}) collective-permute-start(bf16[8,128,128]{2,1,0:T(8,128)(2,1)S(1)} %last_sum.3.rest_0_), channel_id=1, source_target_pairs={{0,1},{1,2},{2,3},{4,5},{5,6},{6,7},{8,9},{9,10},{10,11},{12,13},{... | collective-permute-start | bytes 786440 | tf_op jit(solution)/shard_map/ppermute | solution.py:292
  49.8 9.1 %collective-permute-start.9 = (bf16[8,128,128]{2,1,0:T(8,128)(2,1)S(1)}, bf16[8,128,128]{2,1,0:T(8,128)(2,1)S(1)}, u32[]{:S(2)}, u32[]{:S(2)}) collective-permute-start(bf16[8,128,128]{2,1,0:T(8,128)(2,1)S(1)} %last_sum.2.rest_0_), channel_id=1, source_target_pairs={{1,0},{2,1},{3,2},{5,4},{6,5},{7,6},{9,8},{10,9},{11,10},{13,12},{... | collective-permute-start | bytes 786440 | tf_op jit(solution)/shard_map/ppermute | solution.py:293
  51.1 9.1 %collective-permute-start.6 = (bf16[8,128,128]{2,1,0:T(8,128)(2,1)S(1)}, bf16[8,128,128]{2,1,0:T(8,128)(2,1)S(1)}, u32[]{:S(2)}, u32[]{:S(2)}) collective-permute-start(bf16[8,128,128]{2,1,0:T(8,128)(2,1)S(1)} %last_sum.2.rest_0_), channel_id=1, source_target_pairs={{0,1},{1,2},{2,3},{4,5},{5,6},{6,7},{8,9},{9,10},{10,11},{12,13},{... | collective-permute-start | bytes 786440 | tf_op jit(solution)/shard_map/ppermute | solution.py:292
  55.7 9.2 %collective-permute-start.22 = (bf16[8,128,128]{2,1,0:T(8,128)(2,1)S(1)}, bf16[8,128,128]{2,1,0:T(8,128)(2,1)S(1)}, u32[]{:S(2)}, u32[]{:S(2)}) collective-permute-start(bf16[8,128,128]{2,1,0:T(8,128)(2,1)S(1)} %collective-permute-done.21.rest_4_), channel_id=1, source_target_pairs={{1,0},{2,1},{5,4},{6,5},{9,8},{10,9},{13,12},{14,13},{17,16},{18,1... | collective-permute-start | bytes 786440 | tf_op jit(solution)/shard_map/ppermute | solution.py:293
  57.0 9.1 %collective-permute-start.19 = (bf16[8,128,128]{2,1,0:T(8,128)(2,1)S(1)}, bf16[8,128,128]{2,1,0:T(8,128)(2,1)}, u32[]{:S(2)}, u32[]{:S(2)}) collective-permute-start(bf16[8,128,128]{2,1,0:T(8,128)(2,1)S(1)} %collective-permute-done.18.rest_1_), channel_id=1, source_target_pairs={{1,2},{2,3},{5,6},{6,7},{9,10},{10,11},{13,14},{14,15},{17,18},{18... | collective-permute-start | bytes 786440 | tf_op jit(solution)/shard_map/ppermute | solution.py:292
  59.0 13.6 %collective-permute-start.10 = (bf16[8,128,128]{2,1,0:T(8,128)(2,1)S(1)}, bf16[8,128,128]{2,1,0:T(8,128)(2,1)S(1)}, u32[]{:S(2)}, u32[]{:S(2)}) collective-permute-start(bf16[8,128,128]{2,1,0:T(8,128)(2,1)S(1)} %collective-permute-done.9.rest_4_), channel_id=1, source_target_pairs={{1,0},{2,1},{5,4},{6,5},{9,8},{10,9},{13,12},{14,13},{17,16},{18,1... | collective-permute-start | bytes 786440 | tf_op jit(solution)/shard_map/ppermute | solution.py:293
  60.3 13.6 %collective-permute-start.7 = (bf16[8,128,128]{2,1,0:T(8,128)(2,1)S(1)}, bf16[8,128,128]{2,1,0:T(8,128)(2,1)S(1)}, u32[]{:S(2)}, u32[]{:S(2)}) collective-permute-start(bf16[8,128,128]{2,1,0:T(8,128)(2,1)S(1)} %collective-permute-done.6.rest_1_), channel_id=1, source_target_pairs={{1,2},{2,3},{5,6},{6,7},{9,10},{10,11},{13,14},{14,15},{17,18},{18... | collective-permute-start | bytes 786440 | tf_op jit(solution)/shard_map/ppermute | solution.py:292
  64.9 13.5 %collective-permute-start.23 = (bf16[8,128,128]{2,1,0:T(8,128)(2,1)S(1)}, bf16[8,128,128]{2,1,0:T(8,128)(2,1)}, u32[]{:S(2)}, u32[]{:S(2)}) collective-permute-start(bf16[8,128,128]{2,1,0:T(8,128)(2,1)S(1)} %collective-permute-done.22.rest_5_), channel_id=1, source_target_pairs={{1,0},{5,4},{9,8},{13,12},{17,16},{21,20},{25,24},{29,28}} | collective-permute-start | bytes 786440 | tf_op jit(solution)/shard_map/ppermute | solution.py:293
  66.2 12.2 %collective-permute-start.20 = (bf16[8,128,128]{2,1,0:T(8,128)(2,1)}, bf16[8,128,128]{2,1,0:T(8,128)(2,1)}, u32[]{:S(2)}, u32[]{:S(2)}) collective-permute-start(bf16[8,128,128]{2,1,0:T(8,128)(2,1)} %collective-permute-done.19.rest_2_), channel_id=1, source_target_pairs={{2,3},{6,7},{10,11},{14,15},{18,19},{22,23},{26,27},{30,31}} | collective-permute-start | bytes 786440 | tf_op jit(solution)/shard_map/ppermute | solution.py:292
  72.5 13.8 %collective-permute-start.11 = (bf16[8,128,128]{2,1,0:T(8,128)(2,1)S(1)}, bf16[8,128,128]{2,1,0:T(8,128)(2,1)}, u32[]{:S(2)}, u32[]{:S(2)}) collective-permute-start(bf16[8,128,128]{2,1,0:T(8,128)(2,1)S(1)} %collective-permute-done.10.rest_5_), channel_id=1, source_target_pairs={{1,0},{5,4},{9,8},{13,12},{17,16},{21,20},{25,24},{29,28}} | collective-permute-start | bytes 786440 | tf_op jit(solution)/shard_map/ppermute | solution.py:293
  73.8 12.5 %collective-permute-start.8 = (bf16[8,128,128]{2,1,0:T(8,128)(2,1)S(1)}, bf16[8,128,128]{2,1,0:T(8,128)(2,1)}, u32[]{:S(2)}, u32[]{:S(2)}) collective-permute-start(bf16[8,128,128]{2,1,0:T(8,128)(2,1)S(1)} %collective-permute-done.7.rest_2_), channel_id=1, source_target_pairs={{2,3},{6,7},{10,11},{14,15},{18,19},{22,23},{26,27},{30,31}} | collective-permute-start | bytes 786440 | tf_op jit(solution)/shard_map/ppermute | solution.py:292
  78.4 44.5 %copy-start.1 = (bf16[128,512]{1,0:T(8,128)(2,1)S(1)}, bf16[128,512]{1,0:T(8,128)(2,1)}, u32[]{:S(2)}) copy-start(bf16[128,512]{1,0:T(8,128)(2,1)} %weight_ref.7) | copy-start | bytes 393220
  80.4 33.1 %copy-start.4 = (f32[512,128]{1,0:T(8,128)}, f32[512,128]{1,0:T(8,128)S(1)}, u32[]{:S(2)}) copy-start(f32[512,128]{1,0:T(8,128)S(1)} %get-tuple-element.50.refs_3_) | copy-start | bytes 786436
  80.5 14.7 %collective-permute-start.27 = (bf16[8,128,128]{2,1,0:T(8,128)(2,1)S(1)}, bf16[8,128,128]{2,1,0:T(8,128)(2,1)S(1)}, u32[]{:S(2)}, u32[]{:S(2)}) collective-permute-start(bf16[8,128,128]{2,1,0:T(8,128)(2,1)S(1)} %get-tuple-element.43.rest_0_), channel_id=1, source_target_pairs={{1,0},{2,1},{3,2},{5,4},{6,5},{7,6},{9,8},{10,9},{11,10},{13,12},{... | collective-permute-start | bytes 786440 | tf_op jit(solution)/shard_map/ppermute | solution.py:293
  81.8 14.8 %collective-permute-start.24 = (bf16[8,128,128]{2,1,0:T(8,128)(2,1)S(1)}, bf16[8,128,128]{2,1,0:T(8,128)(2,1)S(1)}, u32[]{:S(2)}, u32[]{:S(2)}) collective-permute-start(bf16[8,128,128]{2,1,0:T(8,128)(2,1)S(1)} %get-tuple-element.43.rest_0_), channel_id=1, source_target_pairs={{0,1},{1,2},{2,3},{4,5},{5,6},{6,7},{8,9},{9,10},{10,11},{12,13},{... | collective-permute-start | bytes 786440 | tf_op jit(solution)/shard_map/ppermute | solution.py:292
  88.3 0.7 copy-start.6
  89.0 11.0 %collective-permute-start.15 = (bf16[8,128,128]{2,1,0:T(8,128)(2,1)S(1)}, bf16[8,128,128]{2,1,0:T(8,128)(2,1)S(1)}, u32[]{:S(2)}, u32[]{:S(2)}) collective-permute-start(bf16[8,128,128]{2,1,0:T(8,128)(2,1)S(1)} %get-tuple-element.38.rest_0_), channel_id=1, source_target_pairs={{1,0},{2,1},{3,2},{5,4},{6,5},{7,6},{9,8},{10,9},{11,10},{13,12},{... | collective-permute-start | bytes 786440 | tf_op jit(solution)/shard_map/ppermute | solution.py:293
  90.3 11.0 %collective-permute-start.12 = (bf16[8,128,128]{2,1,0:T(8,128)(2,1)S(1)}, bf16[8,128,128]{2,1,0:T(8,128)(2,1)S(1)}, u32[]{:S(2)}, u32[]{:S(2)}) collective-permute-start(bf16[8,128,128]{2,1,0:T(8,128)(2,1)S(1)} %get-tuple-element.38.rest_0_), channel_id=1, source_target_pairs={{0,1},{1,2},{2,3},{4,5},{5,6},{6,7},{8,9},{9,10},{10,11},{12,13},{... | collective-permute-start | bytes 786440 | tf_op jit(solution)/shard_map/ppermute | solution.py:292
  95.2 11.1 %collective-permute-start.28 = (bf16[8,128,128]{2,1,0:T(8,128)(2,1)S(1)}, bf16[8,128,128]{2,1,0:T(8,128)(2,1)S(1)}, u32[]{:S(2)}, u32[]{:S(2)}) collective-permute-start(bf16[8,128,128]{2,1,0:T(8,128)(2,1)S(1)} %collective-permute-done.27.rest_4_), channel_id=1, source_target_pairs={{1,0},{2,1},{5,4},{6,5},{9,8},{10,9},{13,12},{14,13},{17,16},{18,1... | collective-permute-start | bytes 786440 | tf_op jit(solution)/shard_map/ppermute | solution.py:293
  96.5 11.1 %collective-permute-start.25 = (bf16[8,128,128]{2,1,0:T(8,128)(2,1)S(1)}, bf16[8,128,128]{2,1,0:T(8,128)(2,1)S(1)}, u32[]{:S(2)}, u32[]{:S(2)}) collective-permute-start(bf16[8,128,128]{2,1,0:T(8,128)(2,1)S(1)} %collective-permute-done.24.rest_1_), channel_id=1, source_target_pairs={{1,2},{2,3},{5,6},{6,7},{9,10},{10,11},{13,14},{14,15},{17,18},{18... | collective-permute-start | bytes 786440 | tf_op jit(solution)/shard_map/ppermute | solution.py:292
  100.0 12.3 %collective-permute-start.16 = (bf16[8,128,128]{2,1,0:T(8,128)(2,1)S(1)}, bf16[8,128,128]{2,1,0:T(8,128)(2,1)S(1)}, u32[]{:S(2)}, u32[]{:S(2)}) collective-permute-start(bf16[8,128,128]{2,1,0:T(8,128)(2,1)S(1)} %collective-permute-done.15.rest_4_), channel_id=1, source_target_pairs={{1,0},{2,1},{5,4},{6,5},{9,8},{10,9},{13,12},{14,13},{17,16},{18,1... | collective-permute-start | bytes 786440 | tf_op jit(solution)/shard_map/ppermute | solution.py:293
  101.3 12.3 %collective-permute-start.13 = (bf16[8,128,128]{2,1,0:T(8,128)(2,1)S(1)}, bf16[8,128,128]{2,1,0:T(8,128)(2,1)S(1)}, u32[]{:S(2)}, u32[]{:S(2)}) collective-permute-start(bf16[8,128,128]{2,1,0:T(8,128)(2,1)S(1)} %collective-permute-done.12.rest_1_), channel_id=1, source_target_pairs={{1,2},{2,3},{5,6},{6,7},{9,10},{10,11},{13,14},{14,15},{17,18},{18... | collective-permute-start | bytes 786440 | tf_op jit(solution)/shard_map/ppermute | solution.py:292
  106.3 16.5 %collective-permute-start.29 = (bf16[8,128,128]{2,1,0:T(8,128)(2,1)S(1)}, bf16[8,128,128]{2,1,0:T(8,128)(2,1)S(1)}, u32[]{:S(2)}, u32[]{:S(2)}) collective-permute-start(bf16[8,128,128]{2,1,0:T(8,128)(2,1)S(1)} %collective-permute-done.28.rest_5_), channel_id=1, source_target_pairs={{1,0},{5,4},{9,8},{13,12},{17,16},{21,20},{25,24},{29,28}} | collective-permute-start | bytes 786440 | tf_op jit(solution)/shard_map/ppermute | solution.py:293
  107.6 15.2 %collective-permute-start.26 = (bf16[8,128,128]{2,1,0:T(8,128)(2,1)S(1)}, bf16[8,128,128]{2,1,0:T(8,128)(2,1)}, u32[]{:S(2)}, u32[]{:S(2)}) collective-permute-start(bf16[8,128,128]{2,1,0:T(8,128)(2,1)S(1)} %collective-permute-done.25.rest_2_), channel_id=1, source_target_pairs={{2,3},{6,7},{10,11},{14,15},{18,19},{22,23},{26,27},{30,31}} | collective-permute-start | bytes 786440 | tf_op jit(solution)/shard_map/ppermute | solution.py:292
  112.2 12.5 %collective-permute-start.17 = (bf16[8,128,128]{2,1,0:T(8,128)(2,1)S(1)}, bf16[8,128,128]{2,1,0:T(8,128)(2,1)S(1)}, u32[]{:S(2)}, u32[]{:S(2)}) collective-permute-start(bf16[8,128,128]{2,1,0:T(8,128)(2,1)S(1)} %collective-permute-done.16.rest_5_), channel_id=1, source_target_pairs={{1,0},{5,4},{9,8},{13,12},{17,16},{21,20},{25,24},{29,28}} | collective-permute-start | bytes 786440 | tf_op jit(solution)/shard_map/ppermute | solution.py:293
  113.5 11.2 %collective-permute-start.14 = (bf16[8,128,128]{2,1,0:T(8,128)(2,1)S(1)}, bf16[8,128,128]{2,1,0:T(8,128)(2,1)S(1)}, u32[]{:S(2)}, u32[]{:S(2)}) collective-permute-start(bf16[8,128,128]{2,1,0:T(8,128)(2,1)S(1)} %collective-permute-done.13.rest_2_), channel_id=1, source_target_pairs={{2,3},{6,7},{10,11},{14,15},{18,19},{22,23},{26,27},{30,31}} | collective-permute-start | bytes 786440 | tf_op jit(solution)/shard_map/ppermute | solution.py:292
  114.5 2.2 %copy-start = (bf16[16384,128]{1,0:T(8,128)(2,1)S(1)}, bf16[16384,128]{1,0:T(8,128)(2,1)}, u32[]{:S(2)}) copy-start(bf16[16384,128]{1,0:T(8,128)(2,1)} %all-gather.2.cloned.1.call-done) | copy-start | bytes 12582916
  122.8 16.1 %copy-start.5 = (f32[512,128]{1,0:T(8,128)S(1)}, f32[512,128]{1,0:T(8,128)}, u32[]{:S(2)}) copy-start(f32[512,128]{1,0:T(8,128)} %copy-done.4) | copy-start | bytes 786436
  122.8 16.1 %copy-start.7 = (f32[512,128]{1,0:T(8,128)S(1)}, f32[512,128]{1,0:T(8,128)}, u32[]{:S(2)}) copy-start(f32[512,128]{1,0:T(8,128)} %copy-done.6) | copy-start | bytes 786436
  132.3 2.7 %collective-permute-start.30 = (bf16[4,8,128,128]{3,2,1,0:T(8,128)(2,1)S(1)}, bf16[4,8,128,128]{3,2,1,0:T(8,128)(2,1)S(1)}, u32[]{:S(2)}, u32[]{:S(2)}) collective-permute-start(bf16[4,8,128,128]{3,2,1,0:T(8,128)(2,1)S(1)} %get-tuple-element.46), channel_id=1, source_target_pairs={{0,4},{4,0},{8,12},{12,8},{16,20},{20,16},{24,28},{28,24},{1,5},{5... | collective-permute-start | bytes 3145736 | tf_op jit(solution)/shard_map/ppermute | solution.py:255
  132.3 4.7 %collective-permute-start.34 = (bf16[4,8,128,128]{3,2,1,0:T(8,128)(2,1)S(1)}, bf16[4,8,128,128]{3,2,1,0:T(8,128)(2,1)S(1)}, u32[]{:S(2)}, u32[]{:S(2)}) collective-permute-start(bf16[4,8,128,128]{3,2,1,0:T(8,128)(2,1)S(1)} %get-tuple-element.55), channel_id=1, source_target_pairs={{0,4},{4,0},{8,12},{12,8},{16,20},{20,16},{24,28},{28,24},{1,5},{5... | collective-permute-start | bytes 3145736 | tf_op jit(solution)/shard_map/ppermute | solution.py:255
  135.4 14.0 %collective-permute-start.31 = (bf16[2,8,128,128]{3,2,1,0:T(8,128)(2,1)S(1)}, bf16[2,8,128,128]{3,2,1,0:T(8,128)(2,1)S(1)}, u32[]{:S(2)}, u32[]{:S(2)}) collective-permute-start(bf16[2,8,128,128]{3,2,1,0:T(8,128)(2,1)S(1)} %get-tuple-element.61), channel_id=1, source_target_pairs={{0,8},{4,12},{8,0},{12,4},{16,24},{20,28},{24,16},{28,20},{1,9},{5... | collective-permute-start | bytes 1572872 | tf_op jit(solution)/shard_map/ppermute | solution.py:255
  137.4 13.8 %collective-permute-start.35 = (bf16[2,8,128,128]{3,2,1,0:T(8,128)(2,1)S(1)}, bf16[2,8,128,128]{3,2,1,0:T(8,128)(2,1)S(1)}, u32[]{:S(2)}, u32[]{:S(2)}) collective-permute-start(bf16[2,8,128,128]{3,2,1,0:T(8,128)(2,1)S(1)} %get-tuple-element.59), channel_id=1, source_target_pairs={{0,16},{4,20},{8,24},{12,28},{16,0},{20,4},{24,8},{28,12},{1,17},{... | collective-permute-start | bytes 1572872 | tf_op jit(solution)/shard_map/ppermute | solution.py:255
  139.2 1.4 collective-permute-start.32
  151.1 5.0 %collective-permute-start.37 = (bf16[128,512]{1,0:T(8,128)(2,1)S(1)}, bf16[128,512]{1,0:T(8,128)(2,1)S(1)}, u32[]{:S(2)}, u32[]{:S(2)}) collective-permute-start(bf16[128,512]{1,0:T(8,128)(2,1)S(1)} %convert_add_fusion.5), channel_id=1, source_target_pairs={{0,8},{4,12},{8,0},{12,4},{16,24},{20,28},{24,16},{28,20},{1,9},{5... | collective-permute-start | bytes 393224 | tf_op jit(solution)/shard_map/ppermute | solution.py:255
  152.6 10.2 %collective-permute-start.33 = (bf16[8,128,128]{2,1,0:T(8,128)(2,1)S(1)}, bf16[8,128,128]{2,1,0:T(8,128)(2,1)S(1)}, u32[]{:S(2)}, u32[]{:S(2)}) collective-permute-start(bf16[8,128,128]{2,1,0:T(8,128)(2,1)S(1)} %get-tuple-element.69), channel_id=1, source_target_pairs={{0,16},{4,20},{8,24},{12,28},{16,0},{20,4},{24,8},{28,12},{1,17},{... | collective-permute-start | bytes 786440 | tf_op jit(solution)/shard_map/ppermute | solution.py:255
  156.1 6.6 %collective-permute-start.38 = (bf16[128,512]{1,0:T(8,128)(2,1)S(1)}, bf16[128,512]{1,0:T(8,128)(2,1)S(1)}, u32[]{:S(2)}, u32[]{:S(2)}) collective-permute-start(bf16[128,512]{1,0:T(8,128)(2,1)S(1)} %add_convert_fusion.12), channel_id=1, source_target_pairs={{0,16},{4,20},{8,24},{12,28},{16,0},{20,4},{24,8},{28,12},{1,17},{... | collective-permute-start | bytes 393224 | tf_op jit(solution)/shard_map/ppermute | solution.py:255
  157.9 6.4 %collective-permute-start.36 = (bf16[8,128,128]{2,1,0:T(8,128)(2,1)S(1)}, bf16[8,128,128]{2,1,0:T(8,128)(2,1)S(1)}, u32[]{:S(2)}, u32[]{:S(2)}) collective-permute-start(bf16[8,128,128]{2,1,0:T(8,128)(2,1)S(1)} %get-tuple-element.67), channel_id=1, source_target_pairs={{0,8},{4,12},{8,0},{12,4},{16,24},{20,28},{24,16},{28,20},{1,9},{5... | collective-permute-start | bytes 786440 | tf_op jit(solution)/shard_map/ppermute | solution.py:255
  162.7 2.6 %collective-permute-start.39 = (f32[128,512]{1,0:T(8,128)S(1)}, f32[128,512]{1,0:T(8,128)S(1)}, u32[]{:S(2)}, u32[]{:S(2)}) collective-permute-start(f32[128,512]{1,0:T(8,128)S(1)} %convert_add_fusion.4), channel_id=1, source_target_pairs={{0,4},{4,0},{8,12},{12,8},{16,20},{20,16},{24,28},{28,24},{1,5},{5... | collective-permute-start | bytes 786440 | tf_op jit(solution)/shard_map/ppermute | solution.py:255
Sparse Core Ops, SparseCore 0:
  44.0 38.0 all-gather.1

commit v6 on v5

--- a/solution.py
+++ b/solution.py
@@ -114,95 +114,126 @@
     )(block_cols, me, edge_tiles, *args)
 
 
-def aggregate_kernel(cols_ref, tiles_ref, values_ref, out_ref, held, table, sems):
-    load = pltpu.make_async_copy(values_ref, table, sems.at[COPIES])
-    load.start()
+def aggregate_kernel(start, cols_ref, tiles_ref, table_ref, out_ref, held, sems):
+    rows = tiles_ref.at[pl.ds(start, held.shape[0])]
     for i in range(COPIES):
-        tile_copy(tiles_ref, held, sems, i).start()
-    load.wait()
+        tile_copy(rows, held, sems, i).start()
     per_row = held.shape[1]
 
     def one_row(r):
         total = None
         for k in range(0, per_row, 2):
             pair = jnp.concatenate([held[r, k], held[r, k + 1]], axis=1)
-            picked = jnp.concatenate([table[cols_ref[r, k]], table[cols_ref[r, k + 1]]], axis=0)
+            left, right = cols_ref[start + r, k], cols_ref[start + r, k + 1]
+            picked = jnp.concatenate([table_ref[left], table_ref[right]], axis=0)
             term = jnp.dot(pair, picked, preferred_element_type=F32)
             total = term if total is None else total + term
         out_ref[r] = total.astype(BF16)
 
-    over_rows(tiles_ref, held, sems, one_row)
-
-
-def aggregate(edge_tiles, block_cols, values):
-    blocks, _, size, _ = edge_tiles.shape
-    feat = values.shape[2]
-    anywhere = pl.BlockSpec(memory_space=pl.ANY)
-    return pl.pallas_call(
-        aggregate_kernel,
-        out_shape=jax.ShapeDtypeStruct((blocks, size, feat), BF16),
-        in_specs=[SMEM, anywhere, anywhere],
+    over_rows(rows, held, sems, one_row)
+
+
+def aggregate(edge_tiles, block_cols, table, start, count):
+    _, per_row, size, _ = edge_tiles.shape
+    feat = table.shape[2]
+    return pl.pallas_call(
+        functools.partial(aggregate_kernel, start),
+        out_shape=jax.ShapeDtypeStruct((count, size, feat), BF16),
+        in_specs=[SMEM, pl.BlockSpec(memory_space=pl.ANY), VMEM],
         out_specs=VMEM,
         scratch_shapes=[
-            pltpu.VMEM(edge_tiles.shape, BF16),
-            pltpu.VMEM(values.shape, BF16),
-            pltpu.SemaphoreType.DMA((COPIES + 1,)),
+            pltpu.VMEM((count, per_row, size, size), BF16),
+            pltpu.SemaphoreType.DMA((COPIES,)),
         ],
         compiler_params=PARAMS,
-        cost_estimate=pl.CostEstimate(flops=2 * edge_tiles.size * feat, bytes_accessed=20_000_000, transcendentals=0),
+        cost_estimate=pl.CostEstimate(flops=2 * edge_tiles.size * feat, bytes_accessed=10_000_000, transcendentals=0),
         name="aggregate",
-    )(block_cols, edge_tiles, values)
-
-
-def sum_kernel(keep_ref, got_ref, out_ref):
-    out_ref[...] = (keep_ref[...].astype(F32) + got_ref[...].astype(F32)).astype(BF16)
-
-
-def last_sum(keep, got):
-    return pl.pallas_call(
-        sum_kernel,
-        out_shape=jax.ShapeDtypeStruct(keep.shape, BF16),
-        in_specs=[VMEM] * 2,
+    )(block_cols, edge_tiles, table)
+
+
+def chip_sum_kernel(groups, *refs):
+    ins, outs = refs[: 2 * groups], refs[2 * groups :]
+    count = ins[0].shape[1]
+    for g in range(groups):
+        keep_ref, got_ref = ins[2 * g : 2 * g + 2]
+        for rel, out in enumerate(outs):
+            out[g * count : (g + 1) * count] = (keep_ref[rel].astype(F32) + got_ref[rel].astype(F32)).astype(BF16)
+
+
+def chip_sum(*pairs):
+    chips, count, feat, size = pairs[0].shape
+    groups = len(pairs) // 2
+    return pl.pallas_call(
+        functools.partial(chip_sum_kernel, groups),
+        out_shape=[jax.ShapeDtypeStruct((groups * count, feat, size), BF16)] * chips,
+        in_specs=[VMEM] * len(pairs),
+        out_specs=[VMEM] * chips,
+        compiler_params=PARAMS,
+        name="chip_sum",
+    )(*pairs)
+
+
+def last_sum_kernel(*refs):
+    refs[-1][...] = sum(ref[...].astype(F32) for ref in refs[:-1]).astype(BF16)
+
+
+def last_sum(terms):
+    return pl.pallas_call(
+        last_sum_kernel,
+        out_shape=jax.ShapeDtypeStruct(terms[0].shape, BF16),
+        in_specs=[VMEM] * len(terms),
         out_specs=VMEM,
         compiler_params=PARAMS,
         name="last_sum",
-    )(keep, got)
+    )(*terms)
 
 
 def finish_kernel(*refs):
     parts, out_ref = refs[:-1], refs[-1]
-    count = parts[0].shape[0]
-    for g in range(GROUPS):
-        for b in range(count):
-            total = parts[2 * g][b].astype(F32) + parts[2 * g + 1][b].astype(F32)
-            out_ref[g * count + b] = total.T.astype(BF16)
+    for b in range(parts[0].shape[0]):
+        out_ref[b] = sum(part[b].astype(F32) for part in parts).T.astype(BF16)
 
 
 def finish(parts):
     count, feat, size = parts[0].shape
     return pl.pallas_call(
         finish_kernel,
-        out_shape=jax.ShapeDtypeStruct((count * GROUPS, size, feat), BF16),
+        out_shape=jax.ShapeDtypeStruct((count, size, feat), BF16),
         in_specs=[VMEM] * len(parts),
         out_specs=VMEM,
         compiler_params=PARAMS,
+        cost_estimate=pl.CostEstimate(flops=0, bytes_accessed=1_000_000_000, transcendentals=0),
         name="finish",
     )(*parts)
 
 
+def arrivals(shards, col, cols):
+    if cols == 4:
+        inner, low = (col == 1) | (col == 2), col < 2
+        return [
+            (col, None, shards[0], None),
+            (jnp.bitwise_xor(col, 1), None, shards[1], None),
+            (jnp.where(low, 2, 1), inner, shards[2], shards[3]),
+            (jnp.where(low, 3, 0), inner, shards[4], shards[5]),
+        ]
+    ups, downs = shards[1:cols], shards[cols:]
+    return [(col, None, shards[0], None)] + [
+        (lax.rem(col - s + cols, cols), col >= s, ups[s - 1], downs[cols - s - 1]) for s in range(1, cols)
+    ]
+
+
 def dense_kernel(cols, masked, col_ref, weight_ref, *rest):
-    shards, rest = rest[: 2 * cols - 1], rest[2 * cols - 1 :]
+    count = 6 if cols == 4 else 2 * cols - 1
+    shards, rest = rest[:count], rest[count:]
     side_ref, rest = rest[0], rest[1:]
     if masked:
         mask_ref, rest = rest[0], rest[1:]
     out_ref, grad_ref, whole_ref = rest
-    own, ups, downs = shards[0], shards[1:cols], shards[cols:]
     col = col_ref[0]
-    blocks, feat, size = own.shape
-    for s in range(cols):
-        place = lax.rem(col - s + cols, cols)
+    blocks, feat, size = shards[0].shape
+    for place, use, one, other in arrivals(shards, col, cols):
         for b in range(blocks):
-            part = own[b] if s == 0 else jnp.where(col >= s, ups[s - 1][b], downs[cols - s - 1][b])
+            part = one[b] if other is None else jnp.where(use, one[b], other[b])
             whole_ref[place, :, b * size : (b + 1) * size] = part
     whole = jnp.concatenate([whole_ref[q] for q in range(cols)], axis=0)
     res = jnp.dot(weight_ref[...], whole, preferred_element_type=F32)
@@ -255,37 +286,22 @@
     return lax.ppermute(value, axis, [(i, i ^ mask) for i in range(lax.axis_size(axis))])
 
 
-def add(a, b):
-    return (a.astype(F32) + b.astype(F32)).astype(BF16)
-
-
-def scatter_group(keep, got, masks, beside):
-    left = sorted(masks, reverse=True)
-    for mask in masks:
-        axis = left.index(mask)
-        part = lambda v, i: lax.index_in_dim(v, i, axis, keepdims=False)
-        sent = swap(add(part(keep, 1), part(got, 1)), mask, "row")
-        keep = add(part(keep, 0), part(got, 0))
-        got = sent
-        left.remove(mask)
-        if beside is not None and mask == masks[0]:
-            got, beside = lax.optimization_barrier((got, beside))
-    return [keep, got], beside
-
-
-def scatter(pieces, rows, beside=None):
-    masks = [1 << b for b in range(1, rows.bit_length() - 1)]
-    lead = (2,) * len(masks)
-    done = []
-    for g in range(GROUPS):
-        keep, got = pieces[2 * g], swap(pieces[2 * g + 1], 1, "row")
-        order = masks if g % 2 == 0 else masks[::-1]
-        terms, beside = scatter_group(keep.reshape(lead + keep.shape[1:]), got.reshape(lead + got.shape[1:]), order, beside)
-        done.append(terms)
-    return done, beside
-
-
-def chain_gather(own, cols):
+def from_chips(parts):
+    return [parts[0]] + [swap(part, 2 * i, "row") for i, part in enumerate(parts) if i > 0]
+
+
+def other_core(pieces):
+    return [v for g in range(GROUPS) for v in (pieces[2 * g], swap(pieces[2 * g + 1], 1, "row"))]
+
+
+def gather_columns(own, cols, beside):
+    if cols == 4:
+        middle, outward = [(1, 2), (2, 1)], [(1, 0), (2, 3)]
+        near = swap(own, 1, "col")
+        across = lax.ppermute(own, "col", middle)
+        near, across, beside = lax.optimization_barrier((near, across, beside))
+        far = lax.ppermute(near, "col", middle)
+        return [own, near, across, lax.ppermute(across, "col", outward), far, lax.ppermute(far, "col", outward)], beside
     ups, downs = [], []
     up, down = own, own
     for s in range(1, cols):
@@ -293,18 +309,16 @@
         down = lax.ppermute(down, "col", [(i, i - 1) for i in range(1, cols - s + 1)])
         ups.append(up)
         downs.append(down)
-    return [own, *ups, *downs]
-
-
-def reduced(value, me):
+    return [own, *ups, *downs], beside
+
+
+def over_chips(value, rows):
     mask = 2
-    while mask < lax.axis_size("row"):
+    while mask < rows:
         value = value.astype(BF16)
         value = value.astype(F32) + swap(value, mask, "row").astype(F32)
         mask *= 2
-    other = swap(value, 1, "row")
-    even = me % 2 == 0
-    return jnp.where(even, other, value), jnp.where(even, value, other)
+    return value
 
 
 def per_device(
@@ -319,27 +333,31 @@
     cut = lambda v, g: v[g * per : (g + 1) * per]
 
     *pieces, mask = spread(edge_tiles, block_cols, [blocked(grad_out)], me_at, rows, blocked(relu_mask))
-    terms, _ = scatter(pieces, rows)
-    terms, node_feats = lax.optimization_barrier((terms, node_feats))
-    table = blocked(lax.all_gather(node_feats, "row", axis=0, tiled=True))
+    pieces = other_core(pieces)
     deltas, seconds, inputs, firsts = [], [], [], []
     hidden = blocked(hidden_act)
     for g in range(GROUPS):
-        shards = chain_gather(last_sum(*terms[g]), cols)
+        own = last_sum(from_chips(chip_sum(*pieces[2 * g : 2 * g + 2])))
+        shards, node_feats = gather_columns(own, cols, node_feats)
         delta, grad = dense(weight_two, shards, cut(hidden, g), cut(mask, g), col_at, cols)
         deltas.append(delta)
         seconds.append(grad)
-    agg_feats = aggregate(edge_tiles, block_cols, table)
+    table = blocked(lax.all_gather(node_feats, "row", axis=0, tiled=True))
     for g in range(GROUPS):
-        shards = chain_gather(deltas[g], cols)
-        out, grad = dense(weight_one, shards, cut(agg_feats, g), None, col_at, cols)
+        agg_feats = aggregate(edge_tiles, block_cols, table, g * per, per)
+        shards, agg_feats = gather_columns(deltas[g], cols, agg_feats)
+        out, grad = dense(weight_one, shards, agg_feats, None, col_at, cols)
         inputs.append(out)
         firsts.append(grad)
     pieces = spread(edge_tiles, block_cols, inputs, me_at, rows)
+    terms = from_chips(chip_sum(*other_core(pieces)))
     keep, send = weight_terms(firsts, seconds, me_at)
-    terms, value = scatter(pieces, rows, keep + swap(send, 1, "row").astype(F32))
-    out = finish([t for pair in terms for t in pair])
-    first_grad, second_grad = reduced(value, me)
+    value = over_chips(keep + swap(send, 1, "row").astype(F32), rows)
+    terms, value = lax.optimization_barrier((terms, value))
+    out = finish(terms)
+    other = swap(value, 1, "row")
+    even = me % 2 == 0
+    first_grad, second_grad = jnp.where(even, other, value), jnp.where(even, value, other)
     return out.reshape(-1, out.shape[2]), first_grad, second_grad
 
 

time: 175 us -> 189 us (1.080)
  waiting for transfers between devices: 60.9 us -> 90.6 us
  starting transfers between devices: 60.7 us -> 45.7 us
  Pallas kernels: 27.9 us -> 30.1 us
  other arithmetic: 3.07 us -> 0.92 us
    ppermute x24 -> x16, starting transfers between devices: 42.4 us -> 16.2 us  [the longest x4 5.35 us: gather_columns(): lax.ppermute(far, 'col', outward)]
    ppermute x24 -> x16, waiting for transfers between devices: 21.9 us -> 44 us  [the longest x4 22.4 us: gather_columns(): lax.ppermute(across, 'col', outward)]
    ppermute x16 -> x21, starting transfers between devices: 18.3 us -> 29.5 us  [swap(): lax.ppermute(value, axis, [(i, i ^ mask) for i in range(lax.axis_size(axi...]
    ppermute x16 -> x21, waiting for transfers between devices: 39 us -> 46.6 us  [swap(): lax.ppermute(value, axis, [(i, i ^ mask) for i in range(lax.axis_size(axi...]
    pallas_call x4 -> x8, Pallas kernels: 7.23 us -> 11.6 us  [the longest x2 8.03 us: aggregate(): pl.pallas_call(functools.partial(aggregate_kernel, start), out_shape=jax....]
    pallas_call x4, Pallas kernels: 6.89 us -> 4.74 us  [dense(): pl.pallas_call(functools.partial(dense_kernel, cols, mask is not None), o...]
    convert_element_type x9 -> x2, other arithmetic: 2.15 us -> 0.06 us  [over_chips(): value = value.astype(BF16)]
    unnamed x20 -> x18, local copies, waits for them, and re-layouts: 4.64 us -> 5.66 us
  transfers between devices with their start and end apart: 41 -> 38, of which waited for: 18 -> 16; matrix products, arithmetic and copies ran while one was open for 2% -> 1% of each run, Pallas kernels for 8% -> 8%
where the time goes in v6:
time: 189 us
  waiting for transfers between devices  90.6 us (48%)
  starting transfers between devices  45.7 us (24%)
  Pallas kernels  30.1 us (16%)
  between operations  14.5 us (8%)
  local copies, waits for them, and re-layouts  6.8 us (4%)
    ppermute x21, waiting for transfers between devices, swap(): lax.ppermute(value, axis, [(i, i ^ mask) for i in range(lax.axis_size(axi...  46.6 us
    ppermute x21, starting transfers between devices, swap(): lax.ppermute(value, axis, [(i, i ^ mask) for i in range(lax.axis_size(axi...  29.5 us
    ppermute x4, waiting for transfers between devices, gather_columns(): lax.ppermute(across, 'col', outward)  22.4 us
    ppermute x4, waiting for transfers between devices, gather_columns(): lax.ppermute(far, 'col', outward)  21.6 us
    pallas_call x2, Pallas kernels, spread(): pl.pallas_call(functools.partial(spread_kernel, first), out_shape=outs, i...  13.6 us
    pallas_call x2, Pallas kernels, aggregate(): pl.pallas_call(functools.partial(aggregate_kernel, start), out_shape=jax....  8.03 us
    unnamed x18, local copies, waits for them, and re-layouts  5.66 us
    ppermute x4, starting transfers between devices, gather_columns(): lax.ppermute(far, 'col', outward)  5.35 us
  transfers between devices with their start and end apart: 38, of which 16 were waited for; matrix products, arithmetic and copies ran while one was open for 1% of the time, Pallas kernels for 8%

profile of v6, /device:TPU:0, one launch (start us, length us, event | category | flops | bytes accessed | tf_op | source)
XLA Modules:
  0.0 188.6 jit_solution(6784308411220789111)
XLA Ops:
  7.2 1.0 copy-done.3
  8.3 0.7 copy-done.6
  9.0 7.0 %spread.2 = (bf16[4,8,128,128]{3,2,1,0:T(8,128)(2,1)S(1)}, bf16[4,8,128,128]{3,2,1,0:T(8,128)(2,1)S(1)}, bf16[4,8,128,128]{3,2,1,0:T(8,128)(2,1)S(1)}, bf16[4,8,...) custom-call(s32[16,20]{1,0:T(8,128)S(1)} %copy-done.6, s32[1]{0:T(128)} %bitcast.me_ref, ...), custom_call_target="tpu_custom_call" | custom-call | flops 1342177280 | bytes 30000000 | tf_op jit(solution)/shard_map/spread/pallas_call | solution.py:105
  16.0 0.5 collective-permute-start
  16.6 2.2 %collective-permute-done.refs_1_ = bf16[4,8,128,128]{3,2,1,0:T(8,128)(2,1)S(1)} collective-permute-done((bf16[4,8,128,128]{3,2,1,0:T(8,128)(2,1)S(1)}, bf16[4,8,128,128]{3,2,1,0:T(8,128)(2,1)S(1)}, u32[]{:S(2)}, u32[]{:S(2)}) %collective-permute-start) | collective-permute-done | bytes 1048608 | tf_op jit(solution)/shard_map/ppermute | solution.py:286
  19.0 2.9 %collective-permute-start.1 = (bf16[8,128,128]{2,1,0:T(8,128)(2,1)S(1)}, bf16[8,128,128]{2,1,0:T(8,128)(2,1)S(1)}, u32[]{:S(2)}, u32[]{:S(2)}) collective-permute-start(bf16[8,128,128]{2,1,0:T(8,128)(2,1)S(1)} %get-tuple-element.54), channel_id=1, source_target_pairs={{0,8},{4,12},{8,0},{12,4},{16,24},{20,28},{24,16},{28,20},{1,9},{5... | collective-permute-start | bytes 786440 | tf_op jit(solution)/shard_map/ppermute | solution.py:286
  22.0 1.5 collective-permute-start.2
  23.8 2.0 %collective-permute-start.12 = (bf16[8,128,128]{2,1,0:T(8,128)(2,1)S(1)}, bf16[8,128,128]{2,1,0:T(8,128)(2,1)S(1)}, u32[]{:S(2)}, u32[]{:S(2)}) collective-permute-start(bf16[8,128,128]{2,1,0:T(8,128)(2,1)S(1)} %get-tuple-element.64), channel_id=1, source_target_pairs={{0,8},{4,12},{8,0},{12,4},{16,24},{20,28},{24,16},{28,20},{1,9},{5... | collective-permute-start | bytes 786440 | tf_op jit(solution)/shard_map/ppermute | solution.py:286
  25.8 1.5 collective-permute-start.13
  27.3 1.8 collective-permute-done.1.refs_1_
  29.1 3.0 %collective-permute-start.14 = (bf16[8,128,128]{2,1,0:T(8,128)(2,1)S(1)}, bf16[8,128,128]{2,1,0:T(8,128)(2,1)S(1)}, u32[]{:S(2)}, u32[]{:S(2)}) collective-permute-start(bf16[8,128,128]{2,1,0:T(8,128)(2,1)S(1)} %get-tuple-element.66), channel_id=1, source_target_pairs={{0,24},{4,28},{8,16},{12,20},{16,8},{20,12},{24,0},{28,4},{1,25},{... | collective-permute-start | bytes 786440 | tf_op jit(solution)/shard_map/ppermute | solution.py:286
  32.1 4.7 %collective-permute-done.2.refs_2_ = bf16[8,128,128]{2,1,0:T(8,128)(2,1)S(1)} collective-permute-done((bf16[8,128,128]{2,1,0:T(8,128)(2,1)S(1)}, bf16[8,128,128]{2,1,0:T(8,128)(2,1)S(1)}, u32[]{:S(2)}, u32[]{:S(2)}) %collective-permute-start.2) | collective-permute-done | bytes 262176 | tf_op jit(solution)/shard_map/ppermute | solution.py:286
  36.9 0.7 collective-permute-start.5
  37.6 4.4 %collective-permute-start.4 = (bf16[8,128,128]{2,1,0:T(8,128)(2,1)S(1)}, bf16[8,128,128]{2,1,0:T(8,128)(2,1)S(1)}, u32[]{:S(2)}, u32[]{:S(2)}) collective-permute-start(bf16[8,128,128]{2,1,0:T(8,128)(2,1)S(1)} %last_sum.2.rest_0_), channel_id=1, source_target_pairs={{0,1},{1,0},{2,3},{3,2},{4,5},{5,4},{6,7},{7,6},{8,9},{9,8},{10,11... | collective-permute-start | bytes 786440 | tf_op jit(solution)/shard_map/ppermute | solution.py:286
  42.1 4.8 %collective-permute-done.13.refs_2_ = bf16[8,128,128]{2,1,0:T(8,128)(2,1)S(1)} collective-permute-done((bf16[8,128,128]{2,1,0:T(8,128)(2,1)S(1)}, bf16[8,128,128]{2,1,0:T(8,128)(2,1)S(1)}, u32[]{:S(2)}, u32[]{:S(2)}) %collective-permute-start.13) | collective-permute-done | bytes 262176 | tf_op jit(solution)/shard_map/ppermute | solution.py:286
  47.0 0.7 collective-permute-start.16
  47.7 4.4 %collective-permute-start.15 = (bf16[8,128,128]{2,1,0:T(8,128)(2,1)S(1)}, bf16[8,128,128]{2,1,0:T(8,128)(2,1)S(1)}, u32[]{:S(2)}, u32[]{:S(2)}) collective-permute-start(bf16[8,128,128]{2,1,0:T(8,128)(2,1)S(1)} %last_sum.3.rest_0_), channel_id=1, source_target_pairs={{0,1},{1,0},{2,3},{3,2},{4,5},{5,4},{6,7},{7,6},{8,9},{9,8},{10,11... | collective-permute-start | bytes 786440 | tf_op jit(solution)/shard_map/ppermute | solution.py:286
  52.2 5.3 %collective-permute-done.15.rest_1_ = bf16[8,128,128]{2,1,0:T(8,128)(2,1)S(1)} collective-permute-done((bf16[8,128,128]{2,1,0:T(8,128)(2,1)S(1)}, bf16[8,128,128]{2,1,0:T(8,128)(2,1)S(1)}, u32[]{:S(2)}, u32[]{:S(2)}) %collective-permute-start.15) | collective-permute-done | bytes 262176 | tf_op jit(solution)/shard_map/ppermute | solution.py:286
  57.5 0.7 collective-permute-start.7
  58.2 0.7 collective-permute-start.21
  58.9 1.3 collective-permute-start.6
  60.2 1.3 collective-permute-start.8
  61.5 1.1 fusion.1
  62.6 1.3 collective-permute-start.20
  63.9 1.3 collective-permute-start.22
  65.3 8.3 %collective-permute-done.6.rest_3_ = bf16[8,128,128]{2,1,0:T(8,128)(2,1)S(1)} collective-permute-done((bf16[8,128,128]{2,1,0:T(8,128)(2,1)S(1)}, bf16[8,128,128]{2,1,0:T(8,128)(2,1)S(1)}, u32[]{:S(2)}, u32[]{:S(2)}) %collective-permute-start.6) | collective-permute-done | bytes 262176 | tf_op jit(solution)/shard_map/ppermute | solution.py:304
  73.6 5.7 %collective-permute-done.8.rest_5_ = bf16[8,128,128]{2,1,0:T(8,128)(2,1)} collective-permute-done((bf16[8,128,128]{2,1,0:T(8,128)(2,1)S(1)}, bf16[8,128,128]{2,1,0:T(8,128)(2,1)}, u32[]{:S(2)}, u32[]{:S(2)}) %collective-permute-start.8) | collective-permute-done | bytes 262176 | tf_op jit(solution)/shard_map/ppermute | solution.py:304
  79.3 1.9 %dense.4 = (bf16[8,128,128]{2,1,0:T(8,128)(2,1)S(1)}, f32[512,128]{1,0:T(8,128)S(1)}) custom-call(s32[1]{0:T(128)} %bitcast.1.col_ref, bf16[128,512]{1,0:T(8,128)(2,1)S(1)} %copy-done.1, bf16[8,128,128]{2,1,0:T(8,128)(2,1)S(1)} %last_sum.2.rest_0_, bf16[8,128,128]{2,1,0:T(8,128)(2,1)S(1)} %collective-permute-done.4.rest_1_, ...), custom_call_target="tpu_custom_call" | custom-call | tf_op jit(solution)/shard_map/dense/pallas_call | solution.py:250
  81.3 0.7 copy-done.4
  82.0 0.7 collective-permute-start.10
  82.6 1.2 collective-permute-start.9
  83.8 1.0 collective-permute-done.20.rest_3_
  84.9 5.6 %collective-permute-done.22.rest_5_ = bf16[8,128,128]{2,1,0:T(8,128)(2,1)S(1)} collective-permute-done((bf16[8,128,128]{2,1,0:T(8,128)(2,1)S(1)}, bf16[8,128,128]{2,1,0:T(8,128)(2,1)S(1)}, u32[]{:S(2)}, u32[]{:S(2)}) %collective-permute-start.22) | collective-permute-done | bytes 262176 | tf_op jit(solution)/shard_map/ppermute | solution.py:304
  90.5 0.9 dense.6
  91.4 0.7 collective-permute-start.24
  92.1 1.3 collective-permute-start.23
  93.4 2.2 %copy-done = bf16[16384,128]{1,0:T(8,128)(2,1)S(1)} copy-done((bf16[16384,128]{1,0:T(8,128)(2,1)S(1)}, bf16[16384,128]{1,0:T(8,128)(2,1)}, u32[]{:S(2)}) %copy-start) | copy-done | bytes 4194328
  95.6 4.0 %aggregate.2.rest_6_ = bf16[8,128,128]{2,1,0:T(8,128)(2,1)S(1)} custom-call(s32[16,20]{1,0:T(8,128)S(1)} %copy-done.7, bf16[16,20,128,128]{3,2,1,0:T(8,128)(2,1)} %tiles_ref.7, bf16[128,128,128]{2,1,0:T(8,128)(2,1)S(1)} %bitcast.8), custom_call_target="tpu_custom_call" | custom-call | flops 1342177280 | bytes 10000000 | tf_op jit(solution)/shard_map/aggregate/pallas_call | solution.py:139
  99.6 0.8 collective-permute-start.18
  100.5 4.0 %aggregate.3.rest_6_ = bf16[8,128,128]{2,1,0:T(8,128)(2,1)S(1)} custom-call(s32[16,20]{1,0:T(8,128)S(1)} %copy-done.7, bf16[16,20,128,128]{3,2,1,0:T(8,128)(2,1)} %tiles_ref.7, bf16[128,128,128]{2,1,0:T(8,128)(2,1)S(1)} %bitcast.9), custom_call_target="tpu_custom_call" | custom-call | flops 1342177280 | bytes 10000000 | tf_op jit(solution)/shard_map/aggregate/pallas_call | solution.py:139
  104.5 0.8 collective-permute-start.26
  105.3 1.3 collective-permute-start.17
  106.6 1.3 collective-permute-start.19
  107.9 1.3 collective-permute-start.25
  109.3 1.5 collective-permute-start.27
  110.7 8.4 %collective-permute-done.17.rest_3_ = bf16[8,128,128]{2,1,0:T(8,128)(2,1)S(1)} collective-permute-done((bf16[8,128,128]{2,1,0:T(8,128)(2,1)S(1)}, bf16[8,128,128]{2,1,0:T(8,128)(2,1)S(1)}, u32[]{:S(2)}, u32[]{:S(2)}) %collective-permute-start.17) | collective-permute-done | bytes 262176 | tf_op jit(solution)/shard_map/ppermute | solution.py:304
  119.1 5.6 %collective-permute-done.19.rest_5_ = bf16[8,128,128]{2,1,0:T(8,128)(2,1)S(1)} collective-permute-done((bf16[8,128,128]{2,1,0:T(8,128)(2,1)S(1)}, bf16[8,128,128]{2,1,0:T(8,128)(2,1)S(1)}, u32[]{:S(2)}, u32[]{:S(2)}) %collective-permute-start.19) | collective-permute-done | bytes 262176 | tf_op jit(solution)/shard_map/ppermute | solution.py:304
  124.7 0.9 dense.5
  125.7 4.7 %collective-permute-done.25.rest_3_ = bf16[8,128,128]{2,1,0:T(8,128)(2,1)S(1)} collective-permute-done((bf16[8,128,128]{2,1,0:T(8,128)(2,1)S(1)}, bf16[8,128,128]{2,1,0:T(8,128)(2,1)S(1)}, u32[]{:S(2)}, u32[]{:S(2)}) %collective-permute-start.25) | collective-permute-done | bytes 262176 | tf_op jit(solution)/shard_map/ppermute | solution.py:304
  130.4 4.6 %collective-permute-done.27.rest_5_ = bf16[8,128,128]{2,1,0:T(8,128)(2,1)S(1)} collective-permute-done((bf16[8,128,128]{2,1,0:T(8,128)(2,1)S(1)}, bf16[8,128,128]{2,1,0:T(8,128)(2,1)S(1)}, u32[]{:S(2)}, u32[]{:S(2)}) %collective-permute-start.27) | collective-permute-done | bytes 262176 | tf_op jit(solution)/shard_map/ppermute | solution.py:304
  135.0 0.9 dense.7
  135.9 6.5 %spread.3 = (bf16[4,8,128,128]{3,2,1,0:T(8,128)(2,1)S(1)}, bf16[4,8,128,128]{3,2,1,0:T(8,128)(2,1)S(1)}, bf16[4,8,128,128]{3,2,1,0:T(8,128)(2,1)S(1)}, bf16[4,8,128,128]{3,2,1,0:T(8,128)(2,1)S(1)}) custom-call(s32[16,20]{1,0:T(8,128)S(1)} %copy-done.7, s32[1]{0:T(128)} %bitcast.me_ref, bf16[16,20,128,128]{3,2,1,0:T(8,128)(2,1)} %tiles_ref.7, ...), custom_call_target="tpu_custom_call" | custom-call | flops 1342177280 | bytes 30000000 | tf_op jit(solution)/shard_map/spread/pallas_call | solution.py:105
  142.6 0.5 collective-permute-start.29
  143.4 3.5 %collective-permute-done.33 = bf16[128,512]{1,0:T(8,128)(2,1)S(1)} collective-permute-done((bf16[128,512]{1,0:T(8,128)(2,1)S(1)}, bf16[128,512]{1,0:T(8,128)(2,1)S(1)}, u32[]{:S(2)}, u32[]{:S(2)}) %collective-permute-start.33) | collective-permute-done | bytes 131104 | tf_op jit(solution)/shard_map/ppermute | solution.py:286
  146.9 1.5 collective-permute-start.34
  148.5 1.0 copy-done.8
  149.5 1.7 chip_sum.5
  151.2 0.6 collective-permute-start.30
  151.8 1.3 collective-permute-start.31
  153.1 1.6 collective-permute-start.32
  154.8 0.6 collective-permute-start.35
  155.4 23.9 %collective-permute-done.35 = bf16[128,512]{1,0:T(8,128)(2,1)S(1)} collective-permute-done((bf16[128,512]{1,0:T(8,128)(2,1)S(1)}, bf16[128,512]{1,0:T(8,128)(2,1)S(1)}, u32[]{:S(2)}, u32[]{:S(2)}) %collective-permute-start.35) | collective-permute-done | bytes 131104 | tf_op jit(solution)/shard_map/ppermute | solution.py:286
  179.4 1.1 finish.1
  180.9 0.8 broadcast_select_fusion
  (52 shorter events, 2.0 us)
Async XLA Ops:
  7.2 86.2 %all-gather.2.cloned.1.call-start = ((), (), s32[]{:S(2)}) async-start(), calls=%async_computation | async-start | bytes 4718592 | tf_op jit(solution)/shard_map/all_gather | solution.py:345
  7.2 1.0 copy-start.3
  8.3 0.7 copy-start.6
  9.0 70.4 %copy-start.1 = (bf16[128,512]{1,0:T(8,128)(2,1)S(1)}, bf16[128,512]{1,0:T(8,128)(2,1)}, u32[]{:S(2)}) copy-start(bf16[128,512]{1,0:T(8,128)(2,1)} %weight_ref.6) | copy-start | bytes 393220
  9.0 84.4 %copy-start.7 = (s32[16,20]{1,0:T(8,128)S(1)}, s32[16,20]{1,0:T(8,128)}, u32[]{:S(2)}) copy-start(s32[16,20]{1,0:T(8,128)} %cols_ref.7) | copy-start | bytes 3844
  16.0 2.8 %collective-permute-start = (bf16[4,8,128,128]{3,2,1,0:T(8,128)(2,1)S(1)}, bf16[4,8,128,128]{3,2,1,0:T(8,128)(2,1)S(1)}, u32[]{:S(2)}, u32[]{:S(2)}) collective-permute-start(bf16[4,8,128,128]{3,2,1,0:T(8,128)(2,1)S(1)} %get-tuple-element.52), channel_id=1, source_target_pairs={{0,4},{4,0},{8,12},{12,8},{16,20},{20,16},{24,28},{28,24},{1,5},{5... | collective-permute-start | bytes 3145736 | tf_op jit(solution)/shard_map/ppermute | solution.py:286
  16.5 7.0 %collective-permute-start.11 = (bf16[4,8,128,128]{3,2,1,0:T(8,128)(2,1)S(1)}, bf16[4,8,128,128]{3,2,1,0:T(8,128)(2,1)S(1)}, u32[]{:S(2)}, u32[]{:S(2)}) collective-permute-start(bf16[4,8,128,128]{3,2,1,0:T(8,128)(2,1)S(1)} %get-tuple-element.62), channel_id=1, source_target_pairs={{0,4},{4,0},{8,12},{12,8},{16,20},{20,16},{24,28},{28,24},{1,5},{5... | collective-permute-start | bytes 3145736 | tf_op jit(solution)/shard_map/ppermute | solution.py:286
  19.0 10.0 %collective-permute-start.1 = (bf16[8,128,128]{2,1,0:T(8,128)(2,1)S(1)}, bf16[8,128,128]{2,1,0:T(8,128)(2,1)S(1)}, u32[]{:S(2)}, u32[]{:S(2)}) collective-permute-start(bf16[8,128,128]{2,1,0:T(8,128)(2,1)S(1)} %get-tuple-element.54), channel_id=1, source_target_pairs={{0,8},{4,12},{8,0},{12,4},{16,24},{20,28},{24,16},{28,20},{1,9},{5... | collective-permute-start | bytes 786440 | tf_op jit(solution)/shard_map/ppermute | solution.py:286
  22.0 14.8 %collective-permute-start.2 = (bf16[8,128,128]{2,1,0:T(8,128)(2,1)S(1)}, bf16[8,128,128]{2,1,0:T(8,128)(2,1)S(1)}, u32[]{:S(2)}, u32[]{:S(2)}) collective-permute-start(bf16[8,128,128]{2,1,0:T(8,128)(2,1)S(1)} %get-tuple-element.55), channel_id=1, source_target_pairs={{0,16},{4,20},{8,24},{12,28},{16,0},{20,4},{24,8},{28,12},{1,17},{... | collective-permute-start | bytes 786440 | tf_op jit(solution)/shard_map/ppermute | solution.py:286
  23.5 13.3 %collective-permute-start.3 = (bf16[8,128,128]{2,1,0:T(8,128)(2,1)S(1)}, bf16[8,128,128]{2,1,0:T(8,128)(2,1)S(1)}, u32[]{:S(2)}, u32[]{:S(2)}) collective-permute-start(bf16[8,128,128]{2,1,0:T(8,128)(2,1)S(1)} %get-tuple-element.56), channel_id=1, source_target_pairs={{0,24},{4,28},{8,16},{12,20},{16,8},{20,12},{24,0},{28,4},{1,25},{... | collective-permute-start | bytes 786440 | tf_op jit(solution)/shard_map/ppermute | solution.py:286
  23.8 18.3 %collective-permute-start.12 = (bf16[8,128,128]{2,1,0:T(8,128)(2,1)S(1)}, bf16[8,128,128]{2,1,0:T(8,128)(2,1)S(1)}, u32[]{:S(2)}, u32[]{:S(2)}) collective-permute-start(bf16[8,128,128]{2,1,0:T(8,128)(2,1)S(1)} %get-tuple-element.64), channel_id=1, source_target_pairs={{0,8},{4,12},{8,0},{12,4},{16,24},{20,28},{24,16},{28,20},{1,9},{5... | collective-permute-start | bytes 786440 | tf_op jit(solution)/shard_map/ppermute | solution.py:286
  25.8 21.1 %collective-permute-start.13 = (bf16[8,128,128]{2,1,0:T(8,128)(2,1)S(1)}, bf16[8,128,128]{2,1,0:T(8,128)(2,1)S(1)}, u32[]{:S(2)}, u32[]{:S(2)}) collective-permute-start(bf16[8,128,128]{2,1,0:T(8,128)(2,1)S(1)} %get-tuple-element.65), channel_id=1, source_target_pairs={{0,16},{4,20},{8,24},{12,28},{16,0},{20,4},{24,8},{28,12},{1,17},{... | collective-permute-start | bytes 786440 | tf_op jit(solution)/shard_map/ppermute | solution.py:286
  29.1 17.8 %collective-permute-start.14 = (bf16[8,128,128]{2,1,0:T(8,128)(2,1)S(1)}, bf16[8,128,128]{2,1,0:T(8,128)(2,1)S(1)}, u32[]{:S(2)}, u32[]{:S(2)}) collective-permute-start(bf16[8,128,128]{2,1,0:T(8,128)(2,1)S(1)} %get-tuple-element.66), channel_id=1, source_target_pairs={{0,24},{4,28},{8,16},{12,20},{16,8},{20,12},{24,0},{28,4},{1,25},{... | collective-permute-start | bytes 786440 | tf_op jit(solution)/shard_map/ppermute | solution.py:286
  36.9 15.2 %collective-permute-start.5 = (bf16[8,128,128]{2,1,0:T(8,128)(2,1)S(1)}, bf16[8,128,128]{2,1,0:T(8,128)(2,1)S(1)}, u32[]{:S(2)}, u32[]{:S(2)}) collective-permute-start(bf16[8,128,128]{2,1,0:T(8,128)(2,1)S(1)} %last_sum.2.rest_0_), channel_id=1, source_target_pairs={{1,2},{2,1},{5,6},{6,5},{9,10},{10,9},{13,14},{14,13},{17,18},{18,... | collective-permute-start | bytes 786440 | tf_op jit(solution)/shard_map/ppermute | solution.py:301
  37.6 14.6 %collective-permute-start.4 = (bf16[8,128,128]{2,1,0:T(8,128)(2,1)S(1)}, bf16[8,128,128]{2,1,0:T(8,128)(2,1)S(1)}, u32[]{:S(2)}, u32[]{:S(2)}) collective-permute-start(bf16[8,128,128]{2,1,0:T(8,128)(2,1)S(1)} %last_sum.2.rest_0_), channel_id=1, source_target_pairs={{0,1},{1,0},{2,3},{3,2},{4,5},{5,4},{6,7},{7,6},{8,9},{9,8},{10,11... | collective-permute-start | bytes 786440 | tf_op jit(solution)/shard_map/ppermute | solution.py:286
  47.0 5.1 %collective-permute-start.16 = (bf16[8,128,128]{2,1,0:T(8,128)(2,1)S(1)}, bf16[8,128,128]{2,1,0:T(8,128)(2,1)S(1)}, u32[]{:S(2)}, u32[]{:S(2)}) collective-permute-start(bf16[8,128,128]{2,1,0:T(8,128)(2,1)S(1)} %last_sum.3.rest_0_), channel_id=1, source_target_pairs={{1,2},{2,1},{5,6},{6,5},{9,10},{10,9},{13,14},{14,13},{17,18},{18,... | collective-permute-start | bytes 786440 | tf_op jit(solution)/shard_map/ppermute | solution.py:301
  47.7 9.8 %collective-permute-start.15 = (bf16[8,128,128]{2,1,0:T(8,128)(2,1)S(1)}, bf16[8,128,128]{2,1,0:T(8,128)(2,1)S(1)}, u32[]{:S(2)}, u32[]{:S(2)}) collective-permute-start(bf16[8,128,128]{2,1,0:T(8,128)(2,1)S(1)} %last_sum.3.rest_0_), channel_id=1, source_target_pairs={{0,1},{1,0},{2,3},{3,2},{4,5},{5,4},{6,7},{7,6},{8,9},{9,8},{10,11... | collective-permute-start | bytes 786440 | tf_op jit(solution)/shard_map/ppermute | solution.py:286
  57.5 2.7 %collective-permute-start.7 = (bf16[8,128,128]{2,1,0:T(8,128)(2,1)S(1)}, bf16[8,128,128]{2,1,0:T(8,128)(2,1)S(1)}, u32[]{:S(2)}, u32[]{:S(2)}) collective-permute-start(bf16[8,128,128]{2,1,0:T(8,128)(2,1)S(1)} %collective-permute-done.4.rest_1_), channel_id=1, source_target_pairs={{1,2},{2,1},{5,6},{6,5},{9,10},{10,9},{13,14},{14,13},{17,18},{18,... | collective-permute-start | bytes 786440 | tf_op jit(solution)/shard_map/ppermute | solution.py:303
  58.2 5.7 %collective-permute-start.21 = (bf16[8,128,128]{2,1,0:T(8,128)(2,1)S(1)}, bf16[8,128,128]{2,1,0:T(8,128)(2,1)S(1)}, u32[]{:S(2)}, u32[]{:S(2)}) collective-permute-start(bf16[8,128,128]{2,1,0:T(8,128)(2,1)S(1)} %collective-permute-done.15.rest_1_), channel_id=1, source_target_pairs={{1,2},{2,1},{5,6},{6,5},{9,10},{10,9},{13,14},{14,13},{17,18},{18,... | collective-permute-start | bytes 786440 | tf_op jit(solution)/shard_map/ppermute | solution.py:303
  58.9 14.7 %collective-permute-start.6 = (bf16[8,128,128]{2,1,0:T(8,128)(2,1)S(1)}, bf16[8,128,128]{2,1,0:T(8,128)(2,1)S(1)}, u32[]{:S(2)}, u32[]{:S(2)}) collective-permute-start(bf16[8,128,128]{2,1,0:T(8,128)(2,1)S(1)} %collective-permute-done.5.rest_2_), channel_id=1, source_target_pairs={{1,0},{2,3},{5,4},{6,7},{9,8},{10,11},{13,12},{14,15},{17,16},{18,... | collective-permute-start | bytes 786440 | tf_op jit(solution)/shard_map/ppermute | solution.py:304
  60.2 19.1 %collective-permute-start.8 = (bf16[8,128,128]{2,1,0:T(8,128)(2,1)S(1)}, bf16[8,128,128]{2,1,0:T(8,128)(2,1)}, u32[]{:S(2)}, u32[]{:S(2)}) collective-permute-start(bf16[8,128,128]{2,1,0:T(8,128)(2,1)S(1)} %collective-permute-done.7.rest_4_), channel_id=1, source_target_pairs={{1,0},{2,3},{5,4},{6,7},{9,8},{10,11},{13,12},{14,15},{17,16},{18,... | collective-permute-start | bytes 786440 | tf_op jit(solution)/shard_map/ppermute | solution.py:304
  62.6 22.2 %collective-permute-start.20 = (bf16[8,128,128]{2,1,0:T(8,128)(2,1)S(1)}, bf16[8,128,128]{2,1,0:T(8,128)(2,1)S(1)}, u32[]{:S(2)}, u32[]{:S(2)}) collective-permute-start(bf16[8,128,128]{2,1,0:T(8,128)(2,1)S(1)} %collective-permute-done.16.rest_2_), channel_id=1, source_target_pairs={{1,0},{2,3},{5,4},{6,7},{9,8},{10,11},{13,12},{14,15},{17,16},{18,... | collective-permute-start | bytes 786440 | tf_op jit(solution)/shard_map/ppermute | solution.py:304
  63.9 26.5 %collective-permute-start.22 = (bf16[8,128,128]{2,1,0:T(8,128)(2,1)S(1)}, bf16[8,128,128]{2,1,0:T(8,128)(2,1)S(1)}, u32[]{:S(2)}, u32[]{:S(2)}) collective-permute-start(bf16[8,128,128]{2,1,0:T(8,128)(2,1)S(1)} %collective-permute-done.21.rest_4_), channel_id=1, source_target_pairs={{1,0},{2,3},{5,4},{6,7},{9,8},{10,11},{13,12},{14,15},{17,16},{18,... | collective-permute-start | bytes 786440 | tf_op jit(solution)/shard_map/ppermute | solution.py:304
  81.3 0.7 copy-start.4
  82.0 17.7 %collective-permute-start.10 = (bf16[8,128,128]{2,1,0:T(8,128)(2,1)S(1)}, bf16[8,128,128]{2,1,0:T(8,128)(2,1)S(1)}, u32[]{:S(2)}, u32[]{:S(2)}) collective-permute-start(bf16[8,128,128]{2,1,0:T(8,128)(2,1)S(1)} %get-tuple-element.60.rest_0_), channel_id=1, source_target_pairs={{1,2},{2,1},{5,6},{6,5},{9,10},{10,9},{13,14},{14,13},{17,18},{18,... | collective-permute-start | bytes 786440 | tf_op jit(solution)/shard_map/ppermute | solution.py:301
  82.6 17.0 %collective-permute-start.9 = (bf16[8,128,128]{2,1,0:T(8,128)(2,1)S(1)}, bf16[8,128,128]{2,1,0:T(8,128)(2,1)S(1)}, u32[]{:S(2)}, u32[]{:S(2)}) collective-permute-start(bf16[8,128,128]{2,1,0:T(8,128)(2,1)S(1)} %get-tuple-element.60.rest_0_), channel_id=1, source_target_pairs={{0,1},{1,0},{2,3},{3,2},{4,5},{5,4},{6,7},{7,6},{8,9},{9,8},{10,11... | collective-permute-start | bytes 786440 | tf_op jit(solution)/shard_map/ppermute | solution.py:286
  91.4 13.1 %collective-permute-start.24 = (bf16[8,128,128]{2,1,0:T(8,128)(2,1)S(1)}, bf16[8,128,128]{2,1,0:T(8,128)(2,1)S(1)}, u32[]{:S(2)}, u32[]{:S(2)}) collective-permute-start(bf16[8,128,128]{2,1,0:T(8,128)(2,1)S(1)} %get-tuple-element.75.rest_0_), channel_id=1, source_target_pairs={{1,2},{2,1},{5,6},{6,5},{9,10},{10,9},{13,14},{14,13},{17,18},{18,... | collective-permute-start | bytes 786440 | tf_op jit(solution)/shard_map/ppermute | solution.py:301
  92.1 12.4 %collective-permute-start.23 = (bf16[8,128,128]{2,1,0:T(8,128)(2,1)S(1)}, bf16[8,128,128]{2,1,0:T(8,128)(2,1)S(1)}, u32[]{:S(2)}, u32[]{:S(2)}) collective-permute-start(bf16[8,128,128]{2,1,0:T(8,128)(2,1)S(1)} %get-tuple-element.75.rest_0_), channel_id=1, source_target_pairs={{0,1},{1,0},{2,3},{3,2},{4,5},{5,4},{6,7},{7,6},{8,9},{9,8},{10,11... | collective-permute-start | bytes 786440 | tf_op jit(solution)/shard_map/ppermute | solution.py:286
  93.4 2.2 %copy-start = (bf16[16384,128]{1,0:T(8,128)(2,1)S(1)}, bf16[16384,128]{1,0:T(8,128)(2,1)}, u32[]{:S(2)}) copy-start(bf16[16384,128]{1,0:T(8,128)(2,1)} %all-gather.2.cloned.1.call-done) | copy-start | bytes 12582916
  99.6 25.1 %copy-start.2 = (bf16[128,512]{1,0:T(8,128)(2,1)S(1)}, bf16[128,512]{1,0:T(8,128)(2,1)}, u32[]{:S(2)}) copy-start(bf16[128,512]{1,0:T(8,128)(2,1)} %weight_ref.7) | copy-start | bytes 393220
  99.6 7.0 %collective-permute-start.18 = (bf16[8,128,128]{2,1,0:T(8,128)(2,1)S(1)}, bf16[8,128,128]{2,1,0:T(8,128)(2,1)S(1)}, u32[]{:S(2)}, u32[]{:S(2)}) collective-permute-start(bf16[8,128,128]{2,1,0:T(8,128)(2,1)S(1)} %collective-permute-done.9.rest_1_), channel_id=1, source_target_pairs={{1,2},{2,1},{5,6},{6,5},{9,10},{10,9},{13,14},{14,13},{17,18},{18,... | collective-permute-start | bytes 786440 | tf_op jit(solution)/shard_map/ppermute | solution.py:303
  104.5 38.6 %copy-start.5 = (f32[512,128]{1,0:T(8,128)S(1)}, f32[512,128]{1,0:T(8,128)}, u32[]{:S(2)}) copy-start(f32[512,128]{1,0:T(8,128)} %copy-done.4) | copy-start | bytes 786436
  104.5 4.7 %collective-permute-start.26 = (bf16[8,128,128]{2,1,0:T(8,128)(2,1)S(1)}, bf16[8,128,128]{2,1,0:T(8,128)(2,1)S(1)}, u32[]{:S(2)}, u32[]{:S(2)}) collective-permute-start(bf16[8,128,128]{2,1,0:T(8,128)(2,1)S(1)} %collective-permute-done.23.rest_1_), channel_id=1, source_target_pairs={{1,2},{2,1},{5,6},{6,5},{9,10},{10,9},{13,14},{14,13},{17,18},{18,... | collective-permute-start | bytes 786440 | tf_op jit(solution)/shard_map/ppermute | solution.py:303
  105.3 13.8 %collective-permute-start.17 = (bf16[8,128,128]{2,1,0:T(8,128)(2,1)S(1)}, bf16[8,128,128]{2,1,0:T(8,128)(2,1)S(1)}, u32[]{:S(2)}, u32[]{:S(2)}) collective-permute-start(bf16[8,128,128]{2,1,0:T(8,128)(2,1)S(1)} %collective-permute-done.10.rest_2_), channel_id=1, source_target_pairs={{1,0},{2,3},{5,4},{6,7},{9,8},{10,11},{13,12},{14,15},{17,16},{18,... | collective-permute-start | bytes 786440 | tf_op jit(solution)/shard_map/ppermute | solution.py:304
  106.6 18.1 %collective-permute-start.19 = (bf16[8,128,128]{2,1,0:T(8,128)(2,1)S(1)}, bf16[8,128,128]{2,1,0:T(8,128)(2,1)S(1)}, u32[]{:S(2)}, u32[]{:S(2)}) collective-permute-start(bf16[8,128,128]{2,1,0:T(8,128)(2,1)S(1)} %collective-permute-done.18.rest_4_), channel_id=1, source_target_pairs={{1,0},{2,3},{5,4},{6,7},{9,8},{10,11},{13,12},{14,15},{17,16},{18,... | collective-permute-start | bytes 786440 | tf_op jit(solution)/shard_map/ppermute | solution.py:304
  107.9 22.4 %collective-permute-start.25 = (bf16[8,128,128]{2,1,0:T(8,128)(2,1)S(1)}, bf16[8,128,128]{2,1,0:T(8,128)(2,1)S(1)}, u32[]{:S(2)}, u32[]{:S(2)}) collective-permute-start(bf16[8,128,128]{2,1,0:T(8,128)(2,1)S(1)} %collective-permute-done.24.rest_2_), channel_id=1, source_target_pairs={{1,0},{2,3},{5,4},{6,7},{9,8},{10,11},{13,12},{14,15},{17,16},{18,... | collective-permute-start | bytes 786440 | tf_op jit(solution)/shard_map/ppermute | solution.py:304
  109.3 25.7 %collective-permute-start.27 = (bf16[8,128,128]{2,1,0:T(8,128)(2,1)S(1)}, bf16[8,128,128]{2,1,0:T(8,128)(2,1)S(1)}, u32[]{:S(2)}, u32[]{:S(2)}) collective-permute-start(bf16[8,128,128]{2,1,0:T(8,128)(2,1)S(1)} %collective-permute-done.26.rest_4_), channel_id=1, source_target_pairs={{1,0},{2,3},{5,4},{6,7},{9,8},{10,11},{13,12},{14,15},{17,16},{18,... | collective-permute-start | bytes 786440 | tf_op jit(solution)/shard_map/ppermute | solution.py:304
  142.5 6.0 %collective-permute-start.28 = (bf16[4,8,128,128]{3,2,1,0:T(8,128)(2,1)S(1)}, bf16[4,8,128,128]{3,2,1,0:T(8,128)(2,1)S(1)}, u32[]{:S(2)}, u32[]{:S(2)}) collective-permute-start(bf16[4,8,128,128]{3,2,1,0:T(8,128)(2,1)S(1)} %get-tuple-element.81), channel_id=1, source_target_pairs={{0,4},{4,0},{8,12},{12,8},{16,20},{20,16},{24,28},{28,24},{1,5},{5... | collective-permute-start | bytes 3145736 | tf_op jit(solution)/shard_map/ppermute | solution.py:286
  142.6 5.9 %collective-permute-start.29 = (bf16[4,8,128,128]{3,2,1,0:T(8,128)(2,1)S(1)}, bf16[4,8,128,128]{3,2,1,0:T(8,128)(2,1)S(1)}, u32[]{:S(2)}, u32[]{:S(2)}) collective-permute-start(bf16[4,8,128,128]{3,2,1,0:T(8,128)(2,1)S(1)} %get-tuple-element.83), channel_id=1, source_target_pairs={{0,4},{4,0},{8,12},{12,8},{16,20},{20,16},{24,28},{28,24},{1,5},{5... | collective-permute-start | bytes 3145736 | tf_op jit(solution)/shard_map/ppermute | solution.py:286
  143.3 3.6 %collective-permute-start.33 = (bf16[128,512]{1,0:T(8,128)(2,1)S(1)}, bf16[128,512]{1,0:T(8,128)(2,1)S(1)}, u32[]{:S(2)}, u32[]{:S(2)}) collective-permute-start(bf16[128,512]{1,0:T(8,128)(2,1)S(1)} %get-tuple-element.93), channel_id=1, source_target_pairs={{0,4},{4,0},{8,12},{12,8},{16,20},{20,16},{24,28},{28,24},{1,5},{5... | collective-permute-start | bytes 393224 | tf_op jit(solution)/shard_map/ppermute | solution.py:286
  146.9 7.8 %collective-permute-start.34 = (bf16[128,512]{1,0:T(8,128)(2,1)S(1)}, bf16[128,512]{1,0:T(8,128)(2,1)S(1)}, u32[]{:S(2)}, u32[]{:S(2)}) collective-permute-start(bf16[128,512]{1,0:T(8,128)(2,1)S(1)} %add_convert_fusion.1), channel_id=1, source_target_pairs={{0,8},{4,12},{8,0},{12,4},{16,24},{20,28},{24,16},{28,20},{1,9},{5... | collective-permute-start | bytes 393224 | tf_op jit(solution)/shard_map/ppermute | solution.py:286
  148.5 1.0 copy-start.8
  151.2 28.1 %collective-permute-start.30 = (bf16[16,128,128]{2,1,0:T(8,128)(2,1)S(1)}, bf16[16,128,128]{2,1,0:T(8,128)(2,1)S(1)}, u32[]{:S(2)}, u32[]{:S(2)}) collective-permute-start(bf16[16,128,128]{2,1,0:T(8,128)(2,1)S(1)} %get-tuple-element.85), channel_id=1, source_target_pairs={{0,8},{4,12},{8,0},{12,4},{16,24},{20,28},{24,16},{28,20},{1,9},{5... | collective-permute-start | bytes 1572872 | tf_op jit(solution)/shard_map/ppermute | solution.py:286
  151.8 27.5 %collective-permute-start.31 = (bf16[16,128,128]{2,1,0:T(8,128)(2,1)S(1)}, bf16[16,128,128]{2,1,0:T(8,128)(2,1)S(1)}, u32[]{:S(2)}, u32[]{:S(2)}) collective-permute-start(bf16[16,128,128]{2,1,0:T(8,128)(2,1)S(1)} %get-tuple-element.86), channel_id=1, source_target_pairs={{0,16},{4,20},{8,24},{12,28},{16,0},{20,4},{24,8},{28,12},{1,17},{... | collective-permute-start | bytes 1572872 | tf_op jit(solution)/shard_map/ppermute | solution.py:286
  153.1 26.2 %collective-permute-start.32 = (bf16[16,128,128]{2,1,0:T(8,128)(2,1)S(1)}, bf16[16,128,128]{2,1,0:T(8,128)(2,1)S(1)}, u32[]{:S(2)}, u32[]{:S(2)}) collective-permute-start(bf16[16,128,128]{2,1,0:T(8,128)(2,1)S(1)} %get-tuple-element.87), channel_id=1, source_target_pairs={{0,24},{4,28},{8,16},{12,20},{16,8},{20,12},{24,0},{28,4},{1,25},{... | collective-permute-start | bytes 1572872 | tf_op jit(solution)/shard_map/ppermute | solution.py:286
  154.8 24.5 %collective-permute-start.35 = (bf16[128,512]{1,0:T(8,128)(2,1)S(1)}, bf16[128,512]{1,0:T(8,128)(2,1)S(1)}, u32[]{:S(2)}, u32[]{:S(2)}) collective-permute-start(bf16[128,512]{1,0:T(8,128)(2,1)S(1)} %add_convert_fusion), channel_id=1, source_target_pairs={{0,16},{4,20},{8,24},{12,28},{16,0},{20,4},{24,8},{28,12},{1,17},{... | collective-permute-start | bytes 393224 | tf_op jit(solution)/shard_map/ppermute | solution.py:286
  179.3 1.6 collective-permute-start.36
Sparse Core Ops, SparseCore 0:
  57.6 35.0 all-gather.1

commit v7 on v5

v7 whole, which is shorter than its diff:
```python
import functools

import jax
import jax.numpy as jnp
from jax import lax
from jax.experimental import pallas as pl
from jax.experimental.pallas import tpu as pltpu
from jax.sharding import PartitionSpec as P

VMEM_LIMIT = 48 * 1024 * 1024
GROUPS = 2
COPIES = 4
F32 = jnp.float32
BF16 = jnp.bfloat16
VMEM = pl.BlockSpec(memory_space=pltpu.VMEM)
SMEM = pl.BlockSpec(memory_space=pltpu.SMEM)
PARAMS = pltpu.CompilerParams(vmem_limit_bytes=VMEM_LIMIT)


def tile_copy(tiles_ref, held, sems, i):
    per = held.shape[0] // COPIES
    part = pl.ds(i * per, per)
    return pltpu.make_async_copy(tiles_ref.at[part], held.at[part], sems.at[i])


def over_rows(tiles_ref, held, sems, one_row):
    per = held.shape[0] // COPIES

    def piece(i, carry):
        tile_copy(tiles_ref, held, sems, i).wait()
        for j in range(per):
            one_row(i * per + j)
        return carry

    lax.fori_loop(0, COPIES, piece, 0)


def spread_kernel(first, cols_ref, me_ref, tiles_ref, vals_ref, *rest):
    if first:
        mask_ref, *rest = rest
        outs, (mask_out, acc, held, sems, left_ref, mask_held) = rest[: 2 * GROUPS], rest[2 * GROUPS :]
        loads = [
            pltpu.make_async_copy(vals_ref, left_ref, sems.at[COPIES]),
            pltpu.make_async_copy(mask_ref, mask_held, sems.at[COPIES + 1]),
        ]
        loads[0].start()
    else:
        outs, (acc, held, sems) = rest[: 2 * GROUPS], rest[2 * GROUPS :]
    for i in range(COPIES):
        tile_copy(tiles_ref, held, sems, i).start()
    if first:
        loads[1].start()
    acc[...] = jnp.zeros_like(acc)
    per_row, size = held.shape[1], held.shape[3]
    me = me_ref[0]
    if first:
        loads[0].wait()

    def one_row(r):
        left = left_ref[r].astype(F32).T.astype(BF16) if first else vals_ref[r]
        for k in range(0, per_row, 2):
            pair = jnp.concatenate([held[r, k], held[r, k + 1]], axis=1)
            both = jnp.dot(left, pair, preferred_element_type=F32)
            for side in range(2):
                acc[cols_ref[r, k + side]] += both[:, side * size : (side + 1) * size]

    over_rows(tiles_ref, held, sems, one_row)
    halves, count = outs[0].shape[:2]
    for g in range(GROUPS):
        for side in range(2):
            for rel in range(halves):
                owner = jnp.bitwise_xor(me, 2 * rel + side)
                start = (owner * GROUPS + g) * count
                outs[2 * g + side][rel] = acc[pl.ds(start, count)].astype(BF16)
    if first:
        loads[1].wait()
        for b in range(mask_held.shape[0]):
            mask_out[b] = mask_held[b].astype(F32).T.astype(BF16)


def spread(edge_tiles, block_cols, vals, me, rows, mask=None):
    blocks, _, size, _ = edge_tiles.shape
    first = mask is not None
    feat = vals.shape[2] if first else vals.shape[1]
    out = jax.ShapeDtypeStruct((rows // 2, blocks // GROUPS, feat, size), BF16)
    outs = [out] * (2 * GROUPS)
    scratch = [
        pltpu.VMEM((rows * blocks, feat, size), F32),
        pltpu.VMEM(edge_tiles.shape, BF16),
        pltpu.SemaphoreType.DMA((COPIES + 2,)),
    ]
    anywhere = pl.BlockSpec(memory_space=pl.ANY)
    if first:
        outs.append(jax.ShapeDtypeStruct((blocks, feat, size), BF16))
        scratch += [pltpu.VMEM(v.shape, v.dtype) for v in (vals, mask)]
        args, place = [vals, mask], anywhere
    else:
        args, place = [vals], VMEM
    return pl.pallas_call(
        functools.partial(spread_kernel, first),
        out_shape=outs,
        in_specs=[SMEM, SMEM, anywhere] + [place] * len(args),
        out_specs=[VMEM] * len(outs),
        scratch_shapes=scratch,
        compiler_params=PARAMS,
        cost_estimate=pl.CostEstimate(flops=2 * edge_tiles.size * feat, bytes_accessed=30_000_000, transcendentals=0),
        name="spread",
    )(block_cols, me, edge_tiles, *args)


def aggregate_kernel(cols_ref, me_ref, tiles_ref, *rest):
    parts, (out_ref, held, table, sems) = rest[:-4], rest[-4:]
    blocks, per_row = held.shape[:2]
    loads = []
    for rel, part in enumerate(parts):
        place = table.at[pl.ds(jnp.bitwise_xor(me_ref[0], rel) * blocks, blocks)]
        loads.append(pltpu.make_async_copy(part, place, sems.at[COPIES + rel]))
    for load in loads:
        load.start()
    for i in range(COPIES):
        tile_copy(tiles_ref, held, sems, i).start()
    for load in loads:
        load.wait()

    def one_row(r):
        total = None
        for k in range(0, per_row, 2):
            pair = jnp.concatenate([held[r, k], held[r, k + 1]], axis=1)
            picked = jnp.concatenate([table[cols_ref[r, k]], table[cols_ref[r, k + 1]]], axis=0)
            term = jnp.dot(pair, picked, preferred_element_type=F32)
            total = term if total is None else total + term
        out_ref[r] = total.astype(BF16)

    over_rows(tiles_ref, held, sems, one_row)


def aggregate(edge_tiles, block_cols, parts, me):
    blocks, _, size, _ = edge_tiles.shape
    feat = parts[0].shape[2]
    anywhere = pl.BlockSpec(memory_space=pl.ANY)
    return pl.pallas_call(
        aggregate_kernel,
        out_shape=jax.ShapeDtypeStruct((blocks, size, feat), BF16),
        in_specs=[SMEM, SMEM, anywhere] + [anywhere] * len(parts),
        out_specs=VMEM,
        scratch_shapes=[
            pltpu.VMEM(edge_tiles.shape, BF16),
            pltpu.VMEM((len(parts) * blocks, size, feat), BF16),
            pltpu.SemaphoreType.DMA((COPIES + len(parts),)),
        ],
        compiler_params=PARAMS,
        cost_estimate=pl.CostEstimate(flops=2 * edge_tiles.size * feat, bytes_accessed=30_000_000, transcendentals=0),
        name="aggregate",
    )(block_cols, me, edge_tiles, *parts)


def finish_kernel(last, *refs):
    parts, out_ref = refs[:-1], refs[-1]
    count = parts[0].shape[0]
    for g in range(GROUPS):
        for b in range(count):
            total = parts[2 * g][b].astype(F32) + parts[2 * g + 1][b].astype(F32)
            out_ref[g * count + b] = (total.T if last else total).astype(BF16)


def finish(parts, last):
    count, feat, size = parts[0].shape
    return pl.pallas_call(
        functools.partial(finish_kernel, last),
        out_shape=jax.ShapeDtypeStruct((count * GROUPS,) + ((size, feat) if last else (feat, size)), BF16),
        in_specs=[VMEM] * len(parts),
        out_specs=VMEM,
        compiler_params=PARAMS,
        cost_estimate=pl.CostEstimate(flops=0, bytes_accessed=1_000_000_000 if last else 1, transcendentals=0),
        name="finish",
    )(*parts)


def dense_kernel(cols, masked, col_ref, weight_ref, *rest):
    shards, rest = rest[:cols], rest[cols:]
    side_ref, rest = rest[0], rest[1:]
    if masked:
        mask_ref, rest = rest[0], rest[1:]
    out_ref, grad_ref, whole_ref = rest
    blocks, feat, size = shards[0].shape
    for m in range(cols):
        place = jnp.bitwise_xor(col_ref[0], m)
        for b in range(blocks):
            whole_ref[place, :, b * size : (b + 1) * size] = shards[m][b]
    half = blocks * size // 2
    total = None
    for h in range(2):
        whole = jnp.concatenate([whole_ref[q, :, h * half : (h + 1) * half] for q in range(cols)], axis=0)
        res = jnp.dot(weight_ref[...], whole, preferred_element_type=F32)
        for i in range(blocks // 2):
            b = h * (blocks // 2) + i
            part = res[:, i * size : (i + 1) * size]
            out_ref[b] = (part * mask_ref[b].astype(F32) if masked else part).astype(BF16)
        side = jnp.concatenate([side_ref[h * (blocks // 2) + i] for i in range(blocks // 2)], axis=0)
        term = jnp.dot(whole, side, preferred_element_type=F32)
        total = term if total is None else total + term
    grad_ref[...] = total


def dense(weight, shards, side, mask, col):
    blocks, feat, size = shards[0].shape
    cols = len(shards)
    args = [weight, *shards, side] + ([] if mask is None else [mask])
    return pl.pallas_call(
        functools.partial(dense_kernel, cols, mask is not None),
        out_shape=[
            jax.ShapeDtypeStruct((blocks, feat, size), BF16),
            jax.ShapeDtypeStruct((cols * feat, side.shape[2]), F32),
        ],
        in_specs=[SMEM] + [VMEM] * len(args),
        out_specs=[VMEM, VMEM],
        scratch_shapes=[pltpu.VMEM((cols, feat, blocks * size), BF16)],
        compiler_params=PARAMS,
        name="dense",
    )(col, *args)


def weight_terms_kernel(me_ref, first_ref, second_ref, keep_ref, send_ref):
    first, second = first_ref[...].T, second_ref[...].T
    even = jnp.bitwise_and(me_ref[0], 1) == 0
    keep_ref[...] = jnp.where(even, second, first)
    send_ref[...] = jnp.where(even, first, second).astype(BF16)


def weight_terms(first, second, me):
    shape = first.shape[::-1]
    return pl.pallas_call(
        weight_terms_kernel,
        out_shape=[jax.ShapeDtypeStruct(shape, F32), jax.ShapeDtypeStruct(shape, BF16)],
        in_specs=[SMEM] + [VMEM] * 2,
        out_specs=[VMEM] * 2,
        compiler_params=PARAMS,
        name="weight_terms",
    )(me, first, second)


def swap(value, mask, axis):
    return lax.ppermute(value, axis, [(i, i ^ mask) for i in range(lax.axis_size(axis))])


def add(a, b):
    return (a.astype(F32) + b.astype(F32)).astype(BF16)


def scatter_group(keep, got, masks, beside):
    left = sorted(masks, reverse=True)
    for mask in masks:
        axis = left.index(mask)
        part = lambda v, i: lax.index_in_dim(v, i, axis, keepdims=False)
        sent = swap(add(part(keep, 1), part(got, 1)), mask, "row")
        keep = add(part(keep, 0), part(got, 0))
        got = sent
        left.remove(mask)
        if beside is not None and mask == masks[0]:
            got, beside = lax.optimization_barrier((got, beside))
    return [keep, got], beside


def scatter(pieces, rows, beside=None):
    masks = [1 << b for b in range(1, rows.bit_length() - 1)]
    lead = (2,) * len(masks)
    done = []
    for g in range(GROUPS):
        keep, got = pieces[2 * g], swap(pieces[2 * g + 1], 1, "row")
        order = masks if g % 2 == 0 else masks[::-1]
        terms, beside = scatter_group(keep.reshape(lead + keep.shape[1:]), got.reshape(lead + got.shape[1:]), order, beside)
        done += terms
    return done, beside


def gather_columns(own, cols):
    if cols == 4:
        far = swap(own, 3, "col")
        return [own, swap(own, 1, "col"), swap(far, 1, "col"), far]
    return [own] + [swap(own, m, "col") for m in range(1, cols)]


def over_chips(value, rows):
    mask = 2
    while mask < rows:
        value = value.astype(BF16)
        value = value.astype(F32) + swap(value, mask, "row").astype(F32)
        mask *= 2
    return value


def per_device(
    node_feats, hidden_act, grad_out, relu_mask, edge_tiles, block_cols, weight_one, weight_two
):
    rows, cols = lax.axis_size("row"), lax.axis_size("col")
    me, col = lax.axis_index("row").astype(jnp.int32), lax.axis_index("col").astype(jnp.int32)
    me_at, col_at = me.reshape(1), col.reshape(1)
    size = edge_tiles.shape[2]
    blocked = lambda v: v.reshape(v.shape[0] // size, size, v.shape[1])
    after = lax.optimization_barrier

    *pieces, mask = spread(edge_tiles, block_cols, blocked(grad_out), me_at, rows, blocked(relu_mask))
    terms, _ = scatter(pieces, rows)
    own, node_feats = after((finish(terms, False), blocked(node_feats)))
    shards = gather_columns(own, cols)
    parts = [node_feats] + [swap(node_feats, rel, "row") for rel in range(2, rows, 2)]
    shards, parts = after((shards, parts))
    delta, second = dense(weight_two, shards, blocked(hidden_act), mask, col_at)
    delta, parts = after((delta, parts))
    shards = gather_columns(delta, cols)
    parts = [v for part in parts for v in (part, swap(part, 1, "row"))]
    agg_feats = aggregate(edge_tiles, block_cols, parts, me_at)
    spread_in, first = dense(weight_one, shards, agg_feats, None, col_at)
    pieces = spread(edge_tiles, block_cols, spread_in, me_at, rows)
    keep, send = weight_terms(first, second, me_at)
    terms, value = scatter(pieces, rows, keep + swap(send, 1, "row").astype(F32))
    out = finish(terms, True)
    value = over_chips(value, rows)
    other = swap(value, 1, "row")
    even = me % 2 == 0
    first_grad, second_grad = jnp.where(even, other, value), jnp.where(even, value, other)
    return out.reshape(-1, out.shape[2]), first_grad, second_grad


def solution(mesh):
    in_specs = (
        P("row", "col"),
        P("row", "col"),
        P("row", "col"),
        P("row", "col"),
        P("row", None, None, None),
        P("row", None),
        P("col", None),
        P("col", None),
    )
    out_specs = (P("row", "col"), P("col", None), P("col", None))
    return jax.shard_map(
        per_device, mesh=mesh, in_specs=in_specs, out_specs=out_specs, check_vma=False
    )
```

time: 175 us -> 161 us (0.920); the launches traced: 173 us -> 161 us
  waiting for transfers between devices: 60.9 us -> 81.2 us
  between operations: 14.6 us -> 0.88 us
  starting transfers between devices: 60.7 us -> 47 us
  local copies, waits for them, and re-layouts: 5.84 us -> 2.8 us
  Pallas kernels: 27.9 us -> 25.7 us
    ppermute x24 -> x0, starting transfers between devices: 42.4 us -> none  [the longest x12 26.9 us: chain_gather(): up = lax.ppermute(up, 'col', [(i, i + 1) for i in range(s - 1, cols - 1)])]
    ppermute x16 -> x29, waiting for transfers between devices: 39 us -> 81.2 us  [swap(): lax.ppermute(value, axis, [(i, i ^ mask) for i in range(lax.axis_size(axi...]
    ppermute x16 -> x29, starting transfers between devices: 18.3 us -> 47 us  [swap(): lax.ppermute(value, axis, [(i, i ^ mask) for i in range(lax.axis_size(axi...]
    ppermute x24 -> x0, waiting for transfers between devices: 21.9 us -> none  [the longest x12 21.8 us: chain_gather(): lax.ppermute(down, 'col', [(i, i - 1) for i in range(1, cols - s + 1)])]
    pallas_call x4 -> x2, Pallas kernels: 6.89 us -> 4.43 us  [dense(): pl.pallas_call(functools.partial(dense_kernel, cols, mask is not None), o...]
    unnamed x20 -> x18, local copies, waits for them, and re-layouts: 4.64 us -> 2.8 us
  transfers between devices with their start and end apart: 41 -> 29, of which waited for: 18 -> 17; matrix products, arithmetic and copies ran while one was open for 2% -> 2% of each run, Pallas kernels for 8% -> 5%
where the time goes in v7:
time: 161 us
  waiting for transfers between devices  81.2 us (50%)
  starting transfers between devices  47 us (29%)
  Pallas kernels  25.7 us (16%)
  other arithmetic  3.28 us (2%)
  local copies, waits for them, and re-layouts  2.8 us (2%)
    ppermute x29, waiting for transfers between devices, swap(): lax.ppermute(value, axis, [(i, i ^ mask) for i in range(lax.axis_size(axi...  81.2 us
    ppermute x29, starting transfers between devices, swap(): lax.ppermute(value, axis, [(i, i ^ mask) for i in range(lax.axis_size(axi...  47 us
    pallas_call x2, Pallas kernels, spread(): pl.pallas_call(functools.partial(spread_kernel, first), out_shape=outs, i...  13.8 us
    pallas_call x1, Pallas kernels, aggregate(): pl.pallas_call(aggregate_kernel, out_shape=jax.ShapeDtypeStruct((blocks,...  6.17 us
    pallas_call x2, Pallas kernels, dense(): pl.pallas_call(functools.partial(dense_kernel, cols, mask is not None), o...  4.43 us
  transfers between devices with their start and end apart: 29, of which 17 were waited for; matrix products, arithmetic and copies ran while one was open for 2% of the time, Pallas kernels for 5%

profile of v7, /device:TPU:0, one launch (start us, length us, event | category | flops | bytes accessed | tf_op | source)
XLA Modules:
  0.0 160.9 jit_solution(5116853068488652200)
XLA Ops:
  0.6 1.0 copy-done.4
  1.7 0.7 copy-done.7
  2.4 7.0 %spread.2 = (bf16[4,8,128,128]{3,2,1,0:T(8,128)(2,1)S(1)}, bf16[4,8,128,128]{3,2,1,0:T(8,128)(2,1)S(1)}, bf16[4,8,128,128]{3,2,1,0:T(8,128)(2,1)S(1)}, bf16[4,8,...) custom-call(s32[16,20]{1,0:T(8,128)S(1)} %copy-done.7, s32[1]{0:T(128)} %bitcast.me_ref, ...), custom_call_target="tpu_custom_call" | custom-call | flops 1342177280 | bytes 30000000 | tf_op jit(solution)/shard_map/spread/pallas_call | solution.py:99
  9.5 0.5 collective-permute-start.3
  10.0 0.1 collective-permute-start
  10.1 2.2 %collective-permute-done.3 = bf16[4,8,128,128]{3,2,1,0:T(8,128)(2,1)S(1)} collective-permute-done((bf16[4,8,128,128]{3,2,1,0:T(8,128)(2,1)S(1)}, bf16[4,8,128,128]{3,2,1,0:T(8,128)(2,1)S(1)}, u32[]{:S(2)}, u32[]{:S(2)}) %collective-permute-start.3) | collective-permute-done | bytes 1048608 | tf_op jit(solution)/shard_map/ppermute | solution.py:243
  12.3 0.5 add_convert_fusion.5
  12.7 2.9 %collective-permute-start.4 = (bf16[2,8,128,128]{3,2,1,0:T(8,128)(2,1)S(1)}, bf16[2,8,128,128]{3,2,1,0:T(8,128)(2,1)S(1)}, u32[]{:S(2)}, u32[]{:S(2)}) collective-permute-start(bf16[2,8,128,128]{3,2,1,0:T(8,128)(2,1)S(1)} %get-tuple-element.76), channel_id=1, source_target_pairs={{0,16},{4,20},{8,24},{12,28},{16,0},{20,4},{24,8},{28,12},{1,17},{... | collective-permute-start | bytes 1572872 | tf_op jit(solution)/shard_map/ppermute | solution.py:243
  15.7 0.4 add_convert_fusion.7
  16.1 1.6 collective-permute-start.1
  17.6 10.3 %collective-permute-done.4 = bf16[2,8,128,128]{3,2,1,0:T(8,128)(2,1)S(1)} collective-permute-done((bf16[2,8,128,128]{3,2,1,0:T(8,128)(2,1)S(1)}, bf16[2,8,128,128]{3,2,1,0:T(8,128)(2,1)S(1)}, u32[]{:S(2)}, u32[]{:S(2)}) %collective-permute-start.4) | collective-permute-done | bytes 524320 | tf_op jit(solution)/shard_map/ppermute | solution.py:243
  27.9 0.1 fusion.7
  28.0 1.8 %collective-permute-start.5 = (bf16[8,128,128]{2,1,0:T(8,128)(2,1)S(1)}, bf16[8,128,128]{2,1,0:T(8,128)(2,1)S(1)}, u32[]{:S(2)}, u32[]{:S(2)}) collective-permute-start(bf16[8,128,128]{2,1,0:T(8,128)(2,1)S(1)} %get-tuple-element.83), channel_id=1, source_target_pairs={{0,8},{4,12},{8,0},{12,4},{16,24},{20,28},{24,16},{28,20},{1,9},{5... | collective-permute-start | bytes 786440 | tf_op jit(solution)/shard_map/ppermute | solution.py:243
  29.8 0.1 fusion.11
  30.0 1.6 collective-permute-start.2
  31.6 4.4 %collective-permute-done.5.refs_3_ = bf16[8,128,128]{2,1,0:T(8,128)(2,1)S(1)} collective-permute-done((bf16[8,128,128]{2,1,0:T(8,128)(2,1)S(1)}, bf16[8,128,128]{2,1,0:T(8,128)(2,1)S(1)}, u32[]{:S(2)}, u32[]{:S(2)}) %collective-permute-start.5) | collective-permute-done | bytes 262176 | tf_op jit(solution)/shard_map/ppermute | solution.py:243
  36.0 1.3 collective-permute-done.2.refs_1_
  37.3 0.1 finish.2.rest_0_
  37.4 3.7 %collective-permute-start.7 = (bf16[16,128,128]{2,1,0:T(8,128)(2,1)S(1)}, bf16[16,128,128]{2,1,0:T(8,128)(2,1)}, u32[]{:S(2)}, u32[]{:S(2)}) collective-permute-start(bf16[16,128,128]{2,1,0:T(8,128)(2,1)S(1)} %finish.2.rest_0_), channel_id=1, source_target_pairs={{0,3},{1,2},{2,1},{3,0},{4,7},{5,6},{6,5},{7,4},{8,11},{9,10},{10,... | collective-permute-start | bytes 1572872 | tf_op jit(solution)/shard_map/ppermute | solution.py:243
  41.1 1.5 collective-permute-start.10
  42.6 1.4 collective-permute-start.11
  44.0 0.6 collective-permute-start.9
  44.6 9.7 %collective-permute-done.7.rest_3_ = bf16[16,128,128]{2,1,0:T(8,128)(2,1)} collective-permute-done((bf16[16,128,128]{2,1,0:T(8,128)(2,1)S(1)}, bf16[16,128,128]{2,1,0:T(8,128)(2,1)}, u32[]{:S(2)}, u32[]{:S(2)}) %collective-permute-start.7) | collective-permute-done | bytes 524320 | tf_op jit(solution)/shard_map/ppermute | solution.py:243
  54.3 8.0 %collective-permute-start.8 = (bf16[16,128,128]{2,1,0:T(8,128)(2,1)}, bf16[16,128,128]{2,1,0:T(8,128)(2,1)}, u32[]{:S(2)}, u32[]{:S(2)}) collective-permute-start(bf16[16,128,128]{2,1,0:T(8,128)(2,1)} %collective-permute-done.7.rest_3_), channel_id=1, source_target_pairs={{0,1},{1,0},{2,3},{3,2},{4,5},{5,4},{6,7},{7,6},{8,9},{9,8},{10,11... | collective-permute-start | bytes 1572872 | tf_op jit(solution)/shard_map/ppermute | solution.py:243
  62.3 1.6 %collective-permute-done.10.rest_4_ = bf16[16,128,128]{2,1,0:T(8,128)(2,1)S(1)} collective-permute-done((bf16[16,128,128]{2,1,0:T(8,128)(2,1)S(1)}, bf16[16,128,128]{2,1,0:T(8,128)(2,1)S(1)}, u32[]{:S(2)}, u32[]{:S(2)}) %collective-permute-start.10) | collective-permute-done | bytes 524320 | tf_op jit(solution)/shard_map/ppermute | solution.py:243
  64.0 1.3 collective-permute-done.9.rest_2_
  65.3 8.6 %collective-permute-done.8.rest_2_ = bf16[16,128,128]{2,1,0:T(8,128)(2,1)} collective-permute-done((bf16[16,128,128]{2,1,0:T(8,128)(2,1)}, bf16[16,128,128]{2,1,0:T(8,128)(2,1)}, u32[]{:S(2)}, u32[]{:S(2)}) %collective-permute-start.8) | collective-permute-done | bytes 524320 | tf_op jit(solution)/shard_map/ppermute | solution.py:243
  73.9 1.0 copy-done.3
  75.0 2.9 %dense.2 = (bf16[16,128,128]{2,1,0:T(8,128)(2,1)S(1)}, f32[512,128]{1,0:T(8,128)S(1)}) custom-call(s32[1]{0:T(128)} %bitcast.1.col_ref, bf16[128,512]{1,0:T(8,128)(2,1)S(1)} %copy-done.5, bf16[16,128,128]{2,1,0:T(8,128)(2,1)S(1)} %finish.2.rest_0_, bf16[16,128,128]{2,1,0:T(8,128)(2,1)} %collective-permute-done.6.rest_1_, ...), custom_call_target="tpu_custom_call" | custom-call | tf_op jit(solution)/shard_map/dense/pallas_call | solution.py:209
  77.9 0.1 collective-permute-start.15
  78.0 3.6 %collective-permute-start.13 = (bf16[16,128,128]{2,1,0:T(8,128)(2,1)S(1)}, bf16[16,128,128]{2,1,0:T(8,128)(2,1)S(1)}, u32[]{:S(2)}, u32[]{:S(2)}) collective-permute-start(bf16[16,128,128]{2,1,0:T(8,128)(2,1)S(1)} %get-tuple-element.53.rest_0_), channel_id=1, source_target_pairs={{0,3},{1,2},{2,1},{3,0},{4,7},{5,6},{6,5},{7,4},{8,11},{9,10},{10,... | collective-permute-start | bytes 1572872 | tf_op jit(solution)/shard_map/ppermute | solution.py:243
  81.6 0.2 collective-permute-start.16
  81.7 0.3 collective-permute-start.17
  82.1 0.2 collective-permute-start.18
  82.3 12.4 %collective-permute-done.13.rest_3_ = bf16[16,128,128]{2,1,0:T(8,128)(2,1)S(1)} collective-permute-done((bf16[16,128,128]{2,1,0:T(8,128)(2,1)S(1)}, bf16[16,128,128]{2,1,0:T(8,128)(2,1)S(1)}, u32[]{:S(2)}, u32[]{:S(2)}) %collective-permute-start.13) | collective-permute-done | bytes 524320 | tf_op jit(solution)/shard_map/ppermute | solution.py:243
  94.6 10.6 %collective-permute-start.14 = (bf16[16,128,128]{2,1,0:T(8,128)(2,1)S(1)}, bf16[16,128,128]{2,1,0:T(8,128)(2,1)S(1)}, u32[]{:S(2)}, u32[]{:S(2)}) collective-permute-start(bf16[16,128,128]{2,1,0:T(8,128)(2,1)S(1)} %collective-permute-done.13.rest_3_), channel_id=1, source_target_pairs={{0,1},{1,0},{2,3},{3,2},{4,5},{5,4},{6,7},{7,6},{8,9},{9,8},{10,11... | collective-permute-start | bytes 1572872 | tf_op jit(solution)/shard_map/ppermute | solution.py:243
  105.3 6.2 %aggregate.1.rest_4_ = bf16[16,128,128]{2,1,0:T(8,128)(2,1)S(1)} custom-call(s32[16,20]{1,0:T(8,128)S(1)} %copy-done.8, s32[1]{0:T(128)} %bitcast.me_ref, bf16[16,20,128,128]{3,2,1,0:T(8,128)(2,1)} %tiles_ref.5, bf16[16,128,128]{2,1,0:T(8,128)(2,1)S(1)} %bitcast.57, bf16[16,128,128]{2,1,0:T(8,128)(2,1)S(1)} %collective-permute-done.15.rest_1_, ...), custom_call_target="tpu_custom_call" | custom-call | flops 1342177280 | bytes 30000000 | tf_op jit(solution)/shard_map/aggregate/pallas_call | solution.py:141
  111.5 5.5 %collective-permute-done.14.rest_2_ = bf16[16,128,128]{2,1,0:T(8,128)(2,1)S(1)} collective-permute-done((bf16[16,128,128]{2,1,0:T(8,128)(2,1)S(1)}, bf16[16,128,128]{2,1,0:T(8,128)(2,1)S(1)}, u32[]{:S(2)}, u32[]{:S(2)}) %collective-permute-start.14) | collective-permute-done | bytes 524320 | tf_op jit(solution)/shard_map/ppermute | solution.py:243
  117.0 1.5 dense.3
  118.6 6.8 %spread.3 = (bf16[4,8,128,128]{3,2,1,0:T(8,128)(2,1)S(1)}, bf16[4,8,128,128]{3,2,1,0:T(8,128)(2,1)S(1)}, bf16[4,8,128,128]{3,2,1,0:T(8,128)(2,1)S(1)}, bf16[4,8,128,128]{3,2,1,0:T(8,128)(2,1)S(1)}) custom-call(s32[16,20]{1,0:T(8,128)S(1)} %copy-done.8, s32[1]{0:T(128)} %bitcast.me_ref, bf16[16,20,128,128]{3,2,1,0:T(8,128)(2,1)} %tiles_ref.5, ...), custom_call_target="tpu_custom_call" | custom-call | flops 1342177280 | bytes 30000000 | tf_op jit(solution)/shard_map/spread/pallas_call | solution.py:99
  125.3 0.1 collective-permute-start.19
  125.4 0.5 collective-permute-start.23
  125.9 2.1 %collective-permute-done.19 = bf16[4,8,128,128]{3,2,1,0:T(8,128)(2,1)S(1)} collective-permute-done((bf16[4,8,128,128]{3,2,1,0:T(8,128)(2,1)S(1)}, bf16[4,8,128,128]{3,2,1,0:T(8,128)(2,1)S(1)}, u32[]{:S(2)}, u32[]{:S(2)}) %collective-permute-start.19) | collective-permute-done | bytes 1048608 | tf_op jit(solution)/shard_map/ppermute | solution.py:243
  128.0 0.4 fusion.1
  128.4 1.4 collective-permute-start.20
  129.9 0.5 add_convert_fusion
  130.3 2.0 %collective-permute-start.24 = (bf16[2,8,128,128]{3,2,1,0:T(8,128)(2,1)S(1)}, bf16[2,8,128,128]{3,2,1,0:T(8,128)(2,1)S(1)}, u32[]{:S(2)}, u32[]{:S(2)}) collective-permute-start(bf16[2,8,128,128]{3,2,1,0:T(8,128)(2,1)S(1)} %get-tuple-element.71), channel_id=1, source_target_pairs={{0,16},{4,20},{8,24},{12,28},{16,0},{20,4},{24,8},{28,12},{1,17},{... | collective-permute-start | bytes 1572872 | tf_op jit(solution)/shard_map/ppermute | solution.py:243
  132.3 0.2 weight_terms.1
  132.5 0.1 collective-permute-start.21
  132.6 1.3 collective-permute-done.21
  133.9 8.5 %collective-permute-done.20 = bf16[2,8,128,128]{3,2,1,0:T(8,128)(2,1)S(1)} collective-permute-done((bf16[2,8,128,128]{3,2,1,0:T(8,128)(2,1)S(1)}, bf16[2,8,128,128]{3,2,1,0:T(8,128)(2,1)S(1)}, u32[]{:S(2)}, u32[]{:S(2)}) %collective-permute-start.20) | collective-permute-done | bytes 524320 | tf_op jit(solution)/shard_map/ppermute | solution.py:243
  142.5 1.8 %collective-permute-done.24 = bf16[2,8,128,128]{3,2,1,0:T(8,128)(2,1)S(1)} collective-permute-done((bf16[2,8,128,128]{3,2,1,0:T(8,128)(2,1)S(1)}, bf16[2,8,128,128]{3,2,1,0:T(8,128)(2,1)S(1)}, u32[]{:S(2)}, u32[]{:S(2)}) %collective-permute-start.24) | collective-permute-done | bytes 524320 | tf_op jit(solution)/shard_map/ppermute | solution.py:243
  144.2 1.3 collective-permute-start.26
  145.6 0.2 fusion.9
  145.8 0.8 collective-permute-start.25
  146.5 4.1 %collective-permute-done.26 = bf16[128,512]{1,0:T(8,128)(2,1)S(1)} collective-permute-done((bf16[128,512]{1,0:T(8,128)(2,1)S(1)}, bf16[128,512]{1,0:T(8,128)(2,1)S(1)}, u32[]{:S(2)}, u32[]{:S(2)}) %collective-permute-start.26) | collective-permute-done | bytes 131104 | tf_op jit(solution)/shard_map/ppermute | solution.py:243
  150.6 1.7 %collective-permute-start.27 = (bf16[128,512]{1,0:T(8,128)(2,1)S(1)}, bf16[128,512]{1,0:T(8,128)(2,1)S(1)}, u32[]{:S(2)}, u32[]{:S(2)}) collective-permute-start(bf16[128,512]{1,0:T(8,128)(2,1)S(1)} %add_convert_fusion.12), channel_id=1, source_target_pairs={{0,16},{4,20},{8,24},{12,28},{16,0},{20,4},{24,8},{28,12},{1,17},{... | collective-permute-start | bytes 393224 | tf_op jit(solution)/shard_map/ppermute | solution.py:243
  152.4 0.2 fusion.13
  152.6 0.4 collective-permute-start.22
  153.0 2.7 %collective-permute-done.27 = bf16[128,512]{1,0:T(8,128)(2,1)S(1)} collective-permute-done((bf16[128,512]{1,0:T(8,128)(2,1)S(1)}, bf16[128,512]{1,0:T(8,128)(2,1)S(1)}, u32[]{:S(2)}, u32[]{:S(2)}) %collective-permute-start.27) | collective-permute-done | bytes 131104 | tf_op jit(solution)/shard_map/ppermute | solution.py:243
  155.7 0.1 collective-permute-start.28
  155.8 3.2 %collective-permute-done.22.refs_1_ = bf16[8,128,128]{2,1,0:T(8,128)(2,1)S(1)} collective-permute-done((bf16[8,128,128]{2,1,0:T(8,128)(2,1)S(1)}, bf16[8,128,128]{2,1,0:T(8,128)(2,1)S(1)}, u32[]{:S(2)}, u32[]{:S(2)}) %collective-permute-start.22) | collective-permute-done | bytes 262176 | tf_op jit(solution)/shard_map/ppermute | solution.py:243
  159.0 1.0 finish.3
  160.0 0.9 broadcast_select_fusion
  (32 shorter events, 0.2 us)
Async XLA Ops:
  0.6 1.0 copy-start.4
  1.7 0.7 copy-start.7
  2.4 38.7 %copy-start = (bf16[2048,128]{1,0:T(8,128)(2,1)S(1)}, bf16[2048,128]{1,0:T(8,128)(2,1)}, u32[]{:S(2)}) copy-start(bf16[2048,128]{1,0:T(8,128)(2,1)} %param.8) | copy-start | bytes 1572868
  2.4 71.6 %copy-start.1 = (bf16[2048,128]{1,0:T(8,128)(2,1)S(1)}, bf16[2048,128]{1,0:T(8,128)(2,1)}, u32[]{:S(2)}) copy-start(bf16[2048,128]{1,0:T(8,128)(2,1)} %param.9) | copy-start | bytes 1572868
  2.4 71.6 %copy-start.5 = (bf16[128,512]{1,0:T(8,128)(2,1)S(1)}, bf16[128,512]{1,0:T(8,128)(2,1)}, u32[]{:S(2)}) copy-start(bf16[128,512]{1,0:T(8,128)(2,1)} %weight_ref.2) | copy-start | bytes 393220
  2.4 102.9 %copy-start.8 = (s32[16,20]{1,0:T(8,128)S(1)}, s32[16,20]{1,0:T(8,128)}, u32[]{:S(2)}) copy-start(s32[16,20]{1,0:T(8,128)} %cols_ref.5) | copy-start | bytes 3844
  9.4 28.0 %copy-start.2 = (bf16[16,128,128]{2,1,0:T(8,128)(2,1)}, bf16[16,128,128]{2,1,0:T(8,128)(2,1)S(1)}, u32[]{:S(2)}) copy-start(bf16[16,128,128]{2,1,0:T(8,128)(2,1)S(1)} %get-tuple-element.47.rest_5_) | copy-start | bytes 1572868
  9.5 2.8 %collective-permute-start.3 = (bf16[4,8,128,128]{3,2,1,0:T(8,128)(2,1)S(1)}, bf16[4,8,128,128]{3,2,1,0:T(8,128)(2,1)S(1)}, u32[]{:S(2)}, u32[]{:S(2)}) collective-permute-start(bf16[4,8,128,128]{3,2,1,0:T(8,128)(2,1)S(1)} %get-tuple-element.40), channel_id=1, source_target_pairs={{0,4},{4,0},{8,12},{12,8},{16,20},{20,16},{24,28},{28,24},{1,5},{5... | collective-permute-start | bytes 3145736 | tf_op jit(solution)/shard_map/ppermute | solution.py:243
  10.0 5.7 %collective-permute-start = (bf16[4,8,128,128]{3,2,1,0:T(8,128)(2,1)S(1)}, bf16[4,8,128,128]{3,2,1,0:T(8,128)(2,1)S(1)}, u32[]{:S(2)}, u32[]{:S(2)}) collective-permute-start(bf16[4,8,128,128]{3,2,1,0:T(8,128)(2,1)S(1)} %get-tuple-element.38), channel_id=1, source_target_pairs={{0,4},{4,0},{8,12},{12,8},{16,20},{20,16},{24,28},{28,24},{1,5},{5... | collective-permute-start | bytes 3145736 | tf_op jit(solution)/shard_map/ppermute | solution.py:243
  12.7 15.2 %collective-permute-start.4 = (bf16[2,8,128,128]{3,2,1,0:T(8,128)(2,1)S(1)}, bf16[2,8,128,128]{3,2,1,0:T(8,128)(2,1)S(1)}, u32[]{:S(2)}, u32[]{:S(2)}) collective-permute-start(bf16[2,8,128,128]{3,2,1,0:T(8,128)(2,1)S(1)} %get-tuple-element.76), channel_id=1, source_target_pairs={{0,16},{4,20},{8,24},{12,28},{16,0},{20,4},{24,8},{28,12},{1,17},{... | collective-permute-start | bytes 1572872 | tf_op jit(solution)/shard_map/ppermute | solution.py:243
  16.1 13.8 %collective-permute-start.1 = (bf16[2,8,128,128]{3,2,1,0:T(8,128)(2,1)S(1)}, bf16[2,8,128,128]{3,2,1,0:T(8,128)(2,1)S(1)}, u32[]{:S(2)}, u32[]{:S(2)}) collective-permute-start(bf16[2,8,128,128]{3,2,1,0:T(8,128)(2,1)S(1)} %get-tuple-element.78), channel_id=1, source_target_pairs={{0,8},{4,12},{8,0},{12,4},{16,24},{20,28},{24,16},{28,20},{1,9},{5... | collective-permute-start | bytes 1572872 | tf_op jit(solution)/shard_map/ppermute | solution.py:243
  28.0 7.9 %collective-permute-start.5 = (bf16[8,128,128]{2,1,0:T(8,128)(2,1)S(1)}, bf16[8,128,128]{2,1,0:T(8,128)(2,1)S(1)}, u32[]{:S(2)}, u32[]{:S(2)}) collective-permute-start(bf16[8,128,128]{2,1,0:T(8,128)(2,1)S(1)} %get-tuple-element.83), channel_id=1, source_target_pairs={{0,8},{4,12},{8,0},{12,4},{16,24},{20,28},{24,16},{28,20},{1,9},{5... | collective-permute-start | bytes 786440 | tf_op jit(solution)/shard_map/ppermute | solution.py:243
  29.8 87.2 %copy-start.6 = (bf16[128,512]{1,0:T(8,128)(2,1)S(1)}, bf16[128,512]{1,0:T(8,128)(2,1)}, u32[]{:S(2)}) copy-start(bf16[128,512]{1,0:T(8,128)(2,1)} %weight_ref.3) | copy-start | bytes 393220
  30.0 7.3 %collective-permute-start.2 = (bf16[8,128,128]{2,1,0:T(8,128)(2,1)S(1)}, bf16[8,128,128]{2,1,0:T(8,128)(2,1)S(1)}, u32[]{:S(2)}, u32[]{:S(2)}) collective-permute-start(bf16[8,128,128]{2,1,0:T(8,128)(2,1)S(1)} %get-tuple-element.85), channel_id=1, source_target_pairs={{0,16},{4,20},{8,24},{12,28},{16,0},{20,4},{24,8},{28,12},{1,17},{... | collective-permute-start | bytes 786440 | tf_op jit(solution)/shard_map/ppermute | solution.py:243
  37.4 16.9 %collective-permute-start.7 = (bf16[16,128,128]{2,1,0:T(8,128)(2,1)S(1)}, bf16[16,128,128]{2,1,0:T(8,128)(2,1)}, u32[]{:S(2)}, u32[]{:S(2)}) collective-permute-start(bf16[16,128,128]{2,1,0:T(8,128)(2,1)S(1)} %finish.2.rest_0_), channel_id=1, source_target_pairs={{0,3},{1,2},{2,1},{3,0},{4,7},{5,6},{6,5},{7,4},{8,11},{9,10},{10,... | collective-permute-start | bytes 1572872 | tf_op jit(solution)/shard_map/ppermute | solution.py:243
  41.1 22.9 %collective-permute-start.10 = (bf16[16,128,128]{2,1,0:T(8,128)(2,1)S(1)}, bf16[16,128,128]{2,1,0:T(8,128)(2,1)S(1)}, u32[]{:S(2)}, u32[]{:S(2)}) collective-permute-start(bf16[16,128,128]{2,1,0:T(8,128)(2,1)S(1)} %bitcast.53), channel_id=1, source_target_pairs={{0,16},{4,20},{8,24},{12,28},{16,0},{20,4},{24,8},{28,12},{1,17},{... | collective-permute-start | bytes 1572872 | tf_op jit(solution)/shard_map/ppermute | solution.py:243
  42.6 21.3 %collective-permute-start.11 = (bf16[16,128,128]{2,1,0:T(8,128)(2,1)S(1)}, bf16[16,128,128]{2,1,0:T(8,128)(2,1)S(1)}, u32[]{:S(2)}, u32[]{:S(2)}) collective-permute-start(bf16[16,128,128]{2,1,0:T(8,128)(2,1)S(1)} %bitcast.54), channel_id=1, source_target_pairs={{0,24},{4,28},{8,16},{12,20},{16,8},{20,12},{24,0},{28,4},{1,25},{... | collective-permute-start | bytes 1572872 | tf_op jit(solution)/shard_map/ppermute | solution.py:243
  44.0 20.0 %collective-permute-start.6 = (bf16[16,128,128]{2,1,0:T(8,128)(2,1)S(1)}, bf16[16,128,128]{2,1,0:T(8,128)(2,1)}, u32[]{:S(2)}, u32[]{:S(2)}) collective-permute-start(bf16[16,128,128]{2,1,0:T(8,128)(2,1)S(1)} %finish.2.rest_0_), channel_id=1, source_target_pairs={{0,1},{1,0},{2,3},{3,2},{4,5},{5,4},{6,7},{7,6},{8,9},{9,8},{10,11... | collective-permute-start | bytes 1572872 | tf_op jit(solution)/shard_map/ppermute | solution.py:243
  44.0 21.3 %collective-permute-start.9 = (bf16[16,128,128]{2,1,0:T(8,128)(2,1)S(1)}, bf16[16,128,128]{2,1,0:T(8,128)(2,1)S(1)}, u32[]{:S(2)}, u32[]{:S(2)}) collective-permute-start(bf16[16,128,128]{2,1,0:T(8,128)(2,1)S(1)} %bitcast.55), channel_id=1, source_target_pairs={{0,8},{4,12},{8,0},{12,4},{16,24},{20,28},{24,16},{28,20},{1,9},{5... | collective-permute-start | bytes 1572872 | tf_op jit(solution)/shard_map/ppermute | solution.py:243
  54.3 19.6 %collective-permute-start.8 = (bf16[16,128,128]{2,1,0:T(8,128)(2,1)}, bf16[16,128,128]{2,1,0:T(8,128)(2,1)}, u32[]{:S(2)}, u32[]{:S(2)}) collective-permute-start(bf16[16,128,128]{2,1,0:T(8,128)(2,1)} %collective-permute-done.7.rest_3_), channel_id=1, source_target_pairs={{0,1},{1,0},{2,3},{3,2},{4,5},{5,4},{6,7},{7,6},{8,9},{9,8},{10,11... | collective-permute-start | bytes 1572872 | tf_op jit(solution)/shard_map/ppermute | solution.py:243
  73.9 1.0 copy-start.3
  77.9 4.4 %collective-permute-start.15 = (bf16[16,128,128]{2,1,0:T(8,128)(2,1)S(1)}, bf16[16,128,128]{2,1,0:T(8,128)(2,1)S(1)}, u32[]{:S(2)}, u32[]{:S(2)}) collective-permute-start(bf16[16,128,128]{2,1,0:T(8,128)(2,1)S(1)} %bitcast.56), channel_id=1, source_target_pairs={{0,4},{4,0},{8,12},{12,8},{16,20},{20,16},{24,28},{28,24},{1,5},{5... | collective-permute-start | bytes 1572872 | tf_op jit(solution)/shard_map/ppermute | solution.py:243
  78.0 16.7 %collective-permute-start.13 = (bf16[16,128,128]{2,1,0:T(8,128)(2,1)S(1)}, bf16[16,128,128]{2,1,0:T(8,128)(2,1)S(1)}, u32[]{:S(2)}, u32[]{:S(2)}) collective-permute-start(bf16[16,128,128]{2,1,0:T(8,128)(2,1)S(1)} %get-tuple-element.53.rest_0_), channel_id=1, source_target_pairs={{0,3},{1,2},{2,1},{3,0},{4,7},{5,6},{6,5},{7,4},{8,11},{9,10},{10,... | collective-permute-start | bytes 1572872 | tf_op jit(solution)/shard_map/ppermute | solution.py:243
  81.6 23.7 %collective-permute-start.16 = (bf16[16,128,128]{2,1,0:T(8,128)(2,1)S(1)}, bf16[16,128,128]{2,1,0:T(8,128)(2,1)S(1)}, u32[]{:S(2)}, u32[]{:S(2)}) collective-permute-start(bf16[16,128,128]{2,1,0:T(8,128)(2,1)S(1)} %collective-permute-done.9.rest_2_), channel_id=1, source_target_pairs={{0,4},{4,0},{8,12},{12,8},{16,20},{20,16},{24,28},{28,24},{1,5},{5... | collective-permute-start | bytes 1572872 | tf_op jit(solution)/shard_map/ppermute | solution.py:243
  81.7 23.5 %collective-permute-start.17 = (bf16[16,128,128]{2,1,0:T(8,128)(2,1)S(1)}, bf16[16,128,128]{2,1,0:T(8,128)(2,1)S(1)}, u32[]{:S(2)}, u32[]{:S(2)}) collective-permute-start(bf16[16,128,128]{2,1,0:T(8,128)(2,1)S(1)} %collective-permute-done.10.rest_4_), channel_id=1, source_target_pairs={{0,4},{4,0},{8,12},{12,8},{16,20},{20,16},{24,28},{28,24},{1,5},{5... | collective-permute-start | bytes 1572872 | tf_op jit(solution)/shard_map/ppermute | solution.py:243
  82.1 23.2 %collective-permute-start.18 = (bf16[16,128,128]{2,1,0:T(8,128)(2,1)S(1)}, bf16[16,128,128]{2,1,0:T(8,128)(2,1)S(1)}, u32[]{:S(2)}, u32[]{:S(2)}) collective-permute-start(bf16[16,128,128]{2,1,0:T(8,128)(2,1)S(1)} %collective-permute-done.11.rest_6_), channel_id=1, source_target_pairs={{0,4},{4,0},{8,12},{12,8},{16,20},{20,16},{24,28},{28,24},{1,5},{5... | collective-permute-start | bytes 1572872 | tf_op jit(solution)/shard_map/ppermute | solution.py:243
  82.3 29.2 %collective-permute-start.12 = (bf16[16,128,128]{2,1,0:T(8,128)(2,1)S(1)}, bf16[16,128,128]{2,1,0:T(8,128)(2,1)S(1)}, u32[]{:S(2)}, u32[]{:S(2)}) collective-permute-start(bf16[16,128,128]{2,1,0:T(8,128)(2,1)S(1)} %get-tuple-element.53.rest_0_), channel_id=1, source_target_pairs={{0,1},{1,0},{2,3},{3,2},{4,5},{5,4},{6,7},{7,6},{8,9},{9,8},{10,11... | collective-permute-start | bytes 1572872 | tf_op jit(solution)/shard_map/ppermute | solution.py:243
  94.6 22.4 %collective-permute-start.14 = (bf16[16,128,128]{2,1,0:T(8,128)(2,1)S(1)}, bf16[16,128,128]{2,1,0:T(8,128)(2,1)S(1)}, u32[]{:S(2)}, u32[]{:S(2)}) collective-permute-start(bf16[16,128,128]{2,1,0:T(8,128)(2,1)S(1)} %collective-permute-done.13.rest_3_), channel_id=1, source_target_pairs={{0,1},{1,0},{2,3},{3,2},{4,5},{5,4},{6,7},{7,6},{8,9},{9,8},{10,11... | collective-permute-start | bytes 1572872 | tf_op jit(solution)/shard_map/ppermute | solution.py:243
  125.3 2.7 %collective-permute-start.19 = (bf16[4,8,128,128]{3,2,1,0:T(8,128)(2,1)S(1)}, bf16[4,8,128,128]{3,2,1,0:T(8,128)(2,1)S(1)}, u32[]{:S(2)}, u32[]{:S(2)}) collective-permute-start(bf16[4,8,128,128]{3,2,1,0:T(8,128)(2,1)S(1)} %get-tuple-element.60), channel_id=1, source_target_pairs={{0,4},{4,0},{8,12},{12,8},{16,20},{20,16},{24,28},{28,24},{1,5},{5... | collective-permute-start | bytes 3145736 | tf_op jit(solution)/shard_map/ppermute | solution.py:243
  125.4 4.5 %collective-permute-start.23 = (bf16[4,8,128,128]{3,2,1,0:T(8,128)(2,1)S(1)}, bf16[4,8,128,128]{3,2,1,0:T(8,128)(2,1)S(1)}, u32[]{:S(2)}, u32[]{:S(2)}) collective-permute-start(bf16[4,8,128,128]{3,2,1,0:T(8,128)(2,1)S(1)} %get-tuple-element.67), channel_id=1, source_target_pairs={{0,4},{4,0},{8,12},{12,8},{16,20},{20,16},{24,28},{28,24},{1,5},{5... | collective-permute-start | bytes 3145736 | tf_op jit(solution)/shard_map/ppermute | solution.py:243
  128.4 14.0 %collective-permute-start.20 = (bf16[2,8,128,128]{3,2,1,0:T(8,128)(2,1)S(1)}, bf16[2,8,128,128]{3,2,1,0:T(8,128)(2,1)S(1)}, u32[]{:S(2)}, u32[]{:S(2)}) collective-permute-start(bf16[2,8,128,128]{3,2,1,0:T(8,128)(2,1)S(1)} %get-tuple-element.73), channel_id=1, source_target_pairs={{0,8},{4,12},{8,0},{12,4},{16,24},{20,28},{24,16},{28,20},{1,9},{5... | collective-permute-start | bytes 1572872 | tf_op jit(solution)/shard_map/ppermute | solution.py:243
  130.3 13.9 %collective-permute-start.24 = (bf16[2,8,128,128]{3,2,1,0:T(8,128)(2,1)S(1)}, bf16[2,8,128,128]{3,2,1,0:T(8,128)(2,1)S(1)}, u32[]{:S(2)}, u32[]{:S(2)}) collective-permute-start(bf16[2,8,128,128]{3,2,1,0:T(8,128)(2,1)S(1)} %get-tuple-element.71), channel_id=1, source_target_pairs={{0,16},{4,20},{8,24},{12,28},{16,0},{20,4},{24,8},{28,12},{1,17},{... | collective-permute-start | bytes 1572872 | tf_op jit(solution)/shard_map/ppermute | solution.py:243
  132.5 1.4 collective-permute-start.21
  144.2 6.4 %collective-permute-start.26 = (bf16[128,512]{1,0:T(8,128)(2,1)S(1)}, bf16[128,512]{1,0:T(8,128)(2,1)S(1)}, u32[]{:S(2)}, u32[]{:S(2)}) collective-permute-start(bf16[128,512]{1,0:T(8,128)(2,1)S(1)} %convert_add_fusion.5), channel_id=1, source_target_pairs={{0,8},{4,12},{8,0},{12,4},{16,24},{20,28},{24,16},{28,20},{1,9},{5... | collective-permute-start | bytes 393224 | tf_op jit(solution)/shard_map/ppermute | solution.py:243
  145.8 10.0 %collective-permute-start.25 = (bf16[8,128,128]{2,1,0:T(8,128)(2,1)S(1)}, bf16[8,128,128]{2,1,0:T(8,128)(2,1)S(1)}, u32[]{:S(2)}, u32[]{:S(2)}) collective-permute-start(bf16[8,128,128]{2,1,0:T(8,128)(2,1)S(1)} %get-tuple-element.79), channel_id=1, source_target_pairs={{0,8},{4,12},{8,0},{12,4},{16,24},{20,28},{24,16},{28,20},{1,9},{5... | collective-permute-start | bytes 786440 | tf_op jit(solution)/shard_map/ppermute | solution.py:243
  150.6 5.0 %collective-permute-start.27 = (bf16[128,512]{1,0:T(8,128)(2,1)S(1)}, bf16[128,512]{1,0:T(8,128)(2,1)S(1)}, u32[]{:S(2)}, u32[]{:S(2)}) collective-permute-start(bf16[128,512]{1,0:T(8,128)(2,1)S(1)} %add_convert_fusion.12), channel_id=1, source_target_pairs={{0,16},{4,20},{8,24},{12,28},{16,0},{20,4},{24,8},{28,12},{1,17},{... | collective-permute-start | bytes 393224 | tf_op jit(solution)/shard_map/ppermute | solution.py:243
  152.6 6.4 %collective-permute-start.22 = (bf16[8,128,128]{2,1,0:T(8,128)(2,1)S(1)}, bf16[8,128,128]{2,1,0:T(8,128)(2,1)S(1)}, u32[]{:S(2)}, u32[]{:S(2)}) collective-permute-start(bf16[8,128,128]{2,1,0:T(8,128)(2,1)S(1)} %get-tuple-element.81), channel_id=1, source_target_pairs={{0,16},{4,20},{8,24},{12,28},{16,0},{20,4},{24,8},{28,12},{1,17},{... | collective-permute-start | bytes 786440 | tf_op jit(solution)/shard_map/ppermute | solution.py:243
  155.7 4.3 %collective-permute-start.28 = (f32[128,512]{1,0:T(8,128)S(1)}, f32[128,512]{1,0:T(8,128)S(1)}, u32[]{:S(2)}, u32[]{:S(2)}) collective-permute-start(f32[128,512]{1,0:T(8,128)S(1)} %convert_add_fusion.4), channel_id=1, source_target_pairs={{0,4},{4,0},{8,12},{12,8},{16,20},{20,16},{24,28},{28,24},{1,5},{5... | collective-permute-start | bytes 786440 | tf_op jit(solution)/shard_map/ppermute | solution.py:243

commit v8 on v7

--- a/solution.py
+++ b/solution.py
@@ -35,17 +35,18 @@
     lax.fori_loop(0, COPIES, piece, 0)
 
 
-def spread_kernel(first, cols_ref, me_ref, tiles_ref, vals_ref, *rest):
+def spread_kernel(first, pieces, cols_ref, me_ref, tiles_ref, *rest):
+    vals, rest = rest[:pieces], rest[pieces:]
     if first:
         mask_ref, *rest = rest
         outs, (mask_out, acc, held, sems, left_ref, mask_held) = rest[: 2 * GROUPS], rest[2 * GROUPS :]
         loads = [
-            pltpu.make_async_copy(vals_ref, left_ref, sems.at[COPIES]),
+            pltpu.make_async_copy(vals[0], left_ref, sems.at[COPIES]),
             pltpu.make_async_copy(mask_ref, mask_held, sems.at[COPIES + 1]),
         ]
         loads[0].start()
     else:
-        outs, (acc, held, sems) = rest[: 2 * GROUPS], rest[2 * GROUPS :]
+        outs, (acc, held, sems, left_ref) = rest[: 2 * GROUPS], rest[2 * GROUPS :]
     for i in range(COPIES):
         tile_copy(tiles_ref, held, sems, i).start()
     if first:
@@ -55,9 +56,13 @@
     me = me_ref[0]
     if first:
         loads[0].wait()
+    else:
+        for g in range(pieces):
+            count = vals[g].shape[0]
+            left_ref[g * count : (g + 1) * count] = vals[g][...]
 
     def one_row(r):
-        left = left_ref[r].astype(F32).T.astype(BF16) if first else vals_ref[r]
+        left = left_ref[r].astype(F32).T.astype(BF16) if first else left_ref[r]
         for k in range(0, per_row, 2):
             pair = jnp.concatenate([held[r, k], held[r, k + 1]], axis=1)
             both = jnp.dot(left, pair, preferred_element_type=F32)
@@ -81,7 +86,7 @@
 def spread(edge_tiles, block_cols, vals, me, rows, mask=None):
     blocks, _, size, _ = edge_tiles.shape
     first = mask is not None
-    feat = vals.shape[2] if first else vals.shape[1]
+    feat = vals[0].shape[2] if first else vals[0].shape[1]
     out = jax.ShapeDtypeStruct((rows // 2, blocks // GROUPS, feat, size), BF16)
     outs = [out] * (2 * GROUPS)
     scratch = [
@@ -92,12 +97,13 @@
     anywhere = pl.BlockSpec(memory_space=pl.ANY)
     if first:
         outs.append(jax.ShapeDtypeStruct((blocks, feat, size), BF16))
-        scratch += [pltpu.VMEM(v.shape, v.dtype) for v in (vals, mask)]
-        args, place = [vals, mask], anywhere
+        scratch += [pltpu.VMEM(v.shape, v.dtype) for v in (vals[0], mask)]
+        args, place = [vals[0], mask], anywhere
     else:
-        args, place = [vals], VMEM
-    return pl.pallas_call(
-        functools.partial(spread_kernel, first),
+        scratch.append(pltpu.VMEM((blocks, feat, size), BF16))
+        args, place = vals, VMEM
+    return pl.pallas_call(
+        functools.partial(spread_kernel, first, len(vals)),
         out_shape=outs,
         in_specs=[SMEM, SMEM, anywhere] + [place] * len(args),
         out_specs=[VMEM] * len(outs),
@@ -157,7 +163,7 @@
 def finish_kernel(last, *refs):
     parts, out_ref = refs[:-1], refs[-1]
     count = parts[0].shape[0]
-    for g in range(GROUPS):
+    for g in range(len(parts) // 2):
         for b in range(count):
             total = parts[2 * g][b].astype(F32) + parts[2 * g + 1][b].astype(F32)
             out_ref[g * count + b] = (total.T if last else total).astype(BF16)
@@ -167,7 +173,7 @@
     count, feat, size = parts[0].shape
     return pl.pallas_call(
         functools.partial(finish_kernel, last),
-        out_shape=jax.ShapeDtypeStruct((count * GROUPS,) + ((size, feat) if last else (feat, size)), BF16),
+        out_shape=jax.ShapeDtypeStruct((count * len(parts) // 2,) + ((size, feat) if last else (feat, size)), BF16),
         in_specs=[VMEM] * len(parts),
         out_specs=VMEM,
         compiler_params=PARAMS,
@@ -187,19 +193,13 @@
         place = jnp.bitwise_xor(col_ref[0], m)
         for b in range(blocks):
             whole_ref[place, :, b * size : (b + 1) * size] = shards[m][b]
-    half = blocks * size // 2
-    total = None
-    for h in range(2):
-        whole = jnp.concatenate([whole_ref[q, :, h * half : (h + 1) * half] for q in range(cols)], axis=0)
-        res = jnp.dot(weight_ref[...], whole, preferred_element_type=F32)
-        for i in range(blocks // 2):
-            b = h * (blocks // 2) + i
-            part = res[:, i * size : (i + 1) * size]
-            out_ref[b] = (part * mask_ref[b].astype(F32) if masked else part).astype(BF16)
-        side = jnp.concatenate([side_ref[h * (blocks // 2) + i] for i in range(blocks // 2)], axis=0)
-        term = jnp.dot(whole, side, preferred_element_type=F32)
-        total = term if total is None else total + term
-    grad_ref[...] = total
+    whole = jnp.concatenate([whole_ref[q] for q in range(cols)], axis=0)
+    res = jnp.dot(weight_ref[...], whole, preferred_element_type=F32)
+    for b in range(blocks):
+        part = res[:, b * size : (b + 1) * size]
+        out_ref[b] = (part * mask_ref[b].astype(F32) if masked else part).astype(BF16)
+    side = jnp.concatenate([side_ref[b] for b in range(blocks)], axis=0)
+    grad_ref[...] = jnp.dot(whole, side, preferred_element_type=F32)
 
 
 def dense(weight, shards, side, mask, col):
@@ -220,23 +220,24 @@
     )(col, *args)
 
 
-def weight_terms_kernel(me_ref, first_ref, second_ref, keep_ref, send_ref):
-    first, second = first_ref[...].T, second_ref[...].T
+def weight_terms_kernel(me_ref, *refs):
+    firsts, seconds, (keep_ref, send_ref) = refs[:GROUPS], refs[GROUPS : 2 * GROUPS], refs[2 * GROUPS :]
+    first, second = sum(r[...] for r in firsts).T, sum(r[...] for r in seconds).T
     even = jnp.bitwise_and(me_ref[0], 1) == 0
     keep_ref[...] = jnp.where(even, second, first)
     send_ref[...] = jnp.where(even, first, second).astype(BF16)
 
 
-def weight_terms(first, second, me):
-    shape = first.shape[::-1]
+def weight_terms(firsts, seconds, me):
+    shape = firsts[0].shape[::-1]
     return pl.pallas_call(
         weight_terms_kernel,
         out_shape=[jax.ShapeDtypeStruct(shape, F32), jax.ShapeDtypeStruct(shape, BF16)],
-        in_specs=[SMEM] + [VMEM] * 2,
+        in_specs=[SMEM] + [VMEM] * (2 * GROUPS),
         out_specs=[VMEM] * 2,
         compiler_params=PARAMS,
         name="weight_terms",
-    )(me, first, second)
+    )(me, *firsts, *seconds)
 
 
 def swap(value, mask, axis):
@@ -269,23 +270,21 @@
         keep, got = pieces[2 * g], swap(pieces[2 * g + 1], 1, "row")
         order = masks if g % 2 == 0 else masks[::-1]
         terms, beside = scatter_group(keep.reshape(lead + keep.shape[1:]), got.reshape(lead + got.shape[1:]), order, beside)
-        done += terms
+        done.append(terms)
     return done, beside
 
 
 def gather_columns(own, cols):
     if cols == 4:
-        far = swap(own, 3, "col")
-        return [own, swap(own, 1, "col"), swap(far, 1, "col"), far]
+        near, far = lax.optimization_barrier((swap(own, 1, "col"), swap(own, 3, "col")))
+        return [own, near, swap(far, 1, "col"), far]
     return [own] + [swap(own, m, "col") for m in range(1, cols)]
 
 
-def over_chips(value, rows):
-    mask = 2
-    while mask < rows:
+def over_chips(value, masks):
+    for mask in masks:
         value = value.astype(BF16)
         value = value.astype(F32) + swap(value, mask, "row").astype(F32)
-        mask *= 2
     return value
 
 
@@ -296,26 +295,47 @@
     me, col = lax.axis_index("row").astype(jnp.int32), lax.axis_index("col").astype(jnp.int32)
     me_at, col_at = me.reshape(1), col.reshape(1)
     size = edge_tiles.shape[2]
+    per = edge_tiles.shape[0] // GROUPS
+    chips = [1 << b for b in range(1, rows.bit_length() - 1)]
+    cut = lambda v, g: v[g * per : (g + 1) * per]
     blocked = lambda v: v.reshape(v.shape[0] // size, size, v.shape[1])
     after = lax.optimization_barrier
 
-    *pieces, mask = spread(edge_tiles, block_cols, blocked(grad_out), me_at, rows, blocked(relu_mask))
-    terms, _ = scatter(pieces, rows)
-    own, node_feats = after((finish(terms, False), blocked(node_feats)))
-    shards = gather_columns(own, cols)
-    parts = [node_feats] + [swap(node_feats, rel, "row") for rel in range(2, rows, 2)]
-    shards, parts = after((shards, parts))
-    delta, second = dense(weight_two, shards, blocked(hidden_act), mask, col_at)
-    delta, parts = after((delta, parts))
-    shards = gather_columns(delta, cols)
-    parts = [v for part in parts for v in (part, swap(part, 1, "row"))]
-    agg_feats = aggregate(edge_tiles, block_cols, parts, me_at)
-    spread_in, first = dense(weight_one, shards, agg_feats, None, col_at)
-    pieces = spread(edge_tiles, block_cols, spread_in, me_at, rows)
-    keep, send = weight_terms(first, second, me_at)
-    terms, value = scatter(pieces, rows, keep + swap(send, 1, "row").astype(F32))
-    out = finish(terms, True)
-    value = over_chips(value, rows)
+    parts = {0: blocked(node_feats)}
+    for rel in chips:
+        parts[rel] = swap(parts[0], rel, "row")
+    *pieces, mask = spread(edge_tiles, block_cols, [blocked(grad_out)], me_at, rows, blocked(relu_mask))
+    pieces, parts = after((pieces, parts))
+    terms, parts = scatter(pieces, rows, parts)
+    for rel in [0] + chips:
+        parts[rel + 1] = swap(parts[rel], 1, "row")
+    hidden = blocked(hidden_act)
+    owns = [finish(terms[g], False) for g in range(GROUPS)]
+    owns, parts = after((owns, parts))
+    for rel in range(2, rows, 2):
+        top = 1 << (rel.bit_length() - 1)
+        if rel not in parts:
+            parts[rel] = swap(parts[rel - top], top, "row")
+    deltas, seconds, inputs, firsts = [], [], [], []
+    for g in range(GROUPS):
+        delta, grad = dense(weight_two, gather_columns(owns[g], cols), cut(hidden, g), cut(mask, g), col_at)
+        deltas.append(delta)
+        seconds.append(grad)
+    deltas[-1], parts = after((deltas[-1], parts))
+    for rel in range(1, rows, 2):
+        if rel not in parts:
+            parts[rel] = swap(parts[rel - 1], 1, "row")
+    agg_feats = aggregate(edge_tiles, block_cols, [parts[rel] for rel in range(rows)], me_at)
+    for g in range(GROUPS):
+        out, grad = dense(weight_one, gather_columns(deltas[g], cols), cut(agg_feats, g), None, col_at)
+        inputs.append(out)
+        firsts.append(grad)
+    pieces = spread(edge_tiles, block_cols, inputs, me_at, rows)
+    keep, send = weight_terms(firsts, seconds, me_at)
+    value = over_chips(keep + swap(send, 1, "row").astype(F32), chips[:1])
+    terms, value = scatter(pieces, rows, value)
+    terms, value = after((terms, over_chips(value, chips[1:])))
+    out = finish([t for pair in terms for t in pair], True)
     other = swap(value, 1, "row")
     even = me % 2 == 0
     first_grad, second_grad = jnp.where(even, other, value), jnp.where(even, value, other)

time: 161 us -> 163 us (1.012)
  starting transfers between devices: 47 us -> 32.5 us
  waiting for transfers between devices: 81.2 us -> 90.5 us
  local copies, waits for them, and re-layouts: 2.8 us -> 8.26 us
    ppermute x29 -> x35, starting transfers between devices: 47 us -> 32.5 us  [swap(): lax.ppermute(value, axis, [(i, i ^ mask) for i in range(lax.axis_size(axi...]
    ppermute x29 -> x35, waiting for transfers between devices: 81.2 us -> 90.5 us  [swap(): lax.ppermute(value, axis, [(i, i ^ mask) for i in range(lax.axis_size(axi...]
    unnamed x18 -> x24, local copies, waits for them, and re-layouts: 2.8 us -> 7.08 us
    pallas_call x2 -> x4, Pallas kernels: 4.43 us -> 5.48 us  [dense(): pl.pallas_call(functools.partial(dense_kernel, cols, mask is not None), o...]
  transfers between devices with their start and end apart: 29 -> 35, of which waited for: 17 -> 23; matrix products, arithmetic and copies ran while one was open for 2% -> 2% of each run, Pallas kernels for 5% -> 12%
where the time goes in v8:
time: 163 us; the launch traced here: 162 us
  waiting for transfers between devices  90.5 us (56%)
  starting transfers between devices  32.5 us (20%)
  Pallas kernels  27 us (17%)
  local copies, waits for them, and re-layouts  8.26 us (5%)
  other arithmetic  3.09 us (2%)
    ppermute x35, waiting for transfers between devices, swap(): lax.ppermute(value, axis, [(i, i ^ mask) for i in range(lax.axis_size(axi...  90.5 us
    ppermute x35, starting transfers between devices, swap(): lax.ppermute(value, axis, [(i, i ^ mask) for i in range(lax.axis_size(axi...  32.5 us
    pallas_call x2, Pallas kernels, spread(): pl.pallas_call(functools.partial(spread_kernel, first, len(vals)), out_sh...  13.9 us
    unnamed x24, local copies, waits for them, and re-layouts  7.08 us
    pallas_call x1, Pallas kernels, aggregate(): pl.pallas_call(aggregate_kernel, out_shape=jax.ShapeDtypeStruct((blocks,...  6.28 us
    pallas_call x4, Pallas kernels, dense(): pl.pallas_call(functools.partial(dense_kernel, cols, mask is not None), o...  5.48 us
  transfers between devices with their start and end apart: 35, of which 23 were waited for; matrix products, arithmetic and copies ran while one was open for 2% of the time, Pallas kernels for 12%

profile of v8, /device:TPU:0, one launch (start us, length us, event | category | flops | bytes accessed | tf_op | source)
XLA Modules:
  0.0 162.3 jit_solution(12632749861641320703)
XLA Ops:
  0.6 3.0 %collective-permute-start = (bf16[16,128,128]{2,1,0:T(8,128)(2,1)}, bf16[16,128,128]{2,1,0:T(8,128)(2,1)S(1)}, u32[]{:S(2)}, u32[]{:S(2)}) collective-permute-start(bf16[16,128,128]{2,1,0:T(8,128)(2,1)} %bitcast.56), channel_id=1, source_target_pairs={{0,8},{4,12},{8,0},{12,4},{16,24},{20,28},{24,16},{28,20},{1,9},{5... | collective-permute-start | bytes 1572872 | tf_op jit(solution)/shard_map/ppermute | solution.py:244
  3.6 1.5 collective-permute-start.1
  5.2 1.0 copy-done.7
  6.2 0.7 copy-done.10
  6.9 7.1 %spread.2 = (bf16[4,8,128,128]{3,2,1,0:T(8,128)(2,1)S(1)}, bf16[4,8,128,128]{3,2,1,0:T(8,128)(2,1)S(1)}, bf16[4,8,128,128]{3,2,1,0:T(8,128)(2,1)S(1)}, bf16[4,8,...) custom-call(s32[16,20]{1,0:T(8,128)S(1)} %copy-done.10, s32[1]{0:T(128)} %bitcast.me_ref, ...), custom_call_target="tpu_custom_call" | custom-call | flops 1342177280 | bytes 30000000 | tf_op jit(solution)/shard_map/spread/pallas_call | solution.py:105
  14.1 1.7 %collective-permute-done.rest_2_ = bf16[16,128,128]{2,1,0:T(8,128)(2,1)S(1)} collective-permute-done((bf16[16,128,128]{2,1,0:T(8,128)(2,1)}, bf16[16,128,128]{2,1,0:T(8,128)(2,1)S(1)}, u32[]{:S(2)}, u32[]{:S(2)}) %collective-permute-start) | collective-permute-done | bytes 524320 | tf_op jit(solution)/shard_map/ppermute | solution.py:244
  15.8 1.5 collective-permute-done.1.rest_4_
  17.2 0.5 collective-permute-start.5
  17.8 2.1 %collective-permute-done.2 = bf16[4,8,128,128]{3,2,1,0:T(8,128)(2,1)S(1)} collective-permute-done((bf16[4,8,128,128]{3,2,1,0:T(8,128)(2,1)S(1)}, bf16[4,8,128,128]{3,2,1,0:T(8,128)(2,1)S(1)}, u32[]{:S(2)}, u32[]{:S(2)}) %collective-permute-start.2) | collective-permute-done | bytes 1048608 | tf_op jit(solution)/shard_map/ppermute | solution.py:244
  20.8 0.6 collective-permute-done.5
  21.9 1.6 collective-permute-start.6
  23.4 10.9 %collective-permute-done.3 = bf16[2,8,128,128]{3,2,1,0:T(8,128)(2,1)S(1)} collective-permute-done((bf16[2,8,128,128]{3,2,1,0:T(8,128)(2,1)S(1)}, bf16[2,8,128,128]{3,2,1,0:T(8,128)(2,1)S(1)}, u32[]{:S(2)}, u32[]{:S(2)}) %collective-permute-start.3) | collective-permute-done | bytes 524320 | tf_op jit(solution)/shard_map/ppermute | solution.py:244
  34.4 1.5 collective-permute-done.6
  36.6 0.8 collective-permute-start.7
  37.6 1.6 collective-permute-start.4
  39.1 6.2 %collective-permute-done.7.refs_1_ = bf16[8,128,128]{2,1,0:T(8,128)(2,1)S(1)} collective-permute-done((bf16[8,128,128]{2,1,0:T(8,128)(2,1)S(1)}, bf16[8,128,128]{2,1,0:T(8,128)(2,1)S(1)}, u32[]{:S(2)}, u32[]{:S(2)}) %collective-permute-start.7) | collective-permute-done | bytes 262176 | tf_op jit(solution)/shard_map/ppermute | solution.py:244
  45.4 0.6 collective-permute-done.4.refs_1_
  46.2 0.8 copy-done.1
  46.9 0.8 copy-done.3
  47.8 1.6 collective-permute-start.17
  49.3 2.5 %collective-permute-start.18 = (bf16[8,128,128]{2,1,0:T(8,128)(2,1)S(1)}, bf16[8,128,128]{2,1,0:T(8,128)(2,1)}, u32[]{:S(2)}, u32[]{:S(2)}) collective-permute-start(bf16[8,128,128]{2,1,0:T(8,128)(2,1)S(1)} %finish.4.rest_0_), channel_id=1, source_target_pairs={{0,3},{1,2},{2,1},{3,0},{4,7},{5,6},{6,5},{7,4},{8,11},{9,10},{10,... | collective-permute-start | bytes 786440 | tf_op jit(solution)/shard_map/ppermute | solution.py:244
  51.8 1.5 collective-permute-start.20
  53.3 0.7 collective-permute-start.11
  54.0 0.9 collective-permute-start.12
  54.9 1.7 %collective-permute-done.17.rest_1_ = bf16[8,128,128]{2,1,0:T(8,128)(2,1)S(1)} collective-permute-done((bf16[8,128,128]{2,1,0:T(8,128)(2,1)S(1)}, bf16[8,128,128]{2,1,0:T(8,128)(2,1)S(1)}, u32[]{:S(2)}, u32[]{:S(2)}) %collective-permute-start.17) | collective-permute-done | bytes 262176 | tf_op jit(solution)/shard_map/ppermute | solution.py:244
  56.6 0.7 copy-done.8
  57.3 7.5 %collective-permute-done.18.rest_3_ = bf16[8,128,128]{2,1,0:T(8,128)(2,1)} collective-permute-done((bf16[8,128,128]{2,1,0:T(8,128)(2,1)S(1)}, bf16[8,128,128]{2,1,0:T(8,128)(2,1)}, u32[]{:S(2)}, u32[]{:S(2)}) %collective-permute-start.18) | collective-permute-done | bytes 262176 | tf_op jit(solution)/shard_map/ppermute | solution.py:244
  64.8 0.6 collective-permute-start.19
  65.5 1.1 fusion.16
  66.6 1.7 %collective-permute-done.11.rest_1_ = bf16[8,128,128]{2,1,0:T(8,128)(2,1)} collective-permute-done((bf16[8,128,128]{2,1,0:T(8,128)(2,1)S(1)}, bf16[8,128,128]{2,1,0:T(8,128)(2,1)}, u32[]{:S(2)}, u32[]{:S(2)}) %collective-permute-start.11) | collective-permute-done | bytes 262176 | tf_op jit(solution)/shard_map/ppermute | solution.py:244
  68.3 7.7 %collective-permute-done.12.rest_3_ = bf16[8,128,128]{2,1,0:T(8,128)(2,1)} collective-permute-done((bf16[8,128,128]{2,1,0:T(8,128)(2,1)S(1)}, bf16[8,128,128]{2,1,0:T(8,128)(2,1)}, u32[]{:S(2)}, u32[]{:S(2)}) %collective-permute-start.12) | collective-permute-done | bytes 262176 | tf_op jit(solution)/shard_map/ppermute | solution.py:244
  76.0 3.2 %collective-permute-done.19.rest_2_ = bf16[8,128,128]{2,1,0:T(8,128)(2,1)} collective-permute-done((bf16[8,128,128]{2,1,0:T(8,128)(2,1)}, bf16[8,128,128]{2,1,0:T(8,128)(2,1)}, u32[]{:S(2)}, u32[]{:S(2)}) %collective-permute-start.19) | collective-permute-done | bytes 262176 | tf_op jit(solution)/shard_map/ppermute | solution.py:244
  79.2 0.9 copy-done.9
  80.2 1.9 %dense.5 = (bf16[8,128,128]{2,1,0:T(8,128)(2,1)S(1)}, f32[512,128]{1,0:T(8,128)S(1)}) custom-call(s32[1]{0:T(128)} %bitcast.1.col_ref, bf16[128,512]{1,0:T(8,128)(2,1)S(1)} %copy-done.5, bf16[8,128,128]{2,1,0:T(8,128)(2,1)S(1)} %finish.4.rest_0_, bf16[8,128,128]{2,1,0:T(8,128)(2,1)S(1)} %copy-done.9, bf16[8,128,128]{2,1,0:T(8,128)(2,1)} %collective-permute-done.19.rest_2_, ...), custom_call_target="tpu_custom_call" | custom-call | tf_op jit(solution)/shard_map/dense/pallas_call | solution.py:209
  82.1 2.1 %collective-permute-start.22 = (bf16[8,128,128]{2,1,0:T(8,128)(2,1)S(1)}, bf16[8,128,128]{2,1,0:T(8,128)(2,1)S(1)}, u32[]{:S(2)}, u32[]{:S(2)}) collective-permute-start(bf16[8,128,128]{2,1,0:T(8,128)(2,1)S(1)} %get-tuple-element.114.rest_0_), channel_id=1, source_target_pairs={{0,1},{1,0},{2,3},{3,2},{4,5},{5,4},{6,7},{7,6},{8,9},{9,8},{10,11... | collective-permute-start | bytes 786440 | tf_op jit(solution)/shard_map/ppermute | solution.py:244
  84.2 2.4 %collective-permute-start.23 = (bf16[8,128,128]{2,1,0:T(8,128)(2,1)S(1)}, bf16[8,128,128]{2,1,0:T(8,128)(2,1)S(1)}, u32[]{:S(2)}, u32[]{:S(2)}) collective-permute-start(bf16[8,128,128]{2,1,0:T(8,128)(2,1)S(1)} %get-tuple-element.114.rest_0_), channel_id=1, source_target_pairs={{0,3},{1,2},{2,1},{3,0},{4,7},{5,6},{6,5},{7,4},{8,11},{9,10},{10,... | collective-permute-start | bytes 786440 | tf_op jit(solution)/shard_map/ppermute | solution.py:244
  86.7 1.9 %dense.4 = (bf16[8,128,128]{2,1,0:T(8,128)(2,1)S(1)}, f32[512,128]{1,0:T(8,128)S(1)}) custom-call(s32[1]{0:T(128)} %bitcast.1.col_ref, bf16[128,512]{1,0:T(8,128)(2,1)S(1)} %copy-done.5, bf16[8,128,128]{2,1,0:T(8,128)(2,1)S(1)} %finish.3.rest_0_, bf16[8,128,128]{2,1,0:T(8,128)(2,1)} %collective-permute-done.11.rest_1_, ...), custom_call_target="tpu_custom_call" | custom-call | tf_op jit(solution)/shard_map/dense/pallas_call | solution.py:209
  88.6 0.7 collective-permute-start.14
  89.3 0.9 collective-permute-start.15
  90.2 1.0 collective-permute-done.22.rest_1_
  91.1 8.3 %collective-permute-done.23.rest_3_ = bf16[8,128,128]{2,1,0:T(8,128)(2,1)S(1)} collective-permute-done((bf16[8,128,128]{2,1,0:T(8,128)(2,1)S(1)}, bf16[8,128,128]{2,1,0:T(8,128)(2,1)S(1)}, u32[]{:S(2)}, u32[]{:S(2)}) %collective-permute-start.23) | collective-permute-done | bytes 262176 | tf_op jit(solution)/shard_map/ppermute | solution.py:244
  99.4 0.6 collective-permute-start.24
  100.0 3.5 %collective-permute-done.14.rest_1_ = bf16[8,128,128]{2,1,0:T(8,128)(2,1)S(1)} collective-permute-done((bf16[8,128,128]{2,1,0:T(8,128)(2,1)S(1)}, bf16[8,128,128]{2,1,0:T(8,128)(2,1)S(1)}, u32[]{:S(2)}, u32[]{:S(2)}) %collective-permute-start.14) | collective-permute-done | bytes 262176 | tf_op jit(solution)/shard_map/ppermute | solution.py:244
  103.5 7.2 %collective-permute-done.15.rest_3_ = bf16[8,128,128]{2,1,0:T(8,128)(2,1)S(1)} collective-permute-done((bf16[8,128,128]{2,1,0:T(8,128)(2,1)S(1)}, bf16[8,128,128]{2,1,0:T(8,128)(2,1)S(1)}, u32[]{:S(2)}, u32[]{:S(2)}) %collective-permute-start.15) | collective-permute-done | bytes 262176 | tf_op jit(solution)/shard_map/ppermute | solution.py:244
  110.7 1.0 copy-done.2
  111.7 1.0 copy-done.4
  112.8 6.3 %aggregate.1 = bf16[16,128,128]{2,1,0:T(8,128)(2,1)S(1)} custom-call(s32[16,20]{1,0:T(8,128)S(1)} %copy-done.11, s32[1]{0:T(128)} %bitcast.me_ref, bf16[16,20,128,128]{3,2,1,0:T(8,128)(2,1)} %tiles_ref.5, bf16[16,128,128]{2,1,0:T(8,128)(2,1)S(1)} %bitcast.59, bf16[16,128,128]{2,1,0:T(8,128)(2,1)S(1)} %copy-done.2, ...), custom_call_target="tpu_custom_call" | custom-call | flops 1342177280 | bytes 30000000 | tf_op jit(solution)/shard_map/aggregate/pallas_call | solution.py:147
  119.1 0.9 dense.7
  120.0 0.9 dense.6
  120.9 6.8 %spread.3 = (bf16[4,8,128,128]{3,2,1,0:T(8,128)(2,1)S(1)}, bf16[4,8,128,128]{3,2,1,0:T(8,128)(2,1)S(1)}, bf16[4,8,128,128]{3,2,1,0:T(8,128)(2,1)S(1)}, bf16[4,8,128,128]{3,2,1,0:T(8,128)(2,1)S(1)}) custom-call(s32[16,20]{1,0:T(8,128)S(1)} %copy-done.11, s32[1]{0:T(128)} %bitcast.me_ref, bf16[16,20,128,128]{3,2,1,0:T(8,128)(2,1)} %tiles_ref.5, ...), custom_call_target="tpu_custom_call" | custom-call | flops 1342177280 | bytes 30000000 | tf_op jit(solution)/shard_map/spread/pallas_call | solution.py:105
  128.6 1.8 %collective-permute-done.30 = bf16[4,8,128,128]{3,2,1,0:T(8,128)(2,1)S(1)} collective-permute-done((bf16[4,8,128,128]{3,2,1,0:T(8,128)(2,1)S(1)}, bf16[4,8,128,128]{3,2,1,0:T(8,128)(2,1)S(1)}, u32[]{:S(2)}, u32[]{:S(2)}) %collective-permute-start.30) | collective-permute-done | bytes 1048608 | tf_op jit(solution)/shard_map/ppermute | solution.py:244
  130.8 1.6 collective-permute-start.31
  132.7 1.3 collective-permute-start.26
  134.0 0.9 collective-permute-start.28
  134.9 14.4 %collective-permute-done.28 = bf16[128,512]{1,0:T(8,128)(2,1)S(1)} collective-permute-done((bf16[128,512]{1,0:T(8,128)(2,1)S(1)}, bf16[128,512]{1,0:T(8,128)(2,1)S(1)}, u32[]{:S(2)}, u32[]{:S(2)}) %collective-permute-start.28) | collective-permute-done | bytes 131104 | tf_op jit(solution)/shard_map/ppermute | solution.py:244
  149.3 1.4 collective-permute-start.33
  150.9 1.3 collective-permute-start.32
  152.3 0.7 collective-permute-start.29
  153.1 1.9 %collective-permute-done.33 = bf16[128,512]{1,0:T(8,128)(2,1)S(1)} collective-permute-done((bf16[128,512]{1,0:T(8,128)(2,1)S(1)}, bf16[128,512]{1,0:T(8,128)(2,1)S(1)}, u32[]{:S(2)}, u32[]{:S(2)}) %collective-permute-start.33) | collective-permute-done | bytes 131104 | tf_op jit(solution)/shard_map/ppermute | solution.py:244
  155.0 3.1 %collective-permute-done.32.refs_3_ = bf16[8,128,128]{2,1,0:T(8,128)(2,1)S(1)} collective-permute-done((bf16[8,128,128]{2,1,0:T(8,128)(2,1)S(1)}, bf16[8,128,128]{2,1,0:T(8,128)(2,1)S(1)}, u32[]{:S(2)}, u32[]{:S(2)}) %collective-permute-start.32) | collective-permute-done | bytes 262176 | tf_op jit(solution)/shard_map/ppermute | solution.py:244
  158.2 1.8 %collective-permute-done.29.refs_1_ = bf16[8,128,128]{2,1,0:T(8,128)(2,1)S(1)} collective-permute-done((bf16[8,128,128]{2,1,0:T(8,128)(2,1)S(1)}, bf16[8,128,128]{2,1,0:T(8,128)(2,1)S(1)}, u32[]{:S(2)}, u32[]{:S(2)}) %collective-permute-start.29) | collective-permute-done | bytes 262176 | tf_op jit(solution)/shard_map/ppermute | solution.py:244
  160.0 1.0 finish.5
  161.0 0.5 collective-permute-done.34
  161.5 0.8 broadcast_select_fusion
  (56 shorter events, 4.5 us)
Async XLA Ops:
  0.6 35.3 %copy-start = (bf16[2048,128]{1,0:T(8,128)(2,1)S(1)}, bf16[2048,128]{1,0:T(8,128)(2,1)}, u32[]{:S(2)}) copy-start(bf16[2048,128]{1,0:T(8,128)(2,1)} %param.8) | copy-start | bytes 1572868
  0.6 15.1 %collective-permute-start = (bf16[16,128,128]{2,1,0:T(8,128)(2,1)}, bf16[16,128,128]{2,1,0:T(8,128)(2,1)S(1)}, u32[]{:S(2)}, u32[]{:S(2)}) collective-permute-start(bf16[16,128,128]{2,1,0:T(8,128)(2,1)} %bitcast.56), channel_id=1, source_target_pairs={{0,8},{4,12},{8,0},{12,4},{16,24},{20,28},{24,16},{28,20},{1,9},{5... | collective-permute-start | bytes 1572872 | tf_op jit(solution)/shard_map/ppermute | solution.py:244
  3.6 13.6 %collective-permute-start.1 = (bf16[16,128,128]{2,1,0:T(8,128)(2,1)}, bf16[16,128,128]{2,1,0:T(8,128)(2,1)S(1)}, u32[]{:S(2)}, u32[]{:S(2)}) collective-permute-start(bf16[16,128,128]{2,1,0:T(8,128)(2,1)} %bitcast.57), channel_id=1, source_target_pairs={{0,16},{4,20},{8,24},{12,28},{16,0},{20,4},{24,8},{28,12},{1,17},{... | collective-permute-start | bytes 1572872 | tf_op jit(solution)/shard_map/ppermute | solution.py:244
  5.2 1.0 copy-start.7
  6.2 0.7 copy-start.10
  6.9 72.3 %copy-start.5 = (bf16[128,512]{1,0:T(8,128)(2,1)S(1)}, bf16[128,512]{1,0:T(8,128)(2,1)}, u32[]{:S(2)}) copy-start(bf16[128,512]{1,0:T(8,128)(2,1)} %weight_ref.5) | copy-start | bytes 393220
  14.1 96.6 %copy-start.11 = (s32[16,20]{1,0:T(8,128)S(1)}, s32[16,20]{1,0:T(8,128)}, u32[]{:S(2)}) copy-start(s32[16,20]{1,0:T(8,128)} %cols_ref.5) | copy-start | bytes 3844
  17.2 2.7 %collective-permute-start.2 = (bf16[4,8,128,128]{3,2,1,0:T(8,128)(2,1)S(1)}, bf16[4,8,128,128]{3,2,1,0:T(8,128)(2,1)S(1)}, u32[]{:S(2)}, u32[]{:S(2)}) collective-permute-start(bf16[4,8,128,128]{3,2,1,0:T(8,128)(2,1)S(1)} %get-tuple-element.75), channel_id=1, source_target_pairs={{0,4},{4,0},{8,12},{12,8},{16,20},{20,16},{24,28},{28,24},{1,5},{5... | collective-permute-start | bytes 3145736 | tf_op jit(solution)/shard_map/ppermute | solution.py:244
  17.2 4.2 %collective-permute-start.5 = (bf16[4,8,128,128]{3,2,1,0:T(8,128)(2,1)S(1)}, bf16[4,8,128,128]{3,2,1,0:T(8,128)(2,1)S(1)}, u32[]{:S(2)}, u32[]{:S(2)}) collective-permute-start(bf16[4,8,128,128]{3,2,1,0:T(8,128)(2,1)S(1)} %get-tuple-element.81), channel_id=1, source_target_pairs={{0,4},{4,0},{8,12},{12,8},{16,20},{20,16},{24,28},{28,24},{1,5},{5... | collective-permute-start | bytes 3145736 | tf_op jit(solution)/shard_map/ppermute | solution.py:244
  20.4 14.0 %collective-permute-start.3 = (bf16[2,8,128,128]{3,2,1,0:T(8,128)(2,1)S(1)}, bf16[2,8,128,128]{3,2,1,0:T(8,128)(2,1)S(1)}, u32[]{:S(2)}, u32[]{:S(2)}) collective-permute-start(bf16[2,8,128,128]{3,2,1,0:T(8,128)(2,1)S(1)} %get-tuple-element.143), channel_id=1, source_target_pairs={{0,8},{4,12},{8,0},{12,4},{16,24},{20,28},{24,16},{28,20},{1,9},{5... | collective-permute-start | bytes 1572872 | tf_op jit(solution)/shard_map/ppermute | solution.py:244
  21.9 14.0 %collective-permute-start.6 = (bf16[2,8,128,128]{3,2,1,0:T(8,128)(2,1)S(1)}, bf16[2,8,128,128]{3,2,1,0:T(8,128)(2,1)S(1)}, u32[]{:S(2)}, u32[]{:S(2)}) collective-permute-start(bf16[2,8,128,128]{3,2,1,0:T(8,128)(2,1)S(1)} %get-tuple-element.141), channel_id=1, source_target_pairs={{0,16},{4,20},{8,24},{12,28},{16,0},{20,4},{24,8},{28,12},{1,17},{... | collective-permute-start | bytes 1572872 | tf_op jit(solution)/shard_map/ppermute | solution.py:244
  35.9 10.2 %collective-permute-start.10 = (bf16[16,128,128]{2,1,0:T(8,128)(2,1)S(1)}, bf16[16,128,128]{2,1,0:T(8,128)(2,1)S(1)}, u32[]{:S(2)}, u32[]{:S(2)}) collective-permute-start(bf16[16,128,128]{2,1,0:T(8,128)(2,1)S(1)} %collective-permute-done.1.rest_4_), channel_id=1, source_target_pairs={{0,4},{4,0},{8,12},{12,8},{16,20},{20,16},{24,28},{28,24},{1,5},{5... | collective-permute-start | bytes 1572872 | tf_op jit(solution)/shard_map/ppermute | solution.py:244
  35.9 10.2 %collective-permute-start.8 = (bf16[16,128,128]{2,1,0:T(8,128)(2,1)S(1)}, bf16[16,128,128]{2,1,0:T(8,128)(2,1)S(1)}, u32[]{:S(2)}, u32[]{:S(2)}) collective-permute-start(bf16[16,128,128]{2,1,0:T(8,128)(2,1)S(1)} %bitcast.58), channel_id=1, source_target_pairs={{0,4},{4,0},{8,12},{12,8},{16,20},{20,16},{24,28},{28,24},{1,5},{5... | collective-permute-start | bytes 1572872 | tf_op jit(solution)/shard_map/ppermute | solution.py:244
  36.4 10.5 %collective-permute-start.9 = (bf16[16,128,128]{2,1,0:T(8,128)(2,1)S(1)}, bf16[16,128,128]{2,1,0:T(8,128)(2,1)S(1)}, u32[]{:S(2)}, u32[]{:S(2)}) collective-permute-start(bf16[16,128,128]{2,1,0:T(8,128)(2,1)S(1)} %collective-permute-done.rest_2_), channel_id=1, source_target_pairs={{0,4},{4,0},{8,12},{12,8},{16,20},{20,16},{24,28},{28,24},{1,5},{5... | collective-permute-start | bytes 1572872 | tf_op jit(solution)/shard_map/ppermute | solution.py:244
  36.6 8.8 %collective-permute-start.7 = (bf16[8,128,128]{2,1,0:T(8,128)(2,1)S(1)}, bf16[8,128,128]{2,1,0:T(8,128)(2,1)S(1)}, u32[]{:S(2)}, u32[]{:S(2)}) collective-permute-start(bf16[8,128,128]{2,1,0:T(8,128)(2,1)S(1)} %get-tuple-element.149), channel_id=1, source_target_pairs={{0,8},{4,12},{8,0},{12,4},{16,24},{20,28},{24,16},{28,20},{1,9},{5... | collective-permute-start | bytes 786440 | tf_op jit(solution)/shard_map/ppermute | solution.py:244
  37.6 8.5 %collective-permute-start.4 = (bf16[8,128,128]{2,1,0:T(8,128)(2,1)S(1)}, bf16[8,128,128]{2,1,0:T(8,128)(2,1)S(1)}, u32[]{:S(2)}, u32[]{:S(2)}) collective-permute-start(bf16[8,128,128]{2,1,0:T(8,128)(2,1)S(1)} %get-tuple-element.151), channel_id=1, source_target_pairs={{0,16},{4,20},{8,24},{12,28},{16,0},{20,4},{24,8},{28,12},{1,17},{... | collective-permute-start | bytes 786440 | tf_op jit(solution)/shard_map/ppermute | solution.py:244
  46.1 0.8 copy-start.1
  46.9 0.8 copy-start.3
  47.8 8.8 %collective-permute-start.17 = (bf16[8,128,128]{2,1,0:T(8,128)(2,1)S(1)}, bf16[8,128,128]{2,1,0:T(8,128)(2,1)S(1)}, u32[]{:S(2)}, u32[]{:S(2)}) collective-permute-start(bf16[8,128,128]{2,1,0:T(8,128)(2,1)S(1)} %finish.4.rest_0_), channel_id=1, source_target_pairs={{0,1},{1,0},{2,3},{3,2},{4,5},{5,4},{6,7},{7,6},{8,9},{9,8},{10,11... | collective-permute-start | bytes 786440 | tf_op jit(solution)/shard_map/ppermute | solution.py:244
  49.3 15.5 %collective-permute-start.18 = (bf16[8,128,128]{2,1,0:T(8,128)(2,1)S(1)}, bf16[8,128,128]{2,1,0:T(8,128)(2,1)}, u32[]{:S(2)}, u32[]{:S(2)}) collective-permute-start(bf16[8,128,128]{2,1,0:T(8,128)(2,1)S(1)} %finish.4.rest_0_), channel_id=1, source_target_pairs={{0,3},{1,2},{2,1},{3,0},{4,7},{5,6},{6,5},{7,4},{8,11},{9,10},{10,... | collective-permute-start | bytes 786440 | tf_op jit(solution)/shard_map/ppermute | solution.py:244
  51.8 30.3 %collective-permute-start.20 = (bf16[16,128,128]{2,1,0:T(8,128)(2,1)S(1)}, bf16[16,128,128]{2,1,0:T(8,128)(2,1)}, u32[]{:S(2)}, u32[]{:S(2)}) collective-permute-start(bf16[16,128,128]{2,1,0:T(8,128)(2,1)S(1)} %collective-permute-done.rest_2_), channel_id=1, source_target_pairs={{0,16},{4,20},{8,24},{12,28},{16,0},{20,4},{24,8},{28,12},{1,17},{... | collective-permute-start | bytes 1572872 | tf_op jit(solution)/shard_map/ppermute | solution.py:244
  53.3 15.0 %collective-permute-start.11 = (bf16[8,128,128]{2,1,0:T(8,128)(2,1)S(1)}, bf16[8,128,128]{2,1,0:T(8,128)(2,1)}, u32[]{:S(2)}, u32[]{:S(2)}) collective-permute-start(bf16[8,128,128]{2,1,0:T(8,128)(2,1)S(1)} %finish.3.rest_0_), channel_id=1, source_target_pairs={{0,1},{1,0},{2,3},{3,2},{4,5},{5,4},{6,7},{7,6},{8,9},{9,8},{10,11... | collective-permute-start | bytes 786440 | tf_op jit(solution)/shard_map/ppermute | solution.py:244
  54.0 22.0 %collective-permute-start.12 = (bf16[8,128,128]{2,1,0:T(8,128)(2,1)S(1)}, bf16[8,128,128]{2,1,0:T(8,128)(2,1)}, u32[]{:S(2)}, u32[]{:S(2)}) collective-permute-start(bf16[8,128,128]{2,1,0:T(8,128)(2,1)S(1)} %finish.3.rest_0_), channel_id=1, source_target_pairs={{0,3},{1,2},{2,1},{3,0},{4,7},{5,6},{6,5},{7,4},{8,11},{9,10},{10,... | collective-permute-start | bytes 786440 | tf_op jit(solution)/shard_map/ppermute | solution.py:244
  56.6 0.7 copy-start.8
  64.8 14.4 %collective-permute-start.19 = (bf16[8,128,128]{2,1,0:T(8,128)(2,1)}, bf16[8,128,128]{2,1,0:T(8,128)(2,1)}, u32[]{:S(2)}, u32[]{:S(2)}) collective-permute-start(bf16[8,128,128]{2,1,0:T(8,128)(2,1)} %collective-permute-done.18.rest_3_), channel_id=1, source_target_pairs={{0,1},{1,0},{2,3},{3,2},{4,5},{5,4},{6,7},{7,6},{8,9},{9,8},{10,11... | collective-permute-start | bytes 786440 | tf_op jit(solution)/shard_map/ppermute | solution.py:244
  65.5 53.7 %copy-start.6 = (bf16[128,512]{1,0:T(8,128)(2,1)S(1)}, bf16[128,512]{1,0:T(8,128)(2,1)}, u32[]{:S(2)}) copy-start(bf16[128,512]{1,0:T(8,128)(2,1)} %weight_ref.7) | copy-start | bytes 393220
  76.0 10.6 %collective-permute-start.13 = (bf16[8,128,128]{2,1,0:T(8,128)(2,1)}, bf16[8,128,128]{2,1,0:T(8,128)(2,1)S(1)}, u32[]{:S(2)}, u32[]{:S(2)}) collective-permute-start(bf16[8,128,128]{2,1,0:T(8,128)(2,1)} %collective-permute-done.12.rest_3_), channel_id=1, source_target_pairs={{0,1},{1,0},{2,3},{3,2},{4,5},{5,4},{6,7},{7,6},{8,9},{9,8},{10,11... | collective-permute-start | bytes 786440 | tf_op jit(solution)/shard_map/ppermute | solution.py:244
  79.2 1.0 copy-start.9
  82.1 28.6 %collective-permute-start.21 = (bf16[16,128,128]{2,1,0:T(8,128)(2,1)}, bf16[16,128,128]{2,1,0:T(8,128)(2,1)S(1)}, u32[]{:S(2)}, u32[]{:S(2)}) collective-permute-start(bf16[16,128,128]{2,1,0:T(8,128)(2,1)} %collective-permute-done.20.rest_6_), channel_id=1, source_target_pairs={{0,4},{4,0},{8,12},{12,8},{16,20},{20,16},{24,28},{28,24},{1,5},{5... | collective-permute-start | bytes 1572872 | tf_op jit(solution)/shard_map/ppermute | solution.py:244
  82.1 9.0 %collective-permute-start.22 = (bf16[8,128,128]{2,1,0:T(8,128)(2,1)S(1)}, bf16[8,128,128]{2,1,0:T(8,128)(2,1)S(1)}, u32[]{:S(2)}, u32[]{:S(2)}) collective-permute-start(bf16[8,128,128]{2,1,0:T(8,128)(2,1)S(1)} %get-tuple-element.114.rest_0_), channel_id=1, source_target_pairs={{0,1},{1,0},{2,3},{3,2},{4,5},{5,4},{6,7},{7,6},{8,9},{9,8},{10,11... | collective-permute-start | bytes 786440 | tf_op jit(solution)/shard_map/ppermute | solution.py:244
  84.2 15.2 %collective-permute-start.23 = (bf16[8,128,128]{2,1,0:T(8,128)(2,1)S(1)}, bf16[8,128,128]{2,1,0:T(8,128)(2,1)S(1)}, u32[]{:S(2)}, u32[]{:S(2)}) collective-permute-start(bf16[8,128,128]{2,1,0:T(8,128)(2,1)S(1)} %get-tuple-element.114.rest_0_), channel_id=1, source_target_pairs={{0,3},{1,2},{2,1},{3,0},{4,7},{5,6},{6,5},{7,4},{8,11},{9,10},{10,... | collective-permute-start | bytes 786440 | tf_op jit(solution)/shard_map/ppermute | solution.py:244
  88.6 14.9 %collective-permute-start.14 = (bf16[8,128,128]{2,1,0:T(8,128)(2,1)S(1)}, bf16[8,128,128]{2,1,0:T(8,128)(2,1)S(1)}, u32[]{:S(2)}, u32[]{:S(2)}) collective-permute-start(bf16[8,128,128]{2,1,0:T(8,128)(2,1)S(1)} %get-tuple-element.93.rest_0_), channel_id=1, source_target_pairs={{0,1},{1,0},{2,3},{3,2},{4,5},{5,4},{6,7},{7,6},{8,9},{9,8},{10,11... | collective-permute-start | bytes 786440 | tf_op jit(solution)/shard_map/ppermute | solution.py:244
  89.3 21.4 %collective-permute-start.15 = (bf16[8,128,128]{2,1,0:T(8,128)(2,1)S(1)}, bf16[8,128,128]{2,1,0:T(8,128)(2,1)S(1)}, u32[]{:S(2)}, u32[]{:S(2)}) collective-permute-start(bf16[8,128,128]{2,1,0:T(8,128)(2,1)S(1)} %get-tuple-element.93.rest_0_), channel_id=1, source_target_pairs={{0,3},{1,2},{2,1},{3,0},{4,7},{5,6},{6,5},{7,4},{8,11},{9,10},{10,... | collective-permute-start | bytes 786440 | tf_op jit(solution)/shard_map/ppermute | solution.py:244
  99.4 19.7 %collective-permute-start.24 = (bf16[8,128,128]{2,1,0:T(8,128)(2,1)S(1)}, bf16[8,128,128]{2,1,0:T(8,128)(2,1)S(1)}, u32[]{:S(2)}, u32[]{:S(2)}) collective-permute-start(bf16[8,128,128]{2,1,0:T(8,128)(2,1)S(1)} %collective-permute-done.23.rest_3_), channel_id=1, source_target_pairs={{0,1},{1,0},{2,3},{3,2},{4,5},{5,4},{6,7},{7,6},{8,9},{9,8},{10,11... | collective-permute-start | bytes 786440 | tf_op jit(solution)/shard_map/ppermute | solution.py:244
  110.7 9.3 %collective-permute-start.16 = (bf16[8,128,128]{2,1,0:T(8,128)(2,1)S(1)}, bf16[8,128,128]{2,1,0:T(8,128)(2,1)S(1)}, u32[]{:S(2)}, u32[]{:S(2)}) collective-permute-start(bf16[8,128,128]{2,1,0:T(8,128)(2,1)S(1)} %collective-permute-done.15.rest_3_), channel_id=1, source_target_pairs={{0,1},{1,0},{2,3},{3,2},{4,5},{5,4},{6,7},{7,6},{8,9},{9,8},{10,11... | collective-permute-start | bytes 786440 | tf_op jit(solution)/shard_map/ppermute | solution.py:244
  110.7 1.0 copy-start.2
  111.7 1.0 copy-start.4
  127.7 2.7 %collective-permute-start.30 = (bf16[4,8,128,128]{3,2,1,0:T(8,128)(2,1)S(1)}, bf16[4,8,128,128]{3,2,1,0:T(8,128)(2,1)S(1)}, u32[]{:S(2)}, u32[]{:S(2)}) collective-permute-start(bf16[4,8,128,128]{3,2,1,0:T(8,128)(2,1)S(1)} %get-tuple-element.128), channel_id=1, source_target_pairs={{0,4},{4,0},{8,12},{12,8},{16,20},{20,16},{24,28},{28,24},{1,5},{5... | collective-permute-start | bytes 3145736 | tf_op jit(solution)/shard_map/ppermute | solution.py:244
  127.7 4.6 %collective-permute-start.25 = (bf16[4,8,128,128]{3,2,1,0:T(8,128)(2,1)S(1)}, bf16[4,8,128,128]{3,2,1,0:T(8,128)(2,1)S(1)}, u32[]{:S(2)}, u32[]{:S(2)}) collective-permute-start(bf16[4,8,128,128]{3,2,1,0:T(8,128)(2,1)S(1)} %get-tuple-element.119), channel_id=1, source_target_pairs={{0,4},{4,0},{8,12},{12,8},{16,20},{20,16},{24,28},{28,24},{1,5},{5... | collective-permute-start | bytes 3145736 | tf_op jit(solution)/shard_map/ppermute | solution.py:244
  128.5 5.5 %collective-permute-start.27 = (bf16[128,512]{1,0:T(8,128)(2,1)S(1)}, bf16[128,512]{1,0:T(8,128)(2,1)S(1)}, u32[]{:S(2)}, u32[]{:S(2)}) collective-permute-start(bf16[128,512]{1,0:T(8,128)(2,1)S(1)} %get-tuple-element.125), channel_id=1, source_target_pairs={{0,4},{4,0},{8,12},{12,8},{16,20},{20,16},{24,28},{28,24},{1,5},{5... | collective-permute-start | bytes 393224 | tf_op jit(solution)/shard_map/ppermute | solution.py:244
  130.8 18.5 %collective-permute-start.31 = (bf16[2,8,128,128]{3,2,1,0:T(8,128)(2,1)S(1)}, bf16[2,8,128,128]{3,2,1,0:T(8,128)(2,1)S(1)}, u32[]{:S(2)}, u32[]{:S(2)}) collective-permute-start(bf16[2,8,128,128]{3,2,1,0:T(8,128)(2,1)S(1)} %get-tuple-element.137), channel_id=1, source_target_pairs={{0,16},{4,20},{8,24},{12,28},{16,0},{20,4},{24,8},{28,12},{1,17},{... | collective-permute-start | bytes 1572872 | tf_op jit(solution)/shard_map/ppermute | solution.py:244
  132.7 16.6 %collective-permute-start.26 = (bf16[2,8,128,128]{3,2,1,0:T(8,128)(2,1)S(1)}, bf16[2,8,128,128]{3,2,1,0:T(8,128)(2,1)S(1)}, u32[]{:S(2)}, u32[]{:S(2)}) collective-permute-start(bf16[2,8,128,128]{3,2,1,0:T(8,128)(2,1)S(1)} %get-tuple-element.139), channel_id=1, source_target_pairs={{0,8},{4,12},{8,0},{12,4},{16,24},{20,28},{24,16},{28,20},{1,9},{5... | collective-permute-start | bytes 1572872 | tf_op jit(solution)/shard_map/ppermute | solution.py:244
  134.0 15.2 %collective-permute-start.28 = (bf16[128,512]{1,0:T(8,128)(2,1)S(1)}, bf16[128,512]{1,0:T(8,128)(2,1)S(1)}, u32[]{:S(2)}, u32[]{:S(2)}) collective-permute-start(bf16[128,512]{1,0:T(8,128)(2,1)S(1)} %add_convert_fusion.12), channel_id=1, source_target_pairs={{0,8},{4,12},{8,0},{12,4},{16,24},{20,28},{24,16},{28,20},{1,9},{5... | collective-permute-start | bytes 393224 | tf_op jit(solution)/shard_map/ppermute | solution.py:244
  149.3 5.7 %collective-permute-start.33 = (bf16[128,512]{1,0:T(8,128)(2,1)S(1)}, bf16[128,512]{1,0:T(8,128)(2,1)S(1)}, u32[]{:S(2)}, u32[]{:S(2)}) collective-permute-start(bf16[128,512]{1,0:T(8,128)(2,1)S(1)} %convert_add_fusion.5), channel_id=1, source_target_pairs={{0,16},{4,20},{8,24},{12,28},{16,0},{20,4},{24,8},{28,12},{1,17},{... | collective-permute-start | bytes 393224 | tf_op jit(solution)/shard_map/ppermute | solution.py:244
  150.9 7.3 %collective-permute-start.32 = (bf16[8,128,128]{2,1,0:T(8,128)(2,1)S(1)}, bf16[8,128,128]{2,1,0:T(8,128)(2,1)S(1)}, u32[]{:S(2)}, u32[]{:S(2)}) collective-permute-start(bf16[8,128,128]{2,1,0:T(8,128)(2,1)S(1)} %get-tuple-element.145), channel_id=1, source_target_pairs={{0,8},{4,12},{8,0},{12,4},{16,24},{20,28},{24,16},{28,20},{1,9},{5... | collective-permute-start | bytes 786440 | tf_op jit(solution)/shard_map/ppermute | solution.py:244
  152.3 7.6 %collective-permute-start.29 = (bf16[8,128,128]{2,1,0:T(8,128)(2,1)S(1)}, bf16[8,128,128]{2,1,0:T(8,128)(2,1)S(1)}, u32[]{:S(2)}, u32[]{:S(2)}) collective-permute-start(bf16[8,128,128]{2,1,0:T(8,128)(2,1)S(1)} %get-tuple-element.147), channel_id=1, source_target_pairs={{0,16},{4,20},{8,24},{12,28},{16,0},{20,4},{24,8},{28,12},{1,17},{... | collective-permute-start | bytes 786440 | tf_op jit(solution)/shard_map/ppermute | solution.py:244
  160.0 1.5 collective-permute-start.34

commit v9 on v8

--- a/solution.py
+++ b/solution.py
@@ -182,62 +182,66 @@
     )(*parts)
 
 
-def dense_kernel(cols, masked, col_ref, weight_ref, *rest):
+def dense_kernel(cols, masked, pieces, col_ref, weight_ref, *rest):
     shards, rest = rest[:cols], rest[cols:]
     side_ref, rest = rest[0], rest[1:]
     if masked:
         mask_ref, rest = rest[0], rest[1:]
-    out_ref, grad_ref, whole_ref = rest
+    outs, (grad_ref, whole_ref) = rest[:pieces], rest[pieces:]
     blocks, feat, size = shards[0].shape
     for m in range(cols):
         place = jnp.bitwise_xor(col_ref[0], m)
         for b in range(blocks):
             whole_ref[place, :, b * size : (b + 1) * size] = shards[m][b]
-    whole = jnp.concatenate([whole_ref[q] for q in range(cols)], axis=0)
-    res = jnp.dot(weight_ref[...], whole, preferred_element_type=F32)
-    for b in range(blocks):
-        part = res[:, b * size : (b + 1) * size]
-        out_ref[b] = (part * mask_ref[b].astype(F32) if masked else part).astype(BF16)
-    side = jnp.concatenate([side_ref[b] for b in range(blocks)], axis=0)
-    grad_ref[...] = jnp.dot(whole, side, preferred_element_type=F32)
-
-
-def dense(weight, shards, side, mask, col):
+    per = blocks // pieces
+    total = None
+    for i, out in enumerate(outs):
+        part = slice(i * per * size, (i + 1) * per * size)
+        whole = jnp.concatenate([whole_ref[q, :, part] for q in range(cols)], axis=0)
+        res = jnp.dot(weight_ref[...], whole, preferred_element_type=F32)
+        for b in range(per):
+            block = res[:, b * size : (b + 1) * size]
+            out[b] = (block * mask_ref[i * per + b].astype(F32) if masked else block).astype(BF16)
+        side = jnp.concatenate([side_ref[i * per + b] for b in range(per)], axis=0)
+        term = jnp.dot(whole, side, preferred_element_type=F32)
+        total = term if total is None else total + term
+    grad_ref[...] = total
+
+
+def dense(weight, shards, side, mask, col, pieces):
     blocks, feat, size = shards[0].shape
     cols = len(shards)
     args = [weight, *shards, side] + ([] if mask is None else [mask])
     return pl.pallas_call(
-        functools.partial(dense_kernel, cols, mask is not None),
-        out_shape=[
-            jax.ShapeDtypeStruct((blocks, feat, size), BF16),
-            jax.ShapeDtypeStruct((cols * feat, side.shape[2]), F32),
-        ],
+        functools.partial(dense_kernel, cols, mask is not None, pieces),
+        out_shape=[jax.ShapeDtypeStruct((blocks // pieces, feat, size), BF16)] * pieces
+        + [jax.ShapeDtypeStruct((cols * feat, side.shape[2]), F32)],
         in_specs=[SMEM] + [VMEM] * len(args),
-        out_specs=[VMEM, VMEM],
+        out_specs=[VMEM] * (pieces + 1),
         scratch_shapes=[pltpu.VMEM((cols, feat, blocks * size), BF16)],
         compiler_params=PARAMS,
         name="dense",
     )(col, *args)
 
 
-def weight_terms_kernel(me_ref, *refs):
-    firsts, seconds, (keep_ref, send_ref) = refs[:GROUPS], refs[GROUPS : 2 * GROUPS], refs[2 * GROUPS :]
-    first, second = sum(r[...] for r in firsts).T, sum(r[...] for r in seconds).T
+def weight_terms_kernel(me_ref, second_ref, *refs):
+    firsts, (keep_ref, send_ref) = refs[:-2], refs[-2:]
+    first, second = sum(r[...] for r in firsts).T, second_ref[...].T
     even = jnp.bitwise_and(me_ref[0], 1) == 0
     keep_ref[...] = jnp.where(even, second, first)
     send_ref[...] = jnp.where(even, first, second).astype(BF16)
 
 
-def weight_terms(firsts, seconds, me):
-    shape = firsts[0].shape[::-1]
+def weight_terms(firsts, second, me):
+    shape = second.shape[::-1]
     return pl.pallas_call(
         weight_terms_kernel,
         out_shape=[jax.ShapeDtypeStruct(shape, F32), jax.ShapeDtypeStruct(shape, BF16)],
-        in_specs=[SMEM] + [VMEM] * (2 * GROUPS),
+        in_specs=[SMEM] + [VMEM] * (1 + len(firsts)),
         out_specs=[VMEM] * 2,
         compiler_params=PARAMS,
         name="weight_terms",
-    )(me, *firsts, *seconds)
+    )(me, second, *firsts)
 
 
 def swap(value, mask, axis):
@@ -274,11 +278,11 @@
     return done, beside
 
 
-def gather_columns(own, cols):
+def gather_columns(own, cols, beside=()):
     if cols == 4:
-        near, far = lax.optimization_barrier((swap(own, 1, "col"), swap(own, 3, "col")))
-        return [own, near, swap(far, 1, "col"), far]
-    return [own] + [swap(own, m, "col") for m in range(1, cols)]
+        near, far, beside = lax.optimization_barrier((swap(own, 1, "col"), swap(own, 3, "col"), beside))
+        return [own, near, swap(far, 1, "col"), far], beside
+    return [own] + [swap(own, m, "col") for m in range(1, cols)], beside
 
 
 def over_chips(value, masks):
@@ -301,40 +305,28 @@
     blocked = lambda v: v.reshape(v.shape[0] // size, size, v.shape[1])
     after = lax.optimization_barrier
 
-    parts = {0: blocked(node_feats)}
-    for rel in chips:
-        parts[rel] = swap(parts[0], rel, "row")
     *pieces, mask = spread(edge_tiles, block_cols, [blocked(grad_out)], me_at, rows, blocked(relu_mask))
-    pieces, parts = after((pieces, parts))
-    terms, parts = scatter(pieces, rows, parts)
-    for rel in [0] + chips:
-        parts[rel + 1] = swap(parts[rel], 1, "row")
-    hidden = blocked(hidden_act)
-    owns = [finish(terms[g], False) for g in range(GROUPS)]
-    owns, parts = after((owns, parts))
-    for rel in range(2, rows, 2):
-        top = 1 << (rel.bit_length() - 1)
-        if rel not in parts:
-            parts[rel] = swap(parts[rel - top], top, "row")
-    deltas, seconds, inputs, firsts = [], [], [], []
+    terms, _ = scatter(pieces, rows)
+    own, node_feats = after((finish([t for pair in terms for t in pair], False), blocked(node_feats)))
+    shards, _ = gather_columns(own, cols)
+    parts = [node_feats] + [swap(node_feats, rel, "row") for rel in range(2, rows, 2)]
+    parts = [v for part in parts for v in (part, swap(part, 1, "row"))]
+    shards, parts = after((shards, parts))
+    *deltas, second = dense(weight_two, shards, blocked(hidden_act), mask, col_at, GROUPS)
+    deltas[0], parts = after((deltas[0], parts))
+    agg_feats = aggregate(edge_tiles, block_cols, parts, me_at)
+    inputs, firsts = [], []
     for g in range(GROUPS):
-        delta, grad = dense(weight_two, gather_columns(owns[g], cols), cut(hidden, g), cut(mask, g), col_at)
-        deltas.append(delta)
-        seconds.append(grad)
-    deltas[-1], parts = after((deltas[-1], parts))
-    for rel in range(1, rows, 2):
-        if rel not in parts:
-            parts[rel] = swap(parts[rel - 1], 1, "row")
-    agg_feats = aggregate(edge_tiles, block_cols, [parts[rel] for rel in range(rows)], me_at)
-    for g in range(GROUPS):
-        out, grad = dense(weight_one, gather_columns(deltas[g], cols), cut(agg_feats, g), None, col_at)
+        shards, beside = gather_columns(deltas[g], cols, agg_feats if g == 0 else ())
+        agg_feats = beside if g == 0 else agg_feats
+        out, grad = dense(weight_one, shards, cut(agg_feats, g), None, col_at, 1)
         inputs.append(out)
         firsts.append(grad)
     pieces = spread(edge_tiles, block_cols, inputs, me_at, rows)
-    keep, send = weight_terms(firsts, seconds, me_at)
-    value = over_chips(keep + swap(send, 1, "row").astype(F32), chips[:1])
+    keep, send = weight_terms(firsts, second, me_at)
+    value = over_chips(keep + swap(send, 1, "row").astype(F32), chips[-1:])
     terms, value = scatter(pieces, rows, value)
-    terms, value = after((terms, over_chips(value, chips[1:])))
+    terms, value = after((terms, over_chips(value, chips[:-1])))
     out = finish([t for pair in terms for t in pair], True)
     other = swap(value, 1, "row")
     even = me % 2 == 0

time: 163 us -> 158 us (0.969)
  waiting for transfers between devices: 90.5 us -> 86.9 us
  local copies, waits for them, and re-layouts: 8.26 us -> 5.7 us
  starting transfers between devices: 32.5 us -> 34.5 us
    ppermute x35 -> x32, waiting for transfers between devices: 90.5 us -> 86.9 us  [swap(): lax.ppermute(value, axis, [(i, i ^ mask) for i in range(lax.axis_size(axi...]
    ppermute x35 -> x32, starting transfers between devices: 32.5 us -> 34.5 us  [swap(): lax.ppermute(value, axis, [(i, i ^ mask) for i in range(lax.axis_size(axi...]
    unnamed x24 -> x22, local copies, waits for them, and re-layouts: 7.08 us -> 5.66 us
    pallas_call x4 -> x3, Pallas kernels: 5.48 us -> 4.42 us  [dense(): pl.pallas_call(functools.partial(dense_kernel, cols, mask is not None, pi...]
  transfers between devices with their start and end apart: 35 -> 32, of which waited for: 23 -> 17; matrix products, arithmetic and copies ran while one was open for 2% -> 1% of each run, Pallas kernels for 12% -> 5%
where the time goes in v9:
time: 158 us; the launch traced here: 157 us
  waiting for transfers between devices  86.9 us (55%)
  starting transfers between devices  34.5 us (22%)
  Pallas kernels  26 us (16%)
  local copies, waits for them, and re-layouts  5.7 us (4%)
  other arithmetic  3.06 us (2%)
    ppermute x32, waiting for transfers between devices, swap(): lax.ppermute(value, axis, [(i, i ^ mask) for i in range(lax.axis_size(axi...  86.9 us
    ppermute x32, starting transfers between devices, swap(): lax.ppermute(value, axis, [(i, i ^ mask) for i in range(lax.axis_size(axi...  34.5 us
    pallas_call x2, Pallas kernels, spread(): pl.pallas_call(functools.partial(spread_kernel, first, len(vals)), out_sh...  13.7 us
    pallas_call x1, Pallas kernels, aggregate(): pl.pallas_call(aggregate_kernel, out_shape=jax.ShapeDtypeStruct((blocks,...  6.5 us
    unnamed x22, local copies, waits for them, and re-layouts  5.66 us
    pallas_call x3, Pallas kernels, dense(): pl.pallas_call(functools.partial(dense_kernel, cols, mask is not None, pi...  4.42 us
  transfers between devices with their start and end apart: 32, of which 17 were waited for; matrix products, arithmetic and copies ran while one was open for 1% of the time, Pallas kernels for 5%

profile of v9, /device:TPU:0, one launch (start us, length us, event | category | flops | bytes accessed | tf_op | source)
XLA Modules:
  0.0 157.0 jit_solution(14010596578466317052)
XLA Ops:
  0.6 1.0 copy-done.7
  1.7 0.7 copy-done.9
  2.4 7.0 %spread.2 = (bf16[4,8,128,128]{3,2,1,0:T(8,128)(2,1)S(1)}, bf16[4,8,128,128]{3,2,1,0:T(8,128)(2,1)S(1)}, bf16[4,8,128,128]{3,2,1,0:T(8,128)(2,1)S(1)}, bf16[4,8,...) custom-call(s32[16,20]{1,0:T(8,128)S(1)} %copy-done.9, s32[1]{0:T(128)} %bitcast.me_ref, ...), custom_call_target="tpu_custom_call" | custom-call | flops 1342177280 | bytes 30000000 | tf_op jit(solution)/shard_map/spread/pallas_call | solution.py:105
  9.4 0.5 collective-permute-start.3
  10.0 2.2 %collective-permute-done.3 = bf16[4,8,128,128]{3,2,1,0:T(8,128)(2,1)S(1)} collective-permute-done((bf16[4,8,128,128]{3,2,1,0:T(8,128)(2,1)S(1)}, bf16[4,8,128,128]{3,2,1,0:T(8,128)(2,1)S(1)}, u32[]{:S(2)}, u32[]{:S(2)}) %collective-permute-start.3) | collective-permute-done | bytes 1048608 | tf_op jit(solution)/shard_map/ppermute | solution.py:248
  12.2 0.5 add_convert_fusion.5
  12.7 2.9 %collective-permute-start.4 = (bf16[2,8,128,128]{3,2,1,0:T(8,128)(2,1)S(1)}, bf16[2,8,128,128]{3,2,1,0:T(8,128)(2,1)S(1)}, u32[]{:S(2)}, u32[]{:S(2)}) collective-permute-start(bf16[2,8,128,128]{3,2,1,0:T(8,128)(2,1)S(1)} %get-tuple-element.122), channel_id=1, source_target_pairs={{0,16},{4,20},{8,24},{12,28},{16,0},{20,4},{24,8},{28,12},{1,17},{... | collective-permute-start | bytes 1572872 | tf_op jit(solution)/shard_map/ppermute | solution.py:248
  15.7 0.3 add_convert_fusion.7
  16.0 1.6 collective-permute-start.1
  17.5 10.3 %collective-permute-done.4 = bf16[2,8,128,128]{3,2,1,0:T(8,128)(2,1)S(1)} collective-permute-done((bf16[2,8,128,128]{3,2,1,0:T(8,128)(2,1)S(1)}, bf16[2,8,128,128]{3,2,1,0:T(8,128)(2,1)S(1)}, u32[]{:S(2)}, u32[]{:S(2)}) %collective-permute-start.4) | collective-permute-done | bytes 524320 | tf_op jit(solution)/shard_map/ppermute | solution.py:248
  28.0 1.8 %collective-permute-start.5 = (bf16[8,128,128]{2,1,0:T(8,128)(2,1)S(1)}, bf16[8,128,128]{2,1,0:T(8,128)(2,1)S(1)}, u32[]{:S(2)}, u32[]{:S(2)}) collective-permute-start(bf16[8,128,128]{2,1,0:T(8,128)(2,1)S(1)} %get-tuple-element.129), channel_id=1, source_target_pairs={{0,8},{4,12},{8,0},{12,4},{16,24},{20,28},{24,16},{28,20},{1,9},{5... | collective-permute-start | bytes 786440 | tf_op jit(solution)/shard_map/ppermute | solution.py:248
  29.8 0.1 fusion.11
  30.0 1.6 %collective-permute-start.2 = (bf16[8,128,128]{2,1,0:T(8,128)(2,1)S(1)}, bf16[8,128,128]{2,1,0:T(8,128)(2,1)S(1)}, u32[]{:S(2)}, u32[]{:S(2)}) collective-permute-start(bf16[8,128,128]{2,1,0:T(8,128)(2,1)S(1)} %get-tuple-element.131), channel_id=1, source_target_pairs={{0,16},{4,20},{8,24},{12,28},{16,0},{20,4},{24,8},{28,12},{1,17},{... | collective-permute-start | bytes 786440 | tf_op jit(solution)/shard_map/ppermute | solution.py:248
  31.5 4.4 %collective-permute-done.5.refs_3_ = bf16[8,128,128]{2,1,0:T(8,128)(2,1)S(1)} collective-permute-done((bf16[8,128,128]{2,1,0:T(8,128)(2,1)S(1)}, bf16[8,128,128]{2,1,0:T(8,128)(2,1)S(1)}, u32[]{:S(2)}, u32[]{:S(2)}) %collective-permute-start.5) | collective-permute-done | bytes 262176 | tf_op jit(solution)/shard_map/ppermute | solution.py:248
  35.9 1.3 collective-permute-done.2.refs_1_
  37.4 1.6 %collective-permute-start.6 = (bf16[16,128,128]{2,1,0:T(8,128)(2,1)S(1)}, bf16[16,128,128]{2,1,0:T(8,128)(2,1)S(1)}, u32[]{:S(2)}, u32[]{:S(2)}) collective-permute-start(bf16[16,128,128]{2,1,0:T(8,128)(2,1)S(1)} %finish.2.rest_0_), channel_id=1, source_target_pairs={{0,1},{1,0},{2,3},{3,2},{4,5},{5,4},{6,7},{7,6},{8,9},{9,8},{10,11... | collective-permute-start | bytes 1572872 | tf_op jit(solution)/shard_map/ppermute | solution.py:248
  39.0 2.5 %collective-permute-start.7 = (bf16[16,128,128]{2,1,0:T(8,128)(2,1)S(1)}, bf16[16,128,128]{2,1,0:T(8,128)(2,1)}, u32[]{:S(2)}, u32[]{:S(2)}) collective-permute-start(bf16[16,128,128]{2,1,0:T(8,128)(2,1)S(1)} %finish.2.rest_0_), channel_id=1, source_target_pairs={{0,3},{1,2},{2,1},{3,0},{4,7},{5,6},{6,5},{7,4},{8,11},{9,10},{10,... | collective-permute-start | bytes 1572872 | tf_op jit(solution)/shard_map/ppermute | solution.py:248
  41.5 1.4 collective-permute-start.10
  42.9 1.6 collective-permute-start.12
  44.5 0.5 collective-permute-start.14
  45.0 6.4 %collective-permute-done.6.rest_1_ = bf16[16,128,128]{2,1,0:T(8,128)(2,1)S(1)} collective-permute-done((bf16[16,128,128]{2,1,0:T(8,128)(2,1)S(1)}, bf16[16,128,128]{2,1,0:T(8,128)(2,1)S(1)}, u32[]{:S(2)}, u32[]{:S(2)}) %collective-permute-start.6) | collective-permute-done | bytes 524320 | tf_op jit(solution)/shard_map/ppermute | solution.py:248
  51.4 0.8 copy-done.4
  52.2 10.7 %collective-permute-done.7.rest_3_ = bf16[16,128,128]{2,1,0:T(8,128)(2,1)} collective-permute-done((bf16[16,128,128]{2,1,0:T(8,128)(2,1)S(1)}, bf16[16,128,128]{2,1,0:T(8,128)(2,1)}, u32[]{:S(2)}, u32[]{:S(2)}) %collective-permute-start.7) | collective-permute-done | bytes 524320 | tf_op jit(solution)/shard_map/ppermute | solution.py:248
  62.9 0.6 collective-permute-start.8
  63.4 1.9 %collective-permute-done.12.rest_4_ = bf16[16,128,128]{2,1,0:T(8,128)(2,1)S(1)} collective-permute-done((bf16[16,128,128]{2,1,0:T(8,128)(2,1)S(1)}, bf16[16,128,128]{2,1,0:T(8,128)(2,1)S(1)}, u32[]{:S(2)}, u32[]{:S(2)}) %collective-permute-start.12) | collective-permute-done | bytes 524320 | tf_op jit(solution)/shard_map/ppermute | solution.py:248
  65.3 0.5 collective-permute-start.15
  65.8 8.3 %collective-permute-done.8.rest_2_ = bf16[16,128,128]{2,1,0:T(8,128)(2,1)} collective-permute-done((bf16[16,128,128]{2,1,0:T(8,128)(2,1)}, bf16[16,128,128]{2,1,0:T(8,128)(2,1)}, u32[]{:S(2)}, u32[]{:S(2)}) %collective-permute-start.8) | collective-permute-done | bytes 524320 | tf_op jit(solution)/shard_map/ppermute | solution.py:248
  74.2 1.0 copy-done.1
  75.2 1.0 copy-done.3
  76.2 1.0 copy-done.5
  77.3 2.7 %dense.3 = (bf16[8,128,128]{2,1,0:T(8,128)(2,1)S(1)}, bf16[8,128,128]{2,1,0:T(8,128)(2,1)S(1)}, f32[512,128]{1,0:T(8,128)S(1)}) custom-call(s32[1]{0:T(128)} %bitcast.1.col_ref, bf16[128,512]{1,0:T(8,128)(2,1)S(1)} %copy-done.8, bf16[16,128,128]{2,1,0:T(8,128)(2,1)S(1)} %finish.2.rest_0_, bf16[16,128,128]{2,1,0:T(8,128)(2,1)S(1)} %copy-done.5, ...), custom_call_target="tpu_custom_call" | custom-call | tf_op jit(solution)/shard_map/dense/pallas_call | solution.py:215
  80.0 0.3 collective-permute-start.19
  80.4 5.6 %collective-permute-start.20 = (bf16[8,128,128]{2,1,0:T(8,128)(2,1)S(1)}, bf16[8,128,128]{2,1,0:T(8,128)(2,1)S(1)}, u32[]{:S(2)}, u32[]{:S(2)}) collective-permute-start(bf16[8,128,128]{2,1,0:T(8,128)(2,1)S(1)} %get-tuple-element.95.rest_0_), channel_id=1, source_target_pairs={{0,3},{1,2},{2,1},{3,0},{4,7},{5,6},{6,5},{7,4},{8,11},{9,10},{10,... | collective-permute-start | bytes 786440 | tf_op jit(solution)/shard_map/ppermute | solution.py:248
  85.9 0.8 collective-permute-start.16
  86.8 0.9 collective-permute-start.17
  87.7 6.5 %aggregate.1 = bf16[16,128,128]{2,1,0:T(8,128)(2,1)S(1)} custom-call(s32[16,20]{1,0:T(8,128)S(1)} %copy-done.10, s32[1]{0:T(128)} %bitcast.me_ref, bf16[16,20,128,128]{3,2,1,0:T(8,128)(2,1)} %tiles_ref.5, bf16[16,128,128]{2,1,0:T(8,128)(2,1)S(1)} %bitcast.57, bf16[16,128,128]{2,1,0:T(8,128)(2,1)S(1)} %collective-permute-done.9.rest_1_, ...), custom_call_target="tpu_custom_call" | custom-call | flops 1342177280 | bytes 30000000 | tf_op jit(solution)/shard_map/aggregate/pallas_call | solution.py:147
  94.2 4.6 %collective-permute-done.20.rest_3_ = bf16[8,128,128]{2,1,0:T(8,128)(2,1)S(1)} collective-permute-done((bf16[8,128,128]{2,1,0:T(8,128)(2,1)S(1)}, bf16[8,128,128]{2,1,0:T(8,128)(2,1)S(1)}, u32[]{:S(2)}, u32[]{:S(2)}) %collective-permute-start.20) | collective-permute-done | bytes 262176 | tf_op jit(solution)/shard_map/ppermute | solution.py:248
  98.8 0.8 collective-permute-start.21
  99.6 10.5 %collective-permute-done.17.rest_3_ = bf16[8,128,128]{2,1,0:T(8,128)(2,1)S(1)} collective-permute-done((bf16[8,128,128]{2,1,0:T(8,128)(2,1)S(1)}, bf16[8,128,128]{2,1,0:T(8,128)(2,1)S(1)}, u32[]{:S(2)}, u32[]{:S(2)}) %collective-permute-start.17) | collective-permute-done | bytes 262176 | tf_op jit(solution)/shard_map/ppermute | solution.py:248
  110.1 0.7 collective-permute-done.21.rest_2_
  110.8 0.9 dense.5
  111.6 4.8 %collective-permute-done.18.rest_2_ = bf16[8,128,128]{2,1,0:T(8,128)(2,1)S(1)} collective-permute-done((bf16[8,128,128]{2,1,0:T(8,128)(2,1)S(1)}, bf16[8,128,128]{2,1,0:T(8,128)(2,1)S(1)}, u32[]{:S(2)}, u32[]{:S(2)}) %collective-permute-start.18) | collective-permute-done | bytes 262176 | tf_op jit(solution)/shard_map/ppermute | solution.py:248
  116.4 0.8 dense.4
  117.3 6.7 %spread.3 = (bf16[4,8,128,128]{3,2,1,0:T(8,128)(2,1)S(1)}, bf16[4,8,128,128]{3,2,1,0:T(8,128)(2,1)S(1)}, bf16[4,8,128,128]{3,2,1,0:T(8,128)(2,1)S(1)}, bf16[4,8,128,128]{3,2,1,0:T(8,128)(2,1)S(1)}) custom-call(s32[16,20]{1,0:T(8,128)S(1)} %copy-done.10, s32[1]{0:T(128)} %bitcast.me_ref, bf16[16,20,128,128]{3,2,1,0:T(8,128)(2,1)} %tiles_ref.5, ...), custom_call_target="tpu_custom_call" | custom-call | flops 1342177280 | bytes 30000000 | tf_op jit(solution)/shard_map/spread/pallas_call | solution.py:105
  124.1 0.5 collective-permute-start.22
  124.6 0.2 weight_terms.1
  124.8 0.1 collective-permute-start.24
  124.9 1.8 %collective-permute-done.27 = bf16[4,8,128,128]{3,2,1,0:T(8,128)(2,1)S(1)} collective-permute-done((bf16[4,8,128,128]{3,2,1,0:T(8,128)(2,1)S(1)}, bf16[4,8,128,128]{3,2,1,0:T(8,128)(2,1)S(1)}, u32[]{:S(2)}, u32[]{:S(2)}) %collective-permute-start.27) | collective-permute-done | bytes 1048608 | tf_op jit(solution)/shard_map/ppermute | solution.py:248
  126.7 0.4 add_convert_fusion
  127.1 1.6 %collective-permute-start.28 = (bf16[2,8,128,128]{3,2,1,0:T(8,128)(2,1)S(1)}, bf16[2,8,128,128]{3,2,1,0:T(8,128)(2,1)S(1)}, u32[]{:S(2)}, u32[]{:S(2)}) collective-permute-start(bf16[2,8,128,128]{3,2,1,0:T(8,128)(2,1)S(1)} %get-tuple-element.117), channel_id=1, source_target_pairs={{0,16},{4,20},{8,24},{12,28},{16,0},{20,4},{24,8},{28,12},{1,17},{... | collective-permute-start | bytes 1572872 | tf_op jit(solution)/shard_map/ppermute | solution.py:248
  128.7 0.4 fusion.1
  129.1 1.8 %collective-permute-start.23 = (bf16[2,8,128,128]{3,2,1,0:T(8,128)(2,1)S(1)}, bf16[2,8,128,128]{3,2,1,0:T(8,128)(2,1)S(1)}, u32[]{:S(2)}, u32[]{:S(2)}) collective-permute-start(bf16[2,8,128,128]{3,2,1,0:T(8,128)(2,1)S(1)} %get-tuple-element.119), channel_id=1, source_target_pairs={{0,8},{4,12},{8,0},{12,4},{16,24},{20,28},{24,16},{28,20},{1,9},{5... | collective-permute-start | bytes 1572872 | tf_op jit(solution)/shard_map/ppermute | solution.py:248
  130.9 1.1 collective-permute-start.25
  132.0 12.0 %collective-permute-done.25 = bf16[128,512]{1,0:T(8,128)(2,1)S(1)} collective-permute-done((bf16[128,512]{1,0:T(8,128)(2,1)S(1)}, bf16[128,512]{1,0:T(8,128)(2,1)S(1)}, u32[]{:S(2)}, u32[]{:S(2)}) %collective-permute-start.25) | collective-permute-done | bytes 131104 | tf_op jit(solution)/shard_map/ppermute | solution.py:248
  144.0 1.6 collective-permute-start.30
  145.6 0.1 fusion.9
  145.7 0.6 collective-permute-start.29
  146.3 0.1 fusion.13
  146.5 1.6 %collective-permute-start.26 = (bf16[8,128,128]{2,1,0:T(8,128)(2,1)S(1)}, bf16[8,128,128]{2,1,0:T(8,128)(2,1)S(1)}, u32[]{:S(2)}, u32[]{:S(2)}) collective-permute-start(bf16[8,128,128]{2,1,0:T(8,128)(2,1)S(1)} %get-tuple-element.127), channel_id=1, source_target_pairs={{0,16},{4,20},{8,24},{12,28},{16,0},{20,4},{24,8},{28,12},{1,17},{... | collective-permute-start | bytes 786440 | tf_op jit(solution)/shard_map/ppermute | solution.py:248
  148.1 2.4 %collective-permute-done.30 = bf16[128,512]{1,0:T(8,128)(2,1)S(1)} collective-permute-done((bf16[128,512]{1,0:T(8,128)(2,1)S(1)}, bf16[128,512]{1,0:T(8,128)(2,1)S(1)}, u32[]{:S(2)}, u32[]{:S(2)}) %collective-permute-start.30) | collective-permute-done | bytes 131104 | tf_op jit(solution)/shard_map/ppermute | solution.py:248
  150.5 4.1 %collective-permute-done.29.refs_3_ = bf16[8,128,128]{2,1,0:T(8,128)(2,1)S(1)} collective-permute-done((bf16[8,128,128]{2,1,0:T(8,128)(2,1)S(1)}, bf16[8,128,128]{2,1,0:T(8,128)(2,1)S(1)}, u32[]{:S(2)}, u32[]{:S(2)}) %collective-permute-start.29) | collective-permute-done | bytes 262176 | tf_op jit(solution)/shard_map/ppermute | solution.py:248
  154.6 1.0 finish.3
  155.6 0.5 collective-permute-done.31
  156.1 0.8 broadcast_select_fusion
  (44 shorter events, 0.6 us)
Async XLA Ops:
  0.6 1.0 copy-start.7
  1.7 0.7 copy-start.9
  2.4 39.1 %copy-start = (bf16[2048,128]{1,0:T(8,128)(2,1)S(1)}, bf16[2048,128]{1,0:T(8,128)(2,1)}, u32[]{:S(2)}) copy-start(bf16[2048,128]{1,0:T(8,128)(2,1)} %param.8) | copy-start | bytes 1572868
  2.4 71.8 %copy-start.8 = (bf16[128,512]{1,0:T(8,128)(2,1)S(1)}, bf16[128,512]{1,0:T(8,128)(2,1)}, u32[]{:S(2)}) copy-start(bf16[128,512]{1,0:T(8,128)(2,1)} %weight_ref.3) | copy-start | bytes 393220
  2.4 85.3 %copy-start.10 = (s32[16,20]{1,0:T(8,128)S(1)}, s32[16,20]{1,0:T(8,128)}, u32[]{:S(2)}) copy-start(s32[16,20]{1,0:T(8,128)} %cols_ref.5) | copy-start | bytes 3844
  9.4 55.9 %copy-start.2 = (bf16[16,128,128]{2,1,0:T(8,128)(2,1)}, bf16[16,128,128]{2,1,0:T(8,128)(2,1)S(1)}, u32[]{:S(2)}) copy-start(bf16[16,128,128]{2,1,0:T(8,128)(2,1)S(1)} %get-tuple-element.72.rest_5_) | copy-start | bytes 1572868
  9.4 2.8 %collective-permute-start.3 = (bf16[4,8,128,128]{3,2,1,0:T(8,128)(2,1)S(1)}, bf16[4,8,128,128]{3,2,1,0:T(8,128)(2,1)S(1)}, u32[]{:S(2)}, u32[]{:S(2)}) collective-permute-start(bf16[4,8,128,128]{3,2,1,0:T(8,128)(2,1)S(1)} %get-tuple-element.63), channel_id=1, source_target_pairs={{0,4},{4,0},{8,12},{12,8},{16,20},{20,16},{24,28},{28,24},{1,5},{5... | collective-permute-start | bytes 3145736 | tf_op jit(solution)/shard_map/ppermute | solution.py:248
  10.0 5.7 %collective-permute-start = (bf16[4,8,128,128]{3,2,1,0:T(8,128)(2,1)S(1)}, bf16[4,8,128,128]{3,2,1,0:T(8,128)(2,1)S(1)}, u32[]{:S(2)}, u32[]{:S(2)}) collective-permute-start(bf16[4,8,128,128]{3,2,1,0:T(8,128)(2,1)S(1)} %get-tuple-element.61), channel_id=1, source_target_pairs={{0,4},{4,0},{8,12},{12,8},{16,20},{20,16},{24,28},{28,24},{1,5},{5... | collective-permute-start | bytes 3145736 | tf_op jit(solution)/shard_map/ppermute | solution.py:248
  12.7 15.2 %collective-permute-start.4 = (bf16[2,8,128,128]{3,2,1,0:T(8,128)(2,1)S(1)}, bf16[2,8,128,128]{3,2,1,0:T(8,128)(2,1)S(1)}, u32[]{:S(2)}, u32[]{:S(2)}) collective-permute-start(bf16[2,8,128,128]{3,2,1,0:T(8,128)(2,1)S(1)} %get-tuple-element.122), channel_id=1, source_target_pairs={{0,16},{4,20},{8,24},{12,28},{16,0},{20,4},{24,8},{28,12},{1,17},{... | collective-permute-start | bytes 1572872 | tf_op jit(solution)/shard_map/ppermute | solution.py:248
  16.0 13.8 %collective-permute-start.1 = (bf16[2,8,128,128]{3,2,1,0:T(8,128)(2,1)S(1)}, bf16[2,8,128,128]{3,2,1,0:T(8,128)(2,1)S(1)}, u32[]{:S(2)}, u32[]{:S(2)}) collective-permute-start(bf16[2,8,128,128]{3,2,1,0:T(8,128)(2,1)S(1)} %get-tuple-element.124), channel_id=1, source_target_pairs={{0,8},{4,12},{8,0},{12,4},{16,24},{20,28},{24,16},{28,20},{1,9},{5... | collective-permute-start | bytes 1572872 | tf_op jit(solution)/shard_map/ppermute | solution.py:248
  28.0 7.9 %collective-permute-start.5 = (bf16[8,128,128]{2,1,0:T(8,128)(2,1)S(1)}, bf16[8,128,128]{2,1,0:T(8,128)(2,1)S(1)}, u32[]{:S(2)}, u32[]{:S(2)}) collective-permute-start(bf16[8,128,128]{2,1,0:T(8,128)(2,1)S(1)} %get-tuple-element.129), channel_id=1, source_target_pairs={{0,8},{4,12},{8,0},{12,4},{16,24},{20,28},{24,16},{28,20},{1,9},{5... | collective-permute-start | bytes 786440 | tf_op jit(solution)/shard_map/ppermute | solution.py:248
  30.0 7.3 %collective-permute-start.2 = (bf16[8,128,128]{2,1,0:T(8,128)(2,1)S(1)}, bf16[8,128,128]{2,1,0:T(8,128)(2,1)S(1)}, u32[]{:S(2)}, u32[]{:S(2)}) collective-permute-start(bf16[8,128,128]{2,1,0:T(8,128)(2,1)S(1)} %get-tuple-element.131), channel_id=1, source_target_pairs={{0,16},{4,20},{8,24},{12,28},{16,0},{20,4},{24,8},{28,12},{1,17},{... | collective-permute-start | bytes 786440 | tf_op jit(solution)/shard_map/ppermute | solution.py:248
  37.3 73.5 %copy-start.6 = (bf16[128,512]{1,0:T(8,128)(2,1)S(1)}, bf16[128,512]{1,0:T(8,128)(2,1)}, u32[]{:S(2)}) copy-start(bf16[128,512]{1,0:T(8,128)(2,1)} %weight_ref.5) | copy-start | bytes 393220
  37.4 14.0 %collective-permute-start.6 = (bf16[16,128,128]{2,1,0:T(8,128)(2,1)S(1)}, bf16[16,128,128]{2,1,0:T(8,128)(2,1)S(1)}, u32[]{:S(2)}, u32[]{:S(2)}) collective-permute-start(bf16[16,128,128]{2,1,0:T(8,128)(2,1)S(1)} %finish.2.rest_0_), channel_id=1, source_target_pairs={{0,1},{1,0},{2,3},{3,2},{4,5},{5,4},{6,7},{7,6},{8,9},{9,8},{10,11... | collective-permute-start | bytes 1572872 | tf_op jit(solution)/shard_map/ppermute | solution.py:248
  39.0 23.8 %collective-permute-start.7 = (bf16[16,128,128]{2,1,0:T(8,128)(2,1)S(1)}, bf16[16,128,128]{2,1,0:T(8,128)(2,1)}, u32[]{:S(2)}, u32[]{:S(2)}) collective-permute-start(bf16[16,128,128]{2,1,0:T(8,128)(2,1)S(1)} %finish.2.rest_0_), channel_id=1, source_target_pairs={{0,3},{1,2},{2,1},{3,0},{4,7},{5,6},{6,5},{7,4},{8,11},{9,10},{10,... | collective-permute-start | bytes 1572872 | tf_op jit(solution)/shard_map/ppermute | solution.py:248
  41.5 21.9 %collective-permute-start.10 = (bf16[16,128,128]{2,1,0:T(8,128)(2,1)S(1)}, bf16[16,128,128]{2,1,0:T(8,128)(2,1)S(1)}, u32[]{:S(2)}, u32[]{:S(2)}) collective-permute-start(bf16[16,128,128]{2,1,0:T(8,128)(2,1)S(1)} %bitcast.53), channel_id=1, source_target_pairs={{0,8},{4,12},{8,0},{12,4},{16,24},{20,28},{24,16},{28,20},{1,9},{5... | collective-permute-start | bytes 1572872 | tf_op jit(solution)/shard_map/ppermute | solution.py:248
  42.9 22.4 %collective-permute-start.12 = (bf16[16,128,128]{2,1,0:T(8,128)(2,1)S(1)}, bf16[16,128,128]{2,1,0:T(8,128)(2,1)S(1)}, u32[]{:S(2)}, u32[]{:S(2)}) collective-permute-start(bf16[16,128,128]{2,1,0:T(8,128)(2,1)S(1)} %bitcast.54), channel_id=1, source_target_pairs={{0,16},{4,20},{8,24},{12,28},{16,0},{20,4},{24,8},{28,12},{1,17},{... | collective-permute-start | bytes 1572872 | tf_op jit(solution)/shard_map/ppermute | solution.py:248
  44.5 20.9 %collective-permute-start.14 = (bf16[16,128,128]{2,1,0:T(8,128)(2,1)S(1)}, bf16[16,128,128]{2,1,0:T(8,128)(2,1)S(1)}, u32[]{:S(2)}, u32[]{:S(2)}) collective-permute-start(bf16[16,128,128]{2,1,0:T(8,128)(2,1)S(1)} %bitcast.55), channel_id=1, source_target_pairs={{0,24},{4,28},{8,16},{12,20},{16,8},{20,12},{24,0},{28,4},{1,25},{... | collective-permute-start | bytes 1572872 | tf_op jit(solution)/shard_map/ppermute | solution.py:248
  51.4 0.8 copy-start.4
  52.2 13.6 %collective-permute-start.9 = (bf16[16,128,128]{2,1,0:T(8,128)(2,1)S(1)}, bf16[16,128,128]{2,1,0:T(8,128)(2,1)S(1)}, u32[]{:S(2)}, u32[]{:S(2)}) collective-permute-start(bf16[16,128,128]{2,1,0:T(8,128)(2,1)S(1)} %bitcast.56), channel_id=1, source_target_pairs={{0,4},{4,0},{8,12},{12,8},{16,20},{20,16},{24,28},{28,24},{1,5},{5... | collective-permute-start | bytes 1572872 | tf_op jit(solution)/shard_map/ppermute | solution.py:248
  62.9 11.3 %collective-permute-start.8 = (bf16[16,128,128]{2,1,0:T(8,128)(2,1)}, bf16[16,128,128]{2,1,0:T(8,128)(2,1)}, u32[]{:S(2)}, u32[]{:S(2)}) collective-permute-start(bf16[16,128,128]{2,1,0:T(8,128)(2,1)} %collective-permute-done.7.rest_3_), channel_id=1, source_target_pairs={{0,1},{1,0},{2,3},{3,2},{4,5},{5,4},{6,7},{7,6},{8,9},{9,8},{10,11... | collective-permute-start | bytes 1572872 | tf_op jit(solution)/shard_map/ppermute | solution.py:248
  63.4 10.7 %collective-permute-start.11 = (bf16[16,128,128]{2,1,0:T(8,128)(2,1)S(1)}, bf16[16,128,128]{2,1,0:T(8,128)(2,1)}, u32[]{:S(2)}, u32[]{:S(2)}) collective-permute-start(bf16[16,128,128]{2,1,0:T(8,128)(2,1)S(1)} %collective-permute-done.10.rest_2_), channel_id=1, source_target_pairs={{0,4},{4,0},{8,12},{12,8},{16,20},{20,16},{24,28},{28,24},{1,5},{5... | collective-permute-start | bytes 1572872 | tf_op jit(solution)/shard_map/ppermute | solution.py:248
  65.3 8.8 %collective-permute-start.13 = (bf16[16,128,128]{2,1,0:T(8,128)(2,1)S(1)}, bf16[16,128,128]{2,1,0:T(8,128)(2,1)}, u32[]{:S(2)}, u32[]{:S(2)}) collective-permute-start(bf16[16,128,128]{2,1,0:T(8,128)(2,1)S(1)} %collective-permute-done.12.rest_4_), channel_id=1, source_target_pairs={{0,4},{4,0},{8,12},{12,8},{16,20},{20,16},{24,28},{28,24},{1,5},{5... | collective-permute-start | bytes 1572872 | tf_op jit(solution)/shard_map/ppermute | solution.py:248
  65.3 8.8 %collective-permute-start.15 = (bf16[16,128,128]{2,1,0:T(8,128)(2,1)S(1)}, bf16[16,128,128]{2,1,0:T(8,128)(2,1)}, u32[]{:S(2)}, u32[]{:S(2)}) collective-permute-start(bf16[16,128,128]{2,1,0:T(8,128)(2,1)S(1)} %collective-permute-done.14.rest_6_), channel_id=1, source_target_pairs={{0,4},{4,0},{8,12},{12,8},{16,20},{20,16},{24,28},{28,24},{1,5},{5... | collective-permute-start | bytes 1572872 | tf_op jit(solution)/shard_map/ppermute | solution.py:248
  74.2 1.0 copy-start.1
  75.2 1.0 copy-start.3
  76.2 1.0 copy-start.5
  80.0 14.2 %collective-permute-start.19 = (bf16[8,128,128]{2,1,0:T(8,128)(2,1)S(1)}, bf16[8,128,128]{2,1,0:T(8,128)(2,1)S(1)}, u32[]{:S(2)}, u32[]{:S(2)}) collective-permute-start(bf16[8,128,128]{2,1,0:T(8,128)(2,1)S(1)} %get-tuple-element.95.rest_0_), channel_id=1, source_target_pairs={{0,1},{1,0},{2,3},{3,2},{4,5},{5,4},{6,7},{7,6},{8,9},{9,8},{10,11... | collective-permute-start | bytes 786440 | tf_op jit(solution)/shard_map/ppermute | solution.py:248
  80.4 18.4 %collective-permute-start.20 = (bf16[8,128,128]{2,1,0:T(8,128)(2,1)S(1)}, bf16[8,128,128]{2,1,0:T(8,128)(2,1)S(1)}, u32[]{:S(2)}, u32[]{:S(2)}) collective-permute-start(bf16[8,128,128]{2,1,0:T(8,128)(2,1)S(1)} %get-tuple-element.95.rest_0_), channel_id=1, source_target_pairs={{0,3},{1,2},{2,1},{3,0},{4,7},{5,6},{6,5},{7,4},{8,11},{9,10},{10,... | collective-permute-start | bytes 786440 | tf_op jit(solution)/shard_map/ppermute | solution.py:248
  85.9 13.7 %collective-permute-start.16 = (bf16[8,128,128]{2,1,0:T(8,128)(2,1)S(1)}, bf16[8,128,128]{2,1,0:T(8,128)(2,1)S(1)}, u32[]{:S(2)}, u32[]{:S(2)}) collective-permute-start(bf16[8,128,128]{2,1,0:T(8,128)(2,1)S(1)} %get-tuple-element.82.rest_0_), channel_id=1, source_target_pairs={{0,1},{1,0},{2,3},{3,2},{4,5},{5,4},{6,7},{7,6},{8,9},{9,8},{10,11... | collective-permute-start | bytes 786440 | tf_op jit(solution)/shard_map/ppermute | solution.py:248
  86.8 23.3 %collective-permute-start.17 = (bf16[8,128,128]{2,1,0:T(8,128)(2,1)S(1)}, bf16[8,128,128]{2,1,0:T(8,128)(2,1)S(1)}, u32[]{:S(2)}, u32[]{:S(2)}) collective-permute-start(bf16[8,128,128]{2,1,0:T(8,128)(2,1)S(1)} %get-tuple-element.82.rest_0_), channel_id=1, source_target_pairs={{0,3},{1,2},{2,1},{3,0},{4,7},{5,6},{6,5},{7,4},{8,11},{9,10},{10,... | collective-permute-start | bytes 786440 | tf_op jit(solution)/shard_map/ppermute | solution.py:248
  98.8 12.0 %collective-permute-start.21 = (bf16[8,128,128]{2,1,0:T(8,128)(2,1)S(1)}, bf16[8,128,128]{2,1,0:T(8,128)(2,1)S(1)}, u32[]{:S(2)}, u32[]{:S(2)}) collective-permute-start(bf16[8,128,128]{2,1,0:T(8,128)(2,1)S(1)} %collective-permute-done.20.rest_3_), channel_id=1, source_target_pairs={{0,1},{1,0},{2,3},{3,2},{4,5},{5,4},{6,7},{7,6},{8,9},{9,8},{10,11... | collective-permute-start | bytes 786440 | tf_op jit(solution)/shard_map/ppermute | solution.py:248
  110.0 6.4 %collective-permute-start.18 = (bf16[8,128,128]{2,1,0:T(8,128)(2,1)S(1)}, bf16[8,128,128]{2,1,0:T(8,128)(2,1)S(1)}, u32[]{:S(2)}, u32[]{:S(2)}) collective-permute-start(bf16[8,128,128]{2,1,0:T(8,128)(2,1)S(1)} %collective-permute-done.17.rest_3_), channel_id=1, source_target_pairs={{0,1},{1,0},{2,3},{3,2},{4,5},{5,4},{6,7},{7,6},{8,9},{9,8},{10,11... | collective-permute-start | bytes 786440 | tf_op jit(solution)/shard_map/ppermute | solution.py:248
  124.0 2.7 %collective-permute-start.27 = (bf16[4,8,128,128]{3,2,1,0:T(8,128)(2,1)S(1)}, bf16[4,8,128,128]{3,2,1,0:T(8,128)(2,1)S(1)}, u32[]{:S(2)}, u32[]{:S(2)}) collective-permute-start(bf16[4,8,128,128]{3,2,1,0:T(8,128)(2,1)S(1)} %get-tuple-element.108), channel_id=1, source_target_pairs={{0,4},{4,0},{8,12},{12,8},{16,20},{20,16},{24,28},{28,24},{1,5},{5... | collective-permute-start | bytes 3145736 | tf_op jit(solution)/shard_map/ppermute | solution.py:248
  124.1 4.7 %collective-permute-start.22 = (bf16[4,8,128,128]{3,2,1,0:T(8,128)(2,1)S(1)}, bf16[4,8,128,128]{3,2,1,0:T(8,128)(2,1)S(1)}, u32[]{:S(2)}, u32[]{:S(2)}) collective-permute-start(bf16[4,8,128,128]{3,2,1,0:T(8,128)(2,1)S(1)} %get-tuple-element.100), channel_id=1, source_target_pairs={{0,4},{4,0},{8,12},{12,8},{16,20},{20,16},{24,28},{28,24},{1,5},{5... | collective-permute-start | bytes 3145736 | tf_op jit(solution)/shard_map/ppermute | solution.py:248
  124.8 6.1 %collective-permute-start.24 = (bf16[128,512]{1,0:T(8,128)(2,1)S(1)}, bf16[128,512]{1,0:T(8,128)(2,1)S(1)}, u32[]{:S(2)}, u32[]{:S(2)}) collective-permute-start(bf16[128,512]{1,0:T(8,128)(2,1)S(1)} %get-tuple-element.105), channel_id=1, source_target_pairs={{0,4},{4,0},{8,12},{12,8},{16,20},{20,16},{24,28},{28,24},{1,5},{5... | collective-permute-start | bytes 393224 | tf_op jit(solution)/shard_map/ppermute | solution.py:248
  127.1 16.9 %collective-permute-start.28 = (bf16[2,8,128,128]{3,2,1,0:T(8,128)(2,1)S(1)}, bf16[2,8,128,128]{3,2,1,0:T(8,128)(2,1)S(1)}, u32[]{:S(2)}, u32[]{:S(2)}) collective-permute-start(bf16[2,8,128,128]{3,2,1,0:T(8,128)(2,1)S(1)} %get-tuple-element.117), channel_id=1, source_target_pairs={{0,16},{4,20},{8,24},{12,28},{16,0},{20,4},{24,8},{28,12},{1,17},{... | collective-permute-start | bytes 1572872 | tf_op jit(solution)/shard_map/ppermute | solution.py:248
  129.1 14.9 %collective-permute-start.23 = (bf16[2,8,128,128]{3,2,1,0:T(8,128)(2,1)S(1)}, bf16[2,8,128,128]{3,2,1,0:T(8,128)(2,1)S(1)}, u32[]{:S(2)}, u32[]{:S(2)}) collective-permute-start(bf16[2,8,128,128]{3,2,1,0:T(8,128)(2,1)S(1)} %get-tuple-element.119), channel_id=1, source_target_pairs={{0,8},{4,12},{8,0},{12,4},{16,24},{20,28},{24,16},{28,20},{1,9},{5... | collective-permute-start | bytes 1572872 | tf_op jit(solution)/shard_map/ppermute | solution.py:248
  130.9 13.1 %collective-permute-start.25 = (bf16[128,512]{1,0:T(8,128)(2,1)S(1)}, bf16[128,512]{1,0:T(8,128)(2,1)S(1)}, u32[]{:S(2)}, u32[]{:S(2)}) collective-permute-start(bf16[128,512]{1,0:T(8,128)(2,1)S(1)} %add_convert_fusion.12), channel_id=1, source_target_pairs={{0,16},{4,20},{8,24},{12,28},{16,0},{20,4},{24,8},{28,12},{1,17},{... | collective-permute-start | bytes 393224 | tf_op jit(solution)/shard_map/ppermute | solution.py:248
  144.0 6.4 %collective-permute-start.30 = (bf16[128,512]{1,0:T(8,128)(2,1)S(1)}, bf16[128,512]{1,0:T(8,128)(2,1)S(1)}, u32[]{:S(2)}, u32[]{:S(2)}) collective-permute-start(bf16[128,512]{1,0:T(8,128)(2,1)S(1)} %convert_add_fusion.5), channel_id=1, source_target_pairs={{0,8},{4,12},{8,0},{12,4},{16,24},{20,28},{24,16},{28,20},{1,9},{5... | collective-permute-start | bytes 393224 | tf_op jit(solution)/shard_map/ppermute | solution.py:248
  145.7 8.9 %collective-permute-start.29 = (bf16[8,128,128]{2,1,0:T(8,128)(2,1)S(1)}, bf16[8,128,128]{2,1,0:T(8,128)(2,1)S(1)}, u32[]{:S(2)}, u32[]{:S(2)}) collective-permute-start(bf16[8,128,128]{2,1,0:T(8,128)(2,1)S(1)} %get-tuple-element.125), channel_id=1, source_target_pairs={{0,8},{4,12},{8,0},{12,4},{16,24},{20,28},{24,16},{28,20},{1,9},{5... | collective-permute-start | bytes 786440 | tf_op jit(solution)/shard_map/ppermute | solution.py:248
  146.5 8.1 %collective-permute-start.26 = (bf16[8,128,128]{2,1,0:T(8,128)(2,1)S(1)}, bf16[8,128,128]{2,1,0:T(8,128)(2,1)S(1)}, u32[]{:S(2)}, u32[]{:S(2)}) collective-permute-start(bf16[8,128,128]{2,1,0:T(8,128)(2,1)S(1)} %get-tuple-element.127), channel_id=1, source_target_pairs={{0,16},{4,20},{8,24},{12,28},{16,0},{20,4},{24,8},{28,12},{1,17},{... | collective-permute-start | bytes 786440 | tf_op jit(solution)/shard_map/ppermute | solution.py:248
  154.6 1.5 collective-permute-start.31

commit v10 on v8

--- a/solution.py
+++ b/solution.py
@@ -115,7 +115,7 @@
 
 
 def aggregate_kernel(cols_ref, me_ref, tiles_ref, *rest):
-    parts, (out_ref, held, table, sems) = rest[:-4], rest[-4:]
+    parts, (out_ref, held, table, sems) = rest[:-5], rest[-4:]
     blocks, per_row = held.shape[:2]
     loads = []
     for rel, part in enumerate(parts):
@@ -140,14 +140,14 @@
     over_rows(tiles_ref, held, sems, one_row)
 
 
-def aggregate(edge_tiles, block_cols, parts, me):
+def aggregate(edge_tiles, block_cols, parts, me, order):
     blocks, _, size, _ = edge_tiles.shape
     feat = parts[0].shape[2]
     anywhere = pl.BlockSpec(memory_space=pl.ANY)
     return pl.pallas_call(
         aggregate_kernel,
         out_shape=jax.ShapeDtypeStruct((blocks, size, feat), BF16),
-        in_specs=[SMEM, SMEM, anywhere] + [anywhere] * len(parts),
+        in_specs=[SMEM, SMEM, anywhere] + [anywhere] * (len(parts) + 1),
         out_specs=VMEM,
         scratch_shapes=[
             pltpu.VMEM(edge_tiles.shape, BF16),
@@ -157,57 +157,65 @@
         compiler_params=PARAMS,
         cost_estimate=pl.CostEstimate(flops=2 * edge_tiles.size * feat, bytes_accessed=30_000_000, transcendentals=0),
         name="aggregate",
-    )(block_cols, me, edge_tiles, *parts)
+    )(block_cols, me, edge_tiles, *parts, order)
 
 
 def finish_kernel(last, *refs):
-    parts, out_ref = refs[:-1], refs[-1]
+    parts, (out_ref, *groups) = refs[: 2 * GROUPS], refs[2 * GROUPS :]
     count = parts[0].shape[0]
-    for g in range(len(parts) // 2):
+    for g in range(GROUPS):
         for b in range(count):
             total = parts[2 * g][b].astype(F32) + parts[2 * g + 1][b].astype(F32)
-            out_ref[g * count + b] = (total.T if last else total).astype(BF16)
+            total = (total.T if last else total).astype(BF16)
+            out_ref[g * count + b] = total
+            if not last:
+                groups[g][b] = total
 
 
 def finish(parts, last):
     count, feat, size = parts[0].shape
+    shape = (size, feat) if last else (feat, size)
+    outs = [jax.ShapeDtypeStruct((count * GROUPS,) + shape, BF16)]
+    if not last:
+        outs += [jax.ShapeDtypeStruct((count,) + shape, BF16)] * GROUPS
     return pl.pallas_call(
         functools.partial(finish_kernel, last),
-        out_shape=jax.ShapeDtypeStruct((count * len(parts) // 2,) + ((size, feat) if last else (feat, size)), BF16),
+        out_shape=outs,
         in_specs=[VMEM] * len(parts),
-        out_specs=VMEM,
+        out_specs=[VMEM] * len(outs),
         compiler_params=PARAMS,
         cost_estimate=pl.CostEstimate(flops=0, bytes_accessed=1_000_000_000 if last else 1, transcendentals=0),
         name="finish",
     )(*parts)
 
 
-def dense_kernel(cols, masked, col_ref, weight_ref, *rest):
+def dense_kernel(cols, start, masked, col_ref, weight_ref, *rest):
     shards, rest = rest[:cols], rest[cols:]
     side_ref, rest = rest[0], rest[1:]
     if masked:
         mask_ref, rest = rest[0], rest[1:]
     out_ref, grad_ref, whole_ref = rest
-    blocks, feat, size = shards[0].shape
+    blocks, feat, size = out_ref.shape
+    at = lambda ref, b: ref[b + start] if ref.shape[0] > blocks else ref[b]
     for m in range(cols):
         place = jnp.bitwise_xor(col_ref[0], m)
         for b in range(blocks):
-            whole_ref[place, :, b * size : (b + 1) * size] = shards[m][b]
+            whole_ref[place, :, b * size : (b + 1) * size] = at(shards[m], b)
     whole = jnp.concatenate([whole_ref[q] for q in range(cols)], axis=0)
     res = jnp.dot(weight_ref[...], whole, preferred_element_type=F32)
     for b in range(blocks):
-        part = res[:, b * size : (b + 1) * size]
-        out_ref[b] = (part * mask_ref[b].astype(F32) if masked else part).astype(BF16)
-    side = jnp.concatenate([side_ref[b] for b in range(blocks)], axis=0)
+        block = res[:, b * size : (b + 1) * size]
+        out_ref[b] = (block * at(mask_ref, b).astype(F32) if masked else block).astype(BF16)
+    side = jnp.concatenate([at(side_ref, b) for b in range(blocks)], axis=0)
     grad_ref[...] = jnp.dot(whole, side, preferred_element_type=F32)
 
 
-def dense(weight, shards, side, mask, col):
-    blocks, feat, size = shards[0].shape
-    cols = len(shards)
+def dense(weight, shards, side, mask, col, g):
+    _, feat, size = shards[0].shape
+    cols, blocks = len(shards), side.shape[0] // GROUPS
     args = [weight, *shards, side] + ([] if mask is None else [mask])
     return pl.pallas_call(
-        functools.partial(dense_kernel, cols, mask is not None),
+        functools.partial(dense_kernel, cols, g * blocks, mask is not None),
         out_shape=[
             jax.ShapeDtypeStruct((blocks, feat, size), BF16),
             jax.ShapeDtypeStruct((cols * feat, side.shape[2]), F32),
@@ -274,11 +282,8 @@
     return done, beside
 
 
-def gather_columns(own, cols):
-    if cols == 4:
-        near, far = lax.optimization_barrier((swap(own, 1, "col"), swap(own, 3, "col")))
-        return [own, near, swap(far, 1, "col"), far]
-    return [own] + [swap(own, m, "col") for m in range(1, cols)]
+def hop(shard, m):
+    return swap(shard, m, "col")
 
 
 def over_chips(value, masks):
@@ -301,41 +306,60 @@
     blocked = lambda v: v.reshape(v.shape[0] // size, size, v.shape[1])
     after = lax.optimization_barrier
 
-    parts = {0: blocked(node_feats)}
+    *pieces, mask = spread(edge_tiles, block_cols, [blocked(grad_out)], me_at, rows, blocked(relu_mask))
+    terms, node_feats = scatter(pieces, rows, blocked(node_feats))
+    hidden = blocked(hidden_act)
+    parts = {0: node_feats, 1: swap(node_feats, 1, "row")}
+    own, *groups = finish([t for pair in terms for t in pair], False)
+    own, parts = after((own, parts))
     for rel in chips:
         parts[rel] = swap(parts[0], rel, "row")
-    *pieces, mask = spread(edge_tiles, block_cols, [blocked(grad_out)], me_at, rows, blocked(relu_mask))
-    pieces, parts = after((pieces, parts))
-    terms, parts = scatter(pieces, rows, parts)
-    for rel in [0] + chips:
+    if cols == 4:
+        near, far = hop(own, 1), [hop(group, 3) for group in groups]
+        shards = [[groups[0], near, hop(far[0], 1), far[0]]]
+        near, far[1], shards, parts = after((near, far[1], shards, parts))
+        shards.append([groups[1], near, hop(far[1], 1), far[1]])
+    else:
+        shards = [[group] + [hop(group, m) for m in range(1, cols)] for group in groups]
+    for rel in chips:
         parts[rel + 1] = swap(parts[rel], 1, "row")
-    hidden = blocked(hidden_act)
-    owns = [finish(terms[g], False) for g in range(GROUPS)]
-    owns, parts = after((owns, parts))
+    shards[0], parts = after((shards[0], parts))
     for rel in range(2, rows, 2):
         top = 1 << (rel.bit_length() - 1)
         if rel not in parts:
             parts[rel] = swap(parts[rel - top], top, "row")
-    deltas, seconds, inputs, firsts = [], [], [], []
-    for g in range(GROUPS):
-        delta, grad = dense(weight_two, gather_columns(owns[g], cols), cut(hidden, g), cut(mask, g), col_at)
-        deltas.append(delta)
-        seconds.append(grad)
-    deltas[-1], parts = after((deltas[-1], parts))
+    delta, second = dense(weight_two, shards[0], hidden, mask, col_at, 0)
+    deltas, seconds, inputs, firsts = [delta], [second], [], []
+    if cols == 4:
+        near, far = [hop(delta, 1)], [hop(delta, 3)]
+    delta, second = dense(weight_two, shards[1], hidden, mask, col_at, 1)
+    deltas.append(delta)
+    seconds.append(second)
+    order = delta
+    if cols == 4:
+        near[0], far[0], parts, order = after((near[0], far[0], parts, order))
+        shards = [[deltas[0], near[0], hop(far[0], 1), far[0]]]
+        near.append(hop(delta, 1))
+        far.append(hop(delta, 3))
+    else:
+        shards = [[delta] + [hop(delta, m) for m in range(1, cols)] for delta in deltas]
     for rel in range(1, rows, 2):
         if rel not in parts:
             parts[rel] = swap(parts[rel - 1], 1, "row")
-    agg_feats = aggregate(edge_tiles, block_cols, [parts[rel] for rel in range(rows)], me_at)
+    agg_feats = aggregate(edge_tiles, block_cols, [parts[rel] for rel in range(rows)], me_at, order)
+    if cols == 4:
+        near[1], far[1], agg_feats = after((near[1], far[1], agg_feats))
+        shards.append([deltas[1], near[1], hop(far[1], 1), far[1]])
     for g in range(GROUPS):
-        out, grad = dense(weight_one, gather_columns(deltas[g], cols), cut(agg_feats, g), None, col_at)
+        out, grad = dense(weight_one, shards[g], agg_feats, None, col_at, g)
         inputs.append(out)
         firsts.append(grad)
     pieces = spread(edge_tiles, block_cols, inputs, me_at, rows)
     keep, send = weight_terms(firsts, seconds, me_at)
-    value = over_chips(keep + swap(send, 1, "row").astype(F32), chips[:1])
+    value = over_chips(keep + swap(send, 1, "row").astype(F32), chips[-1:])
     terms, value = scatter(pieces, rows, value)
-    terms, value = after((terms, over_chips(value, chips[1:])))
-    out = finish([t for pair in terms for t in pair], True)
+    terms, value = after((terms, over_chips(value, chips[:-1])))
+    (out,) = finish([t for pair in terms for t in pair], True)
     other = swap(value, 1, "row")
     even = me % 2 == 0
     first_grad, second_grad = jnp.where(even, other, value), jnp.where(even, value, other)

time: 163 us -> 165 us (1.012)
  waiting for transfers between devices: 90.5 us -> 82.5 us
  local copies, waits for them, and re-layouts: 8.26 us -> 14.9 us
  starting transfers between devices: 32.5 us -> 38.6 us
  Pallas kernels: 27 us -> 24.8 us
    ppermute x35 -> x34, waiting for transfers between devices: 90.5 us -> 82.5 us  [swap(): lax.ppermute(value, axis, [(i, i ^ mask) for i in range(lax.axis_size(axi...]
    unnamed x24 -> x46, local copies, waits for them, and re-layouts: 7.08 us -> 14.9 us
    ppermute x35 -> x34, starting transfers between devices: 32.5 us -> 38.6 us  [swap(): lax.ppermute(value, axis, [(i, i ^ mask) for i in range(lax.axis_size(axi...]
    pallas_call x7 -> x6, Pallas kernels: 6.62 us -> 4.53 us  [the longest x4 3.4 us: dense(): pl.pallas_call(functools.partial(dense_kernel, cols, g * blocks, mask is...]
  transfers between devices with their start and end apart: 35 -> 34, of which waited for: 23 -> 20; matrix products, arithmetic and copies ran while one was open for 2% -> 1% of each run, Pallas kernels for 12% -> 6%
where the time goes in v10:
time: 165 us
  waiting for transfers between devices  82.5 us (50%)
  starting transfers between devices  38.6 us (23%)
  Pallas kernels  24.8 us (15%)
  local copies, waits for them, and re-layouts  14.9 us (9%)
  other arithmetic  3.13 us (2%)
    ppermute x34, waiting for transfers between devices, swap(): lax.ppermute(value, axis, [(i, i ^ mask) for i in range(lax.axis_size(axi...  82.5 us
    ppermute x34, starting transfers between devices, swap(): lax.ppermute(value, axis, [(i, i ^ mask) for i in range(lax.axis_size(axi...  38.6 us
    unnamed x46, local copies, waits for them, and re-layouts  14.9 us
    pallas_call x2, Pallas kernels, spread(): pl.pallas_call(functools.partial(spread_kernel, first, len(vals)), out_sh...  13.7 us
    pallas_call x1, Pallas kernels, aggregate(): pl.pallas_call(aggregate_kernel, out_shape=jax.ShapeDtypeStruct((blocks,...  6.28 us
    pallas_call x4, Pallas kernels, dense(): pl.pallas_call(functools.partial(dense_kernel, cols, g * blocks, mask is...  3.4 us
  transfers between devices with their start and end apart: 34, of which 20 were waited for; matrix products, arithmetic and copies ran while one was open for 1% of the time, Pallas kernels for 6%

profile of v10, /device:TPU:0, one launch (start us, length us, event | category | flops | bytes accessed | tf_op | source)
XLA Modules:
  0.0 164.8 jit_solution(13023273006743530614)
XLA Ops:
  0.7 1.1 copy-done.9
  1.7 0.7 copy-done.21
  2.4 7.0 %spread.2 = (bf16[4,8,128,128]{3,2,1,0:T(8,128)(2,1)S(1)}, bf16[4,8,128,128]{3,2,1,0:T(8,128)(2,1)S(1)}, bf16[4,8,128,128]{3,2,1,0:T(8,128)(2,1)S(1)}, bf16[4,8,...) custom-call(s32[16,20]{1,0:T(8,128)S(1)} %copy-done.21, s32[1]{0:T(128)} %bitcast.me_ref, ...), custom_call_target="tpu_custom_call" | custom-call | flops 1342177280 | bytes 30000000 | tf_op jit(solution)/shard_map/spread/pallas_call | solution.py:105
  10.1 2.2 %collective-permute-done = bf16[4,8,128,128]{3,2,1,0:T(8,128)(2,1)S(1)} collective-permute-done((bf16[4,8,128,128]{3,2,1,0:T(8,128)(2,1)S(1)}, bf16[4,8,128,128]{3,2,1,0:T(8,128)(2,1)S(1)}, u32[]{:S(2)}, u32[]{:S(2)}) %collective-permute-start) | collective-permute-done | bytes 1048608 | tf_op jit(solution)/shard_map/ppermute | solution.py:252
  12.8 2.9 %collective-permute-start.1 = (bf16[2,8,128,128]{3,2,1,0:T(8,128)(2,1)S(1)}, bf16[2,8,128,128]{3,2,1,0:T(8,128)(2,1)S(1)}, u32[]{:S(2)}, u32[]{:S(2)}) collective-permute-start(bf16[2,8,128,128]{3,2,1,0:T(8,128)(2,1)S(1)} %get-tuple-element.151), channel_id=1, source_target_pairs={{0,8},{4,12},{8,0},{12,4},{16,24},{20,28},{24,16},{28,20},{1,9},{5... | collective-permute-start | bytes 1572872 | tf_op jit(solution)/shard_map/ppermute | solution.py:252
  16.1 1.6 collective-permute-start.4
  17.7 10.3 %collective-permute-done.1 = bf16[2,8,128,128]{3,2,1,0:T(8,128)(2,1)S(1)} collective-permute-done((bf16[2,8,128,128]{3,2,1,0:T(8,128)(2,1)S(1)}, bf16[2,8,128,128]{3,2,1,0:T(8,128)(2,1)S(1)}, u32[]{:S(2)}, u32[]{:S(2)}) %collective-permute-start.1) | collective-permute-done | bytes 524320 | tf_op jit(solution)/shard_map/ppermute | solution.py:252
  27.9 1.9 %collective-permute-done.4 = bf16[2,8,128,128]{3,2,1,0:T(8,128)(2,1)S(1)} collective-permute-done((bf16[2,8,128,128]{3,2,1,0:T(8,128)(2,1)S(1)}, bf16[2,8,128,128]{3,2,1,0:T(8,128)(2,1)S(1)}, u32[]{:S(2)}, u32[]{:S(2)}) %collective-permute-start.4) | collective-permute-done | bytes 524320 | tf_op jit(solution)/shard_map/ppermute | solution.py:252
  30.0 1.3 collective-permute-start.5
  31.4 1.6 collective-permute-start.2
  33.0 5.7 %collective-permute-done.5.refs_3_ = bf16[8,128,128]{2,1,0:T(8,128)(2,1)S(1)} collective-permute-done((bf16[8,128,128]{2,1,0:T(8,128)(2,1)S(1)}, bf16[8,128,128]{2,1,0:T(8,128)(2,1)S(1)}, u32[]{:S(2)}, u32[]{:S(2)}) %collective-permute-start.5) | collective-permute-done | bytes 262176 | tf_op jit(solution)/shard_map/ppermute | solution.py:252
  38.8 1.2 collective-permute-done.2.refs_1_
  40.1 3.7 %collective-permute-start.9 = (bf16[8,128,128]{2,1,0:T(8,128)(2,1)S(1)}, bf16[8,128,128]{2,1,0:T(8,128)(2,1)S(1)}, u32[]{:S(2)}, u32[]{:S(2)}) collective-permute-start(bf16[8,128,128]{2,1,0:T(8,128)(2,1)S(1)} %get-tuple-element.96.rest_0_), channel_id=1, source_target_pairs={{0,3},{1,2},{2,1},{3,0},{4,7},{5,6},{6,5},{7,4},{8,11},{9,10},{10,... | collective-permute-start | bytes 786440 | tf_op jit(solution)/shard_map/ppermute | solution.py:252
  43.7 0.7 copy-done.13
  44.4 0.8 collective-permute-start.11
  45.2 1.5 collective-permute-start.12
  46.8 0.9 collective-permute-start.8
  47.7 0.7 copy-done.11
  48.4 2.8 %collective-permute-done.9.rest_3_ = bf16[8,128,128]{2,1,0:T(8,128)(2,1)S(1)} collective-permute-done((bf16[8,128,128]{2,1,0:T(8,128)(2,1)S(1)}, bf16[8,128,128]{2,1,0:T(8,128)(2,1)S(1)}, u32[]{:S(2)}, u32[]{:S(2)}) %collective-permute-start.9) | collective-permute-done | bytes 262176 | tf_op jit(solution)/shard_map/ppermute | solution.py:252
  51.2 4.8 %collective-permute-start.10 = (bf16[8,128,128]{2,1,0:T(8,128)(2,1)S(1)}, bf16[8,128,128]{2,1,0:T(8,128)(2,1)S(1)}, u32[]{:S(2)}, u32[]{:S(2)}) collective-permute-start(bf16[8,128,128]{2,1,0:T(8,128)(2,1)S(1)} %collective-permute-done.9.rest_3_), channel_id=1, source_target_pairs={{0,1},{1,0},{2,3},{3,2},{4,5},{5,4},{6,7},{7,6},{8,9},{9,8},{10,11... | collective-permute-start | bytes 786440 | tf_op jit(solution)/shard_map/ppermute | solution.py:252
  56.0 0.7 copy-done.15
  56.7 11.4 %collective-permute-done.8.rest_3_ = bf16[8,128,128]{2,1,0:T(8,128)(2,1)S(1)} collective-permute-done((bf16[8,128,128]{2,1,0:T(8,128)(2,1)S(1)}, bf16[8,128,128]{2,1,0:T(8,128)(2,1)S(1)}, u32[]{:S(2)}, u32[]{:S(2)}) %collective-permute-start.8) | collective-permute-done | bytes 262176 | tf_op jit(solution)/shard_map/ppermute | solution.py:252
  68.0 4.2 %collective-permute-done.10.rest_2_ = bf16[8,128,128]{2,1,0:T(8,128)(2,1)S(1)} collective-permute-done((bf16[8,128,128]{2,1,0:T(8,128)(2,1)S(1)}, bf16[8,128,128]{2,1,0:T(8,128)(2,1)S(1)}, u32[]{:S(2)}, u32[]{:S(2)}) %collective-permute-start.10) | collective-permute-done | bytes 262176 | tf_op jit(solution)/shard_map/ppermute | solution.py:252
  72.2 0.7 copy-done.19
  73.5 0.8 copy-done.2
  74.9 0.8 copy-done.4
  75.7 0.8 copy-done.6
  76.5 1.5 collective-permute-start.17
  78.0 1.7 %collective-permute-start.18 = (bf16[8,128,128]{2,1,0:T(8,128)(2,1)}, bf16[8,128,128]{2,1,0:T(8,128)(2,1)S(1)}, u32[]{:S(2)}, u32[]{:S(2)}) collective-permute-start(bf16[8,128,128]{2,1,0:T(8,128)(2,1)} %copy-done.17), channel_id=1, source_target_pairs={{0,1},{1,0},{2,3},{3,2},{4,5},{5,4},{6,7},{7,6},{8,9},{9,8},{10,11... | collective-permute-start | bytes 786440 | tf_op jit(solution)/shard_map/ppermute | solution.py:252
  79.7 0.9 copy-done.14
  80.6 0.9 copy-done.16
  81.6 0.9 copy-done.20
  82.5 0.8 dense.4
  83.8 3.1 %collective-permute-start.16 = (bf16[8,128,128]{2,1,0:T(8,128)(2,1)S(1)}, bf16[8,128,128]{2,1,0:T(8,128)(2,1)S(1)}, u32[]{:S(2)}, u32[]{:S(2)}) collective-permute-start(bf16[8,128,128]{2,1,0:T(8,128)(2,1)S(1)} %get-tuple-element.101.rest_0_), channel_id=1, source_target_pairs={{0,3},{1,2},{2,1},{3,0},{4,7},{5,6},{6,5},{7,4},{8,11},{9,10},{10,... | collective-permute-start | bytes 786440 | tf_op jit(solution)/shard_map/ppermute | solution.py:252
  86.9 0.9 copy-done.12
  87.8 0.9 copy-done.18
  88.8 0.8 dense.5
  89.6 2.6 %collective-permute-done.15.rest_1_ = bf16[8,128,128]{2,1,0:T(8,128)(2,1)S(1)} collective-permute-done((bf16[8,128,128]{2,1,0:T(8,128)(2,1)S(1)}, bf16[8,128,128]{2,1,0:T(8,128)(2,1)S(1)}, u32[]{:S(2)}, u32[]{:S(2)}) %collective-permute-start.15) | collective-permute-done | bytes 262176 | tf_op jit(solution)/shard_map/ppermute | solution.py:252
  92.2 6.6 %collective-permute-done.16.rest_3_ = bf16[8,128,128]{2,1,0:T(8,128)(2,1)S(1)} collective-permute-done((bf16[8,128,128]{2,1,0:T(8,128)(2,1)S(1)}, bf16[8,128,128]{2,1,0:T(8,128)(2,1)S(1)}, u32[]{:S(2)}, u32[]{:S(2)}) %collective-permute-start.16) | collective-permute-done | bytes 262176 | tf_op jit(solution)/shard_map/ppermute | solution.py:252
  98.9 2.2 %collective-permute-start.21 = (bf16[8,128,128]{2,1,0:T(8,128)(2,1)S(1)}, bf16[8,128,128]{2,1,0:T(8,128)(2,1)S(1)}, u32[]{:S(2)}, u32[]{:S(2)}) collective-permute-start(bf16[8,128,128]{2,1,0:T(8,128)(2,1)S(1)} %get-tuple-element.120.rest_8_.rest_0_), channel_id=1, source_target_pairs={{0,3},{1,2},{2,1},{3,0},{4,7},{5,6},{6,5},{7,4},{8,11},{9,10},{10,... | collective-permute-start | bytes 786440 | tf_op jit(solution)/shard_map/ppermute | solution.py:252
  101.1 1.1 collective-permute-start.19
  102.1 1.0 copy-done.3
  103.2 1.0 copy-done.5
  104.2 1.0 copy-done.7
  105.3 6.3 %aggregate.1.rest_4_ = bf16[16,128,128]{2,1,0:T(8,128)(2,1)S(1)} custom-call(s32[16,20]{1,0:T(8,128)S(1)} %copy-done.22, s32[1]{0:T(128)} %bitcast.me_ref, bf16[16,20,128,128]{3,2,1,0:T(8,128)(2,1)} %tiles_ref.5, bf16[16,128,128]{2,1,0:T(8,128)(2,1)S(1)} %bitcast.58, bf16[16,128,128]{2,1,0:T(8,128)(2,1)S(1)} %collective-permute-done.6.rest_1_, ...), custom_call_target="tpu_custom_call" | custom-call | flops 1342177280 | bytes 30000000 | tf_op jit(solution)/shard_map/aggregate/pallas_call | solution.py:147
  111.6 2.3 %collective-permute-done.21.rest_3_ = bf16[8,128,128]{2,1,0:T(8,128)(2,1)S(1)} collective-permute-done((bf16[8,128,128]{2,1,0:T(8,128)(2,1)S(1)}, bf16[8,128,128]{2,1,0:T(8,128)(2,1)S(1)}, u32[]{:S(2)}, u32[]{:S(2)}) %collective-permute-start.21) | collective-permute-done | bytes 262176 | tf_op jit(solution)/shard_map/ppermute | solution.py:252
  113.8 1.1 collective-permute-start.23
  114.9 4.3 %collective-permute-done.19.rest_2_ = bf16[8,128,128]{2,1,0:T(8,128)(2,1)S(1)} collective-permute-done((bf16[8,128,128]{2,1,0:T(8,128)(2,1)S(1)}, bf16[8,128,128]{2,1,0:T(8,128)(2,1)S(1)}, u32[]{:S(2)}, u32[]{:S(2)}) %collective-permute-start.19) | collective-permute-done | bytes 262176 | tf_op jit(solution)/shard_map/ppermute | solution.py:252
  119.2 0.9 dense.6
  120.1 4.4 %collective-permute-done.23.rest_2_ = bf16[8,128,128]{2,1,0:T(8,128)(2,1)S(1)} collective-permute-done((bf16[8,128,128]{2,1,0:T(8,128)(2,1)S(1)}, bf16[8,128,128]{2,1,0:T(8,128)(2,1)S(1)}, u32[]{:S(2)}, u32[]{:S(2)}) %collective-permute-start.23) | collective-permute-done | bytes 262176 | tf_op jit(solution)/shard_map/ppermute | solution.py:252
  124.4 0.8 dense.7
  125.3 6.7 %spread.3 = (bf16[4,8,128,128]{3,2,1,0:T(8,128)(2,1)S(1)}, bf16[4,8,128,128]{3,2,1,0:T(8,128)(2,1)S(1)}, bf16[4,8,128,128]{3,2,1,0:T(8,128)(2,1)S(1)}, bf16[4,8,128,128]{3,2,1,0:T(8,128)(2,1)S(1)}) custom-call(s32[16,20]{1,0:T(8,128)S(1)} %copy-done.22, s32[1]{0:T(128)} %bitcast.me_ref, bf16[16,20,128,128]{3,2,1,0:T(8,128)(2,1)} %tiles_ref.5, ...), custom_call_target="tpu_custom_call" | custom-call | flops 1342177280 | bytes 30000000 | tf_op jit(solution)/shard_map/spread/pallas_call | solution.py:105
  132.9 1.8 %collective-permute-done.29 = bf16[4,8,128,128]{3,2,1,0:T(8,128)(2,1)S(1)} collective-permute-done((bf16[4,8,128,128]{3,2,1,0:T(8,128)(2,1)S(1)}, bf16[4,8,128,128]{3,2,1,0:T(8,128)(2,1)S(1)}, u32[]{:S(2)}, u32[]{:S(2)}) %collective-permute-start.29) | collective-permute-done | bytes 1048608 | tf_op jit(solution)/shard_map/ppermute | solution.py:252
  135.1 1.0 collective-permute-start.30
  136.7 1.3 collective-permute-start.25
  138.0 1.0 collective-permute-start.27
  139.0 12.9 %collective-permute-done.27 = bf16[128,512]{1,0:T(8,128)(2,1)S(1)} collective-permute-done((bf16[128,512]{1,0:T(8,128)(2,1)S(1)}, bf16[128,512]{1,0:T(8,128)(2,1)S(1)}, u32[]{:S(2)}, u32[]{:S(2)}) %collective-permute-start.27) | collective-permute-done | bytes 131104 | tf_op jit(solution)/shard_map/ppermute | solution.py:252
  152.0 1.3 collective-permute-start.32
  153.4 0.9 collective-permute-start.31
  154.4 1.0 collective-permute-start.28
  155.5 3.0 %collective-permute-done.32 = bf16[128,512]{1,0:T(8,128)(2,1)S(1)} collective-permute-done((bf16[128,512]{1,0:T(8,128)(2,1)S(1)}, bf16[128,512]{1,0:T(8,128)(2,1)S(1)}, u32[]{:S(2)}, u32[]{:S(2)}) %collective-permute-start.32) | collective-permute-done | bytes 131104 | tf_op jit(solution)/shard_map/ppermute | solution.py:252
  158.5 3.9 %collective-permute-done.31.refs_3_ = bf16[8,128,128]{2,1,0:T(8,128)(2,1)S(1)} collective-permute-done((bf16[8,128,128]{2,1,0:T(8,128)(2,1)S(1)}, bf16[8,128,128]{2,1,0:T(8,128)(2,1)S(1)}, u32[]{:S(2)}, u32[]{:S(2)}) %collective-permute-start.31) | collective-permute-done | bytes 262176 | tf_op jit(solution)/shard_map/ppermute | solution.py:252
  162.4 1.0 finish.3
  163.9 0.8 broadcast_select_fusion
  (72 shorter events, 6.2 us)
Async XLA Ops:
  0.6 29.2 %copy-start.1 = (bf16[2048,128]{1,0:T(8,128)(2,1)S(1)}, bf16[2048,128]{1,0:T(8,128)(2,1)}, u32[]{:S(2)}) copy-start(bf16[2048,128]{1,0:T(8,128)(2,1)} %param.8) | copy-start | bytes 1572868
  0.6 1.1 copy-start.9
  1.7 0.7 copy-start.21
  2.4 77.2 %copy-start = (bf16[2048,128]{1,0:T(8,128)(2,1)S(1)}, bf16[2048,128]{1,0:T(8,128)(2,1)}, u32[]{:S(2)}) copy-start(bf16[2048,128]{1,0:T(8,128)(2,1)} %param.9) | copy-start | bytes 1572868
  2.4 77.2 %copy-start.10 = (bf16[128,512]{1,0:T(8,128)(2,1)S(1)}, bf16[128,512]{1,0:T(8,128)(2,1)}, u32[]{:S(2)}) copy-start(bf16[128,512]{1,0:T(8,128)(2,1)} %weight_ref.5) | copy-start | bytes 393220
  9.5 92.6 %copy-start.22 = (s32[16,20]{1,0:T(8,128)S(1)}, s32[16,20]{1,0:T(8,128)}, u32[]{:S(2)}) copy-start(s32[16,20]{1,0:T(8,128)} %cols_ref.5) | copy-start | bytes 3844
  9.5 2.8 %collective-permute-start = (bf16[4,8,128,128]{3,2,1,0:T(8,128)(2,1)S(1)}, bf16[4,8,128,128]{3,2,1,0:T(8,128)(2,1)S(1)}, u32[]{:S(2)}, u32[]{:S(2)}) collective-permute-start(bf16[4,8,128,128]{3,2,1,0:T(8,128)(2,1)S(1)} %get-tuple-element.75), channel_id=1, source_target_pairs={{0,4},{4,0},{8,12},{12,8},{16,20},{20,16},{24,28},{28,24},{1,5},{5... | collective-permute-start | bytes 3145736 | tf_op jit(solution)/shard_map/ppermute | solution.py:252
  10.0 5.7 %collective-permute-start.3 = (bf16[4,8,128,128]{3,2,1,0:T(8,128)(2,1)S(1)}, bf16[4,8,128,128]{3,2,1,0:T(8,128)(2,1)S(1)}, u32[]{:S(2)}, u32[]{:S(2)}) collective-permute-start(bf16[4,8,128,128]{3,2,1,0:T(8,128)(2,1)S(1)} %get-tuple-element.78), channel_id=1, source_target_pairs={{0,4},{4,0},{8,12},{12,8},{16,20},{20,16},{24,28},{28,24},{1,5},{5... | collective-permute-start | bytes 3145736 | tf_op jit(solution)/shard_map/ppermute | solution.py:252
  12.8 15.2 %collective-permute-start.1 = (bf16[2,8,128,128]{3,2,1,0:T(8,128)(2,1)S(1)}, bf16[2,8,128,128]{3,2,1,0:T(8,128)(2,1)S(1)}, u32[]{:S(2)}, u32[]{:S(2)}) collective-permute-start(bf16[2,8,128,128]{3,2,1,0:T(8,128)(2,1)S(1)} %get-tuple-element.151), channel_id=1, source_target_pairs={{0,8},{4,12},{8,0},{12,4},{16,24},{20,28},{24,16},{28,20},{1,9},{5... | collective-permute-start | bytes 1572872 | tf_op jit(solution)/shard_map/ppermute | solution.py:252
  16.1 13.8 %collective-permute-start.4 = (bf16[2,8,128,128]{3,2,1,0:T(8,128)(2,1)S(1)}, bf16[2,8,128,128]{3,2,1,0:T(8,128)(2,1)S(1)}, u32[]{:S(2)}, u32[]{:S(2)}) collective-permute-start(bf16[2,8,128,128]{3,2,1,0:T(8,128)(2,1)S(1)} %get-tuple-element.149), channel_id=1, source_target_pairs={{0,16},{4,20},{8,24},{12,28},{16,0},{20,4},{24,8},{28,12},{1,17},{... | collective-permute-start | bytes 1572872 | tf_op jit(solution)/shard_map/ppermute | solution.py:252
  29.8 14.6 %collective-permute-start.6 = (bf16[16,128,128]{2,1,0:T(8,128)(2,1)S(1)}, bf16[16,128,128]{2,1,0:T(8,128)(2,1)S(1)}, u32[]{:S(2)}, u32[]{:S(2)}) collective-permute-start(bf16[16,128,128]{2,1,0:T(8,128)(2,1)S(1)} %bitcast.55), channel_id=1, source_target_pairs={{0,4},{4,0},{8,12},{12,8},{16,20},{20,16},{24,28},{28,24},{1,5},{5... | collective-permute-start | bytes 1572872 | tf_op jit(solution)/shard_map/ppermute | solution.py:252
  30.0 8.8 %collective-permute-start.5 = (bf16[8,128,128]{2,1,0:T(8,128)(2,1)S(1)}, bf16[8,128,128]{2,1,0:T(8,128)(2,1)S(1)}, u32[]{:S(2)}, u32[]{:S(2)}) collective-permute-start(bf16[8,128,128]{2,1,0:T(8,128)(2,1)S(1)} %get-tuple-element.157), channel_id=1, source_target_pairs={{0,8},{4,12},{8,0},{12,4},{16,24},{20,28},{24,16},{28,20},{1,9},{5... | collective-permute-start | bytes 786440 | tf_op jit(solution)/shard_map/ppermute | solution.py:252
  31.4 8.5 %collective-permute-start.2 = (bf16[8,128,128]{2,1,0:T(8,128)(2,1)S(1)}, bf16[8,128,128]{2,1,0:T(8,128)(2,1)S(1)}, u32[]{:S(2)}, u32[]{:S(2)}) collective-permute-start(bf16[8,128,128]{2,1,0:T(8,128)(2,1)S(1)} %get-tuple-element.159), channel_id=1, source_target_pairs={{0,16},{4,20},{8,24},{12,28},{16,0},{20,4},{24,8},{28,12},{1,17},{... | collective-permute-start | bytes 786440 | tf_op jit(solution)/shard_map/ppermute | solution.py:252
  40.1 79.1 %copy-start.8 = (bf16[128,512]{1,0:T(8,128)(2,1)S(1)}, bf16[128,512]{1,0:T(8,128)(2,1)}, u32[]{:S(2)}) copy-start(bf16[128,512]{1,0:T(8,128)(2,1)} %weight_ref.7) | copy-start | bytes 393220
  40.1 11.1 %collective-permute-start.9 = (bf16[8,128,128]{2,1,0:T(8,128)(2,1)S(1)}, bf16[8,128,128]{2,1,0:T(8,128)(2,1)S(1)}, u32[]{:S(2)}, u32[]{:S(2)}) collective-permute-start(bf16[8,128,128]{2,1,0:T(8,128)(2,1)S(1)} %get-tuple-element.96.rest_0_), channel_id=1, source_target_pairs={{0,3},{1,2},{2,1},{3,0},{4,7},{5,6},{6,5},{7,4},{8,11},{9,10},{10,... | collective-permute-start | bytes 786440 | tf_op jit(solution)/shard_map/ppermute | solution.py:252
  43.7 0.7 copy-start.13
  44.4 28.4 %collective-permute-start.11 = (bf16[16,128,128]{2,1,0:T(8,128)(2,1)S(1)}, bf16[16,128,128]{2,1,0:T(8,128)(2,1)S(1)}, u32[]{:S(2)}, u32[]{:S(2)}) collective-permute-start(bf16[16,128,128]{2,1,0:T(8,128)(2,1)S(1)} %bitcast.56), channel_id=1, source_target_pairs={{0,8},{4,12},{8,0},{12,4},{16,24},{20,28},{24,16},{28,20},{1,9},{5... | collective-permute-start | bytes 1572872 | tf_op jit(solution)/shard_map/ppermute | solution.py:252
  45.2 27.7 %collective-permute-start.12 = (bf16[16,128,128]{2,1,0:T(8,128)(2,1)S(1)}, bf16[16,128,128]{2,1,0:T(8,128)(2,1)S(1)}, u32[]{:S(2)}, u32[]{:S(2)}) collective-permute-start(bf16[16,128,128]{2,1,0:T(8,128)(2,1)S(1)} %bitcast.57), channel_id=1, source_target_pairs={{0,16},{4,20},{8,24},{12,28},{16,0},{20,4},{24,8},{28,12},{1,17},{... | collective-permute-start | bytes 1572872 | tf_op jit(solution)/shard_map/ppermute | solution.py:252
  46.8 26.1 %collective-permute-start.7 = (bf16[16,128,128]{2,1,0:T(8,128)(2,1)S(1)}, bf16[16,128,128]{2,1,0:T(8,128)(2,1)S(1)}, u32[]{:S(2)}, u32[]{:S(2)}) collective-permute-start(bf16[16,128,128]{2,1,0:T(8,128)(2,1)S(1)} %get-tuple-element.83), channel_id=1, source_target_pairs={{0,1},{1,0},{2,3},{3,2},{4,5},{5,4},{6,7},{7,6},{8,9},{9,8},{10,11... | collective-permute-start | bytes 1572872 | tf_op jit(solution)/shard_map/ppermute | solution.py:252
  46.8 21.3 %collective-permute-start.8 = (bf16[8,128,128]{2,1,0:T(8,128)(2,1)S(1)}, bf16[8,128,128]{2,1,0:T(8,128)(2,1)S(1)}, u32[]{:S(2)}, u32[]{:S(2)}) collective-permute-start(bf16[8,128,128]{2,1,0:T(8,128)(2,1)S(1)} %get-tuple-element.84.rest_0_), channel_id=1, source_target_pairs={{0,3},{1,2},{2,1},{3,0},{4,7},{5,6},{6,5},{7,4},{8,11},{9,10},{10,... | collective-permute-start | bytes 786440 | tf_op jit(solution)/shard_map/ppermute | solution.py:252
  47.7 0.7 copy-start.11
  51.2 21.0 %collective-permute-start.10 = (bf16[8,128,128]{2,1,0:T(8,128)(2,1)S(1)}, bf16[8,128,128]{2,1,0:T(8,128)(2,1)S(1)}, u32[]{:S(2)}, u32[]{:S(2)}) collective-permute-start(bf16[8,128,128]{2,1,0:T(8,128)(2,1)S(1)} %collective-permute-done.9.rest_3_), channel_id=1, source_target_pairs={{0,1},{1,0},{2,3},{3,2},{4,5},{5,4},{6,7},{7,6},{8,9},{9,8},{10,11... | collective-permute-start | bytes 786440 | tf_op jit(solution)/shard_map/ppermute | solution.py:252
  56.0 0.7 copy-start.15
  68.0 7.6 %copy-start.17 = (bf16[8,128,128]{2,1,0:T(8,128)(2,1)}, bf16[8,128,128]{2,1,0:T(8,128)(2,1)S(1)}, u32[]{:S(2)}) copy-start(bf16[8,128,128]{2,1,0:T(8,128)(2,1)S(1)} %collective-permute-done.8.rest_3_) | copy-start | bytes 786436
  72.2 0.7 copy-start.19
  72.9 2.0 %collective-permute-start.13 = (bf16[16,128,128]{2,1,0:T(8,128)(2,1)S(1)}, bf16[16,128,128]{2,1,0:T(8,128)(2,1)S(1)}, u32[]{:S(2)}, u32[]{:S(2)}) collective-permute-start(bf16[16,128,128]{2,1,0:T(8,128)(2,1)S(1)} %collective-permute-done.11.rest_2_), channel_id=1, source_target_pairs={{0,4},{4,0},{8,12},{12,8},{16,20},{20,16},{24,28},{28,24},{1,5},{5... | collective-permute-start | bytes 1572872 | tf_op jit(solution)/shard_map/ppermute | solution.py:252
  73.0 2.7 %collective-permute-start.14 = (bf16[16,128,128]{2,1,0:T(8,128)(2,1)S(1)}, bf16[16,128,128]{2,1,0:T(8,128)(2,1)S(1)}, u32[]{:S(2)}, u32[]{:S(2)}) collective-permute-start(bf16[16,128,128]{2,1,0:T(8,128)(2,1)S(1)} %collective-permute-done.12.rest_4_), channel_id=1, source_target_pairs={{0,4},{4,0},{8,12},{12,8},{16,20},{20,16},{24,28},{28,24},{1,5},{5... | collective-permute-start | bytes 1572872 | tf_op jit(solution)/shard_map/ppermute | solution.py:252
  73.5 0.8 copy-start.2
  74.9 0.8 copy-start.4
  75.7 0.8 copy-start.6
  76.5 22.4 %collective-permute-start.17 = (bf16[16,128,128]{2,1,0:T(8,128)(2,1)S(1)}, bf16[16,128,128]{2,1,0:T(8,128)(2,1)}, u32[]{:S(2)}, u32[]{:S(2)}) collective-permute-start(bf16[16,128,128]{2,1,0:T(8,128)(2,1)S(1)} %collective-permute-done.11.rest_2_), channel_id=1, source_target_pairs={{0,16},{4,20},{8,24},{12,28},{16,0},{20,4},{24,8},{28,12},{1,17},{... | collective-permute-start | bytes 1572872 | tf_op jit(solution)/shard_map/ppermute | solution.py:252
  78.0 8.9 %collective-permute-start.18 = (bf16[8,128,128]{2,1,0:T(8,128)(2,1)}, bf16[8,128,128]{2,1,0:T(8,128)(2,1)S(1)}, u32[]{:S(2)}, u32[]{:S(2)}) collective-permute-start(bf16[8,128,128]{2,1,0:T(8,128)(2,1)} %copy-done.17), channel_id=1, source_target_pairs={{0,1},{1,0},{2,3},{3,2},{4,5},{5,4},{6,7},{7,6},{8,9},{9,8},{10,11... | collective-permute-start | bytes 786440 | tf_op jit(solution)/shard_map/ppermute | solution.py:252
  79.7 1.0 copy-start.14
  80.6 0.9 copy-start.16
  81.6 0.9 copy-start.20
  83.4 8.8 %collective-permute-start.15 = (bf16[8,128,128]{2,1,0:T(8,128)(2,1)S(1)}, bf16[8,128,128]{2,1,0:T(8,128)(2,1)S(1)}, u32[]{:S(2)}, u32[]{:S(2)}) collective-permute-start(bf16[8,128,128]{2,1,0:T(8,128)(2,1)S(1)} %get-tuple-element.101.rest_0_), channel_id=1, source_target_pairs={{0,1},{1,0},{2,3},{3,2},{4,5},{5,4},{6,7},{7,6},{8,9},{9,8},{10,11... | collective-permute-start | bytes 786440 | tf_op jit(solution)/shard_map/ppermute | solution.py:252
  83.8 15.1 %collective-permute-start.16 = (bf16[8,128,128]{2,1,0:T(8,128)(2,1)S(1)}, bf16[8,128,128]{2,1,0:T(8,128)(2,1)S(1)}, u32[]{:S(2)}, u32[]{:S(2)}) collective-permute-start(bf16[8,128,128]{2,1,0:T(8,128)(2,1)S(1)} %get-tuple-element.101.rest_0_), channel_id=1, source_target_pairs={{0,3},{1,2},{2,1},{3,0},{4,7},{5,6},{6,5},{7,4},{8,11},{9,10},{10,... | collective-permute-start | bytes 786440 | tf_op jit(solution)/shard_map/ppermute | solution.py:252
  86.9 1.0 copy-start.12
  87.8 0.9 copy-start.18
  98.9 3.3 %collective-permute-start.22 = (bf16[16,128,128]{2,1,0:T(8,128)(2,1)}, bf16[16,128,128]{2,1,0:T(8,128)(2,1)S(1)}, u32[]{:S(2)}, u32[]{:S(2)}) collective-permute-start(bf16[16,128,128]{2,1,0:T(8,128)(2,1)} %collective-permute-done.17.rest_6_), channel_id=1, source_target_pairs={{0,4},{4,0},{8,12},{12,8},{16,20},{20,16},{24,28},{28,24},{1,5},{5... | collective-permute-start | bytes 1572872 | tf_op jit(solution)/shard_map/ppermute | solution.py:252
  98.9 12.7 %collective-permute-start.20 = (bf16[8,128,128]{2,1,0:T(8,128)(2,1)S(1)}, bf16[8,128,128]{2,1,0:T(8,128)(2,1)S(1)}, u32[]{:S(2)}, u32[]{:S(2)}) collective-permute-start(bf16[8,128,128]{2,1,0:T(8,128)(2,1)S(1)} %get-tuple-element.120.rest_8_.rest_0_), channel_id=1, source_target_pairs={{0,1},{1,0},{2,3},{3,2},{4,5},{5,4},{6,7},{7,6},{8,9},{9,8},{10,11... | collective-permute-start | bytes 786440 | tf_op jit(solution)/shard_map/ppermute | solution.py:252
  98.9 15.0 %collective-permute-start.21 = (bf16[8,128,128]{2,1,0:T(8,128)(2,1)S(1)}, bf16[8,128,128]{2,1,0:T(8,128)(2,1)S(1)}, u32[]{:S(2)}, u32[]{:S(2)}) collective-permute-start(bf16[8,128,128]{2,1,0:T(8,128)(2,1)S(1)} %get-tuple-element.120.rest_8_.rest_0_), channel_id=1, source_target_pairs={{0,3},{1,2},{2,1},{3,0},{4,7},{5,6},{6,5},{7,4},{8,11},{9,10},{10,... | collective-permute-start | bytes 786440 | tf_op jit(solution)/shard_map/ppermute | solution.py:252
  101.1 18.1 %collective-permute-start.19 = (bf16[8,128,128]{2,1,0:T(8,128)(2,1)S(1)}, bf16[8,128,128]{2,1,0:T(8,128)(2,1)S(1)}, u32[]{:S(2)}, u32[]{:S(2)}) collective-permute-start(bf16[8,128,128]{2,1,0:T(8,128)(2,1)S(1)} %collective-permute-done.16.rest_3_), channel_id=1, source_target_pairs={{0,1},{1,0},{2,3},{3,2},{4,5},{5,4},{6,7},{7,6},{8,9},{9,8},{10,11... | collective-permute-start | bytes 786440 | tf_op jit(solution)/shard_map/ppermute | solution.py:252
  102.1 1.0 copy-start.3
  103.2 1.0 copy-start.5
  104.2 1.0 copy-start.7
  113.8 10.6 %collective-permute-start.23 = (bf16[8,128,128]{2,1,0:T(8,128)(2,1)S(1)}, bf16[8,128,128]{2,1,0:T(8,128)(2,1)S(1)}, u32[]{:S(2)}, u32[]{:S(2)}) collective-permute-start(bf16[8,128,128]{2,1,0:T(8,128)(2,1)S(1)} %collective-permute-done.21.rest_3_), channel_id=1, source_target_pairs={{0,1},{1,0},{2,3},{3,2},{4,5},{5,4},{6,7},{7,6},{8,9},{9,8},{10,11... | collective-permute-start | bytes 786440 | tf_op jit(solution)/shard_map/ppermute | solution.py:252
  132.0 2.7 %collective-permute-start.29 = (bf16[4,8,128,128]{3,2,1,0:T(8,128)(2,1)S(1)}, bf16[4,8,128,128]{3,2,1,0:T(8,128)(2,1)S(1)}, u32[]{:S(2)}, u32[]{:S(2)}) collective-permute-start(bf16[4,8,128,128]{3,2,1,0:T(8,128)(2,1)S(1)} %get-tuple-element.136), channel_id=1, source_target_pairs={{0,4},{4,0},{8,12},{12,8},{16,20},{20,16},{24,28},{28,24},{1,5},{5... | collective-permute-start | bytes 3145736 | tf_op jit(solution)/shard_map/ppermute | solution.py:252
  132.1 4.1 %collective-permute-start.24 = (bf16[4,8,128,128]{3,2,1,0:T(8,128)(2,1)S(1)}, bf16[4,8,128,128]{3,2,1,0:T(8,128)(2,1)S(1)}, u32[]{:S(2)}, u32[]{:S(2)}) collective-permute-start(bf16[4,8,128,128]{3,2,1,0:T(8,128)(2,1)S(1)} %get-tuple-element.127), channel_id=1, source_target_pairs={{0,4},{4,0},{8,12},{12,8},{16,20},{20,16},{24,28},{28,24},{1,5},{5... | collective-permute-start | bytes 3145736 | tf_op jit(solution)/shard_map/ppermute | solution.py:252
  132.8 5.2 %collective-permute-start.26 = (bf16[128,512]{1,0:T(8,128)(2,1)S(1)}, bf16[128,512]{1,0:T(8,128)(2,1)S(1)}, u32[]{:S(2)}, u32[]{:S(2)}) collective-permute-start(bf16[128,512]{1,0:T(8,128)(2,1)S(1)} %get-tuple-element.133), channel_id=1, source_target_pairs={{0,4},{4,0},{8,12},{12,8},{16,20},{20,16},{24,28},{28,24},{1,5},{5... | collective-permute-start | bytes 393224 | tf_op jit(solution)/shard_map/ppermute | solution.py:252
  135.1 16.9 %collective-permute-start.30 = (bf16[2,8,128,128]{3,2,1,0:T(8,128)(2,1)S(1)}, bf16[2,8,128,128]{3,2,1,0:T(8,128)(2,1)S(1)}, u32[]{:S(2)}, u32[]{:S(2)}) collective-permute-start(bf16[2,8,128,128]{3,2,1,0:T(8,128)(2,1)S(1)} %get-tuple-element.145), channel_id=1, source_target_pairs={{0,16},{4,20},{8,24},{12,28},{16,0},{20,4},{24,8},{28,12},{1,17},{... | collective-permute-start | bytes 1572872 | tf_op jit(solution)/shard_map/ppermute | solution.py:252
  136.7 15.3 %collective-permute-start.25 = (bf16[2,8,128,128]{3,2,1,0:T(8,128)(2,1)S(1)}, bf16[2,8,128,128]{3,2,1,0:T(8,128)(2,1)S(1)}, u32[]{:S(2)}, u32[]{:S(2)}) collective-permute-start(bf16[2,8,128,128]{3,2,1,0:T(8,128)(2,1)S(1)} %get-tuple-element.147), channel_id=1, source_target_pairs={{0,8},{4,12},{8,0},{12,4},{16,24},{20,28},{24,16},{28,20},{1,9},{5... | collective-permute-start | bytes 1572872 | tf_op jit(solution)/shard_map/ppermute | solution.py:252
  138.0 13.9 %collective-permute-start.27 = (bf16[128,512]{1,0:T(8,128)(2,1)S(1)}, bf16[128,512]{1,0:T(8,128)(2,1)S(1)}, u32[]{:S(2)}, u32[]{:S(2)}) collective-permute-start(bf16[128,512]{1,0:T(8,128)(2,1)S(1)} %add_convert_fusion.12), channel_id=1, source_target_pairs={{0,16},{4,20},{8,24},{12,28},{16,0},{20,4},{24,8},{28,12},{1,17},{... | collective-permute-start | bytes 393224 | tf_op jit(solution)/shard_map/ppermute | solution.py:252
  152.0 6.5 %collective-permute-start.32 = (bf16[128,512]{1,0:T(8,128)(2,1)S(1)}, bf16[128,512]{1,0:T(8,128)(2,1)S(1)}, u32[]{:S(2)}, u32[]{:S(2)}) collective-permute-start(bf16[128,512]{1,0:T(8,128)(2,1)S(1)} %convert_add_fusion.5), channel_id=1, source_target_pairs={{0,8},{4,12},{8,0},{12,4},{16,24},{20,28},{24,16},{28,20},{1,9},{5... | collective-permute-start | bytes 393224 | tf_op jit(solution)/shard_map/ppermute | solution.py:252
  153.4 8.9 %collective-permute-start.31 = (bf16[8,128,128]{2,1,0:T(8,128)(2,1)S(1)}, bf16[8,128,128]{2,1,0:T(8,128)(2,1)S(1)}, u32[]{:S(2)}, u32[]{:S(2)}) collective-permute-start(bf16[8,128,128]{2,1,0:T(8,128)(2,1)S(1)} %get-tuple-element.153), channel_id=1, source_target_pairs={{0,8},{4,12},{8,0},{12,4},{16,24},{20,28},{24,16},{28,20},{1,9},{5... | collective-permute-start | bytes 786440 | tf_op jit(solution)/shard_map/ppermute | solution.py:252
  154.4 7.9 %collective-permute-start.28 = (bf16[8,128,128]{2,1,0:T(8,128)(2,1)S(1)}, bf16[8,128,128]{2,1,0:T(8,128)(2,1)S(1)}, u32[]{:S(2)}, u32[]{:S(2)}) collective-permute-start(bf16[8,128,128]{2,1,0:T(8,128)(2,1)S(1)} %get-tuple-element.155), channel_id=1, source_target_pairs={{0,16},{4,20},{8,24},{12,28},{16,0},{20,4},{24,8},{28,12},{1,17},{... | collective-permute-start | bytes 786440 | tf_op jit(solution)/shard_map/ppermute | solution.py:252
  162.4 1.5 collective-permute-start.33

commit v11 on v9

--- a/solution.py
+++ b/solution.py
@@ -7,14 +7,16 @@
 from jax.experimental.pallas import tpu as pltpu
 from jax.sharding import PartitionSpec as P
 
-VMEM_LIMIT = 48 * 1024 * 1024
 GROUPS = 2
 COPIES = 4
 F32 = jnp.float32
 BF16 = jnp.bfloat16
 VMEM = pl.BlockSpec(memory_space=pltpu.VMEM)
 SMEM = pl.BlockSpec(memory_space=pltpu.SMEM)
-PARAMS = pltpu.CompilerParams(vmem_limit_bytes=VMEM_LIMIT)
+
+
+def params(mib):
+    return pltpu.CompilerParams(vmem_limit_bytes=mib * 1024 * 1024)
 
 
 def tile_copy(tiles_ref, held, sems, i):
@@ -108,7 +110,7 @@
         in_specs=[SMEM, SMEM, anywhere] + [place] * len(args),
         out_specs=[VMEM] * len(outs),
         scratch_shapes=scratch,
-        compiler_params=PARAMS,
+        compiler_params=params(48),
         cost_estimate=pl.CostEstimate(flops=2 * edge_tiles.size * feat, bytes_accessed=30_000_000, transcendentals=0),
         name="spread",
     )(block_cols, me, edge_tiles, *args)
@@ -154,32 +156,41 @@
             pltpu.VMEM((len(parts) * blocks, size, feat), BF16),
             pltpu.SemaphoreType.DMA((COPIES + len(parts),)),
         ],
-        compiler_params=PARAMS,
+        compiler_params=params(48),
         cost_estimate=pl.CostEstimate(flops=2 * edge_tiles.size * feat, bytes_accessed=30_000_000, transcendentals=0),
         name="aggregate",
     )(block_cols, me, edge_tiles, *parts)
 
 
 def finish_kernel(last, *refs):
-    parts, out_ref = refs[:-1], refs[-1]
+    parts, rest = refs[: 2 * GROUPS], refs[2 * GROUPS :]
+    out_ref = rest[3] if last else rest[0]
     count = parts[0].shape[0]
-    for g in range(len(parts) // 2):
+    for g in range(GROUPS):
         for b in range(count):
             total = parts[2 * g][b].astype(F32) + parts[2 * g + 1][b].astype(F32)
             out_ref[g * count + b] = (total.T if last else total).astype(BF16)
-
-
-def finish(parts, last):
+    if last:
+        me_ref, value_ref, other_ref, _, first_ref, second_ref = rest
+        even = jnp.bitwise_and(me_ref[0], 1) == 0
+        first_ref[...] = jnp.where(even, other_ref[...], value_ref[...])
+        second_ref[...] = jnp.where(even, value_ref[...], other_ref[...])
+
+
+def finish(parts, grads=()):
     count, feat, size = parts[0].shape
+    last = len(grads) > 0
+    outs = [jax.ShapeDtypeStruct((count * GROUPS,) + ((size, feat) if last else (feat, size)), BF16)]
+    outs += [jax.ShapeDtypeStruct(grad.shape, F32) for grad in grads[1:]]
     return pl.pallas_call(
         functools.partial(finish_kernel, last),
-        out_shape=jax.ShapeDtypeStruct((count * len(parts) // 2,) + ((size, feat) if last else (feat, size)), BF16),
-        in_specs=[VMEM] * len(parts),
-        out_specs=VMEM,
-        compiler_params=PARAMS,
+        out_shape=outs,
+        in_specs=[VMEM] * len(parts) + [SMEM, VMEM, VMEM][: len(grads)],
+        out_specs=[VMEM] * len(outs),
+        compiler_params=params(12),
         cost_estimate=pl.CostEstimate(flops=0, bytes_accessed=1_000_000_000 if last else 1, transcendentals=0),
         name="finish",
-    )(*parts)
+    )(*parts, *grads)
 
 
 def dense_kernel(cols, masked, pieces, col_ref, weight_ref, *rest):
@@ -187,25 +198,22 @@
     side_ref, rest = rest[0], rest[1:]
     if masked:
         mask_ref, rest = rest[0], rest[1:]
-    outs, (grad_ref, whole_ref) = rest[:pieces], rest[pieces:]
+    outs, (grad_ref,) = rest[:pieces], rest[pieces:]
     blocks, feat, size = shards[0].shape
-    for m in range(cols):
-        place = jnp.bitwise_xor(col_ref[0], m)
-        for b in range(blocks):
-            whole_ref[place, :, b * size : (b + 1) * size] = shards[m][b]
     per = blocks // pieces
     total = None
     for i, out in enumerate(outs):
-        part = slice(i * per * size, (i + 1) * per * size)
-        whole = jnp.concatenate([whole_ref[q, :, part] for q in range(cols)], axis=0)
+        mine = range(i * per, (i + 1) * per)
+        whole = jnp.concatenate([jnp.concatenate([shards[m][b] for b in mine], axis=1) for m in range(cols)], axis=0)
         res = jnp.dot(weight_ref[...], whole, preferred_element_type=F32)
-        for b in range(per):
-            block = res[:, b * size : (b + 1) * size]
-            out[b] = (block * mask_ref[i * per + b].astype(F32) if masked else block).astype(BF16)
-        side = jnp.concatenate([side_ref[i * per + b] for b in range(per)], axis=0)
+        for k, b in enumerate(mine):
+            block = res[:, k * size : (k + 1) * size]
+            out[k] = (block * mask_ref[b].astype(F32) if masked else block).astype(BF16)
+        side = jnp.concatenate([side_ref[b] for b in mine], axis=0)
         term = jnp.dot(whole, side, preferred_element_type=F32)
         total = term if total is None else total + term
-    grad_ref[...] = total
+    for m in range(cols):
+        grad_ref[jnp.bitwise_xor(col_ref[0], m)] = total[m * feat : (m + 1) * feat]
 
 
 def dense(weight, shards, side, mask, col, pieces):
@@ -215,31 +223,33 @@
     return pl.pallas_call(
         functools.partial(dense_kernel, cols, mask is not None, pieces),
         out_shape=[jax.ShapeDtypeStruct((blocks // pieces, feat, size), BF16)] * pieces
-        + [jax.ShapeDtypeStruct((cols * feat, side.shape[2]), F32)],
+        + [jax.ShapeDtypeStruct((cols, feat, side.shape[2]), F32)],
         in_specs=[SMEM] + [VMEM] * len(args),
         out_specs=[VMEM] * (pieces + 1),
-        scratch_shapes=[pltpu.VMEM((cols, feat, blocks * size), BF16)],
-        compiler_params=PARAMS,
+        compiler_params=params(16),
         name="dense",
     )(col, *args)
 
 
 def weight_terms_kernel(me_ref, second_ref, *refs):
     firsts, (keep_ref, send_ref) = refs[:-2], refs[-2:]
-    first, second = sum(r[...] for r in firsts).T, second_ref[...].T
+    cols, feat, width = second_ref.shape
     even = jnp.bitwise_and(me_ref[0], 1) == 0
+    first = jnp.concatenate([sum(r[q] for r in firsts) for q in range(cols)], axis=0).T
+    second = jnp.concatenate([second_ref[q] for q in range(cols)], axis=0).T
     keep_ref[...] = jnp.where(even, second, first)
     send_ref[...] = jnp.where(even, first, second).astype(BF16)
 
 
 def weight_terms(firsts, second, me):
-    shape = second.shape[::-1]
+    cols, feat, width = second.shape
+    shape = (width, cols * feat)
     return pl.pallas_call(
         weight_terms_kernel,
         out_shape=[jax.ShapeDtypeStruct(shape, F32), jax.ShapeDtypeStruct(shape, BF16)],
         in_specs=[SMEM] + [VMEM] * (1 + len(firsts)),
         out_specs=[VMEM] * 2,
-        compiler_params=PARAMS,
+        compiler_params=params(8),
         name="weight_terms",
     )(me, second, *firsts)
 
@@ -305,9 +315,16 @@
     blocked = lambda v: v.reshape(v.shape[0] // size, size, v.shape[1])
     after = lax.optimization_barrier
 
+    def by_distance(weight):
+        split = weight.reshape(weight.shape[0], cols, weight.shape[1] // cols)
+        order = [lax.dynamic_index_in_dim(split, col ^ m, 1, keepdims=False) for m in range(cols)]
+        return jnp.concatenate(order, axis=1)
+
     *pieces, mask = spread(edge_tiles, block_cols, [blocked(grad_out)], me_at, rows, blocked(relu_mask))
     terms, _ = scatter(pieces, rows)
-    own, node_feats = after((finish([t for pair in terms for t in pair], False), blocked(node_feats)))
+    own, node_feats = after((finish([t for pair in terms for t in pair])[0], blocked(node_feats)))
+    own, weight_one, weight_two = after((own, weight_one, weight_two))
+    weight_one, weight_two = by_distance(weight_one), by_distance(weight_two)
     shards, _ = gather_columns(own, cols)
     parts = [node_feats] + [swap(node_feats, rel, "row") for rel in range(2, rows, 2)]
     parts = [v for part in parts for v in (part, swap(part, 1, "row"))]
@@ -326,11 +343,9 @@
     keep, send = weight_terms(firsts, second, me_at)
     value = over_chips(keep + swap(send, 1, "row").astype(F32), chips[-1:])
     terms, value = scatter(pieces, rows, value)
-    terms, value = after((terms, over_chips(value, chips[:-1])))
-    out = finish([t for pair in terms for t in pair], True)
-    other = swap(value, 1, "row")
-    even = me % 2 == 0
-    first_grad, second_grad = jnp.where(even, other, value), jnp.where(even, value, other)
+    value = over_chips(value, chips[:-1])
+    grads = [me_at, value, swap(value, 1, "row")]
+    out, first_grad, second_grad = finish([t for pair in terms for t in pair], grads)
     return out.reshape(-1, out.shape[2]), first_grad, second_grad
 
 

time: 158 us -> 156 us (0.987)
  transfers between devices with their start and end apart: 32 -> 32, of which waited for: 17 -> 16; matrix products, arithmetic and copies ran while one was open for 1% -> 2% of each run, Pallas kernels for 5% -> 5%
where the time goes in v11:
time: 156 us; the launch traced here: 155 us
  waiting for transfers between devices  85.7 us (55%)
  starting transfers between devices  34.6 us (22%)
  Pallas kernels  25.1 us (16%)
  local copies, waits for them, and re-layouts  6.38 us (4%)
  other arithmetic  2.21 us (1%)
    ppermute x32, waiting for transfers between devices, swap(): lax.ppermute(value, axis, [(i, i ^ mask) for i in range(lax.axis_size(axi...  85.7 us
    ppermute x32, starting transfers between devices, swap(): lax.ppermute(value, axis, [(i, i ^ mask) for i in range(lax.axis_size(axi...  34.6 us
    pallas_call x2, Pallas kernels, spread(): pl.pallas_call(functools.partial(spread_kernel, first, len(vals)), out_sh...  13.7 us
    pallas_call x1, Pallas kernels, aggregate(): pl.pallas_call(aggregate_kernel, out_shape=jax.ShapeDtypeStruct((blocks,...  6.5 us
    unnamed x22, local copies, waits for them, and re-layouts  5.66 us
    pallas_call x3, Pallas kernels, dense(): pl.pallas_call(functools.partial(dense_kernel, cols, mask is not None, pi...  3.37 us
  transfers between devices with their start and end apart: 32, of which 16 were waited for; matrix products, arithmetic and copies ran while one was open for 2% of the time, Pallas kernels for 5%

profile of v11, /device:TPU:0, one launch (start us, length us, event | category | flops | bytes accessed | tf_op | source)
XLA Modules:
  0.0 155.0 jit_solution(12294293193682507450)
XLA Ops:
  0.6 1.0 copy-done.6
  1.7 0.7 copy-done.7
  2.4 7.0 %spread.2 = (bf16[4,8,128,128]{3,2,1,0:T(8,128)(2,1)S(1)}, bf16[4,8,128,128]{3,2,1,0:T(8,128)(2,1)S(1)}, bf16[4,8,128,128]{3,2,1,0:T(8,128)(2,1)S(1)}, bf16[4,8,...) custom-call(s32[16,20]{1,0:T(8,128)S(1)} %copy-done.7, s32[1]{0:T(128)} %bitcast.me_ref.refs_4_, ...), custom_call_target="tpu_custom_call" | custom-call | flops 1342177280 | bytes 30000000 | tf_op jit(solution)/shard_map/spread/pallas_call | solution.py:107
  9.4 0.5 collective-permute-start.3
  10.0 2.2 %collective-permute-done.3 = bf16[4,8,128,128]{3,2,1,0:T(8,128)(2,1)S(1)} collective-permute-done((bf16[4,8,128,128]{3,2,1,0:T(8,128)(2,1)S(1)}, bf16[4,8,128,128]{3,2,1,0:T(8,128)(2,1)S(1)}, u32[]{:S(2)}, u32[]{:S(2)}) %collective-permute-start.3) | collective-permute-done | bytes 1048608 | tf_op jit(solution)/shard_map/ppermute | solution.py:258
  12.3 0.5 add_convert_fusion.5
  12.7 3.0 %collective-permute-start.4 = (bf16[2,8,128,128]{3,2,1,0:T(8,128)(2,1)S(1)}, bf16[2,8,128,128]{3,2,1,0:T(8,128)(2,1)S(1)}, u32[]{:S(2)}, u32[]{:S(2)}) collective-permute-start(bf16[2,8,128,128]{3,2,1,0:T(8,128)(2,1)S(1)} %get-tuple-element.124), channel_id=1, source_target_pairs={{0,16},{4,20},{8,24},{12,28},{16,0},{20,4},{24,8},{28,12},{1,17},{... | collective-permute-start | bytes 1572872 | tf_op jit(solution)/shard_map/ppermute | solution.py:258
  15.7 0.3 add_convert_fusion.7
  16.0 1.6 %collective-permute-start.1 = (bf16[2,8,128,128]{3,2,1,0:T(8,128)(2,1)S(1)}, bf16[2,8,128,128]{3,2,1,0:T(8,128)(2,1)S(1)}, u32[]{:S(2)}, u32[]{:S(2)}) collective-permute-start(bf16[2,8,128,128]{3,2,1,0:T(8,128)(2,1)S(1)} %get-tuple-element.126), channel_id=1, source_target_pairs={{0,8},{4,12},{8,0},{12,4},{16,24},{20,28},{24,16},{28,20},{1,9},{5... | collective-permute-start | bytes 1572872 | tf_op jit(solution)/shard_map/ppermute | solution.py:258
  17.6 10.3 %collective-permute-done.4 = bf16[2,8,128,128]{3,2,1,0:T(8,128)(2,1)S(1)} collective-permute-done((bf16[2,8,128,128]{3,2,1,0:T(8,128)(2,1)S(1)}, bf16[2,8,128,128]{3,2,1,0:T(8,128)(2,1)S(1)}, u32[]{:S(2)}, u32[]{:S(2)}) %collective-permute-start.4) | collective-permute-done | bytes 524320 | tf_op jit(solution)/shard_map/ppermute | solution.py:258
  27.9 0.1 fusion.7
  28.0 1.8 %collective-permute-start.5 = (bf16[8,128,128]{2,1,0:T(8,128)(2,1)S(1)}, bf16[8,128,128]{2,1,0:T(8,128)(2,1)S(1)}, u32[]{:S(2)}, u32[]{:S(2)}) collective-permute-start(bf16[8,128,128]{2,1,0:T(8,128)(2,1)S(1)} %get-tuple-element.131), channel_id=1, source_target_pairs={{0,8},{4,12},{8,0},{12,4},{16,24},{20,28},{24,16},{28,20},{1,9},{5... | collective-permute-start | bytes 786440 | tf_op jit(solution)/shard_map/ppermute | solution.py:258
  29.8 0.1 fusion.11
  30.0 1.6 %collective-permute-start.2 = (bf16[8,128,128]{2,1,0:T(8,128)(2,1)S(1)}, bf16[8,128,128]{2,1,0:T(8,128)(2,1)S(1)}, u32[]{:S(2)}, u32[]{:S(2)}) collective-permute-start(bf16[8,128,128]{2,1,0:T(8,128)(2,1)S(1)} %get-tuple-element.133), channel_id=1, source_target_pairs={{0,16},{4,20},{8,24},{12,28},{16,0},{20,4},{24,8},{28,12},{1,17},{... | collective-permute-start | bytes 786440 | tf_op jit(solution)/shard_map/ppermute | solution.py:258
  31.6 4.4 %collective-permute-done.5.refs_3_ = bf16[8,128,128]{2,1,0:T(8,128)(2,1)S(1)} collective-permute-done((bf16[8,128,128]{2,1,0:T(8,128)(2,1)S(1)}, bf16[8,128,128]{2,1,0:T(8,128)(2,1)S(1)}, u32[]{:S(2)}, u32[]{:S(2)}) %collective-permute-start.5) | collective-permute-done | bytes 262176 | tf_op jit(solution)/shard_map/ppermute | solution.py:258
  35.9 1.3 collective-permute-done.2.refs_1_
  37.4 1.6 %collective-permute-start.6 = (bf16[16,128,128]{2,1,0:T(8,128)(2,1)S(1)}, bf16[16,128,128]{2,1,0:T(8,128)(2,1)S(1)}, u32[]{:S(2)}, u32[]{:S(2)}) collective-permute-start(bf16[16,128,128]{2,1,0:T(8,128)(2,1)S(1)} %finish.2.rest_0_), channel_id=1, source_target_pairs={{0,1},{1,0},{2,3},{3,2},{4,5},{5,4},{6,7},{7,6},{8,9},{9,8},{10,11... | collective-permute-start | bytes 1572872 | tf_op jit(solution)/shard_map/ppermute | solution.py:258
  39.0 2.5 %collective-permute-start.7 = (bf16[16,128,128]{2,1,0:T(8,128)(2,1)S(1)}, bf16[16,128,128]{2,1,0:T(8,128)(2,1)}, u32[]{:S(2)}, u32[]{:S(2)}) collective-permute-start(bf16[16,128,128]{2,1,0:T(8,128)(2,1)S(1)} %finish.2.rest_0_), channel_id=1, source_target_pairs={{0,3},{1,2},{2,1},{3,0},{4,7},{5,6},{6,5},{7,4},{8,11},{9,10},{10,... | collective-permute-start | bytes 1572872 | tf_op jit(solution)/shard_map/ppermute | solution.py:258
  41.5 1.4 collective-permute-start.10
  42.9 1.6 %collective-permute-start.12 = (bf16[16,128,128]{2,1,0:T(8,128)(2,1)S(1)}, bf16[16,128,128]{2,1,0:T(8,128)(2,1)S(1)}, u32[]{:S(2)}, u32[]{:S(2)}) collective-permute-start(bf16[16,128,128]{2,1,0:T(8,128)(2,1)S(1)} %bitcast.70), channel_id=1, source_target_pairs={{0,16},{4,20},{8,24},{12,28},{16,0},{20,4},{24,8},{28,12},{1,17},{... | collective-permute-start | bytes 1572872 | tf_op jit(solution)/shard_map/ppermute | solution.py:258
  44.5 0.5 collective-permute-start.14
  45.1 0.3 constant_dynamic-slice_fusion.3
  45.4 6.1 %collective-permute-done.6.rest_1_ = bf16[16,128,128]{2,1,0:T(8,128)(2,1)S(1)} collective-permute-done((bf16[16,128,128]{2,1,0:T(8,128)(2,1)S(1)}, bf16[16,128,128]{2,1,0:T(8,128)(2,1)S(1)}, u32[]{:S(2)}, u32[]{:S(2)}) %collective-permute-start.6) | collective-permute-done | bytes 524320 | tf_op jit(solution)/shard_map/ppermute | solution.py:258
  51.4 0.8 copy-done.4
  52.2 10.7 %collective-permute-done.7.rest_3_ = bf16[16,128,128]{2,1,0:T(8,128)(2,1)} collective-permute-done((bf16[16,128,128]{2,1,0:T(8,128)(2,1)S(1)}, bf16[16,128,128]{2,1,0:T(8,128)(2,1)}, u32[]{:S(2)}, u32[]{:S(2)}) %collective-permute-start.7) | collective-permute-done | bytes 524320 | tf_op jit(solution)/shard_map/ppermute | solution.py:258
  62.9 0.6 collective-permute-start.8
  63.5 1.9 %collective-permute-done.12.rest_4_ = bf16[16,128,128]{2,1,0:T(8,128)(2,1)S(1)} collective-permute-done((bf16[16,128,128]{2,1,0:T(8,128)(2,1)S(1)}, bf16[16,128,128]{2,1,0:T(8,128)(2,1)S(1)}, u32[]{:S(2)}, u32[]{:S(2)}) %collective-permute-start.12) | collective-permute-done | bytes 524320 | tf_op jit(solution)/shard_map/ppermute | solution.py:258
  65.3 0.5 collective-permute-start.15
  65.9 0.3 constant_dynamic-slice_fusion.7
  66.3 7.9 %collective-permute-done.8.rest_2_ = bf16[16,128,128]{2,1,0:T(8,128)(2,1)} collective-permute-done((bf16[16,128,128]{2,1,0:T(8,128)(2,1)}, bf16[16,128,128]{2,1,0:T(8,128)(2,1)}, u32[]{:S(2)}, u32[]{:S(2)}) %collective-permute-start.8) | collective-permute-done | bytes 524320 | tf_op jit(solution)/shard_map/ppermute | solution.py:258
  74.2 1.0 copy-done.1
  75.2 1.0 copy-done.3
  76.2 1.0 copy-done.5
  77.3 2.2 %dense.3 = (bf16[8,128,128]{2,1,0:T(8,128)(2,1)S(1)}, bf16[8,128,128]{2,1,0:T(8,128)(2,1)S(1)}, f32[4,128,128]{2,1,0:T(8,128)S(1)}) custom-call(s32[1]{0:T(128)} %bitcast.1.col_ref, bf16[128,512]{1,0:T(8,128)(2,1)S(1)} %pad_maximum_fusion.1.weight_ref, bf16[16,128,128]{2,1,0:T(8,128)(2,1)S(1)} %finish.2.rest_0_, bf16[16,128,128]{2,1,0:T(8,128)(2,1)S(1)} %copy-done.5, ...), custom_call_target="tpu_custom_call" | custom-call | tf_op jit(solution)/shard_map/dense/pallas_call | solution.py:223
  79.5 0.3 collective-permute-start.19
  79.9 5.5 %collective-permute-start.20 = (bf16[8,128,128]{2,1,0:T(8,128)(2,1)S(1)}, bf16[8,128,128]{2,1,0:T(8,128)(2,1)S(1)}, u32[]{:S(2)}, u32[]{:S(2)}) collective-permute-start(bf16[8,128,128]{2,1,0:T(8,128)(2,1)S(1)} %get-tuple-element.99.rest_0_), channel_id=1, source_target_pairs={{0,3},{1,2},{2,1},{3,0},{4,7},{5,6},{6,5},{7,4},{8,11},{9,10},{10,... | collective-permute-start | bytes 786440 | tf_op jit(solution)/shard_map/ppermute | solution.py:258
  85.4 0.8 collective-permute-start.16
  86.2 0.9 collective-permute-start.17
  87.2 6.5 %aggregate.1 = bf16[16,128,128]{2,1,0:T(8,128)(2,1)S(1)} custom-call(s32[16,20]{1,0:T(8,128)S(1)} %copy-done.8, s32[1]{0:T(128)} %bitcast.me_ref.refs_4_, bf16[16,20,128,128]{3,2,1,0:T(8,128)(2,1)} %tiles_ref.5, bf16[16,128,128]{2,1,0:T(8,128)(2,1)S(1)} %bitcast.73, bf16[16,128,128]{2,1,0:T(8,128)(2,1)S(1)} %collective-permute-done.9.rest_1_, ...), custom_call_target="tpu_custom_call" | custom-call | flops 1342177280 | bytes 30000000 | tf_op jit(solution)/shard_map/aggregate/pallas_call | solution.py:149
  93.7 4.6 %collective-permute-done.20.rest_3_ = bf16[8,128,128]{2,1,0:T(8,128)(2,1)S(1)} collective-permute-done((bf16[8,128,128]{2,1,0:T(8,128)(2,1)S(1)}, bf16[8,128,128]{2,1,0:T(8,128)(2,1)S(1)}, u32[]{:S(2)}, u32[]{:S(2)}) %collective-permute-start.20) | collective-permute-done | bytes 262176 | tf_op jit(solution)/shard_map/ppermute | solution.py:258
  98.2 0.8 collective-permute-start.21
  99.1 10.5 %collective-permute-done.17.rest_3_ = bf16[8,128,128]{2,1,0:T(8,128)(2,1)S(1)} collective-permute-done((bf16[8,128,128]{2,1,0:T(8,128)(2,1)S(1)}, bf16[8,128,128]{2,1,0:T(8,128)(2,1)S(1)}, u32[]{:S(2)}, u32[]{:S(2)}) %collective-permute-start.17) | collective-permute-done | bytes 262176 | tf_op jit(solution)/shard_map/ppermute | solution.py:258
  109.6 0.6 collective-permute-done.21.rest_2_
  110.2 0.6 dense.5
  110.8 5.1 %collective-permute-done.18.rest_2_ = bf16[8,128,128]{2,1,0:T(8,128)(2,1)S(1)} collective-permute-done((bf16[8,128,128]{2,1,0:T(8,128)(2,1)S(1)}, bf16[8,128,128]{2,1,0:T(8,128)(2,1)S(1)}, u32[]{:S(2)}, u32[]{:S(2)}) %collective-permute-start.18) | collective-permute-done | bytes 262176 | tf_op jit(solution)/shard_map/ppermute | solution.py:258
  115.9 0.6 dense.4
  116.5 6.7 %spread.3 = (bf16[4,8,128,128]{3,2,1,0:T(8,128)(2,1)S(1)}, bf16[4,8,128,128]{3,2,1,0:T(8,128)(2,1)S(1)}, bf16[4,8,128,128]{3,2,1,0:T(8,128)(2,1)S(1)}, bf16[4,8,128,128]{3,2,1,0:T(8,128)(2,1)S(1)}) custom-call(s32[16,20]{1,0:T(8,128)S(1)} %copy-done.8, s32[1]{0:T(128)} %bitcast.me_ref.refs_4_, bf16[16,20,128,128]{3,2,1,0:T(8,128)(2,1)} %tiles_ref.5, ...), custom_call_target="tpu_custom_call" | custom-call | flops 1342177280 | bytes 30000000 | tf_op jit(solution)/shard_map/spread/pallas_call | solution.py:107
  123.3 0.5 collective-permute-start.22
  123.8 0.2 weight_terms.1
  124.0 0.1 collective-permute-start.24
  124.1 1.8 %collective-permute-done.27 = bf16[4,8,128,128]{3,2,1,0:T(8,128)(2,1)S(1)} collective-permute-done((bf16[4,8,128,128]{3,2,1,0:T(8,128)(2,1)S(1)}, bf16[4,8,128,128]{3,2,1,0:T(8,128)(2,1)S(1)}, u32[]{:S(2)}, u32[]{:S(2)}) %collective-permute-start.27) | collective-permute-done | bytes 1048608 | tf_op jit(solution)/shard_map/ppermute | solution.py:258
  125.9 0.4 add_convert_fusion
  126.3 1.6 %collective-permute-start.28 = (bf16[2,8,128,128]{3,2,1,0:T(8,128)(2,1)S(1)}, bf16[2,8,128,128]{3,2,1,0:T(8,128)(2,1)S(1)}, u32[]{:S(2)}, u32[]{:S(2)}) collective-permute-start(bf16[2,8,128,128]{3,2,1,0:T(8,128)(2,1)S(1)} %get-tuple-element.119), channel_id=1, source_target_pairs={{0,16},{4,20},{8,24},{12,28},{16,0},{20,4},{24,8},{28,12},{1,17},{... | collective-permute-start | bytes 1572872 | tf_op jit(solution)/shard_map/ppermute | solution.py:258
  127.9 0.4 fusion.1
  128.3 1.8 %collective-permute-start.23 = (bf16[2,8,128,128]{3,2,1,0:T(8,128)(2,1)S(1)}, bf16[2,8,128,128]{3,2,1,0:T(8,128)(2,1)S(1)}, u32[]{:S(2)}, u32[]{:S(2)}) collective-permute-start(bf16[2,8,128,128]{3,2,1,0:T(8,128)(2,1)S(1)} %get-tuple-element.121), channel_id=1, source_target_pairs={{0,8},{4,12},{8,0},{12,4},{16,24},{20,28},{24,16},{28,20},{1,9},{5... | collective-permute-start | bytes 1572872 | tf_op jit(solution)/shard_map/ppermute | solution.py:258
  130.1 1.1 collective-permute-start.25
  131.2 11.9 %collective-permute-done.25 = bf16[128,512]{1,0:T(8,128)(2,1)S(1)} collective-permute-done((bf16[128,512]{1,0:T(8,128)(2,1)S(1)}, bf16[128,512]{1,0:T(8,128)(2,1)S(1)}, u32[]{:S(2)}, u32[]{:S(2)}) %collective-permute-start.25) | collective-permute-done | bytes 131104 | tf_op jit(solution)/shard_map/ppermute | solution.py:258
  143.2 1.6 %collective-permute-start.30 = (bf16[128,512]{1,0:T(8,128)(2,1)S(1)}, bf16[128,512]{1,0:T(8,128)(2,1)S(1)}, u32[]{:S(2)}, u32[]{:S(2)}) collective-permute-start(bf16[128,512]{1,0:T(8,128)(2,1)S(1)} %convert_add_fusion.5), channel_id=1, source_target_pairs={{0,8},{4,12},{8,0},{12,4},{16,24},{20,28},{24,16},{28,20},{1,9},{5... | collective-permute-start | bytes 393224 | tf_op jit(solution)/shard_map/ppermute | solution.py:258
  144.8 0.1 fusion.9
  144.9 0.6 collective-permute-start.29
  145.6 1.6 %collective-permute-start.26 = (bf16[8,128,128]{2,1,0:T(8,128)(2,1)S(1)}, bf16[8,128,128]{2,1,0:T(8,128)(2,1)S(1)}, u32[]{:S(2)}, u32[]{:S(2)}) collective-permute-start(bf16[8,128,128]{2,1,0:T(8,128)(2,1)S(1)} %get-tuple-element.129), channel_id=1, source_target_pairs={{0,16},{4,20},{8,24},{12,28},{16,0},{20,4},{24,8},{28,12},{1,17},{... | collective-permute-start | bytes 786440 | tf_op jit(solution)/shard_map/ppermute | solution.py:258
  147.2 2.4 %collective-permute-done.30 = bf16[128,512]{1,0:T(8,128)(2,1)S(1)} collective-permute-done((bf16[128,512]{1,0:T(8,128)(2,1)S(1)}, bf16[128,512]{1,0:T(8,128)(2,1)S(1)}, u32[]{:S(2)}, u32[]{:S(2)}) %collective-permute-start.30) | collective-permute-done | bytes 131104 | tf_op jit(solution)/shard_map/ppermute | solution.py:258
  149.7 4.0 %collective-permute-done.29.refs_3_ = bf16[8,128,128]{2,1,0:T(8,128)(2,1)S(1)} collective-permute-done((bf16[8,128,128]{2,1,0:T(8,128)(2,1)S(1)}, bf16[8,128,128]{2,1,0:T(8,128)(2,1)S(1)}, u32[]{:S(2)}, u32[]{:S(2)}) %collective-permute-start.29) | collective-permute-done | bytes 262176 | tf_op jit(solution)/shard_map/ppermute | solution.py:258
  153.8 1.2 finish.3
  (53 shorter events, 0.8 us)
Async XLA Ops:
  0.6 1.0 copy-start.6
  1.7 0.7 copy-start.7
  2.4 39.1 %copy-start = (bf16[2048,128]{1,0:T(8,128)(2,1)S(1)}, bf16[2048,128]{1,0:T(8,128)(2,1)}, u32[]{:S(2)}) copy-start(bf16[2048,128]{1,0:T(8,128)(2,1)} %param.8) | copy-start | bytes 1572868
  2.4 42.6 %copy-start.9 = (bf16[128,512]{1,0:T(8,128)(2,1)S(1)}, bf16[128,512]{1,0:T(8,128)(2,1)}, u32[]{:S(2)}) copy-start(bf16[128,512]{1,0:T(8,128)(2,1)} %param.15) | copy-start | bytes 393220
  2.4 63.5 %copy-start.10 = (bf16[128,512]{1,0:T(8,128)(2,1)S(1)}, bf16[128,512]{1,0:T(8,128)(2,1)}, u32[]{:S(2)}) copy-start(bf16[128,512]{1,0:T(8,128)(2,1)} %param.14) | copy-start | bytes 393220
  9.4 33.5 %copy-start.2 = (bf16[16,128,128]{2,1,0:T(8,128)(2,1)}, bf16[16,128,128]{2,1,0:T(8,128)(2,1)S(1)}, u32[]{:S(2)}) copy-start(bf16[16,128,128]{2,1,0:T(8,128)(2,1)S(1)} %get-tuple-element.76.rest_5_) | copy-start | bytes 1572868
  9.4 77.7 %copy-start.8 = (s32[16,20]{1,0:T(8,128)S(1)}, s32[16,20]{1,0:T(8,128)}, u32[]{:S(2)}) copy-start(s32[16,20]{1,0:T(8,128)} %cols_ref.5) | copy-start | bytes 3844
  9.4 2.8 %collective-permute-start.3 = (bf16[4,8,128,128]{3,2,1,0:T(8,128)(2,1)S(1)}, bf16[4,8,128,128]{3,2,1,0:T(8,128)(2,1)S(1)}, u32[]{:S(2)}, u32[]{:S(2)}) collective-permute-start(bf16[4,8,128,128]{3,2,1,0:T(8,128)(2,1)S(1)} %get-tuple-element.64), channel_id=1, source_target_pairs={{0,4},{4,0},{8,12},{12,8},{16,20},{20,16},{24,28},{28,24},{1,5},{5... | collective-permute-start | bytes 3145736 | tf_op jit(solution)/shard_map/ppermute | solution.py:258
  10.0 5.7 %collective-permute-start = (bf16[4,8,128,128]{3,2,1,0:T(8,128)(2,1)S(1)}, bf16[4,8,128,128]{3,2,1,0:T(8,128)(2,1)S(1)}, u32[]{:S(2)}, u32[]{:S(2)}) collective-permute-start(bf16[4,8,128,128]{3,2,1,0:T(8,128)(2,1)S(1)} %get-tuple-element.62), channel_id=1, source_target_pairs={{0,4},{4,0},{8,12},{12,8},{16,20},{20,16},{24,28},{28,24},{1,5},{5... | collective-permute-start | bytes 3145736 | tf_op jit(solution)/shard_map/ppermute | solution.py:258
  12.7 15.2 %collective-permute-start.4 = (bf16[2,8,128,128]{3,2,1,0:T(8,128)(2,1)S(1)}, bf16[2,8,128,128]{3,2,1,0:T(8,128)(2,1)S(1)}, u32[]{:S(2)}, u32[]{:S(2)}) collective-permute-start(bf16[2,8,128,128]{3,2,1,0:T(8,128)(2,1)S(1)} %get-tuple-element.124), channel_id=1, source_target_pairs={{0,16},{4,20},{8,24},{12,28},{16,0},{20,4},{24,8},{28,12},{1,17},{... | collective-permute-start | bytes 1572872 | tf_op jit(solution)/shard_map/ppermute | solution.py:258
  16.0 13.8 %collective-permute-start.1 = (bf16[2,8,128,128]{3,2,1,0:T(8,128)(2,1)S(1)}, bf16[2,8,128,128]{3,2,1,0:T(8,128)(2,1)S(1)}, u32[]{:S(2)}, u32[]{:S(2)}) collective-permute-start(bf16[2,8,128,128]{3,2,1,0:T(8,128)(2,1)S(1)} %get-tuple-element.126), channel_id=1, source_target_pairs={{0,8},{4,12},{8,0},{12,4},{16,24},{20,28},{24,16},{28,20},{1,9},{5... | collective-permute-start | bytes 1572872 | tf_op jit(solution)/shard_map/ppermute | solution.py:258
  28.0 7.9 %collective-permute-start.5 = (bf16[8,128,128]{2,1,0:T(8,128)(2,1)S(1)}, bf16[8,128,128]{2,1,0:T(8,128)(2,1)S(1)}, u32[]{:S(2)}, u32[]{:S(2)}) collective-permute-start(bf16[8,128,128]{2,1,0:T(8,128)(2,1)S(1)} %get-tuple-element.131), channel_id=1, source_target_pairs={{0,8},{4,12},{8,0},{12,4},{16,24},{20,28},{24,16},{28,20},{1,9},{5... | collective-permute-start | bytes 786440 | tf_op jit(solution)/shard_map/ppermute | solution.py:258
  30.0 7.3 %collective-permute-start.2 = (bf16[8,128,128]{2,1,0:T(8,128)(2,1)S(1)}, bf16[8,128,128]{2,1,0:T(8,128)(2,1)S(1)}, u32[]{:S(2)}, u32[]{:S(2)}) collective-permute-start(bf16[8,128,128]{2,1,0:T(8,128)(2,1)S(1)} %get-tuple-element.133), channel_id=1, source_target_pairs={{0,16},{4,20},{8,24},{12,28},{16,0},{20,4},{24,8},{28,12},{1,17},{... | collective-permute-start | bytes 786440 | tf_op jit(solution)/shard_map/ppermute | solution.py:258
  37.4 14.0 %collective-permute-start.6 = (bf16[16,128,128]{2,1,0:T(8,128)(2,1)S(1)}, bf16[16,128,128]{2,1,0:T(8,128)(2,1)S(1)}, u32[]{:S(2)}, u32[]{:S(2)}) collective-permute-start(bf16[16,128,128]{2,1,0:T(8,128)(2,1)S(1)} %finish.2.rest_0_), channel_id=1, source_target_pairs={{0,1},{1,0},{2,3},{3,2},{4,5},{5,4},{6,7},{7,6},{8,9},{9,8},{10,11... | collective-permute-start | bytes 1572872 | tf_op jit(solution)/shard_map/ppermute | solution.py:258
  39.0 23.8 %collective-permute-start.7 = (bf16[16,128,128]{2,1,0:T(8,128)(2,1)S(1)}, bf16[16,128,128]{2,1,0:T(8,128)(2,1)}, u32[]{:S(2)}, u32[]{:S(2)}) collective-permute-start(bf16[16,128,128]{2,1,0:T(8,128)(2,1)S(1)} %finish.2.rest_0_), channel_id=1, source_target_pairs={{0,3},{1,2},{2,1},{3,0},{4,7},{5,6},{6,5},{7,4},{8,11},{9,10},{10,... | collective-permute-start | bytes 1572872 | tf_op jit(solution)/shard_map/ppermute | solution.py:258
  41.5 21.9 %collective-permute-start.10 = (bf16[16,128,128]{2,1,0:T(8,128)(2,1)S(1)}, bf16[16,128,128]{2,1,0:T(8,128)(2,1)S(1)}, u32[]{:S(2)}, u32[]{:S(2)}) collective-permute-start(bf16[16,128,128]{2,1,0:T(8,128)(2,1)S(1)} %bitcast.69), channel_id=1, source_target_pairs={{0,8},{4,12},{8,0},{12,4},{16,24},{20,28},{24,16},{28,20},{1,9},{5... | collective-permute-start | bytes 1572872 | tf_op jit(solution)/shard_map/ppermute | solution.py:258
  42.9 22.4 %collective-permute-start.12 = (bf16[16,128,128]{2,1,0:T(8,128)(2,1)S(1)}, bf16[16,128,128]{2,1,0:T(8,128)(2,1)S(1)}, u32[]{:S(2)}, u32[]{:S(2)}) collective-permute-start(bf16[16,128,128]{2,1,0:T(8,128)(2,1)S(1)} %bitcast.70), channel_id=1, source_target_pairs={{0,16},{4,20},{8,24},{12,28},{16,0},{20,4},{24,8},{28,12},{1,17},{... | collective-permute-start | bytes 1572872 | tf_op jit(solution)/shard_map/ppermute | solution.py:258
  44.5 20.9 %collective-permute-start.14 = (bf16[16,128,128]{2,1,0:T(8,128)(2,1)S(1)}, bf16[16,128,128]{2,1,0:T(8,128)(2,1)S(1)}, u32[]{:S(2)}, u32[]{:S(2)}) collective-permute-start(bf16[16,128,128]{2,1,0:T(8,128)(2,1)S(1)} %bitcast.71), channel_id=1, source_target_pairs={{0,24},{4,28},{8,16},{12,20},{16,8},{20,12},{24,0},{28,4},{1,25},{... | collective-permute-start | bytes 1572872 | tf_op jit(solution)/shard_map/ppermute | solution.py:258
  51.4 0.8 copy-start.4
  52.2 14.0 %collective-permute-start.9 = (bf16[16,128,128]{2,1,0:T(8,128)(2,1)S(1)}, bf16[16,128,128]{2,1,0:T(8,128)(2,1)S(1)}, u32[]{:S(2)}, u32[]{:S(2)}) collective-permute-start(bf16[16,128,128]{2,1,0:T(8,128)(2,1)S(1)} %bitcast.72), channel_id=1, source_target_pairs={{0,4},{4,0},{8,12},{12,8},{16,20},{20,16},{24,28},{28,24},{1,5},{5... | collective-permute-start | bytes 1572872 | tf_op jit(solution)/shard_map/ppermute | solution.py:258
  62.9 11.3 %collective-permute-start.8 = (bf16[16,128,128]{2,1,0:T(8,128)(2,1)}, bf16[16,128,128]{2,1,0:T(8,128)(2,1)}, u32[]{:S(2)}, u32[]{:S(2)}) collective-permute-start(bf16[16,128,128]{2,1,0:T(8,128)(2,1)} %collective-permute-done.7.rest_3_), channel_id=1, source_target_pairs={{0,1},{1,0},{2,3},{3,2},{4,5},{5,4},{6,7},{7,6},{8,9},{9,8},{10,11... | collective-permute-start | bytes 1572872 | tf_op jit(solution)/shard_map/ppermute | solution.py:258
  63.5 10.7 %collective-permute-start.11 = (bf16[16,128,128]{2,1,0:T(8,128)(2,1)S(1)}, bf16[16,128,128]{2,1,0:T(8,128)(2,1)}, u32[]{:S(2)}, u32[]{:S(2)}) collective-permute-start(bf16[16,128,128]{2,1,0:T(8,128)(2,1)S(1)} %collective-permute-done.10.rest_2_), channel_id=1, source_target_pairs={{0,4},{4,0},{8,12},{12,8},{16,20},{20,16},{24,28},{28,24},{1,5},{5... | collective-permute-start | bytes 1572872 | tf_op jit(solution)/shard_map/ppermute | solution.py:258
  65.3 8.8 %collective-permute-start.13 = (bf16[16,128,128]{2,1,0:T(8,128)(2,1)S(1)}, bf16[16,128,128]{2,1,0:T(8,128)(2,1)}, u32[]{:S(2)}, u32[]{:S(2)}) collective-permute-start(bf16[16,128,128]{2,1,0:T(8,128)(2,1)S(1)} %collective-permute-done.12.rest_4_), channel_id=1, source_target_pairs={{0,4},{4,0},{8,12},{12,8},{16,20},{20,16},{24,28},{28,24},{1,5},{5... | collective-permute-start | bytes 1572872 | tf_op jit(solution)/shard_map/ppermute | solution.py:258
  65.3 8.8 %collective-permute-start.15 = (bf16[16,128,128]{2,1,0:T(8,128)(2,1)S(1)}, bf16[16,128,128]{2,1,0:T(8,128)(2,1)}, u32[]{:S(2)}, u32[]{:S(2)}) collective-permute-start(bf16[16,128,128]{2,1,0:T(8,128)(2,1)S(1)} %collective-permute-done.14.rest_6_), channel_id=1, source_target_pairs={{0,4},{4,0},{8,12},{12,8},{16,20},{20,16},{24,28},{28,24},{1,5},{5... | collective-permute-start | bytes 1572872 | tf_op jit(solution)/shard_map/ppermute | solution.py:258
  74.2 1.0 copy-start.1
  75.2 1.0 copy-start.3
  76.2 1.0 copy-start.5
  79.5 14.2 %collective-permute-start.19 = (bf16[8,128,128]{2,1,0:T(8,128)(2,1)S(1)}, bf16[8,128,128]{2,1,0:T(8,128)(2,1)S(1)}, u32[]{:S(2)}, u32[]{:S(2)}) collective-permute-start(bf16[8,128,128]{2,1,0:T(8,128)(2,1)S(1)} %get-tuple-element.99.rest_0_), channel_id=1, source_target_pairs={{0,1},{1,0},{2,3},{3,2},{4,5},{5,4},{6,7},{7,6},{8,9},{9,8},{10,11... | collective-permute-start | bytes 786440 | tf_op jit(solution)/shard_map/ppermute | solution.py:258
  79.9 18.4 %collective-permute-start.20 = (bf16[8,128,128]{2,1,0:T(8,128)(2,1)S(1)}, bf16[8,128,128]{2,1,0:T(8,128)(2,1)S(1)}, u32[]{:S(2)}, u32[]{:S(2)}) collective-permute-start(bf16[8,128,128]{2,1,0:T(8,128)(2,1)S(1)} %get-tuple-element.99.rest_0_), channel_id=1, source_target_pairs={{0,3},{1,2},{2,1},{3,0},{4,7},{5,6},{6,5},{7,4},{8,11},{9,10},{10,... | collective-permute-start | bytes 786440 | tf_op jit(solution)/shard_map/ppermute | solution.py:258
  85.4 13.7 %collective-permute-start.16 = (bf16[8,128,128]{2,1,0:T(8,128)(2,1)S(1)}, bf16[8,128,128]{2,1,0:T(8,128)(2,1)S(1)}, u32[]{:S(2)}, u32[]{:S(2)}) collective-permute-start(bf16[8,128,128]{2,1,0:T(8,128)(2,1)S(1)} %get-tuple-element.86.rest_0_), channel_id=1, source_target_pairs={{0,1},{1,0},{2,3},{3,2},{4,5},{5,4},{6,7},{7,6},{8,9},{9,8},{10,11... | collective-permute-start | bytes 786440 | tf_op jit(solution)/shard_map/ppermute | solution.py:258
  86.2 23.3 %collective-permute-start.17 = (bf16[8,128,128]{2,1,0:T(8,128)(2,1)S(1)}, bf16[8,128,128]{2,1,0:T(8,128)(2,1)S(1)}, u32[]{:S(2)}, u32[]{:S(2)}) collective-permute-start(bf16[8,128,128]{2,1,0:T(8,128)(2,1)S(1)} %get-tuple-element.86.rest_0_), channel_id=1, source_target_pairs={{0,3},{1,2},{2,1},{3,0},{4,7},{5,6},{6,5},{7,4},{8,11},{9,10},{10,... | collective-permute-start | bytes 786440 | tf_op jit(solution)/shard_map/ppermute | solution.py:258
  98.2 12.0 %collective-permute-start.21 = (bf16[8,128,128]{2,1,0:T(8,128)(2,1)S(1)}, bf16[8,128,128]{2,1,0:T(8,128)(2,1)S(1)}, u32[]{:S(2)}, u32[]{:S(2)}) collective-permute-start(bf16[8,128,128]{2,1,0:T(8,128)(2,1)S(1)} %collective-permute-done.20.rest_3_), channel_id=1, source_target_pairs={{0,1},{1,0},{2,3},{3,2},{4,5},{5,4},{6,7},{7,6},{8,9},{9,8},{10,11... | collective-permute-start | bytes 786440 | tf_op jit(solution)/shard_map/ppermute | solution.py:258
  109.5 6.4 %collective-permute-start.18 = (bf16[8,128,128]{2,1,0:T(8,128)(2,1)S(1)}, bf16[8,128,128]{2,1,0:T(8,128)(2,1)S(1)}, u32[]{:S(2)}, u32[]{:S(2)}) collective-permute-start(bf16[8,128,128]{2,1,0:T(8,128)(2,1)S(1)} %collective-permute-done.17.rest_3_), channel_id=1, source_target_pairs={{0,1},{1,0},{2,3},{3,2},{4,5},{5,4},{6,7},{7,6},{8,9},{9,8},{10,11... | collective-permute-start | bytes 786440 | tf_op jit(solution)/shard_map/ppermute | solution.py:258
  123.2 2.7 %collective-permute-start.27 = (bf16[4,8,128,128]{3,2,1,0:T(8,128)(2,1)S(1)}, bf16[4,8,128,128]{3,2,1,0:T(8,128)(2,1)S(1)}, u32[]{:S(2)}, u32[]{:S(2)}) collective-permute-start(bf16[4,8,128,128]{3,2,1,0:T(8,128)(2,1)S(1)} %get-tuple-element.112), channel_id=1, source_target_pairs={{0,4},{4,0},{8,12},{12,8},{16,20},{20,16},{24,28},{28,24},{1,5},{5... | collective-permute-start | bytes 3145736 | tf_op jit(solution)/shard_map/ppermute | solution.py:258
  123.3 4.6 %collective-permute-start.22 = (bf16[4,8,128,128]{3,2,1,0:T(8,128)(2,1)S(1)}, bf16[4,8,128,128]{3,2,1,0:T(8,128)(2,1)S(1)}, u32[]{:S(2)}, u32[]{:S(2)}) collective-permute-start(bf16[4,8,128,128]{3,2,1,0:T(8,128)(2,1)S(1)} %get-tuple-element.104), channel_id=1, source_target_pairs={{0,4},{4,0},{8,12},{12,8},{16,20},{20,16},{24,28},{28,24},{1,5},{5... | collective-permute-start | bytes 3145736 | tf_op jit(solution)/shard_map/ppermute | solution.py:258
  124.0 6.1 %collective-permute-start.24 = (bf16[128,512]{1,0:T(8,128)(2,1)S(1)}, bf16[128,512]{1,0:T(8,128)(2,1)S(1)}, u32[]{:S(2)}, u32[]{:S(2)}) collective-permute-start(bf16[128,512]{1,0:T(8,128)(2,1)S(1)} %get-tuple-element.109), channel_id=1, source_target_pairs={{0,4},{4,0},{8,12},{12,8},{16,20},{20,16},{24,28},{28,24},{1,5},{5... | collective-permute-start | bytes 393224 | tf_op jit(solution)/shard_map/ppermute | solution.py:258
  126.3 16.9 %collective-permute-start.28 = (bf16[2,8,128,128]{3,2,1,0:T(8,128)(2,1)S(1)}, bf16[2,8,128,128]{3,2,1,0:T(8,128)(2,1)S(1)}, u32[]{:S(2)}, u32[]{:S(2)}) collective-permute-start(bf16[2,8,128,128]{3,2,1,0:T(8,128)(2,1)S(1)} %get-tuple-element.119), channel_id=1, source_target_pairs={{0,16},{4,20},{8,24},{12,28},{16,0},{20,4},{24,8},{28,12},{1,17},{... | collective-permute-start | bytes 1572872 | tf_op jit(solution)/shard_map/ppermute | solution.py:258
  128.3 14.9 %collective-permute-start.23 = (bf16[2,8,128,128]{3,2,1,0:T(8,128)(2,1)S(1)}, bf16[2,8,128,128]{3,2,1,0:T(8,128)(2,1)S(1)}, u32[]{:S(2)}, u32[]{:S(2)}) collective-permute-start(bf16[2,8,128,128]{3,2,1,0:T(8,128)(2,1)S(1)} %get-tuple-element.121), channel_id=1, source_target_pairs={{0,8},{4,12},{8,0},{12,4},{16,24},{20,28},{24,16},{28,20},{1,9},{5... | collective-permute-start | bytes 1572872 | tf_op jit(solution)/shard_map/ppermute | solution.py:258
  130.1 13.1 %collective-permute-start.25 = (bf16[128,512]{1,0:T(8,128)(2,1)S(1)}, bf16[128,512]{1,0:T(8,128)(2,1)S(1)}, u32[]{:S(2)}, u32[]{:S(2)}) collective-permute-start(bf16[128,512]{1,0:T(8,128)(2,1)S(1)} %add_convert_fusion.12), channel_id=1, source_target_pairs={{0,16},{4,20},{8,24},{12,28},{16,0},{20,4},{24,8},{28,12},{1,17},{... | collective-permute-start | bytes 393224 | tf_op jit(solution)/shard_map/ppermute | solution.py:258
  143.2 6.4 %collective-permute-start.30 = (bf16[128,512]{1,0:T(8,128)(2,1)S(1)}, bf16[128,512]{1,0:T(8,128)(2,1)S(1)}, u32[]{:S(2)}, u32[]{:S(2)}) collective-permute-start(bf16[128,512]{1,0:T(8,128)(2,1)S(1)} %convert_add_fusion.5), channel_id=1, source_target_pairs={{0,8},{4,12},{8,0},{12,4},{16,24},{20,28},{24,16},{28,20},{1,9},{5... | collective-permute-start | bytes 393224 | tf_op jit(solution)/shard_map/ppermute | solution.py:258
  144.9 8.9 %collective-permute-start.29 = (bf16[8,128,128]{2,1,0:T(8,128)(2,1)S(1)}, bf16[8,128,128]{2,1,0:T(8,128)(2,1)S(1)}, u32[]{:S(2)}, u32[]{:S(2)}) collective-permute-start(bf16[8,128,128]{2,1,0:T(8,128)(2,1)S(1)} %get-tuple-element.127), channel_id=1, source_target_pairs={{0,8},{4,12},{8,0},{12,4},{16,24},{20,28},{24,16},{28,20},{1,9},{5... | collective-permute-start | bytes 786440 | tf_op jit(solution)/shard_map/ppermute | solution.py:258
  145.6 8.1 %collective-permute-start.26 = (bf16[8,128,128]{2,1,0:T(8,128)(2,1)S(1)}, bf16[8,128,128]{2,1,0:T(8,128)(2,1)S(1)}, u32[]{:S(2)}, u32[]{:S(2)}) collective-permute-start(bf16[8,128,128]{2,1,0:T(8,128)(2,1)S(1)} %get-tuple-element.129), channel_id=1, source_target_pairs={{0,16},{4,20},{8,24},{12,28},{16,0},{20,4},{24,8},{28,12},{1,17},{... | collective-permute-start | bytes 786440 | tf_op jit(solution)/shard_map/ppermute | solution.py:258
  149.7 4.1 %collective-permute-start.31 = (f32[128,512]{1,0:T(8,128)S(1)}, f32[128,512]{1,0:T(8,128)S(1)}, u32[]{:S(2)}, u32[]{:S(2)}) collective-permute-start(f32[128,512]{1,0:T(8,128)S(1)} %convert_add_fusion.4.refs_5_), channel_id=1, source_target_pairs={{0,4},{4,0},{8,12},{12,8},{16,20},{20,16},{24,28},{28,24},{1,5},{5... | collective-permute-start | bytes 786440 | tf_op jit(solution)/shard_map/ppermute | solution.py:258

commit v12 on v11

--- a/solution.py
+++ b/solution.py
@@ -37,18 +37,19 @@
     lax.fori_loop(0, COPIES, piece, 0)
 
 
-def spread_kernel(first, pieces, cols_ref, me_ref, tiles_ref, *rest):
-    vals, rest = rest[:pieces], rest[pieces:]
+def spread_kernel(first, start, earlier, cols_ref, me_ref, tiles_ref, vals_ref, *rest):
+    tiles_ref = tiles_ref.at[pl.ds(start, vals_ref.shape[0])]
+    sums, rest = rest[:earlier], rest[earlier:]
     if first:
         mask_ref, *rest = rest
         outs, (mask_out, acc, held, sems, left_ref, mask_held) = rest[: 2 * GROUPS], rest[2 * GROUPS :]
         loads = [
-            pltpu.make_async_copy(vals[0], left_ref, sems.at[COPIES]),
+            pltpu.make_async_copy(vals_ref, left_ref, sems.at[COPIES]),
             pltpu.make_async_copy(mask_ref, mask_held, sems.at[COPIES + 1]),
         ]
         loads[0].start()
     else:
-        outs, (acc, held, sems, left_ref) = rest[: 2 * GROUPS], rest[2 * GROUPS :]
+        outs, (acc, held, sems) = rest[: 2 * GROUPS], rest[2 * GROUPS :]
     for i in range(COPIES):
         tile_copy(tiles_ref, held, sems, i).start()
     if first:
@@ -58,18 +59,14 @@
     me = me_ref[0]
     if first:
         loads[0].wait()
-    else:
-        for g in range(pieces):
-            count = vals[g].shape[0]
-            left_ref[g * count : (g + 1) * count] = vals[g][...]
 
     def one_row(r):
-        left = left_ref[r].astype(F32).T.astype(BF16) if first else left_ref[r]
+        left = left_ref[r].astype(F32).T.astype(BF16) if first else vals_ref[r]
         for k in range(0, per_row, 2):
             pair = jnp.concatenate([held[r, k], held[r, k + 1]], axis=1)
             both = jnp.dot(left, pair, preferred_element_type=F32)
             for side in range(2):
-                acc[cols_ref[r, k + side]] += both[:, side * size : (side + 1) * size]
+                acc[cols_ref[start + r, k + side]] += both[:, side * size : (side + 1) * size]
 
     over_rows(tiles_ref, held, sems, one_row)
     halves, count = outs[0].shape[:2]
@@ -77,40 +74,41 @@
         for side in range(2):
             for rel in range(halves):
                 owner = jnp.bitwise_xor(me, 2 * rel + side)
-                start = (owner * GROUPS + g) * count
-                outs[2 * g + side][rel] = acc[pl.ds(start, count)].astype(BF16)
+                total = acc[pl.ds((owner * GROUPS + g) * count, count)]
+                if earlier:
+                    total = total + sums[2 * g + side][rel].astype(F32)
+                outs[2 * g + side][rel] = total.astype(BF16)
     if first:
         loads[1].wait()
         for b in range(mask_held.shape[0]):
             mask_out[b] = mask_held[b].astype(F32).T.astype(BF16)
 
 
-def spread(edge_tiles, block_cols, vals, me, rows, mask=None):
+def spread(edge_tiles, block_cols, vals, me, rows, mask=None, start=0, earlier=()):
     blocks, _, size, _ = edge_tiles.shape
     first = mask is not None
-    feat = vals[0].shape[2] if first else vals[0].shape[1]
+    feat = vals.shape[2] if first else vals.shape[1]
     out = jax.ShapeDtypeStruct((rows // 2, blocks // GROUPS, feat, size), BF16)
     outs = [out] * (2 * GROUPS)
     scratch = [
         pltpu.VMEM((rows * blocks, feat, size), F32),
-        pltpu.VMEM(edge_tiles.shape, BF16),
+        pltpu.VMEM((vals.shape[0],) + edge_tiles.shape[1:], BF16),
         pltpu.SemaphoreType.DMA((COPIES + 2,)),
     ]
     anywhere = pl.BlockSpec(memory_space=pl.ANY)
     if first:
         outs.append(jax.ShapeDtypeStruct((blocks, feat, size), BF16))
-        scratch += [pltpu.VMEM(v.shape, v.dtype) for v in (vals[0], mask)]
-        args, place = [vals[0], mask], anywhere
+        scratch += [pltpu.VMEM(v.shape, v.dtype) for v in (vals, mask)]
+        args, place = [vals, mask], anywhere
     else:
-        scratch.append(pltpu.VMEM((blocks, feat, size), BF16))
-        args, place = vals, VMEM
-    return pl.pallas_call(
-        functools.partial(spread_kernel, first, len(vals)),
+        args, place = [vals, *earlier], VMEM
+    return pl.pallas_call(
+        functools.partial(spread_kernel, first, start, len(earlier)),
         out_shape=outs,
         in_specs=[SMEM, SMEM, anywhere] + [place] * len(args),
         out_specs=[VMEM] * len(outs),
         scratch_shapes=scratch,
-        compiler_params=params(48),
+        compiler_params=params(48 if first else 28),
         cost_estimate=pl.CostEstimate(flops=2 * edge_tiles.size * feat, bytes_accessed=30_000_000, transcendentals=0),
         name="spread",
     )(block_cols, me, edge_tiles, *args)
@@ -231,27 +229,94 @@
     )(col, *args)
 
 
-def weight_terms_kernel(me_ref, second_ref, *refs):
-    firsts, (keep_ref, send_ref) = refs[:-2], refs[-2:]
-    cols, feat, width = second_ref.shape
+def dense_early_kernel(cols, late, col_ref, weight_ref, *rest):
+    shards, (side_ref, out_ref, grad_ref) = rest[: cols - 1], rest[cols - 1 :]
+    blocks, feat, size = shards[0].shape
+    here = [m for m in range(cols) if m != late]
+    per = blocks // GROUPS
+    weight = jnp.concatenate([weight_ref[:, m * feat : (m + 1) * feat] for m in here], axis=1)
+    total = None
+    for i in range(GROUPS):
+        mine = range(i * per, (i + 1) * per)
+        whole = jnp.concatenate([jnp.concatenate([shard[b] for b in mine], axis=1) for shard in shards], axis=0)
+        out_ref[i] = jnp.dot(weight, whole, preferred_element_type=F32)
+        term = jnp.dot(whole, jnp.concatenate([side_ref[b] for b in mine], axis=0), preferred_element_type=F32)
+        total = term if total is None else total + term
+    for i, m in enumerate(here):
+        grad_ref[jnp.bitwise_xor(col_ref[0], m)] = total[i * feat : (i + 1) * feat]
+
+
+def dense_early(weight, shards, side, col, late):
+    blocks, feat, size = shards[0].shape
+    cols = len(shards)
+    args = [weight, *(v for m, v in enumerate(shards) if m != late), side]
+    return pl.pallas_call(
+        functools.partial(dense_early_kernel, cols, late),
+        out_shape=[
+            jax.ShapeDtypeStruct((GROUPS, feat, blocks // GROUPS * size), F32),
+            jax.ShapeDtypeStruct((cols, feat, side.shape[2]), F32),
+        ],
+        in_specs=[SMEM] + [VMEM] * len(args),
+        out_specs=[VMEM] * 2,
+        compiler_params=params(16),
+        name="dense_early",
+    )(col, *args)
+
+
+def dense_late_kernel(late, weight_ref, shard_ref, part_ref, side_ref, mask_ref, *rest):
+    outs, grad_ref = rest[:GROUPS], rest[GROUPS]
+    blocks, feat, size = shard_ref.shape
+    per = blocks // GROUPS
+    weight = weight_ref[:, late * feat : (late + 1) * feat]
+    total = None
+    for i, out in enumerate(outs):
+        mine = range(i * per, (i + 1) * per)
+        whole = jnp.concatenate([shard_ref[b] for b in mine], axis=1)
+        res = part_ref[i] + jnp.dot(weight, whole, preferred_element_type=F32)
+        for k, b in enumerate(mine):
+            out[k] = (res[:, k * size : (k + 1) * size] * mask_ref[b].astype(F32)).astype(BF16)
+        term = jnp.dot(whole, jnp.concatenate([side_ref[b] for b in mine], axis=0), preferred_element_type=F32)
+        total = term if total is None else total + term
+    grad_ref[...] = total
+
+
+def dense_late(weight, shard, part, side, mask, late):
+    blocks, feat, size = shard.shape
+    return pl.pallas_call(
+        functools.partial(dense_late_kernel, late),
+        out_shape=[jax.ShapeDtypeStruct((blocks // GROUPS, feat, size), BF16)] * GROUPS
+        + [jax.ShapeDtypeStruct((feat, side.shape[2]), F32)],
+        in_specs=[VMEM] * 5,
+        out_specs=[VMEM] * (GROUPS + 1),
+        compiler_params=params(16),
+        name="dense_late",
+    )(weight, shard, part, side, mask)
+
+
+def weight_terms_kernel(late, me_ref, col_ref, second_ref, late_ref, *refs):
+    firsts, (keep_ref, send_ref, held) = refs[:-3], refs[-3:]
+    cols = second_ref.shape[0]
     even = jnp.bitwise_and(me_ref[0], 1) == 0
+    held[...] = second_ref[...]
+    held[jnp.bitwise_xor(col_ref[0], late)] = late_ref[...]
     first = jnp.concatenate([sum(r[q] for r in firsts) for q in range(cols)], axis=0).T
-    second = jnp.concatenate([second_ref[q] for q in range(cols)], axis=0).T
+    second = jnp.concatenate([held[q] for q in range(cols)], axis=0).T
     keep_ref[...] = jnp.where(even, second, first)
     send_ref[...] = jnp.where(even, first, second).astype(BF16)
 
 
-def weight_terms(firsts, second, me):
+def weight_terms(firsts, second, last, me, col, late):
     cols, feat, width = second.shape
     shape = (width, cols * feat)
     return pl.pallas_call(
-        weight_terms_kernel,
+        functools.partial(weight_terms_kernel, late),
         out_shape=[jax.ShapeDtypeStruct(shape, F32), jax.ShapeDtypeStruct(shape, BF16)],
-        in_specs=[SMEM] + [VMEM] * (1 + len(firsts)),
+        in_specs=[SMEM, SMEM] + [VMEM] * (2 + len(firsts)),
         out_specs=[VMEM] * 2,
+        scratch_shapes=[pltpu.VMEM(second.shape, F32)],
         compiler_params=params(8),
         name="weight_terms",
-    )(me, second, *firsts)
+    )(me, col, second, last, *firsts)
 
 
 def swap(value, mask, axis):
@@ -262,30 +327,31 @@
     return (a.astype(F32) + b.astype(F32)).astype(BF16)
 
 
-def scatter_group(keep, got, masks, beside):
-    left = sorted(masks, reverse=True)
-    for mask in masks:
-        axis = left.index(mask)
-        part = lambda v, i: lax.index_in_dim(v, i, axis, keepdims=False)
-        sent = swap(add(part(keep, 1), part(got, 1)), mask, "row")
-        keep = add(part(keep, 0), part(got, 0))
-        got = sent
-        left.remove(mask)
-        if beside is not None and mask == masks[0]:
-            got, beside = lax.optimization_barrier((got, beside))
-    return [keep, got], beside
-
-
-def scatter(pieces, rows, beside=None):
-    masks = [1 << b for b in range(1, rows.bit_length() - 1)]
-    lead = (2,) * len(masks)
-    done = []
-    for g in range(GROUPS):
-        keep, got = pieces[2 * g], swap(pieces[2 * g + 1], 1, "row")
-        order = masks if g % 2 == 0 else masks[::-1]
-        terms, beside = scatter_group(keep.reshape(lead + keep.shape[1:]), got.reshape(lead + got.shape[1:]), order, beside)
-        done.append(terms)
-    return done, beside
+def scatter(pieces, rows, value=None):
+    chips = [1 << b for b in range(1, rows.bit_length() - 1)]
+    shape = (2,) * len(chips) + pieces[0].shape[1:]
+    keeps = [pieces[2 * g].reshape(shape) for g in range(GROUPS)]
+    gots = [swap(pieces[2 * g + 1], 1, "row").reshape(shape) for g in range(GROUPS)]
+    orders = [chips if g % 2 == 0 else chips[::-1] for g in range(GROUPS)]
+    lefts = [chips[::-1] for _ in range(GROUPS)]
+    for level in range(len(chips)):
+        masks = [order[level] for order in orders]
+        sent = []
+        for g in range(GROUPS):
+            axis = lefts[g].index(masks[g])
+            lefts[g] = [m for m in lefts[g] if m != masks[g]]
+            half = lambda v, i: lax.index_in_dim(v, i, axis, keepdims=False)
+            sent.append(add(half(keeps[g], 1), half(gots[g], 1)))
+            keeps[g] = add(half(keeps[g], 0), half(gots[g], 0))
+        if value is not None:
+            keeps, value = lax.optimization_barrier((keeps, value))
+        gots = [swap(sent[g], masks[g], "row") for g in range(GROUPS)]
+        if value is not None:
+            value = value.astype(BF16)
+            value = value.astype(F32) + swap(value, chips[-1 - level], "row").astype(F32)
+            if level < len(chips) - 1:
+                gots, value = lax.optimization_barrier((gots, value))
+    return [t for pair in zip(keeps, gots) for t in pair], value
 
 
 def gather_columns(own, cols, beside=()):
@@ -293,13 +359,6 @@
         near, far, beside = lax.optimization_barrier((swap(own, 1, "col"), swap(own, 3, "col"), beside))
         return [own, near, swap(far, 1, "col"), far], beside
     return [own] + [swap(own, m, "col") for m in range(1, cols)], beside
-
-
-def over_chips(value, masks):
-    for mask in masks:
-        value = value.astype(BF16)
-        value = value.astype(F32) + swap(value, mask, "row").astype(F32)
-    return value
 
 
 def per_device(
@@ -310,7 +369,6 @@
     me_at, col_at = me.reshape(1), col.reshape(1)
     size = edge_tiles.shape[2]
     per = edge_tiles.shape[0] // GROUPS
-    chips = [1 << b for b in range(1, rows.bit_length() - 1)]
     cut = lambda v, g: v[g * per : (g + 1) * per]
     blocked = lambda v: v.reshape(v.shape[0] // size, size, v.shape[1])
     after = lax.optimization_barrier
@@ -320,32 +378,32 @@
         order = [lax.dynamic_index_in_dim(split, col ^ m, 1, keepdims=False) for m in range(cols)]
         return jnp.concatenate(order, axis=1)
 
-    *pieces, mask = spread(edge_tiles, block_cols, [blocked(grad_out)], me_at, rows, blocked(relu_mask))
+    *pieces, mask = spread(edge_tiles, block_cols, blocked(grad_out), me_at, rows, blocked(relu_mask))
     terms, _ = scatter(pieces, rows)
-    own, node_feats = after((finish([t for pair in terms for t in pair])[0], blocked(node_feats)))
+    own, node_feats = after((finish(terms)[0], blocked(node_feats)))
     own, weight_one, weight_two = after((own, weight_one, weight_two))
     weight_one, weight_two = by_distance(weight_one), by_distance(weight_two)
     shards, _ = gather_columns(own, cols)
     parts = [node_feats] + [swap(node_feats, rel, "row") for rel in range(2, rows, 2)]
     parts = [v for part in parts for v in (part, swap(part, 1, "row"))]
-    shards, parts = after((shards, parts))
-    *deltas, second = dense(weight_two, shards, blocked(hidden_act), mask, col_at, GROUPS)
+    late = 2
+    hidden = blocked(hidden_act)
+    part, second = dense_early(weight_two, shards, hidden, col_at, late)
+    arrived, parts = after((shards[late], parts))
+    *deltas, last = dense_late(weight_two, arrived, part, hidden, mask, late)
     deltas[0], parts = after((deltas[0], parts))
     agg_feats = aggregate(edge_tiles, block_cols, parts, me_at)
-    inputs, firsts = [], []
+    pieces, firsts = (), []
     for g in range(GROUPS):
         shards, beside = gather_columns(deltas[g], cols, agg_feats if g == 0 else ())
         agg_feats = beside if g == 0 else agg_feats
         out, grad = dense(weight_one, shards, cut(agg_feats, g), None, col_at, 1)
-        inputs.append(out)
+        pieces = spread(edge_tiles, block_cols, out, me_at, rows, None, g * per, pieces)
         firsts.append(grad)
-    pieces = spread(edge_tiles, block_cols, inputs, me_at, rows)
-    keep, send = weight_terms(firsts, second, me_at)
-    value = over_chips(keep + swap(send, 1, "row").astype(F32), chips[-1:])
-    terms, value = scatter(pieces, rows, value)
-    value = over_chips(value, chips[:-1])
+    keep, send = weight_terms(firsts, second, last, me_at, col_at, late)
+    terms, value = scatter(pieces, rows, keep + swap(send, 1, "row").astype(F32))
     grads = [me_at, value, swap(value, 1, "row")]
-    out, first_grad, second_grad = finish([t for pair in terms for t in pair], grads)
+    out, first_grad, second_grad = finish(terms, grads)
     return out.reshape(-1, out.shape[2]), first_grad, second_grad
 
 

time: 156 us -> 158 us (1.013)
  Pallas kernels: 25.1 us -> 30.5 us
  starting transfers between devices: 34.6 us -> 32 us
  waiting for transfers between devices: 85.7 us -> 83.5 us
    pallas_call x3 -> x6, Pallas kernels: 13.9 us -> 20 us  [the longest x3 16.2 us: spread(): pl.pallas_call(functools.partial(spread_kernel, first, start, len(earlier...]
    ppermute x32, starting transfers between devices: 34.6 us -> 32 us  [swap(): lax.ppermute(value, axis, [(i, i ^ mask) for i in range(lax.axis_size(axi...]
    ppermute x32, waiting for transfers between devices: 85.7 us -> 83.5 us  [swap(): lax.ppermute(value, axis, [(i, i ^ mask) for i in range(lax.axis_size(axi...]
    pallas_call x3 -> x2, Pallas kernels: 3.37 us -> 2.2 us  [dense(): pl.pallas_call(functools.partial(dense_kernel, cols, mask is not None, pi...]
    unnamed x22 -> x40, local copies, waits for them, and re-layouts: 5.66 us -> 6.35 us
  transfers between devices with their start and end apart: 32 -> 32, of which waited for: 16 -> 15; matrix products, arithmetic and copies ran while one was open for 2% -> 3% of each run, Pallas kernels for 5% -> 9%
where the time goes in v12:
time: 158 us; the launch traced here: 157 us
  waiting for transfers between devices  83.5 us (53%)
  starting transfers between devices  32 us (20%)
  Pallas kernels  30.5 us (19%)
  local copies, waits for them, and re-layouts  7.01 us (4%)
  other arithmetic  3.29 us (2%)
    ppermute x32, waiting for transfers between devices, swap(): lax.ppermute(value, axis, [(i, i ^ mask) for i in range(lax.axis_size(axi...  83.5 us
    ppermute x32, starting transfers between devices, swap(): lax.ppermute(value, axis, [(i, i ^ mask) for i in range(lax.axis_size(axi...  32 us
    pallas_call x3, Pallas kernels, spread(): pl.pallas_call(functools.partial(spread_kernel, first, start, len(earlier...  16.2 us
    pallas_call x1, Pallas kernels, aggregate(): pl.pallas_call(aggregate_kernel, out_shape=jax.ShapeDtypeStruct((blocks,...  7.04 us
    unnamed x40, local copies, waits for them, and re-layouts  6.35 us
  transfers between devices with their start and end apart: 32, of which 15 were waited for; matrix products, arithmetic and copies ran while one was open for 3% of the time, Pallas kernels for 9%

profile of v12, /device:TPU:0, one launch (start us, length us, event | category | flops | bytes accessed | tf_op | source)
XLA Modules:
  0.0 157.4 jit_solution(3026433971336298836)
XLA Ops:
  0.6 1.0 copy-done.8
  1.7 0.7 copy-done.9
  2.4 7.0 %spread.3 = (bf16[4,8,128,128]{3,2,1,0:T(8,128)(2,1)S(1)}, bf16[4,8,128,128]{3,2,1,0:T(8,128)(2,1)S(1)}, bf16[4,8,128,128]{3,2,1,0:T(8,128)(2,1)S(1)}, bf16[4,8,...) custom-call(s32[16,20]{1,0:T(8,128)S(1)} %copy-done.9, s32[1]{0:T(128)} %bitcast.me_ref.refs_4_, ...), custom_call_target="tpu_custom_call" | custom-call | flops 1342177280 | bytes 30000000 | tf_op jit(solution)/shard_map/spread/pallas_call | solution.py:105
  9.5 0.5 collective-permute-start
  10.1 2.2 %collective-permute-done = bf16[4,8,128,128]{3,2,1,0:T(8,128)(2,1)S(1)} collective-permute-done((bf16[4,8,128,128]{3,2,1,0:T(8,128)(2,1)S(1)}, bf16[4,8,128,128]{3,2,1,0:T(8,128)(2,1)S(1)}, u32[]{:S(2)}, u32[]{:S(2)}) %collective-permute-start) | collective-permute-done | bytes 1048608 | tf_op jit(solution)/shard_map/ppermute | solution.py:323
  12.3 0.5 add_convert_fusion.7
  12.7 2.9 %collective-permute-start.1 = (bf16[2,8,128,128]{3,2,1,0:T(8,128)(2,1)S(1)}, bf16[2,8,128,128]{3,2,1,0:T(8,128)(2,1)S(1)}, u32[]{:S(2)}, u32[]{:S(2)}) collective-permute-start(bf16[2,8,128,128]{3,2,1,0:T(8,128)(2,1)S(1)} %get-tuple-element.142), channel_id=1, source_target_pairs={{0,8},{4,12},{8,0},{12,4},{16,24},{20,28},{24,16},{28,20},{1,9},{5... | collective-permute-start | bytes 1572872 | tf_op jit(solution)/shard_map/ppermute | solution.py:323
  15.7 0.5 add_convert_fusion.5
  16.1 1.6 %collective-permute-start.4 = (bf16[2,8,128,128]{3,2,1,0:T(8,128)(2,1)S(1)}, bf16[2,8,128,128]{3,2,1,0:T(8,128)(2,1)S(1)}, u32[]{:S(2)}, u32[]{:S(2)}) collective-permute-start(bf16[2,8,128,128]{3,2,1,0:T(8,128)(2,1)S(1)} %get-tuple-element.140), channel_id=1, source_target_pairs={{0,16},{4,20},{8,24},{12,28},{16,0},{20,4},{24,8},{28,12},{1,17},{... | collective-permute-start | bytes 1572872 | tf_op jit(solution)/shard_map/ppermute | solution.py:323
  17.7 10.2 %collective-permute-done.1 = bf16[2,8,128,128]{3,2,1,0:T(8,128)(2,1)S(1)} collective-permute-done((bf16[2,8,128,128]{3,2,1,0:T(8,128)(2,1)S(1)}, bf16[2,8,128,128]{3,2,1,0:T(8,128)(2,1)S(1)}, u32[]{:S(2)}, u32[]{:S(2)}) %collective-permute-start.1) | collective-permute-done | bytes 524320 | tf_op jit(solution)/shard_map/ppermute | solution.py:323
  28.0 1.8 %collective-permute-start.2 = (bf16[8,128,128]{2,1,0:T(8,128)(2,1)S(1)}, bf16[8,128,128]{2,1,0:T(8,128)(2,1)S(1)}, u32[]{:S(2)}, u32[]{:S(2)}) collective-permute-start(bf16[8,128,128]{2,1,0:T(8,128)(2,1)S(1)} %get-tuple-element.149), channel_id=1, source_target_pairs={{0,16},{4,20},{8,24},{12,28},{16,0},{20,4},{24,8},{28,12},{1,17},{... | collective-permute-start | bytes 786440 | tf_op jit(solution)/shard_map/ppermute | solution.py:323
  30.0 1.5 collective-permute-start.5
  31.6 4.4 %collective-permute-done.2.refs_1_ = bf16[8,128,128]{2,1,0:T(8,128)(2,1)S(1)} collective-permute-done((bf16[8,128,128]{2,1,0:T(8,128)(2,1)S(1)}, bf16[8,128,128]{2,1,0:T(8,128)(2,1)S(1)}, u32[]{:S(2)}, u32[]{:S(2)}) %collective-permute-start.2) | collective-permute-done | bytes 262176 | tf_op jit(solution)/shard_map/ppermute | solution.py:323
  35.9 1.4 collective-permute-done.5.refs_3_
  37.4 3.7 %collective-permute-start.7 = (bf16[16,128,128]{2,1,0:T(8,128)(2,1)S(1)}, bf16[16,128,128]{2,1,0:T(8,128)(2,1)}, u32[]{:S(2)}, u32[]{:S(2)}) collective-permute-start(bf16[16,128,128]{2,1,0:T(8,128)(2,1)S(1)} %finish.2.rest_0_), channel_id=1, source_target_pairs={{0,3},{1,2},{2,1},{3,0},{4,7},{5,6},{6,5},{7,4},{8,11},{9,10},{10,... | collective-permute-start | bytes 1572872 | tf_op jit(solution)/shard_map/ppermute | solution.py:323
  41.1 2.6 %collective-permute-start.14 = (bf16[16,128,128]{2,1,0:T(8,128)(2,1)S(1)}, bf16[16,128,128]{2,1,0:T(8,128)(2,1)S(1)}, u32[]{:S(2)}, u32[]{:S(2)}) collective-permute-start(bf16[16,128,128]{2,1,0:T(8,128)(2,1)S(1)} %bitcast.89), channel_id=1, source_target_pairs={{0,24},{4,28},{8,16},{12,20},{16,8},{20,12},{24,0},{28,4},{1,25},{... | collective-permute-start | bytes 1572872 | tf_op jit(solution)/shard_map/ppermute | solution.py:323
  43.7 0.5 collective-permute-start.12
  44.2 0.5 collective-permute-start.10
  44.7 9.6 %collective-permute-done.7.rest_2_ = bf16[16,128,128]{2,1,0:T(8,128)(2,1)} collective-permute-done((bf16[16,128,128]{2,1,0:T(8,128)(2,1)S(1)}, bf16[16,128,128]{2,1,0:T(8,128)(2,1)}, u32[]{:S(2)}, u32[]{:S(2)}) %collective-permute-start.7) | collective-permute-done | bytes 524320 | tf_op jit(solution)/shard_map/ppermute | solution.py:323
  54.3 8.3 %collective-permute-done.6.rest_1_ = bf16[16,128,128]{2,1,0:T(8,128)(2,1)S(1)} collective-permute-done((bf16[16,128,128]{2,1,0:T(8,128)(2,1)S(1)}, bf16[16,128,128]{2,1,0:T(8,128)(2,1)S(1)}, u32[]{:S(2)}, u32[]{:S(2)}) %collective-permute-start.6) | collective-permute-done | bytes 524320 | tf_op jit(solution)/shard_map/ppermute | solution.py:323
  62.6 0.8 copy-done.4
  63.4 1.7 %collective-permute-start.8 = (bf16[16,128,128]{2,1,0:T(8,128)(2,1)}, bf16[16,128,128]{2,1,0:T(8,128)(2,1)}, u32[]{:S(2)}, u32[]{:S(2)}) collective-permute-start(bf16[16,128,128]{2,1,0:T(8,128)(2,1)} %collective-permute-done.7.rest_2_), channel_id=1, source_target_pairs={{0,1},{1,0},{2,3},{3,2},{4,5},{5,4},{6,7},{7,6},{8,9},{9,8},{10,11... | collective-permute-start | bytes 1572872 | tf_op jit(solution)/shard_map/ppermute | solution.py:323
  65.1 0.5 collective-permute-start.13
  65.8 0.6 constant_dynamic-slice_fusion.3
  66.5 1.0 copy-done.5
  67.5 1.9 %dense_early.1 = (f32[2,128,1024]{2,1,0:T(8,128)S(1)}, f32[4,128,128]{2,1,0:T(8,128)S(1)}) custom-call(s32[1]{0:T(128)} %bitcast.1.col_ref, bf16[128,512]{1,0:T(8,128)(2,1)S(1)} %pad_maximum_fusion.1.weight_ref, bf16[16,128,128]{2,1,0:T(8,128)(2,1)S(1)} %finish.2.rest_0_, bf16[16,128,128]{2,1,0:T(8,128)(2,1)S(1)} %copy-done.5, ...), custom_call_target="tpu_custom_call" | custom-call | tf_op jit(solution)/shard_map/dense_early/pallas_call | solution.py:253
  69.4 8.3 %collective-permute-done.8.shard_ref = bf16[16,128,128]{2,1,0:T(8,128)(2,1)} collective-permute-done((bf16[16,128,128]{2,1,0:T(8,128)(2,1)}, bf16[16,128,128]{2,1,0:T(8,128)(2,1)}, u32[]{:S(2)}, u32[]{:S(2)}) %collective-permute-start.8) | collective-permute-done | bytes 524320 | tf_op jit(solution)/shard_map/ppermute | solution.py:323
  77.7 1.0 copy-done.7
  78.8 1.6 %dense_late.1 = (bf16[8,128,128]{2,1,0:T(8,128)(2,1)S(1)}, bf16[8,128,128]{2,1,0:T(8,128)(2,1)S(1)}, f32[128,128]{1,0:T(8,128)S(1)}) custom-call(bf16[128,512]{1,0:T(8,128)(2,1)S(1)} %pad_maximum_fusion.1.weight_ref, bf16[16,128,128]{2,1,0:T(8,128)(2,1)} %collective-permute-done.8.shard_ref, f32[2,128,1024]{2,1,0:T(8,128)S(1)} %get-tuple-element.81.part_ref, ...), custom_call_target="tpu_custom_call" | custom-call | tf_op jit(solution)/shard_map/dense_late/pallas_call | solution.py:285
  80.4 0.9 collective-permute-start.20
  81.3 0.8 collective-permute-start.19
  82.2 2.1 %collective-permute-start.17 = (bf16[8,128,128]{2,1,0:T(8,128)(2,1)S(1)}, bf16[8,128,128]{2,1,0:T(8,128)(2,1)S(1)}, u32[]{:S(2)}, u32[]{:S(2)}) collective-permute-start(bf16[8,128,128]{2,1,0:T(8,128)(2,1)S(1)} %get-tuple-element.83.rest_0_), channel_id=1, source_target_pairs={{0,3},{1,2},{2,1},{3,0},{4,7},{5,6},{6,5},{7,4},{8,11},{9,10},{10,... | collective-permute-start | bytes 786440 | tf_op jit(solution)/shard_map/ppermute | solution.py:323
  84.3 1.1 collective-permute-start.16
  85.5 0.6 copy.58
  86.1 1.0 copy-done.3
  87.1 7.0 %aggregate.1 = bf16[16,128,128]{2,1,0:T(8,128)(2,1)S(1)} custom-call(s32[16,20]{1,0:T(8,128)S(1)} %copy-done.10, s32[1]{0:T(128)} %bitcast.me_ref.refs_4_, bf16[16,20,128,128]{3,2,1,0:T(8,128)(2,1)} %tiles_ref.7, bf16[16,128,128]{2,1,0:T(8,128)(2,1)S(1)} %bitcast.93, bf16[16,128,128]{2,1,0:T(8,128)(2,1)} %collective-permute-done.9.rest_1_, ...), custom_call_target="tpu_custom_call" | custom-call | flops 1342177280 | bytes 30000000 | tf_op jit(solution)/shard_map/aggregate/pallas_call | solution.py:147
  94.2 5.5 %collective-permute-done.19.rest_1_ = bf16[8,128,128]{2,1,0:T(8,128)(2,1)} collective-permute-done((bf16[8,128,128]{2,1,0:T(8,128)(2,1)S(1)}, bf16[8,128,128]{2,1,0:T(8,128)(2,1)}, u32[]{:S(2)}, u32[]{:S(2)}) %collective-permute-start.19) | collective-permute-done | bytes 262176 | tf_op jit(solution)/shard_map/ppermute | solution.py:323
  99.7 0.8 pad_maximum_fusion.weight_ref
  100.5 2.3 %collective-permute-done.17.rest_3_ = bf16[8,128,128]{2,1,0:T(8,128)(2,1)S(1)} collective-permute-done((bf16[8,128,128]{2,1,0:T(8,128)(2,1)S(1)}, bf16[8,128,128]{2,1,0:T(8,128)(2,1)S(1)}, u32[]{:S(2)}, u32[]{:S(2)}) %collective-permute-start.17) | collective-permute-done | bytes 262176 | tf_op jit(solution)/shard_map/ppermute | solution.py:323
  102.8 4.0 %collective-permute-done.16.rest_1_ = bf16[8,128,128]{2,1,0:T(8,128)(2,1)S(1)} collective-permute-done((bf16[8,128,128]{2,1,0:T(8,128)(2,1)S(1)}, bf16[8,128,128]{2,1,0:T(8,128)(2,1)S(1)}, u32[]{:S(2)}, u32[]{:S(2)}) %collective-permute-start.16) | collective-permute-done | bytes 262176 | tf_op jit(solution)/shard_map/ppermute | solution.py:323
  106.8 0.6 collective-permute-start.18
  107.5 4.9 %collective-permute-done.21.rest_2_ = bf16[8,128,128]{2,1,0:T(8,128)(2,1)S(1)} collective-permute-done((bf16[8,128,128]{2,1,0:T(8,128)(2,1)}, bf16[8,128,128]{2,1,0:T(8,128)(2,1)S(1)}, u32[]{:S(2)}, u32[]{:S(2)}) %collective-permute-start.21) | collective-permute-done | bytes 262176 | tf_op jit(solution)/shard_map/ppermute | solution.py:323
  112.5 1.6 %dense.3 = (bf16[8,128,128]{2,1,0:T(8,128)(2,1)S(1)}, f32[4,128,128]{2,1,0:T(8,128)S(1)}) custom-call(s32[1]{0:T(128)} %bitcast.1.col_ref, bf16[128,512]{1,0:T(8,128)(2,1)S(1)} %pad_maximum_fusion.weight_ref, bf16[8,128,128]{2,1,0:T(8,128)(2,1)S(1)} %get-tuple-element.95.rest_0_, bf16[8,128,128]{2,1,0:T(8,128)(2,1)} %collective-permute-done.19.rest_1_, ...), custom_call_target="tpu_custom_call" | custom-call | tf_op jit(solution)/shard_map/dense/pallas_call | solution.py:221
  114.1 4.2 %spread.4 = (bf16[4,8,128,128]{3,2,1,0:T(8,128)(2,1)S(1)}, bf16[4,8,128,128]{3,2,1,0:T(8,128)(2,1)S(1)}, bf16[4,8,128,128]{3,2,1,0:T(8,128)(2,1)S(1)}, bf16[4,8,128,128]{3,2,1,0:T(8,128)(2,1)S(1)}) custom-call(s32[16,20]{1,0:T(8,128)S(1)} %copy-done.10, s32[1]{0:T(128)} %bitcast.me_ref.refs_4_, bf16[16,20,128,128]{3,2,1,0:T(8,128)(2,1)S(1)} %bitcast.84, ...), custom_call_target="tpu_custom_call" | custom-call | flops 1342177280 | bytes 30000000 | tf_op jit(solution)/shard_map/spread/pallas_call | solution.py:105
  118.3 0.6 dense.2
  118.9 5.0 %spread.5 = (bf16[4,8,128,128]{3,2,1,0:T(8,128)(2,1)S(1)}, bf16[4,8,128,128]{3,2,1,0:T(8,128)(2,1)S(1)}, bf16[4,8,128,128]{3,2,1,0:T(8,128)(2,1)S(1)}, bf16[4,8,128,128]{3,2,1,0:T(8,128)(2,1)S(1)}) custom-call(s32[16,20]{1,0:T(8,128)S(1)} %copy-done.10, s32[1]{0:T(128)} %bitcast.me_ref.refs_4_, bf16[16,20,128,128]{3,2,1,0:T(8,128)(2,1)S(1)} %bitcast.84, ...), custom_call_target="tpu_custom_call" | custom-call | flops 1342177280 | bytes 30000000 | tf_op jit(solution)/shard_map/spread/pallas_call | solution.py:105
  124.0 0.5 collective-permute-start.23
  124.5 0.2 weight_terms.1
  124.7 0.1 collective-permute-start.24
  124.8 1.8 %collective-permute-done.22 = bf16[4,8,128,128]{3,2,1,0:T(8,128)(2,1)S(1)} collective-permute-done((bf16[4,8,128,128]{3,2,1,0:T(8,128)(2,1)S(1)}, bf16[4,8,128,128]{3,2,1,0:T(8,128)(2,1)S(1)}, u32[]{:S(2)}, u32[]{:S(2)}) %collective-permute-start.22) | collective-permute-done | bytes 1048608 | tf_op jit(solution)/shard_map/ppermute | solution.py:323
  126.6 0.5 fusion.1
  127.1 1.6 %collective-permute-start.25 = (bf16[2,8,128,128]{3,2,1,0:T(8,128)(2,1)S(1)}, bf16[2,8,128,128]{3,2,1,0:T(8,128)(2,1)S(1)}, u32[]{:S(2)}, u32[]{:S(2)}) collective-permute-start(bf16[2,8,128,128]{3,2,1,0:T(8,128)(2,1)S(1)} %get-tuple-element.138), channel_id=1, source_target_pairs={{0,8},{4,12},{8,0},{12,4},{16,24},{20,28},{24,16},{28,20},{1,9},{5... | collective-permute-start | bytes 1572872 | tf_op jit(solution)/shard_map/ppermute | solution.py:323
  128.7 0.5 add_convert_fusion.2
  129.2 1.8 %collective-permute-start.26 = (bf16[2,8,128,128]{3,2,1,0:T(8,128)(2,1)S(1)}, bf16[2,8,128,128]{3,2,1,0:T(8,128)(2,1)S(1)}, u32[]{:S(2)}, u32[]{:S(2)}) collective-permute-start(bf16[2,8,128,128]{3,2,1,0:T(8,128)(2,1)S(1)} %get-tuple-element.136), channel_id=1, source_target_pairs={{0,16},{4,20},{8,24},{12,28},{16,0},{20,4},{24,8},{28,12},{1,17},{... | collective-permute-start | bytes 1572872 | tf_op jit(solution)/shard_map/ppermute | solution.py:323
  131.1 0.3 collective-permute-start.27
  131.4 14.4 %collective-permute-done.27 = bf16[128,512]{1,0:T(8,128)(2,1)S(1)} collective-permute-done((bf16[128,512]{1,0:T(8,128)(2,1)S(1)}, bf16[128,512]{1,0:T(8,128)(2,1)S(1)}, u32[]{:S(2)}, u32[]{:S(2)}) %collective-permute-start.27) | collective-permute-done | bytes 131104 | tf_op jit(solution)/shard_map/ppermute | solution.py:323
  145.8 0.1 fusion.9
  146.0 0.1 fusion.10
  146.1 1.3 collective-permute-start.30
  147.5 0.8 collective-permute-start.29
  148.2 1.7 %collective-permute-start.28 = (bf16[8,128,128]{2,1,0:T(8,128)(2,1)S(1)}, bf16[8,128,128]{2,1,0:T(8,128)(2,1)S(1)}, u32[]{:S(2)}, u32[]{:S(2)}) collective-permute-start(bf16[8,128,128]{2,1,0:T(8,128)(2,1)S(1)} %get-tuple-element.145), channel_id=1, source_target_pairs={{0,16},{4,20},{8,24},{12,28},{16,0},{20,4},{24,8},{28,12},{1,17},{... | collective-permute-start | bytes 786440 | tf_op jit(solution)/shard_map/ppermute | solution.py:323
  150.0 2.7 %collective-permute-done.30 = bf16[128,512]{1,0:T(8,128)(2,1)S(1)} collective-permute-done((bf16[128,512]{1,0:T(8,128)(2,1)S(1)}, bf16[128,512]{1,0:T(8,128)(2,1)S(1)}, u32[]{:S(2)}, u32[]{:S(2)}) %collective-permute-start.30) | collective-permute-done | bytes 131104 | tf_op jit(solution)/shard_map/ppermute | solution.py:323
  152.8 3.5 %collective-permute-done.29.refs_3_ = bf16[8,128,128]{2,1,0:T(8,128)(2,1)S(1)} collective-permute-done((bf16[8,128,128]{2,1,0:T(8,128)(2,1)S(1)}, bf16[8,128,128]{2,1,0:T(8,128)(2,1)S(1)}, u32[]{:S(2)}, u32[]{:S(2)}) %collective-permute-start.29) | collective-permute-done | bytes 262176 | tf_op jit(solution)/shard_map/ppermute | solution.py:323
  156.2 1.2 finish.3
  (69 shorter events, 1.1 us)
Async XLA Ops:
  0.6 1.0 copy-start.8
  1.7 0.7 copy-start.9
  2.4 38.7 %copy-start.1 = (bf16[2048,128]{1,0:T(8,128)(2,1)S(1)}, bf16[2048,128]{1,0:T(8,128)(2,1)}, u32[]{:S(2)}) copy-start(bf16[2048,128]{1,0:T(8,128)(2,1)} %param.8) | copy-start | bytes 1572868
  2.4 63.3 %copy-start.11 = (bf16[128,512]{1,0:T(8,128)(2,1)S(1)}, bf16[128,512]{1,0:T(8,128)(2,1)}, u32[]{:S(2)}) copy-start(bf16[128,512]{1,0:T(8,128)(2,1)} %param.14) | copy-start | bytes 393220
  2.4 63.4 %copy-start.12 = (bf16[128,512]{1,0:T(8,128)(2,1)S(1)}, bf16[128,512]{1,0:T(8,128)(2,1)}, u32[]{:S(2)}) copy-start(bf16[128,512]{1,0:T(8,128)(2,1)} %param.15) | copy-start | bytes 393220
  2.4 64.1 %copy-start = (bf16[2048,128]{1,0:T(8,128)(2,1)S(1)}, bf16[2048,128]{1,0:T(8,128)(2,1)}, u32[]{:S(2)}) copy-start(bf16[2048,128]{1,0:T(8,128)(2,1)} %param.9) | copy-start | bytes 1572868
  9.4 31.7 %copy-start.6 = (bf16[16,128,128]{2,1,0:T(8,128)(2,1)}, bf16[16,128,128]{2,1,0:T(8,128)(2,1)S(1)}, u32[]{:S(2)}) copy-start(bf16[16,128,128]{2,1,0:T(8,128)(2,1)S(1)} %get-tuple-element.82.mask_ref) | copy-start | bytes 1572868
  9.5 76.6 %copy-start.10 = (s32[16,20]{1,0:T(8,128)S(1)}, s32[16,20]{1,0:T(8,128)}, u32[]{:S(2)}) copy-start(s32[16,20]{1,0:T(8,128)} %cols_ref.7) | copy-start | bytes 3844
  9.5 2.8 %collective-permute-start = (bf16[4,8,128,128]{3,2,1,0:T(8,128)(2,1)S(1)}, bf16[4,8,128,128]{3,2,1,0:T(8,128)(2,1)S(1)}, u32[]{:S(2)}, u32[]{:S(2)}) collective-permute-start(bf16[4,8,128,128]{3,2,1,0:T(8,128)(2,1)S(1)} %get-tuple-element.70), channel_id=1, source_target_pairs={{0,4},{4,0},{8,12},{12,8},{16,20},{20,16},{24,28},{28,24},{1,5},{5... | collective-permute-start | bytes 3145736 | tf_op jit(solution)/shard_map/ppermute | solution.py:323
  10.0 5.7 %collective-permute-start.3 = (bf16[4,8,128,128]{3,2,1,0:T(8,128)(2,1)S(1)}, bf16[4,8,128,128]{3,2,1,0:T(8,128)(2,1)S(1)}, u32[]{:S(2)}, u32[]{:S(2)}) collective-permute-start(bf16[4,8,128,128]{3,2,1,0:T(8,128)(2,1)S(1)} %get-tuple-element.72), channel_id=1, source_target_pairs={{0,4},{4,0},{8,12},{12,8},{16,20},{20,16},{24,28},{28,24},{1,5},{5... | collective-permute-start | bytes 3145736 | tf_op jit(solution)/shard_map/ppermute | solution.py:323
  12.7 15.2 %collective-permute-start.1 = (bf16[2,8,128,128]{3,2,1,0:T(8,128)(2,1)S(1)}, bf16[2,8,128,128]{3,2,1,0:T(8,128)(2,1)S(1)}, u32[]{:S(2)}, u32[]{:S(2)}) collective-permute-start(bf16[2,8,128,128]{3,2,1,0:T(8,128)(2,1)S(1)} %get-tuple-element.142), channel_id=1, source_target_pairs={{0,8},{4,12},{8,0},{12,4},{16,24},{20,28},{24,16},{28,20},{1,9},{5... | collective-permute-start | bytes 1572872 | tf_op jit(solution)/shard_map/ppermute | solution.py:323
  16.1 13.8 %collective-permute-start.4 = (bf16[2,8,128,128]{3,2,1,0:T(8,128)(2,1)S(1)}, bf16[2,8,128,128]{3,2,1,0:T(8,128)(2,1)S(1)}, u32[]{:S(2)}, u32[]{:S(2)}) collective-permute-start(bf16[2,8,128,128]{3,2,1,0:T(8,128)(2,1)S(1)} %get-tuple-element.140), channel_id=1, source_target_pairs={{0,16},{4,20},{8,24},{12,28},{16,0},{20,4},{24,8},{28,12},{1,17},{... | collective-permute-start | bytes 1572872 | tf_op jit(solution)/shard_map/ppermute | solution.py:323
  28.0 7.9 %collective-permute-start.2 = (bf16[8,128,128]{2,1,0:T(8,128)(2,1)S(1)}, bf16[8,128,128]{2,1,0:T(8,128)(2,1)S(1)}, u32[]{:S(2)}, u32[]{:S(2)}) collective-permute-start(bf16[8,128,128]{2,1,0:T(8,128)(2,1)S(1)} %get-tuple-element.149), channel_id=1, source_target_pairs={{0,16},{4,20},{8,24},{12,28},{16,0},{20,4},{24,8},{28,12},{1,17},{... | collective-permute-start | bytes 786440 | tf_op jit(solution)/shard_map/ppermute | solution.py:323
  30.0 7.3 %collective-permute-start.5 = (bf16[8,128,128]{2,1,0:T(8,128)(2,1)S(1)}, bf16[8,128,128]{2,1,0:T(8,128)(2,1)S(1)}, u32[]{:S(2)}, u32[]{:S(2)}) collective-permute-start(bf16[8,128,128]{2,1,0:T(8,128)(2,1)S(1)} %get-tuple-element.147), channel_id=1, source_target_pairs={{0,8},{4,12},{8,0},{12,4},{16,24},{20,28},{24,16},{28,20},{1,9},{5... | collective-permute-start | bytes 786440 | tf_op jit(solution)/shard_map/ppermute | solution.py:323
  37.4 16.9 %collective-permute-start.7 = (bf16[16,128,128]{2,1,0:T(8,128)(2,1)S(1)}, bf16[16,128,128]{2,1,0:T(8,128)(2,1)}, u32[]{:S(2)}, u32[]{:S(2)}) collective-permute-start(bf16[16,128,128]{2,1,0:T(8,128)(2,1)S(1)} %finish.2.rest_0_), channel_id=1, source_target_pairs={{0,3},{1,2},{2,1},{3,0},{4,7},{5,6},{6,5},{7,4},{8,11},{9,10},{10,... | collective-permute-start | bytes 1572872 | tf_op jit(solution)/shard_map/ppermute | solution.py:323
  41.1 21.5 %collective-permute-start.6 = (bf16[16,128,128]{2,1,0:T(8,128)(2,1)S(1)}, bf16[16,128,128]{2,1,0:T(8,128)(2,1)S(1)}, u32[]{:S(2)}, u32[]{:S(2)}) collective-permute-start(bf16[16,128,128]{2,1,0:T(8,128)(2,1)S(1)} %finish.2.rest_0_), channel_id=1, source_target_pairs={{0,1},{1,0},{2,3},{3,2},{4,5},{5,4},{6,7},{7,6},{8,9},{9,8},{10,11... | collective-permute-start | bytes 1572872 | tf_op jit(solution)/shard_map/ppermute | solution.py:323
  41.1 24.0 %collective-permute-start.14 = (bf16[16,128,128]{2,1,0:T(8,128)(2,1)S(1)}, bf16[16,128,128]{2,1,0:T(8,128)(2,1)S(1)}, u32[]{:S(2)}, u32[]{:S(2)}) collective-permute-start(bf16[16,128,128]{2,1,0:T(8,128)(2,1)S(1)} %bitcast.89), channel_id=1, source_target_pairs={{0,24},{4,28},{8,16},{12,20},{16,8},{20,12},{24,0},{28,4},{1,25},{... | collective-permute-start | bytes 1572872 | tf_op jit(solution)/shard_map/ppermute | solution.py:323
  43.7 21.4 %collective-permute-start.12 = (bf16[16,128,128]{2,1,0:T(8,128)(2,1)S(1)}, bf16[16,128,128]{2,1,0:T(8,128)(2,1)S(1)}, u32[]{:S(2)}, u32[]{:S(2)}) collective-permute-start(bf16[16,128,128]{2,1,0:T(8,128)(2,1)S(1)} %bitcast.90), channel_id=1, source_target_pairs={{0,16},{4,20},{8,24},{12,28},{16,0},{20,4},{24,8},{28,12},{1,17},{... | collective-permute-start | bytes 1572872 | tf_op jit(solution)/shard_map/ppermute | solution.py:323
  44.2 21.5 %collective-permute-start.10 = (bf16[16,128,128]{2,1,0:T(8,128)(2,1)S(1)}, bf16[16,128,128]{2,1,0:T(8,128)(2,1)}, u32[]{:S(2)}, u32[]{:S(2)}) collective-permute-start(bf16[16,128,128]{2,1,0:T(8,128)(2,1)S(1)} %bitcast.91), channel_id=1, source_target_pairs={{0,8},{4,12},{8,0},{12,4},{16,24},{20,28},{24,16},{28,20},{1,9},{5... | collective-permute-start | bytes 1572872 | tf_op jit(solution)/shard_map/ppermute | solution.py:323
  54.3 15.1 %collective-permute-start.9 = (bf16[16,128,128]{2,1,0:T(8,128)(2,1)S(1)}, bf16[16,128,128]{2,1,0:T(8,128)(2,1)}, u32[]{:S(2)}, u32[]{:S(2)}) collective-permute-start(bf16[16,128,128]{2,1,0:T(8,128)(2,1)S(1)} %bitcast.92), channel_id=1, source_target_pairs={{0,4},{4,0},{8,12},{12,8},{16,20},{20,16},{24,28},{28,24},{1,5},{5... | collective-permute-start | bytes 1572872 | tf_op jit(solution)/shard_map/ppermute | solution.py:323
  62.6 0.8 copy-start.4
  63.4 14.3 %collective-permute-start.8 = (bf16[16,128,128]{2,1,0:T(8,128)(2,1)}, bf16[16,128,128]{2,1,0:T(8,128)(2,1)}, u32[]{:S(2)}, u32[]{:S(2)}) collective-permute-start(bf16[16,128,128]{2,1,0:T(8,128)(2,1)} %collective-permute-done.7.rest_2_), channel_id=1, source_target_pairs={{0,1},{1,0},{2,3},{3,2},{4,5},{5,4},{6,7},{7,6},{8,9},{9,8},{10,11... | collective-permute-start | bytes 1572872 | tf_op jit(solution)/shard_map/ppermute | solution.py:323
  65.1 12.6 %collective-permute-start.15 = (bf16[16,128,128]{2,1,0:T(8,128)(2,1)S(1)}, bf16[16,128,128]{2,1,0:T(8,128)(2,1)}, u32[]{:S(2)}, u32[]{:S(2)}) collective-permute-start(bf16[16,128,128]{2,1,0:T(8,128)(2,1)S(1)} %collective-permute-done.14.rest_6_), channel_id=1, source_target_pairs={{0,4},{4,0},{8,12},{12,8},{16,20},{20,16},{24,28},{28,24},{1,5},{5... | collective-permute-start | bytes 1572872 | tf_op jit(solution)/shard_map/ppermute | solution.py:323
  65.1 20.3 %copy-start.2 = (bf16[16,128,128]{2,1,0:T(8,128)(2,1)}, bf16[16,128,128]{2,1,0:T(8,128)(2,1)S(1)}, u32[]{:S(2)}) copy-start(bf16[16,128,128]{2,1,0:T(8,128)(2,1)S(1)} %collective-permute-done.12.rest_4_) | copy-start | bytes 1572868
  65.1 12.6 %collective-permute-start.13 = (bf16[16,128,128]{2,1,0:T(8,128)(2,1)S(1)}, bf16[16,128,128]{2,1,0:T(8,128)(2,1)}, u32[]{:S(2)}, u32[]{:S(2)}) collective-permute-start(bf16[16,128,128]{2,1,0:T(8,128)(2,1)S(1)} %collective-permute-done.12.rest_4_), channel_id=1, source_target_pairs={{0,4},{4,0},{8,12},{12,8},{16,20},{20,16},{24,28},{28,24},{1,5},{5... | collective-permute-start | bytes 1572872 | tf_op jit(solution)/shard_map/ppermute | solution.py:323
  65.6 12.1 %collective-permute-start.11 = (bf16[16,128,128]{2,1,0:T(8,128)(2,1)}, bf16[16,128,128]{2,1,0:T(8,128)(2,1)}, u32[]{:S(2)}, u32[]{:S(2)}) collective-permute-start(bf16[16,128,128]{2,1,0:T(8,128)(2,1)} %collective-permute-done.10.rest_2_), channel_id=1, source_target_pairs={{0,4},{4,0},{8,12},{12,8},{16,20},{20,16},{24,28},{28,24},{1,5},{5... | collective-permute-start | bytes 1572872 | tf_op jit(solution)/shard_map/ppermute | solution.py:323
  66.5 1.0 copy-start.5
  77.7 1.0 copy-start.7
  78.8 35.3 %slice-start = ((s8[10485760]{0:T(1024)(128)(4,1)}), s8[4194304]{0:T(1024)(128)(4,1)S(1)}, s32[]{:S(2)}) async-start(s8[10485760]{0:T(1024)(128)(4,1)} %bitcast.83), calls=%async_computation | async-start | bytes 8388608
  80.4 13.8 %collective-permute-start.20 = (bf16[8,128,128]{2,1,0:T(8,128)(2,1)S(1)}, bf16[8,128,128]{2,1,0:T(8,128)(2,1)}, u32[]{:S(2)}, u32[]{:S(2)}) collective-permute-start(bf16[8,128,128]{2,1,0:T(8,128)(2,1)S(1)} %get-tuple-element.95.rest_0_), channel_id=1, source_target_pairs={{0,3},{1,2},{2,1},{3,0},{4,7},{5,6},{6,5},{7,4},{8,11},{9,10},{10,... | collective-permute-start | bytes 786440 | tf_op jit(solution)/shard_map/ppermute | solution.py:323
  81.3 18.4 %collective-permute-start.19 = (bf16[8,128,128]{2,1,0:T(8,128)(2,1)S(1)}, bf16[8,128,128]{2,1,0:T(8,128)(2,1)}, u32[]{:S(2)}, u32[]{:S(2)}) collective-permute-start(bf16[8,128,128]{2,1,0:T(8,128)(2,1)S(1)} %get-tuple-element.95.rest_0_), channel_id=1, source_target_pairs={{0,1},{1,0},{2,3},{3,2},{4,5},{5,4},{6,7},{7,6},{8,9},{9,8},{10,11... | collective-permute-start | bytes 786440 | tf_op jit(solution)/shard_map/ppermute | solution.py:323
  82.2 20.6 %collective-permute-start.17 = (bf16[8,128,128]{2,1,0:T(8,128)(2,1)S(1)}, bf16[8,128,128]{2,1,0:T(8,128)(2,1)S(1)}, u32[]{:S(2)}, u32[]{:S(2)}) collective-permute-start(bf16[8,128,128]{2,1,0:T(8,128)(2,1)S(1)} %get-tuple-element.83.rest_0_), channel_id=1, source_target_pairs={{0,3},{1,2},{2,1},{3,0},{4,7},{5,6},{6,5},{7,4},{8,11},{9,10},{10,... | collective-permute-start | bytes 786440 | tf_op jit(solution)/shard_map/ppermute | solution.py:323
  84.3 22.5 %collective-permute-start.16 = (bf16[8,128,128]{2,1,0:T(8,128)(2,1)S(1)}, bf16[8,128,128]{2,1,0:T(8,128)(2,1)S(1)}, u32[]{:S(2)}, u32[]{:S(2)}) collective-permute-start(bf16[8,128,128]{2,1,0:T(8,128)(2,1)S(1)} %get-tuple-element.83.rest_0_), channel_id=1, source_target_pairs={{0,1},{1,0},{2,3},{3,2},{4,5},{5,4},{6,7},{7,6},{8,9},{9,8},{10,11... | collective-permute-start | bytes 786440 | tf_op jit(solution)/shard_map/ppermute | solution.py:323
  86.1 1.0 copy-start.3
  87.1 27.0 %slice-start.1 = ((s8[10485760]{0:T(1024)(128)(4,1)}), s8[4194304]{0:T(1024)(128)(4,1)S(1)}, s32[]{:S(2)}) async-start(s8[10485760]{0:T(1024)(128)(4,1)} %bitcast.83), calls=%async_computation.1 | async-start | bytes 8388608
  87.1 27.0 %slice-start.2 = ((s8[10485760]{0:T(1024)(128)(4,1)}), s8[2097152]{0:T(1024)(128)(4,1)S(1)}, s32[]{:S(2)}) async-start(s8[10485760]{0:T(1024)(128)(4,1)} %bitcast.83), calls=%async_computation.2 | async-start | bytes 4194304
  99.7 12.7 %collective-permute-start.21 = (bf16[8,128,128]{2,1,0:T(8,128)(2,1)}, bf16[8,128,128]{2,1,0:T(8,128)(2,1)S(1)}, u32[]{:S(2)}, u32[]{:S(2)}) collective-permute-start(bf16[8,128,128]{2,1,0:T(8,128)(2,1)} %collective-permute-done.20.rest_3_), channel_id=1, source_target_pairs={{0,1},{1,0},{2,3},{3,2},{4,5},{5,4},{6,7},{7,6},{8,9},{9,8},{10,11... | collective-permute-start | bytes 786440 | tf_op jit(solution)/shard_map/ppermute | solution.py:323
  106.8 11.4 %collective-permute-start.18 = (bf16[8,128,128]{2,1,0:T(8,128)(2,1)S(1)}, bf16[8,128,128]{2,1,0:T(8,128)(2,1)S(1)}, u32[]{:S(2)}, u32[]{:S(2)}) collective-permute-start(bf16[8,128,128]{2,1,0:T(8,128)(2,1)S(1)} %collective-permute-done.17.rest_3_), channel_id=1, source_target_pairs={{0,1},{1,0},{2,3},{3,2},{4,5},{5,4},{6,7},{7,6},{8,9},{9,8},{10,11... | collective-permute-start | bytes 786440 | tf_op jit(solution)/shard_map/ppermute | solution.py:323
  123.9 2.7 %collective-permute-start.22 = (bf16[4,8,128,128]{3,2,1,0:T(8,128)(2,1)S(1)}, bf16[4,8,128,128]{3,2,1,0:T(8,128)(2,1)S(1)}, u32[]{:S(2)}, u32[]{:S(2)}) collective-permute-start(bf16[4,8,128,128]{3,2,1,0:T(8,128)(2,1)S(1)} %get-tuple-element.114), channel_id=1, source_target_pairs={{0,4},{4,0},{8,12},{12,8},{16,20},{20,16},{24,28},{28,24},{1,5},{5... | collective-permute-start | bytes 3145736 | tf_op jit(solution)/shard_map/ppermute | solution.py:323
  124.0 4.8 %collective-permute-start.23 = (bf16[4,8,128,128]{3,2,1,0:T(8,128)(2,1)S(1)}, bf16[4,8,128,128]{3,2,1,0:T(8,128)(2,1)S(1)}, u32[]{:S(2)}, u32[]{:S(2)}) collective-permute-start(bf16[4,8,128,128]{3,2,1,0:T(8,128)(2,1)S(1)} %get-tuple-element.116), channel_id=1, source_target_pairs={{0,4},{4,0},{8,12},{12,8},{16,20},{20,16},{24,28},{28,24},{1,5},{5... | collective-permute-start | bytes 3145736 | tf_op jit(solution)/shard_map/ppermute | solution.py:323
  124.7 6.4 %collective-permute-start.24 = (bf16[128,512]{1,0:T(8,128)(2,1)S(1)}, bf16[128,512]{1,0:T(8,128)(2,1)S(1)}, u32[]{:S(2)}, u32[]{:S(2)}) collective-permute-start(bf16[128,512]{1,0:T(8,128)(2,1)S(1)} %get-tuple-element.122), channel_id=1, source_target_pairs={{0,4},{4,0},{8,12},{12,8},{16,20},{20,16},{24,28},{28,24},{1,5},{5... | collective-permute-start | bytes 393224 | tf_op jit(solution)/shard_map/ppermute | solution.py:323
  127.1 18.7 %collective-permute-start.25 = (bf16[2,8,128,128]{3,2,1,0:T(8,128)(2,1)S(1)}, bf16[2,8,128,128]{3,2,1,0:T(8,128)(2,1)S(1)}, u32[]{:S(2)}, u32[]{:S(2)}) collective-permute-start(bf16[2,8,128,128]{3,2,1,0:T(8,128)(2,1)S(1)} %get-tuple-element.138), channel_id=1, source_target_pairs={{0,8},{4,12},{8,0},{12,4},{16,24},{20,28},{24,16},{28,20},{1,9},{5... | collective-permute-start | bytes 1572872 | tf_op jit(solution)/shard_map/ppermute | solution.py:323
  129.2 16.6 %collective-permute-start.26 = (bf16[2,8,128,128]{3,2,1,0:T(8,128)(2,1)S(1)}, bf16[2,8,128,128]{3,2,1,0:T(8,128)(2,1)S(1)}, u32[]{:S(2)}, u32[]{:S(2)}) collective-permute-start(bf16[2,8,128,128]{3,2,1,0:T(8,128)(2,1)S(1)} %get-tuple-element.136), channel_id=1, source_target_pairs={{0,16},{4,20},{8,24},{12,28},{16,0},{20,4},{24,8},{28,12},{1,17},{... | collective-permute-start | bytes 1572872 | tf_op jit(solution)/shard_map/ppermute | solution.py:323
  131.1 14.7 %collective-permute-start.27 = (bf16[128,512]{1,0:T(8,128)(2,1)S(1)}, bf16[128,512]{1,0:T(8,128)(2,1)S(1)}, u32[]{:S(2)}, u32[]{:S(2)}) collective-permute-start(bf16[128,512]{1,0:T(8,128)(2,1)S(1)} %convert_add_fusion.4), channel_id=1, source_target_pairs={{0,16},{4,20},{8,24},{12,28},{16,0},{20,4},{24,8},{28,12},{1,17},{... | collective-permute-start | bytes 393224 | tf_op jit(solution)/shard_map/ppermute | solution.py:323
  146.1 6.5 %collective-permute-start.30 = (bf16[128,512]{1,0:T(8,128)(2,1)S(1)}, bf16[128,512]{1,0:T(8,128)(2,1)S(1)}, u32[]{:S(2)}, u32[]{:S(2)}) collective-permute-start(bf16[128,512]{1,0:T(8,128)(2,1)S(1)} %convert_add_fusion.3), channel_id=1, source_target_pairs={{0,8},{4,12},{8,0},{12,4},{16,24},{20,28},{24,16},{28,20},{1,9},{5... | collective-permute-start | bytes 393224 | tf_op jit(solution)/shard_map/ppermute | solution.py:323
  147.5 8.8 %collective-permute-start.29 = (bf16[8,128,128]{2,1,0:T(8,128)(2,1)S(1)}, bf16[8,128,128]{2,1,0:T(8,128)(2,1)S(1)}, u32[]{:S(2)}, u32[]{:S(2)}) collective-permute-start(bf16[8,128,128]{2,1,0:T(8,128)(2,1)S(1)} %get-tuple-element.143), channel_id=1, source_target_pairs={{0,8},{4,12},{8,0},{12,4},{16,24},{20,28},{24,16},{28,20},{1,9},{5... | collective-permute-start | bytes 786440 | tf_op jit(solution)/shard_map/ppermute | solution.py:323
  148.2 8.0 %collective-permute-start.28 = (bf16[8,128,128]{2,1,0:T(8,128)(2,1)S(1)}, bf16[8,128,128]{2,1,0:T(8,128)(2,1)S(1)}, u32[]{:S(2)}, u32[]{:S(2)}) collective-permute-start(bf16[8,128,128]{2,1,0:T(8,128)(2,1)S(1)} %get-tuple-element.145), channel_id=1, source_target_pairs={{0,16},{4,20},{8,24},{12,28},{16,0},{20,4},{24,8},{28,12},{1,17},{... | collective-permute-start | bytes 786440 | tf_op jit(solution)/shard_map/ppermute | solution.py:323
  152.7 3.6 %collective-permute-start.31 = (f32[128,512]{1,0:T(8,128)S(1)}, f32[128,512]{1,0:T(8,128)S(1)}, u32[]{:S(2)}, u32[]{:S(2)}) collective-permute-start(f32[128,512]{1,0:T(8,128)S(1)} %convert_add_fusion.2.refs_5_), channel_id=1, source_target_pairs={{0,4},{4,0},{8,12},{12,8},{16,20},{20,16},{24,28},{28,24},{1,5},{5... | collective-permute-start | bytes 786440 | tf_op jit(solution)/shard_map/ppermute | solution.py:323

commit v13 on v12

--- a/solution.py
+++ b/solution.py
@@ -37,19 +37,18 @@
     lax.fori_loop(0, COPIES, piece, 0)
 
 
-def spread_kernel(first, start, earlier, cols_ref, me_ref, tiles_ref, vals_ref, *rest):
-    tiles_ref = tiles_ref.at[pl.ds(start, vals_ref.shape[0])]
-    sums, rest = rest[:earlier], rest[earlier:]
+def spread_kernel(first, pieces, cols_ref, me_ref, tiles_ref, *rest):
+    vals, rest = rest[:pieces], rest[pieces:]
     if first:
         mask_ref, *rest = rest
         outs, (mask_out, acc, held, sems, left_ref, mask_held) = rest[: 2 * GROUPS], rest[2 * GROUPS :]
         loads = [
-            pltpu.make_async_copy(vals_ref, left_ref, sems.at[COPIES]),
+            pltpu.make_async_copy(vals[0], left_ref, sems.at[COPIES]),
             pltpu.make_async_copy(mask_ref, mask_held, sems.at[COPIES + 1]),
         ]
         loads[0].start()
     else:
-        outs, (acc, held, sems) = rest[: 2 * GROUPS], rest[2 * GROUPS :]
+        outs, (acc, held, sems, left_ref) = rest[: 2 * GROUPS], rest[2 * GROUPS :]
     for i in range(COPIES):
         tile_copy(tiles_ref, held, sems, i).start()
     if first:
@@ -59,14 +58,18 @@
     me = me_ref[0]
     if first:
         loads[0].wait()
+    else:
+        for g in range(pieces):
+            count = vals[g].shape[0]
+            left_ref[g * count : (g + 1) * count] = vals[g][...]
 
     def one_row(r):
-        left = left_ref[r].astype(F32).T.astype(BF16) if first else vals_ref[r]
+        left = left_ref[r].astype(F32).T.astype(BF16) if first else left_ref[r]
         for k in range(0, per_row, 2):
             pair = jnp.concatenate([held[r, k], held[r, k + 1]], axis=1)
             both = jnp.dot(left, pair, preferred_element_type=F32)
             for side in range(2):
-                acc[cols_ref[start + r, k + side]] += both[:, side * size : (side + 1) * size]
+                acc[cols_ref[r, k + side]] += both[:, side * size : (side + 1) * size]
 
     over_rows(tiles_ref, held, sems, one_row)
     halves, count = outs[0].shape[:2]
@@ -74,41 +77,40 @@
         for side in range(2):
             for rel in range(halves):
                 owner = jnp.bitwise_xor(me, 2 * rel + side)
-                total = acc[pl.ds((owner * GROUPS + g) * count, count)]
-                if earlier:
-                    total = total + sums[2 * g + side][rel].astype(F32)
-                outs[2 * g + side][rel] = total.astype(BF16)
+                start = (owner * GROUPS + g) * count
+                outs[2 * g + side][rel] = acc[pl.ds(start, count)].astype(BF16)
     if first:
         loads[1].wait()
         for b in range(mask_held.shape[0]):
             mask_out[b] = mask_held[b].astype(F32).T.astype(BF16)
 
 
-def spread(edge_tiles, block_cols, vals, me, rows, mask=None, start=0, earlier=()):
+def spread(edge_tiles, block_cols, vals, me, rows, mask=None):
     blocks, _, size, _ = edge_tiles.shape
     first = mask is not None
-    feat = vals.shape[2] if first else vals.shape[1]
+    feat = vals[0].shape[2] if first else vals[0].shape[1]
     out = jax.ShapeDtypeStruct((rows // 2, blocks // GROUPS, feat, size), BF16)
     outs = [out] * (2 * GROUPS)
     scratch = [
         pltpu.VMEM((rows * blocks, feat, size), F32),
-        pltpu.VMEM((vals.shape[0],) + edge_tiles.shape[1:], BF16),
+        pltpu.VMEM(edge_tiles.shape, BF16),
         pltpu.SemaphoreType.DMA((COPIES + 2,)),
     ]
     anywhere = pl.BlockSpec(memory_space=pl.ANY)
     if first:
         outs.append(jax.ShapeDtypeStruct((blocks, feat, size), BF16))
-        scratch += [pltpu.VMEM(v.shape, v.dtype) for v in (vals, mask)]
-        args, place = [vals, mask], anywhere
+        scratch += [pltpu.VMEM(v.shape, v.dtype) for v in (vals[0], mask)]
+        args, place = [vals[0], mask], anywhere
     else:
-        args, place = [vals, *earlier], VMEM
-    return pl.pallas_call(
-        functools.partial(spread_kernel, first, start, len(earlier)),
+        scratch.append(pltpu.VMEM((blocks, feat, size), BF16))
+        args, place = vals, VMEM
+    return pl.pallas_call(
+        functools.partial(spread_kernel, first, len(vals)),
         out_shape=outs,
         in_specs=[SMEM, SMEM, anywhere] + [place] * len(args),
         out_specs=[VMEM] * len(outs),
         scratch_shapes=scratch,
-        compiler_params=params(48 if first else 28),
+        compiler_params=params(48),
         cost_estimate=pl.CostEstimate(flops=2 * edge_tiles.size * feat, bytes_accessed=30_000_000, transcendentals=0),
         name="spread",
     )(block_cols, me, edge_tiles, *args)
@@ -354,9 +356,13 @@
     return [t for pair in zip(keeps, gots) for t in pair], value
 
 
-def gather_columns(own, cols, beside=()):
+def gather_columns(own, cols, beside=(), tied=True):
     if cols == 4:
-        near, far, beside = lax.optimization_barrier((swap(own, 1, "col"), swap(own, 3, "col"), beside))
+        near, far = swap(own, 1, "col"), swap(own, 3, "col")
+        if tied:
+            near, far, beside = lax.optimization_barrier((near, far, beside))
+        else:
+            near, beside = lax.optimization_barrier((near, beside))
         return [own, near, swap(far, 1, "col"), far], beside
     return [own] + [swap(own, m, "col") for m in range(1, cols)], beside
 
@@ -378,13 +384,13 @@
         order = [lax.dynamic_index_in_dim(split, col ^ m, 1, keepdims=False) for m in range(cols)]
         return jnp.concatenate(order, axis=1)
 
-    *pieces, mask = spread(edge_tiles, block_cols, blocked(grad_out), me_at, rows, blocked(relu_mask))
+    *pieces, mask = spread(edge_tiles, block_cols, [blocked(grad_out)], me_at, rows, blocked(relu_mask))
     terms, _ = scatter(pieces, rows)
     own, node_feats = after((finish(terms)[0], blocked(node_feats)))
     own, weight_one, weight_two = after((own, weight_one, weight_two))
     weight_one, weight_two = by_distance(weight_one), by_distance(weight_two)
-    shards, _ = gather_columns(own, cols)
     parts = [node_feats] + [swap(node_feats, rel, "row") for rel in range(2, rows, 2)]
+    shards, parts[0] = gather_columns(own, cols, node_feats, False)
     parts = [v for part in parts for v in (part, swap(part, 1, "row"))]
     late = 2
     hidden = blocked(hidden_act)
@@ -393,13 +399,14 @@
     *deltas, last = dense_late(weight_two, arrived, part, hidden, mask, late)
     deltas[0], parts = after((deltas[0], parts))
     agg_feats = aggregate(edge_tiles, block_cols, parts, me_at)
-    pieces, firsts = (), []
+    inputs, firsts = [], []
     for g in range(GROUPS):
         shards, beside = gather_columns(deltas[g], cols, agg_feats if g == 0 else ())
         agg_feats = beside if g == 0 else agg_feats
         out, grad = dense(weight_one, shards, cut(agg_feats, g), None, col_at, 1)
-        pieces = spread(edge_tiles, block_cols, out, me_at, rows, None, g * per, pieces)
+        inputs.append(out)
         firsts.append(grad)
+    pieces = spread(edge_tiles, block_cols, inputs, me_at, rows)
     keep, send = weight_terms(firsts, second, last, me_at, col_at, late)
     terms, value = scatter(pieces, rows, keep + swap(send, 1, "row").astype(F32))
     grads = [me_at, value, swap(value, 1, "row")]

time: 158 us -> 158 us (level)
  starting transfers between devices: 32 us -> 37.4 us
  Pallas kernels: 30.5 us -> 26.4 us
  local copies, waits for them, and re-layouts: 7.01 us -> 5.34 us
    ppermute x32, starting transfers between devices: 32 us -> 37.4 us  [swap(): lax.ppermute(value, axis, [(i, i ^ mask) for i in range(lax.axis_size(axi...]
    pallas_call x3 -> x2, Pallas kernels: 16.2 us -> 13.7 us  [spread(): pl.pallas_call(functools.partial(spread_kernel, first, len(vals)), out_sh...]
    unnamed x40 -> x30, local copies, waits for them, and re-layouts: 6.35 us -> 4.68 us
  transfers between devices with their start and end apart: 32 -> 32, of which waited for: 15 -> 17; matrix products, arithmetic and copies ran while one was open for 3% -> 2% of each run, Pallas kernels for 9% -> 6%
where the time goes in v13:
time: 158 us; the launch traced here: 157 us
  waiting for transfers between devices  84.9 us (54%)
  starting transfers between devices  37.4 us (24%)
  Pallas kernels  26.4 us (17%)
  local copies, waits for them, and re-layouts  5.34 us (3%)
  other arithmetic  2.21 us (1%)
    ppermute x32, waiting for transfers between devices, swap(): lax.ppermute(value, axis, [(i, i ^ mask) for i in range(lax.axis_size(axi...  84.9 us
    ppermute x32, starting transfers between devices, swap(): lax.ppermute(value, axis, [(i, i ^ mask) for i in range(lax.axis_size(axi...  37.4 us
    pallas_call x2, Pallas kernels, spread(): pl.pallas_call(functools.partial(spread_kernel, first, len(vals)), out_sh...  13.7 us
    pallas_call x1, Pallas kernels, aggregate(): pl.pallas_call(aggregate_kernel, out_shape=jax.ShapeDtypeStruct((blocks,...  6.59 us
    unnamed x30, local copies, waits for them, and re-layouts  4.68 us
  transfers between devices with their start and end apart: 32, of which 17 were waited for; matrix products, arithmetic and copies ran while one was open for 2% of the time, Pallas kernels for 6%

profile of v13, /device:TPU:0, one launch (start us, length us, event | category | flops | bytes accessed | tf_op | source)
XLA Modules:
  0.0 157.3 jit_solution(5526067001021781974)
XLA Ops:
  0.6 1.0 copy-done.6
  1.7 0.7 copy-done.7
  2.4 7.0 %spread.2 = (bf16[4,8,128,128]{3,2,1,0:T(8,128)(2,1)S(1)}, bf16[4,8,128,128]{3,2,1,0:T(8,128)(2,1)S(1)}, bf16[4,8,128,128]{3,2,1,0:T(8,128)(2,1)S(1)}, bf16[4,8,...) custom-call(s32[16,20]{1,0:T(8,128)S(1)} %copy-done.7, s32[1]{0:T(128)} %bitcast.me_ref.refs_4_, ...), custom_call_target="tpu_custom_call" | custom-call | flops 1342177280 | bytes 30000000 | tf_op jit(solution)/shard_map/spread/pallas_call | solution.py:107
  9.5 0.5 collective-permute-start
  10.1 2.2 %collective-permute-done = bf16[4,8,128,128]{3,2,1,0:T(8,128)(2,1)S(1)} collective-permute-done((bf16[4,8,128,128]{3,2,1,0:T(8,128)(2,1)S(1)}, bf16[4,8,128,128]{3,2,1,0:T(8,128)(2,1)S(1)}, u32[]{:S(2)}, u32[]{:S(2)}) %collective-permute-start) | collective-permute-done | bytes 1048608 | tf_op jit(solution)/shard_map/ppermute | solution.py:325
  12.3 0.5 add_convert_fusion.7
  12.7 2.9 %collective-permute-start.1 = (bf16[2,8,128,128]{3,2,1,0:T(8,128)(2,1)S(1)}, bf16[2,8,128,128]{3,2,1,0:T(8,128)(2,1)S(1)}, u32[]{:S(2)}, u32[]{:S(2)}) collective-permute-start(bf16[2,8,128,128]{3,2,1,0:T(8,128)(2,1)S(1)} %get-tuple-element.134), channel_id=1, source_target_pairs={{0,8},{4,12},{8,0},{12,4},{16,24},{20,28},{24,16},{28,20},{1,9},{5... | collective-permute-start | bytes 1572872 | tf_op jit(solution)/shard_map/ppermute | solution.py:325
  15.7 0.3 add_convert_fusion.5
  16.0 1.6 %collective-permute-start.4 = (bf16[2,8,128,128]{3,2,1,0:T(8,128)(2,1)S(1)}, bf16[2,8,128,128]{3,2,1,0:T(8,128)(2,1)S(1)}, u32[]{:S(2)}, u32[]{:S(2)}) collective-permute-start(bf16[2,8,128,128]{3,2,1,0:T(8,128)(2,1)S(1)} %get-tuple-element.132), channel_id=1, source_target_pairs={{0,16},{4,20},{8,24},{12,28},{16,0},{20,4},{24,8},{28,12},{1,17},{... | collective-permute-start | bytes 1572872 | tf_op jit(solution)/shard_map/ppermute | solution.py:325
  17.6 10.3 %collective-permute-done.1 = bf16[2,8,128,128]{3,2,1,0:T(8,128)(2,1)S(1)} collective-permute-done((bf16[2,8,128,128]{3,2,1,0:T(8,128)(2,1)S(1)}, bf16[2,8,128,128]{3,2,1,0:T(8,128)(2,1)S(1)}, u32[]{:S(2)}, u32[]{:S(2)}) %collective-permute-start.1) | collective-permute-done | bytes 524320 | tf_op jit(solution)/shard_map/ppermute | solution.py:325
  27.9 0.1 fusion.12
  28.0 1.8 %collective-permute-start.2 = (bf16[8,128,128]{2,1,0:T(8,128)(2,1)S(1)}, bf16[8,128,128]{2,1,0:T(8,128)(2,1)S(1)}, u32[]{:S(2)}, u32[]{:S(2)}) collective-permute-start(bf16[8,128,128]{2,1,0:T(8,128)(2,1)S(1)} %get-tuple-element.141), channel_id=1, source_target_pairs={{0,16},{4,20},{8,24},{12,28},{16,0},{20,4},{24,8},{28,12},{1,17},{... | collective-permute-start | bytes 786440 | tf_op jit(solution)/shard_map/ppermute | solution.py:325
  30.0 1.6 collective-permute-start.5
  31.6 4.4 %collective-permute-done.2.refs_1_ = bf16[8,128,128]{2,1,0:T(8,128)(2,1)S(1)} collective-permute-done((bf16[8,128,128]{2,1,0:T(8,128)(2,1)S(1)}, bf16[8,128,128]{2,1,0:T(8,128)(2,1)S(1)}, u32[]{:S(2)}, u32[]{:S(2)}) %collective-permute-start.2) | collective-permute-done | bytes 262176 | tf_op jit(solution)/shard_map/ppermute | solution.py:325
  35.9 1.4 collective-permute-done.5.refs_3_
  37.4 1.6 %collective-permute-start.8 = (bf16[16,128,128]{2,1,0:T(8,128)(2,1)S(1)}, bf16[16,128,128]{2,1,0:T(8,128)(2,1)S(1)}, u32[]{:S(2)}, u32[]{:S(2)}) collective-permute-start(bf16[16,128,128]{2,1,0:T(8,128)(2,1)S(1)} %finish.2.rest_0_), channel_id=1, source_target_pairs={{0,1},{1,0},{2,3},{3,2},{4,5},{5,4},{6,7},{7,6},{8,9},{9,8},{10,11... | collective-permute-start | bytes 1572872 | tf_op jit(solution)/shard_map/ppermute | solution.py:325
  39.1 2.5 %collective-permute-start.6 = (bf16[16,128,128]{2,1,0:T(8,128)(2,1)S(1)}, bf16[16,128,128]{2,1,0:T(8,128)(2,1)}, u32[]{:S(2)}, u32[]{:S(2)}) collective-permute-start(bf16[16,128,128]{2,1,0:T(8,128)(2,1)S(1)} %finish.2.rest_0_), channel_id=1, source_target_pairs={{0,3},{1,2},{2,1},{3,0},{4,7},{5,6},{6,5},{7,4},{8,11},{9,10},{10,... | collective-permute-start | bytes 1572872 | tf_op jit(solution)/shard_map/ppermute | solution.py:325
  41.6 2.4 %collective-permute-start.14 = (bf16[16,128,128]{2,1,0:T(8,128)(2,1)S(1)}, bf16[16,128,128]{2,1,0:T(8,128)(2,1)S(1)}, u32[]{:S(2)}, u32[]{:S(2)}) collective-permute-start(bf16[16,128,128]{2,1,0:T(8,128)(2,1)S(1)} %bitcast.87), channel_id=1, source_target_pairs={{0,24},{4,28},{8,16},{12,20},{16,8},{20,12},{24,0},{28,4},{1,25},{... | collective-permute-start | bytes 1572872 | tf_op jit(solution)/shard_map/ppermute | solution.py:325
  43.9 0.6 collective-permute-start.12
  44.5 0.5 collective-permute-start.10
  45.1 6.4 %collective-permute-done.8.rest_1_ = bf16[16,128,128]{2,1,0:T(8,128)(2,1)S(1)} collective-permute-done((bf16[16,128,128]{2,1,0:T(8,128)(2,1)S(1)}, bf16[16,128,128]{2,1,0:T(8,128)(2,1)S(1)}, u32[]{:S(2)}, u32[]{:S(2)}) %collective-permute-start.8) | collective-permute-done | bytes 524320 | tf_op jit(solution)/shard_map/ppermute | solution.py:325
  51.5 0.8 copy-done.2
  52.3 10.7 %collective-permute-done.6.rest_2_ = bf16[16,128,128]{2,1,0:T(8,128)(2,1)} collective-permute-done((bf16[16,128,128]{2,1,0:T(8,128)(2,1)S(1)}, bf16[16,128,128]{2,1,0:T(8,128)(2,1)}, u32[]{:S(2)}, u32[]{:S(2)}) %collective-permute-start.6) | collective-permute-done | bytes 524320 | tf_op jit(solution)/shard_map/ppermute | solution.py:325
  62.9 0.6 collective-permute-start.7
  63.5 1.6 %collective-permute-done.12.rest_4_ = bf16[16,128,128]{2,1,0:T(8,128)(2,1)S(1)} collective-permute-done((bf16[16,128,128]{2,1,0:T(8,128)(2,1)S(1)}, bf16[16,128,128]{2,1,0:T(8,128)(2,1)S(1)}, u32[]{:S(2)}, u32[]{:S(2)}) %collective-permute-start.12) | collective-permute-done | bytes 524320 | tf_op jit(solution)/shard_map/ppermute | solution.py:325
  65.1 0.5 collective-permute-start.11
  65.7 0.6 constant_dynamic-slice_fusion.3
  66.3 1.0 copy-done.3
  67.4 1.9 %dense_early.1 = (f32[2,128,1024]{2,1,0:T(8,128)S(1)}, f32[4,128,128]{2,1,0:T(8,128)S(1)}) custom-call(s32[1]{0:T(128)} %bitcast.1.col_ref, bf16[128,512]{1,0:T(8,128)(2,1)S(1)} %pad_maximum_fusion.1.weight_ref, bf16[16,128,128]{2,1,0:T(8,128)(2,1)S(1)} %finish.2.rest_0_, bf16[16,128,128]{2,1,0:T(8,128)(2,1)S(1)} %copy-done.3, ...), custom_call_target="tpu_custom_call" | custom-call | tf_op jit(solution)/shard_map/dense_early/pallas_call | solution.py:255
  69.3 4.9 %collective-permute-done.7.shard_ref = bf16[16,128,128]{2,1,0:T(8,128)(2,1)} collective-permute-done((bf16[16,128,128]{2,1,0:T(8,128)(2,1)}, bf16[16,128,128]{2,1,0:T(8,128)(2,1)}, u32[]{:S(2)}, u32[]{:S(2)}) %collective-permute-start.7) | collective-permute-done | bytes 524320 | tf_op jit(solution)/shard_map/ppermute | solution.py:325
  74.2 1.0 copy-done.5
  75.2 1.5 dense_late.1
  76.8 5.6 %collective-permute-start.17 = (bf16[8,128,128]{2,1,0:T(8,128)(2,1)S(1)}, bf16[8,128,128]{2,1,0:T(8,128)(2,1)S(1)}, u32[]{:S(2)}, u32[]{:S(2)}) collective-permute-start(bf16[8,128,128]{2,1,0:T(8,128)(2,1)S(1)} %get-tuple-element.88.rest_0_), channel_id=1, source_target_pairs={{0,3},{1,2},{2,1},{3,0},{4,7},{5,6},{6,5},{7,4},{8,11},{9,10},{10,... | collective-permute-start | bytes 786440 | tf_op jit(solution)/shard_map/ppermute | solution.py:325
  82.4 0.4 collective-permute-start.20
  82.7 1.7 %collective-permute-start.19 = (bf16[8,128,128]{2,1,0:T(8,128)(2,1)S(1)}, bf16[8,128,128]{2,1,0:T(8,128)(2,1)S(1)}, u32[]{:S(2)}, u32[]{:S(2)}) collective-permute-start(bf16[8,128,128]{2,1,0:T(8,128)(2,1)S(1)} %get-tuple-element.101.rest_0_), channel_id=1, source_target_pairs={{0,1},{1,0},{2,3},{3,2},{4,5},{5,4},{6,7},{7,6},{8,9},{9,8},{10,11... | collective-permute-start | bytes 786440 | tf_op jit(solution)/shard_map/ppermute | solution.py:325
  84.5 6.6 %aggregate.1 = bf16[16,128,128]{2,1,0:T(8,128)(2,1)S(1)} custom-call(s32[16,20]{1,0:T(8,128)S(1)} %copy-done.8, s32[1]{0:T(128)} %bitcast.me_ref.refs_4_, bf16[16,20,128,128]{3,2,1,0:T(8,128)(2,1)} %tiles_ref.5, bf16[16,128,128]{2,1,0:T(8,128)(2,1)S(1)} %bitcast.91, bf16[16,128,128]{2,1,0:T(8,128)(2,1)} %collective-permute-done.9.rest_1_, ...), custom_call_target="tpu_custom_call" | custom-call | flops 1342177280 | bytes 30000000 | tf_op jit(solution)/shard_map/aggregate/pallas_call | solution.py:149
  91.1 4.3 %collective-permute-done.16.rest_1_ = bf16[8,128,128]{2,1,0:T(8,128)(2,1)S(1)} collective-permute-done((bf16[8,128,128]{2,1,0:T(8,128)(2,1)S(1)}, bf16[8,128,128]{2,1,0:T(8,128)(2,1)S(1)}, u32[]{:S(2)}, u32[]{:S(2)}) %collective-permute-start.16) | collective-permute-done | bytes 262176 | tf_op jit(solution)/shard_map/ppermute | solution.py:325
  95.4 1.8 %collective-permute-start.18 = (bf16[8,128,128]{2,1,0:T(8,128)(2,1)S(1)}, bf16[8,128,128]{2,1,0:T(8,128)(2,1)S(1)}, u32[]{:S(2)}, u32[]{:S(2)}) collective-permute-start(bf16[8,128,128]{2,1,0:T(8,128)(2,1)S(1)} %collective-permute-done.17.rest_3_), channel_id=1, source_target_pairs={{0,1},{1,0},{2,3},{3,2},{4,5},{5,4},{6,7},{7,6},{8,9},{9,8},{10,11... | collective-permute-start | bytes 786440 | tf_op jit(solution)/shard_map/ppermute | solution.py:325
  97.2 3.7 %collective-permute-done.20.rest_3_ = bf16[8,128,128]{2,1,0:T(8,128)(2,1)S(1)} collective-permute-done((bf16[8,128,128]{2,1,0:T(8,128)(2,1)S(1)}, bf16[8,128,128]{2,1,0:T(8,128)(2,1)S(1)}, u32[]{:S(2)}, u32[]{:S(2)}) %collective-permute-start.20) | collective-permute-done | bytes 262176 | tf_op jit(solution)/shard_map/ppermute | solution.py:325
  100.9 5.1 %collective-permute-done.19.rest_1_ = bf16[8,128,128]{2,1,0:T(8,128)(2,1)S(1)} collective-permute-done((bf16[8,128,128]{2,1,0:T(8,128)(2,1)S(1)}, bf16[8,128,128]{2,1,0:T(8,128)(2,1)S(1)}, u32[]{:S(2)}, u32[]{:S(2)}) %collective-permute-start.19) | collective-permute-done | bytes 262176 | tf_op jit(solution)/shard_map/ppermute | solution.py:325
  106.0 2.5 %collective-permute-start.21 = (bf16[8,128,128]{2,1,0:T(8,128)(2,1)S(1)}, bf16[8,128,128]{2,1,0:T(8,128)(2,1)S(1)}, u32[]{:S(2)}, u32[]{:S(2)}) collective-permute-start(bf16[8,128,128]{2,1,0:T(8,128)(2,1)S(1)} %collective-permute-done.20.rest_3_), channel_id=1, source_target_pairs={{0,1},{1,0},{2,3},{3,2},{4,5},{5,4},{6,7},{7,6},{8,9},{9,8},{10,11... | collective-permute-start | bytes 786440 | tf_op jit(solution)/shard_map/ppermute | solution.py:325
  108.5 3.1 %collective-permute-done.18.rest_2_ = bf16[8,128,128]{2,1,0:T(8,128)(2,1)S(1)} collective-permute-done((bf16[8,128,128]{2,1,0:T(8,128)(2,1)S(1)}, bf16[8,128,128]{2,1,0:T(8,128)(2,1)S(1)}, u32[]{:S(2)}, u32[]{:S(2)}) %collective-permute-start.18) | collective-permute-done | bytes 262176 | tf_op jit(solution)/shard_map/ppermute | solution.py:325
  111.6 0.6 dense.2
  112.2 4.6 %collective-permute-done.21.rest_2_ = bf16[8,128,128]{2,1,0:T(8,128)(2,1)S(1)} collective-permute-done((bf16[8,128,128]{2,1,0:T(8,128)(2,1)S(1)}, bf16[8,128,128]{2,1,0:T(8,128)(2,1)S(1)}, u32[]{:S(2)}, u32[]{:S(2)}) %collective-permute-start.21) | collective-permute-done | bytes 262176 | tf_op jit(solution)/shard_map/ppermute | solution.py:325
  116.8 0.6 dense.3
  117.3 6.7 %spread.3 = (bf16[4,8,128,128]{3,2,1,0:T(8,128)(2,1)S(1)}, bf16[4,8,128,128]{3,2,1,0:T(8,128)(2,1)S(1)}, bf16[4,8,128,128]{3,2,1,0:T(8,128)(2,1)S(1)}, bf16[4,8,128,128]{3,2,1,0:T(8,128)(2,1)S(1)}) custom-call(s32[16,20]{1,0:T(8,128)S(1)} %copy-done.8, s32[1]{0:T(128)} %bitcast.me_ref.refs_4_, bf16[16,20,128,128]{3,2,1,0:T(8,128)(2,1)} %tiles_ref.5, ...), custom_call_target="tpu_custom_call" | custom-call | flops 1342177280 | bytes 30000000 | tf_op jit(solution)/shard_map/spread/pallas_call | solution.py:107
  124.1 0.5 collective-permute-start.23
  124.6 0.2 weight_terms.1
  124.8 0.1 collective-permute-start.24
  125.0 1.8 %collective-permute-done.22 = bf16[4,8,128,128]{3,2,1,0:T(8,128)(2,1)S(1)} collective-permute-done((bf16[4,8,128,128]{3,2,1,0:T(8,128)(2,1)S(1)}, bf16[4,8,128,128]{3,2,1,0:T(8,128)(2,1)S(1)}, u32[]{:S(2)}, u32[]{:S(2)}) %collective-permute-start.22) | collective-permute-done | bytes 1048608 | tf_op jit(solution)/shard_map/ppermute | solution.py:325
  126.8 0.4 fusion.1
  127.1 1.6 collective-permute-start.25
  128.7 0.4 add_convert_fusion.2
  129.1 1.8 %collective-permute-start.26 = (bf16[2,8,128,128]{3,2,1,0:T(8,128)(2,1)S(1)}, bf16[2,8,128,128]{3,2,1,0:T(8,128)(2,1)S(1)}, u32[]{:S(2)}, u32[]{:S(2)}) collective-permute-start(bf16[2,8,128,128]{3,2,1,0:T(8,128)(2,1)S(1)} %get-tuple-element.128), channel_id=1, source_target_pairs={{0,16},{4,20},{8,24},{12,28},{16,0},{20,4},{24,8},{28,12},{1,17},{... | collective-permute-start | bytes 1572872 | tf_op jit(solution)/shard_map/ppermute | solution.py:325
  130.9 0.4 collective-permute-start.27
  131.3 14.4 %collective-permute-done.27 = bf16[128,512]{1,0:T(8,128)(2,1)S(1)} collective-permute-done((bf16[128,512]{1,0:T(8,128)(2,1)S(1)}, bf16[128,512]{1,0:T(8,128)(2,1)S(1)}, u32[]{:S(2)}, u32[]{:S(2)}) %collective-permute-start.27) | collective-permute-done | bytes 131104 | tf_op jit(solution)/shard_map/ppermute | solution.py:325
  145.7 0.1 fusion.9
  145.9 0.1 fusion.10
  146.0 1.4 collective-permute-start.30
  147.4 0.7 collective-permute-start.29
  148.1 1.7 %collective-permute-start.28 = (bf16[8,128,128]{2,1,0:T(8,128)(2,1)S(1)}, bf16[8,128,128]{2,1,0:T(8,128)(2,1)S(1)}, u32[]{:S(2)}, u32[]{:S(2)}) collective-permute-start(bf16[8,128,128]{2,1,0:T(8,128)(2,1)S(1)} %get-tuple-element.137), channel_id=1, source_target_pairs={{0,16},{4,20},{8,24},{12,28},{16,0},{20,4},{24,8},{28,12},{1,17},{... | collective-permute-start | bytes 786440 | tf_op jit(solution)/shard_map/ppermute | solution.py:325
  149.8 2.7 %collective-permute-done.30 = bf16[128,512]{1,0:T(8,128)(2,1)S(1)} collective-permute-done((bf16[128,512]{1,0:T(8,128)(2,1)S(1)}, bf16[128,512]{1,0:T(8,128)(2,1)S(1)}, u32[]{:S(2)}, u32[]{:S(2)}) %collective-permute-start.30) | collective-permute-done | bytes 131104 | tf_op jit(solution)/shard_map/ppermute | solution.py:325
  152.6 3.4 %collective-permute-done.29.refs_3_ = bf16[8,128,128]{2,1,0:T(8,128)(2,1)S(1)} collective-permute-done((bf16[8,128,128]{2,1,0:T(8,128)(2,1)S(1)}, bf16[8,128,128]{2,1,0:T(8,128)(2,1)S(1)}, u32[]{:S(2)}, u32[]{:S(2)}) %collective-permute-start.29) | collective-permute-done | bytes 262176 | tf_op jit(solution)/shard_map/ppermute | solution.py:325
  156.1 1.2 finish.3
  (57 shorter events, 0.9 us)
Async XLA Ops:
  0.6 1.0 copy-start.6
  1.7 0.7 copy-start.7
  2.4 39.2 %copy-start.1 = (bf16[2048,128]{1,0:T(8,128)(2,1)S(1)}, bf16[2048,128]{1,0:T(8,128)(2,1)}, u32[]{:S(2)}) copy-start(bf16[2048,128]{1,0:T(8,128)(2,1)} %param.8) | copy-start | bytes 1572868
  2.4 63.2 %copy-start.9 = (bf16[128,512]{1,0:T(8,128)(2,1)S(1)}, bf16[128,512]{1,0:T(8,128)(2,1)}, u32[]{:S(2)}) copy-start(bf16[128,512]{1,0:T(8,128)(2,1)} %param.14) | copy-start | bytes 393220
  2.4 63.2 %copy-start.10 = (bf16[128,512]{1,0:T(8,128)(2,1)S(1)}, bf16[128,512]{1,0:T(8,128)(2,1)}, u32[]{:S(2)}) copy-start(bf16[128,512]{1,0:T(8,128)(2,1)} %param.15) | copy-start | bytes 393220
  2.4 63.9 %copy-start = (bf16[2048,128]{1,0:T(8,128)(2,1)S(1)}, bf16[2048,128]{1,0:T(8,128)(2,1)}, u32[]{:S(2)}) copy-start(bf16[2048,128]{1,0:T(8,128)(2,1)} %param.9) | copy-start | bytes 1572868
  9.4 55.7 %copy-start.4 = (bf16[16,128,128]{2,1,0:T(8,128)(2,1)}, bf16[16,128,128]{2,1,0:T(8,128)(2,1)S(1)}, u32[]{:S(2)}) copy-start(bf16[16,128,128]{2,1,0:T(8,128)(2,1)S(1)} %get-tuple-element.78.mask_ref) | copy-start | bytes 1572868
  9.4 75.0 %copy-start.8 = (s32[16,20]{1,0:T(8,128)S(1)}, s32[16,20]{1,0:T(8,128)}, u32[]{:S(2)}) copy-start(s32[16,20]{1,0:T(8,128)} %cols_ref.5) | copy-start | bytes 3844
  9.5 2.8 %collective-permute-start = (bf16[4,8,128,128]{3,2,1,0:T(8,128)(2,1)S(1)}, bf16[4,8,128,128]{3,2,1,0:T(8,128)(2,1)S(1)}, u32[]{:S(2)}, u32[]{:S(2)}) collective-permute-start(bf16[4,8,128,128]{3,2,1,0:T(8,128)(2,1)S(1)} %get-tuple-element.66), channel_id=1, source_target_pairs={{0,4},{4,0},{8,12},{12,8},{16,20},{20,16},{24,28},{28,24},{1,5},{5... | collective-permute-start | bytes 3145736 | tf_op jit(solution)/shard_map/ppermute | solution.py:325
  10.0 5.7 %collective-permute-start.3 = (bf16[4,8,128,128]{3,2,1,0:T(8,128)(2,1)S(1)}, bf16[4,8,128,128]{3,2,1,0:T(8,128)(2,1)S(1)}, u32[]{:S(2)}, u32[]{:S(2)}) collective-permute-start(bf16[4,8,128,128]{3,2,1,0:T(8,128)(2,1)S(1)} %get-tuple-element.68), channel_id=1, source_target_pairs={{0,4},{4,0},{8,12},{12,8},{16,20},{20,16},{24,28},{28,24},{1,5},{5... | collective-permute-start | bytes 3145736 | tf_op jit(solution)/shard_map/ppermute | solution.py:325
  12.7 15.2 %collective-permute-start.1 = (bf16[2,8,128,128]{3,2,1,0:T(8,128)(2,1)S(1)}, bf16[2,8,128,128]{3,2,1,0:T(8,128)(2,1)S(1)}, u32[]{:S(2)}, u32[]{:S(2)}) collective-permute-start(bf16[2,8,128,128]{3,2,1,0:T(8,128)(2,1)S(1)} %get-tuple-element.134), channel_id=1, source_target_pairs={{0,8},{4,12},{8,0},{12,4},{16,24},{20,28},{24,16},{28,20},{1,9},{5... | collective-permute-start | bytes 1572872 | tf_op jit(solution)/shard_map/ppermute | solution.py:325
  16.0 13.9 %collective-permute-start.4 = (bf16[2,8,128,128]{3,2,1,0:T(8,128)(2,1)S(1)}, bf16[2,8,128,128]{3,2,1,0:T(8,128)(2,1)S(1)}, u32[]{:S(2)}, u32[]{:S(2)}) collective-permute-start(bf16[2,8,128,128]{3,2,1,0:T(8,128)(2,1)S(1)} %get-tuple-element.132), channel_id=1, source_target_pairs={{0,16},{4,20},{8,24},{12,28},{16,0},{20,4},{24,8},{28,12},{1,17},{... | collective-permute-start | bytes 1572872 | tf_op jit(solution)/shard_map/ppermute | solution.py:325
  28.0 7.9 %collective-permute-start.2 = (bf16[8,128,128]{2,1,0:T(8,128)(2,1)S(1)}, bf16[8,128,128]{2,1,0:T(8,128)(2,1)S(1)}, u32[]{:S(2)}, u32[]{:S(2)}) collective-permute-start(bf16[8,128,128]{2,1,0:T(8,128)(2,1)S(1)} %get-tuple-element.141), channel_id=1, source_target_pairs={{0,16},{4,20},{8,24},{12,28},{16,0},{20,4},{24,8},{28,12},{1,17},{... | collective-permute-start | bytes 786440 | tf_op jit(solution)/shard_map/ppermute | solution.py:325
  30.0 7.3 %collective-permute-start.5 = (bf16[8,128,128]{2,1,0:T(8,128)(2,1)S(1)}, bf16[8,128,128]{2,1,0:T(8,128)(2,1)S(1)}, u32[]{:S(2)}, u32[]{:S(2)}) collective-permute-start(bf16[8,128,128]{2,1,0:T(8,128)(2,1)S(1)} %get-tuple-element.139), channel_id=1, source_target_pairs={{0,8},{4,12},{8,0},{12,4},{16,24},{20,28},{24,16},{28,20},{1,9},{5... | collective-permute-start | bytes 786440 | tf_op jit(solution)/shard_map/ppermute | solution.py:325
  37.4 14.0 %collective-permute-start.8 = (bf16[16,128,128]{2,1,0:T(8,128)(2,1)S(1)}, bf16[16,128,128]{2,1,0:T(8,128)(2,1)S(1)}, u32[]{:S(2)}, u32[]{:S(2)}) collective-permute-start(bf16[16,128,128]{2,1,0:T(8,128)(2,1)S(1)} %finish.2.rest_0_), channel_id=1, source_target_pairs={{0,1},{1,0},{2,3},{3,2},{4,5},{5,4},{6,7},{7,6},{8,9},{9,8},{10,11... | collective-permute-start | bytes 1572872 | tf_op jit(solution)/shard_map/ppermute | solution.py:325
  39.1 23.8 %collective-permute-start.6 = (bf16[16,128,128]{2,1,0:T(8,128)(2,1)S(1)}, bf16[16,128,128]{2,1,0:T(8,128)(2,1)}, u32[]{:S(2)}, u32[]{:S(2)}) collective-permute-start(bf16[16,128,128]{2,1,0:T(8,128)(2,1)S(1)} %finish.2.rest_0_), channel_id=1, source_target_pairs={{0,3},{1,2},{2,1},{3,0},{4,7},{5,6},{6,5},{7,4},{8,11},{9,10},{10,... | collective-permute-start | bytes 1572872 | tf_op jit(solution)/shard_map/ppermute | solution.py:325
  41.6 21.9 %collective-permute-start.14 = (bf16[16,128,128]{2,1,0:T(8,128)(2,1)S(1)}, bf16[16,128,128]{2,1,0:T(8,128)(2,1)S(1)}, u32[]{:S(2)}, u32[]{:S(2)}) collective-permute-start(bf16[16,128,128]{2,1,0:T(8,128)(2,1)S(1)} %bitcast.87), channel_id=1, source_target_pairs={{0,24},{4,28},{8,16},{12,20},{16,8},{20,12},{24,0},{28,4},{1,25},{... | collective-permute-start | bytes 1572872 | tf_op jit(solution)/shard_map/ppermute | solution.py:325
  43.9 21.2 %collective-permute-start.12 = (bf16[16,128,128]{2,1,0:T(8,128)(2,1)S(1)}, bf16[16,128,128]{2,1,0:T(8,128)(2,1)S(1)}, u32[]{:S(2)}, u32[]{:S(2)}) collective-permute-start(bf16[16,128,128]{2,1,0:T(8,128)(2,1)S(1)} %bitcast.88), channel_id=1, source_target_pairs={{0,16},{4,20},{8,24},{12,28},{16,0},{20,4},{24,8},{28,12},{1,17},{... | collective-permute-start | bytes 1572872 | tf_op jit(solution)/shard_map/ppermute | solution.py:325
  44.5 20.6 %collective-permute-start.10 = (bf16[16,128,128]{2,1,0:T(8,128)(2,1)S(1)}, bf16[16,128,128]{2,1,0:T(8,128)(2,1)S(1)}, u32[]{:S(2)}, u32[]{:S(2)}) collective-permute-start(bf16[16,128,128]{2,1,0:T(8,128)(2,1)S(1)} %bitcast.89), channel_id=1, source_target_pairs={{0,8},{4,12},{8,0},{12,4},{16,24},{20,28},{24,16},{28,20},{1,9},{5... | collective-permute-start | bytes 1572872 | tf_op jit(solution)/shard_map/ppermute | solution.py:325
  51.5 0.8 copy-start.2
  52.3 17.0 %collective-permute-start.9 = (bf16[16,128,128]{2,1,0:T(8,128)(2,1)S(1)}, bf16[16,128,128]{2,1,0:T(8,128)(2,1)}, u32[]{:S(2)}, u32[]{:S(2)}) collective-permute-start(bf16[16,128,128]{2,1,0:T(8,128)(2,1)S(1)} %bitcast.90), channel_id=1, source_target_pairs={{0,4},{4,0},{8,12},{12,8},{16,20},{20,16},{24,28},{28,24},{1,5},{5... | collective-permute-start | bytes 1572872 | tf_op jit(solution)/shard_map/ppermute | solution.py:325
  62.9 11.3 %collective-permute-start.7 = (bf16[16,128,128]{2,1,0:T(8,128)(2,1)}, bf16[16,128,128]{2,1,0:T(8,128)(2,1)}, u32[]{:S(2)}, u32[]{:S(2)}) collective-permute-start(bf16[16,128,128]{2,1,0:T(8,128)(2,1)} %collective-permute-done.6.rest_2_), channel_id=1, source_target_pairs={{0,1},{1,0},{2,3},{3,2},{4,5},{5,4},{6,7},{7,6},{8,9},{9,8},{10,11... | collective-permute-start | bytes 1572872 | tf_op jit(solution)/shard_map/ppermute | solution.py:325
  63.5 10.7 %collective-permute-start.15 = (bf16[16,128,128]{2,1,0:T(8,128)(2,1)S(1)}, bf16[16,128,128]{2,1,0:T(8,128)(2,1)}, u32[]{:S(2)}, u32[]{:S(2)}) collective-permute-start(bf16[16,128,128]{2,1,0:T(8,128)(2,1)S(1)} %collective-permute-done.14.rest_6_), channel_id=1, source_target_pairs={{0,4},{4,0},{8,12},{12,8},{16,20},{20,16},{24,28},{28,24},{1,5},{5... | collective-permute-start | bytes 1572872 | tf_op jit(solution)/shard_map/ppermute | solution.py:325
  65.1 9.1 %collective-permute-start.13 = (bf16[16,128,128]{2,1,0:T(8,128)(2,1)S(1)}, bf16[16,128,128]{2,1,0:T(8,128)(2,1)}, u32[]{:S(2)}, u32[]{:S(2)}) collective-permute-start(bf16[16,128,128]{2,1,0:T(8,128)(2,1)S(1)} %collective-permute-done.12.rest_4_), channel_id=1, source_target_pairs={{0,4},{4,0},{8,12},{12,8},{16,20},{20,16},{24,28},{28,24},{1,5},{5... | collective-permute-start | bytes 1572872 | tf_op jit(solution)/shard_map/ppermute | solution.py:325
  65.1 9.1 %collective-permute-start.11 = (bf16[16,128,128]{2,1,0:T(8,128)(2,1)S(1)}, bf16[16,128,128]{2,1,0:T(8,128)(2,1)}, u32[]{:S(2)}, u32[]{:S(2)}) collective-permute-start(bf16[16,128,128]{2,1,0:T(8,128)(2,1)S(1)} %collective-permute-done.10.rest_2_), channel_id=1, source_target_pairs={{0,4},{4,0},{8,12},{12,8},{16,20},{20,16},{24,28},{28,24},{1,5},{5... | collective-permute-start | bytes 1572872 | tf_op jit(solution)/shard_map/ppermute | solution.py:325
  66.3 1.0 copy-start.3
  74.2 1.0 copy-start.5
  76.8 14.3 %collective-permute-start.17 = (bf16[8,128,128]{2,1,0:T(8,128)(2,1)S(1)}, bf16[8,128,128]{2,1,0:T(8,128)(2,1)S(1)}, u32[]{:S(2)}, u32[]{:S(2)}) collective-permute-start(bf16[8,128,128]{2,1,0:T(8,128)(2,1)S(1)} %get-tuple-element.88.rest_0_), channel_id=1, source_target_pairs={{0,3},{1,2},{2,1},{3,0},{4,7},{5,6},{6,5},{7,4},{8,11},{9,10},{10,... | collective-permute-start | bytes 786440 | tf_op jit(solution)/shard_map/ppermute | solution.py:325
  82.4 13.0 %collective-permute-start.16 = (bf16[8,128,128]{2,1,0:T(8,128)(2,1)S(1)}, bf16[8,128,128]{2,1,0:T(8,128)(2,1)S(1)}, u32[]{:S(2)}, u32[]{:S(2)}) collective-permute-start(bf16[8,128,128]{2,1,0:T(8,128)(2,1)S(1)} %get-tuple-element.88.rest_0_), channel_id=1, source_target_pairs={{0,1},{1,0},{2,3},{3,2},{4,5},{5,4},{6,7},{7,6},{8,9},{9,8},{10,11... | collective-permute-start | bytes 786440 | tf_op jit(solution)/shard_map/ppermute | solution.py:325
  82.4 18.5 %collective-permute-start.20 = (bf16[8,128,128]{2,1,0:T(8,128)(2,1)S(1)}, bf16[8,128,128]{2,1,0:T(8,128)(2,1)S(1)}, u32[]{:S(2)}, u32[]{:S(2)}) collective-permute-start(bf16[8,128,128]{2,1,0:T(8,128)(2,1)S(1)} %get-tuple-element.101.rest_0_), channel_id=1, source_target_pairs={{0,3},{1,2},{2,1},{3,0},{4,7},{5,6},{6,5},{7,4},{8,11},{9,10},{10,... | collective-permute-start | bytes 786440 | tf_op jit(solution)/shard_map/ppermute | solution.py:325
  82.7 23.3 %collective-permute-start.19 = (bf16[8,128,128]{2,1,0:T(8,128)(2,1)S(1)}, bf16[8,128,128]{2,1,0:T(8,128)(2,1)S(1)}, u32[]{:S(2)}, u32[]{:S(2)}) collective-permute-start(bf16[8,128,128]{2,1,0:T(8,128)(2,1)S(1)} %get-tuple-element.101.rest_0_), channel_id=1, source_target_pairs={{0,1},{1,0},{2,3},{3,2},{4,5},{5,4},{6,7},{7,6},{8,9},{9,8},{10,11... | collective-permute-start | bytes 786440 | tf_op jit(solution)/shard_map/ppermute | solution.py:325
  95.4 16.2 %collective-permute-start.18 = (bf16[8,128,128]{2,1,0:T(8,128)(2,1)S(1)}, bf16[8,128,128]{2,1,0:T(8,128)(2,1)S(1)}, u32[]{:S(2)}, u32[]{:S(2)}) collective-permute-start(bf16[8,128,128]{2,1,0:T(8,128)(2,1)S(1)} %collective-permute-done.17.rest_3_), channel_id=1, source_target_pairs={{0,1},{1,0},{2,3},{3,2},{4,5},{5,4},{6,7},{7,6},{8,9},{9,8},{10,11... | collective-permute-start | bytes 786440 | tf_op jit(solution)/shard_map/ppermute | solution.py:325
  106.0 10.8 %collective-permute-start.21 = (bf16[8,128,128]{2,1,0:T(8,128)(2,1)S(1)}, bf16[8,128,128]{2,1,0:T(8,128)(2,1)S(1)}, u32[]{:S(2)}, u32[]{:S(2)}) collective-permute-start(bf16[8,128,128]{2,1,0:T(8,128)(2,1)S(1)} %collective-permute-done.20.rest_3_), channel_id=1, source_target_pairs={{0,1},{1,0},{2,3},{3,2},{4,5},{5,4},{6,7},{7,6},{8,9},{9,8},{10,11... | collective-permute-start | bytes 786440 | tf_op jit(solution)/shard_map/ppermute | solution.py:325
  124.0 2.7 %collective-permute-start.22 = (bf16[4,8,128,128]{3,2,1,0:T(8,128)(2,1)S(1)}, bf16[4,8,128,128]{3,2,1,0:T(8,128)(2,1)S(1)}, u32[]{:S(2)}, u32[]{:S(2)}) collective-permute-start(bf16[4,8,128,128]{3,2,1,0:T(8,128)(2,1)S(1)} %get-tuple-element.106), channel_id=1, source_target_pairs={{0,4},{4,0},{8,12},{12,8},{16,20},{20,16},{24,28},{28,24},{1,5},{5... | collective-permute-start | bytes 3145736 | tf_op jit(solution)/shard_map/ppermute | solution.py:325
  124.1 4.6 %collective-permute-start.23 = (bf16[4,8,128,128]{3,2,1,0:T(8,128)(2,1)S(1)}, bf16[4,8,128,128]{3,2,1,0:T(8,128)(2,1)S(1)}, u32[]{:S(2)}, u32[]{:S(2)}) collective-permute-start(bf16[4,8,128,128]{3,2,1,0:T(8,128)(2,1)S(1)} %get-tuple-element.108), channel_id=1, source_target_pairs={{0,4},{4,0},{8,12},{12,8},{16,20},{20,16},{24,28},{28,24},{1,5},{5... | collective-permute-start | bytes 3145736 | tf_op jit(solution)/shard_map/ppermute | solution.py:325
  124.8 6.0 %collective-permute-start.24 = (bf16[128,512]{1,0:T(8,128)(2,1)S(1)}, bf16[128,512]{1,0:T(8,128)(2,1)S(1)}, u32[]{:S(2)}, u32[]{:S(2)}) collective-permute-start(bf16[128,512]{1,0:T(8,128)(2,1)S(1)} %get-tuple-element.114), channel_id=1, source_target_pairs={{0,4},{4,0},{8,12},{12,8},{16,20},{20,16},{24,28},{28,24},{1,5},{5... | collective-permute-start | bytes 393224 | tf_op jit(solution)/shard_map/ppermute | solution.py:325
  127.1 18.5 %collective-permute-start.25 = (bf16[2,8,128,128]{3,2,1,0:T(8,128)(2,1)S(1)}, bf16[2,8,128,128]{3,2,1,0:T(8,128)(2,1)S(1)}, u32[]{:S(2)}, u32[]{:S(2)}) collective-permute-start(bf16[2,8,128,128]{3,2,1,0:T(8,128)(2,1)S(1)} %get-tuple-element.130), channel_id=1, source_target_pairs={{0,8},{4,12},{8,0},{12,4},{16,24},{20,28},{24,16},{28,20},{1,9},{5... | collective-permute-start | bytes 1572872 | tf_op jit(solution)/shard_map/ppermute | solution.py:325
  129.1 16.6 %collective-permute-start.26 = (bf16[2,8,128,128]{3,2,1,0:T(8,128)(2,1)S(1)}, bf16[2,8,128,128]{3,2,1,0:T(8,128)(2,1)S(1)}, u32[]{:S(2)}, u32[]{:S(2)}) collective-permute-start(bf16[2,8,128,128]{3,2,1,0:T(8,128)(2,1)S(1)} %get-tuple-element.128), channel_id=1, source_target_pairs={{0,16},{4,20},{8,24},{12,28},{16,0},{20,4},{24,8},{28,12},{1,17},{... | collective-permute-start | bytes 1572872 | tf_op jit(solution)/shard_map/ppermute | solution.py:325
  130.9 14.8 %collective-permute-start.27 = (bf16[128,512]{1,0:T(8,128)(2,1)S(1)}, bf16[128,512]{1,0:T(8,128)(2,1)S(1)}, u32[]{:S(2)}, u32[]{:S(2)}) collective-permute-start(bf16[128,512]{1,0:T(8,128)(2,1)S(1)} %convert_add_fusion.4), channel_id=1, source_target_pairs={{0,16},{4,20},{8,24},{12,28},{16,0},{20,4},{24,8},{28,12},{1,17},{... | collective-permute-start | bytes 393224 | tf_op jit(solution)/shard_map/ppermute | solution.py:325
  146.0 6.5 %collective-permute-start.30 = (bf16[128,512]{1,0:T(8,128)(2,1)S(1)}, bf16[128,512]{1,0:T(8,128)(2,1)S(1)}, u32[]{:S(2)}, u32[]{:S(2)}) collective-permute-start(bf16[128,512]{1,0:T(8,128)(2,1)S(1)} %convert_add_fusion.3), channel_id=1, source_target_pairs={{0,8},{4,12},{8,0},{12,4},{16,24},{20,28},{24,16},{28,20},{1,9},{5... | collective-permute-start | bytes 393224 | tf_op jit(solution)/shard_map/ppermute | solution.py:325
  147.4 8.7 %collective-permute-start.29 = (bf16[8,128,128]{2,1,0:T(8,128)(2,1)S(1)}, bf16[8,128,128]{2,1,0:T(8,128)(2,1)S(1)}, u32[]{:S(2)}, u32[]{:S(2)}) collective-permute-start(bf16[8,128,128]{2,1,0:T(8,128)(2,1)S(1)} %get-tuple-element.135), channel_id=1, source_target_pairs={{0,8},{4,12},{8,0},{12,4},{16,24},{20,28},{24,16},{28,20},{1,9},{5... | collective-permute-start | bytes 786440 | tf_op jit(solution)/shard_map/ppermute | solution.py:325
  148.1 8.0 %collective-permute-start.28 = (bf16[8,128,128]{2,1,0:T(8,128)(2,1)S(1)}, bf16[8,128,128]{2,1,0:T(8,128)(2,1)S(1)}, u32[]{:S(2)}, u32[]{:S(2)}) collective-permute-start(bf16[8,128,128]{2,1,0:T(8,128)(2,1)S(1)} %get-tuple-element.137), channel_id=1, source_target_pairs={{0,16},{4,20},{8,24},{12,28},{16,0},{20,4},{24,8},{28,12},{1,17},{... | collective-permute-start | bytes 786440 | tf_op jit(solution)/shard_map/ppermute | solution.py:325
  152.6 3.5 %collective-permute-start.31 = (f32[128,512]{1,0:T(8,128)S(1)}, f32[128,512]{1,0:T(8,128)S(1)}, u32[]{:S(2)}, u32[]{:S(2)}) collective-permute-start(f32[128,512]{1,0:T(8,128)S(1)} %convert_add_fusion.2.refs_5_), channel_id=1, source_target_pairs={{0,4},{4,0},{8,12},{12,8},{16,20},{20,16},{24,28},{28,24},{1,5},{5... | collective-permute-start | bytes 786440 | tf_op jit(solution)/shard_map/ppermute | solution.py:325

commit v14 on v13

--- a/solution.py
+++ b/solution.py
@@ -334,7 +334,7 @@
     shape = (2,) * len(chips) + pieces[0].shape[1:]
     keeps = [pieces[2 * g].reshape(shape) for g in range(GROUPS)]
     gots = [swap(pieces[2 * g + 1], 1, "row").reshape(shape) for g in range(GROUPS)]
-    orders = [chips if g % 2 == 0 else chips[::-1] for g in range(GROUPS)]
+    orders = [chips if g % 2 else chips[::-1] for g in range(GROUPS)]
     lefts = [chips[::-1] for _ in range(GROUPS)]
     for level in range(len(chips)):
         masks = [order[level] for order in orders]
@@ -400,10 +400,14 @@
     deltas[0], parts = after((deltas[0], parts))
     agg_feats = aggregate(edge_tiles, block_cols, parts, me_at)
     inputs, firsts = [], []
+    shards = []
     for g in range(GROUPS):
-        shards, beside = gather_columns(deltas[g], cols, agg_feats if g == 0 else ())
+        arrived, beside = gather_columns(deltas[g], cols, agg_feats if g == 0 else (), g == 0)
         agg_feats = beside if g == 0 else agg_feats
-        out, grad = dense(weight_one, shards, cut(agg_feats, g), None, col_at, 1)
+        shards.append(arrived)
+    shards[0][2], shards[1][1] = after((shards[0][2], shards[1][1]))
+    for g in range(GROUPS):
+        out, grad = dense(weight_one, shards[g], cut(agg_feats, g), None, col_at, 1)
         inputs.append(out)
         firsts.append(grad)
     pieces = spread(edge_tiles, block_cols, inputs, me_at, rows)

time: 158 us -> 157 us (level)
  waiting for transfers between devices: 84.9 us -> 82.6 us
    ppermute x32, waiting for transfers between devices: 84.9 us -> 82.6 us  [swap(): lax.ppermute(value, axis, [(i, i ^ mask) for i in range(lax.axis_size(axi...]
  transfers between devices with their start and end apart: 32 -> 32, of which waited for: 17 -> 19; matrix products, arithmetic and copies ran while one was open for 2% -> 2% of each run, Pallas kernels for 6% -> 6%
where the time goes in v14:
time: 157 us; the launch traced here: 156 us
  waiting for transfers between devices  82.6 us (53%)
  starting transfers between devices  38.6 us (25%)
  Pallas kernels  26.4 us (17%)
  local copies, waits for them, and re-layouts  5.34 us (3%)
  other arithmetic  2.21 us (1%)
    ppermute x32, waiting for transfers between devices, swap(): lax.ppermute(value, axis, [(i, i ^ mask) for i in range(lax.axis_size(axi...  82.6 us
    ppermute x32, starting transfers between devices, swap(): lax.ppermute(value, axis, [(i, i ^ mask) for i in range(lax.axis_size(axi...  38.6 us
    pallas_call x2, Pallas kernels, spread(): pl.pallas_call(functools.partial(spread_kernel, first, len(vals)), out_sh...  13.7 us
    pallas_call x1, Pallas kernels, aggregate(): pl.pallas_call(aggregate_kernel, out_shape=jax.ShapeDtypeStruct((blocks,...  6.59 us
    unnamed x30, local copies, waits for them, and re-layouts  4.68 us
  transfers between devices with their start and end apart: 32, of which 19 were waited for; matrix products, arithmetic and copies ran while one was open for 2% of the time, Pallas kernels for 6%

profile of v14, /device:TPU:0, one launch (start us, length us, event | category | flops | bytes accessed | tf_op | source)
XLA Modules:
  0.0 156.1 jit_solution(193894023004298741)
XLA Ops:
  0.6 1.0 copy-done.6
  1.7 0.7 copy-done.7
  2.4 7.0 %spread.2 = (bf16[4,8,128,128]{3,2,1,0:T(8,128)(2,1)S(1)}, bf16[4,8,128,128]{3,2,1,0:T(8,128)(2,1)S(1)}, bf16[4,8,128,128]{3,2,1,0:T(8,128)(2,1)S(1)}, bf16[4,8,...) custom-call(s32[16,20]{1,0:T(8,128)S(1)} %copy-done.7, s32[1]{0:T(128)} %bitcast.me_ref.refs_4_, ...), custom_call_target="tpu_custom_call" | custom-call | flops 1342177280 | bytes 30000000 | tf_op jit(solution)/shard_map/spread/pallas_call | solution.py:107
  9.5 0.5 collective-permute-start
  10.1 2.2 %collective-permute-done = bf16[4,8,128,128]{3,2,1,0:T(8,128)(2,1)S(1)} collective-permute-done((bf16[4,8,128,128]{3,2,1,0:T(8,128)(2,1)S(1)}, bf16[4,8,128,128]{3,2,1,0:T(8,128)(2,1)S(1)}, u32[]{:S(2)}, u32[]{:S(2)}) %collective-permute-start) | collective-permute-done | bytes 1048608 | tf_op jit(solution)/shard_map/ppermute | solution.py:325
  12.3 0.5 add_convert_fusion.7
  12.7 3.0 %collective-permute-start.1 = (bf16[2,8,128,128]{3,2,1,0:T(8,128)(2,1)S(1)}, bf16[2,8,128,128]{3,2,1,0:T(8,128)(2,1)S(1)}, u32[]{:S(2)}, u32[]{:S(2)}) collective-permute-start(bf16[2,8,128,128]{3,2,1,0:T(8,128)(2,1)S(1)} %get-tuple-element.134), channel_id=1, source_target_pairs={{0,16},{4,20},{8,24},{12,28},{16,0},{20,4},{24,8},{28,12},{1,17},{... | collective-permute-start | bytes 1572872 | tf_op jit(solution)/shard_map/ppermute | solution.py:325
  15.7 0.3 add_convert_fusion.5
  16.0 1.6 collective-permute-start.4
  17.6 10.3 %collective-permute-done.1 = bf16[2,8,128,128]{3,2,1,0:T(8,128)(2,1)S(1)} collective-permute-done((bf16[2,8,128,128]{3,2,1,0:T(8,128)(2,1)S(1)}, bf16[2,8,128,128]{3,2,1,0:T(8,128)(2,1)S(1)}, u32[]{:S(2)}, u32[]{:S(2)}) %collective-permute-start.1) | collective-permute-done | bytes 524320 | tf_op jit(solution)/shard_map/ppermute | solution.py:325
  28.1 1.8 %collective-permute-start.2 = (bf16[8,128,128]{2,1,0:T(8,128)(2,1)S(1)}, bf16[8,128,128]{2,1,0:T(8,128)(2,1)S(1)}, u32[]{:S(2)}, u32[]{:S(2)}) collective-permute-start(bf16[8,128,128]{2,1,0:T(8,128)(2,1)S(1)} %get-tuple-element.141), channel_id=1, source_target_pairs={{0,8},{4,12},{8,0},{12,4},{16,24},{20,28},{24,16},{28,20},{1,9},{5... | collective-permute-start | bytes 786440 | tf_op jit(solution)/shard_map/ppermute | solution.py:325
  30.0 1.6 %collective-permute-start.5 = (bf16[8,128,128]{2,1,0:T(8,128)(2,1)S(1)}, bf16[8,128,128]{2,1,0:T(8,128)(2,1)S(1)}, u32[]{:S(2)}, u32[]{:S(2)}) collective-permute-start(bf16[8,128,128]{2,1,0:T(8,128)(2,1)S(1)} %get-tuple-element.139), channel_id=1, source_target_pairs={{0,16},{4,20},{8,24},{12,28},{16,0},{20,4},{24,8},{28,12},{1,17},{... | collective-permute-start | bytes 786440 | tf_op jit(solution)/shard_map/ppermute | solution.py:325
  31.6 4.4 %collective-permute-done.2.refs_1_ = bf16[8,128,128]{2,1,0:T(8,128)(2,1)S(1)} collective-permute-done((bf16[8,128,128]{2,1,0:T(8,128)(2,1)S(1)}, bf16[8,128,128]{2,1,0:T(8,128)(2,1)S(1)}, u32[]{:S(2)}, u32[]{:S(2)}) %collective-permute-start.2) | collective-permute-done | bytes 262176 | tf_op jit(solution)/shard_map/ppermute | solution.py:325
  36.0 1.3 collective-permute-done.5.refs_3_
  37.4 1.6 %collective-permute-start.8 = (bf16[16,128,128]{2,1,0:T(8,128)(2,1)S(1)}, bf16[16,128,128]{2,1,0:T(8,128)(2,1)S(1)}, u32[]{:S(2)}, u32[]{:S(2)}) collective-permute-start(bf16[16,128,128]{2,1,0:T(8,128)(2,1)S(1)} %finish.2.rest_0_), channel_id=1, source_target_pairs={{0,1},{1,0},{2,3},{3,2},{4,5},{5,4},{6,7},{7,6},{8,9},{9,8},{10,11... | collective-permute-start | bytes 1572872 | tf_op jit(solution)/shard_map/ppermute | solution.py:325
  39.1 2.5 %collective-permute-start.6 = (bf16[16,128,128]{2,1,0:T(8,128)(2,1)S(1)}, bf16[16,128,128]{2,1,0:T(8,128)(2,1)}, u32[]{:S(2)}, u32[]{:S(2)}) collective-permute-start(bf16[16,128,128]{2,1,0:T(8,128)(2,1)S(1)} %finish.2.rest_0_), channel_id=1, source_target_pairs={{0,3},{1,2},{2,1},{3,0},{4,7},{5,6},{6,5},{7,4},{8,11},{9,10},{10,... | collective-permute-start | bytes 1572872 | tf_op jit(solution)/shard_map/ppermute | solution.py:325
  41.5 2.4 %collective-permute-start.14 = (bf16[16,128,128]{2,1,0:T(8,128)(2,1)S(1)}, bf16[16,128,128]{2,1,0:T(8,128)(2,1)S(1)}, u32[]{:S(2)}, u32[]{:S(2)}) collective-permute-start(bf16[16,128,128]{2,1,0:T(8,128)(2,1)S(1)} %bitcast.87), channel_id=1, source_target_pairs={{0,24},{4,28},{8,16},{12,20},{16,8},{20,12},{24,0},{28,4},{1,25},{... | collective-permute-start | bytes 1572872 | tf_op jit(solution)/shard_map/ppermute | solution.py:325
  43.9 0.5 collective-permute-start.12
  44.4 0.6 collective-permute-start.10
  45.0 6.4 %collective-permute-done.8.rest_1_ = bf16[16,128,128]{2,1,0:T(8,128)(2,1)S(1)} collective-permute-done((bf16[16,128,128]{2,1,0:T(8,128)(2,1)S(1)}, bf16[16,128,128]{2,1,0:T(8,128)(2,1)S(1)}, u32[]{:S(2)}, u32[]{:S(2)}) %collective-permute-start.8) | collective-permute-done | bytes 524320 | tf_op jit(solution)/shard_map/ppermute | solution.py:325
  51.4 0.8 copy-done.2
  52.2 10.7 %collective-permute-done.6.rest_2_ = bf16[16,128,128]{2,1,0:T(8,128)(2,1)} collective-permute-done((bf16[16,128,128]{2,1,0:T(8,128)(2,1)S(1)}, bf16[16,128,128]{2,1,0:T(8,128)(2,1)}, u32[]{:S(2)}, u32[]{:S(2)}) %collective-permute-start.6) | collective-permute-done | bytes 524320 | tf_op jit(solution)/shard_map/ppermute | solution.py:325
  62.9 0.6 collective-permute-start.7
  63.5 1.6 %collective-permute-done.12.rest_4_ = bf16[16,128,128]{2,1,0:T(8,128)(2,1)S(1)} collective-permute-done((bf16[16,128,128]{2,1,0:T(8,128)(2,1)S(1)}, bf16[16,128,128]{2,1,0:T(8,128)(2,1)S(1)}, u32[]{:S(2)}, u32[]{:S(2)}) %collective-permute-start.12) | collective-permute-done | bytes 524320 | tf_op jit(solution)/shard_map/ppermute | solution.py:325
  65.1 0.4 collective-permute-start.11
  65.7 0.6 constant_dynamic-slice_fusion.3
  66.3 1.0 copy-done.3
  67.4 1.9 %dense_early.1 = (f32[2,128,1024]{2,1,0:T(8,128)S(1)}, f32[4,128,128]{2,1,0:T(8,128)S(1)}) custom-call(s32[1]{0:T(128)} %bitcast.1.col_ref, bf16[128,512]{1,0:T(8,128)(2,1)S(1)} %pad_maximum_fusion.1.weight_ref, bf16[16,128,128]{2,1,0:T(8,128)(2,1)S(1)} %finish.2.rest_0_, bf16[16,128,128]{2,1,0:T(8,128)(2,1)S(1)} %copy-done.3, ...), custom_call_target="tpu_custom_call" | custom-call | tf_op jit(solution)/shard_map/dense_early/pallas_call | solution.py:255
  69.3 4.9 %collective-permute-done.7.shard_ref = bf16[16,128,128]{2,1,0:T(8,128)(2,1)} collective-permute-done((bf16[16,128,128]{2,1,0:T(8,128)(2,1)}, bf16[16,128,128]{2,1,0:T(8,128)(2,1)}, u32[]{:S(2)}, u32[]{:S(2)}) %collective-permute-start.7) | collective-permute-done | bytes 524320 | tf_op jit(solution)/shard_map/ppermute | solution.py:325
  74.2 1.0 copy-done.5
  75.2 1.5 dense_late.1
  76.7 5.6 %collective-permute-start.17 = (bf16[8,128,128]{2,1,0:T(8,128)(2,1)S(1)}, bf16[8,128,128]{2,1,0:T(8,128)(2,1)S(1)}, u32[]{:S(2)}, u32[]{:S(2)}) collective-permute-start(bf16[8,128,128]{2,1,0:T(8,128)(2,1)S(1)} %get-tuple-element.88.rest_0_), channel_id=1, source_target_pairs={{0,3},{1,2},{2,1},{3,0},{4,7},{5,6},{6,5},{7,4},{8,11},{9,10},{10,... | collective-permute-start | bytes 786440 | tf_op jit(solution)/shard_map/ppermute | solution.py:325
  82.3 0.4 collective-permute-start.20
  82.7 1.7 %collective-permute-start.19 = (bf16[8,128,128]{2,1,0:T(8,128)(2,1)S(1)}, bf16[8,128,128]{2,1,0:T(8,128)(2,1)S(1)}, u32[]{:S(2)}, u32[]{:S(2)}) collective-permute-start(bf16[8,128,128]{2,1,0:T(8,128)(2,1)S(1)} %get-tuple-element.99.rest_0_), channel_id=1, source_target_pairs={{0,1},{1,0},{2,3},{3,2},{4,5},{5,4},{6,7},{7,6},{8,9},{9,8},{10,11... | collective-permute-start | bytes 786440 | tf_op jit(solution)/shard_map/ppermute | solution.py:325
  84.4 6.6 %aggregate.1 = bf16[16,128,128]{2,1,0:T(8,128)(2,1)S(1)} custom-call(s32[16,20]{1,0:T(8,128)S(1)} %copy-done.8, s32[1]{0:T(128)} %bitcast.me_ref.refs_4_, bf16[16,20,128,128]{3,2,1,0:T(8,128)(2,1)} %tiles_ref.5, bf16[16,128,128]{2,1,0:T(8,128)(2,1)S(1)} %bitcast.91, bf16[16,128,128]{2,1,0:T(8,128)(2,1)} %collective-permute-done.9.rest_1_, ...), custom_call_target="tpu_custom_call" | custom-call | flops 1342177280 | bytes 30000000 | tf_op jit(solution)/shard_map/aggregate/pallas_call | solution.py:149
  91.0 4.3 %collective-permute-done.16.rest_1_ = bf16[8,128,128]{2,1,0:T(8,128)(2,1)S(1)} collective-permute-done((bf16[8,128,128]{2,1,0:T(8,128)(2,1)S(1)}, bf16[8,128,128]{2,1,0:T(8,128)(2,1)S(1)}, u32[]{:S(2)}, u32[]{:S(2)}) %collective-permute-start.16) | collective-permute-done | bytes 262176 | tf_op jit(solution)/shard_map/ppermute | solution.py:325
  95.4 1.8 %collective-permute-start.18 = (bf16[8,128,128]{2,1,0:T(8,128)(2,1)S(1)}, bf16[8,128,128]{2,1,0:T(8,128)(2,1)S(1)}, u32[]{:S(2)}, u32[]{:S(2)}) collective-permute-start(bf16[8,128,128]{2,1,0:T(8,128)(2,1)S(1)} %collective-permute-done.17.rest_3_), channel_id=1, source_target_pairs={{0,1},{1,0},{2,3},{3,2},{4,5},{5,4},{6,7},{7,6},{8,9},{9,8},{10,11... | collective-permute-start | bytes 786440 | tf_op jit(solution)/shard_map/ppermute | solution.py:325
  97.2 3.7 %collective-permute-done.20.rest_3_ = bf16[8,128,128]{2,1,0:T(8,128)(2,1)S(1)} collective-permute-done((bf16[8,128,128]{2,1,0:T(8,128)(2,1)S(1)}, bf16[8,128,128]{2,1,0:T(8,128)(2,1)S(1)}, u32[]{:S(2)}, u32[]{:S(2)}) %collective-permute-start.20) | collective-permute-done | bytes 262176 | tf_op jit(solution)/shard_map/ppermute | solution.py:325
  100.9 3.2 %collective-permute-start.21 = (bf16[8,128,128]{2,1,0:T(8,128)(2,1)S(1)}, bf16[8,128,128]{2,1,0:T(8,128)(2,1)S(1)}, u32[]{:S(2)}, u32[]{:S(2)}) collective-permute-start(bf16[8,128,128]{2,1,0:T(8,128)(2,1)S(1)} %collective-permute-done.20.rest_3_), channel_id=1, source_target_pairs={{0,1},{1,0},{2,3},{3,2},{4,5},{5,4},{6,7},{7,6},{8,9},{9,8},{10,11... | collective-permute-start | bytes 786440 | tf_op jit(solution)/shard_map/ppermute | solution.py:325
  104.1 1.9 %collective-permute-done.19.rest_1_ = bf16[8,128,128]{2,1,0:T(8,128)(2,1)S(1)} collective-permute-done((bf16[8,128,128]{2,1,0:T(8,128)(2,1)S(1)}, bf16[8,128,128]{2,1,0:T(8,128)(2,1)S(1)}, u32[]{:S(2)}, u32[]{:S(2)}) %collective-permute-start.19) | collective-permute-done | bytes 262176 | tf_op jit(solution)/shard_map/ppermute | solution.py:325
  106.0 5.6 %collective-permute-done.18.rest_2_ = bf16[8,128,128]{2,1,0:T(8,128)(2,1)S(1)} collective-permute-done((bf16[8,128,128]{2,1,0:T(8,128)(2,1)S(1)}, bf16[8,128,128]{2,1,0:T(8,128)(2,1)S(1)}, u32[]{:S(2)}, u32[]{:S(2)}) %collective-permute-start.18) | collective-permute-done | bytes 262176 | tf_op jit(solution)/shard_map/ppermute | solution.py:325
  111.6 0.6 dense.2
  112.2 4.6 %collective-permute-done.21.rest_2_ = bf16[8,128,128]{2,1,0:T(8,128)(2,1)S(1)} collective-permute-done((bf16[8,128,128]{2,1,0:T(8,128)(2,1)S(1)}, bf16[8,128,128]{2,1,0:T(8,128)(2,1)S(1)}, u32[]{:S(2)}, u32[]{:S(2)}) %collective-permute-start.21) | collective-permute-done | bytes 262176 | tf_op jit(solution)/shard_map/ppermute | solution.py:325
  116.7 0.6 dense.3
  117.3 6.7 %spread.3 = (bf16[4,8,128,128]{3,2,1,0:T(8,128)(2,1)S(1)}, bf16[4,8,128,128]{3,2,1,0:T(8,128)(2,1)S(1)}, bf16[4,8,128,128]{3,2,1,0:T(8,128)(2,1)S(1)}, bf16[4,8,128,128]{3,2,1,0:T(8,128)(2,1)S(1)}) custom-call(s32[16,20]{1,0:T(8,128)S(1)} %copy-done.8, s32[1]{0:T(128)} %bitcast.me_ref.refs_4_, bf16[16,20,128,128]{3,2,1,0:T(8,128)(2,1)} %tiles_ref.5, ...), custom_call_target="tpu_custom_call" | custom-call | flops 1342177280 | bytes 30000000 | tf_op jit(solution)/shard_map/spread/pallas_call | solution.py:107
  124.1 0.5 collective-permute-start.23
  124.6 0.2 weight_terms.1
  124.8 0.1 collective-permute-start.24
  124.9 1.8 %collective-permute-done.22 = bf16[4,8,128,128]{3,2,1,0:T(8,128)(2,1)S(1)} collective-permute-done((bf16[4,8,128,128]{3,2,1,0:T(8,128)(2,1)S(1)}, bf16[4,8,128,128]{3,2,1,0:T(8,128)(2,1)S(1)}, u32[]{:S(2)}, u32[]{:S(2)}) %collective-permute-start.22) | collective-permute-done | bytes 1048608 | tf_op jit(solution)/shard_map/ppermute | solution.py:325
  126.7 0.4 add_convert_fusion.3
  127.1 1.6 %collective-permute-start.25 = (bf16[2,8,128,128]{3,2,1,0:T(8,128)(2,1)S(1)}, bf16[2,8,128,128]{3,2,1,0:T(8,128)(2,1)S(1)}, u32[]{:S(2)}, u32[]{:S(2)}) collective-permute-start(bf16[2,8,128,128]{3,2,1,0:T(8,128)(2,1)S(1)} %get-tuple-element.130), channel_id=1, source_target_pairs={{0,16},{4,20},{8,24},{12,28},{16,0},{20,4},{24,8},{28,12},{1,17},{... | collective-permute-start | bytes 1572872 | tf_op jit(solution)/shard_map/ppermute | solution.py:325
  128.7 0.4 fusion.1
  129.1 1.8 %collective-permute-start.26 = (bf16[2,8,128,128]{3,2,1,0:T(8,128)(2,1)S(1)}, bf16[2,8,128,128]{3,2,1,0:T(8,128)(2,1)S(1)}, u32[]{:S(2)}, u32[]{:S(2)}) collective-permute-start(bf16[2,8,128,128]{3,2,1,0:T(8,128)(2,1)S(1)} %get-tuple-element.128), channel_id=1, source_target_pairs={{0,8},{4,12},{8,0},{12,4},{16,24},{20,28},{24,16},{28,20},{1,9},{5... | collective-permute-start | bytes 1572872 | tf_op jit(solution)/shard_map/ppermute | solution.py:325
  130.9 1.1 collective-permute-start.27
  132.0 11.9 %collective-permute-done.27 = bf16[128,512]{1,0:T(8,128)(2,1)S(1)} collective-permute-done((bf16[128,512]{1,0:T(8,128)(2,1)S(1)}, bf16[128,512]{1,0:T(8,128)(2,1)S(1)}, u32[]{:S(2)}, u32[]{:S(2)}) %collective-permute-start.27) | collective-permute-done | bytes 131104 | tf_op jit(solution)/shard_map/ppermute | solution.py:325
  144.0 0.1 fusion.9
  144.2 0.1 fusion.10
  144.3 1.6 collective-permute-start.30
  145.9 1.7 %collective-permute-start.29 = (bf16[8,128,128]{2,1,0:T(8,128)(2,1)S(1)}, bf16[8,128,128]{2,1,0:T(8,128)(2,1)S(1)}, u32[]{:S(2)}, u32[]{:S(2)}) collective-permute-start(bf16[8,128,128]{2,1,0:T(8,128)(2,1)S(1)} %get-tuple-element.135), channel_id=1, source_target_pairs={{0,16},{4,20},{8,24},{12,28},{16,0},{20,4},{24,8},{28,12},{1,17},{... | collective-permute-start | bytes 786440 | tf_op jit(solution)/shard_map/ppermute | solution.py:325
  147.6 0.3 collective-permute-start.28
  147.9 1.9 %collective-permute-done.30 = bf16[128,512]{1,0:T(8,128)(2,1)S(1)} collective-permute-done((bf16[128,512]{1,0:T(8,128)(2,1)S(1)}, bf16[128,512]{1,0:T(8,128)(2,1)S(1)}, u32[]{:S(2)}, u32[]{:S(2)}) %collective-permute-start.30) | collective-permute-done | bytes 131104 | tf_op jit(solution)/shard_map/ppermute | solution.py:325
  149.9 3.3 %collective-permute-done.29.refs_3_ = bf16[8,128,128]{2,1,0:T(8,128)(2,1)S(1)} collective-permute-done((bf16[8,128,128]{2,1,0:T(8,128)(2,1)S(1)}, bf16[8,128,128]{2,1,0:T(8,128)(2,1)S(1)}, u32[]{:S(2)}, u32[]{:S(2)}) %collective-permute-start.29) | collective-permute-done | bytes 262176 | tf_op jit(solution)/shard_map/ppermute | solution.py:325
  153.3 1.7 %collective-permute-done.28.refs_1_ = bf16[8,128,128]{2,1,0:T(8,128)(2,1)S(1)} collective-permute-done((bf16[8,128,128]{2,1,0:T(8,128)(2,1)S(1)}, bf16[8,128,128]{2,1,0:T(8,128)(2,1)S(1)}, u32[]{:S(2)}, u32[]{:S(2)}) %collective-permute-start.28) | collective-permute-done | bytes 262176 | tf_op jit(solution)/shard_map/ppermute | solution.py:325
  155.0 1.2 finish.3
  (57 shorter events, 1.1 us)
Async XLA Ops:
  0.6 1.0 copy-start.6
  1.7 0.7 copy-start.7
  2.4 39.1 %copy-start.1 = (bf16[2048,128]{1,0:T(8,128)(2,1)S(1)}, bf16[2048,128]{1,0:T(8,128)(2,1)}, u32[]{:S(2)}) copy-start(bf16[2048,128]{1,0:T(8,128)(2,1)} %param.8) | copy-start | bytes 1572868
  2.4 63.2 %copy-start.9 = (bf16[128,512]{1,0:T(8,128)(2,1)S(1)}, bf16[128,512]{1,0:T(8,128)(2,1)}, u32[]{:S(2)}) copy-start(bf16[128,512]{1,0:T(8,128)(2,1)} %param.14) | copy-start | bytes 393220
  2.4 63.2 %copy-start.10 = (bf16[128,512]{1,0:T(8,128)(2,1)S(1)}, bf16[128,512]{1,0:T(8,128)(2,1)}, u32[]{:S(2)}) copy-start(bf16[128,512]{1,0:T(8,128)(2,1)} %param.15) | copy-start | bytes 393220
  2.4 63.9 %copy-start = (bf16[2048,128]{1,0:T(8,128)(2,1)S(1)}, bf16[2048,128]{1,0:T(8,128)(2,1)}, u32[]{:S(2)}) copy-start(bf16[2048,128]{1,0:T(8,128)(2,1)} %param.9) | copy-start | bytes 1572868
  9.4 55.7 %copy-start.4 = (bf16[16,128,128]{2,1,0:T(8,128)(2,1)}, bf16[16,128,128]{2,1,0:T(8,128)(2,1)S(1)}, u32[]{:S(2)}) copy-start(bf16[16,128,128]{2,1,0:T(8,128)(2,1)S(1)} %get-tuple-element.78.mask_ref) | copy-start | bytes 1572868
  9.4 75.0 %copy-start.8 = (s32[16,20]{1,0:T(8,128)S(1)}, s32[16,20]{1,0:T(8,128)}, u32[]{:S(2)}) copy-start(s32[16,20]{1,0:T(8,128)} %cols_ref.5) | copy-start | bytes 3844
  9.5 2.8 %collective-permute-start = (bf16[4,8,128,128]{3,2,1,0:T(8,128)(2,1)S(1)}, bf16[4,8,128,128]{3,2,1,0:T(8,128)(2,1)S(1)}, u32[]{:S(2)}, u32[]{:S(2)}) collective-permute-start(bf16[4,8,128,128]{3,2,1,0:T(8,128)(2,1)S(1)} %get-tuple-element.66), channel_id=1, source_target_pairs={{0,4},{4,0},{8,12},{12,8},{16,20},{20,16},{24,28},{28,24},{1,5},{5... | collective-permute-start | bytes 3145736 | tf_op jit(solution)/shard_map/ppermute | solution.py:325
  10.0 5.7 %collective-permute-start.3 = (bf16[4,8,128,128]{3,2,1,0:T(8,128)(2,1)S(1)}, bf16[4,8,128,128]{3,2,1,0:T(8,128)(2,1)S(1)}, u32[]{:S(2)}, u32[]{:S(2)}) collective-permute-start(bf16[4,8,128,128]{3,2,1,0:T(8,128)(2,1)S(1)} %get-tuple-element.68), channel_id=1, source_target_pairs={{0,4},{4,0},{8,12},{12,8},{16,20},{20,16},{24,28},{28,24},{1,5},{5... | collective-permute-start | bytes 3145736 | tf_op jit(solution)/shard_map/ppermute | solution.py:325
  12.7 15.2 %collective-permute-start.1 = (bf16[2,8,128,128]{3,2,1,0:T(8,128)(2,1)S(1)}, bf16[2,8,128,128]{3,2,1,0:T(8,128)(2,1)S(1)}, u32[]{:S(2)}, u32[]{:S(2)}) collective-permute-start(bf16[2,8,128,128]{3,2,1,0:T(8,128)(2,1)S(1)} %get-tuple-element.134), channel_id=1, source_target_pairs={{0,16},{4,20},{8,24},{12,28},{16,0},{20,4},{24,8},{28,12},{1,17},{... | collective-permute-start | bytes 1572872 | tf_op jit(solution)/shard_map/ppermute | solution.py:325
  16.0 13.8 %collective-permute-start.4 = (bf16[2,8,128,128]{3,2,1,0:T(8,128)(2,1)S(1)}, bf16[2,8,128,128]{3,2,1,0:T(8,128)(2,1)S(1)}, u32[]{:S(2)}, u32[]{:S(2)}) collective-permute-start(bf16[2,8,128,128]{3,2,1,0:T(8,128)(2,1)S(1)} %get-tuple-element.132), channel_id=1, source_target_pairs={{0,8},{4,12},{8,0},{12,4},{16,24},{20,28},{24,16},{28,20},{1,9},{5... | collective-permute-start | bytes 1572872 | tf_op jit(solution)/shard_map/ppermute | solution.py:325
  28.1 7.9 %collective-permute-start.2 = (bf16[8,128,128]{2,1,0:T(8,128)(2,1)S(1)}, bf16[8,128,128]{2,1,0:T(8,128)(2,1)S(1)}, u32[]{:S(2)}, u32[]{:S(2)}) collective-permute-start(bf16[8,128,128]{2,1,0:T(8,128)(2,1)S(1)} %get-tuple-element.141), channel_id=1, source_target_pairs={{0,8},{4,12},{8,0},{12,4},{16,24},{20,28},{24,16},{28,20},{1,9},{5... | collective-permute-start | bytes 786440 | tf_op jit(solution)/shard_map/ppermute | solution.py:325
  30.0 7.3 %collective-permute-start.5 = (bf16[8,128,128]{2,1,0:T(8,128)(2,1)S(1)}, bf16[8,128,128]{2,1,0:T(8,128)(2,1)S(1)}, u32[]{:S(2)}, u32[]{:S(2)}) collective-permute-start(bf16[8,128,128]{2,1,0:T(8,128)(2,1)S(1)} %get-tuple-element.139), channel_id=1, source_target_pairs={{0,16},{4,20},{8,24},{12,28},{16,0},{20,4},{24,8},{28,12},{1,17},{... | collective-permute-start | bytes 786440 | tf_op jit(solution)/shard_map/ppermute | solution.py:325
  37.4 14.0 %collective-permute-start.8 = (bf16[16,128,128]{2,1,0:T(8,128)(2,1)S(1)}, bf16[16,128,128]{2,1,0:T(8,128)(2,1)S(1)}, u32[]{:S(2)}, u32[]{:S(2)}) collective-permute-start(bf16[16,128,128]{2,1,0:T(8,128)(2,1)S(1)} %finish.2.rest_0_), channel_id=1, source_target_pairs={{0,1},{1,0},{2,3},{3,2},{4,5},{5,4},{6,7},{7,6},{8,9},{9,8},{10,11... | collective-permute-start | bytes 1572872 | tf_op jit(solution)/shard_map/ppermute | solution.py:325
  39.1 23.8 %collective-permute-start.6 = (bf16[16,128,128]{2,1,0:T(8,128)(2,1)S(1)}, bf16[16,128,128]{2,1,0:T(8,128)(2,1)}, u32[]{:S(2)}, u32[]{:S(2)}) collective-permute-start(bf16[16,128,128]{2,1,0:T(8,128)(2,1)S(1)} %finish.2.rest_0_), channel_id=1, source_target_pairs={{0,3},{1,2},{2,1},{3,0},{4,7},{5,6},{6,5},{7,4},{8,11},{9,10},{10,... | collective-permute-start | bytes 1572872 | tf_op jit(solution)/shard_map/ppermute | solution.py:325
  41.5 21.9 %collective-permute-start.14 = (bf16[16,128,128]{2,1,0:T(8,128)(2,1)S(1)}, bf16[16,128,128]{2,1,0:T(8,128)(2,1)S(1)}, u32[]{:S(2)}, u32[]{:S(2)}) collective-permute-start(bf16[16,128,128]{2,1,0:T(8,128)(2,1)S(1)} %bitcast.87), channel_id=1, source_target_pairs={{0,24},{4,28},{8,16},{12,20},{16,8},{20,12},{24,0},{28,4},{1,25},{... | collective-permute-start | bytes 1572872 | tf_op jit(solution)/shard_map/ppermute | solution.py:325
  43.9 21.1 %collective-permute-start.12 = (bf16[16,128,128]{2,1,0:T(8,128)(2,1)S(1)}, bf16[16,128,128]{2,1,0:T(8,128)(2,1)S(1)}, u32[]{:S(2)}, u32[]{:S(2)}) collective-permute-start(bf16[16,128,128]{2,1,0:T(8,128)(2,1)S(1)} %bitcast.88), channel_id=1, source_target_pairs={{0,16},{4,20},{8,24},{12,28},{16,0},{20,4},{24,8},{28,12},{1,17},{... | collective-permute-start | bytes 1572872 | tf_op jit(solution)/shard_map/ppermute | solution.py:325
  44.4 20.8 %collective-permute-start.10 = (bf16[16,128,128]{2,1,0:T(8,128)(2,1)S(1)}, bf16[16,128,128]{2,1,0:T(8,128)(2,1)S(1)}, u32[]{:S(2)}, u32[]{:S(2)}) collective-permute-start(bf16[16,128,128]{2,1,0:T(8,128)(2,1)S(1)} %bitcast.89), channel_id=1, source_target_pairs={{0,8},{4,12},{8,0},{12,4},{16,24},{20,28},{24,16},{28,20},{1,9},{5... | collective-permute-start | bytes 1572872 | tf_op jit(solution)/shard_map/ppermute | solution.py:325
  51.4 0.8 copy-start.2
  52.2 17.1 %collective-permute-start.9 = (bf16[16,128,128]{2,1,0:T(8,128)(2,1)S(1)}, bf16[16,128,128]{2,1,0:T(8,128)(2,1)}, u32[]{:S(2)}, u32[]{:S(2)}) collective-permute-start(bf16[16,128,128]{2,1,0:T(8,128)(2,1)S(1)} %bitcast.90), channel_id=1, source_target_pairs={{0,4},{4,0},{8,12},{12,8},{16,20},{20,16},{24,28},{28,24},{1,5},{5... | collective-permute-start | bytes 1572872 | tf_op jit(solution)/shard_map/ppermute | solution.py:325
  62.9 11.3 %collective-permute-start.7 = (bf16[16,128,128]{2,1,0:T(8,128)(2,1)}, bf16[16,128,128]{2,1,0:T(8,128)(2,1)}, u32[]{:S(2)}, u32[]{:S(2)}) collective-permute-start(bf16[16,128,128]{2,1,0:T(8,128)(2,1)} %collective-permute-done.6.rest_2_), channel_id=1, source_target_pairs={{0,1},{1,0},{2,3},{3,2},{4,5},{5,4},{6,7},{7,6},{8,9},{9,8},{10,11... | collective-permute-start | bytes 1572872 | tf_op jit(solution)/shard_map/ppermute | solution.py:325
  63.5 10.7 %collective-permute-start.15 = (bf16[16,128,128]{2,1,0:T(8,128)(2,1)S(1)}, bf16[16,128,128]{2,1,0:T(8,128)(2,1)}, u32[]{:S(2)}, u32[]{:S(2)}) collective-permute-start(bf16[16,128,128]{2,1,0:T(8,128)(2,1)S(1)} %collective-permute-done.14.rest_6_), channel_id=1, source_target_pairs={{0,4},{4,0},{8,12},{12,8},{16,20},{20,16},{24,28},{28,24},{1,5},{5... | collective-permute-start | bytes 1572872 | tf_op jit(solution)/shard_map/ppermute | solution.py:325
  65.1 9.1 %collective-permute-start.13 = (bf16[16,128,128]{2,1,0:T(8,128)(2,1)S(1)}, bf16[16,128,128]{2,1,0:T(8,128)(2,1)}, u32[]{:S(2)}, u32[]{:S(2)}) collective-permute-start(bf16[16,128,128]{2,1,0:T(8,128)(2,1)S(1)} %collective-permute-done.12.rest_4_), channel_id=1, source_target_pairs={{0,4},{4,0},{8,12},{12,8},{16,20},{20,16},{24,28},{28,24},{1,5},{5... | collective-permute-start | bytes 1572872 | tf_op jit(solution)/shard_map/ppermute | solution.py:325
  65.1 9.0 %collective-permute-start.11 = (bf16[16,128,128]{2,1,0:T(8,128)(2,1)S(1)}, bf16[16,128,128]{2,1,0:T(8,128)(2,1)}, u32[]{:S(2)}, u32[]{:S(2)}) collective-permute-start(bf16[16,128,128]{2,1,0:T(8,128)(2,1)S(1)} %collective-permute-done.10.rest_2_), channel_id=1, source_target_pairs={{0,4},{4,0},{8,12},{12,8},{16,20},{20,16},{24,28},{28,24},{1,5},{5... | collective-permute-start | bytes 1572872 | tf_op jit(solution)/shard_map/ppermute | solution.py:325
  66.3 1.0 copy-start.3
  74.2 1.0 copy-start.5
  76.7 14.3 %collective-permute-start.17 = (bf16[8,128,128]{2,1,0:T(8,128)(2,1)S(1)}, bf16[8,128,128]{2,1,0:T(8,128)(2,1)S(1)}, u32[]{:S(2)}, u32[]{:S(2)}) collective-permute-start(bf16[8,128,128]{2,1,0:T(8,128)(2,1)S(1)} %get-tuple-element.88.rest_0_), channel_id=1, source_target_pairs={{0,3},{1,2},{2,1},{3,0},{4,7},{5,6},{6,5},{7,4},{8,11},{9,10},{10,... | collective-permute-start | bytes 786440 | tf_op jit(solution)/shard_map/ppermute | solution.py:325
  82.3 13.0 %collective-permute-start.16 = (bf16[8,128,128]{2,1,0:T(8,128)(2,1)S(1)}, bf16[8,128,128]{2,1,0:T(8,128)(2,1)S(1)}, u32[]{:S(2)}, u32[]{:S(2)}) collective-permute-start(bf16[8,128,128]{2,1,0:T(8,128)(2,1)S(1)} %get-tuple-element.88.rest_0_), channel_id=1, source_target_pairs={{0,1},{1,0},{2,3},{3,2},{4,5},{5,4},{6,7},{7,6},{8,9},{9,8},{10,11... | collective-permute-start | bytes 786440 | tf_op jit(solution)/shard_map/ppermute | solution.py:325
  82.3 18.5 %collective-permute-start.20 = (bf16[8,128,128]{2,1,0:T(8,128)(2,1)S(1)}, bf16[8,128,128]{2,1,0:T(8,128)(2,1)S(1)}, u32[]{:S(2)}, u32[]{:S(2)}) collective-permute-start(bf16[8,128,128]{2,1,0:T(8,128)(2,1)S(1)} %get-tuple-element.99.rest_0_), channel_id=1, source_target_pairs={{0,3},{1,2},{2,1},{3,0},{4,7},{5,6},{6,5},{7,4},{8,11},{9,10},{10,... | collective-permute-start | bytes 786440 | tf_op jit(solution)/shard_map/ppermute | solution.py:325
  82.7 23.3 %collective-permute-start.19 = (bf16[8,128,128]{2,1,0:T(8,128)(2,1)S(1)}, bf16[8,128,128]{2,1,0:T(8,128)(2,1)S(1)}, u32[]{:S(2)}, u32[]{:S(2)}) collective-permute-start(bf16[8,128,128]{2,1,0:T(8,128)(2,1)S(1)} %get-tuple-element.99.rest_0_), channel_id=1, source_target_pairs={{0,1},{1,0},{2,3},{3,2},{4,5},{5,4},{6,7},{7,6},{8,9},{9,8},{10,11... | collective-permute-start | bytes 786440 | tf_op jit(solution)/shard_map/ppermute | solution.py:325
  95.4 16.2 %collective-permute-start.18 = (bf16[8,128,128]{2,1,0:T(8,128)(2,1)S(1)}, bf16[8,128,128]{2,1,0:T(8,128)(2,1)S(1)}, u32[]{:S(2)}, u32[]{:S(2)}) collective-permute-start(bf16[8,128,128]{2,1,0:T(8,128)(2,1)S(1)} %collective-permute-done.17.rest_3_), channel_id=1, source_target_pairs={{0,1},{1,0},{2,3},{3,2},{4,5},{5,4},{6,7},{7,6},{8,9},{9,8},{10,11... | collective-permute-start | bytes 786440 | tf_op jit(solution)/shard_map/ppermute | solution.py:325
  100.9 15.9 %collective-permute-start.21 = (bf16[8,128,128]{2,1,0:T(8,128)(2,1)S(1)}, bf16[8,128,128]{2,1,0:T(8,128)(2,1)S(1)}, u32[]{:S(2)}, u32[]{:S(2)}) collective-permute-start(bf16[8,128,128]{2,1,0:T(8,128)(2,1)S(1)} %collective-permute-done.20.rest_3_), channel_id=1, source_target_pairs={{0,1},{1,0},{2,3},{3,2},{4,5},{5,4},{6,7},{7,6},{8,9},{9,8},{10,11... | collective-permute-start | bytes 786440 | tf_op jit(solution)/shard_map/ppermute | solution.py:325
  124.0 2.7 %collective-permute-start.22 = (bf16[4,8,128,128]{3,2,1,0:T(8,128)(2,1)S(1)}, bf16[4,8,128,128]{3,2,1,0:T(8,128)(2,1)S(1)}, u32[]{:S(2)}, u32[]{:S(2)}) collective-permute-start(bf16[4,8,128,128]{3,2,1,0:T(8,128)(2,1)S(1)} %get-tuple-element.106), channel_id=1, source_target_pairs={{0,4},{4,0},{8,12},{12,8},{16,20},{20,16},{24,28},{28,24},{1,5},{5... | collective-permute-start | bytes 3145736 | tf_op jit(solution)/shard_map/ppermute | solution.py:325
  124.1 4.6 %collective-permute-start.23 = (bf16[4,8,128,128]{3,2,1,0:T(8,128)(2,1)S(1)}, bf16[4,8,128,128]{3,2,1,0:T(8,128)(2,1)S(1)}, u32[]{:S(2)}, u32[]{:S(2)}) collective-permute-start(bf16[4,8,128,128]{3,2,1,0:T(8,128)(2,1)S(1)} %get-tuple-element.108), channel_id=1, source_target_pairs={{0,4},{4,0},{8,12},{12,8},{16,20},{20,16},{24,28},{28,24},{1,5},{5... | collective-permute-start | bytes 3145736 | tf_op jit(solution)/shard_map/ppermute | solution.py:325
  124.8 6.1 %collective-permute-start.24 = (bf16[128,512]{1,0:T(8,128)(2,1)S(1)}, bf16[128,512]{1,0:T(8,128)(2,1)S(1)}, u32[]{:S(2)}, u32[]{:S(2)}) collective-permute-start(bf16[128,512]{1,0:T(8,128)(2,1)S(1)} %get-tuple-element.114), channel_id=1, source_target_pairs={{0,4},{4,0},{8,12},{12,8},{16,20},{20,16},{24,28},{28,24},{1,5},{5... | collective-permute-start | bytes 393224 | tf_op jit(solution)/shard_map/ppermute | solution.py:325
  127.1 16.9 %collective-permute-start.25 = (bf16[2,8,128,128]{3,2,1,0:T(8,128)(2,1)S(1)}, bf16[2,8,128,128]{3,2,1,0:T(8,128)(2,1)S(1)}, u32[]{:S(2)}, u32[]{:S(2)}) collective-permute-start(bf16[2,8,128,128]{3,2,1,0:T(8,128)(2,1)S(1)} %get-tuple-element.130), channel_id=1, source_target_pairs={{0,16},{4,20},{8,24},{12,28},{16,0},{20,4},{24,8},{28,12},{1,17},{... | collective-permute-start | bytes 1572872 | tf_op jit(solution)/shard_map/ppermute | solution.py:325
  129.1 14.9 %collective-permute-start.26 = (bf16[2,8,128,128]{3,2,1,0:T(8,128)(2,1)S(1)}, bf16[2,8,128,128]{3,2,1,0:T(8,128)(2,1)S(1)}, u32[]{:S(2)}, u32[]{:S(2)}) collective-permute-start(bf16[2,8,128,128]{3,2,1,0:T(8,128)(2,1)S(1)} %get-tuple-element.128), channel_id=1, source_target_pairs={{0,8},{4,12},{8,0},{12,4},{16,24},{20,28},{24,16},{28,20},{1,9},{5... | collective-permute-start | bytes 1572872 | tf_op jit(solution)/shard_map/ppermute | solution.py:325
  130.9 13.1 %collective-permute-start.27 = (bf16[128,512]{1,0:T(8,128)(2,1)S(1)}, bf16[128,512]{1,0:T(8,128)(2,1)S(1)}, u32[]{:S(2)}, u32[]{:S(2)}) collective-permute-start(bf16[128,512]{1,0:T(8,128)(2,1)S(1)} %convert_add_fusion.4), channel_id=1, source_target_pairs={{0,16},{4,20},{8,24},{12,28},{16,0},{20,4},{24,8},{28,12},{1,17},{... | collective-permute-start | bytes 393224 | tf_op jit(solution)/shard_map/ppermute | solution.py:325
  144.3 5.5 %collective-permute-start.30 = (bf16[128,512]{1,0:T(8,128)(2,1)S(1)}, bf16[128,512]{1,0:T(8,128)(2,1)S(1)}, u32[]{:S(2)}, u32[]{:S(2)}) collective-permute-start(bf16[128,512]{1,0:T(8,128)(2,1)S(1)} %convert_add_fusion.3), channel_id=1, source_target_pairs={{0,8},{4,12},{8,0},{12,4},{16,24},{20,28},{24,16},{28,20},{1,9},{5... | collective-permute-start | bytes 393224 | tf_op jit(solution)/shard_map/ppermute | solution.py:325
  145.9 7.4 %collective-permute-start.29 = (bf16[8,128,128]{2,1,0:T(8,128)(2,1)S(1)}, bf16[8,128,128]{2,1,0:T(8,128)(2,1)S(1)}, u32[]{:S(2)}, u32[]{:S(2)}) collective-permute-start(bf16[8,128,128]{2,1,0:T(8,128)(2,1)S(1)} %get-tuple-element.135), channel_id=1, source_target_pairs={{0,16},{4,20},{8,24},{12,28},{16,0},{20,4},{24,8},{28,12},{1,17},{... | collective-permute-start | bytes 786440 | tf_op jit(solution)/shard_map/ppermute | solution.py:325
  147.6 7.4 %collective-permute-start.28 = (bf16[8,128,128]{2,1,0:T(8,128)(2,1)S(1)}, bf16[8,128,128]{2,1,0:T(8,128)(2,1)S(1)}, u32[]{:S(2)}, u32[]{:S(2)}) collective-permute-start(bf16[8,128,128]{2,1,0:T(8,128)(2,1)S(1)} %get-tuple-element.137), channel_id=1, source_target_pairs={{0,8},{4,12},{8,0},{12,4},{16,24},{20,28},{24,16},{28,20},{1,9},{5... | collective-permute-start | bytes 786440 | tf_op jit(solution)/shard_map/ppermute | solution.py:325
  149.9 5.1 %collective-permute-start.31 = (f32[128,512]{1,0:T(8,128)S(1)}, f32[128,512]{1,0:T(8,128)S(1)}, u32[]{:S(2)}, u32[]{:S(2)}) collective-permute-start(f32[128,512]{1,0:T(8,128)S(1)} %convert_add_fusion.2.refs_5_), channel_id=1, source_target_pairs={{0,4},{4,0},{8,12},{12,8},{16,20},{20,16},{24,28},{28,24},{1,5},{5... | collective-permute-start | bytes 786440 | tf_op jit(solution)/shard_map/ppermute | solution.py:325

commit v15 on v14

--- a/solution.py
+++ b/solution.py
@@ -69,7 +69,7 @@
             pair = jnp.concatenate([held[r, k], held[r, k + 1]], axis=1)
             both = jnp.dot(left, pair, preferred_element_type=F32)
             for side in range(2):
-                acc[cols_ref[r, k + side]] += both[:, side * size : (side + 1) * size]
+                acc[cols_ref[r * per_row + k + side]] += both[:, side * size : (side + 1) * size]
 
     over_rows(tiles_ref, held, sems, one_row)
     halves, count = outs[0].shape[:2]
@@ -134,7 +134,8 @@
         total = None
         for k in range(0, per_row, 2):
             pair = jnp.concatenate([held[r, k], held[r, k + 1]], axis=1)
-            picked = jnp.concatenate([table[cols_ref[r, k]], table[cols_ref[r, k + 1]]], axis=0)
+            at = r * per_row + k
+            picked = jnp.concatenate([table[cols_ref[at]], table[cols_ref[at + 1]]], axis=0)
             term = jnp.dot(pair, picked, preferred_element_type=F32)
             total = term if total is None else total + term
         out_ref[r] = total.astype(BF16)
@@ -360,7 +361,7 @@
     if cols == 4:
         near, far = swap(own, 1, "col"), swap(own, 3, "col")
         if tied:
-            near, far, beside = lax.optimization_barrier((near, far, beside))
+            far, near, beside = lax.optimization_barrier((far, near, beside))
         else:
             near, beside = lax.optimization_barrier((near, beside))
         return [own, near, swap(far, 1, "col"), far], beside
@@ -384,6 +385,7 @@
         order = [lax.dynamic_index_in_dim(split, col ^ m, 1, keepdims=False) for m in range(cols)]
         return jnp.concatenate(order, axis=1)
 
+    block_cols = block_cols.reshape(-1)
     *pieces, mask = spread(edge_tiles, block_cols, [blocked(grad_out)], me_at, rows, blocked(relu_mask))
     terms, _ = scatter(pieces, rows)
     own, node_feats = after((finish(terms)[0], blocked(node_feats)))
@@ -402,10 +404,9 @@
     inputs, firsts = [], []
     shards = []
     for g in range(GROUPS):
-        arrived, beside = gather_columns(deltas[g], cols, agg_feats if g == 0 else (), g == 0)
+        arrived, beside = gather_columns(deltas[g], cols, agg_feats if g == 0 else ())
         agg_feats = beside if g == 0 else agg_feats
         shards.append(arrived)
-    shards[0][2], shards[1][1] = after((shards[0][2], shards[1][1]))
     for g in range(GROUPS):
         out, grad = dense(weight_one, shards[g], cut(agg_feats, g), None, col_at, 1)
         inputs.append(out)

time: 157 us -> 153 us (0.975)
  starting transfers between devices: 38.6 us -> 34.5 us
    ppermute x32, starting transfers between devices: 38.6 us -> 34.5 us  [swap(): lax.ppermute(value, axis, [(i, i ^ mask) for i in range(lax.axis_size(axi...]
    unnamed x30 -> x26, local copies, waits for them, and re-layouts: 4.68 us -> 3.98 us
  transfers between devices with their start and end apart: 32 -> 32, of which waited for: 19 -> 18; matrix products, arithmetic and copies ran while one was open for 2% -> 2% of each run, Pallas kernels for 6% -> 6%
where the time goes in v15:
time: 153 us; the launch traced here: 152 us
  waiting for transfers between devices  83.2 us (54%)
  starting transfers between devices  34.5 us (23%)
  Pallas kernels  26 us (17%)
  local copies, waits for them, and re-layouts  5.42 us (4%)
  other arithmetic  2.17 us (1%)
    ppermute x32, waiting for transfers between devices, swap(): lax.ppermute(value, axis, [(i, i ^ mask) for i in range(lax.axis_size(axi...  83.2 us
    ppermute x32, starting transfers between devices, swap(): lax.ppermute(value, axis, [(i, i ^ mask) for i in range(lax.axis_size(axi...  34.5 us
    pallas_call x2, Pallas kernels, spread(): pl.pallas_call(functools.partial(spread_kernel, first, len(vals)), out_sh...  13.5 us
    pallas_call x1, Pallas kernels, aggregate(): pl.pallas_call(aggregate_kernel, out_shape=jax.ShapeDtypeStruct((blocks,...  6.49 us
    unnamed x26, local copies, waits for them, and re-layouts  3.98 us
  transfers between devices with their start and end apart: 32, of which 18 were waited for; matrix products, arithmetic and copies ran while one was open for 2% of the time, Pallas kernels for 6%

profile of v15, /device:TPU:0, one launch (start us, length us, event | category | flops | bytes accessed | tf_op | source)
XLA Modules:
  0.0 152.3 jit_solution(9306712156957056251)
XLA Ops:
  0.6 0.8 reshape.122.cols_ref
  1.4 1.0 copy-done.1
  2.5 6.9 %spread.2 = (bf16[4,8,128,128]{3,2,1,0:T(8,128)(2,1)S(1)}, bf16[4,8,128,128]{3,2,1,0:T(8,128)(2,1)S(1)}, bf16[4,8,128,128]{3,2,1,0:T(8,128)(2,1)S(1)}, bf16[4,8,...) custom-call(s32[320]{0:T(512)S(1)} %reshape.122.cols_ref, s32[1]{0:T(128)} %bitcast.me_ref.refs_4_, ...), custom_call_target="tpu_custom_call" | custom-call | flops 1342177280 | bytes 30000000 | tf_op jit(solution)/shard_map/spread/pallas_call | solution.py:107
  9.4 0.5 collective-permute-start
  10.0 2.2 %collective-permute-done = bf16[4,8,128,128]{3,2,1,0:T(8,128)(2,1)S(1)} collective-permute-done((bf16[4,8,128,128]{3,2,1,0:T(8,128)(2,1)S(1)}, bf16[4,8,128,128]{3,2,1,0:T(8,128)(2,1)S(1)}, u32[]{:S(2)}, u32[]{:S(2)}) %collective-permute-start) | collective-permute-done | bytes 1048608 | tf_op jit(solution)/shard_map/ppermute | solution.py:326
  12.2 0.5 add_convert_fusion.7
  12.7 2.9 %collective-permute-start.1 = (bf16[2,8,128,128]{3,2,1,0:T(8,128)(2,1)S(1)}, bf16[2,8,128,128]{3,2,1,0:T(8,128)(2,1)S(1)}, u32[]{:S(2)}, u32[]{:S(2)}) collective-permute-start(bf16[2,8,128,128]{3,2,1,0:T(8,128)(2,1)S(1)} %get-tuple-element.134), channel_id=1, source_target_pairs={{0,16},{4,20},{8,24},{12,28},{16,0},{20,4},{24,8},{28,12},{1,17},{... | collective-permute-start | bytes 1572872 | tf_op jit(solution)/shard_map/ppermute | solution.py:326
  15.6 0.3 add_convert_fusion.5
  16.0 1.6 %collective-permute-start.4 = (bf16[2,8,128,128]{3,2,1,0:T(8,128)(2,1)S(1)}, bf16[2,8,128,128]{3,2,1,0:T(8,128)(2,1)S(1)}, u32[]{:S(2)}, u32[]{:S(2)}) collective-permute-start(bf16[2,8,128,128]{3,2,1,0:T(8,128)(2,1)S(1)} %get-tuple-element.132), channel_id=1, source_target_pairs={{0,8},{4,12},{8,0},{12,4},{16,24},{20,28},{24,16},{28,20},{1,9},{5... | collective-permute-start | bytes 1572872 | tf_op jit(solution)/shard_map/ppermute | solution.py:326
  17.5 10.3 %collective-permute-done.1 = bf16[2,8,128,128]{3,2,1,0:T(8,128)(2,1)S(1)} collective-permute-done((bf16[2,8,128,128]{3,2,1,0:T(8,128)(2,1)S(1)}, bf16[2,8,128,128]{3,2,1,0:T(8,128)(2,1)S(1)}, u32[]{:S(2)}, u32[]{:S(2)}) %collective-permute-start.1) | collective-permute-done | bytes 524320 | tf_op jit(solution)/shard_map/ppermute | solution.py:326
  27.9 0.1 fusion.6
  28.0 1.8 %collective-permute-start.2 = (bf16[8,128,128]{2,1,0:T(8,128)(2,1)S(1)}, bf16[8,128,128]{2,1,0:T(8,128)(2,1)S(1)}, u32[]{:S(2)}, u32[]{:S(2)}) collective-permute-start(bf16[8,128,128]{2,1,0:T(8,128)(2,1)S(1)} %get-tuple-element.141), channel_id=1, source_target_pairs={{0,8},{4,12},{8,0},{12,4},{16,24},{20,28},{24,16},{28,20},{1,9},{5... | collective-permute-start | bytes 786440 | tf_op jit(solution)/shard_map/ppermute | solution.py:326
  29.9 1.6 %collective-permute-start.5 = (bf16[8,128,128]{2,1,0:T(8,128)(2,1)S(1)}, bf16[8,128,128]{2,1,0:T(8,128)(2,1)S(1)}, u32[]{:S(2)}, u32[]{:S(2)}) collective-permute-start(bf16[8,128,128]{2,1,0:T(8,128)(2,1)S(1)} %get-tuple-element.139), channel_id=1, source_target_pairs={{0,16},{4,20},{8,24},{12,28},{16,0},{20,4},{24,8},{28,12},{1,17},{... | collective-permute-start | bytes 786440 | tf_op jit(solution)/shard_map/ppermute | solution.py:326
  31.5 4.4 %collective-permute-done.2.refs_1_ = bf16[8,128,128]{2,1,0:T(8,128)(2,1)S(1)} collective-permute-done((bf16[8,128,128]{2,1,0:T(8,128)(2,1)S(1)}, bf16[8,128,128]{2,1,0:T(8,128)(2,1)S(1)}, u32[]{:S(2)}, u32[]{:S(2)}) %collective-permute-start.2) | collective-permute-done | bytes 262176 | tf_op jit(solution)/shard_map/ppermute | solution.py:326
  35.9 1.3 collective-permute-done.5.refs_3_
  37.4 1.6 %collective-permute-start.8 = (bf16[16,128,128]{2,1,0:T(8,128)(2,1)S(1)}, bf16[16,128,128]{2,1,0:T(8,128)(2,1)S(1)}, u32[]{:S(2)}, u32[]{:S(2)}) collective-permute-start(bf16[16,128,128]{2,1,0:T(8,128)(2,1)S(1)} %finish.2.rest_0_), channel_id=1, source_target_pairs={{0,1},{1,0},{2,3},{3,2},{4,5},{5,4},{6,7},{7,6},{8,9},{9,8},{10,11... | collective-permute-start | bytes 1572872 | tf_op jit(solution)/shard_map/ppermute | solution.py:326
  39.0 2.5 %collective-permute-start.6 = (bf16[16,128,128]{2,1,0:T(8,128)(2,1)S(1)}, bf16[16,128,128]{2,1,0:T(8,128)(2,1)}, u32[]{:S(2)}, u32[]{:S(2)}) collective-permute-start(bf16[16,128,128]{2,1,0:T(8,128)(2,1)S(1)} %finish.2.rest_0_), channel_id=1, source_target_pairs={{0,3},{1,2},{2,1},{3,0},{4,7},{5,6},{6,5},{7,4},{8,11},{9,10},{10,... | collective-permute-start | bytes 1572872 | tf_op jit(solution)/shard_map/ppermute | solution.py:326
  41.5 2.4 %collective-permute-start.14 = (bf16[16,128,128]{2,1,0:T(8,128)(2,1)S(1)}, bf16[16,128,128]{2,1,0:T(8,128)(2,1)S(1)}, u32[]{:S(2)}, u32[]{:S(2)}) collective-permute-start(bf16[16,128,128]{2,1,0:T(8,128)(2,1)S(1)} %bitcast.88), channel_id=1, source_target_pairs={{0,24},{4,28},{8,16},{12,20},{16,8},{20,12},{24,0},{28,4},{1,25},{... | collective-permute-start | bytes 1572872 | tf_op jit(solution)/shard_map/ppermute | solution.py:326
  43.9 0.5 collective-permute-start.12
  44.3 0.6 collective-permute-start.10
  45.0 6.4 %collective-permute-done.8.rest_1_ = bf16[16,128,128]{2,1,0:T(8,128)(2,1)S(1)} collective-permute-done((bf16[16,128,128]{2,1,0:T(8,128)(2,1)S(1)}, bf16[16,128,128]{2,1,0:T(8,128)(2,1)S(1)}, u32[]{:S(2)}, u32[]{:S(2)}) %collective-permute-start.8) | collective-permute-done | bytes 524320 | tf_op jit(solution)/shard_map/ppermute | solution.py:326
  51.4 0.8 copy-done.3
  52.2 10.7 %collective-permute-done.6.rest_2_ = bf16[16,128,128]{2,1,0:T(8,128)(2,1)} collective-permute-done((bf16[16,128,128]{2,1,0:T(8,128)(2,1)S(1)}, bf16[16,128,128]{2,1,0:T(8,128)(2,1)}, u32[]{:S(2)}, u32[]{:S(2)}) %collective-permute-start.6) | collective-permute-done | bytes 524320 | tf_op jit(solution)/shard_map/ppermute | solution.py:326
  62.8 0.6 collective-permute-start.7
  63.4 1.6 %collective-permute-done.12.rest_4_ = bf16[16,128,128]{2,1,0:T(8,128)(2,1)S(1)} collective-permute-done((bf16[16,128,128]{2,1,0:T(8,128)(2,1)S(1)}, bf16[16,128,128]{2,1,0:T(8,128)(2,1)S(1)}, u32[]{:S(2)}, u32[]{:S(2)}) %collective-permute-start.12) | collective-permute-done | bytes 524320 | tf_op jit(solution)/shard_map/ppermute | solution.py:326
  65.1 0.4 collective-permute-start.11
  65.6 0.6 constant_dynamic-slice_fusion.3
  66.3 1.0 copy-done.4
  67.3 1.9 %dense_early.1 = (f32[2,128,1024]{2,1,0:T(8,128)S(1)}, f32[4,128,128]{2,1,0:T(8,128)S(1)}) custom-call(s32[1]{0:T(128)} %bitcast.1.col_ref, bf16[128,512]{1,0:T(8,128)(2,1)S(1)} %pad_maximum_fusion.1.weight_ref, bf16[16,128,128]{2,1,0:T(8,128)(2,1)S(1)} %finish.2.rest_0_, bf16[16,128,128]{2,1,0:T(8,128)(2,1)S(1)} %copy-done.4, ...), custom_call_target="tpu_custom_call" | custom-call | tf_op jit(solution)/shard_map/dense_early/pallas_call | solution.py:256
  69.2 4.9 %collective-permute-done.7.shard_ref = bf16[16,128,128]{2,1,0:T(8,128)(2,1)} collective-permute-done((bf16[16,128,128]{2,1,0:T(8,128)(2,1)}, bf16[16,128,128]{2,1,0:T(8,128)(2,1)}, u32[]{:S(2)}, u32[]{:S(2)}) %collective-permute-start.7) | collective-permute-done | bytes 524320 | tf_op jit(solution)/shard_map/ppermute | solution.py:326
  74.1 1.0 copy-done.6
  75.2 1.5 dense_late.1
  76.7 0.3 collective-permute-start.17
  77.0 5.5 %collective-permute-start.16 = (bf16[8,128,128]{2,1,0:T(8,128)(2,1)S(1)}, bf16[8,128,128]{2,1,0:T(8,128)(2,1)S(1)}, u32[]{:S(2)}, u32[]{:S(2)}) collective-permute-start(bf16[8,128,128]{2,1,0:T(8,128)(2,1)S(1)} %get-tuple-element.88.rest_0_), channel_id=1, source_target_pairs={{0,3},{1,2},{2,1},{3,0},{4,7},{5,6},{6,5},{7,4},{8,11},{9,10},{10,... | collective-permute-start | bytes 786440 | tf_op jit(solution)/shard_map/ppermute | solution.py:326
  82.6 0.8 collective-permute-start.20
  83.4 0.9 collective-permute-start.19
  84.4 6.5 %aggregate.1 = bf16[16,128,128]{2,1,0:T(8,128)(2,1)S(1)} custom-call(s32[320]{0:T(512)S(1)} %reshape.122.cols_ref, s32[1]{0:T(128)} %bitcast.me_ref.refs_4_, bf16[16,20,128,128]{3,2,1,0:T(8,128)(2,1)} %tiles_ref.5, bf16[16,128,128]{2,1,0:T(8,128)(2,1)S(1)} %bitcast.92, bf16[16,128,128]{2,1,0:T(8,128)(2,1)} %collective-permute-done.9.rest_1_, ...), custom_call_target="tpu_custom_call" | custom-call | flops 1342177280 | bytes 30000000 | tf_op jit(solution)/shard_map/aggregate/pallas_call | solution.py:150
  90.9 4.6 %collective-permute-done.16.rest_3_ = bf16[8,128,128]{2,1,0:T(8,128)(2,1)S(1)} collective-permute-done((bf16[8,128,128]{2,1,0:T(8,128)(2,1)S(1)}, bf16[8,128,128]{2,1,0:T(8,128)(2,1)S(1)}, u32[]{:S(2)}, u32[]{:S(2)}) %collective-permute-start.16) | collective-permute-done | bytes 262176 | tf_op jit(solution)/shard_map/ppermute | solution.py:326
  95.4 0.8 collective-permute-start.18
  96.2 10.5 %collective-permute-done.19.rest_3_ = bf16[8,128,128]{2,1,0:T(8,128)(2,1)S(1)} collective-permute-done((bf16[8,128,128]{2,1,0:T(8,128)(2,1)S(1)}, bf16[8,128,128]{2,1,0:T(8,128)(2,1)S(1)}, u32[]{:S(2)}, u32[]{:S(2)}) %collective-permute-start.19) | collective-permute-done | bytes 262176 | tf_op jit(solution)/shard_map/ppermute | solution.py:326
  106.8 0.6 collective-permute-done.18.rest_2_
  107.4 0.6 dense.2
  108.0 5.1 %collective-permute-done.21.rest_2_ = bf16[8,128,128]{2,1,0:T(8,128)(2,1)S(1)} collective-permute-done((bf16[8,128,128]{2,1,0:T(8,128)(2,1)S(1)}, bf16[8,128,128]{2,1,0:T(8,128)(2,1)S(1)}, u32[]{:S(2)}, u32[]{:S(2)}) %collective-permute-start.21) | collective-permute-done | bytes 262176 | tf_op jit(solution)/shard_map/ppermute | solution.py:326
  113.1 0.6 dense.3
  113.7 6.6 %spread.3 = (bf16[4,8,128,128]{3,2,1,0:T(8,128)(2,1)S(1)}, bf16[4,8,128,128]{3,2,1,0:T(8,128)(2,1)S(1)}, bf16[4,8,128,128]{3,2,1,0:T(8,128)(2,1)S(1)}, bf16[4,8,128,128]{3,2,1,0:T(8,128)(2,1)S(1)}) custom-call(s32[320]{0:T(512)S(1)} %reshape.122.cols_ref, s32[1]{0:T(128)} %bitcast.me_ref.refs_4_, bf16[16,20,128,128]{3,2,1,0:T(8,128)(2,1)} %tiles_ref.5, ...), custom_call_target="tpu_custom_call" | custom-call | flops 1342177280 | bytes 30000000 | tf_op jit(solution)/shard_map/spread/pallas_call | solution.py:107
  120.3 0.5 collective-permute-start.23
  120.8 0.2 weight_terms.1
  121.0 0.1 collective-permute-start.24
  121.2 1.8 %collective-permute-done.22 = bf16[4,8,128,128]{3,2,1,0:T(8,128)(2,1)S(1)} collective-permute-done((bf16[4,8,128,128]{3,2,1,0:T(8,128)(2,1)S(1)}, bf16[4,8,128,128]{3,2,1,0:T(8,128)(2,1)S(1)}, u32[]{:S(2)}, u32[]{:S(2)}) %collective-permute-start.22) | collective-permute-done | bytes 1048608 | tf_op jit(solution)/shard_map/ppermute | solution.py:326
  123.0 0.3 add_convert_fusion.3
  123.3 1.6 %collective-permute-start.25 = (bf16[2,8,128,128]{3,2,1,0:T(8,128)(2,1)S(1)}, bf16[2,8,128,128]{3,2,1,0:T(8,128)(2,1)S(1)}, u32[]{:S(2)}, u32[]{:S(2)}) collective-permute-start(bf16[2,8,128,128]{3,2,1,0:T(8,128)(2,1)S(1)} %get-tuple-element.130), channel_id=1, source_target_pairs={{0,16},{4,20},{8,24},{12,28},{16,0},{20,4},{24,8},{28,12},{1,17},{... | collective-permute-start | bytes 1572872 | tf_op jit(solution)/shard_map/ppermute | solution.py:326
  124.9 0.4 fusion.1
  125.3 1.8 %collective-permute-start.26 = (bf16[2,8,128,128]{3,2,1,0:T(8,128)(2,1)S(1)}, bf16[2,8,128,128]{3,2,1,0:T(8,128)(2,1)S(1)}, u32[]{:S(2)}, u32[]{:S(2)}) collective-permute-start(bf16[2,8,128,128]{3,2,1,0:T(8,128)(2,1)S(1)} %get-tuple-element.128), channel_id=1, source_target_pairs={{0,8},{4,12},{8,0},{12,4},{16,24},{20,28},{24,16},{28,20},{1,9},{5... | collective-permute-start | bytes 1572872 | tf_op jit(solution)/shard_map/ppermute | solution.py:326
  127.1 1.2 collective-permute-start.27
  128.2 11.9 %collective-permute-done.27 = bf16[128,512]{1,0:T(8,128)(2,1)S(1)} collective-permute-done((bf16[128,512]{1,0:T(8,128)(2,1)S(1)}, bf16[128,512]{1,0:T(8,128)(2,1)S(1)}, u32[]{:S(2)}, u32[]{:S(2)}) %collective-permute-start.27) | collective-permute-done | bytes 131104 | tf_op jit(solution)/shard_map/ppermute | solution.py:326
  140.2 0.1 fusion.9
  140.3 0.1 fusion.10
  140.5 1.6 %collective-permute-start.30 = (bf16[128,512]{1,0:T(8,128)(2,1)S(1)}, bf16[128,512]{1,0:T(8,128)(2,1)S(1)}, u32[]{:S(2)}, u32[]{:S(2)}) collective-permute-start(bf16[128,512]{1,0:T(8,128)(2,1)S(1)} %convert_add_fusion.3), channel_id=1, source_target_pairs={{0,8},{4,12},{8,0},{12,4},{16,24},{20,28},{24,16},{28,20},{1,9},{5... | collective-permute-start | bytes 393224 | tf_op jit(solution)/shard_map/ppermute | solution.py:326
  142.1 1.7 %collective-permute-start.29 = (bf16[8,128,128]{2,1,0:T(8,128)(2,1)S(1)}, bf16[8,128,128]{2,1,0:T(8,128)(2,1)S(1)}, u32[]{:S(2)}, u32[]{:S(2)}) collective-permute-start(bf16[8,128,128]{2,1,0:T(8,128)(2,1)S(1)} %get-tuple-element.135), channel_id=1, source_target_pairs={{0,16},{4,20},{8,24},{12,28},{16,0},{20,4},{24,8},{28,12},{1,17},{... | collective-permute-start | bytes 786440 | tf_op jit(solution)/shard_map/ppermute | solution.py:326
  143.8 0.3 collective-permute-start.28
  144.1 1.9 %collective-permute-done.30 = bf16[128,512]{1,0:T(8,128)(2,1)S(1)} collective-permute-done((bf16[128,512]{1,0:T(8,128)(2,1)S(1)}, bf16[128,512]{1,0:T(8,128)(2,1)S(1)}, u32[]{:S(2)}, u32[]{:S(2)}) %collective-permute-start.30) | collective-permute-done | bytes 131104 | tf_op jit(solution)/shard_map/ppermute | solution.py:326
  146.1 3.4 %collective-permute-done.29.refs_3_ = bf16[8,128,128]{2,1,0:T(8,128)(2,1)S(1)} collective-permute-done((bf16[8,128,128]{2,1,0:T(8,128)(2,1)S(1)}, bf16[8,128,128]{2,1,0:T(8,128)(2,1)S(1)}, u32[]{:S(2)}, u32[]{:S(2)}) %collective-permute-start.29) | collective-permute-done | bytes 262176 | tf_op jit(solution)/shard_map/ppermute | solution.py:326
  149.5 1.7 %collective-permute-done.28.refs_1_ = bf16[8,128,128]{2,1,0:T(8,128)(2,1)S(1)} collective-permute-done((bf16[8,128,128]{2,1,0:T(8,128)(2,1)S(1)}, bf16[8,128,128]{2,1,0:T(8,128)(2,1)S(1)}, u32[]{:S(2)}, u32[]{:S(2)}) %collective-permute-start.28) | collective-permute-done | bytes 262176 | tf_op jit(solution)/shard_map/ppermute | solution.py:326
  151.1 1.2 finish.3
  (54 shorter events, 0.9 us)
Async XLA Ops:
  1.4 1.0 copy-start.1
  2.5 39.0 %copy-start.2 = (bf16[2048,128]{1,0:T(8,128)(2,1)S(1)}, bf16[2048,128]{1,0:T(8,128)(2,1)}, u32[]{:S(2)}) copy-start(bf16[2048,128]{1,0:T(8,128)(2,1)} %param.8) | copy-start | bytes 1572868
  2.5 63.1 %copy-start.7 = (bf16[128,512]{1,0:T(8,128)(2,1)S(1)}, bf16[128,512]{1,0:T(8,128)(2,1)}, u32[]{:S(2)}) copy-start(bf16[128,512]{1,0:T(8,128)(2,1)} %param.14) | copy-start | bytes 393220
  2.5 63.1 %copy-start.8 = (bf16[128,512]{1,0:T(8,128)(2,1)S(1)}, bf16[128,512]{1,0:T(8,128)(2,1)}, u32[]{:S(2)}) copy-start(bf16[128,512]{1,0:T(8,128)(2,1)} %param.15) | copy-start | bytes 393220
  2.5 63.8 %copy-start = (bf16[2048,128]{1,0:T(8,128)(2,1)S(1)}, bf16[2048,128]{1,0:T(8,128)(2,1)}, u32[]{:S(2)}) copy-start(bf16[2048,128]{1,0:T(8,128)(2,1)} %param.9) | copy-start | bytes 1572868
  9.4 55.7 %copy-start.5 = (bf16[16,128,128]{2,1,0:T(8,128)(2,1)}, bf16[16,128,128]{2,1,0:T(8,128)(2,1)S(1)}, u32[]{:S(2)}) copy-start(bf16[16,128,128]{2,1,0:T(8,128)(2,1)S(1)} %get-tuple-element.78.mask_ref) | copy-start | bytes 1572868
  9.4 2.8 %collective-permute-start = (bf16[4,8,128,128]{3,2,1,0:T(8,128)(2,1)S(1)}, bf16[4,8,128,128]{3,2,1,0:T(8,128)(2,1)S(1)}, u32[]{:S(2)}, u32[]{:S(2)}) collective-permute-start(bf16[4,8,128,128]{3,2,1,0:T(8,128)(2,1)S(1)} %get-tuple-element.66), channel_id=1, source_target_pairs={{0,4},{4,0},{8,12},{12,8},{16,20},{20,16},{24,28},{28,24},{1,5},{5... | collective-permute-start | bytes 3145736 | tf_op jit(solution)/shard_map/ppermute | solution.py:326
  9.9 5.7 %collective-permute-start.3 = (bf16[4,8,128,128]{3,2,1,0:T(8,128)(2,1)S(1)}, bf16[4,8,128,128]{3,2,1,0:T(8,128)(2,1)S(1)}, u32[]{:S(2)}, u32[]{:S(2)}) collective-permute-start(bf16[4,8,128,128]{3,2,1,0:T(8,128)(2,1)S(1)} %get-tuple-element.68), channel_id=1, source_target_pairs={{0,4},{4,0},{8,12},{12,8},{16,20},{20,16},{24,28},{28,24},{1,5},{5... | collective-permute-start | bytes 3145736 | tf_op jit(solution)/shard_map/ppermute | solution.py:326
  12.7 15.2 %collective-permute-start.1 = (bf16[2,8,128,128]{3,2,1,0:T(8,128)(2,1)S(1)}, bf16[2,8,128,128]{3,2,1,0:T(8,128)(2,1)S(1)}, u32[]{:S(2)}, u32[]{:S(2)}) collective-permute-start(bf16[2,8,128,128]{3,2,1,0:T(8,128)(2,1)S(1)} %get-tuple-element.134), channel_id=1, source_target_pairs={{0,16},{4,20},{8,24},{12,28},{16,0},{20,4},{24,8},{28,12},{1,17},{... | collective-permute-start | bytes 1572872 | tf_op jit(solution)/shard_map/ppermute | solution.py:326
  16.0 13.8 %collective-permute-start.4 = (bf16[2,8,128,128]{3,2,1,0:T(8,128)(2,1)S(1)}, bf16[2,8,128,128]{3,2,1,0:T(8,128)(2,1)S(1)}, u32[]{:S(2)}, u32[]{:S(2)}) collective-permute-start(bf16[2,8,128,128]{3,2,1,0:T(8,128)(2,1)S(1)} %get-tuple-element.132), channel_id=1, source_target_pairs={{0,8},{4,12},{8,0},{12,4},{16,24},{20,28},{24,16},{28,20},{1,9},{5... | collective-permute-start | bytes 1572872 | tf_op jit(solution)/shard_map/ppermute | solution.py:326
  28.0 7.9 %collective-permute-start.2 = (bf16[8,128,128]{2,1,0:T(8,128)(2,1)S(1)}, bf16[8,128,128]{2,1,0:T(8,128)(2,1)S(1)}, u32[]{:S(2)}, u32[]{:S(2)}) collective-permute-start(bf16[8,128,128]{2,1,0:T(8,128)(2,1)S(1)} %get-tuple-element.141), channel_id=1, source_target_pairs={{0,8},{4,12},{8,0},{12,4},{16,24},{20,28},{24,16},{28,20},{1,9},{5... | collective-permute-start | bytes 786440 | tf_op jit(solution)/shard_map/ppermute | solution.py:326
  29.9 7.3 %collective-permute-start.5 = (bf16[8,128,128]{2,1,0:T(8,128)(2,1)S(1)}, bf16[8,128,128]{2,1,0:T(8,128)(2,1)S(1)}, u32[]{:S(2)}, u32[]{:S(2)}) collective-permute-start(bf16[8,128,128]{2,1,0:T(8,128)(2,1)S(1)} %get-tuple-element.139), channel_id=1, source_target_pairs={{0,16},{4,20},{8,24},{12,28},{16,0},{20,4},{24,8},{28,12},{1,17},{... | collective-permute-start | bytes 786440 | tf_op jit(solution)/shard_map/ppermute | solution.py:326
  37.4 14.0 %collective-permute-start.8 = (bf16[16,128,128]{2,1,0:T(8,128)(2,1)S(1)}, bf16[16,128,128]{2,1,0:T(8,128)(2,1)S(1)}, u32[]{:S(2)}, u32[]{:S(2)}) collective-permute-start(bf16[16,128,128]{2,1,0:T(8,128)(2,1)S(1)} %finish.2.rest_0_), channel_id=1, source_target_pairs={{0,1},{1,0},{2,3},{3,2},{4,5},{5,4},{6,7},{7,6},{8,9},{9,8},{10,11... | collective-permute-start | bytes 1572872 | tf_op jit(solution)/shard_map/ppermute | solution.py:326
  39.0 23.8 %collective-permute-start.6 = (bf16[16,128,128]{2,1,0:T(8,128)(2,1)S(1)}, bf16[16,128,128]{2,1,0:T(8,128)(2,1)}, u32[]{:S(2)}, u32[]{:S(2)}) collective-permute-start(bf16[16,128,128]{2,1,0:T(8,128)(2,1)S(1)} %finish.2.rest_0_), channel_id=1, source_target_pairs={{0,3},{1,2},{2,1},{3,0},{4,7},{5,6},{6,5},{7,4},{8,11},{9,10},{10,... | collective-permute-start | bytes 1572872 | tf_op jit(solution)/shard_map/ppermute | solution.py:326
  41.5 21.9 %collective-permute-start.14 = (bf16[16,128,128]{2,1,0:T(8,128)(2,1)S(1)}, bf16[16,128,128]{2,1,0:T(8,128)(2,1)S(1)}, u32[]{:S(2)}, u32[]{:S(2)}) collective-permute-start(bf16[16,128,128]{2,1,0:T(8,128)(2,1)S(1)} %bitcast.88), channel_id=1, source_target_pairs={{0,24},{4,28},{8,16},{12,20},{16,8},{20,12},{24,0},{28,4},{1,25},{... | collective-permute-start | bytes 1572872 | tf_op jit(solution)/shard_map/ppermute | solution.py:326
  43.9 21.1 %collective-permute-start.12 = (bf16[16,128,128]{2,1,0:T(8,128)(2,1)S(1)}, bf16[16,128,128]{2,1,0:T(8,128)(2,1)S(1)}, u32[]{:S(2)}, u32[]{:S(2)}) collective-permute-start(bf16[16,128,128]{2,1,0:T(8,128)(2,1)S(1)} %bitcast.89), channel_id=1, source_target_pairs={{0,16},{4,20},{8,24},{12,28},{16,0},{20,4},{24,8},{28,12},{1,17},{... | collective-permute-start | bytes 1572872 | tf_op jit(solution)/shard_map/ppermute | solution.py:326
  44.3 20.8 %collective-permute-start.10 = (bf16[16,128,128]{2,1,0:T(8,128)(2,1)S(1)}, bf16[16,128,128]{2,1,0:T(8,128)(2,1)S(1)}, u32[]{:S(2)}, u32[]{:S(2)}) collective-permute-start(bf16[16,128,128]{2,1,0:T(8,128)(2,1)S(1)} %bitcast.90), channel_id=1, source_target_pairs={{0,8},{4,12},{8,0},{12,4},{16,24},{20,28},{24,16},{28,20},{1,9},{5... | collective-permute-start | bytes 1572872 | tf_op jit(solution)/shard_map/ppermute | solution.py:326
  51.4 0.8 copy-start.3
  52.2 17.1 %collective-permute-start.9 = (bf16[16,128,128]{2,1,0:T(8,128)(2,1)S(1)}, bf16[16,128,128]{2,1,0:T(8,128)(2,1)}, u32[]{:S(2)}, u32[]{:S(2)}) collective-permute-start(bf16[16,128,128]{2,1,0:T(8,128)(2,1)S(1)} %bitcast.91), channel_id=1, source_target_pairs={{0,4},{4,0},{8,12},{12,8},{16,20},{20,16},{24,28},{28,24},{1,5},{5... | collective-permute-start | bytes 1572872 | tf_op jit(solution)/shard_map/ppermute | solution.py:326
  62.8 11.3 %collective-permute-start.7 = (bf16[16,128,128]{2,1,0:T(8,128)(2,1)}, bf16[16,128,128]{2,1,0:T(8,128)(2,1)}, u32[]{:S(2)}, u32[]{:S(2)}) collective-permute-start(bf16[16,128,128]{2,1,0:T(8,128)(2,1)} %collective-permute-done.6.rest_2_), channel_id=1, source_target_pairs={{0,1},{1,0},{2,3},{3,2},{4,5},{5,4},{6,7},{7,6},{8,9},{9,8},{10,11... | collective-permute-start | bytes 1572872 | tf_op jit(solution)/shard_map/ppermute | solution.py:326
  63.4 10.7 %collective-permute-start.15 = (bf16[16,128,128]{2,1,0:T(8,128)(2,1)S(1)}, bf16[16,128,128]{2,1,0:T(8,128)(2,1)}, u32[]{:S(2)}, u32[]{:S(2)}) collective-permute-start(bf16[16,128,128]{2,1,0:T(8,128)(2,1)S(1)} %collective-permute-done.14.rest_6_), channel_id=1, source_target_pairs={{0,4},{4,0},{8,12},{12,8},{16,20},{20,16},{24,28},{28,24},{1,5},{5... | collective-permute-start | bytes 1572872 | tf_op jit(solution)/shard_map/ppermute | solution.py:326
  65.0 9.1 %collective-permute-start.13 = (bf16[16,128,128]{2,1,0:T(8,128)(2,1)S(1)}, bf16[16,128,128]{2,1,0:T(8,128)(2,1)}, u32[]{:S(2)}, u32[]{:S(2)}) collective-permute-start(bf16[16,128,128]{2,1,0:T(8,128)(2,1)S(1)} %collective-permute-done.12.rest_4_), channel_id=1, source_target_pairs={{0,4},{4,0},{8,12},{12,8},{16,20},{20,16},{24,28},{28,24},{1,5},{5... | collective-permute-start | bytes 1572872 | tf_op jit(solution)/shard_map/ppermute | solution.py:326
  65.1 9.0 %collective-permute-start.11 = (bf16[16,128,128]{2,1,0:T(8,128)(2,1)S(1)}, bf16[16,128,128]{2,1,0:T(8,128)(2,1)}, u32[]{:S(2)}, u32[]{:S(2)}) collective-permute-start(bf16[16,128,128]{2,1,0:T(8,128)(2,1)S(1)} %collective-permute-done.10.rest_2_), channel_id=1, source_target_pairs={{0,4},{4,0},{8,12},{12,8},{16,20},{20,16},{24,28},{28,24},{1,5},{5... | collective-permute-start | bytes 1572872 | tf_op jit(solution)/shard_map/ppermute | solution.py:326
  66.3 1.0 copy-start.4
  74.1 1.0 copy-start.6
  76.7 14.2 %collective-permute-start.17 = (bf16[8,128,128]{2,1,0:T(8,128)(2,1)S(1)}, bf16[8,128,128]{2,1,0:T(8,128)(2,1)S(1)}, u32[]{:S(2)}, u32[]{:S(2)}) collective-permute-start(bf16[8,128,128]{2,1,0:T(8,128)(2,1)S(1)} %get-tuple-element.88.rest_0_), channel_id=1, source_target_pairs={{0,1},{1,0},{2,3},{3,2},{4,5},{5,4},{6,7},{7,6},{8,9},{9,8},{10,11... | collective-permute-start | bytes 786440 | tf_op jit(solution)/shard_map/ppermute | solution.py:326
  77.0 18.4 %collective-permute-start.16 = (bf16[8,128,128]{2,1,0:T(8,128)(2,1)S(1)}, bf16[8,128,128]{2,1,0:T(8,128)(2,1)S(1)}, u32[]{:S(2)}, u32[]{:S(2)}) collective-permute-start(bf16[8,128,128]{2,1,0:T(8,128)(2,1)S(1)} %get-tuple-element.88.rest_0_), channel_id=1, source_target_pairs={{0,3},{1,2},{2,1},{3,0},{4,7},{5,6},{6,5},{7,4},{8,11},{9,10},{10,... | collective-permute-start | bytes 786440 | tf_op jit(solution)/shard_map/ppermute | solution.py:326
  82.6 13.7 %collective-permute-start.20 = (bf16[8,128,128]{2,1,0:T(8,128)(2,1)S(1)}, bf16[8,128,128]{2,1,0:T(8,128)(2,1)S(1)}, u32[]{:S(2)}, u32[]{:S(2)}) collective-permute-start(bf16[8,128,128]{2,1,0:T(8,128)(2,1)S(1)} %get-tuple-element.101.rest_0_), channel_id=1, source_target_pairs={{0,1},{1,0},{2,3},{3,2},{4,5},{5,4},{6,7},{7,6},{8,9},{9,8},{10,11... | collective-permute-start | bytes 786440 | tf_op jit(solution)/shard_map/ppermute | solution.py:326
  83.4 23.3 %collective-permute-start.19 = (bf16[8,128,128]{2,1,0:T(8,128)(2,1)S(1)}, bf16[8,128,128]{2,1,0:T(8,128)(2,1)S(1)}, u32[]{:S(2)}, u32[]{:S(2)}) collective-permute-start(bf16[8,128,128]{2,1,0:T(8,128)(2,1)S(1)} %get-tuple-element.101.rest_0_), channel_id=1, source_target_pairs={{0,3},{1,2},{2,1},{3,0},{4,7},{5,6},{6,5},{7,4},{8,11},{9,10},{10,... | collective-permute-start | bytes 786440 | tf_op jit(solution)/shard_map/ppermute | solution.py:326
  95.4 12.0 %collective-permute-start.18 = (bf16[8,128,128]{2,1,0:T(8,128)(2,1)S(1)}, bf16[8,128,128]{2,1,0:T(8,128)(2,1)S(1)}, u32[]{:S(2)}, u32[]{:S(2)}) collective-permute-start(bf16[8,128,128]{2,1,0:T(8,128)(2,1)S(1)} %collective-permute-done.16.rest_3_), channel_id=1, source_target_pairs={{0,1},{1,0},{2,3},{3,2},{4,5},{5,4},{6,7},{7,6},{8,9},{9,8},{10,11... | collective-permute-start | bytes 786440 | tf_op jit(solution)/shard_map/ppermute | solution.py:326
  106.7 6.4 %collective-permute-start.21 = (bf16[8,128,128]{2,1,0:T(8,128)(2,1)S(1)}, bf16[8,128,128]{2,1,0:T(8,128)(2,1)S(1)}, u32[]{:S(2)}, u32[]{:S(2)}) collective-permute-start(bf16[8,128,128]{2,1,0:T(8,128)(2,1)S(1)} %collective-permute-done.19.rest_3_), channel_id=1, source_target_pairs={{0,1},{1,0},{2,3},{3,2},{4,5},{5,4},{6,7},{7,6},{8,9},{9,8},{10,11... | collective-permute-start | bytes 786440 | tf_op jit(solution)/shard_map/ppermute | solution.py:326
  120.2 2.7 %collective-permute-start.22 = (bf16[4,8,128,128]{3,2,1,0:T(8,128)(2,1)S(1)}, bf16[4,8,128,128]{3,2,1,0:T(8,128)(2,1)S(1)}, u32[]{:S(2)}, u32[]{:S(2)}) collective-permute-start(bf16[4,8,128,128]{3,2,1,0:T(8,128)(2,1)S(1)} %get-tuple-element.106), channel_id=1, source_target_pairs={{0,4},{4,0},{8,12},{12,8},{16,20},{20,16},{24,28},{28,24},{1,5},{5... | collective-permute-start | bytes 3145736 | tf_op jit(solution)/shard_map/ppermute | solution.py:326
  120.3 4.6 %collective-permute-start.23 = (bf16[4,8,128,128]{3,2,1,0:T(8,128)(2,1)S(1)}, bf16[4,8,128,128]{3,2,1,0:T(8,128)(2,1)S(1)}, u32[]{:S(2)}, u32[]{:S(2)}) collective-permute-start(bf16[4,8,128,128]{3,2,1,0:T(8,128)(2,1)S(1)} %get-tuple-element.108), channel_id=1, source_target_pairs={{0,4},{4,0},{8,12},{12,8},{16,20},{20,16},{24,28},{28,24},{1,5},{5... | collective-permute-start | bytes 3145736 | tf_op jit(solution)/shard_map/ppermute | solution.py:326
  121.0 6.0 %collective-permute-start.24 = (bf16[128,512]{1,0:T(8,128)(2,1)S(1)}, bf16[128,512]{1,0:T(8,128)(2,1)S(1)}, u32[]{:S(2)}, u32[]{:S(2)}) collective-permute-start(bf16[128,512]{1,0:T(8,128)(2,1)S(1)} %get-tuple-element.114), channel_id=1, source_target_pairs={{0,4},{4,0},{8,12},{12,8},{16,20},{20,16},{24,28},{28,24},{1,5},{5... | collective-permute-start | bytes 393224 | tf_op jit(solution)/shard_map/ppermute | solution.py:326
  123.3 16.9 %collective-permute-start.25 = (bf16[2,8,128,128]{3,2,1,0:T(8,128)(2,1)S(1)}, bf16[2,8,128,128]{3,2,1,0:T(8,128)(2,1)S(1)}, u32[]{:S(2)}, u32[]{:S(2)}) collective-permute-start(bf16[2,8,128,128]{3,2,1,0:T(8,128)(2,1)S(1)} %get-tuple-element.130), channel_id=1, source_target_pairs={{0,16},{4,20},{8,24},{12,28},{16,0},{20,4},{24,8},{28,12},{1,17},{... | collective-permute-start | bytes 1572872 | tf_op jit(solution)/shard_map/ppermute | solution.py:326
  125.3 14.9 %collective-permute-start.26 = (bf16[2,8,128,128]{3,2,1,0:T(8,128)(2,1)S(1)}, bf16[2,8,128,128]{3,2,1,0:T(8,128)(2,1)S(1)}, u32[]{:S(2)}, u32[]{:S(2)}) collective-permute-start(bf16[2,8,128,128]{3,2,1,0:T(8,128)(2,1)S(1)} %get-tuple-element.128), channel_id=1, source_target_pairs={{0,8},{4,12},{8,0},{12,4},{16,24},{20,28},{24,16},{28,20},{1,9},{5... | collective-permute-start | bytes 1572872 | tf_op jit(solution)/shard_map/ppermute | solution.py:326
  127.1 13.1 %collective-permute-start.27 = (bf16[128,512]{1,0:T(8,128)(2,1)S(1)}, bf16[128,512]{1,0:T(8,128)(2,1)S(1)}, u32[]{:S(2)}, u32[]{:S(2)}) collective-permute-start(bf16[128,512]{1,0:T(8,128)(2,1)S(1)} %convert_add_fusion.4), channel_id=1, source_target_pairs={{0,16},{4,20},{8,24},{12,28},{16,0},{20,4},{24,8},{28,12},{1,17},{... | collective-permute-start | bytes 393224 | tf_op jit(solution)/shard_map/ppermute | solution.py:326
  140.5 5.5 %collective-permute-start.30 = (bf16[128,512]{1,0:T(8,128)(2,1)S(1)}, bf16[128,512]{1,0:T(8,128)(2,1)S(1)}, u32[]{:S(2)}, u32[]{:S(2)}) collective-permute-start(bf16[128,512]{1,0:T(8,128)(2,1)S(1)} %convert_add_fusion.3), channel_id=1, source_target_pairs={{0,8},{4,12},{8,0},{12,4},{16,24},{20,28},{24,16},{28,20},{1,9},{5... | collective-permute-start | bytes 393224 | tf_op jit(solution)/shard_map/ppermute | solution.py:326
  142.1 7.4 %collective-permute-start.29 = (bf16[8,128,128]{2,1,0:T(8,128)(2,1)S(1)}, bf16[8,128,128]{2,1,0:T(8,128)(2,1)S(1)}, u32[]{:S(2)}, u32[]{:S(2)}) collective-permute-start(bf16[8,128,128]{2,1,0:T(8,128)(2,1)S(1)} %get-tuple-element.135), channel_id=1, source_target_pairs={{0,16},{4,20},{8,24},{12,28},{16,0},{20,4},{24,8},{28,12},{1,17},{... | collective-permute-start | bytes 786440 | tf_op jit(solution)/shard_map/ppermute | solution.py:326
  143.8 7.3 %collective-permute-start.28 = (bf16[8,128,128]{2,1,0:T(8,128)(2,1)S(1)}, bf16[8,128,128]{2,1,0:T(8,128)(2,1)S(1)}, u32[]{:S(2)}, u32[]{:S(2)}) collective-permute-start(bf16[8,128,128]{2,1,0:T(8,128)(2,1)S(1)} %get-tuple-element.137), channel_id=1, source_target_pairs={{0,8},{4,12},{8,0},{12,4},{16,24},{20,28},{24,16},{28,20},{1,9},{5... | collective-permute-start | bytes 786440 | tf_op jit(solution)/shard_map/ppermute | solution.py:326
  146.0 5.1 %collective-permute-start.31 = (f32[128,512]{1,0:T(8,128)S(1)}, f32[128,512]{1,0:T(8,128)S(1)}, u32[]{:S(2)}, u32[]{:S(2)}) collective-permute-start(f32[128,512]{1,0:T(8,128)S(1)} %convert_add_fusion.2.refs_5_), channel_id=1, source_target_pairs={{0,4},{4,0},{8,12},{12,8},{16,20},{20,16},{24,28},{28,24},{1,5},{5... | collective-permute-start | bytes 786440 | tf_op jit(solution)/shard_map/ppermute | solution.py:326

commit v16 on v15

--- a/solution.py
+++ b/solution.py
@@ -233,7 +233,8 @@
 
 
 def dense_early_kernel(cols, late, col_ref, weight_ref, *rest):
-    shards, (side_ref, out_ref, grad_ref) = rest[: cols - 1], rest[cols - 1 :]
+    shards, (side_ref, mask_ref, out_ref, grad_ref, mask_out) = rest[: cols - 1], rest[cols - 1 :]
+    mask_out[...] = mask_ref[...]
     blocks, feat, size = shards[0].shape
     here = [m for m in range(cols) if m != late]
     per = blocks // GROUPS
@@ -249,18 +250,19 @@
         grad_ref[jnp.bitwise_xor(col_ref[0], m)] = total[i * feat : (i + 1) * feat]
 
 
-def dense_early(weight, shards, side, col, late):
+def dense_early(weight, shards, side, mask, col, late):
     blocks, feat, size = shards[0].shape
     cols = len(shards)
-    args = [weight, *(v for m, v in enumerate(shards) if m != late), side]
+    args = [weight, *(v for m, v in enumerate(shards) if m != late), side, mask]
     return pl.pallas_call(
         functools.partial(dense_early_kernel, cols, late),
         out_shape=[
             jax.ShapeDtypeStruct((GROUPS, feat, blocks // GROUPS * size), F32),
             jax.ShapeDtypeStruct((cols, feat, side.shape[2]), F32),
+            jax.ShapeDtypeStruct(mask.shape, BF16),
         ],
         in_specs=[SMEM] + [VMEM] * len(args),
-        out_specs=[VMEM] * 2,
+        out_specs=[VMEM] * 3,
         compiler_params=params(16),
         name="dense_early",
     )(col, *args)
@@ -396,7 +398,7 @@
     parts = [v for part in parts for v in (part, swap(part, 1, "row"))]
     late = 2
     hidden = blocked(hidden_act)
-    part, second = dense_early(weight_two, shards, hidden, col_at, late)
+    part, second, mask = dense_early(weight_two, shards, hidden, mask, col_at, late)
     arrived, parts = after((shards[late], parts))
     *deltas, last = dense_late(weight_two, arrived, part, hidden, mask, late)
     deltas[0], parts = after((deltas[0], parts))

time: 153 us -> 152 us (level)
  no operation moved by 1% of the time
where the time goes in v16:
time: 152 us; the launch traced here: 151 us
  waiting for transfers between devices  82.2 us (54%)
  starting transfers between devices  34.5 us (23%)
  Pallas kernels  26.1 us (17%)
  local copies, waits for them, and re-layouts  5.42 us (4%)
  other arithmetic  2.17 us (1%)
    ppermute x32, waiting for transfers between devices, swap(): lax.ppermute(value, axis, [(i, i ^ mask) for i in range(lax.axis_size(axi...  82.2 us
    ppermute x32, starting transfers between devices, swap(): lax.ppermute(value, axis, [(i, i ^ mask) for i in range(lax.axis_size(axi...  34.5 us
    pallas_call x2, Pallas kernels, spread(): pl.pallas_call(functools.partial(spread_kernel, first, len(vals)), out_sh...  13.5 us
    pallas_call x1, Pallas kernels, aggregate(): pl.pallas_call(aggregate_kernel, out_shape=jax.ShapeDtypeStruct((blocks,...  6.48 us
    unnamed x26, local copies, waits for them, and re-layouts  3.98 us
  transfers between devices with their start and end apart: 32, of which 18 were waited for; matrix products, arithmetic and copies ran while one was open for 2% of the time, Pallas kernels for 6%

profile of v16, /device:TPU:0, one launch (start us, length us, event | category | flops | bytes accessed | tf_op | source)
XLA Modules:
  0.0 151.3 jit_solution(7898193088215628287)
XLA Ops:
  0.6 0.8 reshape.122.cols_ref
  1.4 1.0 copy-done.1
  2.5 6.9 %spread.2 = (bf16[4,8,128,128]{3,2,1,0:T(8,128)(2,1)S(1)}, bf16[4,8,128,128]{3,2,1,0:T(8,128)(2,1)S(1)}, bf16[4,8,128,128]{3,2,1,0:T(8,128)(2,1)S(1)}, bf16[4,8,...) custom-call(s32[320]{0:T(512)S(1)} %reshape.122.cols_ref, s32[1]{0:T(128)} %bitcast.me_ref.refs_4_, ...), custom_call_target="tpu_custom_call" | custom-call | flops 1342177280 | bytes 30000000 | tf_op jit(solution)/shard_map/spread/pallas_call | solution.py:107
  9.4 0.5 collective-permute-start
  10.0 2.2 %collective-permute-done = bf16[4,8,128,128]{3,2,1,0:T(8,128)(2,1)S(1)} collective-permute-done((bf16[4,8,128,128]{3,2,1,0:T(8,128)(2,1)S(1)}, bf16[4,8,128,128]{3,2,1,0:T(8,128)(2,1)S(1)}, u32[]{:S(2)}, u32[]{:S(2)}) %collective-permute-start) | collective-permute-done | bytes 1048608 | tf_op jit(solution)/shard_map/ppermute | solution.py:328
  12.2 0.5 add_convert_fusion.7
  12.7 3.0 %collective-permute-start.1 = (bf16[2,8,128,128]{3,2,1,0:T(8,128)(2,1)S(1)}, bf16[2,8,128,128]{3,2,1,0:T(8,128)(2,1)S(1)}, u32[]{:S(2)}, u32[]{:S(2)}) collective-permute-start(bf16[2,8,128,128]{3,2,1,0:T(8,128)(2,1)S(1)} %get-tuple-element.136), channel_id=1, source_target_pairs={{0,16},{4,20},{8,24},{12,28},{16,0},{20,4},{24,8},{28,12},{1,17},{... | collective-permute-start | bytes 1572872 | tf_op jit(solution)/shard_map/ppermute | solution.py:328
  15.6 0.3 add_convert_fusion.5
  16.0 1.6 %collective-permute-start.4 = (bf16[2,8,128,128]{3,2,1,0:T(8,128)(2,1)S(1)}, bf16[2,8,128,128]{3,2,1,0:T(8,128)(2,1)S(1)}, u32[]{:S(2)}, u32[]{:S(2)}) collective-permute-start(bf16[2,8,128,128]{3,2,1,0:T(8,128)(2,1)S(1)} %get-tuple-element.134), channel_id=1, source_target_pairs={{0,8},{4,12},{8,0},{12,4},{16,24},{20,28},{24,16},{28,20},{1,9},{5... | collective-permute-start | bytes 1572872 | tf_op jit(solution)/shard_map/ppermute | solution.py:328
  17.5 10.3 %collective-permute-done.1 = bf16[2,8,128,128]{3,2,1,0:T(8,128)(2,1)S(1)} collective-permute-done((bf16[2,8,128,128]{3,2,1,0:T(8,128)(2,1)S(1)}, bf16[2,8,128,128]{3,2,1,0:T(8,128)(2,1)S(1)}, u32[]{:S(2)}, u32[]{:S(2)}) %collective-permute-start.1) | collective-permute-done | bytes 524320 | tf_op jit(solution)/shard_map/ppermute | solution.py:328
  27.9 0.1 fusion.6
  28.0 1.8 %collective-permute-start.2 = (bf16[8,128,128]{2,1,0:T(8,128)(2,1)S(1)}, bf16[8,128,128]{2,1,0:T(8,128)(2,1)S(1)}, u32[]{:S(2)}, u32[]{:S(2)}) collective-permute-start(bf16[8,128,128]{2,1,0:T(8,128)(2,1)S(1)} %get-tuple-element.143), channel_id=1, source_target_pairs={{0,8},{4,12},{8,0},{12,4},{16,24},{20,28},{24,16},{28,20},{1,9},{5... | collective-permute-start | bytes 786440 | tf_op jit(solution)/shard_map/ppermute | solution.py:328
  29.9 1.6 %collective-permute-start.5 = (bf16[8,128,128]{2,1,0:T(8,128)(2,1)S(1)}, bf16[8,128,128]{2,1,0:T(8,128)(2,1)S(1)}, u32[]{:S(2)}, u32[]{:S(2)}) collective-permute-start(bf16[8,128,128]{2,1,0:T(8,128)(2,1)S(1)} %get-tuple-element.141), channel_id=1, source_target_pairs={{0,16},{4,20},{8,24},{12,28},{16,0},{20,4},{24,8},{28,12},{1,17},{... | collective-permute-start | bytes 786440 | tf_op jit(solution)/shard_map/ppermute | solution.py:328
  31.5 4.4 %collective-permute-done.2.refs_1_ = bf16[8,128,128]{2,1,0:T(8,128)(2,1)S(1)} collective-permute-done((bf16[8,128,128]{2,1,0:T(8,128)(2,1)S(1)}, bf16[8,128,128]{2,1,0:T(8,128)(2,1)S(1)}, u32[]{:S(2)}, u32[]{:S(2)}) %collective-permute-start.2) | collective-permute-done | bytes 262176 | tf_op jit(solution)/shard_map/ppermute | solution.py:328
  35.9 1.3 collective-permute-done.5.refs_3_
  37.4 1.6 %collective-permute-start.8 = (bf16[16,128,128]{2,1,0:T(8,128)(2,1)S(1)}, bf16[16,128,128]{2,1,0:T(8,128)(2,1)S(1)}, u32[]{:S(2)}, u32[]{:S(2)}) collective-permute-start(bf16[16,128,128]{2,1,0:T(8,128)(2,1)S(1)} %finish.2.rest_0_), channel_id=1, source_target_pairs={{0,1},{1,0},{2,3},{3,2},{4,5},{5,4},{6,7},{7,6},{8,9},{9,8},{10,11... | collective-permute-start | bytes 1572872 | tf_op jit(solution)/shard_map/ppermute | solution.py:328
  39.0 2.5 %collective-permute-start.6 = (bf16[16,128,128]{2,1,0:T(8,128)(2,1)S(1)}, bf16[16,128,128]{2,1,0:T(8,128)(2,1)}, u32[]{:S(2)}, u32[]{:S(2)}) collective-permute-start(bf16[16,128,128]{2,1,0:T(8,128)(2,1)S(1)} %finish.2.rest_0_), channel_id=1, source_target_pairs={{0,3},{1,2},{2,1},{3,0},{4,7},{5,6},{6,5},{7,4},{8,11},{9,10},{10,... | collective-permute-start | bytes 1572872 | tf_op jit(solution)/shard_map/ppermute | solution.py:328
  41.5 2.4 %collective-permute-start.14 = (bf16[16,128,128]{2,1,0:T(8,128)(2,1)S(1)}, bf16[16,128,128]{2,1,0:T(8,128)(2,1)S(1)}, u32[]{:S(2)}, u32[]{:S(2)}) collective-permute-start(bf16[16,128,128]{2,1,0:T(8,128)(2,1)S(1)} %bitcast.88), channel_id=1, source_target_pairs={{0,24},{4,28},{8,16},{12,20},{16,8},{20,12},{24,0},{28,4},{1,25},{... | collective-permute-start | bytes 1572872 | tf_op jit(solution)/shard_map/ppermute | solution.py:328
  43.9 0.5 collective-permute-start.12
  44.3 0.6 collective-permute-start.10
  45.0 6.4 %collective-permute-done.8.rest_1_ = bf16[16,128,128]{2,1,0:T(8,128)(2,1)S(1)} collective-permute-done((bf16[16,128,128]{2,1,0:T(8,128)(2,1)S(1)}, bf16[16,128,128]{2,1,0:T(8,128)(2,1)S(1)}, u32[]{:S(2)}, u32[]{:S(2)}) %collective-permute-start.8) | collective-permute-done | bytes 524320 | tf_op jit(solution)/shard_map/ppermute | solution.py:328
  51.4 0.8 copy-done.5
  52.2 10.7 %collective-permute-done.6.rest_2_ = bf16[16,128,128]{2,1,0:T(8,128)(2,1)} collective-permute-done((bf16[16,128,128]{2,1,0:T(8,128)(2,1)S(1)}, bf16[16,128,128]{2,1,0:T(8,128)(2,1)}, u32[]{:S(2)}, u32[]{:S(2)}) %collective-permute-start.6) | collective-permute-done | bytes 524320 | tf_op jit(solution)/shard_map/ppermute | solution.py:328
  62.8 0.6 collective-permute-start.7
  63.4 1.6 %collective-permute-done.12.rest_4_ = bf16[16,128,128]{2,1,0:T(8,128)(2,1)S(1)} collective-permute-done((bf16[16,128,128]{2,1,0:T(8,128)(2,1)S(1)}, bf16[16,128,128]{2,1,0:T(8,128)(2,1)S(1)}, u32[]{:S(2)}, u32[]{:S(2)}) %collective-permute-start.12) | collective-permute-done | bytes 524320 | tf_op jit(solution)/shard_map/ppermute | solution.py:328
  65.1 0.4 collective-permute-start.11
  65.6 0.6 constant_dynamic-slice_fusion.3
  66.3 1.0 copy-done.4
  67.3 1.0 copy-done.6
  68.4 1.9 %dense_early.1 = (f32[2,128,1024]{2,1,0:T(8,128)S(1)}, f32[4,128,128]{2,1,0:T(8,128)S(1)}, bf16[16,128,128]{2,1,0:T(8,128)(2,1)S(1)}) custom-call(s32[1]{0:T(128)} %bitcast.1.col_ref, bf16[128,512]{1,0:T(8,128)(2,1)S(1)} %pad_maximum_fusion.1.weight_ref, bf16[16,128,128]{2,1,0:T(8,128)(2,1)S(1)} %finish.2.rest_0_, bf16[16,128,128]{2,1,0:T(8,128)(2,1)S(1)} %copy-done.6, ...), custom_call_target="tpu_custom_call" | custom-call | tf_op jit(solution)/shard_map/dense_early/pallas_call | solution.py:257
  70.3 3.8 %collective-permute-done.7.shard_ref = bf16[16,128,128]{2,1,0:T(8,128)(2,1)} collective-permute-done((bf16[16,128,128]{2,1,0:T(8,128)(2,1)}, bf16[16,128,128]{2,1,0:T(8,128)(2,1)}, u32[]{:S(2)}, u32[]{:S(2)}) %collective-permute-start.7) | collective-permute-done | bytes 524320 | tf_op jit(solution)/shard_map/ppermute | solution.py:328
  74.1 1.5 dense_late.1
  75.6 0.3 collective-permute-start.17
  76.0 5.5 %collective-permute-start.16 = (bf16[8,128,128]{2,1,0:T(8,128)(2,1)S(1)}, bf16[8,128,128]{2,1,0:T(8,128)(2,1)S(1)}, u32[]{:S(2)}, u32[]{:S(2)}) collective-permute-start(bf16[8,128,128]{2,1,0:T(8,128)(2,1)S(1)} %get-tuple-element.90.rest_0_), channel_id=1, source_target_pairs={{0,3},{1,2},{2,1},{3,0},{4,7},{5,6},{6,5},{7,4},{8,11},{9,10},{10,... | collective-permute-start | bytes 786440 | tf_op jit(solution)/shard_map/ppermute | solution.py:328
  81.5 0.8 collective-permute-start.20
  82.4 0.9 collective-permute-start.19
  83.3 6.5 %aggregate.1 = bf16[16,128,128]{2,1,0:T(8,128)(2,1)S(1)} custom-call(s32[320]{0:T(512)S(1)} %reshape.122.cols_ref, s32[1]{0:T(128)} %bitcast.me_ref.refs_4_, bf16[16,20,128,128]{3,2,1,0:T(8,128)(2,1)} %tiles_ref.5, bf16[16,128,128]{2,1,0:T(8,128)(2,1)S(1)} %bitcast.92, bf16[16,128,128]{2,1,0:T(8,128)(2,1)} %collective-permute-done.9.rest_1_, ...), custom_call_target="tpu_custom_call" | custom-call | flops 1342177280 | bytes 30000000 | tf_op jit(solution)/shard_map/aggregate/pallas_call | solution.py:150
  89.8 4.6 %collective-permute-done.16.rest_3_ = bf16[8,128,128]{2,1,0:T(8,128)(2,1)S(1)} collective-permute-done((bf16[8,128,128]{2,1,0:T(8,128)(2,1)S(1)}, bf16[8,128,128]{2,1,0:T(8,128)(2,1)S(1)}, u32[]{:S(2)}, u32[]{:S(2)}) %collective-permute-start.16) | collective-permute-done | bytes 262176 | tf_op jit(solution)/shard_map/ppermute | solution.py:328
  94.4 0.8 collective-permute-start.18
  95.2 10.5 %collective-permute-done.19.rest_3_ = bf16[8,128,128]{2,1,0:T(8,128)(2,1)S(1)} collective-permute-done((bf16[8,128,128]{2,1,0:T(8,128)(2,1)S(1)}, bf16[8,128,128]{2,1,0:T(8,128)(2,1)S(1)}, u32[]{:S(2)}, u32[]{:S(2)}) %collective-permute-start.19) | collective-permute-done | bytes 262176 | tf_op jit(solution)/shard_map/ppermute | solution.py:328
  105.7 0.6 collective-permute-done.18.rest_2_
  106.4 0.6 dense.2
  107.0 5.1 %collective-permute-done.21.rest_2_ = bf16[8,128,128]{2,1,0:T(8,128)(2,1)S(1)} collective-permute-done((bf16[8,128,128]{2,1,0:T(8,128)(2,1)S(1)}, bf16[8,128,128]{2,1,0:T(8,128)(2,1)S(1)}, u32[]{:S(2)}, u32[]{:S(2)}) %collective-permute-start.21) | collective-permute-done | bytes 262176 | tf_op jit(solution)/shard_map/ppermute | solution.py:328
  112.0 0.6 dense.3
  112.6 6.6 %spread.3 = (bf16[4,8,128,128]{3,2,1,0:T(8,128)(2,1)S(1)}, bf16[4,8,128,128]{3,2,1,0:T(8,128)(2,1)S(1)}, bf16[4,8,128,128]{3,2,1,0:T(8,128)(2,1)S(1)}, bf16[4,8,128,128]{3,2,1,0:T(8,128)(2,1)S(1)}) custom-call(s32[320]{0:T(512)S(1)} %reshape.122.cols_ref, s32[1]{0:T(128)} %bitcast.me_ref.refs_4_, bf16[16,20,128,128]{3,2,1,0:T(8,128)(2,1)} %tiles_ref.5, ...), custom_call_target="tpu_custom_call" | custom-call | flops 1342177280 | bytes 30000000 | tf_op jit(solution)/shard_map/spread/pallas_call | solution.py:107
  119.3 0.5 collective-permute-start.23
  119.8 0.2 weight_terms.1
  120.0 0.1 collective-permute-start.24
  120.1 1.8 %collective-permute-done.22 = bf16[4,8,128,128]{3,2,1,0:T(8,128)(2,1)S(1)} collective-permute-done((bf16[4,8,128,128]{3,2,1,0:T(8,128)(2,1)S(1)}, bf16[4,8,128,128]{3,2,1,0:T(8,128)(2,1)S(1)}, u32[]{:S(2)}, u32[]{:S(2)}) %collective-permute-start.22) | collective-permute-done | bytes 1048608 | tf_op jit(solution)/shard_map/ppermute | solution.py:328
  121.9 0.3 add_convert_fusion.3
  122.2 1.6 %collective-permute-start.25 = (bf16[2,8,128,128]{3,2,1,0:T(8,128)(2,1)S(1)}, bf16[2,8,128,128]{3,2,1,0:T(8,128)(2,1)S(1)}, u32[]{:S(2)}, u32[]{:S(2)}) collective-permute-start(bf16[2,8,128,128]{3,2,1,0:T(8,128)(2,1)S(1)} %get-tuple-element.132), channel_id=1, source_target_pairs={{0,16},{4,20},{8,24},{12,28},{16,0},{20,4},{24,8},{28,12},{1,17},{... | collective-permute-start | bytes 1572872 | tf_op jit(solution)/shard_map/ppermute | solution.py:328
  123.8 0.4 fusion.1
  124.2 1.8 %collective-permute-start.26 = (bf16[2,8,128,128]{3,2,1,0:T(8,128)(2,1)S(1)}, bf16[2,8,128,128]{3,2,1,0:T(8,128)(2,1)S(1)}, u32[]{:S(2)}, u32[]{:S(2)}) collective-permute-start(bf16[2,8,128,128]{3,2,1,0:T(8,128)(2,1)S(1)} %get-tuple-element.130), channel_id=1, source_target_pairs={{0,8},{4,12},{8,0},{12,4},{16,24},{20,28},{24,16},{28,20},{1,9},{5... | collective-permute-start | bytes 1572872 | tf_op jit(solution)/shard_map/ppermute | solution.py:328
  126.0 1.2 collective-permute-start.27
  127.2 11.9 %collective-permute-done.27 = bf16[128,512]{1,0:T(8,128)(2,1)S(1)} collective-permute-done((bf16[128,512]{1,0:T(8,128)(2,1)S(1)}, bf16[128,512]{1,0:T(8,128)(2,1)S(1)}, u32[]{:S(2)}, u32[]{:S(2)}) %collective-permute-start.27) | collective-permute-done | bytes 131104 | tf_op jit(solution)/shard_map/ppermute | solution.py:328
  139.1 0.1 fusion.9
  139.3 0.1 fusion.10
  139.4 1.6 %collective-permute-start.30 = (bf16[128,512]{1,0:T(8,128)(2,1)S(1)}, bf16[128,512]{1,0:T(8,128)(2,1)S(1)}, u32[]{:S(2)}, u32[]{:S(2)}) collective-permute-start(bf16[128,512]{1,0:T(8,128)(2,1)S(1)} %convert_add_fusion.3), channel_id=1, source_target_pairs={{0,8},{4,12},{8,0},{12,4},{16,24},{20,28},{24,16},{28,20},{1,9},{5... | collective-permute-start | bytes 393224 | tf_op jit(solution)/shard_map/ppermute | solution.py:328
  141.0 1.7 %collective-permute-start.29 = (bf16[8,128,128]{2,1,0:T(8,128)(2,1)S(1)}, bf16[8,128,128]{2,1,0:T(8,128)(2,1)S(1)}, u32[]{:S(2)}, u32[]{:S(2)}) collective-permute-start(bf16[8,128,128]{2,1,0:T(8,128)(2,1)S(1)} %get-tuple-element.137), channel_id=1, source_target_pairs={{0,16},{4,20},{8,24},{12,28},{16,0},{20,4},{24,8},{28,12},{1,17},{... | collective-permute-start | bytes 786440 | tf_op jit(solution)/shard_map/ppermute | solution.py:328
  142.7 0.3 collective-permute-start.28
  143.1 1.9 %collective-permute-done.30 = bf16[128,512]{1,0:T(8,128)(2,1)S(1)} collective-permute-done((bf16[128,512]{1,0:T(8,128)(2,1)S(1)}, bf16[128,512]{1,0:T(8,128)(2,1)S(1)}, u32[]{:S(2)}, u32[]{:S(2)}) %collective-permute-start.30) | collective-permute-done | bytes 131104 | tf_op jit(solution)/shard_map/ppermute | solution.py:328
  145.1 3.3 %collective-permute-done.29.refs_3_ = bf16[8,128,128]{2,1,0:T(8,128)(2,1)S(1)} collective-permute-done((bf16[8,128,128]{2,1,0:T(8,128)(2,1)S(1)}, bf16[8,128,128]{2,1,0:T(8,128)(2,1)S(1)}, u32[]{:S(2)}, u32[]{:S(2)}) %collective-permute-start.29) | collective-permute-done | bytes 262176 | tf_op jit(solution)/shard_map/ppermute | solution.py:328
  148.4 1.7 %collective-permute-done.28.refs_1_ = bf16[8,128,128]{2,1,0:T(8,128)(2,1)S(1)} collective-permute-done((bf16[8,128,128]{2,1,0:T(8,128)(2,1)S(1)}, bf16[8,128,128]{2,1,0:T(8,128)(2,1)S(1)}, u32[]{:S(2)}, u32[]{:S(2)}) %collective-permute-start.28) | collective-permute-done | bytes 262176 | tf_op jit(solution)/shard_map/ppermute | solution.py:328
  150.1 1.2 finish.3
  (54 shorter events, 0.9 us)
Async XLA Ops:
  1.4 1.0 copy-start.1
  2.5 39.0 %copy-start.2 = (bf16[2048,128]{1,0:T(8,128)(2,1)S(1)}, bf16[2048,128]{1,0:T(8,128)(2,1)}, u32[]{:S(2)}) copy-start(bf16[2048,128]{1,0:T(8,128)(2,1)} %param.8) | copy-start | bytes 1572868
  2.5 63.1 %copy-start.7 = (bf16[128,512]{1,0:T(8,128)(2,1)S(1)}, bf16[128,512]{1,0:T(8,128)(2,1)}, u32[]{:S(2)}) copy-start(bf16[128,512]{1,0:T(8,128)(2,1)} %param.14) | copy-start | bytes 393220
  2.5 63.1 %copy-start.8 = (bf16[128,512]{1,0:T(8,128)(2,1)S(1)}, bf16[128,512]{1,0:T(8,128)(2,1)}, u32[]{:S(2)}) copy-start(bf16[128,512]{1,0:T(8,128)(2,1)} %param.15) | copy-start | bytes 393220
  2.5 63.8 %copy-start = (bf16[2048,128]{1,0:T(8,128)(2,1)S(1)}, bf16[2048,128]{1,0:T(8,128)(2,1)}, u32[]{:S(2)}) copy-start(bf16[2048,128]{1,0:T(8,128)(2,1)} %param.9) | copy-start | bytes 1572868
  9.4 55.7 %copy-start.3 = (bf16[16,128,128]{2,1,0:T(8,128)(2,1)}, bf16[16,128,128]{2,1,0:T(8,128)(2,1)S(1)}, u32[]{:S(2)}) copy-start(bf16[16,128,128]{2,1,0:T(8,128)(2,1)S(1)} %get-tuple-element.78.rest_4_) | copy-start | bytes 1572868
  9.4 2.8 %collective-permute-start = (bf16[4,8,128,128]{3,2,1,0:T(8,128)(2,1)S(1)}, bf16[4,8,128,128]{3,2,1,0:T(8,128)(2,1)S(1)}, u32[]{:S(2)}, u32[]{:S(2)}) collective-permute-start(bf16[4,8,128,128]{3,2,1,0:T(8,128)(2,1)S(1)} %get-tuple-element.67), channel_id=1, source_target_pairs={{0,4},{4,0},{8,12},{12,8},{16,20},{20,16},{24,28},{28,24},{1,5},{5... | collective-permute-start | bytes 3145736 | tf_op jit(solution)/shard_map/ppermute | solution.py:328
  9.9 5.7 %collective-permute-start.3 = (bf16[4,8,128,128]{3,2,1,0:T(8,128)(2,1)S(1)}, bf16[4,8,128,128]{3,2,1,0:T(8,128)(2,1)S(1)}, u32[]{:S(2)}, u32[]{:S(2)}) collective-permute-start(bf16[4,8,128,128]{3,2,1,0:T(8,128)(2,1)S(1)} %get-tuple-element.69), channel_id=1, source_target_pairs={{0,4},{4,0},{8,12},{12,8},{16,20},{20,16},{24,28},{28,24},{1,5},{5... | collective-permute-start | bytes 3145736 | tf_op jit(solution)/shard_map/ppermute | solution.py:328
  12.7 15.2 %collective-permute-start.1 = (bf16[2,8,128,128]{3,2,1,0:T(8,128)(2,1)S(1)}, bf16[2,8,128,128]{3,2,1,0:T(8,128)(2,1)S(1)}, u32[]{:S(2)}, u32[]{:S(2)}) collective-permute-start(bf16[2,8,128,128]{3,2,1,0:T(8,128)(2,1)S(1)} %get-tuple-element.136), channel_id=1, source_target_pairs={{0,16},{4,20},{8,24},{12,28},{16,0},{20,4},{24,8},{28,12},{1,17},{... | collective-permute-start | bytes 1572872 | tf_op jit(solution)/shard_map/ppermute | solution.py:328
  16.0 13.8 %collective-permute-start.4 = (bf16[2,8,128,128]{3,2,1,0:T(8,128)(2,1)S(1)}, bf16[2,8,128,128]{3,2,1,0:T(8,128)(2,1)S(1)}, u32[]{:S(2)}, u32[]{:S(2)}) collective-permute-start(bf16[2,8,128,128]{3,2,1,0:T(8,128)(2,1)S(1)} %get-tuple-element.134), channel_id=1, source_target_pairs={{0,8},{4,12},{8,0},{12,4},{16,24},{20,28},{24,16},{28,20},{1,9},{5... | collective-permute-start | bytes 1572872 | tf_op jit(solution)/shard_map/ppermute | solution.py:328
  28.0 7.9 %collective-permute-start.2 = (bf16[8,128,128]{2,1,0:T(8,128)(2,1)S(1)}, bf16[8,128,128]{2,1,0:T(8,128)(2,1)S(1)}, u32[]{:S(2)}, u32[]{:S(2)}) collective-permute-start(bf16[8,128,128]{2,1,0:T(8,128)(2,1)S(1)} %get-tuple-element.143), channel_id=1, source_target_pairs={{0,8},{4,12},{8,0},{12,4},{16,24},{20,28},{24,16},{28,20},{1,9},{5... | collective-permute-start | bytes 786440 | tf_op jit(solution)/shard_map/ppermute | solution.py:328
  29.9 7.3 %collective-permute-start.5 = (bf16[8,128,128]{2,1,0:T(8,128)(2,1)S(1)}, bf16[8,128,128]{2,1,0:T(8,128)(2,1)S(1)}, u32[]{:S(2)}, u32[]{:S(2)}) collective-permute-start(bf16[8,128,128]{2,1,0:T(8,128)(2,1)S(1)} %get-tuple-element.141), channel_id=1, source_target_pairs={{0,16},{4,20},{8,24},{12,28},{16,0},{20,4},{24,8},{28,12},{1,17},{... | collective-permute-start | bytes 786440 | tf_op jit(solution)/shard_map/ppermute | solution.py:328
  37.4 14.0 %collective-permute-start.8 = (bf16[16,128,128]{2,1,0:T(8,128)(2,1)S(1)}, bf16[16,128,128]{2,1,0:T(8,128)(2,1)S(1)}, u32[]{:S(2)}, u32[]{:S(2)}) collective-permute-start(bf16[16,128,128]{2,1,0:T(8,128)(2,1)S(1)} %finish.2.rest_0_), channel_id=1, source_target_pairs={{0,1},{1,0},{2,3},{3,2},{4,5},{5,4},{6,7},{7,6},{8,9},{9,8},{10,11... | collective-permute-start | bytes 1572872 | tf_op jit(solution)/shard_map/ppermute | solution.py:328
  39.0 23.8 %collective-permute-start.6 = (bf16[16,128,128]{2,1,0:T(8,128)(2,1)S(1)}, bf16[16,128,128]{2,1,0:T(8,128)(2,1)}, u32[]{:S(2)}, u32[]{:S(2)}) collective-permute-start(bf16[16,128,128]{2,1,0:T(8,128)(2,1)S(1)} %finish.2.rest_0_), channel_id=1, source_target_pairs={{0,3},{1,2},{2,1},{3,0},{4,7},{5,6},{6,5},{7,4},{8,11},{9,10},{10,... | collective-permute-start | bytes 1572872 | tf_op jit(solution)/shard_map/ppermute | solution.py:328
  41.5 21.9 %collective-permute-start.14 = (bf16[16,128,128]{2,1,0:T(8,128)(2,1)S(1)}, bf16[16,128,128]{2,1,0:T(8,128)(2,1)S(1)}, u32[]{:S(2)}, u32[]{:S(2)}) collective-permute-start(bf16[16,128,128]{2,1,0:T(8,128)(2,1)S(1)} %bitcast.88), channel_id=1, source_target_pairs={{0,24},{4,28},{8,16},{12,20},{16,8},{20,12},{24,0},{28,4},{1,25},{... | collective-permute-start | bytes 1572872 | tf_op jit(solution)/shard_map/ppermute | solution.py:328
  43.9 21.1 %collective-permute-start.12 = (bf16[16,128,128]{2,1,0:T(8,128)(2,1)S(1)}, bf16[16,128,128]{2,1,0:T(8,128)(2,1)S(1)}, u32[]{:S(2)}, u32[]{:S(2)}) collective-permute-start(bf16[16,128,128]{2,1,0:T(8,128)(2,1)S(1)} %bitcast.89), channel_id=1, source_target_pairs={{0,16},{4,20},{8,24},{12,28},{16,0},{20,4},{24,8},{28,12},{1,17},{... | collective-permute-start | bytes 1572872 | tf_op jit(solution)/shard_map/ppermute | solution.py:328
  44.3 20.8 %collective-permute-start.10 = (bf16[16,128,128]{2,1,0:T(8,128)(2,1)S(1)}, bf16[16,128,128]{2,1,0:T(8,128)(2,1)S(1)}, u32[]{:S(2)}, u32[]{:S(2)}) collective-permute-start(bf16[16,128,128]{2,1,0:T(8,128)(2,1)S(1)} %bitcast.90), channel_id=1, source_target_pairs={{0,8},{4,12},{8,0},{12,4},{16,24},{20,28},{24,16},{28,20},{1,9},{5... | collective-permute-start | bytes 1572872 | tf_op jit(solution)/shard_map/ppermute | solution.py:328
  51.4 0.8 copy-start.5
  52.2 18.1 %collective-permute-start.9 = (bf16[16,128,128]{2,1,0:T(8,128)(2,1)S(1)}, bf16[16,128,128]{2,1,0:T(8,128)(2,1)}, u32[]{:S(2)}, u32[]{:S(2)}) collective-permute-start(bf16[16,128,128]{2,1,0:T(8,128)(2,1)S(1)} %bitcast.91), channel_id=1, source_target_pairs={{0,4},{4,0},{8,12},{12,8},{16,20},{20,16},{24,28},{28,24},{1,5},{5... | collective-permute-start | bytes 1572872 | tf_op jit(solution)/shard_map/ppermute | solution.py:328
  62.8 11.3 %collective-permute-start.7 = (bf16[16,128,128]{2,1,0:T(8,128)(2,1)}, bf16[16,128,128]{2,1,0:T(8,128)(2,1)}, u32[]{:S(2)}, u32[]{:S(2)}) collective-permute-start(bf16[16,128,128]{2,1,0:T(8,128)(2,1)} %collective-permute-done.6.rest_2_), channel_id=1, source_target_pairs={{0,1},{1,0},{2,3},{3,2},{4,5},{5,4},{6,7},{7,6},{8,9},{9,8},{10,11... | collective-permute-start | bytes 1572872 | tf_op jit(solution)/shard_map/ppermute | solution.py:328
  63.4 10.7 %collective-permute-start.15 = (bf16[16,128,128]{2,1,0:T(8,128)(2,1)S(1)}, bf16[16,128,128]{2,1,0:T(8,128)(2,1)}, u32[]{:S(2)}, u32[]{:S(2)}) collective-permute-start(bf16[16,128,128]{2,1,0:T(8,128)(2,1)S(1)} %collective-permute-done.14.rest_6_), channel_id=1, source_target_pairs={{0,4},{4,0},{8,12},{12,8},{16,20},{20,16},{24,28},{28,24},{1,5},{5... | collective-permute-start | bytes 1572872 | tf_op jit(solution)/shard_map/ppermute | solution.py:328
  65.0 9.1 %collective-permute-start.13 = (bf16[16,128,128]{2,1,0:T(8,128)(2,1)S(1)}, bf16[16,128,128]{2,1,0:T(8,128)(2,1)}, u32[]{:S(2)}, u32[]{:S(2)}) collective-permute-start(bf16[16,128,128]{2,1,0:T(8,128)(2,1)S(1)} %collective-permute-done.12.rest_4_), channel_id=1, source_target_pairs={{0,4},{4,0},{8,12},{12,8},{16,20},{20,16},{24,28},{28,24},{1,5},{5... | collective-permute-start | bytes 1572872 | tf_op jit(solution)/shard_map/ppermute | solution.py:328
  65.1 9.0 %collective-permute-start.11 = (bf16[16,128,128]{2,1,0:T(8,128)(2,1)S(1)}, bf16[16,128,128]{2,1,0:T(8,128)(2,1)}, u32[]{:S(2)}, u32[]{:S(2)}) collective-permute-start(bf16[16,128,128]{2,1,0:T(8,128)(2,1)S(1)} %collective-permute-done.10.rest_2_), channel_id=1, source_target_pairs={{0,4},{4,0},{8,12},{12,8},{16,20},{20,16},{24,28},{28,24},{1,5},{5... | collective-permute-start | bytes 1572872 | tf_op jit(solution)/shard_map/ppermute | solution.py:328
  66.3 1.0 copy-start.4
  67.3 1.0 copy-start.6
  75.6 14.2 %collective-permute-start.17 = (bf16[8,128,128]{2,1,0:T(8,128)(2,1)S(1)}, bf16[8,128,128]{2,1,0:T(8,128)(2,1)S(1)}, u32[]{:S(2)}, u32[]{:S(2)}) collective-permute-start(bf16[8,128,128]{2,1,0:T(8,128)(2,1)S(1)} %get-tuple-element.90.rest_0_), channel_id=1, source_target_pairs={{0,1},{1,0},{2,3},{3,2},{4,5},{5,4},{6,7},{7,6},{8,9},{9,8},{10,11... | collective-permute-start | bytes 786440 | tf_op jit(solution)/shard_map/ppermute | solution.py:328
  76.0 18.4 %collective-permute-start.16 = (bf16[8,128,128]{2,1,0:T(8,128)(2,1)S(1)}, bf16[8,128,128]{2,1,0:T(8,128)(2,1)S(1)}, u32[]{:S(2)}, u32[]{:S(2)}) collective-permute-start(bf16[8,128,128]{2,1,0:T(8,128)(2,1)S(1)} %get-tuple-element.90.rest_0_), channel_id=1, source_target_pairs={{0,3},{1,2},{2,1},{3,0},{4,7},{5,6},{6,5},{7,4},{8,11},{9,10},{10,... | collective-permute-start | bytes 786440 | tf_op jit(solution)/shard_map/ppermute | solution.py:328
  81.5 13.7 %collective-permute-start.20 = (bf16[8,128,128]{2,1,0:T(8,128)(2,1)S(1)}, bf16[8,128,128]{2,1,0:T(8,128)(2,1)S(1)}, u32[]{:S(2)}, u32[]{:S(2)}) collective-permute-start(bf16[8,128,128]{2,1,0:T(8,128)(2,1)S(1)} %get-tuple-element.103.rest_0_), channel_id=1, source_target_pairs={{0,1},{1,0},{2,3},{3,2},{4,5},{5,4},{6,7},{7,6},{8,9},{9,8},{10,11... | collective-permute-start | bytes 786440 | tf_op jit(solution)/shard_map/ppermute | solution.py:328
  82.4 23.3 %collective-permute-start.19 = (bf16[8,128,128]{2,1,0:T(8,128)(2,1)S(1)}, bf16[8,128,128]{2,1,0:T(8,128)(2,1)S(1)}, u32[]{:S(2)}, u32[]{:S(2)}) collective-permute-start(bf16[8,128,128]{2,1,0:T(8,128)(2,1)S(1)} %get-tuple-element.103.rest_0_), channel_id=1, source_target_pairs={{0,3},{1,2},{2,1},{3,0},{4,7},{5,6},{6,5},{7,4},{8,11},{9,10},{10,... | collective-permute-start | bytes 786440 | tf_op jit(solution)/shard_map/ppermute | solution.py:328
  94.4 12.0 %collective-permute-start.18 = (bf16[8,128,128]{2,1,0:T(8,128)(2,1)S(1)}, bf16[8,128,128]{2,1,0:T(8,128)(2,1)S(1)}, u32[]{:S(2)}, u32[]{:S(2)}) collective-permute-start(bf16[8,128,128]{2,1,0:T(8,128)(2,1)S(1)} %collective-permute-done.16.rest_3_), channel_id=1, source_target_pairs={{0,1},{1,0},{2,3},{3,2},{4,5},{5,4},{6,7},{7,6},{8,9},{9,8},{10,11... | collective-permute-start | bytes 786440 | tf_op jit(solution)/shard_map/ppermute | solution.py:328
  105.7 6.4 %collective-permute-start.21 = (bf16[8,128,128]{2,1,0:T(8,128)(2,1)S(1)}, bf16[8,128,128]{2,1,0:T(8,128)(2,1)S(1)}, u32[]{:S(2)}, u32[]{:S(2)}) collective-permute-start(bf16[8,128,128]{2,1,0:T(8,128)(2,1)S(1)} %collective-permute-done.19.rest_3_), channel_id=1, source_target_pairs={{0,1},{1,0},{2,3},{3,2},{4,5},{5,4},{6,7},{7,6},{8,9},{9,8},{10,11... | collective-permute-start | bytes 786440 | tf_op jit(solution)/shard_map/ppermute | solution.py:328
  119.2 2.7 %collective-permute-start.22 = (bf16[4,8,128,128]{3,2,1,0:T(8,128)(2,1)S(1)}, bf16[4,8,128,128]{3,2,1,0:T(8,128)(2,1)S(1)}, u32[]{:S(2)}, u32[]{:S(2)}) collective-permute-start(bf16[4,8,128,128]{3,2,1,0:T(8,128)(2,1)S(1)} %get-tuple-element.108), channel_id=1, source_target_pairs={{0,4},{4,0},{8,12},{12,8},{16,20},{20,16},{24,28},{28,24},{1,5},{5... | collective-permute-start | bytes 3145736 | tf_op jit(solution)/shard_map/ppermute | solution.py:328
  119.3 4.6 %collective-permute-start.23 = (bf16[4,8,128,128]{3,2,1,0:T(8,128)(2,1)S(1)}, bf16[4,8,128,128]{3,2,1,0:T(8,128)(2,1)S(1)}, u32[]{:S(2)}, u32[]{:S(2)}) collective-permute-start(bf16[4,8,128,128]{3,2,1,0:T(8,128)(2,1)S(1)} %get-tuple-element.110), channel_id=1, source_target_pairs={{0,4},{4,0},{8,12},{12,8},{16,20},{20,16},{24,28},{28,24},{1,5},{5... | collective-permute-start | bytes 3145736 | tf_op jit(solution)/shard_map/ppermute | solution.py:328
  120.0 6.0 %collective-permute-start.24 = (bf16[128,512]{1,0:T(8,128)(2,1)S(1)}, bf16[128,512]{1,0:T(8,128)(2,1)S(1)}, u32[]{:S(2)}, u32[]{:S(2)}) collective-permute-start(bf16[128,512]{1,0:T(8,128)(2,1)S(1)} %get-tuple-element.116), channel_id=1, source_target_pairs={{0,4},{4,0},{8,12},{12,8},{16,20},{20,16},{24,28},{28,24},{1,5},{5... | collective-permute-start | bytes 393224 | tf_op jit(solution)/shard_map/ppermute | solution.py:328
  122.2 16.9 %collective-permute-start.25 = (bf16[2,8,128,128]{3,2,1,0:T(8,128)(2,1)S(1)}, bf16[2,8,128,128]{3,2,1,0:T(8,128)(2,1)S(1)}, u32[]{:S(2)}, u32[]{:S(2)}) collective-permute-start(bf16[2,8,128,128]{3,2,1,0:T(8,128)(2,1)S(1)} %get-tuple-element.132), channel_id=1, source_target_pairs={{0,16},{4,20},{8,24},{12,28},{16,0},{20,4},{24,8},{28,12},{1,17},{... | collective-permute-start | bytes 1572872 | tf_op jit(solution)/shard_map/ppermute | solution.py:328
  124.2 14.9 %collective-permute-start.26 = (bf16[2,8,128,128]{3,2,1,0:T(8,128)(2,1)S(1)}, bf16[2,8,128,128]{3,2,1,0:T(8,128)(2,1)S(1)}, u32[]{:S(2)}, u32[]{:S(2)}) collective-permute-start(bf16[2,8,128,128]{3,2,1,0:T(8,128)(2,1)S(1)} %get-tuple-element.130), channel_id=1, source_target_pairs={{0,8},{4,12},{8,0},{12,4},{16,24},{20,28},{24,16},{28,20},{1,9},{5... | collective-permute-start | bytes 1572872 | tf_op jit(solution)/shard_map/ppermute | solution.py:328
  126.0 13.1 %collective-permute-start.27 = (bf16[128,512]{1,0:T(8,128)(2,1)S(1)}, bf16[128,512]{1,0:T(8,128)(2,1)S(1)}, u32[]{:S(2)}, u32[]{:S(2)}) collective-permute-start(bf16[128,512]{1,0:T(8,128)(2,1)S(1)} %convert_add_fusion.4), channel_id=1, source_target_pairs={{0,16},{4,20},{8,24},{12,28},{16,0},{20,4},{24,8},{28,12},{1,17},{... | collective-permute-start | bytes 393224 | tf_op jit(solution)/shard_map/ppermute | solution.py:328
  139.4 5.5 %collective-permute-start.30 = (bf16[128,512]{1,0:T(8,128)(2,1)S(1)}, bf16[128,512]{1,0:T(8,128)(2,1)S(1)}, u32[]{:S(2)}, u32[]{:S(2)}) collective-permute-start(bf16[128,512]{1,0:T(8,128)(2,1)S(1)} %convert_add_fusion.3), channel_id=1, source_target_pairs={{0,8},{4,12},{8,0},{12,4},{16,24},{20,28},{24,16},{28,20},{1,9},{5... | collective-permute-start | bytes 393224 | tf_op jit(solution)/shard_map/ppermute | solution.py:328
  141.0 7.4 %collective-permute-start.29 = (bf16[8,128,128]{2,1,0:T(8,128)(2,1)S(1)}, bf16[8,128,128]{2,1,0:T(8,128)(2,1)S(1)}, u32[]{:S(2)}, u32[]{:S(2)}) collective-permute-start(bf16[8,128,128]{2,1,0:T(8,128)(2,1)S(1)} %get-tuple-element.137), channel_id=1, source_target_pairs={{0,16},{4,20},{8,24},{12,28},{16,0},{20,4},{24,8},{28,12},{1,17},{... | collective-permute-start | bytes 786440 | tf_op jit(solution)/shard_map/ppermute | solution.py:328
  142.7 7.4 %collective-permute-start.28 = (bf16[8,128,128]{2,1,0:T(8,128)(2,1)S(1)}, bf16[8,128,128]{2,1,0:T(8,128)(2,1)S(1)}, u32[]{:S(2)}, u32[]{:S(2)}) collective-permute-start(bf16[8,128,128]{2,1,0:T(8,128)(2,1)S(1)} %get-tuple-element.139), channel_id=1, source_target_pairs={{0,8},{4,12},{8,0},{12,4},{16,24},{20,28},{24,16},{28,20},{1,9},{5... | collective-permute-start | bytes 786440 | tf_op jit(solution)/shard_map/ppermute | solution.py:328
  145.0 5.1 %collective-permute-start.31 = (f32[128,512]{1,0:T(8,128)S(1)}, f32[128,512]{1,0:T(8,128)S(1)}, u32[]{:S(2)}, u32[]{:S(2)}) collective-permute-start(f32[128,512]{1,0:T(8,128)S(1)} %convert_add_fusion.2.refs_5_), channel_id=1, source_target_pairs={{0,4},{4,0},{8,12},{12,8},{16,20},{20,16},{24,28},{28,24},{1,5},{5... | collective-permute-start | bytes 786440 | tf_op jit(solution)/shard_map/ppermute | solution.py:328

commit v17 on v16

--- a/solution.py
+++ b/solution.py
@@ -406,9 +406,10 @@
     inputs, firsts = [], []
     shards = []
     for g in range(GROUPS):
-        arrived, beside = gather_columns(deltas[g], cols, agg_feats if g == 0 else ())
+        arrived, beside = gather_columns(deltas[g], cols, agg_feats if g == 0 else (), g == 0)
         agg_feats = beside if g == 0 else agg_feats
         shards.append(arrived)
+    shards[0][2], shards[1][1] = after((shards[0][2], shards[1][1]))
     for g in range(GROUPS):
         out, grad = dense(weight_one, shards[g], cut(agg_feats, g), None, col_at, 1)
         inputs.append(out)

time: 152 us -> 152 us (level)
  waiting for transfers between devices: 82.2 us -> 72.7 us
  starting transfers between devices: 34.5 us -> 43.4 us
    ppermute x32, waiting for transfers between devices: 82.2 us -> 72.7 us  [swap(): lax.ppermute(value, axis, [(i, i ^ mask) for i in range(lax.axis_size(axi...]
    ppermute x32, starting transfers between devices: 34.5 us -> 43.4 us  [swap(): lax.ppermute(value, axis, [(i, i ^ mask) for i in range(lax.axis_size(axi...]
  transfers between devices with their start and end apart: 32 -> 32, of which waited for: 18 -> 17; matrix products, arithmetic and copies ran while one was open for 2% -> 2% of each run, Pallas kernels for 6% -> 6%
where the time goes in v17:
time: 152 us; the launch traced here: 151 us
  waiting for transfers between devices  72.7 us (48%)
  starting transfers between devices  43.4 us (29%)
  Pallas kernels  26.1 us (17%)
  local copies, waits for them, and re-layouts  5.42 us (4%)
  other arithmetic  2.17 us (1%)
    ppermute x32, waiting for transfers between devices, swap(): lax.ppermute(value, axis, [(i, i ^ mask) for i in range(lax.axis_size(axi...  72.7 us
    ppermute x32, starting transfers between devices, swap(): lax.ppermute(value, axis, [(i, i ^ mask) for i in range(lax.axis_size(axi...  43.4 us
    pallas_call x2, Pallas kernels, spread(): pl.pallas_call(functools.partial(spread_kernel, first, len(vals)), out_sh...  13.5 us
    pallas_call x1, Pallas kernels, aggregate(): pl.pallas_call(aggregate_kernel, out_shape=jax.ShapeDtypeStruct((blocks,...  6.48 us
    unnamed x26, local copies, waits for them, and re-layouts  3.98 us
  transfers between devices with their start and end apart: 32, of which 17 were waited for; matrix products, arithmetic and copies ran while one was open for 2% of the time, Pallas kernels for 6%

profile of v17, /device:TPU:0, one launch (start us, length us, event | category | flops | bytes accessed | tf_op | source)
XLA Modules:
  0.0 150.8 jit_solution(8691747531960104875)
XLA Ops:
  0.6 0.8 reshape.122.cols_ref
  1.4 1.0 copy-done.1
  2.5 6.9 %spread.2 = (bf16[4,8,128,128]{3,2,1,0:T(8,128)(2,1)S(1)}, bf16[4,8,128,128]{3,2,1,0:T(8,128)(2,1)S(1)}, bf16[4,8,128,128]{3,2,1,0:T(8,128)(2,1)S(1)}, bf16[4,8,...) custom-call(s32[320]{0:T(512)S(1)} %reshape.122.cols_ref, s32[1]{0:T(128)} %bitcast.me_ref.refs_4_, ...), custom_call_target="tpu_custom_call" | custom-call | flops 1342177280 | bytes 30000000 | tf_op jit(solution)/shard_map/spread/pallas_call | solution.py:107
  9.4 0.5 collective-permute-start
  10.0 2.2 %collective-permute-done = bf16[4,8,128,128]{3,2,1,0:T(8,128)(2,1)S(1)} collective-permute-done((bf16[4,8,128,128]{3,2,1,0:T(8,128)(2,1)S(1)}, bf16[4,8,128,128]{3,2,1,0:T(8,128)(2,1)S(1)}, u32[]{:S(2)}, u32[]{:S(2)}) %collective-permute-start) | collective-permute-done | bytes 1048608 | tf_op jit(solution)/shard_map/ppermute | solution.py:328
  12.2 0.5 add_convert_fusion.7
  12.7 3.0 %collective-permute-start.1 = (bf16[2,8,128,128]{3,2,1,0:T(8,128)(2,1)S(1)}, bf16[2,8,128,128]{3,2,1,0:T(8,128)(2,1)S(1)}, u32[]{:S(2)}, u32[]{:S(2)}) collective-permute-start(bf16[2,8,128,128]{3,2,1,0:T(8,128)(2,1)S(1)} %get-tuple-element.136), channel_id=1, source_target_pairs={{0,16},{4,20},{8,24},{12,28},{16,0},{20,4},{24,8},{28,12},{1,17},{... | collective-permute-start | bytes 1572872 | tf_op jit(solution)/shard_map/ppermute | solution.py:328
  15.6 0.3 add_convert_fusion.5
  16.0 1.6 %collective-permute-start.4 = (bf16[2,8,128,128]{3,2,1,0:T(8,128)(2,1)S(1)}, bf16[2,8,128,128]{3,2,1,0:T(8,128)(2,1)S(1)}, u32[]{:S(2)}, u32[]{:S(2)}) collective-permute-start(bf16[2,8,128,128]{3,2,1,0:T(8,128)(2,1)S(1)} %get-tuple-element.134), channel_id=1, source_target_pairs={{0,8},{4,12},{8,0},{12,4},{16,24},{20,28},{24,16},{28,20},{1,9},{5... | collective-permute-start | bytes 1572872 | tf_op jit(solution)/shard_map/ppermute | solution.py:328
  17.5 10.3 %collective-permute-done.1 = bf16[2,8,128,128]{3,2,1,0:T(8,128)(2,1)S(1)} collective-permute-done((bf16[2,8,128,128]{3,2,1,0:T(8,128)(2,1)S(1)}, bf16[2,8,128,128]{3,2,1,0:T(8,128)(2,1)S(1)}, u32[]{:S(2)}, u32[]{:S(2)}) %collective-permute-start.1) | collective-permute-done | bytes 524320 | tf_op jit(solution)/shard_map/ppermute | solution.py:328
  27.9 0.1 fusion.6
  28.0 1.8 %collective-permute-start.2 = (bf16[8,128,128]{2,1,0:T(8,128)(2,1)S(1)}, bf16[8,128,128]{2,1,0:T(8,128)(2,1)S(1)}, u32[]{:S(2)}, u32[]{:S(2)}) collective-permute-start(bf16[8,128,128]{2,1,0:T(8,128)(2,1)S(1)} %get-tuple-element.143), channel_id=1, source_target_pairs={{0,8},{4,12},{8,0},{12,4},{16,24},{20,28},{24,16},{28,20},{1,9},{5... | collective-permute-start | bytes 786440 | tf_op jit(solution)/shard_map/ppermute | solution.py:328
  29.8 0.1 fusion.12
  29.9 1.6 %collective-permute-start.5 = (bf16[8,128,128]{2,1,0:T(8,128)(2,1)S(1)}, bf16[8,128,128]{2,1,0:T(8,128)(2,1)S(1)}, u32[]{:S(2)}, u32[]{:S(2)}) collective-permute-start(bf16[8,128,128]{2,1,0:T(8,128)(2,1)S(1)} %get-tuple-element.141), channel_id=1, source_target_pairs={{0,16},{4,20},{8,24},{12,28},{16,0},{20,4},{24,8},{28,12},{1,17},{... | collective-permute-start | bytes 786440 | tf_op jit(solution)/shard_map/ppermute | solution.py:328
  31.5 4.4 %collective-permute-done.2.refs_1_ = bf16[8,128,128]{2,1,0:T(8,128)(2,1)S(1)} collective-permute-done((bf16[8,128,128]{2,1,0:T(8,128)(2,1)S(1)}, bf16[8,128,128]{2,1,0:T(8,128)(2,1)S(1)}, u32[]{:S(2)}, u32[]{:S(2)}) %collective-permute-start.2) | collective-permute-done | bytes 262176 | tf_op jit(solution)/shard_map/ppermute | solution.py:328
  35.9 1.3 collective-permute-done.5.refs_3_
  37.4 1.6 %collective-permute-start.8 = (bf16[16,128,128]{2,1,0:T(8,128)(2,1)S(1)}, bf16[16,128,128]{2,1,0:T(8,128)(2,1)S(1)}, u32[]{:S(2)}, u32[]{:S(2)}) collective-permute-start(bf16[16,128,128]{2,1,0:T(8,128)(2,1)S(1)} %finish.2.rest_0_), channel_id=1, source_target_pairs={{0,1},{1,0},{2,3},{3,2},{4,5},{5,4},{6,7},{7,6},{8,9},{9,8},{10,11... | collective-permute-start | bytes 1572872 | tf_op jit(solution)/shard_map/ppermute | solution.py:328
  39.0 2.5 %collective-permute-start.6 = (bf16[16,128,128]{2,1,0:T(8,128)(2,1)S(1)}, bf16[16,128,128]{2,1,0:T(8,128)(2,1)}, u32[]{:S(2)}, u32[]{:S(2)}) collective-permute-start(bf16[16,128,128]{2,1,0:T(8,128)(2,1)S(1)} %finish.2.rest_0_), channel_id=1, source_target_pairs={{0,3},{1,2},{2,1},{3,0},{4,7},{5,6},{6,5},{7,4},{8,11},{9,10},{10,... | collective-permute-start | bytes 1572872 | tf_op jit(solution)/shard_map/ppermute | solution.py:328
  41.5 2.4 %collective-permute-start.14 = (bf16[16,128,128]{2,1,0:T(8,128)(2,1)S(1)}, bf16[16,128,128]{2,1,0:T(8,128)(2,1)S(1)}, u32[]{:S(2)}, u32[]{:S(2)}) collective-permute-start(bf16[16,128,128]{2,1,0:T(8,128)(2,1)S(1)} %bitcast.88), channel_id=1, source_target_pairs={{0,24},{4,28},{8,16},{12,20},{16,8},{20,12},{24,0},{28,4},{1,25},{... | collective-permute-start | bytes 1572872 | tf_op jit(solution)/shard_map/ppermute | solution.py:328
  43.9 0.5 collective-permute-start.12
  44.3 0.6 collective-permute-start.10
  45.0 6.4 %collective-permute-done.8.rest_1_ = bf16[16,128,128]{2,1,0:T(8,128)(2,1)S(1)} collective-permute-done((bf16[16,128,128]{2,1,0:T(8,128)(2,1)S(1)}, bf16[16,128,128]{2,1,0:T(8,128)(2,1)S(1)}, u32[]{:S(2)}, u32[]{:S(2)}) %collective-permute-start.8) | collective-permute-done | bytes 524320 | tf_op jit(solution)/shard_map/ppermute | solution.py:328
  51.4 0.8 copy-done.5
  52.2 10.7 %collective-permute-done.6.rest_2_ = bf16[16,128,128]{2,1,0:T(8,128)(2,1)} collective-permute-done((bf16[16,128,128]{2,1,0:T(8,128)(2,1)S(1)}, bf16[16,128,128]{2,1,0:T(8,128)(2,1)}, u32[]{:S(2)}, u32[]{:S(2)}) %collective-permute-start.6) | collective-permute-done | bytes 524320 | tf_op jit(solution)/shard_map/ppermute | solution.py:328
  62.8 0.6 collective-permute-start.7
  63.4 1.6 %collective-permute-done.12.rest_4_ = bf16[16,128,128]{2,1,0:T(8,128)(2,1)S(1)} collective-permute-done((bf16[16,128,128]{2,1,0:T(8,128)(2,1)S(1)}, bf16[16,128,128]{2,1,0:T(8,128)(2,1)S(1)}, u32[]{:S(2)}, u32[]{:S(2)}) %collective-permute-start.12) | collective-permute-done | bytes 524320 | tf_op jit(solution)/shard_map/ppermute | solution.py:328
  65.1 0.4 collective-permute-start.11
  65.6 0.6 constant_dynamic-slice_fusion.3
  66.3 1.0 copy-done.4
  67.3 1.0 copy-done.6
  68.4 1.9 %dense_early.1 = (f32[2,128,1024]{2,1,0:T(8,128)S(1)}, f32[4,128,128]{2,1,0:T(8,128)S(1)}, bf16[16,128,128]{2,1,0:T(8,128)(2,1)S(1)}) custom-call(s32[1]{0:T(128)} %bitcast.1.col_ref, bf16[128,512]{1,0:T(8,128)(2,1)S(1)} %pad_maximum_fusion.1.weight_ref, bf16[16,128,128]{2,1,0:T(8,128)(2,1)S(1)} %finish.2.rest_0_, bf16[16,128,128]{2,1,0:T(8,128)(2,1)S(1)} %copy-done.6, ...), custom_call_target="tpu_custom_call" | custom-call | tf_op jit(solution)/shard_map/dense_early/pallas_call | solution.py:257
  70.3 3.8 %collective-permute-done.7.shard_ref = bf16[16,128,128]{2,1,0:T(8,128)(2,1)} collective-permute-done((bf16[16,128,128]{2,1,0:T(8,128)(2,1)}, bf16[16,128,128]{2,1,0:T(8,128)(2,1)}, u32[]{:S(2)}, u32[]{:S(2)}) %collective-permute-start.7) | collective-permute-done | bytes 524320 | tf_op jit(solution)/shard_map/ppermute | solution.py:328
  74.1 1.5 %dense_late.1 = (bf16[8,128,128]{2,1,0:T(8,128)(2,1)S(1)}, bf16[8,128,128]{2,1,0:T(8,128)(2,1)S(1)}, f32[128,128]{1,0:T(8,128)S(1)}) custom-call(bf16[128,512]{1,0:T(8,128)(2,1)S(1)} %pad_maximum_fusion.1.weight_ref, bf16[16,128,128]{2,1,0:T(8,128)(2,1)} %collective-permute-done.7.shard_ref, f32[2,128,1024]{2,1,0:T(8,128)S(1)} %get-tuple-element.79.part_ref, ...), custom_call_target="tpu_custom_call" | custom-call | tf_op jit(solution)/shard_map/dense_late/pallas_call | solution.py:290
  75.6 0.3 collective-permute-start.17
  76.0 5.5 %collective-permute-start.16 = (bf16[8,128,128]{2,1,0:T(8,128)(2,1)S(1)}, bf16[8,128,128]{2,1,0:T(8,128)(2,1)S(1)}, u32[]{:S(2)}, u32[]{:S(2)}) collective-permute-start(bf16[8,128,128]{2,1,0:T(8,128)(2,1)S(1)} %get-tuple-element.90.rest_0_), channel_id=1, source_target_pairs={{0,3},{1,2},{2,1},{3,0},{4,7},{5,6},{6,5},{7,4},{8,11},{9,10},{10,... | collective-permute-start | bytes 786440 | tf_op jit(solution)/shard_map/ppermute | solution.py:328
  81.6 0.8 collective-permute-start.19
  82.5 6.5 %aggregate.1 = bf16[16,128,128]{2,1,0:T(8,128)(2,1)S(1)} custom-call(s32[320]{0:T(512)S(1)} %reshape.122.cols_ref, s32[1]{0:T(128)} %bitcast.me_ref.refs_4_, bf16[16,20,128,128]{3,2,1,0:T(8,128)(2,1)} %tiles_ref.5, bf16[16,128,128]{2,1,0:T(8,128)(2,1)S(1)} %bitcast.92, bf16[16,128,128]{2,1,0:T(8,128)(2,1)} %collective-permute-done.9.rest_1_, ...), custom_call_target="tpu_custom_call" | custom-call | flops 1342177280 | bytes 30000000 | tf_op jit(solution)/shard_map/aggregate/pallas_call | solution.py:150
  89.0 5.5 %collective-permute-done.16.rest_3_ = bf16[8,128,128]{2,1,0:T(8,128)(2,1)S(1)} collective-permute-done((bf16[8,128,128]{2,1,0:T(8,128)(2,1)S(1)}, bf16[8,128,128]{2,1,0:T(8,128)(2,1)S(1)}, u32[]{:S(2)}, u32[]{:S(2)}) %collective-permute-start.16) | collective-permute-done | bytes 262176 | tf_op jit(solution)/shard_map/ppermute | solution.py:328
  94.5 6.3 %collective-permute-start.18 = (bf16[8,128,128]{2,1,0:T(8,128)(2,1)S(1)}, bf16[8,128,128]{2,1,0:T(8,128)(2,1)S(1)}, u32[]{:S(2)}, u32[]{:S(2)}) collective-permute-start(bf16[8,128,128]{2,1,0:T(8,128)(2,1)S(1)} %collective-permute-done.16.rest_3_), channel_id=1, source_target_pairs={{0,1},{1,0},{2,3},{3,2},{4,5},{5,4},{6,7},{7,6},{8,9},{9,8},{10,11... | collective-permute-start | bytes 786440 | tf_op jit(solution)/shard_map/ppermute | solution.py:328
  100.8 4.3 %collective-permute-start.21 = (bf16[8,128,128]{2,1,0:T(8,128)(2,1)S(1)}, bf16[8,128,128]{2,1,0:T(8,128)(2,1)S(1)}, u32[]{:S(2)}, u32[]{:S(2)}) collective-permute-start(bf16[8,128,128]{2,1,0:T(8,128)(2,1)S(1)} %collective-permute-done.20.rest_3_), channel_id=1, source_target_pairs={{0,1},{1,0},{2,3},{3,2},{4,5},{5,4},{6,7},{7,6},{8,9},{9,8},{10,11... | collective-permute-start | bytes 786440 | tf_op jit(solution)/shard_map/ppermute | solution.py:328
  105.2 1.7 %collective-permute-done.18.rest_2_ = bf16[8,128,128]{2,1,0:T(8,128)(2,1)S(1)} collective-permute-done((bf16[8,128,128]{2,1,0:T(8,128)(2,1)S(1)}, bf16[8,128,128]{2,1,0:T(8,128)(2,1)S(1)}, u32[]{:S(2)}, u32[]{:S(2)}) %collective-permute-start.18) | collective-permute-done | bytes 262176 | tf_op jit(solution)/shard_map/ppermute | solution.py:328
  106.9 0.6 dense.2
  107.5 4.0 %collective-permute-done.21.rest_2_ = bf16[8,128,128]{2,1,0:T(8,128)(2,1)S(1)} collective-permute-done((bf16[8,128,128]{2,1,0:T(8,128)(2,1)S(1)}, bf16[8,128,128]{2,1,0:T(8,128)(2,1)S(1)}, u32[]{:S(2)}, u32[]{:S(2)}) %collective-permute-start.21) | collective-permute-done | bytes 262176 | tf_op jit(solution)/shard_map/ppermute | solution.py:328
  111.5 0.6 dense.3
  112.1 6.6 %spread.3 = (bf16[4,8,128,128]{3,2,1,0:T(8,128)(2,1)S(1)}, bf16[4,8,128,128]{3,2,1,0:T(8,128)(2,1)S(1)}, bf16[4,8,128,128]{3,2,1,0:T(8,128)(2,1)S(1)}, bf16[4,8,128,128]{3,2,1,0:T(8,128)(2,1)S(1)}) custom-call(s32[320]{0:T(512)S(1)} %reshape.122.cols_ref, s32[1]{0:T(128)} %bitcast.me_ref.refs_4_, bf16[16,20,128,128]{3,2,1,0:T(8,128)(2,1)} %tiles_ref.5, ...), custom_call_target="tpu_custom_call" | custom-call | flops 1342177280 | bytes 30000000 | tf_op jit(solution)/shard_map/spread/pallas_call | solution.py:107
  118.8 0.5 collective-permute-start.23
  119.3 0.2 weight_terms.1
  119.5 0.1 collective-permute-start.24
  119.6 1.8 %collective-permute-done.22 = bf16[4,8,128,128]{3,2,1,0:T(8,128)(2,1)S(1)} collective-permute-done((bf16[4,8,128,128]{3,2,1,0:T(8,128)(2,1)S(1)}, bf16[4,8,128,128]{3,2,1,0:T(8,128)(2,1)S(1)}, u32[]{:S(2)}, u32[]{:S(2)}) %collective-permute-start.22) | collective-permute-done | bytes 1048608 | tf_op jit(solution)/shard_map/ppermute | solution.py:328
  121.4 0.3 add_convert_fusion.3
  121.8 1.6 %collective-permute-start.25 = (bf16[2,8,128,128]{3,2,1,0:T(8,128)(2,1)S(1)}, bf16[2,8,128,128]{3,2,1,0:T(8,128)(2,1)S(1)}, u32[]{:S(2)}, u32[]{:S(2)}) collective-permute-start(bf16[2,8,128,128]{3,2,1,0:T(8,128)(2,1)S(1)} %get-tuple-element.132), channel_id=1, source_target_pairs={{0,16},{4,20},{8,24},{12,28},{16,0},{20,4},{24,8},{28,12},{1,17},{... | collective-permute-start | bytes 1572872 | tf_op jit(solution)/shard_map/ppermute | solution.py:328
  123.3 0.4 fusion.1
  123.7 1.8 %collective-permute-start.26 = (bf16[2,8,128,128]{3,2,1,0:T(8,128)(2,1)S(1)}, bf16[2,8,128,128]{3,2,1,0:T(8,128)(2,1)S(1)}, u32[]{:S(2)}, u32[]{:S(2)}) collective-permute-start(bf16[2,8,128,128]{3,2,1,0:T(8,128)(2,1)S(1)} %get-tuple-element.130), channel_id=1, source_target_pairs={{0,8},{4,12},{8,0},{12,4},{16,24},{20,28},{24,16},{28,20},{1,9},{5... | collective-permute-start | bytes 1572872 | tf_op jit(solution)/shard_map/ppermute | solution.py:328
  125.5 1.2 collective-permute-start.27
  126.7 11.9 %collective-permute-done.27 = bf16[128,512]{1,0:T(8,128)(2,1)S(1)} collective-permute-done((bf16[128,512]{1,0:T(8,128)(2,1)S(1)}, bf16[128,512]{1,0:T(8,128)(2,1)S(1)}, u32[]{:S(2)}, u32[]{:S(2)}) %collective-permute-start.27) | collective-permute-done | bytes 131104 | tf_op jit(solution)/shard_map/ppermute | solution.py:328
  138.7 0.1 fusion.9
  138.8 0.1 fusion.10
  139.0 1.5 %collective-permute-start.30 = (bf16[128,512]{1,0:T(8,128)(2,1)S(1)}, bf16[128,512]{1,0:T(8,128)(2,1)S(1)}, u32[]{:S(2)}, u32[]{:S(2)}) collective-permute-start(bf16[128,512]{1,0:T(8,128)(2,1)S(1)} %convert_add_fusion.3), channel_id=1, source_target_pairs={{0,8},{4,12},{8,0},{12,4},{16,24},{20,28},{24,16},{28,20},{1,9},{5... | collective-permute-start | bytes 393224 | tf_op jit(solution)/shard_map/ppermute | solution.py:328
  140.5 1.7 %collective-permute-start.29 = (bf16[8,128,128]{2,1,0:T(8,128)(2,1)S(1)}, bf16[8,128,128]{2,1,0:T(8,128)(2,1)S(1)}, u32[]{:S(2)}, u32[]{:S(2)}) collective-permute-start(bf16[8,128,128]{2,1,0:T(8,128)(2,1)S(1)} %get-tuple-element.137), channel_id=1, source_target_pairs={{0,16},{4,20},{8,24},{12,28},{16,0},{20,4},{24,8},{28,12},{1,17},{... | collective-permute-start | bytes 786440 | tf_op jit(solution)/shard_map/ppermute | solution.py:328
  142.2 0.3 collective-permute-start.28
  142.6 1.9 %collective-permute-done.30 = bf16[128,512]{1,0:T(8,128)(2,1)S(1)} collective-permute-done((bf16[128,512]{1,0:T(8,128)(2,1)S(1)}, bf16[128,512]{1,0:T(8,128)(2,1)S(1)}, u32[]{:S(2)}, u32[]{:S(2)}) %collective-permute-start.30) | collective-permute-done | bytes 131104 | tf_op jit(solution)/shard_map/ppermute | solution.py:328
  144.6 3.3 %collective-permute-done.29.refs_3_ = bf16[8,128,128]{2,1,0:T(8,128)(2,1)S(1)} collective-permute-done((bf16[8,128,128]{2,1,0:T(8,128)(2,1)S(1)}, bf16[8,128,128]{2,1,0:T(8,128)(2,1)S(1)}, u32[]{:S(2)}, u32[]{:S(2)}) %collective-permute-start.29) | collective-permute-done | bytes 262176 | tf_op jit(solution)/shard_map/ppermute | solution.py:328
  147.9 1.7 %collective-permute-done.28.refs_1_ = bf16[8,128,128]{2,1,0:T(8,128)(2,1)S(1)} collective-permute-done((bf16[8,128,128]{2,1,0:T(8,128)(2,1)S(1)}, bf16[8,128,128]{2,1,0:T(8,128)(2,1)S(1)}, u32[]{:S(2)}, u32[]{:S(2)}) %collective-permute-start.28) | collective-permute-done | bytes 262176 | tf_op jit(solution)/shard_map/ppermute | solution.py:328
  149.6 1.2 finish.3
  (54 shorter events, 0.8 us)
Async XLA Ops:
  1.4 1.0 copy-start.1
  2.5 39.0 %copy-start.2 = (bf16[2048,128]{1,0:T(8,128)(2,1)S(1)}, bf16[2048,128]{1,0:T(8,128)(2,1)}, u32[]{:S(2)}) copy-start(bf16[2048,128]{1,0:T(8,128)(2,1)} %param.8) | copy-start | bytes 1572868
  2.5 63.1 %copy-start.7 = (bf16[128,512]{1,0:T(8,128)(2,1)S(1)}, bf16[128,512]{1,0:T(8,128)(2,1)}, u32[]{:S(2)}) copy-start(bf16[128,512]{1,0:T(8,128)(2,1)} %param.14) | copy-start | bytes 393220
  2.5 63.1 %copy-start.8 = (bf16[128,512]{1,0:T(8,128)(2,1)S(1)}, bf16[128,512]{1,0:T(8,128)(2,1)}, u32[]{:S(2)}) copy-start(bf16[128,512]{1,0:T(8,128)(2,1)} %param.15) | copy-start | bytes 393220
  2.5 63.8 %copy-start = (bf16[2048,128]{1,0:T(8,128)(2,1)S(1)}, bf16[2048,128]{1,0:T(8,128)(2,1)}, u32[]{:S(2)}) copy-start(bf16[2048,128]{1,0:T(8,128)(2,1)} %param.9) | copy-start | bytes 1572868
  9.4 55.7 %copy-start.3 = (bf16[16,128,128]{2,1,0:T(8,128)(2,1)}, bf16[16,128,128]{2,1,0:T(8,128)(2,1)S(1)}, u32[]{:S(2)}) copy-start(bf16[16,128,128]{2,1,0:T(8,128)(2,1)S(1)} %get-tuple-element.78.rest_4_) | copy-start | bytes 1572868
  9.4 2.8 %collective-permute-start = (bf16[4,8,128,128]{3,2,1,0:T(8,128)(2,1)S(1)}, bf16[4,8,128,128]{3,2,1,0:T(8,128)(2,1)S(1)}, u32[]{:S(2)}, u32[]{:S(2)}) collective-permute-start(bf16[4,8,128,128]{3,2,1,0:T(8,128)(2,1)S(1)} %get-tuple-element.67), channel_id=1, source_target_pairs={{0,4},{4,0},{8,12},{12,8},{16,20},{20,16},{24,28},{28,24},{1,5},{5... | collective-permute-start | bytes 3145736 | tf_op jit(solution)/shard_map/ppermute | solution.py:328
  9.9 5.7 %collective-permute-start.3 = (bf16[4,8,128,128]{3,2,1,0:T(8,128)(2,1)S(1)}, bf16[4,8,128,128]{3,2,1,0:T(8,128)(2,1)S(1)}, u32[]{:S(2)}, u32[]{:S(2)}) collective-permute-start(bf16[4,8,128,128]{3,2,1,0:T(8,128)(2,1)S(1)} %get-tuple-element.69), channel_id=1, source_target_pairs={{0,4},{4,0},{8,12},{12,8},{16,20},{20,16},{24,28},{28,24},{1,5},{5... | collective-permute-start | bytes 3145736 | tf_op jit(solution)/shard_map/ppermute | solution.py:328
  12.7 15.2 %collective-permute-start.1 = (bf16[2,8,128,128]{3,2,1,0:T(8,128)(2,1)S(1)}, bf16[2,8,128,128]{3,2,1,0:T(8,128)(2,1)S(1)}, u32[]{:S(2)}, u32[]{:S(2)}) collective-permute-start(bf16[2,8,128,128]{3,2,1,0:T(8,128)(2,1)S(1)} %get-tuple-element.136), channel_id=1, source_target_pairs={{0,16},{4,20},{8,24},{12,28},{16,0},{20,4},{24,8},{28,12},{1,17},{... | collective-permute-start | bytes 1572872 | tf_op jit(solution)/shard_map/ppermute | solution.py:328
  16.0 13.8 %collective-permute-start.4 = (bf16[2,8,128,128]{3,2,1,0:T(8,128)(2,1)S(1)}, bf16[2,8,128,128]{3,2,1,0:T(8,128)(2,1)S(1)}, u32[]{:S(2)}, u32[]{:S(2)}) collective-permute-start(bf16[2,8,128,128]{3,2,1,0:T(8,128)(2,1)S(1)} %get-tuple-element.134), channel_id=1, source_target_pairs={{0,8},{4,12},{8,0},{12,4},{16,24},{20,28},{24,16},{28,20},{1,9},{5... | collective-permute-start | bytes 1572872 | tf_op jit(solution)/shard_map/ppermute | solution.py:328
  28.0 7.9 %collective-permute-start.2 = (bf16[8,128,128]{2,1,0:T(8,128)(2,1)S(1)}, bf16[8,128,128]{2,1,0:T(8,128)(2,1)S(1)}, u32[]{:S(2)}, u32[]{:S(2)}) collective-permute-start(bf16[8,128,128]{2,1,0:T(8,128)(2,1)S(1)} %get-tuple-element.143), channel_id=1, source_target_pairs={{0,8},{4,12},{8,0},{12,4},{16,24},{20,28},{24,16},{28,20},{1,9},{5... | collective-permute-start | bytes 786440 | tf_op jit(solution)/shard_map/ppermute | solution.py:328
  29.9 7.3 %collective-permute-start.5 = (bf16[8,128,128]{2,1,0:T(8,128)(2,1)S(1)}, bf16[8,128,128]{2,1,0:T(8,128)(2,1)S(1)}, u32[]{:S(2)}, u32[]{:S(2)}) collective-permute-start(bf16[8,128,128]{2,1,0:T(8,128)(2,1)S(1)} %get-tuple-element.141), channel_id=1, source_target_pairs={{0,16},{4,20},{8,24},{12,28},{16,0},{20,4},{24,8},{28,12},{1,17},{... | collective-permute-start | bytes 786440 | tf_op jit(solution)/shard_map/ppermute | solution.py:328
  37.4 14.0 %collective-permute-start.8 = (bf16[16,128,128]{2,1,0:T(8,128)(2,1)S(1)}, bf16[16,128,128]{2,1,0:T(8,128)(2,1)S(1)}, u32[]{:S(2)}, u32[]{:S(2)}) collective-permute-start(bf16[16,128,128]{2,1,0:T(8,128)(2,1)S(1)} %finish.2.rest_0_), channel_id=1, source_target_pairs={{0,1},{1,0},{2,3},{3,2},{4,5},{5,4},{6,7},{7,6},{8,9},{9,8},{10,11... | collective-permute-start | bytes 1572872 | tf_op jit(solution)/shard_map/ppermute | solution.py:328
  39.0 23.8 %collective-permute-start.6 = (bf16[16,128,128]{2,1,0:T(8,128)(2,1)S(1)}, bf16[16,128,128]{2,1,0:T(8,128)(2,1)}, u32[]{:S(2)}, u32[]{:S(2)}) collective-permute-start(bf16[16,128,128]{2,1,0:T(8,128)(2,1)S(1)} %finish.2.rest_0_), channel_id=1, source_target_pairs={{0,3},{1,2},{2,1},{3,0},{4,7},{5,6},{6,5},{7,4},{8,11},{9,10},{10,... | collective-permute-start | bytes 1572872 | tf_op jit(solution)/shard_map/ppermute | solution.py:328
  41.5 21.9 %collective-permute-start.14 = (bf16[16,128,128]{2,1,0:T(8,128)(2,1)S(1)}, bf16[16,128,128]{2,1,0:T(8,128)(2,1)S(1)}, u32[]{:S(2)}, u32[]{:S(2)}) collective-permute-start(bf16[16,128,128]{2,1,0:T(8,128)(2,1)S(1)} %bitcast.88), channel_id=1, source_target_pairs={{0,24},{4,28},{8,16},{12,20},{16,8},{20,12},{24,0},{28,4},{1,25},{... | collective-permute-start | bytes 1572872 | tf_op jit(solution)/shard_map/ppermute | solution.py:328
  43.9 21.1 %collective-permute-start.12 = (bf16[16,128,128]{2,1,0:T(8,128)(2,1)S(1)}, bf16[16,128,128]{2,1,0:T(8,128)(2,1)S(1)}, u32[]{:S(2)}, u32[]{:S(2)}) collective-permute-start(bf16[16,128,128]{2,1,0:T(8,128)(2,1)S(1)} %bitcast.89), channel_id=1, source_target_pairs={{0,16},{4,20},{8,24},{12,28},{16,0},{20,4},{24,8},{28,12},{1,17},{... | collective-permute-start | bytes 1572872 | tf_op jit(solution)/shard_map/ppermute | solution.py:328
  44.3 20.8 %collective-permute-start.10 = (bf16[16,128,128]{2,1,0:T(8,128)(2,1)S(1)}, bf16[16,128,128]{2,1,0:T(8,128)(2,1)S(1)}, u32[]{:S(2)}, u32[]{:S(2)}) collective-permute-start(bf16[16,128,128]{2,1,0:T(8,128)(2,1)S(1)} %bitcast.90), channel_id=1, source_target_pairs={{0,8},{4,12},{8,0},{12,4},{16,24},{20,28},{24,16},{28,20},{1,9},{5... | collective-permute-start | bytes 1572872 | tf_op jit(solution)/shard_map/ppermute | solution.py:328
  51.4 0.8 copy-start.5
  52.2 18.1 %collective-permute-start.9 = (bf16[16,128,128]{2,1,0:T(8,128)(2,1)S(1)}, bf16[16,128,128]{2,1,0:T(8,128)(2,1)}, u32[]{:S(2)}, u32[]{:S(2)}) collective-permute-start(bf16[16,128,128]{2,1,0:T(8,128)(2,1)S(1)} %bitcast.91), channel_id=1, source_target_pairs={{0,4},{4,0},{8,12},{12,8},{16,20},{20,16},{24,28},{28,24},{1,5},{5... | collective-permute-start | bytes 1572872 | tf_op jit(solution)/shard_map/ppermute | solution.py:328
  62.8 11.3 %collective-permute-start.7 = (bf16[16,128,128]{2,1,0:T(8,128)(2,1)}, bf16[16,128,128]{2,1,0:T(8,128)(2,1)}, u32[]{:S(2)}, u32[]{:S(2)}) collective-permute-start(bf16[16,128,128]{2,1,0:T(8,128)(2,1)} %collective-permute-done.6.rest_2_), channel_id=1, source_target_pairs={{0,1},{1,0},{2,3},{3,2},{4,5},{5,4},{6,7},{7,6},{8,9},{9,8},{10,11... | collective-permute-start | bytes 1572872 | tf_op jit(solution)/shard_map/ppermute | solution.py:328
  63.4 10.7 %collective-permute-start.15 = (bf16[16,128,128]{2,1,0:T(8,128)(2,1)S(1)}, bf16[16,128,128]{2,1,0:T(8,128)(2,1)}, u32[]{:S(2)}, u32[]{:S(2)}) collective-permute-start(bf16[16,128,128]{2,1,0:T(8,128)(2,1)S(1)} %collective-permute-done.14.rest_6_), channel_id=1, source_target_pairs={{0,4},{4,0},{8,12},{12,8},{16,20},{20,16},{24,28},{28,24},{1,5},{5... | collective-permute-start | bytes 1572872 | tf_op jit(solution)/shard_map/ppermute | solution.py:328
  65.0 9.1 %collective-permute-start.13 = (bf16[16,128,128]{2,1,0:T(8,128)(2,1)S(1)}, bf16[16,128,128]{2,1,0:T(8,128)(2,1)}, u32[]{:S(2)}, u32[]{:S(2)}) collective-permute-start(bf16[16,128,128]{2,1,0:T(8,128)(2,1)S(1)} %collective-permute-done.12.rest_4_), channel_id=1, source_target_pairs={{0,4},{4,0},{8,12},{12,8},{16,20},{20,16},{24,28},{28,24},{1,5},{5... | collective-permute-start | bytes 1572872 | tf_op jit(solution)/shard_map/ppermute | solution.py:328
  65.1 9.0 %collective-permute-start.11 = (bf16[16,128,128]{2,1,0:T(8,128)(2,1)S(1)}, bf16[16,128,128]{2,1,0:T(8,128)(2,1)}, u32[]{:S(2)}, u32[]{:S(2)}) collective-permute-start(bf16[16,128,128]{2,1,0:T(8,128)(2,1)S(1)} %collective-permute-done.10.rest_2_), channel_id=1, source_target_pairs={{0,4},{4,0},{8,12},{12,8},{16,20},{20,16},{24,28},{28,24},{1,5},{5... | collective-permute-start | bytes 1572872 | tf_op jit(solution)/shard_map/ppermute | solution.py:328
  66.3 1.0 copy-start.4
  67.3 1.0 copy-start.6
  75.6 13.3 %collective-permute-start.17 = (bf16[8,128,128]{2,1,0:T(8,128)(2,1)S(1)}, bf16[8,128,128]{2,1,0:T(8,128)(2,1)S(1)}, u32[]{:S(2)}, u32[]{:S(2)}) collective-permute-start(bf16[8,128,128]{2,1,0:T(8,128)(2,1)S(1)} %get-tuple-element.90.rest_0_), channel_id=1, source_target_pairs={{0,1},{1,0},{2,3},{3,2},{4,5},{5,4},{6,7},{7,6},{8,9},{9,8},{10,11... | collective-permute-start | bytes 786440 | tf_op jit(solution)/shard_map/ppermute | solution.py:328
  76.0 18.5 %collective-permute-start.16 = (bf16[8,128,128]{2,1,0:T(8,128)(2,1)S(1)}, bf16[8,128,128]{2,1,0:T(8,128)(2,1)S(1)}, u32[]{:S(2)}, u32[]{:S(2)}) collective-permute-start(bf16[8,128,128]{2,1,0:T(8,128)(2,1)S(1)} %get-tuple-element.90.rest_0_), channel_id=1, source_target_pairs={{0,3},{1,2},{2,1},{3,0},{4,7},{5,6},{6,5},{7,4},{8,11},{9,10},{10,... | collective-permute-start | bytes 786440 | tf_op jit(solution)/shard_map/ppermute | solution.py:328
  81.5 19.3 %collective-permute-start.20 = (bf16[8,128,128]{2,1,0:T(8,128)(2,1)S(1)}, bf16[8,128,128]{2,1,0:T(8,128)(2,1)S(1)}, u32[]{:S(2)}, u32[]{:S(2)}) collective-permute-start(bf16[8,128,128]{2,1,0:T(8,128)(2,1)S(1)} %get-tuple-element.101.rest_0_), channel_id=1, source_target_pairs={{0,3},{1,2},{2,1},{3,0},{4,7},{5,6},{6,5},{7,4},{8,11},{9,10},{10,... | collective-permute-start | bytes 786440 | tf_op jit(solution)/shard_map/ppermute | solution.py:328
  81.6 23.6 %collective-permute-start.19 = (bf16[8,128,128]{2,1,0:T(8,128)(2,1)S(1)}, bf16[8,128,128]{2,1,0:T(8,128)(2,1)S(1)}, u32[]{:S(2)}, u32[]{:S(2)}) collective-permute-start(bf16[8,128,128]{2,1,0:T(8,128)(2,1)S(1)} %get-tuple-element.101.rest_0_), channel_id=1, source_target_pairs={{0,1},{1,0},{2,3},{3,2},{4,5},{5,4},{6,7},{7,6},{8,9},{9,8},{10,11... | collective-permute-start | bytes 786440 | tf_op jit(solution)/shard_map/ppermute | solution.py:328
  94.5 12.4 %collective-permute-start.18 = (bf16[8,128,128]{2,1,0:T(8,128)(2,1)S(1)}, bf16[8,128,128]{2,1,0:T(8,128)(2,1)S(1)}, u32[]{:S(2)}, u32[]{:S(2)}) collective-permute-start(bf16[8,128,128]{2,1,0:T(8,128)(2,1)S(1)} %collective-permute-done.16.rest_3_), channel_id=1, source_target_pairs={{0,1},{1,0},{2,3},{3,2},{4,5},{5,4},{6,7},{7,6},{8,9},{9,8},{10,11... | collective-permute-start | bytes 786440 | tf_op jit(solution)/shard_map/ppermute | solution.py:328
  100.8 10.7 %collective-permute-start.21 = (bf16[8,128,128]{2,1,0:T(8,128)(2,1)S(1)}, bf16[8,128,128]{2,1,0:T(8,128)(2,1)S(1)}, u32[]{:S(2)}, u32[]{:S(2)}) collective-permute-start(bf16[8,128,128]{2,1,0:T(8,128)(2,1)S(1)} %collective-permute-done.20.rest_3_), channel_id=1, source_target_pairs={{0,1},{1,0},{2,3},{3,2},{4,5},{5,4},{6,7},{7,6},{8,9},{9,8},{10,11... | collective-permute-start | bytes 786440 | tf_op jit(solution)/shard_map/ppermute | solution.py:328
  118.7 2.7 %collective-permute-start.22 = (bf16[4,8,128,128]{3,2,1,0:T(8,128)(2,1)S(1)}, bf16[4,8,128,128]{3,2,1,0:T(8,128)(2,1)S(1)}, u32[]{:S(2)}, u32[]{:S(2)}) collective-permute-start(bf16[4,8,128,128]{3,2,1,0:T(8,128)(2,1)S(1)} %get-tuple-element.108), channel_id=1, source_target_pairs={{0,4},{4,0},{8,12},{12,8},{16,20},{20,16},{24,28},{28,24},{1,5},{5... | collective-permute-start | bytes 3145736 | tf_op jit(solution)/shard_map/ppermute | solution.py:328
  118.8 4.6 %collective-permute-start.23 = (bf16[4,8,128,128]{3,2,1,0:T(8,128)(2,1)S(1)}, bf16[4,8,128,128]{3,2,1,0:T(8,128)(2,1)S(1)}, u32[]{:S(2)}, u32[]{:S(2)}) collective-permute-start(bf16[4,8,128,128]{3,2,1,0:T(8,128)(2,1)S(1)} %get-tuple-element.110), channel_id=1, source_target_pairs={{0,4},{4,0},{8,12},{12,8},{16,20},{20,16},{24,28},{28,24},{1,5},{5... | collective-permute-start | bytes 3145736 | tf_op jit(solution)/shard_map/ppermute | solution.py:328
  119.5 6.0 %collective-permute-start.24 = (bf16[128,512]{1,0:T(8,128)(2,1)S(1)}, bf16[128,512]{1,0:T(8,128)(2,1)S(1)}, u32[]{:S(2)}, u32[]{:S(2)}) collective-permute-start(bf16[128,512]{1,0:T(8,128)(2,1)S(1)} %get-tuple-element.116), channel_id=1, source_target_pairs={{0,4},{4,0},{8,12},{12,8},{16,20},{20,16},{24,28},{28,24},{1,5},{5... | collective-permute-start | bytes 393224 | tf_op jit(solution)/shard_map/ppermute | solution.py:328
  121.8 16.9 %collective-permute-start.25 = (bf16[2,8,128,128]{3,2,1,0:T(8,128)(2,1)S(1)}, bf16[2,8,128,128]{3,2,1,0:T(8,128)(2,1)S(1)}, u32[]{:S(2)}, u32[]{:S(2)}) collective-permute-start(bf16[2,8,128,128]{3,2,1,0:T(8,128)(2,1)S(1)} %get-tuple-element.132), channel_id=1, source_target_pairs={{0,16},{4,20},{8,24},{12,28},{16,0},{20,4},{24,8},{28,12},{1,17},{... | collective-permute-start | bytes 1572872 | tf_op jit(solution)/shard_map/ppermute | solution.py:328
  123.7 14.9 %collective-permute-start.26 = (bf16[2,8,128,128]{3,2,1,0:T(8,128)(2,1)S(1)}, bf16[2,8,128,128]{3,2,1,0:T(8,128)(2,1)S(1)}, u32[]{:S(2)}, u32[]{:S(2)}) collective-permute-start(bf16[2,8,128,128]{3,2,1,0:T(8,128)(2,1)S(1)} %get-tuple-element.130), channel_id=1, source_target_pairs={{0,8},{4,12},{8,0},{12,4},{16,24},{20,28},{24,16},{28,20},{1,9},{5... | collective-permute-start | bytes 1572872 | tf_op jit(solution)/shard_map/ppermute | solution.py:328
  125.5 13.1 %collective-permute-start.27 = (bf16[128,512]{1,0:T(8,128)(2,1)S(1)}, bf16[128,512]{1,0:T(8,128)(2,1)S(1)}, u32[]{:S(2)}, u32[]{:S(2)}) collective-permute-start(bf16[128,512]{1,0:T(8,128)(2,1)S(1)} %convert_add_fusion.4), channel_id=1, source_target_pairs={{0,16},{4,20},{8,24},{12,28},{16,0},{20,4},{24,8},{28,12},{1,17},{... | collective-permute-start | bytes 393224 | tf_op jit(solution)/shard_map/ppermute | solution.py:328
  139.0 5.5 %collective-permute-start.30 = (bf16[128,512]{1,0:T(8,128)(2,1)S(1)}, bf16[128,512]{1,0:T(8,128)(2,1)S(1)}, u32[]{:S(2)}, u32[]{:S(2)}) collective-permute-start(bf16[128,512]{1,0:T(8,128)(2,1)S(1)} %convert_add_fusion.3), channel_id=1, source_target_pairs={{0,8},{4,12},{8,0},{12,4},{16,24},{20,28},{24,16},{28,20},{1,9},{5... | collective-permute-start | bytes 393224 | tf_op jit(solution)/shard_map/ppermute | solution.py:328
  140.5 7.4 %collective-permute-start.29 = (bf16[8,128,128]{2,1,0:T(8,128)(2,1)S(1)}, bf16[8,128,128]{2,1,0:T(8,128)(2,1)S(1)}, u32[]{:S(2)}, u32[]{:S(2)}) collective-permute-start(bf16[8,128,128]{2,1,0:T(8,128)(2,1)S(1)} %get-tuple-element.137), channel_id=1, source_target_pairs={{0,16},{4,20},{8,24},{12,28},{16,0},{20,4},{24,8},{28,12},{1,17},{... | collective-permute-start | bytes 786440 | tf_op jit(solution)/shard_map/ppermute | solution.py:328
  142.2 7.4 %collective-permute-start.28 = (bf16[8,128,128]{2,1,0:T(8,128)(2,1)S(1)}, bf16[8,128,128]{2,1,0:T(8,128)(2,1)S(1)}, u32[]{:S(2)}, u32[]{:S(2)}) collective-permute-start(bf16[8,128,128]{2,1,0:T(8,128)(2,1)S(1)} %get-tuple-element.139), channel_id=1, source_target_pairs={{0,8},{4,12},{8,0},{12,4},{16,24},{20,28},{24,16},{28,20},{1,9},{5... | collective-permute-start | bytes 786440 | tf_op jit(solution)/shard_map/ppermute | solution.py:328
  144.5 5.1 %collective-permute-start.31 = (f32[128,512]{1,0:T(8,128)S(1)}, f32[128,512]{1,0:T(8,128)S(1)}, u32[]{:S(2)}, u32[]{:S(2)}) collective-permute-start(f32[128,512]{1,0:T(8,128)S(1)} %convert_add_fusion.2.refs_5_), channel_id=1, source_target_pairs={{0,4},{4,0},{8,12},{12,8},{16,20},{20,16},{24,28},{28,24},{1,5},{5... | collective-permute-start | bytes 786440 | tf_op jit(solution)/shard_map/ppermute | solution.py:328

commit v18 on v17

--- a/solution.py
+++ b/solution.py
@@ -8,7 +8,7 @@
 from jax.sharding import PartitionSpec as P
 
 GROUPS = 2
-COPIES = 4
+COPIES = 2
 F32 = jnp.float32
 BF16 = jnp.bfloat16
 VMEM = pl.BlockSpec(memory_space=pltpu.VMEM)

time: 152 us -> 152 us (level)
  no operation moved by 1% of the time
where the time goes in v18:
time: 152 us; the launch traced here: 151 us
  waiting for transfers between devices  72.3 us (48%)
  starting transfers between devices  43.4 us (29%)
  Pallas kernels  27 us (18%)
  local copies, waits for them, and re-layouts  5.42 us (4%)
  other arithmetic  2.17 us (1%)
    ppermute x32, waiting for transfers between devices, swap(): lax.ppermute(value, axis, [(i, i ^ mask) for i in range(lax.axis_size(axi...  72.3 us
    ppermute x32, starting transfers between devices, swap(): lax.ppermute(value, axis, [(i, i ^ mask) for i in range(lax.axis_size(axi...  43.4 us
    pallas_call x2, Pallas kernels, spread(): pl.pallas_call(functools.partial(spread_kernel, first, len(vals)), out_sh...  14 us
    pallas_call x1, Pallas kernels, aggregate(): pl.pallas_call(aggregate_kernel, out_shape=jax.ShapeDtypeStruct((blocks,...  6.91 us
    unnamed x26, local copies, waits for them, and re-layouts  3.98 us
  transfers between devices with their start and end apart: 32, of which 17 were waited for; matrix products, arithmetic and copies ran while one was open for 2% of the time, Pallas kernels for 6%

profile of v18, /device:TPU:0, one launch (start us, length us, event | category | flops | bytes accessed | tf_op | source)
XLA Modules:
  0.0 151.3 jit_solution(3632292077590463533)
XLA Ops:
  0.6 0.8 reshape.122.cols_ref
  1.4 1.0 copy-done.1
  2.5 7.2 %spread.2 = (bf16[4,8,128,128]{3,2,1,0:T(8,128)(2,1)S(1)}, bf16[4,8,128,128]{3,2,1,0:T(8,128)(2,1)S(1)}, bf16[4,8,128,128]{3,2,1,0:T(8,128)(2,1)S(1)}, bf16[4,8,...) custom-call(s32[320]{0:T(512)S(1)} %reshape.122.cols_ref, s32[1]{0:T(128)} %bitcast.me_ref.refs_4_, ...), custom_call_target="tpu_custom_call" | custom-call | flops 1342177280 | bytes 30000000 | tf_op jit(solution)/shard_map/spread/pallas_call | solution.py:107
  9.7 0.5 collective-permute-start
  10.3 2.2 %collective-permute-done = bf16[4,8,128,128]{3,2,1,0:T(8,128)(2,1)S(1)} collective-permute-done((bf16[4,8,128,128]{3,2,1,0:T(8,128)(2,1)S(1)}, bf16[4,8,128,128]{3,2,1,0:T(8,128)(2,1)S(1)}, u32[]{:S(2)}, u32[]{:S(2)}) %collective-permute-start) | collective-permute-done | bytes 1048608 | tf_op jit(solution)/shard_map/ppermute | solution.py:328
  12.5 0.5 add_convert_fusion.7
  13.0 3.0 %collective-permute-start.1 = (bf16[2,8,128,128]{3,2,1,0:T(8,128)(2,1)S(1)}, bf16[2,8,128,128]{3,2,1,0:T(8,128)(2,1)S(1)}, u32[]{:S(2)}, u32[]{:S(2)}) collective-permute-start(bf16[2,8,128,128]{3,2,1,0:T(8,128)(2,1)S(1)} %get-tuple-element.136), channel_id=1, source_target_pairs={{0,16},{4,20},{8,24},{12,28},{16,0},{20,4},{24,8},{28,12},{1,17},{... | collective-permute-start | bytes 1572872 | tf_op jit(solution)/shard_map/ppermute | solution.py:328
  15.9 0.3 add_convert_fusion.5
  16.3 1.6 %collective-permute-start.4 = (bf16[2,8,128,128]{3,2,1,0:T(8,128)(2,1)S(1)}, bf16[2,8,128,128]{3,2,1,0:T(8,128)(2,1)S(1)}, u32[]{:S(2)}, u32[]{:S(2)}) collective-permute-start(bf16[2,8,128,128]{3,2,1,0:T(8,128)(2,1)S(1)} %get-tuple-element.134), channel_id=1, source_target_pairs={{0,8},{4,12},{8,0},{12,4},{16,24},{20,28},{24,16},{28,20},{1,9},{5... | collective-permute-start | bytes 1572872 | tf_op jit(solution)/shard_map/ppermute | solution.py:328
  17.8 10.3 %collective-permute-done.1 = bf16[2,8,128,128]{3,2,1,0:T(8,128)(2,1)S(1)} collective-permute-done((bf16[2,8,128,128]{3,2,1,0:T(8,128)(2,1)S(1)}, bf16[2,8,128,128]{3,2,1,0:T(8,128)(2,1)S(1)}, u32[]{:S(2)}, u32[]{:S(2)}) %collective-permute-start.1) | collective-permute-done | bytes 524320 | tf_op jit(solution)/shard_map/ppermute | solution.py:328
  28.2 0.1 fusion.6
  28.3 1.8 %collective-permute-start.2 = (bf16[8,128,128]{2,1,0:T(8,128)(2,1)S(1)}, bf16[8,128,128]{2,1,0:T(8,128)(2,1)S(1)}, u32[]{:S(2)}, u32[]{:S(2)}) collective-permute-start(bf16[8,128,128]{2,1,0:T(8,128)(2,1)S(1)} %get-tuple-element.143), channel_id=1, source_target_pairs={{0,8},{4,12},{8,0},{12,4},{16,24},{20,28},{24,16},{28,20},{1,9},{5... | collective-permute-start | bytes 786440 | tf_op jit(solution)/shard_map/ppermute | solution.py:328
  30.1 0.1 fusion.12
  30.2 1.6 %collective-permute-start.5 = (bf16[8,128,128]{2,1,0:T(8,128)(2,1)S(1)}, bf16[8,128,128]{2,1,0:T(8,128)(2,1)S(1)}, u32[]{:S(2)}, u32[]{:S(2)}) collective-permute-start(bf16[8,128,128]{2,1,0:T(8,128)(2,1)S(1)} %get-tuple-element.141), channel_id=1, source_target_pairs={{0,16},{4,20},{8,24},{12,28},{16,0},{20,4},{24,8},{28,12},{1,17},{... | collective-permute-start | bytes 786440 | tf_op jit(solution)/shard_map/ppermute | solution.py:328
  31.8 4.4 %collective-permute-done.2.refs_1_ = bf16[8,128,128]{2,1,0:T(8,128)(2,1)S(1)} collective-permute-done((bf16[8,128,128]{2,1,0:T(8,128)(2,1)S(1)}, bf16[8,128,128]{2,1,0:T(8,128)(2,1)S(1)}, u32[]{:S(2)}, u32[]{:S(2)}) %collective-permute-start.2) | collective-permute-done | bytes 262176 | tf_op jit(solution)/shard_map/ppermute | solution.py:328
  36.2 1.3 collective-permute-done.5.refs_3_
  37.7 1.6 %collective-permute-start.8 = (bf16[16,128,128]{2,1,0:T(8,128)(2,1)S(1)}, bf16[16,128,128]{2,1,0:T(8,128)(2,1)S(1)}, u32[]{:S(2)}, u32[]{:S(2)}) collective-permute-start(bf16[16,128,128]{2,1,0:T(8,128)(2,1)S(1)} %finish.2.rest_0_), channel_id=1, source_target_pairs={{0,1},{1,0},{2,3},{3,2},{4,5},{5,4},{6,7},{7,6},{8,9},{9,8},{10,11... | collective-permute-start | bytes 1572872 | tf_op jit(solution)/shard_map/ppermute | solution.py:328
  39.3 2.5 %collective-permute-start.6 = (bf16[16,128,128]{2,1,0:T(8,128)(2,1)S(1)}, bf16[16,128,128]{2,1,0:T(8,128)(2,1)}, u32[]{:S(2)}, u32[]{:S(2)}) collective-permute-start(bf16[16,128,128]{2,1,0:T(8,128)(2,1)S(1)} %finish.2.rest_0_), channel_id=1, source_target_pairs={{0,3},{1,2},{2,1},{3,0},{4,7},{5,6},{6,5},{7,4},{8,11},{9,10},{10,... | collective-permute-start | bytes 1572872 | tf_op jit(solution)/shard_map/ppermute | solution.py:328
  41.8 2.4 %collective-permute-start.14 = (bf16[16,128,128]{2,1,0:T(8,128)(2,1)S(1)}, bf16[16,128,128]{2,1,0:T(8,128)(2,1)S(1)}, u32[]{:S(2)}, u32[]{:S(2)}) collective-permute-start(bf16[16,128,128]{2,1,0:T(8,128)(2,1)S(1)} %bitcast.88), channel_id=1, source_target_pairs={{0,24},{4,28},{8,16},{12,20},{16,8},{20,12},{24,0},{28,4},{1,25},{... | collective-permute-start | bytes 1572872 | tf_op jit(solution)/shard_map/ppermute | solution.py:328
  44.2 0.5 collective-permute-start.12
  44.6 0.6 collective-permute-start.10
  45.3 6.4 %collective-permute-done.8.rest_1_ = bf16[16,128,128]{2,1,0:T(8,128)(2,1)S(1)} collective-permute-done((bf16[16,128,128]{2,1,0:T(8,128)(2,1)S(1)}, bf16[16,128,128]{2,1,0:T(8,128)(2,1)S(1)}, u32[]{:S(2)}, u32[]{:S(2)}) %collective-permute-start.8) | collective-permute-done | bytes 524320 | tf_op jit(solution)/shard_map/ppermute | solution.py:328
  51.7 0.8 copy-done.5
  52.5 10.7 %collective-permute-done.6.rest_2_ = bf16[16,128,128]{2,1,0:T(8,128)(2,1)} collective-permute-done((bf16[16,128,128]{2,1,0:T(8,128)(2,1)S(1)}, bf16[16,128,128]{2,1,0:T(8,128)(2,1)}, u32[]{:S(2)}, u32[]{:S(2)}) %collective-permute-start.6) | collective-permute-done | bytes 524320 | tf_op jit(solution)/shard_map/ppermute | solution.py:328
  63.1 0.6 collective-permute-start.7
  63.7 1.6 %collective-permute-done.12.rest_4_ = bf16[16,128,128]{2,1,0:T(8,128)(2,1)S(1)} collective-permute-done((bf16[16,128,128]{2,1,0:T(8,128)(2,1)S(1)}, bf16[16,128,128]{2,1,0:T(8,128)(2,1)S(1)}, u32[]{:S(2)}, u32[]{:S(2)}) %collective-permute-start.12) | collective-permute-done | bytes 524320 | tf_op jit(solution)/shard_map/ppermute | solution.py:328
  65.4 0.4 collective-permute-start.11
  65.9 0.6 constant_dynamic-slice_fusion.3
  66.6 1.0 copy-done.4
  67.6 1.0 copy-done.6
  68.7 1.9 %dense_early.1 = (f32[2,128,1024]{2,1,0:T(8,128)S(1)}, f32[4,128,128]{2,1,0:T(8,128)S(1)}, bf16[16,128,128]{2,1,0:T(8,128)(2,1)S(1)}) custom-call(s32[1]{0:T(128)} %bitcast.1.col_ref, bf16[128,512]{1,0:T(8,128)(2,1)S(1)} %pad_maximum_fusion.1.weight_ref, bf16[16,128,128]{2,1,0:T(8,128)(2,1)S(1)} %finish.2.rest_0_, bf16[16,128,128]{2,1,0:T(8,128)(2,1)S(1)} %copy-done.6, ...), custom_call_target="tpu_custom_call" | custom-call | tf_op jit(solution)/shard_map/dense_early/pallas_call | solution.py:257
  70.6 3.8 %collective-permute-done.7.shard_ref = bf16[16,128,128]{2,1,0:T(8,128)(2,1)} collective-permute-done((bf16[16,128,128]{2,1,0:T(8,128)(2,1)}, bf16[16,128,128]{2,1,0:T(8,128)(2,1)}, u32[]{:S(2)}, u32[]{:S(2)}) %collective-permute-start.7) | collective-permute-done | bytes 524320 | tf_op jit(solution)/shard_map/ppermute | solution.py:328
  74.4 1.5 dense_late.1
  75.9 0.3 collective-permute-start.17
  76.3 5.5 %collective-permute-start.16 = (bf16[8,128,128]{2,1,0:T(8,128)(2,1)S(1)}, bf16[8,128,128]{2,1,0:T(8,128)(2,1)S(1)}, u32[]{:S(2)}, u32[]{:S(2)}) collective-permute-start(bf16[8,128,128]{2,1,0:T(8,128)(2,1)S(1)} %get-tuple-element.90.rest_0_), channel_id=1, source_target_pairs={{0,3},{1,2},{2,1},{3,0},{4,7},{5,6},{6,5},{7,4},{8,11},{9,10},{10,... | collective-permute-start | bytes 786440 | tf_op jit(solution)/shard_map/ppermute | solution.py:328
  81.9 0.8 collective-permute-start.19
  82.8 6.9 %aggregate.1 = bf16[16,128,128]{2,1,0:T(8,128)(2,1)S(1)} custom-call(s32[320]{0:T(512)S(1)} %reshape.122.cols_ref, s32[1]{0:T(128)} %bitcast.me_ref.refs_4_, bf16[16,20,128,128]{3,2,1,0:T(8,128)(2,1)} %tiles_ref.5, bf16[16,128,128]{2,1,0:T(8,128)(2,1)S(1)} %bitcast.92, bf16[16,128,128]{2,1,0:T(8,128)(2,1)} %collective-permute-done.9.rest_1_, ...), custom_call_target="tpu_custom_call" | custom-call | flops 1342177280 | bytes 30000000 | tf_op jit(solution)/shard_map/aggregate/pallas_call | solution.py:150
  89.7 5.1 %collective-permute-done.16.rest_3_ = bf16[8,128,128]{2,1,0:T(8,128)(2,1)S(1)} collective-permute-done((bf16[8,128,128]{2,1,0:T(8,128)(2,1)S(1)}, bf16[8,128,128]{2,1,0:T(8,128)(2,1)S(1)}, u32[]{:S(2)}, u32[]{:S(2)}) %collective-permute-start.16) | collective-permute-done | bytes 262176 | tf_op jit(solution)/shard_map/ppermute | solution.py:328
  94.8 6.3 %collective-permute-start.18 = (bf16[8,128,128]{2,1,0:T(8,128)(2,1)S(1)}, bf16[8,128,128]{2,1,0:T(8,128)(2,1)S(1)}, u32[]{:S(2)}, u32[]{:S(2)}) collective-permute-start(bf16[8,128,128]{2,1,0:T(8,128)(2,1)S(1)} %collective-permute-done.16.rest_3_), channel_id=1, source_target_pairs={{0,1},{1,0},{2,3},{3,2},{4,5},{5,4},{6,7},{7,6},{8,9},{9,8},{10,11... | collective-permute-start | bytes 786440 | tf_op jit(solution)/shard_map/ppermute | solution.py:328
  101.1 4.3 %collective-permute-start.21 = (bf16[8,128,128]{2,1,0:T(8,128)(2,1)S(1)}, bf16[8,128,128]{2,1,0:T(8,128)(2,1)S(1)}, u32[]{:S(2)}, u32[]{:S(2)}) collective-permute-start(bf16[8,128,128]{2,1,0:T(8,128)(2,1)S(1)} %collective-permute-done.20.rest_3_), channel_id=1, source_target_pairs={{0,1},{1,0},{2,3},{3,2},{4,5},{5,4},{6,7},{7,6},{8,9},{9,8},{10,11... | collective-permute-start | bytes 786440 | tf_op jit(solution)/shard_map/ppermute | solution.py:328
  105.5 1.7 %collective-permute-done.18.rest_2_ = bf16[8,128,128]{2,1,0:T(8,128)(2,1)S(1)} collective-permute-done((bf16[8,128,128]{2,1,0:T(8,128)(2,1)S(1)}, bf16[8,128,128]{2,1,0:T(8,128)(2,1)S(1)}, u32[]{:S(2)}, u32[]{:S(2)}) %collective-permute-start.18) | collective-permute-done | bytes 262176 | tf_op jit(solution)/shard_map/ppermute | solution.py:328
  107.2 0.6 dense.2
  107.8 4.0 %collective-permute-done.21.rest_2_ = bf16[8,128,128]{2,1,0:T(8,128)(2,1)S(1)} collective-permute-done((bf16[8,128,128]{2,1,0:T(8,128)(2,1)S(1)}, bf16[8,128,128]{2,1,0:T(8,128)(2,1)S(1)}, u32[]{:S(2)}, u32[]{:S(2)}) %collective-permute-start.21) | collective-permute-done | bytes 262176 | tf_op jit(solution)/shard_map/ppermute | solution.py:328
  111.8 0.6 dense.3
  112.4 6.8 %spread.3 = (bf16[4,8,128,128]{3,2,1,0:T(8,128)(2,1)S(1)}, bf16[4,8,128,128]{3,2,1,0:T(8,128)(2,1)S(1)}, bf16[4,8,128,128]{3,2,1,0:T(8,128)(2,1)S(1)}, bf16[4,8,128,128]{3,2,1,0:T(8,128)(2,1)S(1)}) custom-call(s32[320]{0:T(512)S(1)} %reshape.122.cols_ref, s32[1]{0:T(128)} %bitcast.me_ref.refs_4_, bf16[16,20,128,128]{3,2,1,0:T(8,128)(2,1)} %tiles_ref.5, ...), custom_call_target="tpu_custom_call" | custom-call | flops 1342177280 | bytes 30000000 | tf_op jit(solution)/shard_map/spread/pallas_call | solution.py:107
  119.3 0.5 collective-permute-start.23
  119.8 0.2 weight_terms.1
  120.0 0.1 collective-permute-start.24
  120.2 1.8 %collective-permute-done.22 = bf16[4,8,128,128]{3,2,1,0:T(8,128)(2,1)S(1)} collective-permute-done((bf16[4,8,128,128]{3,2,1,0:T(8,128)(2,1)S(1)}, bf16[4,8,128,128]{3,2,1,0:T(8,128)(2,1)S(1)}, u32[]{:S(2)}, u32[]{:S(2)}) %collective-permute-start.22) | collective-permute-done | bytes 1048608 | tf_op jit(solution)/shard_map/ppermute | solution.py:328
  122.0 0.3 add_convert_fusion.3
  122.3 1.6 %collective-permute-start.25 = (bf16[2,8,128,128]{3,2,1,0:T(8,128)(2,1)S(1)}, bf16[2,8,128,128]{3,2,1,0:T(8,128)(2,1)S(1)}, u32[]{:S(2)}, u32[]{:S(2)}) collective-permute-start(bf16[2,8,128,128]{3,2,1,0:T(8,128)(2,1)S(1)} %get-tuple-element.132), channel_id=1, source_target_pairs={{0,16},{4,20},{8,24},{12,28},{16,0},{20,4},{24,8},{28,12},{1,17},{... | collective-permute-start | bytes 1572872 | tf_op jit(solution)/shard_map/ppermute | solution.py:328
  123.9 0.4 fusion.1
  124.3 1.8 %collective-permute-start.26 = (bf16[2,8,128,128]{3,2,1,0:T(8,128)(2,1)S(1)}, bf16[2,8,128,128]{3,2,1,0:T(8,128)(2,1)S(1)}, u32[]{:S(2)}, u32[]{:S(2)}) collective-permute-start(bf16[2,8,128,128]{3,2,1,0:T(8,128)(2,1)S(1)} %get-tuple-element.130), channel_id=1, source_target_pairs={{0,8},{4,12},{8,0},{12,4},{16,24},{20,28},{24,16},{28,20},{1,9},{5... | collective-permute-start | bytes 1572872 | tf_op jit(solution)/shard_map/ppermute | solution.py:328
  126.1 1.2 collective-permute-start.27
  127.3 11.9 %collective-permute-done.27 = bf16[128,512]{1,0:T(8,128)(2,1)S(1)} collective-permute-done((bf16[128,512]{1,0:T(8,128)(2,1)S(1)}, bf16[128,512]{1,0:T(8,128)(2,1)S(1)}, u32[]{:S(2)}, u32[]{:S(2)}) %collective-permute-start.27) | collective-permute-done | bytes 131104 | tf_op jit(solution)/shard_map/ppermute | solution.py:328
  139.2 0.1 fusion.9
  139.4 0.1 fusion.10
  139.5 1.6 %collective-permute-start.30 = (bf16[128,512]{1,0:T(8,128)(2,1)S(1)}, bf16[128,512]{1,0:T(8,128)(2,1)S(1)}, u32[]{:S(2)}, u32[]{:S(2)}) collective-permute-start(bf16[128,512]{1,0:T(8,128)(2,1)S(1)} %convert_add_fusion.3), channel_id=1, source_target_pairs={{0,8},{4,12},{8,0},{12,4},{16,24},{20,28},{24,16},{28,20},{1,9},{5... | collective-permute-start | bytes 393224 | tf_op jit(solution)/shard_map/ppermute | solution.py:328
  141.1 1.7 %collective-permute-start.29 = (bf16[8,128,128]{2,1,0:T(8,128)(2,1)S(1)}, bf16[8,128,128]{2,1,0:T(8,128)(2,1)S(1)}, u32[]{:S(2)}, u32[]{:S(2)}) collective-permute-start(bf16[8,128,128]{2,1,0:T(8,128)(2,1)S(1)} %get-tuple-element.137), channel_id=1, source_target_pairs={{0,16},{4,20},{8,24},{12,28},{16,0},{20,4},{24,8},{28,12},{1,17},{... | collective-permute-start | bytes 786440 | tf_op jit(solution)/shard_map/ppermute | solution.py:328
  142.8 0.3 collective-permute-start.28
  143.1 1.9 %collective-permute-done.30 = bf16[128,512]{1,0:T(8,128)(2,1)S(1)} collective-permute-done((bf16[128,512]{1,0:T(8,128)(2,1)S(1)}, bf16[128,512]{1,0:T(8,128)(2,1)S(1)}, u32[]{:S(2)}, u32[]{:S(2)}) %collective-permute-start.30) | collective-permute-done | bytes 131104 | tf_op jit(solution)/shard_map/ppermute | solution.py:328
  145.1 3.3 %collective-permute-done.29.refs_3_ = bf16[8,128,128]{2,1,0:T(8,128)(2,1)S(1)} collective-permute-done((bf16[8,128,128]{2,1,0:T(8,128)(2,1)S(1)}, bf16[8,128,128]{2,1,0:T(8,128)(2,1)S(1)}, u32[]{:S(2)}, u32[]{:S(2)}) %collective-permute-start.29) | collective-permute-done | bytes 262176 | tf_op jit(solution)/shard_map/ppermute | solution.py:328
  148.5 1.7 %collective-permute-done.28.refs_1_ = bf16[8,128,128]{2,1,0:T(8,128)(2,1)S(1)} collective-permute-done((bf16[8,128,128]{2,1,0:T(8,128)(2,1)S(1)}, bf16[8,128,128]{2,1,0:T(8,128)(2,1)S(1)}, u32[]{:S(2)}, u32[]{:S(2)}) %collective-permute-start.28) | collective-permute-done | bytes 262176 | tf_op jit(solution)/shard_map/ppermute | solution.py:328
  150.2 1.2 finish.3
  (54 shorter events, 0.8 us)
Async XLA Ops:
  1.4 1.0 copy-start.1
  2.5 39.3 %copy-start.2 = (bf16[2048,128]{1,0:T(8,128)(2,1)S(1)}, bf16[2048,128]{1,0:T(8,128)(2,1)}, u32[]{:S(2)}) copy-start(bf16[2048,128]{1,0:T(8,128)(2,1)} %param.8) | copy-start | bytes 1572868
  2.5 63.4 %copy-start.7 = (bf16[128,512]{1,0:T(8,128)(2,1)S(1)}, bf16[128,512]{1,0:T(8,128)(2,1)}, u32[]{:S(2)}) copy-start(bf16[128,512]{1,0:T(8,128)(2,1)} %param.14) | copy-start | bytes 393220
  2.5 63.4 %copy-start.8 = (bf16[128,512]{1,0:T(8,128)(2,1)S(1)}, bf16[128,512]{1,0:T(8,128)(2,1)}, u32[]{:S(2)}) copy-start(bf16[128,512]{1,0:T(8,128)(2,1)} %param.15) | copy-start | bytes 393220
  2.5 64.1 %copy-start = (bf16[2048,128]{1,0:T(8,128)(2,1)S(1)}, bf16[2048,128]{1,0:T(8,128)(2,1)}, u32[]{:S(2)}) copy-start(bf16[2048,128]{1,0:T(8,128)(2,1)} %param.9) | copy-start | bytes 1572868
  9.7 55.7 %copy-start.3 = (bf16[16,128,128]{2,1,0:T(8,128)(2,1)}, bf16[16,128,128]{2,1,0:T(8,128)(2,1)S(1)}, u32[]{:S(2)}) copy-start(bf16[16,128,128]{2,1,0:T(8,128)(2,1)S(1)} %get-tuple-element.78.rest_4_) | copy-start | bytes 1572868
  9.7 2.8 %collective-permute-start = (bf16[4,8,128,128]{3,2,1,0:T(8,128)(2,1)S(1)}, bf16[4,8,128,128]{3,2,1,0:T(8,128)(2,1)S(1)}, u32[]{:S(2)}, u32[]{:S(2)}) collective-permute-start(bf16[4,8,128,128]{3,2,1,0:T(8,128)(2,1)S(1)} %get-tuple-element.67), channel_id=1, source_target_pairs={{0,4},{4,0},{8,12},{12,8},{16,20},{20,16},{24,28},{28,24},{1,5},{5... | collective-permute-start | bytes 3145736 | tf_op jit(solution)/shard_map/ppermute | solution.py:328
  10.2 5.7 %collective-permute-start.3 = (bf16[4,8,128,128]{3,2,1,0:T(8,128)(2,1)S(1)}, bf16[4,8,128,128]{3,2,1,0:T(8,128)(2,1)S(1)}, u32[]{:S(2)}, u32[]{:S(2)}) collective-permute-start(bf16[4,8,128,128]{3,2,1,0:T(8,128)(2,1)S(1)} %get-tuple-element.69), channel_id=1, source_target_pairs={{0,4},{4,0},{8,12},{12,8},{16,20},{20,16},{24,28},{28,24},{1,5},{5... | collective-permute-start | bytes 3145736 | tf_op jit(solution)/shard_map/ppermute | solution.py:328
  13.0 15.2 %collective-permute-start.1 = (bf16[2,8,128,128]{3,2,1,0:T(8,128)(2,1)S(1)}, bf16[2,8,128,128]{3,2,1,0:T(8,128)(2,1)S(1)}, u32[]{:S(2)}, u32[]{:S(2)}) collective-permute-start(bf16[2,8,128,128]{3,2,1,0:T(8,128)(2,1)S(1)} %get-tuple-element.136), channel_id=1, source_target_pairs={{0,16},{4,20},{8,24},{12,28},{16,0},{20,4},{24,8},{28,12},{1,17},{... | collective-permute-start | bytes 1572872 | tf_op jit(solution)/shard_map/ppermute | solution.py:328
  16.3 13.8 %collective-permute-start.4 = (bf16[2,8,128,128]{3,2,1,0:T(8,128)(2,1)S(1)}, bf16[2,8,128,128]{3,2,1,0:T(8,128)(2,1)S(1)}, u32[]{:S(2)}, u32[]{:S(2)}) collective-permute-start(bf16[2,8,128,128]{3,2,1,0:T(8,128)(2,1)S(1)} %get-tuple-element.134), channel_id=1, source_target_pairs={{0,8},{4,12},{8,0},{12,4},{16,24},{20,28},{24,16},{28,20},{1,9},{5... | collective-permute-start | bytes 1572872 | tf_op jit(solution)/shard_map/ppermute | solution.py:328
  28.3 7.9 %collective-permute-start.2 = (bf16[8,128,128]{2,1,0:T(8,128)(2,1)S(1)}, bf16[8,128,128]{2,1,0:T(8,128)(2,1)S(1)}, u32[]{:S(2)}, u32[]{:S(2)}) collective-permute-start(bf16[8,128,128]{2,1,0:T(8,128)(2,1)S(1)} %get-tuple-element.143), channel_id=1, source_target_pairs={{0,8},{4,12},{8,0},{12,4},{16,24},{20,28},{24,16},{28,20},{1,9},{5... | collective-permute-start | bytes 786440 | tf_op jit(solution)/shard_map/ppermute | solution.py:328
  30.2 7.3 %collective-permute-start.5 = (bf16[8,128,128]{2,1,0:T(8,128)(2,1)S(1)}, bf16[8,128,128]{2,1,0:T(8,128)(2,1)S(1)}, u32[]{:S(2)}, u32[]{:S(2)}) collective-permute-start(bf16[8,128,128]{2,1,0:T(8,128)(2,1)S(1)} %get-tuple-element.141), channel_id=1, source_target_pairs={{0,16},{4,20},{8,24},{12,28},{16,0},{20,4},{24,8},{28,12},{1,17},{... | collective-permute-start | bytes 786440 | tf_op jit(solution)/shard_map/ppermute | solution.py:328
  37.7 14.0 %collective-permute-start.8 = (bf16[16,128,128]{2,1,0:T(8,128)(2,1)S(1)}, bf16[16,128,128]{2,1,0:T(8,128)(2,1)S(1)}, u32[]{:S(2)}, u32[]{:S(2)}) collective-permute-start(bf16[16,128,128]{2,1,0:T(8,128)(2,1)S(1)} %finish.2.rest_0_), channel_id=1, source_target_pairs={{0,1},{1,0},{2,3},{3,2},{4,5},{5,4},{6,7},{7,6},{8,9},{9,8},{10,11... | collective-permute-start | bytes 1572872 | tf_op jit(solution)/shard_map/ppermute | solution.py:328
  39.3 23.8 %collective-permute-start.6 = (bf16[16,128,128]{2,1,0:T(8,128)(2,1)S(1)}, bf16[16,128,128]{2,1,0:T(8,128)(2,1)}, u32[]{:S(2)}, u32[]{:S(2)}) collective-permute-start(bf16[16,128,128]{2,1,0:T(8,128)(2,1)S(1)} %finish.2.rest_0_), channel_id=1, source_target_pairs={{0,3},{1,2},{2,1},{3,0},{4,7},{5,6},{6,5},{7,4},{8,11},{9,10},{10,... | collective-permute-start | bytes 1572872 | tf_op jit(solution)/shard_map/ppermute | solution.py:328
  41.8 21.9 %collective-permute-start.14 = (bf16[16,128,128]{2,1,0:T(8,128)(2,1)S(1)}, bf16[16,128,128]{2,1,0:T(8,128)(2,1)S(1)}, u32[]{:S(2)}, u32[]{:S(2)}) collective-permute-start(bf16[16,128,128]{2,1,0:T(8,128)(2,1)S(1)} %bitcast.88), channel_id=1, source_target_pairs={{0,24},{4,28},{8,16},{12,20},{16,8},{20,12},{24,0},{28,4},{1,25},{... | collective-permute-start | bytes 1572872 | tf_op jit(solution)/shard_map/ppermute | solution.py:328
  44.2 21.1 %collective-permute-start.12 = (bf16[16,128,128]{2,1,0:T(8,128)(2,1)S(1)}, bf16[16,128,128]{2,1,0:T(8,128)(2,1)S(1)}, u32[]{:S(2)}, u32[]{:S(2)}) collective-permute-start(bf16[16,128,128]{2,1,0:T(8,128)(2,1)S(1)} %bitcast.89), channel_id=1, source_target_pairs={{0,16},{4,20},{8,24},{12,28},{16,0},{20,4},{24,8},{28,12},{1,17},{... | collective-permute-start | bytes 1572872 | tf_op jit(solution)/shard_map/ppermute | solution.py:328
  44.6 20.8 %collective-permute-start.10 = (bf16[16,128,128]{2,1,0:T(8,128)(2,1)S(1)}, bf16[16,128,128]{2,1,0:T(8,128)(2,1)S(1)}, u32[]{:S(2)}, u32[]{:S(2)}) collective-permute-start(bf16[16,128,128]{2,1,0:T(8,128)(2,1)S(1)} %bitcast.90), channel_id=1, source_target_pairs={{0,8},{4,12},{8,0},{12,4},{16,24},{20,28},{24,16},{28,20},{1,9},{5... | collective-permute-start | bytes 1572872 | tf_op jit(solution)/shard_map/ppermute | solution.py:328
  51.7 0.8 copy-start.5
  52.5 18.1 %collective-permute-start.9 = (bf16[16,128,128]{2,1,0:T(8,128)(2,1)S(1)}, bf16[16,128,128]{2,1,0:T(8,128)(2,1)}, u32[]{:S(2)}, u32[]{:S(2)}) collective-permute-start(bf16[16,128,128]{2,1,0:T(8,128)(2,1)S(1)} %bitcast.91), channel_id=1, source_target_pairs={{0,4},{4,0},{8,12},{12,8},{16,20},{20,16},{24,28},{28,24},{1,5},{5... | collective-permute-start | bytes 1572872 | tf_op jit(solution)/shard_map/ppermute | solution.py:328
  63.1 11.3 %collective-permute-start.7 = (bf16[16,128,128]{2,1,0:T(8,128)(2,1)}, bf16[16,128,128]{2,1,0:T(8,128)(2,1)}, u32[]{:S(2)}, u32[]{:S(2)}) collective-permute-start(bf16[16,128,128]{2,1,0:T(8,128)(2,1)} %collective-permute-done.6.rest_2_), channel_id=1, source_target_pairs={{0,1},{1,0},{2,3},{3,2},{4,5},{5,4},{6,7},{7,6},{8,9},{9,8},{10,11... | collective-permute-start | bytes 1572872 | tf_op jit(solution)/shard_map/ppermute | solution.py:328
  63.7 10.7 %collective-permute-start.15 = (bf16[16,128,128]{2,1,0:T(8,128)(2,1)S(1)}, bf16[16,128,128]{2,1,0:T(8,128)(2,1)}, u32[]{:S(2)}, u32[]{:S(2)}) collective-permute-start(bf16[16,128,128]{2,1,0:T(8,128)(2,1)S(1)} %collective-permute-done.14.rest_6_), channel_id=1, source_target_pairs={{0,4},{4,0},{8,12},{12,8},{16,20},{20,16},{24,28},{28,24},{1,5},{5... | collective-permute-start | bytes 1572872 | tf_op jit(solution)/shard_map/ppermute | solution.py:328
  65.3 9.1 %collective-permute-start.13 = (bf16[16,128,128]{2,1,0:T(8,128)(2,1)S(1)}, bf16[16,128,128]{2,1,0:T(8,128)(2,1)}, u32[]{:S(2)}, u32[]{:S(2)}) collective-permute-start(bf16[16,128,128]{2,1,0:T(8,128)(2,1)S(1)} %collective-permute-done.12.rest_4_), channel_id=1, source_target_pairs={{0,4},{4,0},{8,12},{12,8},{16,20},{20,16},{24,28},{28,24},{1,5},{5... | collective-permute-start | bytes 1572872 | tf_op jit(solution)/shard_map/ppermute | solution.py:328
  65.4 9.0 %collective-permute-start.11 = (bf16[16,128,128]{2,1,0:T(8,128)(2,1)S(1)}, bf16[16,128,128]{2,1,0:T(8,128)(2,1)}, u32[]{:S(2)}, u32[]{:S(2)}) collective-permute-start(bf16[16,128,128]{2,1,0:T(8,128)(2,1)S(1)} %collective-permute-done.10.rest_2_), channel_id=1, source_target_pairs={{0,4},{4,0},{8,12},{12,8},{16,20},{20,16},{24,28},{28,24},{1,5},{5... | collective-permute-start | bytes 1572872 | tf_op jit(solution)/shard_map/ppermute | solution.py:328
  66.6 1.0 copy-start.4
  67.6 1.0 copy-start.6
  75.9 13.7 %collective-permute-start.17 = (bf16[8,128,128]{2,1,0:T(8,128)(2,1)S(1)}, bf16[8,128,128]{2,1,0:T(8,128)(2,1)S(1)}, u32[]{:S(2)}, u32[]{:S(2)}) collective-permute-start(bf16[8,128,128]{2,1,0:T(8,128)(2,1)S(1)} %get-tuple-element.90.rest_0_), channel_id=1, source_target_pairs={{0,1},{1,0},{2,3},{3,2},{4,5},{5,4},{6,7},{7,6},{8,9},{9,8},{10,11... | collective-permute-start | bytes 786440 | tf_op jit(solution)/shard_map/ppermute | solution.py:328
  76.3 18.5 %collective-permute-start.16 = (bf16[8,128,128]{2,1,0:T(8,128)(2,1)S(1)}, bf16[8,128,128]{2,1,0:T(8,128)(2,1)S(1)}, u32[]{:S(2)}, u32[]{:S(2)}) collective-permute-start(bf16[8,128,128]{2,1,0:T(8,128)(2,1)S(1)} %get-tuple-element.90.rest_0_), channel_id=1, source_target_pairs={{0,3},{1,2},{2,1},{3,0},{4,7},{5,6},{6,5},{7,4},{8,11},{9,10},{10,... | collective-permute-start | bytes 786440 | tf_op jit(solution)/shard_map/ppermute | solution.py:328
  81.8 19.3 %collective-permute-start.20 = (bf16[8,128,128]{2,1,0:T(8,128)(2,1)S(1)}, bf16[8,128,128]{2,1,0:T(8,128)(2,1)S(1)}, u32[]{:S(2)}, u32[]{:S(2)}) collective-permute-start(bf16[8,128,128]{2,1,0:T(8,128)(2,1)S(1)} %get-tuple-element.101.rest_0_), channel_id=1, source_target_pairs={{0,3},{1,2},{2,1},{3,0},{4,7},{5,6},{6,5},{7,4},{8,11},{9,10},{10,... | collective-permute-start | bytes 786440 | tf_op jit(solution)/shard_map/ppermute | solution.py:328
  81.9 23.6 %collective-permute-start.19 = (bf16[8,128,128]{2,1,0:T(8,128)(2,1)S(1)}, bf16[8,128,128]{2,1,0:T(8,128)(2,1)S(1)}, u32[]{:S(2)}, u32[]{:S(2)}) collective-permute-start(bf16[8,128,128]{2,1,0:T(8,128)(2,1)S(1)} %get-tuple-element.101.rest_0_), channel_id=1, source_target_pairs={{0,1},{1,0},{2,3},{3,2},{4,5},{5,4},{6,7},{7,6},{8,9},{9,8},{10,11... | collective-permute-start | bytes 786440 | tf_op jit(solution)/shard_map/ppermute | solution.py:328
  94.8 12.4 %collective-permute-start.18 = (bf16[8,128,128]{2,1,0:T(8,128)(2,1)S(1)}, bf16[8,128,128]{2,1,0:T(8,128)(2,1)S(1)}, u32[]{:S(2)}, u32[]{:S(2)}) collective-permute-start(bf16[8,128,128]{2,1,0:T(8,128)(2,1)S(1)} %collective-permute-done.16.rest_3_), channel_id=1, source_target_pairs={{0,1},{1,0},{2,3},{3,2},{4,5},{5,4},{6,7},{7,6},{8,9},{9,8},{10,11... | collective-permute-start | bytes 786440 | tf_op jit(solution)/shard_map/ppermute | solution.py:328
  101.1 10.7 %collective-permute-start.21 = (bf16[8,128,128]{2,1,0:T(8,128)(2,1)S(1)}, bf16[8,128,128]{2,1,0:T(8,128)(2,1)S(1)}, u32[]{:S(2)}, u32[]{:S(2)}) collective-permute-start(bf16[8,128,128]{2,1,0:T(8,128)(2,1)S(1)} %collective-permute-done.20.rest_3_), channel_id=1, source_target_pairs={{0,1},{1,0},{2,3},{3,2},{4,5},{5,4},{6,7},{7,6},{8,9},{9,8},{10,11... | collective-permute-start | bytes 786440 | tf_op jit(solution)/shard_map/ppermute | solution.py:328
  119.3 2.7 %collective-permute-start.22 = (bf16[4,8,128,128]{3,2,1,0:T(8,128)(2,1)S(1)}, bf16[4,8,128,128]{3,2,1,0:T(8,128)(2,1)S(1)}, u32[]{:S(2)}, u32[]{:S(2)}) collective-permute-start(bf16[4,8,128,128]{3,2,1,0:T(8,128)(2,1)S(1)} %get-tuple-element.108), channel_id=1, source_target_pairs={{0,4},{4,0},{8,12},{12,8},{16,20},{20,16},{24,28},{28,24},{1,5},{5... | collective-permute-start | bytes 3145736 | tf_op jit(solution)/shard_map/ppermute | solution.py:328
  119.3 4.6 %collective-permute-start.23 = (bf16[4,8,128,128]{3,2,1,0:T(8,128)(2,1)S(1)}, bf16[4,8,128,128]{3,2,1,0:T(8,128)(2,1)S(1)}, u32[]{:S(2)}, u32[]{:S(2)}) collective-permute-start(bf16[4,8,128,128]{3,2,1,0:T(8,128)(2,1)S(1)} %get-tuple-element.110), channel_id=1, source_target_pairs={{0,4},{4,0},{8,12},{12,8},{16,20},{20,16},{24,28},{28,24},{1,5},{5... | collective-permute-start | bytes 3145736 | tf_op jit(solution)/shard_map/ppermute | solution.py:328
  120.0 6.0 %collective-permute-start.24 = (bf16[128,512]{1,0:T(8,128)(2,1)S(1)}, bf16[128,512]{1,0:T(8,128)(2,1)S(1)}, u32[]{:S(2)}, u32[]{:S(2)}) collective-permute-start(bf16[128,512]{1,0:T(8,128)(2,1)S(1)} %get-tuple-element.116), channel_id=1, source_target_pairs={{0,4},{4,0},{8,12},{12,8},{16,20},{20,16},{24,28},{28,24},{1,5},{5... | collective-permute-start | bytes 393224 | tf_op jit(solution)/shard_map/ppermute | solution.py:328
  122.3 16.9 %collective-permute-start.25 = (bf16[2,8,128,128]{3,2,1,0:T(8,128)(2,1)S(1)}, bf16[2,8,128,128]{3,2,1,0:T(8,128)(2,1)S(1)}, u32[]{:S(2)}, u32[]{:S(2)}) collective-permute-start(bf16[2,8,128,128]{3,2,1,0:T(8,128)(2,1)S(1)} %get-tuple-element.132), channel_id=1, source_target_pairs={{0,16},{4,20},{8,24},{12,28},{16,0},{20,4},{24,8},{28,12},{1,17},{... | collective-permute-start | bytes 1572872 | tf_op jit(solution)/shard_map/ppermute | solution.py:328
  124.3 14.9 %collective-permute-start.26 = (bf16[2,8,128,128]{3,2,1,0:T(8,128)(2,1)S(1)}, bf16[2,8,128,128]{3,2,1,0:T(8,128)(2,1)S(1)}, u32[]{:S(2)}, u32[]{:S(2)}) collective-permute-start(bf16[2,8,128,128]{3,2,1,0:T(8,128)(2,1)S(1)} %get-tuple-element.130), channel_id=1, source_target_pairs={{0,8},{4,12},{8,0},{12,4},{16,24},{20,28},{24,16},{28,20},{1,9},{5... | collective-permute-start | bytes 1572872 | tf_op jit(solution)/shard_map/ppermute | solution.py:328
  126.1 13.1 %collective-permute-start.27 = (bf16[128,512]{1,0:T(8,128)(2,1)S(1)}, bf16[128,512]{1,0:T(8,128)(2,1)S(1)}, u32[]{:S(2)}, u32[]{:S(2)}) collective-permute-start(bf16[128,512]{1,0:T(8,128)(2,1)S(1)} %convert_add_fusion.4), channel_id=1, source_target_pairs={{0,16},{4,20},{8,24},{12,28},{16,0},{20,4},{24,8},{28,12},{1,17},{... | collective-permute-start | bytes 393224 | tf_op jit(solution)/shard_map/ppermute | solution.py:328
  139.5 5.5 %collective-permute-start.30 = (bf16[128,512]{1,0:T(8,128)(2,1)S(1)}, bf16[128,512]{1,0:T(8,128)(2,1)S(1)}, u32[]{:S(2)}, u32[]{:S(2)}) collective-permute-start(bf16[128,512]{1,0:T(8,128)(2,1)S(1)} %convert_add_fusion.3), channel_id=1, source_target_pairs={{0,8},{4,12},{8,0},{12,4},{16,24},{20,28},{24,16},{28,20},{1,9},{5... | collective-permute-start | bytes 393224 | tf_op jit(solution)/shard_map/ppermute | solution.py:328
  141.1 7.4 %collective-permute-start.29 = (bf16[8,128,128]{2,1,0:T(8,128)(2,1)S(1)}, bf16[8,128,128]{2,1,0:T(8,128)(2,1)S(1)}, u32[]{:S(2)}, u32[]{:S(2)}) collective-permute-start(bf16[8,128,128]{2,1,0:T(8,128)(2,1)S(1)} %get-tuple-element.137), channel_id=1, source_target_pairs={{0,16},{4,20},{8,24},{12,28},{16,0},{20,4},{24,8},{28,12},{1,17},{... | collective-permute-start | bytes 786440 | tf_op jit(solution)/shard_map/ppermute | solution.py:328
  142.8 7.4 %collective-permute-start.28 = (bf16[8,128,128]{2,1,0:T(8,128)(2,1)S(1)}, bf16[8,128,128]{2,1,0:T(8,128)(2,1)S(1)}, u32[]{:S(2)}, u32[]{:S(2)}) collective-permute-start(bf16[8,128,128]{2,1,0:T(8,128)(2,1)S(1)} %get-tuple-element.139), channel_id=1, source_target_pairs={{0,8},{4,12},{8,0},{12,4},{16,24},{20,28},{24,16},{28,20},{1,9},{5... | collective-permute-start | bytes 786440 | tf_op jit(solution)/shard_map/ppermute | solution.py:328
  145.1 5.1 %collective-permute-start.31 = (f32[128,512]{1,0:T(8,128)S(1)}, f32[128,512]{1,0:T(8,128)S(1)}, u32[]{:S(2)}, u32[]{:S(2)}) collective-permute-start(f32[128,512]{1,0:T(8,128)S(1)} %convert_add_fusion.2.refs_5_), channel_id=1, source_target_pairs={{0,4},{4,0},{8,12},{12,8},{16,20},{20,16},{24,28},{28,24},{1,5},{5... | collective-permute-start | bytes 786440 | tf_op jit(solution)/shard_map/ppermute | solution.py:328
